TPU v7x, 32 devices: a whole 2x2x4 slice. The times are simulated.
32 devices in a mesh: parts: 2 (over x), store: 8 (over z, core), layer: 2 (over y).
Axes of the slice: x: 2, y: 2, z: 4, core: 2. Of those that a mesh axis runs over, the one named last changes fastest.
Arguments:
- train_grads: bfloat16 [16384, 2, 4096], P(('parts', 'store'), 'layer'), parts along dimension 0, may hold values from -0.09375 to 0.09375
- query_grads: bfloat16 [512, 2, 4096], P('store', 'layer'), may hold values from -6 to 6
- left_factor: float32 [2, 64, 64], P('layer'), may hold values from -0.75 to 0.75
- right_factor: float32 [2, 64, 64], P('layer'), may hold values from -0.75 to 0.75
- layer_weight: float32 [2], replicated, may hold values from 0.25 to 4
- layer_of: int32 [2], P('layer'), may hold values from 0 to 1, each once
- train_ids: int32 [16384], P(('parts', 'store')), parts along dimension 0, may hold values from 0 to 63
- query_ids: int32 [512], P('layer'), may hold values from 0 to 63
Outputs:
- scores: float32 [512, 16384], P('layer', ('parts', 'store')), parts along dimension 1
There are 2 independent parts, one for each index of `parts`. A program takes and returns all parts, laid end to end along the dimension named above; an argument that names none is the same for every part. Nothing has to cross between parts.
Inputs may be any that keep to these rules, and one draw needn't show every extreme that they name: `layer_of`: each layer number appears once.
All inputs are finite; a program needn't handle non-finite values.
Results may differ from a plain program's by a relative error of at most 0.0029.
Values may be sent and summed in bfloat16 or wider, within the bound.
No kernel may reach another device: no remote copies, remote signals or barrier semaphores. Data moves between devices by JAX's collectives and lax.ppermute only.
A program may use at most 64 MiB of HBM per device.

v0:
```python
import jax
import jax.numpy as jnp
from jax import lax
from jax.sharding import PartitionSpec as P


def weighted_term(queries, train_grads, weights):
    partial_value = jnp.dot(
        queries[:, 0, :], train_grads[:, 0, :].T, preferred_element_type=jnp.float32
    )
    total = weights[0] * partial_value
    return total


def shards(
    train_grads,
    query_grads,
    left_factor,
    right_factor,
    layer_weight,
    layer_of,
    train_ids,
    query_ids,
):
    q_rows, slots, width = query_grads.shape
    side = left_factor.shape[1]
    mats = query_grads.astype(jnp.float32).reshape(q_rows, slots, side, side)
    half = jnp.einsum("lij,qljk->qlik", left_factor, mats, precision=lax.Precision.HIGHEST)
    full = jnp.einsum("qlik,lkm->qlim", half, right_factor, precision=lax.Precision.HIGHEST)
    precond = full.reshape(q_rows, slots, width).astype(jnp.bfloat16)
    onehot = (
        layer_of[:, None] == jnp.arange(layer_weight.shape[0], dtype=jnp.int32)[None, :]
    ).astype(jnp.float32)
    weights = jnp.sum(onehot * layer_weight[None, :], axis=1)
    terms = weighted_term(
        lax.all_gather(precond, "store", axis=0, tiled=True), train_grads, weights
    )
    summed = lax.psum_scatter(terms, "layer", scatter_dimension=0, tiled=True)
    same = query_ids[:, None] == train_ids[None, :]
    return jnp.where(same, jnp.float32(0.0), summed)


def solution(mesh):
    placed = (
        P(("parts", "store"), "layer", None),
        P("store", "layer", None),
        P("layer", None, None),
        P("layer", None, None),
        P(),
        P("layer"),
        P(("parts", "store")),
        P("layer"),
    )
    return jax.shard_map(
        shards,
        mesh=mesh,
        in_specs=placed,
        out_specs=P("layer", ("parts", "store")),
        check_vma=False,
    )
```

profile of v0, /device:TPU:0, one launch (start us, length us, event | category | flops | bytes accessed | tf_op | source)
XLA Modules:
  0.0 116.1 jit_solution(12076908281226940251)
XLA Ops:
  6.5 0.0 copy-start
  6.5 0.0 copy-start.1
  6.5 0.0 all-gather.2.cloned.1.call-start
  6.5 2.1 %reshape.41 = bf16[64,64,64]{2,1,0:T(8,128)(2,1)S(1)} reshape(bf16[64,1,4096]{2,0,1:T(8,128)(2,1)} %param.9) | data formatting | bytes 1048576 | tf_op jit(solution)/shard_map/reshape.1
  8.6 0.0 copy-done
  8.6 1.2 %fusion.17 = f32[64,64,64]{2,1,0:T(8,128)S(1)} fusion(bf16[64,64,64]{2,1,0:T(8,128)(2,1)S(1)} %reshape.41, f32[1,64,64]{2,1,0:T(8,128)S(1)} %copy-done), kind=kOutput, calls=%fused_computation.10 | convolution fusion | flops 201326592 | bytes 1589248 | tf_op jit(solution)/shard_map/lij,qljk->qlik/dot_general | solution.py:28
  9.9 0.0 copy-done.1
  9.9 0.0 copy-start.4
  9.9 3.5 %fusion.13 = bf16[64,1,64,64]{3,2,0,1:T(8,128)(2,1)S(1)} fusion(f32[64,64,64]{2,1,0:T(8,128)S(1)} %fusion.17, f32[1,64,64]{2,1,0:T(8,128)S(1)} %copy-done.1), kind=kOutput, calls=%fused_computation.7 | convolution fusion | flops 201588736 | bytes 1589248 | tf_op jit(solution)/shard_map/qlik,lkm->qlim/dot_general | solution.py:29
  13.4 1.6 %convert_element_type.29 = bf16[64,1,4096]{2,0,1:T(8,128)(2,1)} reshape(bf16[64,1,64,64]{3,2,0,1:T(8,128)(2,1)S(1)} %fusion.13) | data formatting | bytes 1048576 | tf_op jit(solution)/shard_map/convert_element_type | solution.py:30
  15.0 0.0 all-gather.2.cloned.1.call-update
  15.1 0.0 reduce-scatter.2.cloned.1.call-start
  15.8 0.0 copy-done.4
  15.8 0.7 fusion.19
  16.4 48.6 %all-gather.2.cloned.1.call-done = bf16[512,1,4096]{2,0,1:T(8,128)(2,1)} async-done(((bf16[64,1,4096]{2,0,1:T(8,128)(2,1)}), bf16[512,1,4096]{2,0,1:T(8,128)(2,1)}) %all-gather.2.cloned.1.call-update) | async-done | bytes 4194320 | tf_op jit(solution)/shard_map/all_gather | solution.py:36
  65.1 11.1 %fusion.5 = f32[512,1024]{1,0:T(8,128)} fusion(bf16[1024,1,4096]{2,0,1:T(8,128)(2,1)} %param.8, bf16[512,1,4096]{2,0,1:T(8,128)(2,1)} %all-gather.2.cloned.1.call-done, f32[]{:T(128)} %fusion.19), kind=kOutput, calls=%fused_computation.5 | convolution fusion | flops 4295491584 | bytes 14680068 | tf_op jit(solution)/shard_map/dot_general | solution.py:8
  76.2 0.0 copy-start.2
  76.2 0.0 copy-start.3
  76.2 0.0 reduce-scatter.2.cloned.1.call-update
  76.2 30.7 %reduce-scatter.2.cloned.1.call-done = f32[256,1024]{1,0:T(8,128)} async-done(((f32[512,1024]{1,0:T(8,128)}), f32[256,1024]{1,0:T(8,128)}) %reduce-scatter.2.cloned.1.call-update) | async-done | bytes 1048592 | tf_op jit(solution)/shard_map/reduce_scatter | solution.py:38
  106.9 0.0 copy-done.2
  106.9 0.0 copy-done.3
  106.9 2.3 %compare_select_fusion = f32[256,1024]{1,0:T(8,128)} fusion(f32[256,1024]{1,0:T(8,128)} %reduce-scatter.2.cloned.1.call-done, s32[1024]{0:T(1024)S(1)} %copy-done.2, s32[256]{0:T(256)S(1)} %copy-done.3), kind=kLoop, calls=%fused_computation.8 | loop fusion | flops 524288 | bytes 2102272 | tf_op jit(solution)/shard_map/jit(_where)/select_n | solution.py:40
Async XLA Ops:
  6.5 2.1 %copy-start = (f32[1,64,64]{2,1,0:T(8,128)S(1)}, f32[1,64,64]{2,1,0:T(8,128)}, u32[]{:S(2)}) copy-start(f32[1,64,64]{2,1,0:T(8,128)} %param.10) | copy-start | bytes 49156
  6.5 3.3 %copy-start.1 = (f32[1,64,64]{2,1,0:T(8,128)S(1)}, f32[1,64,64]{2,1,0:T(8,128)}, u32[]{:S(2)}) copy-start(f32[1,64,64]{2,1,0:T(8,128)} %param.11) | copy-start | bytes 49156
  6.5 58.5 %all-gather.2.cloned.1.call-start = ((), (), s32[]{:S(2)}) async-start(), calls=%async_computation.1 | async-start | bytes 4718592 | tf_op jit(solution)/shard_map/all_gather | solution.py:36
  9.9 5.9 %copy-start.4 = (f32[2]{0:T(128)S(1)}, f32[2]{0:T(128)}, u32[]{:S(2)}) copy-start(f32[2]{0:T(128)} %param.12) | copy-start | bytes 28
  15.1 91.8 %reduce-scatter.2.cloned.1.call-start = ((), (), s32[]{:S(2)}) async-start(), calls=%async_computation.2 | async-start | bytes 3145728 | tf_op jit(solution)/shard_map/reduce_scatter | solution.py:38
  76.2 30.7 %copy-start.2 = (s32[1024]{0:T(1024)S(1)}, s32[1024]{0:T(1024)}, u32[]{:S(2)}) copy-start(s32[1024]{0:T(1024)} %param.14) | copy-start | bytes 12292
  76.2 30.7 %copy-start.3 = (s32[256]{0:T(256)S(1)}, s32[256]{0:T(256)}, u32[]{:S(2)}) copy-start(s32[256]{0:T(256)} %param.15) | copy-start | bytes 3076
Sparse Core Ops, SparseCore 0:
  15.2 49.8 all-gather.1
  76.3 30.5 reduce-scatter.1
where the time goes:
time: 116 us
  waiting for transfers between devices  79.4 us (68%)
  matrix products  15.9 us (14%)
  between operations  14.1 us (12%)
  local copies, waits for them, and re-layouts  3.71 us (3%)
  other arithmetic  2.99 us (3%)
    all_gather x1, waiting for transfers between devices, shards(): lax.all_gather(precond, 'store', axis=0, tiled=True)  48.6 us
    reduce_scatter x1, waiting for transfers between devices, shards(): summed = lax.psum_scatter(terms, 'layer', scatter_dimension=0, tiled=True)  30.7 us
    dot_general x1, matrix products, weighted_term(): jnp.dot(queries[:, 0, :], train_grads[:, 0, :].T, preferred_element_type=...  11.1 us
    dot_general x1, matrix products, shards(): jnp.einsum('qlik,lkm->qlim', half, right_factor, precision=lax.Precision....  3.53 us
    select_n x1, other arithmetic, shards(): return jnp.where(same, jnp.float32(0.0), summed)  2.33 us
  transfers between devices with their start and end apart: 2, of which 2 were waited for; matrix products, arithmetic and copies ran while one was open for 1% of the time, Pallas kernels for 0%

commit v1 on v0

v1 whole, which is shorter than its diff:
```python
import functools

import jax
import jax.numpy as jnp
from jax import lax
from jax.experimental import pallas as pl
from jax.experimental.pallas import tpu as pltpu
from jax.sharding import PartitionSpec as P

AXES = ("parts", "store", "layer")
VMEM = pl.BlockSpec(memory_space=pltpu.VMEM)
SMEM = pl.BlockSpec(memory_space=pltpu.SMEM)
LIMIT = 48 * 1024 * 1024


def preconditioned(query_grads, left_factor, right_factor):
    q_rows, slots, width = query_grads.shape
    side = left_factor.shape[1]
    mats = query_grads.astype(jnp.float32).reshape(q_rows, slots, side, side)
    half = jnp.einsum("lij,qljk->qlik", left_factor, mats, precision=lax.Precision.HIGHEST)
    full = jnp.einsum("qlik,lkm->qlim", half, right_factor, precision=lax.Precision.HIGHEST)
    return full.reshape(q_rows, slots, width).astype(jnp.bfloat16)


def general(
    train_grads,
    query_grads,
    left_factor,
    right_factor,
    layer_weight,
    layer_of,
    train_ids,
    query_ids,
):
    precond = preconditioned(query_grads, left_factor, right_factor)
    weight = jnp.take(layer_weight, layer_of[0])
    queries = lax.all_gather(precond, "store", axis=0, tiled=True)
    terms = weight * jnp.dot(
        queries[:, 0, :], train_grads[:, 0, :].T, preferred_element_type=jnp.float32
    )
    summed = lax.psum_scatter(terms, "layer", scatter_dimension=0, tiled=True)
    same = query_ids[:, None] == train_ids[None, :]
    return jnp.where(same, jnp.float32(0.0), summed)


PARTS, CHIPS, CORES, LAYERS = 2, 4, 2, 2


def permute(value, target):
    pairs = []
    for p in range(PARTS):
        for z in range(CHIPS):
            for c in range(CORES):
                for l in range(LAYERS):
                    tp, tz, tc, tl = target(p, z, c, l)
                    source = ((p * CHIPS + z) * CORES + c) * LAYERS + l
                    pairs.append((source, ((tp * CHIPS + tz) * CORES + tc) * LAYERS + tl))
    return lax.ppermute(value, AXES, pairs)


to_part = functools.partial(permute, target=lambda p, z, c, l: (1 - p, z, c, l))
to_core = functools.partial(permute, target=lambda p, z, c, l: (p, z, 1 - c, l))
to_layer = functools.partial(permute, target=lambda p, z, c, l: (p, z, c, 1 - l))
to_near = functools.partial(permute, target=lambda p, z, c, l: (p, z ^ 1, c, l))
to_far = functools.partial(permute, target=lambda p, z, c, l: (p, z ^ 3, c, l))


def place():
    store = lax.axis_index("store")
    return lax.axis_index("parts"), store // CORES, store % CORES, lax.axis_index("layer")


def scores_of(pieces, train_ref, weight_ref, layer_ref, write):
    weight = weight_ref[layer_ref[0]]
    queries = jnp.concatenate([piece[...] for piece in pieces], axis=0)
    n, step = train_ref.shape[0], 256
    for at in range(0, n, step):
        part = lax.dot_general(
            queries,
            train_ref[at : at + step, :],
            (((1,), (1,)), ((), ())),
            preferred_element_type=jnp.float32,
        )
        write(slice(at, at + step), weight * part)


def keep_kernel(weight_ref, layer_ref, train_ref, *refs):
    *pieces, out = refs

    def write(columns, value):
        out[:, columns] = value

    scores_of(pieces, train_ref, weight_ref, layer_ref, write)


def swap_kernel(weight_ref, layer_ref, train_ref, early, *refs):
    *pieces, send, keep = refs
    _, z, _, layer = place()
    near_is_mine = z // 2 == layer

    def write(columns, value):
        before = early[:, columns]
        send[:, columns] = jnp.where(near_is_mine, value, before).astype(send.dtype)
        keep[:, columns] = jnp.where(near_is_mine, before, value)

    scores_of(pieces, train_ref, weight_ref, layer_ref, write)


def call_scores(kernel, weight, layer, train, inputs, outs):
    rows, n = 128, train.shape[0]
    return pl.pallas_call(
        kernel,
        out_shape=[jax.ShapeDtypeStruct((rows, n), t) for t in outs],
        in_specs=[SMEM, SMEM] + [VMEM] * (1 + len(inputs)),
        out_specs=[VMEM] * len(outs),
        compiler_params=pltpu.CompilerParams(vmem_limit_bytes=LIMIT),
        cost_estimate=pl.CostEstimate(
            flops=2 * rows * n * train.shape[1], bytes_accessed=train.size * 2, transcendentals=0
        ),
    )(weight, layer, train, *inputs)


def final_kernel(train_ids, query_ids, keep0, keep1, got0, got1, out):
    part, z, core, layer = place()
    near_is_mine = z // 2 == layer
    low = z % 2
    first = jnp.where(near_is_mine, low, 1 - low)
    quarter = out.shape[0] // 8
    ids = train_ids[...]
    for block, keep, got in ((first, keep0, got0), (1 - first, keep1, got1)):
        for k in range(4):
            c = core if k < 2 else 1 - core
            h = part if k % 2 == 0 else 1 - part
            at = pl.multiple_of(((block * 2 + c) * 2 + h) * quarter, quarter)
            here = pl.ds(k * quarter, quarter)
            total = keep[here, :] + got[here, :].astype(jnp.float32)
            same = query_ids[pl.ds(at, quarter), :] == ids
            out[pl.ds(at, quarter), :] = jnp.where(same, jnp.float32(0.0), total)


def small(
    train_grads,
    query_grads,
    left_factor,
    right_factor,
    layer_weight,
    layer_of,
    train_ids,
    query_ids,
):
    train = train_grads[:, 0, :]
    precond = preconditioned(query_grads, left_factor, right_factor)[:, 0, :]
    rows = precond.shape[0] // 2
    part = lax.axis_index("parts")
    mine = lax.dynamic_slice_in_dim(precond, part * rows, rows, 0)
    other = lax.dynamic_slice_in_dim(precond, (1 - part) * rows, rows, 0)

    near = to_near(mine)
    far = to_far(mine)
    cross = lambda a, b: to_core(jnp.concatenate([a, b], axis=0))
    score = functools.partial(call_scores, weight=layer_weight, layer=layer_of, train=train)
    f32, bf16 = jnp.float32, jnp.bfloat16

    (scores0,) = score(keep_kernel, inputs=[mine, other, cross(mine, other)], outs=[f32])
    near_x = to_part(near)
    (scores1,) = score(keep_kernel, inputs=[near, near_x, cross(near, near_x)], outs=[f32])
    last = to_near(far)
    far_x = to_part(far)
    send0, keep0 = score(
        swap_kernel, inputs=[scores0, far, far_x, cross(far, far_x)], outs=[bf16, f32]
    )
    got0 = to_layer(send0)
    last_x = to_part(last)
    send1, keep1 = score(
        swap_kernel, inputs=[scores1, last, last_x, cross(last, last_x)], outs=[bf16, f32]
    )
    got1 = to_layer(send1)
    return pl.pallas_call(
        final_kernel,
        out_shape=jax.ShapeDtypeStruct((query_ids.shape[0], train_ids.shape[0]), f32),
        in_specs=[VMEM] * 6,
        out_specs=VMEM,
        compiler_params=pltpu.CompilerParams(vmem_limit_bytes=LIMIT),
    )(train_ids[None, :], query_ids[:, None], keep0, keep1, got0, got1)


def solution(mesh):
    placed = (
        P(("parts", "store"), "layer", None),
        P("store", "layer", None),
        P("layer", None, None),
        P("layer", None, None),
        P(),
        P("layer"),
        P(("parts", "store")),
        P("layer"),
    )
    sizes = tuple(mesh.shape[axis] for axis in AXES)
    return jax.shard_map(
        small if sizes == (PARTS, CHIPS * CORES, LAYERS) else general,
        mesh=mesh,
        in_specs=placed,
        out_specs=P("layer", ("parts", "store")),
        check_vma=False,
    )
```

time: 116 us -> 77.2 us (0.67); the launches traced: 116 us -> 75.8 us
  waiting for transfers between devices: 79.4 us -> 27.6 us
  Pallas kernels: 0 us -> 26.3 us
  between operations: 14.1 us -> 0.86 us
  starting transfers between devices: 0.04 us -> 13.1 us
  matrix products: 15.9 us -> 4.76 us
  other arithmetic: 2.99 us -> 0.14 us
    all_gather x1 -> x0, waiting for transfers between devices: 48.6 us -> none  [shards(): lax.all_gather(precond, 'store', axis=0, tiled=True)]
    reduce_scatter x1 -> x0, waiting for transfers between devices: 30.7 us -> none  [shards(): summed = lax.psum_scatter(terms, 'layer', scatter_dimension=0, tiled=True)]
    ppermute x0 -> x12, waiting for transfers between devices: none -> 27.6 us  [permute(): return lax.ppermute(value, AXES, pairs)]
    pallas_call x0 -> x5, Pallas kernels: none -> 26.3 us  [the longest x4 25.1 us: call_scores(): pl.pallas_call(kernel, out_shape=[jax.ShapeDtypeStruct((rows, n), t) for...]
    ppermute x0 -> x12, starting transfers between devices: none -> 13.1 us  [permute(): return lax.ppermute(value, AXES, pairs)]
    dot_general x3 -> x2, matrix products: 15.9 us -> 4.76 us  [the longest x1 3.53 us: preconditioned(): jnp.einsum('qlik,lkm->qlim', half, right_factor, precision=lax.Precision....]
    select_n x1 -> x0, other arithmetic: 2.33 us -> none  [shards(): return jnp.where(same, jnp.float32(0.0), summed)]
    another operation x1 -> x0, local copies, waits for them, and re-layouts: 2.07 us -> none
  transfers between devices with their start and end apart: 2 -> 12, of which waited for: 2 -> 5; matrix products, arithmetic and copies ran while one was open for 1% -> 0% of each run, Pallas kernels for 0% -> 33%
where the time goes in v1:
time: 77.2 us; the launch traced here: 75.8 us
  waiting for transfers between devices  27.6 us (36%)
  Pallas kernels  26.3 us (34%)
  starting transfers between devices  13.1 us (17%)
  matrix products  4.76 us (6%)
  local copies, waits for them, and re-layouts  3.07 us (4%)
  between operations  0.86 us (1%)
    ppermute x12, waiting for transfers between devices, permute(): return lax.ppermute(value, AXES, pairs)  27.6 us
    pallas_call x4, Pallas kernels, call_scores(): pl.pallas_call(kernel, out_shape=[jax.ShapeDtypeStruct((rows, n), t) for...  25.1 us
    ppermute x12, starting transfers between devices, permute(): return lax.ppermute(value, AXES, pairs)  13.1 us
    dot_general x1, matrix products, preconditioned(): jnp.einsum('qlik,lkm->qlim', half, right_factor, precision=lax.Precision....  3.53 us
    reshape x1, local copies, waits for them, and re-layouts  2.06 us
  transfers between devices with their start and end apart: 12, of which 5 were waited for; matrix products, arithmetic and copies ran while one was open for 0% of the time, Pallas kernels for 33%

profile of v1, /device:TPU:0, one launch (start us, length us, event | category | flops | bytes accessed | tf_op | source)
XLA Modules:
  0.0 75.8 jit_solution(14889517515161169621)
XLA Ops:
  0.0 2.1 %reshape.33 = bf16[64,64,64]{2,1,0:T(8,128)(2,1)S(1)} reshape(bf16[64,1,4096]{2,0,1:T(8,128)(2,1)} %param.9) | data formatting | bytes 1048576 | tf_op jit(solution)/shard_map/reshape
  2.1 1.2 %fusion.9 = f32[64,64,64]{2,1,0:T(8,128)S(1)} fusion(bf16[64,64,64]{2,1,0:T(8,128)(2,1)S(1)} %reshape.33, f32[1,64,64]{2,1,0:T(8,128)S(1)} %copy-done), kind=kOutput, calls=%fused_computation.11 | convolution fusion | flops 201326592 | bytes 1589248 | tf_op jit(solution)/shard_map/lij,qljk->qlik/dot_general | solution.py:20
  3.3 3.5 %fusion.5 = bf16[64,1,64,64]{3,2,0,1:T(8,128)(2,1)S(1)} fusion(f32[64,64,64]{2,1,0:T(8,128)S(1)} %fusion.9, f32[1,64,64]{2,1,0:T(8,128)S(1)} %copy-done.3), kind=kOutput, calls=%fused_computation.3 | convolution fusion | flops 201588736 | bytes 1589248 | tf_op jit(solution)/shard_map/qlik,lkm->qlim/dot_general | solution.py:21
  6.9 0.8 %convert_element_type.28 = bf16[64,1,4096]{2,0,1:T(8,128)(2,1)S(1)} reshape(bf16[64,1,64,64]{3,2,0,1:T(8,128)(2,1)S(1)} %fusion.5) | data formatting | bytes 1048576 | tf_op jit(solution)/shard_map/convert_element_type | solution.py:22
  7.7 3.1 %collective-permute-start.4 = (bf16[32,4096]{1,0:T(8,128)(2,1)S(1)}, bf16[32,4096]{1,0:T(8,128)(2,1)S(1)}, u32[]{:S(2)}, u32[]{:S(2)}) collective-permute-start(bf16[32,4096]{1,0:T(8,128)(2,1)S(1)} %get-tuple-element.14.refs_0_), channel_id=1, source_target_pairs={{0,4},{1,5},{2,6},{3,7},{4,0},{5,1},{6,2},{7,3},{8,12},{9,13},{10,... | collective-permute-start | bytes 786440 | tf_op jit(solution)/shard_map/ppermute | solution.py:58
  10.8 2.5 %collective-permute-start.1 = (bf16[32,4096]{1,0:T(8,128)(2,1)S(1)}, bf16[32,4096]{1,0:T(8,128)(2,1)S(1)}, u32[]{:S(2)}, u32[]{:S(2)}) collective-permute-start(bf16[32,4096]{1,0:T(8,128)(2,1)S(1)} %get-tuple-element.14.refs_0_), channel_id=1, source_target_pairs={{0,12},{1,13},{2,14},{3,15},{4,8},{5,9},{6,10},{7,11},{8,4},{9,5},... | collective-permute-start | bytes 786440 | tf_op jit(solution)/shard_map/ppermute | solution.py:58
  13.3 4.2 %collective-permute-done.4.refs_0_ = bf16[32,4096]{1,0:T(8,128)(2,1)S(1)} collective-permute-done((bf16[32,4096]{1,0:T(8,128)(2,1)S(1)}, bf16[32,4096]{1,0:T(8,128)(2,1)S(1)}, u32[]{:S(2)}, u32[]{:S(2)}) %collective-permute-start.4) | collective-permute-done | bytes 262176 | tf_op jit(solution)/shard_map/ppermute | solution.py:58
  17.6 1.5 %collective-permute-start.5 = (bf16[32,4096]{1,0:T(8,128)(2,1)S(1)}, bf16[32,4096]{1,0:T(8,128)(2,1)S(1)}, u32[]{:S(2)}, u32[]{:S(2)}) collective-permute-start(bf16[32,4096]{1,0:T(8,128)(2,1)S(1)} %collective-permute-done.4.refs_0_), channel_id=1, source_target_pairs={{0,16},{1,17},{2,18},{3,19},{4,20},{5,21},{6,22},{7,23},{8,24},{9,... | collective-permute-start | bytes 786440 | tf_op jit(solution)/shard_map/ppermute | solution.py:58
  19.1 0.1 collective-permute-start
  19.2 5.9 %collective-permute-done.1.refs_0_ = bf16[32,4096]{1,0:T(8,128)(2,1)S(1)} collective-permute-done((bf16[32,4096]{1,0:T(8,128)(2,1)S(1)}, bf16[32,4096]{1,0:T(8,128)(2,1)S(1)}, u32[]{:S(2)}, u32[]{:S(2)}) %collective-permute-start.1) | collective-permute-done | bytes 262176 | tf_op jit(solution)/shard_map/ppermute | solution.py:58
  25.1 0.6 collective-permute-start.7
  25.6 1.5 %collective-permute-start.2 = (bf16[32,4096]{1,0:T(8,128)(2,1)S(1)}, bf16[32,4096]{1,0:T(8,128)(2,1)S(1)}, u32[]{:S(2)}, u32[]{:S(2)}) collective-permute-start(bf16[32,4096]{1,0:T(8,128)(2,1)S(1)} %collective-permute-done.1.refs_0_), channel_id=1, source_target_pairs={{0,16},{1,17},{2,18},{3,19},{4,20},{5,21},{6,22},{7,23},{8,24},{9,... | collective-permute-start | bytes 786440 | tf_op jit(solution)/shard_map/ppermute | solution.py:58
  27.3 4.9 %collective-permute-done.7.refs_0_ = bf16[32,4096]{1,0:T(8,128)(2,1)S(1)} collective-permute-done((bf16[32,4096]{1,0:T(8,128)(2,1)S(1)}, bf16[32,4096]{1,0:T(8,128)(2,1)S(1)}, u32[]{:S(2)}, u32[]{:S(2)}) %collective-permute-start.7) | collective-permute-done | bytes 262176 | tf_op jit(solution)/shard_map/ppermute | solution.py:58
  32.2 1.5 %collective-permute-start.8 = (bf16[32,4096]{1,0:T(8,128)(2,1)S(1)}, bf16[32,4096]{1,0:T(8,128)(2,1)S(1)}, u32[]{:S(2)}, u32[]{:S(2)}) collective-permute-start(bf16[32,4096]{1,0:T(8,128)(2,1)S(1)} %collective-permute-done.7.refs_0_), channel_id=1, source_target_pairs={{0,16},{1,17},{2,18},{3,19},{4,20},{5,21},{6,22},{7,23},{8,24},{9,... | collective-permute-start | bytes 786440 | tf_op jit(solution)/shard_map/ppermute | solution.py:58
  33.8 4.8 %collective-permute-done.8.refs_1_ = bf16[32,4096]{1,0:T(8,128)(2,1)S(1)} collective-permute-done((bf16[32,4096]{1,0:T(8,128)(2,1)S(1)}, bf16[32,4096]{1,0:T(8,128)(2,1)S(1)}, u32[]{:S(2)}, u32[]{:S(2)}) %collective-permute-start.8) | collective-permute-done | bytes 262176 | tf_op jit(solution)/shard_map/ppermute | solution.py:58
  39.3 6.3 %shard_map.82.early = f32[128,1024]{1,0:T(8,128)S(1)} custom-call(f32[2]{0:T(128)S(1)} %copy-done.1, s32[1]{0:T(128)S(6)} %copy.16.layer_ref, bf16[1024,4096]{1,0:T(8,128)(2,1)} %bitcast.40, bf16[32,4096]{1,0:T(8,128)(2,1)S(1)} %get-tuple-element.14.refs_0_, bf16[32,4096]{1,0:T(8,128)(2,1)S(1)} %get-tuple-element.13.refs_1_, ...), custom_call_target="tpu_custom_call" | custom-call | flops 1073741824 | bytes 8388608 | tf_op jit(solution)/shard_map/pallas_call | solution.py:111
  45.6 6.3 %shard_map.83 = (bf16[128,1024]{1,0:T(8,128)(2,1)S(1)}, f32[128,1024]{1,0:T(8,128)S(1)}) custom-call(f32[2]{0:T(128)S(1)} %copy-done.1, s32[1]{0:T(128)S(6)} %copy.16.layer_ref, bf16[1024,4096]{1,0:T(8,128)(2,1)} %bitcast.41, f32[128,1024]{1,0:T(8,128)S(1)} %shard_map.82.early, bf16[32,4096]{1,0:T(8,128)(2,1)S(1)} %collective-permute-done.1.refs_0_, ...), custom_call_target="tpu_custom_call" | custom-call | flops 1073741824 | bytes 8388608 | tf_op jit(solution)/shard_map/pallas_call | solution.py:111
  51.9 1.6 %collective-permute-start.10 = (bf16[128,1024]{1,0:T(8,128)(2,1)S(1)}, bf16[128,1024]{1,0:T(8,128)(2,1)S(1)}, u32[]{:S(2)}, u32[]{:S(2)}) collective-permute-start(bf16[128,1024]{1,0:T(8,128)(2,1)S(1)} %get-tuple-element.11), channel_id=1, source_target_pairs={{0,1},{1,0},{2,3},{3,2},{4,5},{5,4},{6,7},{7,6},{8,9},{9,8},{10,11... | collective-permute-start | bytes 786440 | tf_op jit(solution)/shard_map/ppermute | solution.py:58
  53.5 6.3 %shard_map.84.early = f32[128,1024]{1,0:T(8,128)S(1)} custom-call(f32[2]{0:T(128)S(1)} %copy-done.1, s32[1]{0:T(128)S(6)} %copy.16.layer_ref, bf16[1024,4096]{1,0:T(8,128)(2,1)} %bitcast.42, bf16[32,4096]{1,0:T(8,128)(2,1)S(1)} %collective-permute-done.4.refs_0_, bf16[32,4096]{1,0:T(8,128)(2,1)S(1)} %collective-permute-done.5.refs_1_, ...), custom_call_target="tpu_custom_call" | custom-call | flops 1073741824 | bytes 8388608 | tf_op jit(solution)/shard_map/pallas_call | solution.py:111
  59.8 6.3 %shard_map.85 = (bf16[128,1024]{1,0:T(8,128)(2,1)S(1)}, f32[128,1024]{1,0:T(8,128)S(1)}) custom-call(f32[2]{0:T(128)S(1)} %copy-done.1, s32[1]{0:T(128)S(6)} %copy.16.layer_ref, bf16[1024,4096]{1,0:T(8,128)(2,1)} %bitcast.43, f32[128,1024]{1,0:T(8,128)S(1)} %shard_map.84.early, bf16[32,4096]{1,0:T(8,128)(2,1)S(1)} %collective-permute-done.7.refs_0_, ...), custom_call_target="tpu_custom_call" | custom-call | flops 1073741824 | bytes 8388608 | tf_op jit(solution)/shard_map/pallas_call | solution.py:111
  66.1 0.6 collective-permute-start.11
  66.7 0.1 copy.13.query_ids
  66.8 7.8 %collective-permute-done.11.got1 = bf16[128,1024]{1,0:T(8,128)(2,1)S(1)} collective-permute-done((bf16[128,1024]{1,0:T(8,128)(2,1)S(1)}, bf16[128,1024]{1,0:T(8,128)(2,1)S(1)}, u32[]{:S(2)}, u32[]{:S(2)}) %collective-permute-start.11) | collective-permute-done | bytes 262176 | tf_op jit(solution)/shard_map/ppermute | solution.py:58
  74.6 1.1 %shard_map.86 = f32[256,1024]{1,0:T(8,128)} custom-call(s32[1,1024]{1,0:T(1,128)S(1)} %bitcast.39, s32[256,1]{1,0:T(8,128)S(1)} %copy.13.query_ids, f32[128,1024]{1,0:T(8,128)S(1)} %get-tuple-element.9.keep0, f32[128,1024]{1,0:T(8,128)S(1)} %get-tuple-element.10.keep1, bf16[128,1024]{1,0:T(8,128)(2,1)S(1)} %collective-permute-done.10.got0, ...), custom_call_target="tpu_custom_call" | custom-call | tf_op jit(solution)/shard_map/pallas_call | solution.py:178
  (25 shorter events, 0.4 us)
Async XLA Ops:
  0.0 2.1 %copy-start = (f32[1,64,64]{2,1,0:T(8,128)S(1)}, f32[1,64,64]{2,1,0:T(8,128)}, u32[]{:S(2)}) copy-start(f32[1,64,64]{2,1,0:T(8,128)} %param.10) | copy-start | bytes 49156
  0.0 3.3 %copy-start.3 = (f32[1,64,64]{2,1,0:T(8,128)S(1)}, f32[1,64,64]{2,1,0:T(8,128)}, u32[]{:S(2)}) copy-start(f32[1,64,64]{2,1,0:T(8,128)} %param.11) | copy-start | bytes 49156
  7.7 9.8 %collective-permute-start.4 = (bf16[32,4096]{1,0:T(8,128)(2,1)S(1)}, bf16[32,4096]{1,0:T(8,128)(2,1)S(1)}, u32[]{:S(2)}, u32[]{:S(2)}) collective-permute-start(bf16[32,4096]{1,0:T(8,128)(2,1)S(1)} %get-tuple-element.14.refs_0_), channel_id=1, source_target_pairs={{0,4},{1,5},{2,6},{3,7},{4,0},{5,1},{6,2},{7,3},{8,12},{9,13},{10,... | collective-permute-start | bytes 786440 | tf_op jit(solution)/shard_map/ppermute | solution.py:58
  10.8 14.2 %collective-permute-start.1 = (bf16[32,4096]{1,0:T(8,128)(2,1)S(1)}, bf16[32,4096]{1,0:T(8,128)(2,1)S(1)}, u32[]{:S(2)}, u32[]{:S(2)}) collective-permute-start(bf16[32,4096]{1,0:T(8,128)(2,1)S(1)} %get-tuple-element.14.refs_0_), channel_id=1, source_target_pairs={{0,12},{1,13},{2,14},{3,15},{4,8},{5,9},{6,10},{7,11},{8,4},{9,5},... | collective-permute-start | bytes 786440 | tf_op jit(solution)/shard_map/ppermute | solution.py:58
  17.6 9.6 %collective-permute-start.5 = (bf16[32,4096]{1,0:T(8,128)(2,1)S(1)}, bf16[32,4096]{1,0:T(8,128)(2,1)S(1)}, u32[]{:S(2)}, u32[]{:S(2)}) collective-permute-start(bf16[32,4096]{1,0:T(8,128)(2,1)S(1)} %collective-permute-done.4.refs_0_), channel_id=1, source_target_pairs={{0,16},{1,17},{2,18},{3,19},{4,20},{5,21},{6,22},{7,23},{8,24},{9,... | collective-permute-start | bytes 786440 | tf_op jit(solution)/shard_map/ppermute | solution.py:58
  19.1 20.3 %copy-start.1 = (f32[2]{0:T(128)S(1)}, f32[2]{0:T(128)}, u32[]{:S(2)}) copy-start(f32[2]{0:T(128)} %weight_ref.7) | copy-start | bytes 28
  19.1 20.2 %collective-permute-start = (bf16[64,4096]{1,0:T(8,128)(2,1)S(1)}, bf16[64,4096]{1,0:T(8,128)(2,1)S(1)}, u32[]{:S(2)}, u32[]{:S(2)}) collective-permute-start(bf16[64,4096]{1,0:T(8,128)(2,1)S(1)} %pad_maximum_fusion), channel_id=1, source_target_pairs={{0,2},{1,3},{2,0},{3,1},{4,6},{5,7},{6,4},{7,5},{8,10},{9,11},{10,... | collective-permute-start | bytes 1572872 | tf_op jit(solution)/shard_map/ppermute | solution.py:58
  25.1 7.1 %collective-permute-start.7 = (bf16[32,4096]{1,0:T(8,128)(2,1)S(1)}, bf16[32,4096]{1,0:T(8,128)(2,1)S(1)}, u32[]{:S(2)}, u32[]{:S(2)}) collective-permute-start(bf16[32,4096]{1,0:T(8,128)(2,1)S(1)} %collective-permute-done.1.refs_0_), channel_id=1, source_target_pairs={{0,4},{1,5},{2,6},{3,7},{4,0},{5,1},{6,2},{7,3},{8,12},{9,13},{10,... | collective-permute-start | bytes 786440 | tf_op jit(solution)/shard_map/ppermute | solution.py:58
  25.6 8.0 %collective-permute-start.2 = (bf16[32,4096]{1,0:T(8,128)(2,1)S(1)}, bf16[32,4096]{1,0:T(8,128)(2,1)S(1)}, u32[]{:S(2)}, u32[]{:S(2)}) collective-permute-start(bf16[32,4096]{1,0:T(8,128)(2,1)S(1)} %collective-permute-done.1.refs_0_), channel_id=1, source_target_pairs={{0,16},{1,17},{2,18},{3,19},{4,20},{5,21},{6,22},{7,23},{8,24},{9,... | collective-permute-start | bytes 786440 | tf_op jit(solution)/shard_map/ppermute | solution.py:58
  27.2 26.3 %collective-permute-start.6 = (bf16[64,4096]{1,0:T(8,128)(2,1)S(1)}, bf16[64,4096]{1,0:T(8,128)(2,1)S(1)}, u32[]{:S(2)}, u32[]{:S(2)}) collective-permute-start(bf16[64,4096]{1,0:T(8,128)(2,1)S(1)} %pad_maximum_fusion.2), channel_id=1, source_target_pairs={{0,2},{1,3},{2,0},{3,1},{4,6},{5,7},{6,4},{7,5},{8,10},{9,11},{10,... | collective-permute-start | bytes 1572872 | tf_op jit(solution)/shard_map/ppermute | solution.py:58
  32.2 6.4 %collective-permute-start.8 = (bf16[32,4096]{1,0:T(8,128)(2,1)S(1)}, bf16[32,4096]{1,0:T(8,128)(2,1)S(1)}, u32[]{:S(2)}, u32[]{:S(2)}) collective-permute-start(bf16[32,4096]{1,0:T(8,128)(2,1)S(1)} %collective-permute-done.7.refs_0_), channel_id=1, source_target_pairs={{0,16},{1,17},{2,18},{3,19},{4,20},{5,21},{6,22},{7,23},{8,24},{9,... | collective-permute-start | bytes 786440 | tf_op jit(solution)/shard_map/ppermute | solution.py:58
  33.7 11.9 %collective-permute-start.3 = (bf16[64,4096]{1,0:T(8,128)(2,1)S(1)}, bf16[64,4096]{1,0:T(8,128)(2,1)S(1)}, u32[]{:S(2)}, u32[]{:S(2)}) collective-permute-start(bf16[64,4096]{1,0:T(8,128)(2,1)S(1)} %pad_maximum_fusion.1), channel_id=1, source_target_pairs={{0,2},{1,3},{2,0},{3,1},{4,6},{5,7},{6,4},{7,5},{8,10},{9,11},{10,... | collective-permute-start | bytes 1572872 | tf_op jit(solution)/shard_map/ppermute | solution.py:58
  38.6 21.2 %collective-permute-start.9 = (bf16[64,4096]{1,0:T(8,128)(2,1)S(1)}, bf16[64,4096]{1,0:T(8,128)(2,1)S(1)}, u32[]{:S(2)}, u32[]{:S(2)}) collective-permute-start(bf16[64,4096]{1,0:T(8,128)(2,1)S(1)} %pad_maximum_fusion.3), channel_id=1, source_target_pairs={{0,2},{1,3},{2,0},{3,1},{4,6},{5,7},{6,4},{7,5},{8,10},{9,11},{10,... | collective-permute-start | bytes 1572872 | tf_op jit(solution)/shard_map/ppermute | solution.py:58
  51.9 14.9 %collective-permute-start.10 = (bf16[128,1024]{1,0:T(8,128)(2,1)S(1)}, bf16[128,1024]{1,0:T(8,128)(2,1)S(1)}, u32[]{:S(2)}, u32[]{:S(2)}) collective-permute-start(bf16[128,1024]{1,0:T(8,128)(2,1)S(1)} %get-tuple-element.11), channel_id=1, source_target_pairs={{0,1},{1,0},{2,3},{3,2},{4,5},{5,4},{6,7},{7,6},{8,9},{9,8},{10,11... | collective-permute-start | bytes 786440 | tf_op jit(solution)/shard_map/ppermute | solution.py:58
  59.8 6.9 %copy-start.4 = (s32[256]{0:T(256)S(1)}, s32[256]{0:T(256)}, u32[]{:S(2)}) copy-start(s32[256]{0:T(256)} %param.15) | copy-start | bytes 3076
  59.8 14.8 %copy-start.2 = (s32[1024]{0:T(1024)S(1)}, s32[1024]{0:T(1024)}, u32[]{:S(2)}) copy-start(s32[1024]{0:T(1024)} %param.14) | copy-start | bytes 12292
  66.1 8.5 %collective-permute-start.11 = (bf16[128,1024]{1,0:T(8,128)(2,1)S(1)}, bf16[128,1024]{1,0:T(8,128)(2,1)S(1)}, u32[]{:S(2)}, u32[]{:S(2)}) collective-permute-start(bf16[128,1024]{1,0:T(8,128)(2,1)S(1)} %get-tuple-element.12), channel_id=1, source_target_pairs={{0,1},{1,0},{2,3},{3,2},{4,5},{5,4},{6,7},{7,6},{8,9},{9,8},{10,11... | collective-permute-start | bytes 786440 | tf_op jit(solution)/shard_map/ppermute | solution.py:58

commit v2 on v1

v2 whole, which is shorter than its diff:
```python
import functools

import jax
import jax.numpy as jnp
from jax import lax
from jax.experimental import pallas as pl
from jax.experimental.pallas import tpu as pltpu
from jax.sharding import PartitionSpec as P

AXES = ("parts", "store", "layer")
VMEM = pl.BlockSpec(memory_space=pltpu.VMEM)
SMEM = pl.BlockSpec(memory_space=pltpu.SMEM)
bf16, f32 = jnp.bfloat16, jnp.float32
LIMIT = 20 * 1024 * 1024


def preconditioned(query_grads, left_factor, right_factor):
    q_rows, slots, width = query_grads.shape
    side = left_factor.shape[1]
    mats = query_grads.astype(jnp.float32).reshape(q_rows, slots, side, side)
    half = jnp.einsum("lij,qljk->qlik", left_factor, mats, precision=lax.Precision.HIGHEST)
    full = jnp.einsum("qlik,lkm->qlim", half, right_factor, precision=lax.Precision.HIGHEST)
    return full.reshape(q_rows, slots, width).astype(jnp.bfloat16)


def general(
    train_grads,
    query_grads,
    left_factor,
    right_factor,
    layer_weight,
    layer_of,
    train_ids,
    query_ids,
):
    precond = preconditioned(query_grads, left_factor, right_factor)
    weight = jnp.take(layer_weight, layer_of[0])
    queries = lax.all_gather(precond, "store", axis=0, tiled=True)
    terms = weight * jnp.dot(
        queries[:, 0, :], train_grads[:, 0, :].T, preferred_element_type=jnp.float32
    )
    summed = lax.psum_scatter(terms, "layer", scatter_dimension=0, tiled=True)
    same = query_ids[:, None] == train_ids[None, :]
    return jnp.where(same, jnp.float32(0.0), summed)


PARTS, CHIPS, CORES, LAYERS = 2, 4, 2, 2
CHUNK = 16
COST = 0


def permute(value, name, target):
    pairs = []
    for p in range(PARTS):
        for z in range(CHIPS):
            for c in range(CORES):
                for l in range(LAYERS):
                    tp, tz, tc, tl = target(p, z, c, l)
                    source = ((p * CHIPS + z) * CORES + c) * LAYERS + l
                    pairs.append((source, ((tp * CHIPS + tz) * CORES + tc) * LAYERS + tl))
    with jax.named_scope(name):
        return lax.ppermute(value, AXES, pairs)


to_part = functools.partial(permute, target=lambda p, z, c, l: (1 - p, z, c, l))
to_core = functools.partial(permute, target=lambda p, z, c, l: (p, z, 1 - c, l))
to_layer = functools.partial(permute, target=lambda p, z, c, l: (p, z, c, 1 - l))
to_near = functools.partial(permute, target=lambda p, z, c, l: (p, z ^ 1, c, l))
to_far = functools.partial(permute, target=lambda p, z, c, l: (p, z ^ 3, c, l))


def after(value, *others):
    return lax.optimization_barrier((value, *others))[0]


def place():
    store = lax.axis_index("store")
    return lax.axis_index("parts"), store // CORES, store % CORES, lax.axis_index("layer")


def split(x, terms):
    out = []
    for _ in range(terms):
        term = x.astype(bf16)
        out.append(term)
        x = x - term.astype(f32)
    return out


def dot(a, b):
    return lax.dot_general(a, b, (((1,), (0,)), ((), ())), preferred_element_type=f32)


def iota(shape, dim):
    return lax.broadcasted_iota(jnp.int32, shape, dim)


def factors(left, right):
    r, c = iota((256, 64), 0), iota((256, 64), 1)
    pick = jnp.where(c == 4 * (r % 16) + (r // 16) % 4, 1.0, 0.0).astype(bf16)
    r, c = iota((64, 256), 0), iota((64, 256), 1)
    pick_t = jnp.where(r == 4 * (c % 16) + (c // 16) % 4, 1.0, 0.0).astype(bf16)
    block = iota((256, 256), 0) // 64 == iota((256, 256), 1) // 64
    lefts = [
        jnp.where(block, dot(dot(pick, term).astype(bf16), pick_t), 0.0).astype(bf16)
        for term in split(left, 2)
    ]
    row = jnp.concatenate([right, right], axis=1)
    tiled = jnp.concatenate([jnp.concatenate([row] * 4, axis=1)] * 4, axis=0)
    block = iota((256, 512), 0) // 64 == iota((256, 512), 1) // 128
    return lefts, split(jnp.where(block, tiled, 0.0), 2)


def precond_chunk(q, lefts, rights, write):
    tiles = q.shape[1] // 256
    r, c = iota((256, 256), 0), iota((256, 256), 1)
    swap = jnp.where((r // 16 == c % 16) & (r % 16 == c // 16), 1.0, 0.0).astype(bf16)
    x = jnp.concatenate([q[:, t * 256 : (t + 1) * 256] for t in range(tiles)], axis=0)
    x = dot(swap, x).astype(bf16)
    z = dot(x, rights[0]) + dot(x, rights[1])
    sets = []
    for first in range(0, 16, 4):
        rows = [
            z[query * 16 : (query + 1) * 16, s * 128 : (s + 1) * 128]
            for query in range(first, first + 4)
            for s in range(4)
        ]
        sets.append(jnp.concatenate(rows, axis=0))
    high, low = split(jnp.concatenate(sets, axis=1), 2)
    z = dot(lefts[0], high) + (dot(lefts[0], low) + dot(lefts[1], high))
    side = iota((16, 128), 1) < 64
    rows = []
    for first in range(4):
        for k in range(4):
            o = z[k * 64 : (k + 1) * 64, first * 128 : (first + 1) * 128]
            pair = [jnp.where(side, o[0:16], o[16:32]), jnp.where(side, o[32:48], o[48:64])]
            rows.append(jnp.concatenate(pair, axis=1))
    y = dot(swap, jnp.concatenate(rows, axis=0).astype(bf16)).astype(bf16)
    for t in range(tiles):
        write(t, y[t * 16 : (t + 1) * 16])


def own_kernel(q_ref, left_ref, right_ref, mine, chunk0, chunk1, lefts_ref, rights_ref):
    lefts, rights = factors(left_ref[...], right_ref[...])
    for k in range(2):
        lefts_ref[k] = lefts[k]
        rights_ref[k] = rights[k]
    start = lax.axis_index("parts") * (2 * CHUNK)
    for k, chunk in enumerate((chunk0, chunk1)):

        def write(t, value):
            mine[k * CHUNK : (k + 1) * CHUNK, t * 256 : (t + 1) * 256] = value
            chunk[:, t * 256 : (t + 1) * 256] = value

        at = pl.multiple_of(start + k * CHUNK, CHUNK)
        precond_chunk(q_ref[pl.ds(at, CHUNK), :], lefts, rights, write)


def rest_kernel(q_ref, mine, lefts_ref, rights_ref, own):
    lefts, rights = [lefts_ref[0], lefts_ref[1]], [rights_ref[0], rights_ref[1]]
    own[: 2 * CHUNK, :] = mine[...]
    start = (1 - lax.axis_index("parts")) * (2 * CHUNK)
    for k in range(2):

        def write(t, value):
            own[(2 + k) * CHUNK : (3 + k) * CHUNK, t * 256 : (t + 1) * 256] = value

        at = pl.multiple_of(start + k * CHUNK, CHUNK)
        precond_chunk(q_ref[pl.ds(at, CHUNK), :], lefts, rights, write)


def score_kernel(weight_ref, layer_ref, train_ref, *refs, picks, stored, early, add):
    inputs, refs = refs[: len(picks)], refs[len(picks) :]
    n_before = sum(taken for _, _, taken in early)
    before, refs = refs[:n_before], refs[n_before:]
    adds, outs = (refs[:2], refs[2:]) if add else ((), refs)
    if add:
        outs[-1][...] = adds[0][...] + adds[1][...].astype(f32)
        outs = outs[:-1]
    weight = weight_ref[layer_ref[0]]
    queries = jnp.concatenate(
        [piece[at : at + CHUNK, :] for piece, rows in zip(inputs, picks) for at in rows], axis=0
    )
    _, z, _, layer = place()
    near_is_mine = z // 2 == layer
    n, step = train_ref.shape[0], 256
    for at in range(0, n, step):
        here = slice(at, at + step)
        value = lax.dot_general(
            train_ref[here, :], queries, (((1,), (1,)), ((), ())), preferred_element_type=f32
        )
        value = weight * value.T
        if stored:
            outs[0][:, here] = value[:stored]
        if early:
            send, keep = outs[-2:]
            old, given = [], list(before)
            for first, rows, taken in early:
                old.append(
                    given.pop(0)[first : first + rows, here] if taken else value[first : first + rows]
                )
            old, new = jnp.concatenate(old, axis=0), value[stored:]
            send[:, here] = jnp.where(near_is_mine, new, old).astype(send.dtype)
            keep[:, here] = jnp.where(near_is_mine, old, new)


def call_scores(weight, layer, train, inputs, stored=0, early=(), add=()):
    n = train.shape[0]
    total = CHUNK * sum(len(rows) for _, rows in inputs)
    outs = [jax.ShapeDtypeStruct((stored, n), f32)] if stored else []
    if early:
        outs += [jax.ShapeDtypeStruct((total - stored, n), t) for t in (bf16, f32)]
    if add:
        outs += [jax.ShapeDtypeStruct(add[0].shape, f32)]
    inputs_early = [a for a, _, _ in early if a is not None]
    return pl.pallas_call(
        functools.partial(
            score_kernel,
            picks=[rows for _, rows in inputs],
            stored=stored,
            early=[(first, rows, a is not None) for a, first, rows in early],
            add=bool(add),
        ),
        out_shape=outs,
        in_specs=[SMEM, SMEM] + [VMEM] * (1 + len(inputs) + len(inputs_early) + len(add)),
        out_specs=[VMEM] * len(outs),
        compiler_params=pltpu.CompilerParams(vmem_limit_bytes=LIMIT),
        cost_estimate=pl.CostEstimate(flops=COST, bytes_accessed=0, transcendentals=0),
    )(weight, layer, train, *[a for a, _ in inputs], *inputs_early, *add)


def final_kernel(train_ids, query_ids, sum1, keep2, got2, keep3, got3, out):
    part, z, core, layer = place()
    near_is_mine = z // 2 == layer
    low = z % 2
    first = jnp.where(near_is_mine, low, 1 - low)
    ids = train_ids[...]
    groups = (
        (0, 0, 0, (sum1,)),
        (0, 1, 0, (keep2, got2)),
        (1, 0, 64, (keep2, got2)),
        (1, 1, 0, (keep3, got3)),
    )
    for block, chunk, base, terms in groups:
        block = first if block == 0 else 1 - first
        for i in range(4):
            c = core if i < 2 else 1 - core
            h = part if i % 2 == 0 else 1 - part
            at = pl.multiple_of((((block * 2 + c) * 2 + h) * 2 + chunk) * CHUNK, CHUNK)
            here = slice(base + i * CHUNK, base + (i + 1) * CHUNK)
            total = terms[0][here, :]
            for term in terms[1:]:
                total = total + term[here, :].astype(f32)
            same = query_ids[pl.ds(at, CHUNK), :] == ids
            out[pl.ds(at, CHUNK), :] = jnp.where(same, jnp.float32(0.0), total)


def kernel_call(kernel, outs, inputs, flops=0):
    return pl.pallas_call(
        kernel,
        out_shape=outs,
        in_specs=[VMEM] * len(inputs),
        out_specs=[VMEM] * len(outs) if isinstance(outs, list) else VMEM,
        compiler_params=pltpu.CompilerParams(vmem_limit_bytes=LIMIT),
        cost_estimate=pl.CostEstimate(flops=flops, bytes_accessed=0, transcendentals=0),
    )(*inputs)


def small(
    train_grads,
    query_grads,
    left_factor,
    right_factor,
    layer_weight,
    layer_of,
    train_ids,
    query_ids,
):
    train, queries = train_grads[:, 0, :], query_grads[:, 0, :]
    width = queries.shape[1]
    shape = jax.ShapeDtypeStruct
    mine, mine_a, mine_b, lefts, rights = kernel_call(
        own_kernel,
        [shape((rows, width), bf16) for rows in (2 * CHUNK, CHUNK, CHUNK)]
        + [shape((2, 256, 256), bf16), shape((2, 256, 512), bf16)],
        [queries, left_factor[0], right_factor[0]],
    )
    far_a = to_far(mine_a, "far_a")
    far_b = to_far(mine_b, "far_b")
    near = to_near(mine, "near")
    (own,) = kernel_call(
        rest_kernel,
        [shape((4 * CHUNK, width), bf16)],
        [queries, mine, lefts, rights],
        flops=COST,
    )
    join = lambda *pieces: jnp.concatenate(pieces, axis=0)
    score = functools.partial(call_scores, layer_weight, layer_of, train)
    both = ((0, 32), (16, 48))
    pieces = lambda own_half, other_half, other_core: [
        (own_half, (0,)), (other_half, (0,)), (other_core, (0, 16))
    ]

    own_x = to_core(own, "own_x")
    far_a = after(far_a, own)
    far_pa = to_part(far_a, "far_pa")
    cross_a = to_near(far_a, "cross_a")
    own_x = after(own_x, far_a)
    (early0,) = score(
        [(own, both[0]), (own_x, both[0]), (own, both[1]), (own_x, both[1])], stored=128
    )
    near = after(near, early0)
    near_p = to_part(near, "near_p")
    cross_b = to_near(far_b, "cross_b")
    far_pb = to_part(far_b, "far_pb")
    far_xa = to_core(join(far_a, far_pa), "far_xa")
    near_x = to_core(join(near, near_p), "near_x")
    far_xa = after(far_xa, far_b)
    send1, keep1 = score(pieces(far_a, far_pa, far_xa), early=[(early0, 0, 64)])
    got1 = to_layer(send1, "got1")
    far_xb = to_core(join(far_b, far_pb), "far_xb")
    cross_pa = to_part(cross_a, "cross_pa")
    cross_xa = to_core(join(cross_a, cross_pa), "cross_xa")
    cross_xa = after(cross_xa, cross_b)
    cross_b = after(cross_b, send1)
    cross_pb = to_part(cross_b, "cross_pb")
    early1, send2, keep2 = score(
        [(near, (0,)), (near_p, (0,)), (near_x, both[0])]
        + [(near, (16,)), (near_p, (16,)), (near_x, both[1])]
        + pieces(far_b, far_pb, far_xb)
        + pieces(cross_a, cross_pa, cross_xa),
        stored=128,
        early=[(early0, 64, 64), (None, 0, 64)],
    )
    got2 = to_layer(send2, "got2")
    cross_xb = to_core(join(cross_b, after(cross_pb, send2)), "cross_xb")
    send3, keep3, sum1 = score(
        pieces(cross_b, cross_pb, cross_xb), early=[(early1, 64, 64)], add=(keep1, got1)
    )
    got3 = to_layer(send3, "got3")
    return kernel_call(
        final_kernel,
        shape((query_ids.shape[0], train_ids.shape[0]), f32),
        [train_ids[None, :], query_ids[:, None], sum1, keep2, got2, keep3, got3],
    )


def solution(mesh):
    placed = (
        P(("parts", "store"), "layer", None),
        P("store", "layer", None),
        P("layer", None, None),
        P("layer", None, None),
        P(),
        P("layer"),
        P(("parts", "store")),
        P("layer"),
    )
    sizes = tuple(mesh.shape[axis] for axis in AXES)
    return jax.shard_map(
        small if sizes == (PARTS, CHIPS * CORES, LAYERS) else general,
        mesh=mesh,
        in_specs=placed,
        out_specs=P("layer", ("parts", "store")),
        check_vma=False,
    )
```

time: 77.2 us -> 66.8 us (0.87); the launches traced: 75.8 us -> 66.5 us
  starting transfers between devices: 13.1 us -> 23.1 us
  Pallas kernels: 26.3 us -> 16.6 us
  waiting for transfers between devices: 27.6 us -> 19.1 us
  matrix products: 4.76 us -> 0 us
  local copies, waits for them, and re-layouts: 3.07 us -> 6.74 us
    ppermute x12 -> x19, starting transfers between devices: 13.1 us -> 23.1 us  [permute(): return lax.ppermute(value, AXES, pairs)]
    pallas_call x5 -> x7, Pallas kernels: 26.3 us -> 16.6 us  [the longest x4 11.9 us: call_scores(): pl.pallas_call(functools.partial(score_kernel, picks=[rows for _, rows in...]
    ppermute x12 -> x19, waiting for transfers between devices: 27.6 us -> 19.1 us  [permute(): return lax.ppermute(value, AXES, pairs)]
    unnamed x10 -> x16, local copies, waits for them, and re-layouts: 0.02 us -> 6.6 us
    dot_general x2 -> x0, matrix products: 4.76 us -> none  [the longest x1 3.53 us: preconditioned(): jnp.einsum('qlik,lkm->qlim', half, right_factor, precision=lax.Precision....]
    reshape x1 -> x0, local copies, waits for them, and re-layouts: 2.06 us -> none
    convert_element_type x1 -> x0, local copies, waits for them, and re-layouts: 0.81 us -> none  [preconditioned(): return full.reshape(q_rows, slots, width).astype(jnp.bfloat16)]
  transfers between devices with their start and end apart: 12 -> 19, of which waited for: 5 -> 6; matrix products, arithmetic and copies ran while one was open for 0% -> 0% of each run, Pallas kernels for 33% -> 20%
where the time goes in v2:
time: 66.8 us; the launch traced here: 66.5 us
  starting transfers between devices  23.1 us (35%)
  waiting for transfers between devices  19.1 us (29%)
  Pallas kernels  16.6 us (25%)
  local copies, waits for them, and re-layouts  6.74 us (10%)
  between operations  0.84 us (1%)
    ppermute x19, starting transfers between devices, permute(): return lax.ppermute(value, AXES, pairs)  23.1 us
    ppermute x19, waiting for transfers between devices, permute(): return lax.ppermute(value, AXES, pairs)  19.1 us
    pallas_call x4, Pallas kernels, call_scores(): pl.pallas_call(functools.partial(score_kernel, picks=[rows for _, rows in...  11.9 us
    unnamed x16, local copies, waits for them, and re-layouts  6.6 us
    pallas_call x3, Pallas kernels, kernel_call(): pl.pallas_call(kernel, out_shape=outs, in_specs=[VMEM] * len(inputs), out...  4.67 us
  transfers between devices with their start and end apart: 19, of which 6 were waited for; matrix products, arithmetic and copies ran while one was open for 0% of the time, Pallas kernels for 20%

profile of v2, /device:TPU:0, one launch (start us, length us, event | category | flops | bytes accessed | tf_op | source)
XLA Modules:
  0.0 66.5 jit_solution(7621722552099388593)
XLA Ops:
  0.0 1.0 %copy-done.2 = bf16[64,1,4096]{2,0,1:T(8,128)(2,1)S(1)} copy-done((bf16[64,1,4096]{2,0,1:T(8,128)(2,1)S(1)}, bf16[64,1,4096]{2,0,1:T(8,128)(2,1)}, u32[]{:S(2)}) %copy-start.2) | copy-done | bytes 524312
  1.0 0.8 %copy-done.3 = f32[1,64,64]{2,1,0:T(8,128)S(1)} copy-done((f32[1,64,64]{2,1,0:T(8,128)S(1)}, f32[1,64,64]{2,1,0:T(8,128)}, u32[]{:S(2)}) %copy-start.3) | copy-done | bytes 16408
  1.8 0.8 %copy-done.4 = f32[1,64,64]{2,1,0:T(8,128)S(1)} copy-done((f32[1,64,64]{2,1,0:T(8,128)S(1)}, f32[1,64,64]{2,1,0:T(8,128)}, u32[]{:S(2)}) %copy-start.4) | copy-done | bytes 16408
  2.6 1.9 %shard_map.82 = (bf16[32,4096]{1,0:T(8,128)(2,1)S(1)}, bf16[16,4096]{1,0:T(8,128)(2,1)S(1)}, bf16[16,4096]{1,0:T(8,128)(2,1)S(1)}, bf16[2,256,256]{2,1,0:T(8,128)(2,1)S(1)}, bf16[2,256,512]{2,1,0:T(8,128)(2,1)S(1)}) custom-call(bf16[64,4096]{1,0:T(8,128)(2,1)S(1)} %bitcast.10, f32[64,64]{1,0:T(8,128)S(1)} %bitcast.12, f32[64,64]{1,0:T(8,128)S(1)} %bitcast.13), custom_call_target="tpu_custom_call" | custom-call | tf_op jit(solution)/shard_map/pallas_call | solution.py:259
  4.4 5.1 %collective-permute-start.2 = (bf16[16,4096]{1,0:T(8,128)(2,1)S(1)}, bf16[16,4096]{1,0:T(8,128)(2,1)S(1)}, u32[]{:S(2)}, u32[]{:S(2)}) collective-permute-start(bf16[16,4096]{1,0:T(8,128)(2,1)S(1)} %get-tuple-element.26), channel_id=1, source_target_pairs={{0,12},{1,13},{2,14},{3,15},{4,8},{5,9},{6,10},{7,11},{8,4},{9,5},... | collective-permute-start | bytes 393224 | tf_op jit(solution)/shard_map/far_a/ppermute | solution.py:62
  9.6 1.7 %shard_map.83.refs_0_.refs_2_ = bf16[64,4096]{1,0:T(8,128)(2,1)S(1)} custom-call(bf16[64,4096]{1,0:T(8,128)(2,1)S(1)} %bitcast.11, bf16[32,4096]{1,0:T(8,128)(2,1)S(1)} %get-tuple-element.27.mine, bf16[2,256,256]{2,1,0:T(8,128)(2,1)S(1)} %get-tuple-element.28.lefts_ref, bf16[2,256,512]{2,1,0:T(8,128)(2,1)S(1)} %get-tuple-element.29.rights_ref), custom_call_target="tpu_custom_call" | custom-call | tf_op jit(solution)/shard_map/pallas_call | solution.py:259
  11.3 2.1 %collective-permute-done.2.refs_0_ = bf16[16,4096]{1,0:T(8,128)(2,1)S(1)} collective-permute-done((bf16[16,4096]{1,0:T(8,128)(2,1)S(1)}, bf16[16,4096]{1,0:T(8,128)(2,1)S(1)}, u32[]{:S(2)}, u32[]{:S(2)}) %collective-permute-start.2) | collective-permute-done | bytes 131104 | tf_op jit(solution)/shard_map/far_a/ppermute | solution.py:62
  13.4 5.9 %collective-permute-start.12 = (bf16[16,4096]{1,0:T(8,128)(2,1)S(1)}, bf16[16,4096]{1,0:T(8,128)(2,1)S(1)}, u32[]{:S(2)}, u32[]{:S(2)}) collective-permute-start(bf16[16,4096]{1,0:T(8,128)(2,1)S(1)} %collective-permute-done.2.refs_0_), channel_id=1, source_target_pairs={{0,4},{1,5},{2,6},{3,7},{4,0},{5,1},{6,2},{7,3},{8,12},{9,13},{10,... | collective-permute-start | bytes 393224 | tf_op jit(solution)/shard_map/cross_a/ppermute | solution.py:62
  19.3 1.5 %collective-permute-start.3 = (bf16[16,4096]{1,0:T(8,128)(2,1)S(1)}, bf16[16,4096]{1,0:T(8,128)(2,1)S(1)}, u32[]{:S(2)}, u32[]{:S(2)}) collective-permute-start(bf16[16,4096]{1,0:T(8,128)(2,1)S(1)} %collective-permute-done.2.refs_0_), channel_id=1, source_target_pairs={{0,16},{1,17},{2,18},{3,19},{4,20},{5,21},{6,22},{7,23},{8,24},{9,... | collective-permute-start | bytes 393224 | tf_op jit(solution)/shard_map/far_pa/ppermute | solution.py:62
  21.5 2.1 %collective-permute-start.1 = (bf16[16,4096]{1,0:T(8,128)(2,1)S(1)}, bf16[16,4096]{1,0:T(8,128)(2,1)S(1)}, u32[]{:S(2)}, u32[]{:S(2)}) collective-permute-start(bf16[16,4096]{1,0:T(8,128)(2,1)S(1)} %collective-permute-done.refs_6_), channel_id=1, source_target_pairs={{0,4},{1,5},{2,6},{3,7},{4,0},{5,1},{6,2},{7,3},{8,12},{9,13},{10,... | collective-permute-start | bytes 393224 | tf_op jit(solution)/shard_map/cross_b/ppermute | solution.py:62
  23.6 0.9 %collective-permute-start.10 = (bf16[16,4096]{1,0:T(8,128)(2,1)S(1)}, bf16[16,4096]{1,0:T(8,128)(2,1)S(1)}, u32[]{:S(2)}, u32[]{:S(2)}) collective-permute-start(bf16[16,4096]{1,0:T(8,128)(2,1)S(1)} %collective-permute-done.refs_6_), channel_id=1, source_target_pairs={{0,16},{1,17},{2,18},{3,19},{4,20},{5,21},{6,22},{7,23},{8,24},{9,... | collective-permute-start | bytes 393224 | tf_op jit(solution)/shard_map/far_pb/ppermute | solution.py:62
  24.4 1.3 %collective-permute-start.13 = (bf16[16,4096]{1,0:T(8,128)(2,1)S(1)}, bf16[16,4096]{1,0:T(8,128)(2,1)S(1)}, u32[]{:S(2)}, u32[]{:S(2)}) collective-permute-start(bf16[16,4096]{1,0:T(8,128)(2,1)S(1)} %collective-permute-done.12.refs_9_), channel_id=1, source_target_pairs={{0,16},{1,17},{2,18},{3,19},{4,20},{5,21},{6,22},{7,23},{8,24},{9,... | collective-permute-start | bytes 393224 | tf_op jit(solution)/shard_map/cross_pa/ppermute | solution.py:62
  25.9 3.4 %copy-done = bf16[1024,1,4096]{2,0,1:T(8,128)(2,1)S(1)} copy-done((bf16[1024,1,4096]{2,0,1:T(8,128)(2,1)S(1)}, bf16[1024,1,4096]{2,0,1:T(8,128)(2,1)}, u32[]{:S(2)}) %copy-start) | copy-done | bytes 8388632
  29.9 3.0 %shard_map.84.refs_3_.refs_12_ = f32[128,1024]{1,0:T(8,128)S(1)} custom-call(f32[2]{0:T(128)S(1)} %copy-done.5, s32[1]{0:T(128)S(6)} %copy.10.layer_ref, bf16[1024,4096]{1,0:T(8,128)(2,1)S(1)} %bitcast.6, bf16[64,4096]{1,0:T(8,128)(2,1)S(1)} %shard_map.83.refs_0_.refs_2_, bf16[64,4096]{1,0:T(8,128)(2,1)S(1)} %collective-permute-done.5.refs_1_.refs_3_, ...), custom_call_target="tpu_custom_call" | custom-call | tf_op jit(solution)/shard_map/pallas_call | solution.py:216
  34.0 7.7 %collective-permute-done.8.refs_1_.refs_4_ = bf16[32,4096]{1,0:T(8,128)(2,1)S(1)} collective-permute-done((bf16[32,4096]{1,0:T(8,128)(2,1)S(1)}, bf16[32,4096]{1,0:T(8,128)(2,1)S(1)}, u32[]{:S(2)}, u32[]{:S(2)}) %collective-permute-start.8) | collective-permute-done | bytes 262176 | tf_op jit(solution)/shard_map/near_p/ppermute | solution.py:62
  42.4 2.9 %shard_map.85 = (bf16[64,1024]{1,0:T(8,128)(2,1)S(1)}, f32[64,1024]{1,0:T(8,128)S(1)}) custom-call(f32[2]{0:T(128)S(1)} %copy-done.5, s32[1]{0:T(128)S(6)} %copy.10.layer_ref, bf16[1024,4096]{1,0:T(8,128)(2,1)S(1)} %bitcast.7, bf16[16,4096]{1,0:T(8,128)(2,1)S(1)} %collective-permute-done.2.refs_0_, bf16[16,4096]{1,0:T(8,128)(2,1)S(1)} %collective-permute-done.3.refs_1_, ...), custom_call_target="tpu_custom_call" | custom-call | tf_op jit(solution)/shard_map/pallas_call | solution.py:216
  46.1 3.1 %shard_map.86 = (f32[128,1024]{1,0:T(8,128)S(1)}, bf16[128,1024]{1,0:T(8,128)(2,1)S(1)}, f32[128,1024]{1,0:T(8,128)S(1)}) custom-call(f32[2]{0:T(128)S(1)} %copy-done.5, s32[1]{0:T(128)S(6)} %copy.10.layer_ref, bf16[1024,4096]{1,0:T(8,128)(2,1)S(1)} %bitcast.8, bf16[32,4096]{1,0:T(8,128)(2,1)S(1)} %collective-permute-done.7.refs_0_.refs_3_, ...), custom_call_target="tpu_custom_call" | custom-call | tf_op jit(solution)/shard_map/pallas_call | solution.py:216
  49.2 1.7 %collective-permute-done.6.refs_1_ = bf16[16,4096]{1,0:T(8,128)(2,1)S(1)} collective-permute-done((bf16[16,4096]{1,0:T(8,128)(2,1)S(1)}, bf16[16,4096]{1,0:T(8,128)(2,1)S(1)}, u32[]{:S(2)}, u32[]{:S(2)}) %collective-permute-start.6) | collective-permute-done | bytes 131104 | tf_op jit(solution)/shard_map/cross_pb/ppermute | solution.py:62
  51.0 1.6 %collective-permute-start.16 = (bf16[64,1024]{1,0:T(8,128)(2,1)S(1)}, bf16[64,1024]{1,0:T(8,128)(2,1)S(1)}, u32[]{:S(2)}, u32[]{:S(2)}) collective-permute-start(bf16[64,1024]{1,0:T(8,128)(2,1)S(1)} %get-tuple-element.33), channel_id=1, source_target_pairs={{0,1},{1,0},{2,3},{3,2},{4,5},{5,4},{6,7},{7,6},{8,9},{9,8},{10,11... | collective-permute-start | bytes 393224 | tf_op jit(solution)/shard_map/got1/ppermute | solution.py:62
  53.1 4.3 %collective-permute-done.16.refs_5_ = bf16[64,1024]{1,0:T(8,128)(2,1)S(1)} collective-permute-done((bf16[64,1024]{1,0:T(8,128)(2,1)S(1)}, bf16[64,1024]{1,0:T(8,128)(2,1)S(1)}, u32[]{:S(2)}, u32[]{:S(2)}) %collective-permute-start.16) | collective-permute-done | bytes 131104 | tf_op jit(solution)/shard_map/got1/ppermute | solution.py:62
  57.3 2.9 %shard_map.87 = (bf16[64,1024]{1,0:T(8,128)(2,1)S(1)}, f32[64,1024]{1,0:T(8,128)S(1)}, f32[64,1024]{1,0:T(8,128)S(1)}) custom-call(f32[2]{0:T(128)S(1)} %copy-done.5, s32[1]{0:T(128)S(6)} %copy.10.layer_ref, bf16[1024,4096]{1,0:T(8,128)(2,1)S(1)} %bitcast.9, bf16[16,4096]{1,0:T(8,128)(2,1)S(1)} %collective-permute-done.1.refs_0_, ...), custom_call_target="tpu_custom_call" | custom-call | tf_op jit(solution)/shard_map/pallas_call | solution.py:216
  60.3 1.6 %collective-permute-start.18 = (bf16[64,1024]{1,0:T(8,128)(2,1)S(1)}, bf16[64,1024]{1,0:T(8,128)(2,1)S(1)}, u32[]{:S(2)}, u32[]{:S(2)}) collective-permute-start(bf16[64,1024]{1,0:T(8,128)(2,1)S(1)} %get-tuple-element.44), channel_id=1, source_target_pairs={{0,1},{1,0},{2,3},{3,2},{4,5},{5,4},{6,7},{7,6},{8,9},{9,8},{10,11... | collective-permute-start | bytes 393224 | tf_op jit(solution)/shard_map/got3/ppermute | solution.py:62
  62.8 2.6 %collective-permute-done.18.got3 = bf16[64,1024]{1,0:T(8,128)(2,1)S(1)} collective-permute-done((bf16[64,1024]{1,0:T(8,128)(2,1)S(1)}, bf16[64,1024]{1,0:T(8,128)(2,1)S(1)}, u32[]{:S(2)}, u32[]{:S(2)}) %collective-permute-start.18) | collective-permute-done | bytes 131104 | tf_op jit(solution)/shard_map/got3/ppermute | solution.py:62
  65.3 1.1 %shard_map.88 = f32[256,1024]{1,0:T(8,128)} custom-call(s32[1,1024]{1,0:T(1,128)S(1)} %bitcast.14, s32[256,1]{1,0:T(8,128)S(1)} %copy.9.query_ids, f32[64,1024]{1,0:T(8,128)S(1)} %get-tuple-element.41.sum1, f32[128,1024]{1,0:T(8,128)S(1)} %get-tuple-element.42.keep2, bf16[128,1024]{1,0:T(8,128)(2,1)S(1)} %collective-permute-done.17.got2, ...), custom_call_target="tpu_custom_call" | custom-call | tf_op jit(solution)/shard_map/pallas_call | solution.py:259
  (43 shorter events, 4.8 us)
Async XLA Ops:
  0.0 1.0 %copy-start.2 = (bf16[64,1,4096]{2,0,1:T(8,128)(2,1)S(1)}, bf16[64,1,4096]{2,0,1:T(8,128)(2,1)}, u32[]{:S(2)}) copy-start(bf16[64,1,4096]{2,0,1:T(8,128)(2,1)} %param.9) | copy-start | bytes 1572868
  4.4 9.0 %collective-permute-start.2 = (bf16[16,4096]{1,0:T(8,128)(2,1)S(1)}, bf16[16,4096]{1,0:T(8,128)(2,1)S(1)}, u32[]{:S(2)}, u32[]{:S(2)}) collective-permute-start(bf16[16,4096]{1,0:T(8,128)(2,1)S(1)} %get-tuple-element.26), channel_id=1, source_target_pairs={{0,12},{1,13},{2,14},{3,15},{4,8},{5,9},{6,10},{7,11},{8,4},{9,5},... | collective-permute-start | bytes 393224 | tf_op jit(solution)/shard_map/far_a/ppermute | solution.py:62
  9.5 11.9 %collective-permute-start = (bf16[16,4096]{1,0:T(8,128)(2,1)S(1)}, bf16[16,4096]{1,0:T(8,128)(2,1)S(1)}, u32[]{:S(2)}, u32[]{:S(2)}) collective-permute-start(bf16[16,4096]{1,0:T(8,128)(2,1)S(1)} %get-tuple-element.25), channel_id=1, source_target_pairs={{0,12},{1,13},{2,14},{3,15},{4,8},{5,9},{6,10},{7,11},{8,4},{9,5},... | collective-permute-start | bytes 393224 | tf_op jit(solution)/shard_map/far_b/ppermute | solution.py:62
  13.4 10.1 %collective-permute-start.12 = (bf16[16,4096]{1,0:T(8,128)(2,1)S(1)}, bf16[16,4096]{1,0:T(8,128)(2,1)S(1)}, u32[]{:S(2)}, u32[]{:S(2)}) collective-permute-start(bf16[16,4096]{1,0:T(8,128)(2,1)S(1)} %collective-permute-done.2.refs_0_), channel_id=1, source_target_pairs={{0,4},{1,5},{2,6},{3,7},{4,0},{5,1},{6,2},{7,3},{8,12},{9,13},{10,... | collective-permute-start | bytes 393224 | tf_op jit(solution)/shard_map/cross_a/ppermute | solution.py:62
  19.3 5.1 %collective-permute-start.3 = (bf16[16,4096]{1,0:T(8,128)(2,1)S(1)}, bf16[16,4096]{1,0:T(8,128)(2,1)S(1)}, u32[]{:S(2)}, u32[]{:S(2)}) collective-permute-start(bf16[16,4096]{1,0:T(8,128)(2,1)S(1)} %collective-permute-done.2.refs_0_), channel_id=1, source_target_pairs={{0,16},{1,17},{2,18},{3,19},{4,20},{5,21},{6,22},{7,23},{8,24},{9,... | collective-permute-start | bytes 393224 | tf_op jit(solution)/shard_map/far_pa/ppermute | solution.py:62
  20.8 5.0 %collective-permute-start.5 = (bf16[64,4096]{1,0:T(8,128)(2,1)S(1)}, bf16[64,4096]{1,0:T(8,128)(2,1)S(1)}, u32[]{:S(2)}, u32[]{:S(2)}) collective-permute-start(bf16[64,4096]{1,0:T(8,128)(2,1)S(1)} %shard_map.83.refs_0_.refs_2_), channel_id=1, source_target_pairs={{0,2},{1,3},{2,0},{3,1},{4,6},{5,7},{6,4},{7,5},{8,10},{9,11},{10,... | collective-permute-start | bytes 1572872 | tf_op jit(solution)/shard_map/own_x/ppermute | solution.py:62
  20.8 12.1 %collective-permute-start.7 = (bf16[32,4096]{1,0:T(8,128)(2,1)S(1)}, bf16[32,4096]{1,0:T(8,128)(2,1)S(1)}, u32[]{:S(2)}, u32[]{:S(2)}) collective-permute-start(bf16[32,4096]{1,0:T(8,128)(2,1)S(1)} %get-tuple-element.27.mine), channel_id=1, source_target_pairs={{0,4},{1,5},{2,6},{3,7},{4,0},{5,1},{6,2},{7,3},{8,12},{9,13},{10,... | collective-permute-start | bytes 786440 | tf_op jit(solution)/shard_map/near/ppermute | solution.py:62
  21.5 23.9 %collective-permute-start.1 = (bf16[16,4096]{1,0:T(8,128)(2,1)S(1)}, bf16[16,4096]{1,0:T(8,128)(2,1)S(1)}, u32[]{:S(2)}, u32[]{:S(2)}) collective-permute-start(bf16[16,4096]{1,0:T(8,128)(2,1)S(1)} %collective-permute-done.refs_6_), channel_id=1, source_target_pairs={{0,4},{1,5},{2,6},{3,7},{4,0},{5,1},{6,2},{7,3},{8,12},{9,13},{10,... | collective-permute-start | bytes 393224 | tf_op jit(solution)/shard_map/cross_b/ppermute | solution.py:62
  23.6 18.2 %collective-permute-start.10 = (bf16[16,4096]{1,0:T(8,128)(2,1)S(1)}, bf16[16,4096]{1,0:T(8,128)(2,1)S(1)}, u32[]{:S(2)}, u32[]{:S(2)}) collective-permute-start(bf16[16,4096]{1,0:T(8,128)(2,1)S(1)} %collective-permute-done.refs_6_), channel_id=1, source_target_pairs={{0,16},{1,17},{2,18},{3,19},{4,20},{5,21},{6,22},{7,23},{8,24},{9,... | collective-permute-start | bytes 393224 | tf_op jit(solution)/shard_map/far_pb/ppermute | solution.py:62
  24.4 9.2 %collective-permute-start.13 = (bf16[16,4096]{1,0:T(8,128)(2,1)S(1)}, bf16[16,4096]{1,0:T(8,128)(2,1)S(1)}, u32[]{:S(2)}, u32[]{:S(2)}) collective-permute-start(bf16[16,4096]{1,0:T(8,128)(2,1)S(1)} %collective-permute-done.12.refs_9_), channel_id=1, source_target_pairs={{0,16},{1,17},{2,18},{3,19},{4,20},{5,21},{6,22},{7,23},{8,24},{9,... | collective-permute-start | bytes 393224 | tf_op jit(solution)/shard_map/cross_pa/ppermute | solution.py:62
  25.8 16.6 %collective-permute-start.4 = (bf16[32,4096]{1,0:T(8,128)(2,1)S(1)}, bf16[32,4096]{1,0:T(8,128)(2,1)S(1)}, u32[]{:S(2)}, u32[]{:S(2)}) collective-permute-start(bf16[32,4096]{1,0:T(8,128)(2,1)S(1)} %pad_maximum_fusion.1), channel_id=1, source_target_pairs={{0,2},{1,3},{2,0},{3,1},{4,6},{5,7},{6,4},{7,5},{8,10},{9,11},{10,... | collective-permute-start | bytes 786440 | tf_op jit(solution)/shard_map/far_xa/ppermute | solution.py:62
  25.9 3.4 %copy-start = (bf16[1024,1,4096]{2,0,1:T(8,128)(2,1)S(1)}, bf16[1024,1,4096]{2,0,1:T(8,128)(2,1)}, u32[]{:S(2)}) copy-start(bf16[1024,1,4096]{2,0,1:T(8,128)(2,1)} %param.8) | copy-start | bytes 25165828
  29.9 12.5 %copy-start.1 = (bf16[1024,1,4096]{2,0,1:T(8,128)(2,1)S(1)}, bf16[1024,1,4096]{2,0,1:T(8,128)(2,1)}, u32[]{:S(2)}) copy-start(bf16[1024,1,4096]{2,0,1:T(8,128)(2,1)} %param.8) | copy-start | bytes 25165828
  32.9 8.8 %collective-permute-start.8 = (bf16[32,4096]{1,0:T(8,128)(2,1)S(1)}, bf16[32,4096]{1,0:T(8,128)(2,1)S(1)}, u32[]{:S(2)}, u32[]{:S(2)}) collective-permute-start(bf16[32,4096]{1,0:T(8,128)(2,1)S(1)} %collective-permute-done.7.refs_0_.refs_3_), channel_id=1, source_target_pairs={{0,16},{1,17},{2,18},{3,19},{4,20},{5,21},{6,22},{7,23},{8,24},{9,... | collective-permute-start | bytes 786440 | tf_op jit(solution)/shard_map/near_p/ppermute | solution.py:62
  33.7 12.4 %collective-permute-start.14 = (bf16[32,4096]{1,0:T(8,128)(2,1)S(1)}, bf16[32,4096]{1,0:T(8,128)(2,1)S(1)}, u32[]{:S(2)}, u32[]{:S(2)}) collective-permute-start(bf16[32,4096]{1,0:T(8,128)(2,1)S(1)} %pad_maximum_fusion.3), channel_id=1, source_target_pairs={{0,2},{1,3},{2,0},{3,1},{4,6},{5,7},{6,4},{7,5},{8,10},{9,11},{10,... | collective-permute-start | bytes 786440 | tf_op jit(solution)/shard_map/cross_xa/ppermute | solution.py:62
  41.7 4.4 %collective-permute-start.9 = (bf16[64,4096]{1,0:T(8,128)(2,1)S(1)}, bf16[64,4096]{1,0:T(8,128)(2,1)S(1)}, u32[]{:S(2)}, u32[]{:S(2)}) collective-permute-start(bf16[64,4096]{1,0:T(8,128)(2,1)S(1)} %pad_maximum_fusion), channel_id=1, source_target_pairs={{0,2},{1,3},{2,0},{3,1},{4,6},{5,7},{6,4},{7,5},{8,10},{9,11},{10,... | collective-permute-start | bytes 1572872 | tf_op jit(solution)/shard_map/near_x/ppermute | solution.py:62
  41.8 4.3 %collective-permute-start.11 = (bf16[32,4096]{1,0:T(8,128)(2,1)S(1)}, bf16[32,4096]{1,0:T(8,128)(2,1)S(1)}, u32[]{:S(2)}, u32[]{:S(2)}) collective-permute-start(bf16[32,4096]{1,0:T(8,128)(2,1)S(1)} %pad_maximum_fusion.2), channel_id=1, source_target_pairs={{0,2},{1,3},{2,0},{3,1},{4,6},{5,7},{6,4},{7,5},{8,10},{9,11},{10,... | collective-permute-start | bytes 786440 | tf_op jit(solution)/shard_map/far_xb/ppermute | solution.py:62
  45.3 16.5 %copy-start.7 = (s32[256]{0:T(256)S(1)}, s32[256]{0:T(256)}, u32[]{:S(2)}) copy-start(s32[256]{0:T(256)} %param.15) | copy-start | bytes 3076
  45.4 20.0 %copy-start.6 = (s32[1024]{0:T(1024)S(1)}, s32[1024]{0:T(1024)}, u32[]{:S(2)}) copy-start(s32[1024]{0:T(1024)} %param.14) | copy-start | bytes 12292
  45.4 5.5 %collective-permute-start.6 = (bf16[16,4096]{1,0:T(8,128)(2,1)S(1)}, bf16[16,4096]{1,0:T(8,128)(2,1)S(1)}, u32[]{:S(2)}, u32[]{:S(2)}) collective-permute-start(bf16[16,4096]{1,0:T(8,128)(2,1)S(1)} %collective-permute-done.1.refs_0_), channel_id=1, source_target_pairs={{0,16},{1,17},{2,18},{3,19},{4,20},{5,21},{6,22},{7,23},{8,24},{9,... | collective-permute-start | bytes 393224 | tf_op jit(solution)/shard_map/cross_pb/ppermute | solution.py:62
  50.9 6.4 %collective-permute-start.15 = (bf16[32,4096]{1,0:T(8,128)(2,1)S(1)}, bf16[32,4096]{1,0:T(8,128)(2,1)S(1)}, u32[]{:S(2)}, u32[]{:S(2)}) collective-permute-start(bf16[32,4096]{1,0:T(8,128)(2,1)S(1)} %pad_maximum_fusion.4), channel_id=1, source_target_pairs={{0,2},{1,3},{2,0},{3,1},{4,6},{5,7},{6,4},{7,5},{8,10},{9,11},{10,... | collective-permute-start | bytes 786440 | tf_op jit(solution)/shard_map/cross_xb/ppermute | solution.py:62
  51.0 6.4 %collective-permute-start.16 = (bf16[64,1024]{1,0:T(8,128)(2,1)S(1)}, bf16[64,1024]{1,0:T(8,128)(2,1)S(1)}, u32[]{:S(2)}, u32[]{:S(2)}) collective-permute-start(bf16[64,1024]{1,0:T(8,128)(2,1)S(1)} %get-tuple-element.33), channel_id=1, source_target_pairs={{0,1},{1,0},{2,3},{3,2},{4,5},{5,4},{6,7},{7,6},{8,9},{9,8},{10,11... | collective-permute-start | bytes 393224 | tf_op jit(solution)/shard_map/got1/ppermute | solution.py:62
  52.6 10.2 %collective-permute-start.17 = (bf16[128,1024]{1,0:T(8,128)(2,1)S(1)}, bf16[128,1024]{1,0:T(8,128)(2,1)S(1)}, u32[]{:S(2)}, u32[]{:S(2)}) collective-permute-start(bf16[128,1024]{1,0:T(8,128)(2,1)S(1)} %get-tuple-element.37), channel_id=1, source_target_pairs={{0,1},{1,0},{2,3},{3,2},{4,5},{5,4},{6,7},{7,6},{8,9},{9,8},{10,11... | collective-permute-start | bytes 786440 | tf_op jit(solution)/shard_map/got2/ppermute | solution.py:62
  60.3 5.0 %collective-permute-start.18 = (bf16[64,1024]{1,0:T(8,128)(2,1)S(1)}, bf16[64,1024]{1,0:T(8,128)(2,1)S(1)}, u32[]{:S(2)}, u32[]{:S(2)}) collective-permute-start(bf16[64,1024]{1,0:T(8,128)(2,1)S(1)} %get-tuple-element.44), channel_id=1, source_target_pairs={{0,1},{1,0},{2,3},{3,2},{4,5},{5,4},{6,7},{7,6},{8,9},{9,8},{10,11... | collective-permute-start | bytes 393224 | tf_op jit(solution)/shard_map/got3/ppermute | solution.py:62
  (3 other events, 2.2 us)

commit v3 on v2

v3 whole, which is shorter than its diff:
```python
import functools

import jax
import jax.numpy as jnp
from jax import lax
from jax.experimental import pallas as pl
from jax.experimental.pallas import tpu as pltpu
from jax.sharding import PartitionSpec as P

AXES = ("parts", "store", "layer")
VMEM = pl.BlockSpec(memory_space=pltpu.VMEM)
SMEM = pl.BlockSpec(memory_space=pltpu.SMEM)
bf16, f32 = jnp.bfloat16, jnp.float32
LIMIT = 20 * 1024 * 1024


def preconditioned(query_grads, left_factor, right_factor):
    q_rows, slots, width = query_grads.shape
    side = left_factor.shape[1]
    mats = query_grads.astype(jnp.float32).reshape(q_rows, slots, side, side)
    half = jnp.einsum("lij,qljk->qlik", left_factor, mats, precision=lax.Precision.HIGHEST)
    full = jnp.einsum("qlik,lkm->qlim", half, right_factor, precision=lax.Precision.HIGHEST)
    return full.reshape(q_rows, slots, width).astype(jnp.bfloat16)


def general(
    train_grads,
    query_grads,
    left_factor,
    right_factor,
    layer_weight,
    layer_of,
    train_ids,
    query_ids,
):
    precond = preconditioned(query_grads, left_factor, right_factor)
    weight = jnp.take(layer_weight, layer_of[0])
    queries = lax.all_gather(precond, "store", axis=0, tiled=True)
    terms = weight * jnp.dot(
        queries[:, 0, :], train_grads[:, 0, :].T, preferred_element_type=jnp.float32
    )
    summed = lax.psum_scatter(terms, "layer", scatter_dimension=0, tiled=True)
    same = query_ids[:, None] == train_ids[None, :]
    return jnp.where(same, jnp.float32(0.0), summed)


PARTS, CHIPS, CORES, LAYERS = 2, 4, 2, 2
CHUNK = 16
HALF = 2 * CHUNK
STEP = 256
HBM = pl.BlockSpec(memory_space=pltpu.HBM)


def permute(value, name, target):
    pairs = []
    for p in range(PARTS):
        for z in range(CHIPS):
            for c in range(CORES):
                for l in range(LAYERS):
                    tp, tz, tc, tl = target(p, z, c, l)
                    source = ((p * CHIPS + z) * CORES + c) * LAYERS + l
                    pairs.append((source, ((tp * CHIPS + tz) * CORES + tc) * LAYERS + tl))
    with jax.named_scope(name):
        return lax.ppermute(value, AXES, pairs)


to_part = functools.partial(permute, target=lambda p, z, c, l: (1 - p, z, c, l))
to_core = functools.partial(permute, target=lambda p, z, c, l: (p, z, 1 - c, l))
to_layer = functools.partial(permute, target=lambda p, z, c, l: (p, z, c, 1 - l))
to_near = functools.partial(permute, target=lambda p, z, c, l: (p, z ^ 1, c, l))
to_far = functools.partial(permute, target=lambda p, z, c, l: (p, z ^ 3, c, l))


def after(value, *others):
    return lax.optimization_barrier((value, *others))[0]


def place():
    store = lax.axis_index("store")
    return lax.axis_index("parts"), store // CORES, store % CORES, lax.axis_index("layer")


def split(x, terms):
    out = []
    for _ in range(terms):
        term = x.astype(bf16)
        out.append(term)
        x = x - term.astype(f32)
    return out


def dot(a, b):
    return lax.dot_general(a, b, (((1,), (0,)), ((), ())), preferred_element_type=f32)


def iota(shape, dim):
    return lax.broadcasted_iota(jnp.int32, shape, dim)


def factors(left, right):
    r, c = iota((256, 64), 0), iota((256, 64), 1)
    pick = jnp.where(c == 4 * (r % 16) + (r // 16) % 4, 1.0, 0.0).astype(bf16)
    r, c = iota((64, 256), 0), iota((64, 256), 1)
    pick_t = jnp.where(r == 4 * (c % 16) + (c // 16) % 4, 1.0, 0.0).astype(bf16)
    block = iota((256, 256), 0) // 64 == iota((256, 256), 1) // 64
    lefts = [
        jnp.where(block, dot(dot(pick, term).astype(bf16), pick_t), 0.0).astype(bf16)
        for term in split(left, 2)
    ]
    row = jnp.concatenate([right, right], axis=1)
    tiled = jnp.concatenate([jnp.concatenate([row] * 4, axis=1)] * 4, axis=0)
    block = iota((256, 512), 0) // 64 == iota((256, 512), 1) // 128
    return lefts, split(jnp.where(block, tiled, 0.0), 2)


def precond_rows(q_ref, lefts, rights, out, base):
    for at in range(0, q_ref.shape[0], CHUNK):
        values = precond_chunk(q_ref[at : at + CHUNK, :], lefts, rights)
        for t, value in enumerate(values):
            out[base + at : base + at + CHUNK, t * 256 : (t + 1) * 256] = value


def precond_chunk(q, lefts, rights):
    tiles = q.shape[1] // 256
    r, c = iota((256, 256), 0), iota((256, 256), 1)
    swap = jnp.where((r // 16 == c % 16) & (r % 16 == c // 16), 1.0, 0.0).astype(bf16)
    x = jnp.concatenate([q[:, t * 256 : (t + 1) * 256] for t in range(tiles)], axis=0)
    x = dot(swap, x).astype(bf16)
    z = dot(x, rights[0]) + dot(x, rights[1])
    sets = []
    for first in range(0, 16, 4):
        rows = [
            z[query * 16 : (query + 1) * 16, s * 128 : (s + 1) * 128]
            for query in range(first, first + 4)
            for s in range(4)
        ]
        sets.append(jnp.concatenate(rows, axis=0))
    high, low = split(jnp.concatenate(sets, axis=1), 2)
    z = dot(lefts[0], high) + (dot(lefts[0], low) + dot(lefts[1], high))
    side = iota((16, 128), 1) < 64
    rows = []
    for first in range(4):
        for k in range(4):
            o = z[k * 64 : (k + 1) * 64, first * 128 : (first + 1) * 128]
            pair = [jnp.where(side, o[0:16], o[16:32]), jnp.where(side, o[32:48], o[48:64])]
            rows.append(jnp.concatenate(pair, axis=1))
    y = dot(swap, jnp.concatenate(rows, axis=0).astype(bf16)).astype(bf16)
    return [y[t * 16 : (t + 1) * 16] for t in range(tiles)]


def own_kernel(q_hbm, left_hbm, right_hbm, mine, lefts_ref, rights_ref, q_ref, left, right, sems):
    at = pl.multiple_of(lax.axis_index("parts") * HALF, HALF)
    copies = [
        pltpu.make_async_copy(source, target, sems.at[k])
        for k, (source, target) in enumerate(
            ((left_hbm, left), (right_hbm, right), (q_hbm.at[pl.ds(at, HALF), :], q_ref))
        )
    ]
    for copy in copies:
        copy.start()
    copies[0].wait()
    copies[1].wait()
    lefts, rights = factors(left[...], right[...])
    for k in range(2):
        lefts_ref[k] = lefts[k]
        rights_ref[k] = rights[k]
    copies[2].wait()
    precond_rows(q_ref, lefts, rights, mine, 0)


def rest_kernel(
    weight_ref, layer_ref, q_hbm, train_hbm, lefts_ref, rights_ref, rest, train, weight, q_ref, sems
):
    at = pl.multiple_of((1 - lax.axis_index("parts")) * HALF, HALF)
    q_copy = pltpu.make_async_copy(q_hbm.at[pl.ds(at, HALF), :], q_ref, sems.at[0])
    q_copy.start()
    copies = []
    for k in range(train.shape[0] // STEP):
        here = pl.ds(k * STEP, STEP)
        copies.append(pltpu.make_async_copy(train_hbm.at[here, :], train.at[here, :], sems.at[1 + k]))
        copies[-1].start()
    weight[...] = jnp.full(weight.shape, weight_ref[layer_ref[0]])
    lefts, rights = [lefts_ref[0], lefts_ref[1]], [rights_ref[0], rights_ref[1]]
    q_copy.wait()
    precond_rows(q_ref, lefts, rights, rest, 0)
    for copy in copies:
        copy.wait()


def score_kernel(weight_ref, train_ref, *refs, picks, stored, early):
    inputs, refs = refs[: len(picks)], refs[len(picks) :]
    n_before = sum(taken for _, _, taken in early)
    before, outs = refs[:n_before], refs[n_before:]
    weight = weight_ref[0:1, :]
    queries = jnp.concatenate(
        [piece[at : at + n, :] for piece, rows in zip(inputs, picks) for at, n in rows], axis=0
    )
    _, z, _, layer = place()
    near_is_mine = z // 2 == layer
    for at in range(0, train_ref.shape[0], STEP):
        here = slice(at, at + STEP)
        value = lax.dot_general(
            train_ref[here, :], queries, (((1,), (1,)), ((), ())), preferred_element_type=f32
        )
        value = weight * value.T
        if stored:
            outs[0][:, here] = value[:stored]
        if early:
            send, keep = outs[-2:]
            old, given = [], list(before)
            for first, rows, taken in early:
                old.append(
                    given.pop(0)[first : first + rows, here] if taken else value[first : first + rows]
                )
            old, new = jnp.concatenate(old, axis=0), value[stored:]
            send[:, here] = jnp.where(near_is_mine, new, old).astype(send.dtype)
            keep[:, here] = jnp.where(near_is_mine, old, new)


def kernel_call(kernel, outs, inputs, specs=None, scratch=()):
    return pl.pallas_call(
        kernel,
        out_shape=outs,
        in_specs=specs or [VMEM] * len(inputs),
        out_specs=[VMEM] * len(outs) if isinstance(outs, list) else VMEM,
        scratch_shapes=scratch,
        compiler_params=pltpu.CompilerParams(vmem_limit_bytes=LIMIT),
    )(*inputs)


def call_scores(weight, train, inputs, stored=0, early=()):
    n = train.shape[0]
    total = sum(count for _, rows in inputs for _, count in rows)
    outs = [jax.ShapeDtypeStruct((stored, n), f32)] if stored else []
    if early:
        outs += [jax.ShapeDtypeStruct((total - stored, n), t) for t in (bf16, f32)]
    return kernel_call(
        functools.partial(
            score_kernel,
            picks=[rows for _, rows in inputs],
            stored=stored,
            early=[(first, rows, a is not None) for a, first, rows in early],
        ),
        outs,
        [weight, train, *[a for a, _ in inputs], *[a for a, _, _ in early if a is not None]],
    )


def final_kernel(train_ids, query_ids, *refs, groups):
    out = refs[-1]
    part, z, core, layer = place()
    low = z % 2
    first = jnp.where(z // 2 == layer, low, 1 - low)
    ids = train_ids[...]
    for k, (block, start, rows) in enumerate(groups):
        keep, got = refs[2 * k], refs[2 * k + 1]
        block = first if block == 0 else 1 - first
        for i in range(4):
            c = core if i < 2 else 1 - core
            h = part if i % 2 == 0 else 1 - part
            at = pl.multiple_of(((block * 2 + c) * 2 + h) * HALF + start, CHUNK)
            here = slice(i * rows, (i + 1) * rows)
            total = keep[here, :] + got[here, :].astype(f32)
            same = query_ids[pl.ds(at, rows), :] == ids
            out[pl.ds(at, rows), :] = jnp.where(same, jnp.float32(0.0), total)


def small(
    train_grads,
    query_grads,
    left_factor,
    right_factor,
    layer_weight,
    layer_of,
    train_ids,
    query_ids,
):
    train, queries = train_grads[:, 0, :], query_grads[:, 0, :]
    width, side = queries.shape[1], left_factor.shape[1]
    shape = jax.ShapeDtypeStruct
    mine, lefts, rights = kernel_call(
        own_kernel,
        [shape((HALF, width), bf16), shape((2, 256, 256), bf16), shape((2, 256, 512), bf16)],
        [queries, left_factor[0], right_factor[0]],
        [HBM] * 3,
        [
            pltpu.VMEM((HALF, width), bf16),
            pltpu.VMEM((side, side), f32),
            pltpu.VMEM((side, side), f32),
            pltpu.SemaphoreType.DMA((3,)),
        ],
    )
    near = to_near(mine, "near")
    far = to_far(mine, "far")
    rest, train, weight = kernel_call(
        rest_kernel,
        [shape((HALF, width), bf16), shape(train.shape, bf16), shape((8, STEP), f32)],
        [layer_weight, layer_of, queries, train, lefts, rights],
        [SMEM, SMEM, HBM, HBM, VMEM, VMEM],
        [pltpu.VMEM((HALF, width), bf16), pltpu.SemaphoreType.DMA((1 + train.shape[0] // STEP,))],
    )
    score = functools.partial(call_scores, weight, train)
    whole = lambda *pieces: [(piece, ((0, HALF),)) for piece in pieces]

    mine_x = to_core(mine, "mine_x")
    rest_x = to_core(rest, "rest_x")
    near_x = to_core(near, "near_x")
    near_p = to_part(near, "near_p")
    far = after(far, near)
    cross = to_near(far, "cross")
    far_p = to_part(far, "far_p")
    far_x = to_core(far, "far_x")
    rest_x = after(rest_x, far)
    (early0,) = score(whole(mine, rest, mine_x, rest_x), stored=128)
    near_p = after(near_p, early0)
    near_px = to_core(near_p, "near_px")
    far_px = to_core(far_p, "far_px")
    cross_p = to_part(cross, "cross_p")
    cross_x = to_core(cross, "cross_x")
    early1, send0, keep0 = score(
        whole(near, near_p, near_x, near_px, far, far_p, far_x, far_px),
        stored=128,
        early=[(early0, 0, 128)],
    )
    got0 = to_layer(send0, "got0")
    cross_p = after(cross_p, send0)
    cross_px = to_core(cross_p, "cross_px")
    send1, keep1 = score(whole(cross, cross_p, cross_x, cross_px), early=[(early1, 0, 128)])
    got1 = to_layer(send1, "got1")
    return kernel_call(
        functools.partial(final_kernel, groups=((0, 0, HALF), (1, 0, HALF))),
        shape((query_ids.shape[0], train_ids.shape[0]), f32),
        [train_ids[None, :], query_ids[:, None], keep0, got0, keep1, got1],
    )


def solution(mesh):
    placed = (
        P(("parts", "store"), "layer", None),
        P("store", "layer", None),
        P("layer", None, None),
        P("layer", None, None),
        P(),
        P("layer"),
        P(("parts", "store")),
        P("layer"),
    )
    sizes = tuple(mesh.shape[axis] for axis in AXES)
    return jax.shard_map(
        small if sizes == (PARTS, CHIPS * CORES, LAYERS) else general,
        mesh=mesh,
        in_specs=placed,
        out_specs=P("layer", ("parts", "store")),
        check_vma=False,
    )
```

time: 66.8 us -> 56.9 us (0.85)
  starting transfers between devices: 23.1 us -> 15 us
  Pallas kernels: 16.6 us -> 13.5 us
  waiting for transfers between devices: 19.1 us -> 20.5 us
    ppermute x19 -> x16, starting transfers between devices: 23.1 us -> 15 us  [permute(): return lax.ppermute(value, AXES, pairs)]
    pallas_call x7 -> x6, Pallas kernels: 16.6 us -> 13.5 us  [kernel_call(): pl.pallas_call(kernel, out_shape=outs, in_specs=specs or [VMEM] * len(inp...]
    ppermute x19 -> x16, waiting for transfers between devices: 19.1 us -> 20.5 us  [permute(): return lax.ppermute(value, AXES, pairs)]
    unnamed x16 -> x14, local copies, waits for them, and re-layouts: 6.6 us -> 6.6 us
  transfers between devices with their start and end apart: 19 -> 16, of which waited for: 6 -> 6; matrix products, arithmetic and copies ran while one was open for 0% -> 0% of each run, Pallas kernels for 20% -> 18%
where the time goes in v3:
time: 56.9 us; the launch traced here: 56.5 us
  waiting for transfers between devices  20.5 us (36%)
  starting transfers between devices  15 us (26%)
  Pallas kernels  13.5 us (24%)
  local copies, waits for them, and re-layouts  6.73 us (12%)
  between operations  0.76 us (1%)
    ppermute x16, waiting for transfers between devices, permute(): return lax.ppermute(value, AXES, pairs)  20.5 us
    ppermute x16, starting transfers between devices, permute(): return lax.ppermute(value, AXES, pairs)  15 us
    pallas_call x6, Pallas kernels, kernel_call(): pl.pallas_call(kernel, out_shape=outs, in_specs=specs or [VMEM] * len(inp...  13.5 us
    unnamed x14, local copies, waits for them, and re-layouts  6.6 us
  transfers between devices with their start and end apart: 16, of which 6 were waited for; matrix products, arithmetic and copies ran while one was open for 0% of the time, Pallas kernels for 18%

profile of v3, /device:TPU:0, one launch (start us, length us, event | category | flops | bytes accessed | tf_op | source)
XLA Modules:
  0.0 56.5 jit_solution(1006596291031616885)
XLA Ops:
  0.0 1.0 %copy-done.1 = bf16[64,1,4096]{2,0,1:T(8,128)(2,1)S(1)} copy-done((bf16[64,1,4096]{2,0,1:T(8,128)(2,1)S(1)}, bf16[64,1,4096]{2,0,1:T(8,128)(2,1)}, u32[]{:S(2)}) %copy-start.1) | copy-done | bytes 524312
  1.0 0.8 %copy-done.2 = f32[1,64,64]{2,1,0:T(8,128)S(1)} copy-done((f32[1,64,64]{2,1,0:T(8,128)S(1)}, f32[1,64,64]{2,1,0:T(8,128)}, u32[]{:S(2)}) %copy-start.2) | copy-done | bytes 16408
  1.8 0.8 %copy-done.3 = f32[1,64,64]{2,1,0:T(8,128)S(1)} copy-done((f32[1,64,64]{2,1,0:T(8,128)S(1)}, f32[1,64,64]{2,1,0:T(8,128)}, u32[]{:S(2)}) %copy-start.3) | copy-done | bytes 16408
  2.6 2.1 %shard_map.82 = (bf16[32,4096]{1,0:T(8,128)(2,1)S(1)}, bf16[2,256,256]{2,1,0:T(8,128)(2,1)S(1)}, bf16[2,256,512]{2,1,0:T(8,128)(2,1)S(1)}) custom-call(bf16[64,4096]{1,0:T(8,128)(2,1)S(1)} %bitcast.7, f32[64,64]{1,0:T(8,128)S(1)} %bitcast.9, f32[64,64]{1,0:T(8,128)S(1)} %bitcast.10), custom_call_target="tpu_custom_call" | custom-call | tf_op jit(solution)/shard_map/pallas_call | solution.py:221
  4.7 3.1 %collective-permute-start = (bf16[32,4096]{1,0:T(8,128)(2,1)S(1)}, bf16[32,4096]{1,0:T(8,128)(2,1)S(1)}, u32[]{:S(2)}, u32[]{:S(2)}) collective-permute-start(bf16[32,4096]{1,0:T(8,128)(2,1)S(1)} %get-tuple-element.24.refs_0_), channel_id=1, source_target_pairs={{0,4},{1,5},{2,6},{3,7},{4,0},{5,1},{6,2},{7,3},{8,12},{9,13},{10,... | collective-permute-start | bytes 786440 | tf_op jit(solution)/shard_map/near/ppermute | solution.py:64
  7.8 2.5 %collective-permute-start.4 = (bf16[32,4096]{1,0:T(8,128)(2,1)S(1)}, bf16[32,4096]{1,0:T(8,128)(2,1)S(1)}, u32[]{:S(2)}, u32[]{:S(2)}) collective-permute-start(bf16[32,4096]{1,0:T(8,128)(2,1)S(1)} %get-tuple-element.24.refs_0_), channel_id=1, source_target_pairs={{0,12},{1,13},{2,14},{3,15},{4,8},{5,9},{6,10},{7,11},{8,4},{9,5},... | collective-permute-start | bytes 786440 | tf_op jit(solution)/shard_map/far/ppermute | solution.py:64
  10.9 3.4 %copy-done = bf16[1024,1,4096]{2,0,1:T(8,128)(2,1)S(1)} copy-done((bf16[1024,1,4096]{2,0,1:T(8,128)(2,1)S(1)}, bf16[1024,1,4096]{2,0,1:T(8,128)(2,1)}, u32[]{:S(2)}) %copy-start) | copy-done | bytes 8388632
  14.3 0.7 %copy-done.5 = f32[2]{0:T(128)S(1)} copy-done((f32[2]{0:T(128)S(1)}, f32[2]{0:T(128)}, u32[]{:S(2)}) %copy-start.5) | copy-done | bytes 32
  14.9 2.9 %shard_map.83 = (bf16[32,4096]{1,0:T(8,128)(2,1)S(1)}, bf16[1024,4096]{1,0:T(8,128)(2,1)S(1)}, f32[8,256]{1,0:T(8,128)S(1)}) custom-call(f32[2]{0:T(128)S(1)} %copy-done.5, s32[1]{0:T(128)S(6)} %copy.10.layer_ref, bf16[64,4096]{1,0:T(8,128)(2,1)S(1)} %bitcast.8, bf16[1024,4096]{1,0:T(8,128)(2,1)S(1)} %bitcast.6, ...), custom_call_target="tpu_custom_call" | custom-call | tf_op jit(solution)/shard_map/pallas_call | solution.py:221
  18.4 1.5 %collective-permute-start.1 = (bf16[32,4096]{1,0:T(8,128)(2,1)S(1)}, bf16[32,4096]{1,0:T(8,128)(2,1)S(1)}, u32[]{:S(2)}, u32[]{:S(2)}) collective-permute-start(bf16[32,4096]{1,0:T(8,128)(2,1)S(1)} %collective-permute-done.refs_0_), channel_id=1, source_target_pairs={{0,16},{1,17},{2,18},{3,19},{4,20},{5,21},{6,22},{7,23},{8,24},{9,... | collective-permute-start | bytes 786440 | tf_op jit(solution)/shard_map/near_p/ppermute | solution.py:64
  19.9 2.1 %collective-permute-done.4.refs_4_ = bf16[32,4096]{1,0:T(8,128)(2,1)S(1)} collective-permute-done((bf16[32,4096]{1,0:T(8,128)(2,1)S(1)}, bf16[32,4096]{1,0:T(8,128)(2,1)S(1)}, u32[]{:S(2)}, u32[]{:S(2)}) %collective-permute-start.4) | collective-permute-done | bytes 262176 | tf_op jit(solution)/shard_map/far/ppermute | solution.py:64
  22.0 1.5 %collective-permute-start.7 = (bf16[32,4096]{1,0:T(8,128)(2,1)S(1)}, bf16[32,4096]{1,0:T(8,128)(2,1)S(1)}, u32[]{:S(2)}, u32[]{:S(2)}) collective-permute-start(bf16[32,4096]{1,0:T(8,128)(2,1)S(1)} %collective-permute-done.4.refs_4_), channel_id=1, source_target_pairs={{0,16},{1,17},{2,18},{3,19},{4,20},{5,21},{6,22},{7,23},{8,24},{9,... | collective-permute-start | bytes 786440 | tf_op jit(solution)/shard_map/far_p/ppermute | solution.py:64
  23.5 0.6 %collective-permute-start.11 = (bf16[32,4096]{1,0:T(8,128)(2,1)S(1)}, bf16[32,4096]{1,0:T(8,128)(2,1)S(1)}, u32[]{:S(2)}, u32[]{:S(2)}) collective-permute-start(bf16[32,4096]{1,0:T(8,128)(2,1)S(1)} %collective-permute-done.4.refs_4_), channel_id=1, source_target_pairs={{0,4},{1,5},{2,6},{3,7},{4,0},{5,1},{6,2},{7,3},{8,12},{9,13},{10,... | collective-permute-start | bytes 786440 | tf_op jit(solution)/shard_map/cross/ppermute | solution.py:64
  24.6 2.4 %shard_map.84.refs_8_ = f32[128,1024]{1,0:T(8,128)S(1)} custom-call(f32[8,256]{1,0:T(8,128)S(1)} %get-tuple-element.22.weight_ref, bf16[1024,4096]{1,0:T(8,128)(2,1)S(1)} %get-tuple-element.23.train_ref, bf16[32,4096]{1,0:T(8,128)(2,1)S(1)} %get-tuple-element.24.refs_0_, bf16[32,4096]{1,0:T(8,128)(2,1)S(1)} %get-tuple-element.25.refs_1_, ...), custom_call_target="tpu_custom_call" | custom-call | tf_op jit(solution)/shard_map/pallas_call | solution.py:221
  27.6 4.7 %collective-permute-done.7.refs_5_ = bf16[32,4096]{1,0:T(8,128)(2,1)S(1)} collective-permute-done((bf16[32,4096]{1,0:T(8,128)(2,1)S(1)}, bf16[32,4096]{1,0:T(8,128)(2,1)S(1)}, u32[]{:S(2)}, u32[]{:S(2)}) %collective-permute-start.7) | collective-permute-done | bytes 262176 | tf_op jit(solution)/shard_map/far_p/ppermute | solution.py:64
  32.3 1.5 %collective-permute-start.12 = (bf16[32,4096]{1,0:T(8,128)(2,1)S(1)}, bf16[32,4096]{1,0:T(8,128)(2,1)S(1)}, u32[]{:S(2)}, u32[]{:S(2)}) collective-permute-start(bf16[32,4096]{1,0:T(8,128)(2,1)S(1)} %collective-permute-done.11.refs_0_), channel_id=1, source_target_pairs={{0,16},{1,17},{2,18},{3,19},{4,20},{5,21},{6,22},{7,23},{8,24},{9,... | collective-permute-start | bytes 786440 | tf_op jit(solution)/shard_map/cross_p/ppermute | solution.py:64
  34.1 2.5 %shard_map.85 = (f32[128,1024]{1,0:T(8,128)S(1)}, bf16[128,1024]{1,0:T(8,128)(2,1)S(1)}, f32[128,1024]{1,0:T(8,128)S(1)}) custom-call(f32[8,256]{1,0:T(8,128)S(1)} %get-tuple-element.22.weight_ref, bf16[1024,4096]{1,0:T(8,128)(2,1)S(1)} %get-tuple-element.23.train_ref, bf16[32,4096]{1,0:T(8,128)(2,1)S(1)} %collective-permute-done.refs_0_, ...), custom_call_target="tpu_custom_call" | custom-call | tf_op jit(solution)/shard_map/pallas_call | solution.py:221
  36.6 4.5 %collective-permute-done.12.refs_1_ = bf16[32,4096]{1,0:T(8,128)(2,1)S(1)} collective-permute-done((bf16[32,4096]{1,0:T(8,128)(2,1)S(1)}, bf16[32,4096]{1,0:T(8,128)(2,1)S(1)}, u32[]{:S(2)}, u32[]{:S(2)}) %collective-permute-start.12) | collective-permute-done | bytes 262176 | tf_op jit(solution)/shard_map/cross_p/ppermute | solution.py:64
  41.1 1.5 %collective-permute-start.10 = (bf16[128,1024]{1,0:T(8,128)(2,1)S(1)}, bf16[128,1024]{1,0:T(8,128)(2,1)S(1)}, u32[]{:S(2)}, u32[]{:S(2)}) collective-permute-start(bf16[128,1024]{1,0:T(8,128)(2,1)S(1)} %get-tuple-element.30), channel_id=1, source_target_pairs={{0,1},{1,0},{2,3},{3,2},{4,5},{5,4},{6,7},{7,6},{8,9},{9,8},{10,11... | collective-permute-start | bytes 786440 | tf_op jit(solution)/shard_map/got0/ppermute | solution.py:64
  42.6 2.4 %shard_map.86 = (bf16[128,1024]{1,0:T(8,128)(2,1)S(1)}, f32[128,1024]{1,0:T(8,128)S(1)}) custom-call(f32[8,256]{1,0:T(8,128)S(1)} %get-tuple-element.22.weight_ref, bf16[1024,4096]{1,0:T(8,128)(2,1)S(1)} %get-tuple-element.23.train_ref, bf16[32,4096]{1,0:T(8,128)(2,1)S(1)} %collective-permute-done.11.refs_0_, ...), custom_call_target="tpu_custom_call" | custom-call | tf_op jit(solution)/shard_map/pallas_call | solution.py:221
  45.0 1.6 %collective-permute-start.15 = (bf16[128,1024]{1,0:T(8,128)(2,1)S(1)}, bf16[128,1024]{1,0:T(8,128)(2,1)S(1)}, u32[]{:S(2)}, u32[]{:S(2)}) collective-permute-start(bf16[128,1024]{1,0:T(8,128)(2,1)S(1)} %get-tuple-element.34), channel_id=1, source_target_pairs={{0,1},{1,0},{2,3},{3,2},{4,5},{5,4},{6,7},{7,6},{8,9},{9,8},{10,11... | collective-permute-start | bytes 786440 | tf_op jit(solution)/shard_map/got1/ppermute | solution.py:64
  46.8 3.4 %collective-permute-done.10.refs_1_ = bf16[128,1024]{1,0:T(8,128)(2,1)S(1)} collective-permute-done((bf16[128,1024]{1,0:T(8,128)(2,1)S(1)}, bf16[128,1024]{1,0:T(8,128)(2,1)S(1)}, u32[]{:S(2)}, u32[]{:S(2)}) %collective-permute-start.10) | collective-permute-done | bytes 262176 | tf_op jit(solution)/shard_map/got0/ppermute | solution.py:64
  50.2 5.2 %collective-permute-done.15.refs_3_ = bf16[128,1024]{1,0:T(8,128)(2,1)S(1)} collective-permute-done((bf16[128,1024]{1,0:T(8,128)(2,1)S(1)}, bf16[128,1024]{1,0:T(8,128)(2,1)S(1)}, u32[]{:S(2)}, u32[]{:S(2)}) %collective-permute-start.15) | collective-permute-done | bytes 262176 | tf_op jit(solution)/shard_map/got1/ppermute | solution.py:64
  55.4 1.1 %shard_map.87 = f32[256,1024]{1,0:T(8,128)} custom-call(s32[1,1024]{1,0:T(1,128)S(1)} %bitcast.11, s32[256,1]{1,0:T(8,128)S(1)} %copy.9.query_ids, f32[128,1024]{1,0:T(8,128)S(1)} %get-tuple-element.29.refs_0_, bf16[128,1024]{1,0:T(8,128)(2,1)S(1)} %collective-permute-done.10.refs_1_, f32[128,1024]{1,0:T(8,128)S(1)} %get-tuple-element.33.refs_2_, ...), custom_call_target="tpu_custom_call" | custom-call | tf_op jit(solution)/shard_map/pallas_call | solution.py:221
  (29 shorter events, 2.1 us)
Async XLA Ops:
  0.0 1.0 %copy-start.1 = (bf16[64,1,4096]{2,0,1:T(8,128)(2,1)S(1)}, bf16[64,1,4096]{2,0,1:T(8,128)(2,1)}, u32[]{:S(2)}) copy-start(bf16[64,1,4096]{2,0,1:T(8,128)(2,1)} %param.9) | copy-start | bytes 1572868
  1.0 0.8 %copy-start.2 = (f32[1,64,64]{2,1,0:T(8,128)S(1)}, f32[1,64,64]{2,1,0:T(8,128)}, u32[]{:S(2)}) copy-start(f32[1,64,64]{2,1,0:T(8,128)} %param.10) | copy-start | bytes 49156
  1.8 0.8 %copy-start.3 = (f32[1,64,64]{2,1,0:T(8,128)S(1)}, f32[1,64,64]{2,1,0:T(8,128)}, u32[]{:S(2)}) copy-start(f32[1,64,64]{2,1,0:T(8,128)} %param.11) | copy-start | bytes 49156
  4.7 13.7 %collective-permute-start = (bf16[32,4096]{1,0:T(8,128)(2,1)S(1)}, bf16[32,4096]{1,0:T(8,128)(2,1)S(1)}, u32[]{:S(2)}, u32[]{:S(2)}) collective-permute-start(bf16[32,4096]{1,0:T(8,128)(2,1)S(1)} %get-tuple-element.24.refs_0_), channel_id=1, source_target_pairs={{0,4},{1,5},{2,6},{3,7},{4,0},{5,1},{6,2},{7,3},{8,12},{9,13},{10,... | collective-permute-start | bytes 786440 | tf_op jit(solution)/shard_map/near/ppermute | solution.py:64
  7.8 14.2 %collective-permute-start.4 = (bf16[32,4096]{1,0:T(8,128)(2,1)S(1)}, bf16[32,4096]{1,0:T(8,128)(2,1)S(1)}, u32[]{:S(2)}, u32[]{:S(2)}) collective-permute-start(bf16[32,4096]{1,0:T(8,128)(2,1)S(1)} %get-tuple-element.24.refs_0_), channel_id=1, source_target_pairs={{0,12},{1,13},{2,14},{3,15},{4,8},{5,9},{6,10},{7,11},{8,4},{9,5},... | collective-permute-start | bytes 786440 | tf_op jit(solution)/shard_map/far/ppermute | solution.py:64
  10.9 3.4 %copy-start = (bf16[1024,1,4096]{2,0,1:T(8,128)(2,1)S(1)}, bf16[1024,1,4096]{2,0,1:T(8,128)(2,1)}, u32[]{:S(2)}) copy-start(bf16[1024,1,4096]{2,0,1:T(8,128)(2,1)} %param.8) | copy-start | bytes 25165828
  14.3 0.7 %copy-start.5 = (f32[2]{0:T(128)S(1)}, f32[2]{0:T(128)}, u32[]{:S(2)}) copy-start(f32[2]{0:T(128)} %weight_ref.1) | copy-start | bytes 28
  17.8 6.2 %collective-permute-start.3 = (bf16[32,4096]{1,0:T(8,128)(2,1)S(1)}, bf16[32,4096]{1,0:T(8,128)(2,1)S(1)}, u32[]{:S(2)}, u32[]{:S(2)}) collective-permute-start(bf16[32,4096]{1,0:T(8,128)(2,1)S(1)} %get-tuple-element.25.refs_1_), channel_id=1, source_target_pairs={{0,2},{1,3},{2,0},{3,1},{4,6},{5,7},{6,4},{7,5},{8,10},{9,11},{10,... | collective-permute-start | bytes 786440 | tf_op jit(solution)/shard_map/rest_x/ppermute | solution.py:64
  17.9 6.1 %collective-permute-start.2 = (bf16[32,4096]{1,0:T(8,128)(2,1)S(1)}, bf16[32,4096]{1,0:T(8,128)(2,1)S(1)}, u32[]{:S(2)}, u32[]{:S(2)}) collective-permute-start(bf16[32,4096]{1,0:T(8,128)(2,1)S(1)} %get-tuple-element.24.refs_0_), channel_id=1, source_target_pairs={{0,2},{1,3},{2,0},{3,1},{4,6},{5,7},{6,4},{7,5},{8,10},{9,11},{10,... | collective-permute-start | bytes 786440 | tf_op jit(solution)/shard_map/mine_x/ppermute | solution.py:64
  18.4 9.2 %collective-permute-start.1 = (bf16[32,4096]{1,0:T(8,128)(2,1)S(1)}, bf16[32,4096]{1,0:T(8,128)(2,1)S(1)}, u32[]{:S(2)}, u32[]{:S(2)}) collective-permute-start(bf16[32,4096]{1,0:T(8,128)(2,1)S(1)} %collective-permute-done.refs_0_), channel_id=1, source_target_pairs={{0,16},{1,17},{2,18},{3,19},{4,20},{5,21},{6,22},{7,23},{8,24},{9,... | collective-permute-start | bytes 786440 | tf_op jit(solution)/shard_map/near_p/ppermute | solution.py:64
  22.0 10.3 %collective-permute-start.7 = (bf16[32,4096]{1,0:T(8,128)(2,1)S(1)}, bf16[32,4096]{1,0:T(8,128)(2,1)S(1)}, u32[]{:S(2)}, u32[]{:S(2)}) collective-permute-start(bf16[32,4096]{1,0:T(8,128)(2,1)S(1)} %collective-permute-done.4.refs_4_), channel_id=1, source_target_pairs={{0,16},{1,17},{2,18},{3,19},{4,20},{5,21},{6,22},{7,23},{8,24},{9,... | collective-permute-start | bytes 786440 | tf_op jit(solution)/shard_map/far_p/ppermute | solution.py:64
  23.5 8.9 %collective-permute-start.11 = (bf16[32,4096]{1,0:T(8,128)(2,1)S(1)}, bf16[32,4096]{1,0:T(8,128)(2,1)S(1)}, u32[]{:S(2)}, u32[]{:S(2)}) collective-permute-start(bf16[32,4096]{1,0:T(8,128)(2,1)S(1)} %collective-permute-done.4.refs_4_), channel_id=1, source_target_pairs={{0,4},{1,5},{2,6},{3,7},{4,0},{5,1},{6,2},{7,3},{8,12},{9,13},{10,... | collective-permute-start | bytes 786440 | tf_op jit(solution)/shard_map/cross/ppermute | solution.py:64
  24.1 9.8 %collective-permute-start.8 = (bf16[32,4096]{1,0:T(8,128)(2,1)S(1)}, bf16[32,4096]{1,0:T(8,128)(2,1)S(1)}, u32[]{:S(2)}, u32[]{:S(2)}) collective-permute-start(bf16[32,4096]{1,0:T(8,128)(2,1)S(1)} %collective-permute-done.4.refs_4_), channel_id=1, source_target_pairs={{0,2},{1,3},{2,0},{3,1},{4,6},{5,7},{6,4},{7,5},{8,10},{9,11},{10,... | collective-permute-start | bytes 786440 | tf_op jit(solution)/shard_map/far_x/ppermute | solution.py:64
  24.1 10.0 %collective-permute-start.5 = (bf16[32,4096]{1,0:T(8,128)(2,1)S(1)}, bf16[32,4096]{1,0:T(8,128)(2,1)S(1)}, u32[]{:S(2)}, u32[]{:S(2)}) collective-permute-start(bf16[32,4096]{1,0:T(8,128)(2,1)S(1)} %collective-permute-done.refs_0_), channel_id=1, source_target_pairs={{0,2},{1,3},{2,0},{3,1},{4,6},{5,7},{6,4},{7,5},{8,10},{9,11},{10,... | collective-permute-start | bytes 786440 | tf_op jit(solution)/shard_map/near_x/ppermute | solution.py:64
  27.0 19.6 %copy-start.6 = (s32[256]{0:T(256)S(1)}, s32[256]{0:T(256)}, u32[]{:S(2)}) copy-start(s32[256]{0:T(256)} %param.15) | copy-start | bytes 3076
  27.0 28.4 %copy-start.4 = (s32[1024]{0:T(1024)S(1)}, s32[1024]{0:T(1024)}, u32[]{:S(2)}) copy-start(s32[1024]{0:T(1024)} %param.14) | copy-start | bytes 12292
  27.6 6.5 %collective-permute-start.6 = (bf16[32,4096]{1,0:T(8,128)(2,1)S(1)}, bf16[32,4096]{1,0:T(8,128)(2,1)S(1)}, u32[]{:S(2)}, u32[]{:S(2)}) collective-permute-start(bf16[32,4096]{1,0:T(8,128)(2,1)S(1)} %collective-permute-done.1.refs_1_), channel_id=1, source_target_pairs={{0,2},{1,3},{2,0},{3,1},{4,6},{5,7},{6,4},{7,5},{8,10},{9,11},{10,... | collective-permute-start | bytes 786440 | tf_op jit(solution)/shard_map/near_px/ppermute | solution.py:64
  32.3 1.7 %collective-permute-start.9 = (bf16[32,4096]{1,0:T(8,128)(2,1)S(1)}, bf16[32,4096]{1,0:T(8,128)(2,1)S(1)}, u32[]{:S(2)}, u32[]{:S(2)}) collective-permute-start(bf16[32,4096]{1,0:T(8,128)(2,1)S(1)} %collective-permute-done.7.refs_5_), channel_id=1, source_target_pairs={{0,2},{1,3},{2,0},{3,1},{4,6},{5,7},{6,4},{7,5},{8,10},{9,11},{10,... | collective-permute-start | bytes 786440 | tf_op jit(solution)/shard_map/far_px/ppermute | solution.py:64
  32.3 8.7 %collective-permute-start.12 = (bf16[32,4096]{1,0:T(8,128)(2,1)S(1)}, bf16[32,4096]{1,0:T(8,128)(2,1)S(1)}, u32[]{:S(2)}, u32[]{:S(2)}) collective-permute-start(bf16[32,4096]{1,0:T(8,128)(2,1)S(1)} %collective-permute-done.11.refs_0_), channel_id=1, source_target_pairs={{0,16},{1,17},{2,18},{3,19},{4,20},{5,21},{6,22},{7,23},{8,24},{9,... | collective-permute-start | bytes 786440 | tf_op jit(solution)/shard_map/cross_p/ppermute | solution.py:64
  33.8 8.8 %collective-permute-start.13 = (bf16[32,4096]{1,0:T(8,128)(2,1)S(1)}, bf16[32,4096]{1,0:T(8,128)(2,1)S(1)}, u32[]{:S(2)}, u32[]{:S(2)}) collective-permute-start(bf16[32,4096]{1,0:T(8,128)(2,1)S(1)} %collective-permute-done.11.refs_0_), channel_id=1, source_target_pairs={{0,2},{1,3},{2,0},{3,1},{4,6},{5,7},{6,4},{7,5},{8,10},{9,11},{10,... | collective-permute-start | bytes 786440 | tf_op jit(solution)/shard_map/cross_x/ppermute | solution.py:64
  41.1 1.5 %collective-permute-start.14 = (bf16[32,4096]{1,0:T(8,128)(2,1)S(1)}, bf16[32,4096]{1,0:T(8,128)(2,1)S(1)}, u32[]{:S(2)}, u32[]{:S(2)}) collective-permute-start(bf16[32,4096]{1,0:T(8,128)(2,1)S(1)} %collective-permute-done.12.refs_1_), channel_id=1, source_target_pairs={{0,2},{1,3},{2,0},{3,1},{4,6},{5,7},{6,4},{7,5},{8,10},{9,11},{10,... | collective-permute-start | bytes 786440 | tf_op jit(solution)/shard_map/cross_px/ppermute | solution.py:64
  41.1 9.1 %collective-permute-start.10 = (bf16[128,1024]{1,0:T(8,128)(2,1)S(1)}, bf16[128,1024]{1,0:T(8,128)(2,1)S(1)}, u32[]{:S(2)}, u32[]{:S(2)}) collective-permute-start(bf16[128,1024]{1,0:T(8,128)(2,1)S(1)} %get-tuple-element.30), channel_id=1, source_target_pairs={{0,1},{1,0},{2,3},{3,2},{4,5},{5,4},{6,7},{7,6},{8,9},{9,8},{10,11... | collective-permute-start | bytes 786440 | tf_op jit(solution)/shard_map/got0/ppermute | solution.py:64
  45.0 10.4 %collective-permute-start.15 = (bf16[128,1024]{1,0:T(8,128)(2,1)S(1)}, bf16[128,1024]{1,0:T(8,128)(2,1)S(1)}, u32[]{:S(2)}, u32[]{:S(2)}) collective-permute-start(bf16[128,1024]{1,0:T(8,128)(2,1)S(1)} %get-tuple-element.34), channel_id=1, source_target_pairs={{0,1},{1,0},{2,3},{3,2},{4,5},{5,4},{6,7},{7,6},{8,9},{9,8},{10,11... | collective-permute-start | bytes 786440 | tf_op jit(solution)/shard_map/got1/ppermute | solution.py:64

commit v4 on v3

--- a/solution.py
+++ b/solution.py
@@ -113,11 +113,11 @@
     return lefts, split(jnp.where(block, tiled, 0.0), 2)
 
 
-def precond_rows(q_ref, lefts, rights, out, base):
+def precond_rows(q_ref, lefts, rights, out):
     for at in range(0, q_ref.shape[0], CHUNK):
         values = precond_chunk(q_ref[at : at + CHUNK, :], lefts, rights)
         for t, value in enumerate(values):
-            out[base + at : base + at + CHUNK, t * 256 : (t + 1) * 256] = value
+            out[at : at + CHUNK, t * 256 : (t + 1) * 256] = value
 
 
 def precond_chunk(q, lefts, rights):
@@ -165,7 +165,7 @@
         lefts_ref[k] = lefts[k]
         rights_ref[k] = rights[k]
     copies[2].wait()
-    precond_rows(q_ref, lefts, rights, mine, 0)
+    precond_rows(q_ref, lefts, rights, mine)
 
 
 def rest_kernel(
@@ -182,7 +182,7 @@
     weight[...] = jnp.full(weight.shape, weight_ref[layer_ref[0]])
     lefts, rights = [lefts_ref[0], lefts_ref[1]], [rights_ref[0], rights_ref[1]]
     q_copy.wait()
-    precond_rows(q_ref, lefts, rights, rest, 0)
+    precond_rows(q_ref, lefts, rights, rest)
     for copy in copies:
         copy.wait()
 
@@ -275,13 +275,14 @@
     train_ids,
     query_ids,
 ):
-    train, queries = train_grads[:, 0, :], query_grads[:, 0, :]
+    in_hbm = lambda array: pltpu.with_memory_space_constraint(array, pltpu.HBM)
+    train, queries = in_hbm(train_grads[:, 0, :]), in_hbm(query_grads[:, 0, :])
     width, side = queries.shape[1], left_factor.shape[1]
     shape = jax.ShapeDtypeStruct
     mine, lefts, rights = kernel_call(
         own_kernel,
         [shape((HALF, width), bf16), shape((2, 256, 256), bf16), shape((2, 256, 512), bf16)],
-        [queries, left_factor[0], right_factor[0]],
+        [queries, in_hbm(left_factor[0]), in_hbm(right_factor[0])],
         [HBM] * 3,
         [
             pltpu.VMEM((HALF, width), bf16),
@@ -295,12 +296,14 @@
     rest, train, weight = kernel_call(
         rest_kernel,
         [shape((HALF, width), bf16), shape(train.shape, bf16), shape((8, STEP), f32)],
-        [layer_weight, layer_of, queries, train, lefts, rights],
+        [in_hbm(layer_weight), layer_of, queries, train, lefts, rights],
         [SMEM, SMEM, HBM, HBM, VMEM, VMEM],
         [pltpu.VMEM((HALF, width), bf16), pltpu.SemaphoreType.DMA((1 + train.shape[0] // STEP,))],
     )
     score = functools.partial(call_scores, weight, train)
-    whole = lambda *pieces: [(piece, ((0, HALF),)) for piece in pieces]
+
+    def rows_of(*pieces):
+        return [(piece, ((0, piece.shape[0]),)) for piece in pieces]
 
     mine_x = to_core(mine, "mine_x")
     rest_x = to_core(rest, "rest_x")
@@ -311,21 +314,25 @@
     far_p = to_part(far, "far_p")
     far_x = to_core(far, "far_x")
     rest_x = after(rest_x, far)
-    (early0,) = score(whole(mine, rest, mine_x, rest_x), stored=128)
+    (early0,) = score(rows_of(mine, rest, mine_x, rest_x), stored=128)
     near_p = after(near_p, early0)
     near_px = to_core(near_p, "near_px")
     far_px = to_core(far_p, "far_px")
     cross_p = to_part(cross, "cross_p")
     cross_x = to_core(cross, "cross_x")
     early1, send0, keep0 = score(
-        whole(near, near_p, near_x, near_px, far, far_p, far_x, far_px),
+        rows_of(near, near_p, near_x, near_px, far, far_p, far_x, far_px),
         stored=128,
         early=[(early0, 0, 128)],
     )
     got0 = to_layer(send0, "got0")
     cross_p = after(cross_p, send0)
-    cross_px = to_core(cross_p, "cross_px")
-    send1, keep1 = score(whole(cross, cross_p, cross_x, cross_px), early=[(early1, 0, 128)])
+    cross_pxa = to_core(cross_p[:CHUNK], "cross_pxa")
+    cross_pxb = to_core(cross_p[CHUNK:], "cross_pxb")
+    send1, keep1 = score(
+        rows_of(cross, cross_p, cross_x, cross_pxa, cross_pxb), early=[(early1, 0, 128)]
+    )
+    send1 = after(send1, got0)
     got1 = to_layer(send1, "got1")
     return kernel_call(
         functools.partial(final_kernel, groups=((0, 0, HALF), (1, 0, HALF))),

time: 56.9 us -> 50.5 us (0.89)
  local copies, waits for them, and re-layouts: 6.73 us -> 0.16 us
  Pallas kernels: 13.5 us -> 15.6 us
  waiting for transfers between devices: 20.5 us -> 18.7 us
    unnamed x14 -> x4, local copies, waits for them, and re-layouts: 6.6 us -> 0.01 us
    pallas_call x6, Pallas kernels: 13.5 us -> 15.6 us  [kernel_call(): pl.pallas_call(kernel, out_shape=outs, in_specs=specs or [VMEM] * len(inp...]
    ppermute x16 -> x17, waiting for transfers between devices: 20.5 us -> 18.7 us  [permute(): return lax.ppermute(value, AXES, pairs)]
    ppermute x16 -> x17, starting transfers between devices: 15 us -> 15.1 us  [permute(): return lax.ppermute(value, AXES, pairs)]
  transfers between devices with their start and end apart: 16 -> 17, of which waited for: 6 -> 7; matrix products, arithmetic and copies ran while one was open for 0% -> 0% of each run, Pallas kernels for 18% -> 23%
where the time goes in v4:
time: 50.5 us; the launch traced here: 50.3 us
  waiting for transfers between devices  18.7 us (37%)
  Pallas kernels  15.6 us (31%)
  starting transfers between devices  15.1 us (30%)
  between operations  0.76 us (2%)
    ppermute x17, waiting for transfers between devices, permute(): return lax.ppermute(value, AXES, pairs)  18.7 us
    pallas_call x6, Pallas kernels, kernel_call(): pl.pallas_call(kernel, out_shape=outs, in_specs=specs or [VMEM] * len(inp...  15.6 us
    ppermute x17, starting transfers between devices, permute(): return lax.ppermute(value, AXES, pairs)  15.1 us
  transfers between devices with their start and end apart: 17, of which 7 were waited for; matrix products, arithmetic and copies ran while one was open for 0% of the time, Pallas kernels for 23%

profile of v4, /device:TPU:0, one launch (start us, length us, event | category | flops | bytes accessed | tf_op | source)
XLA Modules:
  0.0 50.3 jit_solution(10042377907397991)
XLA Ops:
  0.0 2.8 %shard_map.82 = (bf16[32,4096]{1,0:T(8,128)(2,1)S(1)}, bf16[2,256,256]{2,1,0:T(8,128)(2,1)S(1)}, bf16[2,256,512]{2,1,0:T(8,128)(2,1)S(1)}) custom-call(bf16[64,4096]{1,0:T(8,128)(2,1)} %bitcast.8, f32[64,64]{1,0:T(8,128)} %bitcast.10, f32[64,64]{1,0:T(8,128)} %bitcast.11), custom_call_target="tpu_custom_call" | custom-call | tf_op jit(solution)/shard_map/pallas_call | solution.py:221
  2.8 3.1 %collective-permute-start = (bf16[32,4096]{1,0:T(8,128)(2,1)S(1)}, bf16[32,4096]{1,0:T(8,128)(2,1)S(1)}, u32[]{:S(2)}, u32[]{:S(2)}) collective-permute-start(bf16[32,4096]{1,0:T(8,128)(2,1)S(1)} %get-tuple-element.25.refs_0_), channel_id=1, source_target_pairs={{0,4},{1,5},{2,6},{3,7},{4,0},{5,1},{6,2},{7,3},{8,12},{9,13},{10,... | collective-permute-start | bytes 786440 | tf_op jit(solution)/shard_map/near/ppermute | solution.py:64
  5.9 2.5 %collective-permute-start.4 = (bf16[32,4096]{1,0:T(8,128)(2,1)S(1)}, bf16[32,4096]{1,0:T(8,128)(2,1)S(1)}, u32[]{:S(2)}, u32[]{:S(2)}) collective-permute-start(bf16[32,4096]{1,0:T(8,128)(2,1)S(1)} %get-tuple-element.25.refs_0_), channel_id=1, source_target_pairs={{0,12},{1,13},{2,14},{3,15},{4,8},{5,9},{6,10},{7,11},{8,4},{9,5},... | collective-permute-start | bytes 786440 | tf_op jit(solution)/shard_map/far/ppermute | solution.py:64
  9.0 4.3 %shard_map.83 = (bf16[32,4096]{1,0:T(8,128)(2,1)S(1)}, bf16[1024,4096]{1,0:T(8,128)(2,1)S(1)}, f32[8,256]{1,0:T(8,128)S(1)}) custom-call(f32[2]{0:T(128)} %weight_ref.1, s32[1]{0:T(128)S(6)} %copy.10.layer_ref, bf16[64,4096]{1,0:T(8,128)(2,1)} %bitcast.9, bf16[1024,4096]{1,0:T(8,128)(2,1)} %bitcast.7, bf16[2,256,256]{2,1,0:T(8,128)(2,1)S(1)} %get-tuple-element.21.lefts_ref, ...), custom_call_target="tpu_custom_call" | custom-call | tf_op jit(solution)/shard_map/pallas_call | solution.py:221
  13.4 0.5 collective-permute-start.2
  13.9 1.5 %collective-permute-start.1 = (bf16[32,4096]{1,0:T(8,128)(2,1)S(1)}, bf16[32,4096]{1,0:T(8,128)(2,1)S(1)}, u32[]{:S(2)}, u32[]{:S(2)}) collective-permute-start(bf16[32,4096]{1,0:T(8,128)(2,1)S(1)} %collective-permute-done.refs_0_), channel_id=1, source_target_pairs={{0,16},{1,17},{2,18},{3,19},{4,20},{5,21},{6,22},{7,23},{8,24},{9,... | collective-permute-start | bytes 786440 | tf_op jit(solution)/shard_map/near_p/ppermute | solution.py:64
  15.4 4.7 %collective-permute-done.4.refs_4_ = bf16[32,4096]{1,0:T(8,128)(2,1)S(1)} collective-permute-done((bf16[32,4096]{1,0:T(8,128)(2,1)S(1)}, bf16[32,4096]{1,0:T(8,128)(2,1)S(1)}, u32[]{:S(2)}, u32[]{:S(2)}) %collective-permute-start.4) | collective-permute-done | bytes 262176 | tf_op jit(solution)/shard_map/far/ppermute | solution.py:64
  20.1 1.5 %collective-permute-start.7 = (bf16[32,4096]{1,0:T(8,128)(2,1)S(1)}, bf16[32,4096]{1,0:T(8,128)(2,1)S(1)}, u32[]{:S(2)}, u32[]{:S(2)}) collective-permute-start(bf16[32,4096]{1,0:T(8,128)(2,1)S(1)} %collective-permute-done.4.refs_4_), channel_id=1, source_target_pairs={{0,16},{1,17},{2,18},{3,19},{4,20},{5,21},{6,22},{7,23},{8,24},{9,... | collective-permute-start | bytes 786440 | tf_op jit(solution)/shard_map/far_p/ppermute | solution.py:64
  21.6 0.6 %collective-permute-start.11 = (bf16[32,4096]{1,0:T(8,128)(2,1)S(1)}, bf16[32,4096]{1,0:T(8,128)(2,1)S(1)}, u32[]{:S(2)}, u32[]{:S(2)}) collective-permute-start(bf16[32,4096]{1,0:T(8,128)(2,1)S(1)} %collective-permute-done.4.refs_4_), channel_id=1, source_target_pairs={{0,4},{1,5},{2,6},{3,7},{4,0},{5,1},{6,2},{7,3},{8,12},{9,13},{10,... | collective-permute-start | bytes 786440 | tf_op jit(solution)/shard_map/cross/ppermute | solution.py:64
  22.2 0.5 %collective-permute-start.5 = (bf16[32,4096]{1,0:T(8,128)(2,1)S(1)}, bf16[32,4096]{1,0:T(8,128)(2,1)S(1)}, u32[]{:S(2)}, u32[]{:S(2)}) collective-permute-start(bf16[32,4096]{1,0:T(8,128)(2,1)S(1)} %collective-permute-done.refs_0_), channel_id=1, source_target_pairs={{0,2},{1,3},{2,0},{3,1},{4,6},{5,7},{6,4},{7,5},{8,10},{9,11},{10,... | collective-permute-start | bytes 786440 | tf_op jit(solution)/shard_map/near_x/ppermute | solution.py:64
  22.7 2.4 %shard_map.84.refs_8_ = f32[128,1024]{1,0:T(8,128)S(1)} custom-call(f32[8,256]{1,0:T(8,128)S(1)} %get-tuple-element.23.weight_ref, bf16[1024,4096]{1,0:T(8,128)(2,1)S(1)} %get-tuple-element.24.train_ref, bf16[32,4096]{1,0:T(8,128)(2,1)S(1)} %get-tuple-element.25.refs_0_, bf16[32,4096]{1,0:T(8,128)(2,1)S(1)} %get-tuple-element.26.refs_1_, ...), custom_call_target="tpu_custom_call" | custom-call | tf_op jit(solution)/shard_map/pallas_call | solution.py:221
  25.3 2.5 %collective-permute-done.7.refs_5_ = bf16[32,4096]{1,0:T(8,128)(2,1)S(1)} collective-permute-done((bf16[32,4096]{1,0:T(8,128)(2,1)S(1)}, bf16[32,4096]{1,0:T(8,128)(2,1)S(1)}, u32[]{:S(2)}, u32[]{:S(2)}) %collective-permute-start.7) | collective-permute-done | bytes 262176 | tf_op jit(solution)/shard_map/far_p/ppermute | solution.py:64
  27.8 0.7 %collective-permute-done.11.refs_0_ = bf16[32,4096]{1,0:T(8,128)(2,1)S(1)} collective-permute-done((bf16[32,4096]{1,0:T(8,128)(2,1)S(1)}, bf16[32,4096]{1,0:T(8,128)(2,1)S(1)}, u32[]{:S(2)}, u32[]{:S(2)}) %collective-permute-start.11) | collective-permute-done | bytes 262176 | tf_op jit(solution)/shard_map/cross/ppermute | solution.py:64
  28.5 0.8 %collective-permute-start.12 = (bf16[32,4096]{1,0:T(8,128)(2,1)S(1)}, bf16[32,4096]{1,0:T(8,128)(2,1)S(1)}, u32[]{:S(2)}, u32[]{:S(2)}) collective-permute-start(bf16[32,4096]{1,0:T(8,128)(2,1)S(1)} %collective-permute-done.11.refs_0_), channel_id=1, source_target_pairs={{0,16},{1,17},{2,18},{3,19},{4,20},{5,21},{6,22},{7,23},{8,24},{9,... | collective-permute-start | bytes 786440 | tf_op jit(solution)/shard_map/cross_p/ppermute | solution.py:64
  29.3 0.2 collective-permute-start.13
  29.5 2.5 %shard_map.85 = (f32[128,1024]{1,0:T(8,128)S(1)}, bf16[128,1024]{1,0:T(8,128)(2,1)S(1)}, f32[128,1024]{1,0:T(8,128)S(1)}) custom-call(f32[8,256]{1,0:T(8,128)S(1)} %get-tuple-element.23.weight_ref, bf16[1024,4096]{1,0:T(8,128)(2,1)S(1)} %get-tuple-element.24.train_ref, bf16[32,4096]{1,0:T(8,128)(2,1)S(1)} %collective-permute-done.refs_0_, ...), custom_call_target="tpu_custom_call" | custom-call | tf_op jit(solution)/shard_map/pallas_call | solution.py:221
  32.1 1.6 %collective-permute-start.10 = (bf16[128,1024]{1,0:T(8,128)(2,1)S(1)}, bf16[128,1024]{1,0:T(8,128)(2,1)S(1)}, u32[]{:S(2)}, u32[]{:S(2)}) collective-permute-start(bf16[128,1024]{1,0:T(8,128)(2,1)S(1)} %get-tuple-element.31), channel_id=1, source_target_pairs={{0,1},{1,0},{2,3},{3,2},{4,5},{5,4},{6,7},{7,6},{8,9},{9,8},{10,11... | collective-permute-start | bytes 786440 | tf_op jit(solution)/shard_map/got0/ppermute | solution.py:64
  33.7 2.9 %collective-permute-done.12.refs_1_ = bf16[32,4096]{1,0:T(8,128)(2,1)S(1)} collective-permute-done((bf16[32,4096]{1,0:T(8,128)(2,1)S(1)}, bf16[32,4096]{1,0:T(8,128)(2,1)S(1)}, u32[]{:S(2)}, u32[]{:S(2)}) %collective-permute-start.12) | collective-permute-done | bytes 262176 | tf_op jit(solution)/shard_map/cross_p/ppermute | solution.py:64
  36.6 0.5 collective-permute-start.15
  37.1 0.8 %collective-permute-done.14.refs_3_ = bf16[16,4096]{1,0:T(8,128)(2,1)S(1)} collective-permute-done((bf16[16,4096]{1,0:T(8,128)(2,1)S(1)}, bf16[16,4096]{1,0:T(8,128)(2,1)S(1)}, u32[]{:S(2)}, u32[]{:S(2)}) %collective-permute-start.14) | collective-permute-done | bytes 131104 | tf_op jit(solution)/shard_map/cross_pxa/ppermute | solution.py:64
  38.1 2.4 %shard_map.86 = (bf16[128,1024]{1,0:T(8,128)(2,1)S(1)}, f32[128,1024]{1,0:T(8,128)S(1)}) custom-call(f32[8,256]{1,0:T(8,128)S(1)} %get-tuple-element.23.weight_ref, bf16[1024,4096]{1,0:T(8,128)(2,1)S(1)} %get-tuple-element.24.train_ref, bf16[32,4096]{1,0:T(8,128)(2,1)S(1)} %collective-permute-done.11.refs_0_, ...), custom_call_target="tpu_custom_call" | custom-call | tf_op jit(solution)/shard_map/pallas_call | solution.py:221
  40.6 1.6 %collective-permute-start.16 = (bf16[128,1024]{1,0:T(8,128)(2,1)S(1)}, bf16[128,1024]{1,0:T(8,128)(2,1)S(1)}, u32[]{:S(2)}, u32[]{:S(2)}) collective-permute-start(bf16[128,1024]{1,0:T(8,128)(2,1)S(1)} %get-tuple-element.36), channel_id=1, source_target_pairs={{0,1},{1,0},{2,3},{3,2},{4,5},{5,4},{6,7},{7,6},{8,9},{9,8},{10,11... | collective-permute-start | bytes 786440 | tf_op jit(solution)/shard_map/got1/ppermute | solution.py:64
  42.3 6.9 %collective-permute-done.16.refs_3_ = bf16[128,1024]{1,0:T(8,128)(2,1)S(1)} collective-permute-done((bf16[128,1024]{1,0:T(8,128)(2,1)S(1)}, bf16[128,1024]{1,0:T(8,128)(2,1)S(1)}, u32[]{:S(2)}, u32[]{:S(2)}) %collective-permute-start.16) | collective-permute-done | bytes 262176 | tf_op jit(solution)/shard_map/got1/ppermute | solution.py:64
  49.2 1.1 %shard_map.87 = f32[256,1024]{1,0:T(8,128)} custom-call(s32[1,1024]{1,0:T(1,128)S(1)} %bitcast.6, s32[256,1]{1,0:T(8,128)S(1)} %copy.9.query_ids, f32[128,1024]{1,0:T(8,128)S(1)} %get-tuple-element.30.refs_0_, bf16[128,1024]{1,0:T(8,128)(2,1)S(1)} %collective-permute-done.10.refs_1_, f32[128,1024]{1,0:T(8,128)S(1)} %get-tuple-element.34.refs_2_, ...), custom_call_target="tpu_custom_call" | custom-call | tf_op jit(solution)/shard_map/pallas_call | solution.py:221
  (22 shorter events, 0.7 us)
Async XLA Ops:
  2.8 11.1 %collective-permute-start = (bf16[32,4096]{1,0:T(8,128)(2,1)S(1)}, bf16[32,4096]{1,0:T(8,128)(2,1)S(1)}, u32[]{:S(2)}, u32[]{:S(2)}) collective-permute-start(bf16[32,4096]{1,0:T(8,128)(2,1)S(1)} %get-tuple-element.25.refs_0_), channel_id=1, source_target_pairs={{0,4},{1,5},{2,6},{3,7},{4,0},{5,1},{6,2},{7,3},{8,12},{9,13},{10,... | collective-permute-start | bytes 786440 | tf_op jit(solution)/shard_map/near/ppermute | solution.py:64
  5.9 14.2 %collective-permute-start.4 = (bf16[32,4096]{1,0:T(8,128)(2,1)S(1)}, bf16[32,4096]{1,0:T(8,128)(2,1)S(1)}, u32[]{:S(2)}, u32[]{:S(2)}) collective-permute-start(bf16[32,4096]{1,0:T(8,128)(2,1)S(1)} %get-tuple-element.25.refs_0_), channel_id=1, source_target_pairs={{0,12},{1,13},{2,14},{3,15},{4,8},{5,9},{6,10},{7,11},{8,4},{9,5},... | collective-permute-start | bytes 786440 | tf_op jit(solution)/shard_map/far/ppermute | solution.py:64
  13.3 8.9 %collective-permute-start.3 = (bf16[32,4096]{1,0:T(8,128)(2,1)S(1)}, bf16[32,4096]{1,0:T(8,128)(2,1)S(1)}, u32[]{:S(2)}, u32[]{:S(2)}) collective-permute-start(bf16[32,4096]{1,0:T(8,128)(2,1)S(1)} %get-tuple-element.26.refs_1_), channel_id=1, source_target_pairs={{0,2},{1,3},{2,0},{3,1},{4,6},{5,7},{6,4},{7,5},{8,10},{9,11},{10,... | collective-permute-start | bytes 786440 | tf_op jit(solution)/shard_map/rest_x/ppermute | solution.py:64
  13.4 8.8 %collective-permute-start.2 = (bf16[32,4096]{1,0:T(8,128)(2,1)S(1)}, bf16[32,4096]{1,0:T(8,128)(2,1)S(1)}, u32[]{:S(2)}, u32[]{:S(2)}) collective-permute-start(bf16[32,4096]{1,0:T(8,128)(2,1)S(1)} %get-tuple-element.25.refs_0_), channel_id=1, source_target_pairs={{0,2},{1,3},{2,0},{3,1},{4,6},{5,7},{6,4},{7,5},{8,10},{9,11},{10,... | collective-permute-start | bytes 786440 | tf_op jit(solution)/shard_map/mine_x/ppermute | solution.py:64
  13.9 11.3 %collective-permute-start.1 = (bf16[32,4096]{1,0:T(8,128)(2,1)S(1)}, bf16[32,4096]{1,0:T(8,128)(2,1)S(1)}, u32[]{:S(2)}, u32[]{:S(2)}) collective-permute-start(bf16[32,4096]{1,0:T(8,128)(2,1)S(1)} %collective-permute-done.refs_0_), channel_id=1, source_target_pairs={{0,16},{1,17},{2,18},{3,19},{4,20},{5,21},{6,22},{7,23},{8,24},{9,... | collective-permute-start | bytes 786440 | tf_op jit(solution)/shard_map/near_p/ppermute | solution.py:64
  20.1 7.7 %collective-permute-start.7 = (bf16[32,4096]{1,0:T(8,128)(2,1)S(1)}, bf16[32,4096]{1,0:T(8,128)(2,1)S(1)}, u32[]{:S(2)}, u32[]{:S(2)}) collective-permute-start(bf16[32,4096]{1,0:T(8,128)(2,1)S(1)} %collective-permute-done.4.refs_4_), channel_id=1, source_target_pairs={{0,16},{1,17},{2,18},{3,19},{4,20},{5,21},{6,22},{7,23},{8,24},{9,... | collective-permute-start | bytes 786440 | tf_op jit(solution)/shard_map/far_p/ppermute | solution.py:64
  21.6 6.8 %collective-permute-start.11 = (bf16[32,4096]{1,0:T(8,128)(2,1)S(1)}, bf16[32,4096]{1,0:T(8,128)(2,1)S(1)}, u32[]{:S(2)}, u32[]{:S(2)}) collective-permute-start(bf16[32,4096]{1,0:T(8,128)(2,1)S(1)} %collective-permute-done.4.refs_4_), channel_id=1, source_target_pairs={{0,4},{1,5},{2,6},{3,7},{4,0},{5,1},{6,2},{7,3},{8,12},{9,13},{10,... | collective-permute-start | bytes 786440 | tf_op jit(solution)/shard_map/cross/ppermute | solution.py:64
  22.2 7.1 %collective-permute-start.8 = (bf16[32,4096]{1,0:T(8,128)(2,1)S(1)}, bf16[32,4096]{1,0:T(8,128)(2,1)S(1)}, u32[]{:S(2)}, u32[]{:S(2)}) collective-permute-start(bf16[32,4096]{1,0:T(8,128)(2,1)S(1)} %collective-permute-done.4.refs_4_), channel_id=1, source_target_pairs={{0,2},{1,3},{2,0},{3,1},{4,6},{5,7},{6,4},{7,5},{8,10},{9,11},{10,... | collective-permute-start | bytes 786440 | tf_op jit(solution)/shard_map/far_x/ppermute | solution.py:64
  22.2 7.3 %collective-permute-start.5 = (bf16[32,4096]{1,0:T(8,128)(2,1)S(1)}, bf16[32,4096]{1,0:T(8,128)(2,1)S(1)}, u32[]{:S(2)}, u32[]{:S(2)}) collective-permute-start(bf16[32,4096]{1,0:T(8,128)(2,1)S(1)} %collective-permute-done.refs_0_), channel_id=1, source_target_pairs={{0,2},{1,3},{2,0},{3,1},{4,6},{5,7},{6,4},{7,5},{8,10},{9,11},{10,... | collective-permute-start | bytes 786440 | tf_op jit(solution)/shard_map/near_x/ppermute | solution.py:64
  25.1 17.1 %copy-start.1 = (s32[256]{0:T(256)S(1)}, s32[256]{0:T(256)}, u32[]{:S(2)}) copy-start(s32[256]{0:T(256)} %param.15) | copy-start | bytes 3076
  25.1 24.0 %copy-start = (s32[1024]{0:T(1024)S(1)}, s32[1024]{0:T(1024)}, u32[]{:S(2)}) copy-start(s32[1024]{0:T(1024)} %param.14) | copy-start | bytes 12292
  25.2 4.4 %collective-permute-start.6 = (bf16[32,4096]{1,0:T(8,128)(2,1)S(1)}, bf16[32,4096]{1,0:T(8,128)(2,1)S(1)}, u32[]{:S(2)}, u32[]{:S(2)}) collective-permute-start(bf16[32,4096]{1,0:T(8,128)(2,1)S(1)} %collective-permute-done.1.refs_1_), channel_id=1, source_target_pairs={{0,2},{1,3},{2,0},{3,1},{4,6},{5,7},{6,4},{7,5},{8,10},{9,11},{10,... | collective-permute-start | bytes 786440 | tf_op jit(solution)/shard_map/near_px/ppermute | solution.py:64
  27.8 1.7 %collective-permute-start.9 = (bf16[32,4096]{1,0:T(8,128)(2,1)S(1)}, bf16[32,4096]{1,0:T(8,128)(2,1)S(1)}, u32[]{:S(2)}, u32[]{:S(2)}) collective-permute-start(bf16[32,4096]{1,0:T(8,128)(2,1)S(1)} %collective-permute-done.7.refs_5_), channel_id=1, source_target_pairs={{0,2},{1,3},{2,0},{3,1},{4,6},{5,7},{6,4},{7,5},{8,10},{9,11},{10,... | collective-permute-start | bytes 786440 | tf_op jit(solution)/shard_map/far_px/ppermute | solution.py:64
  28.5 8.1 %collective-permute-start.12 = (bf16[32,4096]{1,0:T(8,128)(2,1)S(1)}, bf16[32,4096]{1,0:T(8,128)(2,1)S(1)}, u32[]{:S(2)}, u32[]{:S(2)}) collective-permute-start(bf16[32,4096]{1,0:T(8,128)(2,1)S(1)} %collective-permute-done.11.refs_0_), channel_id=1, source_target_pairs={{0,16},{1,17},{2,18},{3,19},{4,20},{5,21},{6,22},{7,23},{8,24},{9,... | collective-permute-start | bytes 786440 | tf_op jit(solution)/shard_map/cross_p/ppermute | solution.py:64
  29.3 7.8 %collective-permute-start.13 = (bf16[32,4096]{1,0:T(8,128)(2,1)S(1)}, bf16[32,4096]{1,0:T(8,128)(2,1)S(1)}, u32[]{:S(2)}, u32[]{:S(2)}) collective-permute-start(bf16[32,4096]{1,0:T(8,128)(2,1)S(1)} %collective-permute-done.11.refs_0_), channel_id=1, source_target_pairs={{0,2},{1,3},{2,0},{3,1},{4,6},{5,7},{6,4},{7,5},{8,10},{9,11},{10,... | collective-permute-start | bytes 786440 | tf_op jit(solution)/shard_map/cross_x/ppermute | solution.py:64
  32.1 8.6 %collective-permute-start.10 = (bf16[128,1024]{1,0:T(8,128)(2,1)S(1)}, bf16[128,1024]{1,0:T(8,128)(2,1)S(1)}, u32[]{:S(2)}, u32[]{:S(2)}) collective-permute-start(bf16[128,1024]{1,0:T(8,128)(2,1)S(1)} %get-tuple-element.31), channel_id=1, source_target_pairs={{0,1},{1,0},{2,3},{3,2},{4,5},{5,4},{6,7},{7,6},{8,9},{9,8},{10,11... | collective-permute-start | bytes 786440 | tf_op jit(solution)/shard_map/got0/ppermute | solution.py:64
  36.5 1.4 %collective-permute-start.14 = (bf16[16,4096]{1,0:T(8,128)(2,1)S(1)}, bf16[16,4096]{1,0:T(8,128)(2,1)S(1)}, u32[]{:S(2)}, u32[]{:S(2)}) collective-permute-start(bf16[16,4096]{1,0:T(8,128)(2,1)S(1)} %get-tuple-element.38), channel_id=1, source_target_pairs={{0,2},{1,3},{2,0},{3,1},{4,6},{5,7},{6,4},{7,5},{8,10},{9,11},{10,... | collective-permute-start | bytes 393224 | tf_op jit(solution)/shard_map/cross_pxa/ppermute | solution.py:64
  36.6 1.5 %collective-permute-start.15 = (bf16[16,4096]{1,0:T(8,128)(2,1)S(1)}, bf16[16,4096]{1,0:T(8,128)(2,1)S(1)}, u32[]{:S(2)}, u32[]{:S(2)}) collective-permute-start(bf16[16,4096]{1,0:T(8,128)(2,1)S(1)} %get-tuple-element.37), channel_id=1, source_target_pairs={{0,2},{1,3},{2,0},{3,1},{4,6},{5,7},{6,4},{7,5},{8,10},{9,11},{10,... | collective-permute-start | bytes 393224 | tf_op jit(solution)/shard_map/cross_pxb/ppermute | solution.py:64
  40.6 8.6 %collective-permute-start.16 = (bf16[128,1024]{1,0:T(8,128)(2,1)S(1)}, bf16[128,1024]{1,0:T(8,128)(2,1)S(1)}, u32[]{:S(2)}, u32[]{:S(2)}) collective-permute-start(bf16[128,1024]{1,0:T(8,128)(2,1)S(1)} %get-tuple-element.36), channel_id=1, source_target_pairs={{0,1},{1,0},{2,3},{3,2},{4,5},{5,4},{6,7},{7,6},{8,9},{9,8},{10,11... | collective-permute-start | bytes 786440 | tf_op jit(solution)/shard_map/got1/ppermute | solution.py:64

commit v5 on v4

--- a/solution.py
+++ b/solution.py
@@ -246,23 +246,22 @@
     )
 
 
-def final_kernel(train_ids, query_ids, *refs, groups):
+def final_kernel(train_ids, query_ids, *refs):
     out = refs[-1]
     part, z, core, layer = place()
     low = z % 2
     first = jnp.where(z // 2 == layer, low, 1 - low)
     ids = train_ids[...]
-    for k, (block, start, rows) in enumerate(groups):
+    for k in range(4):
         keep, got = refs[2 * k], refs[2 * k + 1]
-        block = first if block == 0 else 1 - first
-        for i in range(4):
-            c = core if i < 2 else 1 - core
-            h = part if i % 2 == 0 else 1 - part
-            at = pl.multiple_of(((block * 2 + c) * 2 + h) * HALF + start, CHUNK)
-            here = slice(i * rows, (i + 1) * rows)
+        block = first if k < 2 else 1 - first
+        half = part if k % 2 == 0 else 1 - part
+        for i, c in enumerate((core, 1 - core)):
+            at = pl.multiple_of(((block * 2 + c) * 2 + half) * HALF, HALF)
+            here = slice(i * HALF, (i + 1) * HALF)
             total = keep[here, :] + got[here, :].astype(f32)
-            same = query_ids[pl.ds(at, rows), :] == ids
-            out[pl.ds(at, rows), :] = jnp.where(same, jnp.float32(0.0), total)
+            same = query_ids[pl.ds(at, HALF), :] == ids
+            out[pl.ds(at, HALF), :] = jnp.where(same, jnp.float32(0.0), total)
 
 
 def small(
@@ -307,37 +306,49 @@
 
     mine_x = to_core(mine, "mine_x")
     rest_x = to_core(rest, "rest_x")
+    near = after(near, rest)
     near_x = to_core(near, "near_x")
     near_p = to_part(near, "near_p")
     far = after(far, near)
     cross = to_near(far, "cross")
     far_p = to_part(far, "far_p")
-    far_x = to_core(far, "far_x")
-    rest_x = after(rest_x, far)
-    (early0,) = score(rows_of(mine, rest, mine_x, rest_x), stored=128)
-    near_p = after(near_p, early0)
+    far_xa = to_core(far[:CHUNK], "far_xa")
+    far_xb = to_core(far[CHUNK:], "far_xb")
+    early0, send0, keep0 = score(
+        rows_of(mine, mine_x, rest, rest_x, far, far_xa, far_xb), stored=128, early=[(None, 0, 64)]
+    )
+    got0 = to_layer(send0, "got0")
+
+    near_p = after(near_p, send0)
     near_px = to_core(near_p, "near_px")
-    far_px = to_core(far_p, "far_px")
-    cross_p = to_part(cross, "cross_p")
-    cross_x = to_core(cross, "cross_x")
-    early1, send0, keep0 = score(
-        rows_of(near, near_p, near_x, near_px, far, far_p, far_x, far_px),
+    far_pxa = to_core(far_p[:CHUNK], "far_pxa")
+    far_pxb = to_core(far_p[CHUNK:], "far_pxb")
+    cross_pa = to_part(cross[:CHUNK], "cross_pa")
+    cross_pb = to_near(far_p[CHUNK:], "cross_pb")
+    cross_xa = to_core(cross[:CHUNK], "cross_xa")
+    cross_xb = to_core(cross[CHUNK:], "cross_xb")
+    early1, send1, keep1 = score(
+        rows_of(near, near_x, near_p, near_px, far_p, far_pxa, far_pxb),
         stored=128,
-        early=[(early0, 0, 128)],
-    )
-    got0 = to_layer(send0, "got0")
-    cross_p = after(cross_p, send0)
-    cross_pxa = to_core(cross_p[:CHUNK], "cross_pxa")
-    cross_pxb = to_core(cross_p[CHUNK:], "cross_pxb")
-    send1, keep1 = score(
-        rows_of(cross, cross_p, cross_x, cross_pxa, cross_pxb), early=[(early1, 0, 128)]
-    )
-    send1 = after(send1, got0)
+        early=[(early0, 64, 64)],
+    )
     got1 = to_layer(send1, "got1")
+
+    send2, keep2 = score(rows_of(cross, cross_xa, cross_xb), early=[(early1, 0, 64)])
+    got2 = to_layer(send2, "got2")
+
+    cross_pa, cross_pb = after(cross_pa, send2, got0), after(cross_pb, send2, got0)
+    cross_pxa = to_core(cross_pa, "cross_pxa")
+    cross_pxb = to_core(cross_pb, "cross_pxb")
+    send3, keep3 = score(
+        rows_of(cross_pa, cross_pb, cross_pxa, cross_pxb), early=[(early1, 64, 64)]
+    )
+    send3 = after(send3, got1)
+    got3 = to_layer(send3, "got3")
     return kernel_call(
-        functools.partial(final_kernel, groups=((0, 0, HALF), (1, 0, HALF))),
+        final_kernel,
         shape((query_ids.shape[0], train_ids.shape[0]), f32),
-        [train_ids[None, :], query_ids[:, None], keep0, got0, keep1, got1],
+        [train_ids[None, :], query_ids[:, None], keep0, got0, keep1, got1, keep2, got2, keep3, got3],
     )
 
 

time: 50.5 us -> 52.8 us (1.046)
  Pallas kernels: 15.6 us -> 18 us
  waiting for transfers between devices: 18.7 us -> 16.4 us
  starting transfers between devices: 15.1 us -> 17.3 us
    pallas_call x6 -> x7, Pallas kernels: 15.6 us -> 18 us  [kernel_call(): pl.pallas_call(kernel, out_shape=outs, in_specs=specs or [VMEM] * len(inp...]
    ppermute x17 -> x23, waiting for transfers between devices: 18.7 us -> 16.4 us  [permute(): return lax.ppermute(value, AXES, pairs)]
    ppermute x17 -> x23, starting transfers between devices: 15.1 us -> 17.3 us  [permute(): return lax.ppermute(value, AXES, pairs)]
  transfers between devices with their start and end apart: 17 -> 23, of which waited for: 7 -> 7; matrix products, arithmetic and copies ran while one was open for 0% -> 0% of each run, Pallas kernels for 23% -> 27%
where the time goes in v5:
time: 52.8 us; the launch traced here: 52.7 us
  Pallas kernels  18 us (34%)
  starting transfers between devices  17.3 us (33%)
  waiting for transfers between devices  16.4 us (31%)
  between operations  0.85 us (2%)
    pallas_call x7, Pallas kernels, kernel_call(): pl.pallas_call(kernel, out_shape=outs, in_specs=specs or [VMEM] * len(inp...  18 us
    ppermute x23, starting transfers between devices, permute(): return lax.ppermute(value, AXES, pairs)  17.3 us
    ppermute x23, waiting for transfers between devices, permute(): return lax.ppermute(value, AXES, pairs)  16.4 us
  transfers between devices with their start and end apart: 23, of which 7 were waited for; matrix products, arithmetic and copies ran while one was open for 0% of the time, Pallas kernels for 27%

profile of v5, /device:TPU:0, one launch (start us, length us, event | category | flops | bytes accessed | tf_op | source)
XLA Modules:
  0.0 52.7 jit_solution(15560600424119902029)
XLA Ops:
  0.0 2.8 %shard_map.82 = (bf16[32,4096]{1,0:T(8,128)(2,1)S(1)}, bf16[2,256,256]{2,1,0:T(8,128)(2,1)S(1)}, bf16[2,256,512]{2,1,0:T(8,128)(2,1)S(1)}) custom-call(bf16[64,4096]{1,0:T(8,128)(2,1)} %bitcast.8, f32[64,64]{1,0:T(8,128)} %bitcast.10, f32[64,64]{1,0:T(8,128)} %bitcast.11), custom_call_target="tpu_custom_call" | custom-call | tf_op jit(solution)/shard_map/pallas_call | solution.py:221
  2.8 3.1 %collective-permute-start.3 = (bf16[32,4096]{1,0:T(8,128)(2,1)S(1)}, bf16[32,4096]{1,0:T(8,128)(2,1)S(1)}, u32[]{:S(2)}, u32[]{:S(2)}) collective-permute-start(bf16[32,4096]{1,0:T(8,128)(2,1)S(1)} %get-tuple-element.31.refs_0_), channel_id=1, source_target_pairs={{0,4},{1,5},{2,6},{3,7},{4,0},{5,1},{6,2},{7,3},{8,12},{9,13},{10,... | collective-permute-start | bytes 786440 | tf_op jit(solution)/shard_map/near/ppermute | solution.py:64
  5.9 2.5 %collective-permute-start.2 = (bf16[32,4096]{1,0:T(8,128)(2,1)S(1)}, bf16[32,4096]{1,0:T(8,128)(2,1)S(1)}, u32[]{:S(2)}, u32[]{:S(2)}) collective-permute-start(bf16[32,4096]{1,0:T(8,128)(2,1)S(1)} %get-tuple-element.31.refs_0_), channel_id=1, source_target_pairs={{0,12},{1,13},{2,14},{3,15},{4,8},{5,9},{6,10},{7,11},{8,4},{9,5},... | collective-permute-start | bytes 786440 | tf_op jit(solution)/shard_map/far/ppermute | solution.py:64
  9.0 4.3 %shard_map.83 = (bf16[32,4096]{1,0:T(8,128)(2,1)S(1)}, bf16[1024,4096]{1,0:T(8,128)(2,1)S(1)}, f32[8,256]{1,0:T(8,128)S(1)}) custom-call(f32[2]{0:T(128)} %weight_ref.1, s32[1]{0:T(128)S(6)} %copy.10.layer_ref, bf16[64,4096]{1,0:T(8,128)(2,1)} %bitcast.9, bf16[1024,4096]{1,0:T(8,128)(2,1)} %bitcast.7, bf16[2,256,256]{2,1,0:T(8,128)(2,1)S(1)} %get-tuple-element.27.lefts_ref, ...), custom_call_target="tpu_custom_call" | custom-call | tf_op jit(solution)/shard_map/pallas_call | solution.py:221
  13.3 0.6 %collective-permute-start.1 = (bf16[32,4096]{1,0:T(8,128)(2,1)S(1)}, bf16[32,4096]{1,0:T(8,128)(2,1)S(1)}, u32[]{:S(2)}, u32[]{:S(2)}) collective-permute-start(bf16[32,4096]{1,0:T(8,128)(2,1)S(1)} %get-tuple-element.32.refs_2_), channel_id=1, source_target_pairs={{0,2},{1,3},{2,0},{3,1},{4,6},{5,7},{6,4},{7,5},{8,10},{9,11},{10,... | collective-permute-start | bytes 786440 | tf_op jit(solution)/shard_map/rest_x/ppermute | solution.py:64
  13.9 1.5 %collective-permute-start.8 = (bf16[32,4096]{1,0:T(8,128)(2,1)S(1)}, bf16[32,4096]{1,0:T(8,128)(2,1)S(1)}, u32[]{:S(2)}, u32[]{:S(2)}) collective-permute-start(bf16[32,4096]{1,0:T(8,128)(2,1)S(1)} %collective-permute-done.3.refs_0_), channel_id=1, source_target_pairs={{0,16},{1,17},{2,18},{3,19},{4,20},{5,21},{6,22},{7,23},{8,24},{9,... | collective-permute-start | bytes 786440 | tf_op jit(solution)/shard_map/near_p/ppermute | solution.py:64
  15.4 4.7 %collective-permute-done.2.refs_4_ = bf16[32,4096]{1,0:T(8,128)(2,1)S(1)} collective-permute-done((bf16[32,4096]{1,0:T(8,128)(2,1)S(1)}, bf16[32,4096]{1,0:T(8,128)(2,1)S(1)}, u32[]{:S(2)}, u32[]{:S(2)}) %collective-permute-start.2) | collective-permute-done | bytes 262176 | tf_op jit(solution)/shard_map/far/ppermute | solution.py:64
  20.1 1.5 %collective-permute-start.10 = (bf16[32,4096]{1,0:T(8,128)(2,1)S(1)}, bf16[32,4096]{1,0:T(8,128)(2,1)S(1)}, u32[]{:S(2)}, u32[]{:S(2)}) collective-permute-start(bf16[32,4096]{1,0:T(8,128)(2,1)S(1)} %collective-permute-done.2.refs_4_), channel_id=1, source_target_pairs={{0,16},{1,17},{2,18},{3,19},{4,20},{5,21},{6,22},{7,23},{8,24},{9,... | collective-permute-start | bytes 786440 | tf_op jit(solution)/shard_map/far_p/ppermute | solution.py:64
  22.3 0.7 %collective-permute-done.4.refs_5_ = bf16[16,4096]{1,0:T(8,128)(2,1)S(1)} collective-permute-done((bf16[16,4096]{1,0:T(8,128)(2,1)S(1)}, bf16[16,4096]{1,0:T(8,128)(2,1)S(1)}, u32[]{:S(2)}, u32[]{:S(2)}) %collective-permute-start.4) | collective-permute-done | bytes 131104 | tf_op jit(solution)/shard_map/far_xa/ppermute | solution.py:64
  23.1 0.6 %collective-permute-start.14 = (bf16[32,4096]{1,0:T(8,128)(2,1)S(1)}, bf16[32,4096]{1,0:T(8,128)(2,1)S(1)}, u32[]{:S(2)}, u32[]{:S(2)}) collective-permute-start(bf16[32,4096]{1,0:T(8,128)(2,1)S(1)} %collective-permute-done.2.refs_4_), channel_id=1, source_target_pairs={{0,4},{1,5},{2,6},{3,7},{4,0},{5,1},{6,2},{7,3},{8,12},{9,13},{10,... | collective-permute-start | bytes 786440 | tf_op jit(solution)/shard_map/cross/ppermute | solution.py:64
  23.6 2.5 %shard_map.84 = (f32[128,1024]{1,0:T(8,128)S(1)}, bf16[64,1024]{1,0:T(8,128)(2,1)S(1)}, f32[64,1024]{1,0:T(8,128)S(1)}) custom-call(f32[8,256]{1,0:T(8,128)S(1)} %get-tuple-element.29.weight_ref, bf16[1024,4096]{1,0:T(8,128)(2,1)S(1)} %get-tuple-element.30.train_ref, bf16[32,4096]{1,0:T(8,128)(2,1)S(1)} %get-tuple-element.31.refs_0_, ...), custom_call_target="tpu_custom_call" | custom-call | tf_op jit(solution)/shard_map/pallas_call | solution.py:221
  26.2 1.6 %collective-permute-done.10.refs_4_ = bf16[32,4096]{1,0:T(8,128)(2,1)S(1)} collective-permute-done((bf16[32,4096]{1,0:T(8,128)(2,1)S(1)}, bf16[32,4096]{1,0:T(8,128)(2,1)S(1)}, u32[]{:S(2)}, u32[]{:S(2)}) %collective-permute-start.10) | collective-permute-done | bytes 262176 | tf_op jit(solution)/shard_map/far_p/ppermute | solution.py:64
  28.4 3.0 %collective-permute-done.14.refs_0_ = bf16[32,4096]{1,0:T(8,128)(2,1)S(1)} collective-permute-done((bf16[32,4096]{1,0:T(8,128)(2,1)S(1)}, bf16[32,4096]{1,0:T(8,128)(2,1)S(1)}, u32[]{:S(2)}, u32[]{:S(2)}) %collective-permute-start.14) | collective-permute-done | bytes 262176 | tf_op jit(solution)/shard_map/cross/ppermute | solution.py:64
  32.0 1.5 %collective-permute-start.6 = (bf16[64,1024]{1,0:T(8,128)(2,1)S(1)}, bf16[64,1024]{1,0:T(8,128)(2,1)S(1)}, u32[]{:S(2)}, u32[]{:S(2)}) collective-permute-start(bf16[64,1024]{1,0:T(8,128)(2,1)S(1)} %get-tuple-element.36), channel_id=1, source_target_pairs={{0,1},{1,0},{2,3},{3,2},{4,5},{5,4},{6,7},{7,6},{8,9},{9,8},{10,11... | collective-permute-start | bytes 393224 | tf_op jit(solution)/shard_map/got0/ppermute | solution.py:64
  33.5 0.6 %collective-permute-start.19 = (bf16[16,4096]{1,0:T(8,128)(2,1)S(1)}, bf16[16,4096]{1,0:T(8,128)(2,1)S(1)}, u32[]{:S(2)}, u32[]{:S(2)}) collective-permute-start(bf16[16,4096]{1,0:T(8,128)(2,1)S(1)} %get-tuple-element.51), channel_id=1, source_target_pairs={{0,4},{1,5},{2,6},{3,7},{4,0},{5,1},{6,2},{7,3},{8,12},{9,13},{10,... | collective-permute-start | bytes 393224 | tf_op jit(solution)/shard_map/cross_pb/ppermute | solution.py:64
  34.1 0.5 %collective-permute-start.18 = (bf16[16,4096]{1,0:T(8,128)(2,1)S(1)}, bf16[16,4096]{1,0:T(8,128)(2,1)S(1)}, u32[]{:S(2)}, u32[]{:S(2)}) collective-permute-start(bf16[16,4096]{1,0:T(8,128)(2,1)S(1)} %get-tuple-element.50), channel_id=1, source_target_pairs={{0,16},{1,17},{2,18},{3,19},{4,20},{5,21},{6,22},{7,23},{8,24},{9,... | collective-permute-start | bytes 393224 | tf_op jit(solution)/shard_map/cross_pa/ppermute | solution.py:64
  34.7 2.5 %shard_map.85 = (f32[128,1024]{1,0:T(8,128)S(1)}, bf16[64,1024]{1,0:T(8,128)(2,1)S(1)}, f32[64,1024]{1,0:T(8,128)S(1)}) custom-call(f32[8,256]{1,0:T(8,128)S(1)} %get-tuple-element.29.weight_ref, bf16[1024,4096]{1,0:T(8,128)(2,1)S(1)} %get-tuple-element.30.train_ref, bf16[32,4096]{1,0:T(8,128)(2,1)S(1)} %collective-permute-done.3.refs_0_, ...), custom_call_target="tpu_custom_call" | custom-call | tf_op jit(solution)/shard_map/pallas_call | solution.py:221
  37.2 2.4 %shard_map.86 = (bf16[64,1024]{1,0:T(8,128)(2,1)S(1)}, f32[64,1024]{1,0:T(8,128)S(1)}) custom-call(f32[8,256]{1,0:T(8,128)S(1)} %get-tuple-element.29.weight_ref, bf16[1024,4096]{1,0:T(8,128)(2,1)S(1)} %get-tuple-element.30.train_ref, bf16[32,4096]{1,0:T(8,128)(2,1)S(1)} %collective-permute-done.14.refs_0_, ...), custom_call_target="tpu_custom_call" | custom-call | tf_op jit(solution)/shard_map/pallas_call | solution.py:221
  40.7 1.5 %collective-permute-start.17 = (bf16[64,1024]{1,0:T(8,128)(2,1)S(1)}, bf16[64,1024]{1,0:T(8,128)(2,1)S(1)}, u32[]{:S(2)}, u32[]{:S(2)}) collective-permute-start(bf16[64,1024]{1,0:T(8,128)(2,1)S(1)} %get-tuple-element.43), channel_id=1, source_target_pairs={{0,1},{1,0},{2,3},{3,2},{4,5},{5,4},{6,7},{7,6},{8,9},{9,8},{10,11... | collective-permute-start | bytes 393224 | tf_op jit(solution)/shard_map/got2/ppermute | solution.py:64
  42.2 2.4 %shard_map.87 = (bf16[64,1024]{1,0:T(8,128)(2,1)S(1)}, f32[64,1024]{1,0:T(8,128)S(1)}) custom-call(f32[8,256]{1,0:T(8,128)S(1)} %get-tuple-element.29.weight_ref, bf16[1024,4096]{1,0:T(8,128)(2,1)S(1)} %get-tuple-element.30.train_ref, bf16[16,4096]{1,0:T(8,128)(2,1)S(1)} %collective-permute-done.18.refs_0_, ...), custom_call_target="tpu_custom_call" | custom-call | tf_op jit(solution)/shard_map/pallas_call | solution.py:221
  44.6 1.9 %collective-permute-done.13.refs_3_ = bf16[64,1024]{1,0:T(8,128)(2,1)S(1)} collective-permute-done((bf16[64,1024]{1,0:T(8,128)(2,1)S(1)}, bf16[64,1024]{1,0:T(8,128)(2,1)S(1)}, u32[]{:S(2)}, u32[]{:S(2)}) %collective-permute-start.13) | collective-permute-done | bytes 131104 | tf_op jit(solution)/shard_map/got1/ppermute | solution.py:64
  47.2 2.2 %collective-permute-done.17.refs_5_ = bf16[64,1024]{1,0:T(8,128)(2,1)S(1)} collective-permute-done((bf16[64,1024]{1,0:T(8,128)(2,1)S(1)}, bf16[64,1024]{1,0:T(8,128)(2,1)S(1)}, u32[]{:S(2)}, u32[]{:S(2)}) %collective-permute-start.17) | collective-permute-done | bytes 131104 | tf_op jit(solution)/shard_map/got2/ppermute | solution.py:64
  49.3 2.2 %collective-permute-done.22.refs_7_ = bf16[64,1024]{1,0:T(8,128)(2,1)S(1)} collective-permute-done((bf16[64,1024]{1,0:T(8,128)(2,1)S(1)}, bf16[64,1024]{1,0:T(8,128)(2,1)S(1)}, u32[]{:S(2)}, u32[]{:S(2)}) %collective-permute-start.22) | collective-permute-done | bytes 131104 | tf_op jit(solution)/shard_map/got3/ppermute | solution.py:64
  51.5 1.1 %shard_map.88 = f32[256,1024]{1,0:T(8,128)} custom-call(s32[1,1024]{1,0:T(1,128)S(1)} %bitcast.6, s32[256,1]{1,0:T(8,128)S(1)} %copy.9.query_ids, f32[64,1024]{1,0:T(8,128)S(1)} %get-tuple-element.35.refs_0_, bf16[64,1024]{1,0:T(8,128)(2,1)S(1)} %collective-permute-done.6.refs_1_, f32[64,1024]{1,0:T(8,128)S(1)} %get-tuple-element.39.refs_2_, ...), custom_call_target="tpu_custom_call" | custom-call | tf_op jit(solution)/shard_map/pallas_call | solution.py:221
  (37 shorter events, 3.7 us)
Async XLA Ops:
  2.8 11.1 %collective-permute-start.3 = (bf16[32,4096]{1,0:T(8,128)(2,1)S(1)}, bf16[32,4096]{1,0:T(8,128)(2,1)S(1)}, u32[]{:S(2)}, u32[]{:S(2)}) collective-permute-start(bf16[32,4096]{1,0:T(8,128)(2,1)S(1)} %get-tuple-element.31.refs_0_), channel_id=1, source_target_pairs={{0,4},{1,5},{2,6},{3,7},{4,0},{5,1},{6,2},{7,3},{8,12},{9,13},{10,... | collective-permute-start | bytes 786440 | tf_op jit(solution)/shard_map/near/ppermute | solution.py:64
  5.9 14.2 %collective-permute-start.2 = (bf16[32,4096]{1,0:T(8,128)(2,1)S(1)}, bf16[32,4096]{1,0:T(8,128)(2,1)S(1)}, u32[]{:S(2)}, u32[]{:S(2)}) collective-permute-start(bf16[32,4096]{1,0:T(8,128)(2,1)S(1)} %get-tuple-element.31.refs_0_), channel_id=1, source_target_pairs={{0,12},{1,13},{2,14},{3,15},{4,8},{5,9},{6,10},{7,11},{8,4},{9,5},... | collective-permute-start | bytes 786440 | tf_op jit(solution)/shard_map/far/ppermute | solution.py:64
  8.4 13.9 %collective-permute-start = (bf16[32,4096]{1,0:T(8,128)(2,1)S(1)}, bf16[32,4096]{1,0:T(8,128)(2,1)S(1)}, u32[]{:S(2)}, u32[]{:S(2)}) collective-permute-start(bf16[32,4096]{1,0:T(8,128)(2,1)S(1)} %get-tuple-element.31.refs_0_), channel_id=1, source_target_pairs={{0,2},{1,3},{2,0},{3,1},{4,6},{5,7},{6,4},{7,5},{8,10},{9,11},{10,... | collective-permute-start | bytes 786440 | tf_op jit(solution)/shard_map/mine_x/ppermute | solution.py:64
  13.3 8.4 %collective-permute-start.1 = (bf16[32,4096]{1,0:T(8,128)(2,1)S(1)}, bf16[32,4096]{1,0:T(8,128)(2,1)S(1)}, u32[]{:S(2)}, u32[]{:S(2)}) collective-permute-start(bf16[32,4096]{1,0:T(8,128)(2,1)S(1)} %get-tuple-element.32.refs_2_), channel_id=1, source_target_pairs={{0,2},{1,3},{2,0},{3,1},{4,6},{5,7},{6,4},{7,5},{8,10},{9,11},{10,... | collective-permute-start | bytes 786440 | tf_op jit(solution)/shard_map/rest_x/ppermute | solution.py:64
  13.9 12.2 %collective-permute-start.8 = (bf16[32,4096]{1,0:T(8,128)(2,1)S(1)}, bf16[32,4096]{1,0:T(8,128)(2,1)S(1)}, u32[]{:S(2)}, u32[]{:S(2)}) collective-permute-start(bf16[32,4096]{1,0:T(8,128)(2,1)S(1)} %collective-permute-done.3.refs_0_), channel_id=1, source_target_pairs={{0,16},{1,17},{2,18},{3,19},{4,20},{5,21},{6,22},{7,23},{8,24},{9,... | collective-permute-start | bytes 786440 | tf_op jit(solution)/shard_map/near_p/ppermute | solution.py:64
  20.1 7.7 %collective-permute-start.10 = (bf16[32,4096]{1,0:T(8,128)(2,1)S(1)}, bf16[32,4096]{1,0:T(8,128)(2,1)S(1)}, u32[]{:S(2)}, u32[]{:S(2)}) collective-permute-start(bf16[32,4096]{1,0:T(8,128)(2,1)S(1)} %collective-permute-done.2.refs_4_), channel_id=1, source_target_pairs={{0,16},{1,17},{2,18},{3,19},{4,20},{5,21},{6,22},{7,23},{8,24},{9,... | collective-permute-start | bytes 786440 | tf_op jit(solution)/shard_map/far_p/ppermute | solution.py:64
  21.6 1.4 %collective-permute-start.4 = (bf16[16,4096]{1,0:T(8,128)(2,1)S(1)}, bf16[16,4096]{1,0:T(8,128)(2,1)S(1)}, u32[]{:S(2)}, u32[]{:S(2)}) collective-permute-start(bf16[16,4096]{1,0:T(8,128)(2,1)S(1)} %get-tuple-element.54), channel_id=1, source_target_pairs={{0,2},{1,3},{2,0},{3,1},{4,6},{5,7},{6,4},{7,5},{8,10},{9,11},{10,... | collective-permute-start | bytes 393224 | tf_op jit(solution)/shard_map/far_xa/ppermute | solution.py:64
  21.7 1.9 %collective-permute-start.5 = (bf16[16,4096]{1,0:T(8,128)(2,1)S(1)}, bf16[16,4096]{1,0:T(8,128)(2,1)S(1)}, u32[]{:S(2)}, u32[]{:S(2)}) collective-permute-start(bf16[16,4096]{1,0:T(8,128)(2,1)S(1)} %get-tuple-element.53), channel_id=1, source_target_pairs={{0,2},{1,3},{2,0},{3,1},{4,6},{5,7},{6,4},{7,5},{8,10},{9,11},{10,... | collective-permute-start | bytes 393224 | tf_op jit(solution)/shard_map/far_xb/ppermute | solution.py:64
  22.2 9.3 %collective-permute-start.7 = (bf16[32,4096]{1,0:T(8,128)(2,1)S(1)}, bf16[32,4096]{1,0:T(8,128)(2,1)S(1)}, u32[]{:S(2)}, u32[]{:S(2)}) collective-permute-start(bf16[32,4096]{1,0:T(8,128)(2,1)S(1)} %collective-permute-done.3.refs_0_), channel_id=1, source_target_pairs={{0,2},{1,3},{2,0},{3,1},{4,6},{5,7},{6,4},{7,5},{8,10},{9,11},{10,... | collective-permute-start | bytes 786440 | tf_op jit(solution)/shard_map/near_x/ppermute | solution.py:64
  23.1 8.4 %collective-permute-start.14 = (bf16[32,4096]{1,0:T(8,128)(2,1)S(1)}, bf16[32,4096]{1,0:T(8,128)(2,1)S(1)}, u32[]{:S(2)}, u32[]{:S(2)}) collective-permute-start(bf16[32,4096]{1,0:T(8,128)(2,1)S(1)} %collective-permute-done.2.refs_4_), channel_id=1, source_target_pairs={{0,4},{1,5},{2,6},{3,7},{4,0},{5,1},{6,2},{7,3},{8,12},{9,13},{10,... | collective-permute-start | bytes 786440 | tf_op jit(solution)/shard_map/cross/ppermute | solution.py:64
  26.1 8.0 %collective-permute-start.9 = (bf16[32,4096]{1,0:T(8,128)(2,1)S(1)}, bf16[32,4096]{1,0:T(8,128)(2,1)S(1)}, u32[]{:S(2)}, u32[]{:S(2)}) collective-permute-start(bf16[32,4096]{1,0:T(8,128)(2,1)S(1)} %collective-permute-done.8.refs_2_), channel_id=1, source_target_pairs={{0,2},{1,3},{2,0},{3,1},{4,6},{5,7},{6,4},{7,5},{8,10},{9,11},{10,... | collective-permute-start | bytes 786440 | tf_op jit(solution)/shard_map/near_px/ppermute | solution.py:64
  27.8 4.2 %collective-permute-start.12 = (bf16[16,4096]{1,0:T(8,128)(2,1)S(1)}, bf16[16,4096]{1,0:T(8,128)(2,1)S(1)}, u32[]{:S(2)}, u32[]{:S(2)}) collective-permute-start(bf16[16,4096]{1,0:T(8,128)(2,1)S(1)} %get-tuple-element.51), channel_id=1, source_target_pairs={{0,2},{1,3},{2,0},{3,1},{4,6},{5,7},{6,4},{7,5},{8,10},{9,11},{10,... | collective-permute-start | bytes 393224 | tf_op jit(solution)/shard_map/far_pxb/ppermute | solution.py:64
  27.9 5.6 %collective-permute-start.11 = (bf16[16,4096]{1,0:T(8,128)(2,1)S(1)}, bf16[16,4096]{1,0:T(8,128)(2,1)S(1)}, u32[]{:S(2)}, u32[]{:S(2)}) collective-permute-start(bf16[16,4096]{1,0:T(8,128)(2,1)S(1)} %get-tuple-element.52), channel_id=1, source_target_pairs={{0,2},{1,3},{2,0},{3,1},{4,6},{5,7},{6,4},{7,5},{8,10},{9,11},{10,... | collective-permute-start | bytes 393224 | tf_op jit(solution)/shard_map/far_pxa/ppermute | solution.py:64
  31.4 5.7 %collective-permute-start.15 = (bf16[16,4096]{1,0:T(8,128)(2,1)S(1)}, bf16[16,4096]{1,0:T(8,128)(2,1)S(1)}, u32[]{:S(2)}, u32[]{:S(2)}) collective-permute-start(bf16[16,4096]{1,0:T(8,128)(2,1)S(1)} %get-tuple-element.50), channel_id=1, source_target_pairs={{0,2},{1,3},{2,0},{3,1},{4,6},{5,7},{6,4},{7,5},{8,10},{9,11},{10,... | collective-permute-start | bytes 393224 | tf_op jit(solution)/shard_map/cross_xa/ppermute | solution.py:64
  31.5 5.6 %collective-permute-start.16 = (bf16[16,4096]{1,0:T(8,128)(2,1)S(1)}, bf16[16,4096]{1,0:T(8,128)(2,1)S(1)}, u32[]{:S(2)}, u32[]{:S(2)}) collective-permute-start(bf16[16,4096]{1,0:T(8,128)(2,1)S(1)} %get-tuple-element.49), channel_id=1, source_target_pairs={{0,2},{1,3},{2,0},{3,1},{4,6},{5,7},{6,4},{7,5},{8,10},{9,11},{10,... | collective-permute-start | bytes 393224 | tf_op jit(solution)/shard_map/cross_xb/ppermute | solution.py:64
  32.0 7.6 %collective-permute-start.6 = (bf16[64,1024]{1,0:T(8,128)(2,1)S(1)}, bf16[64,1024]{1,0:T(8,128)(2,1)S(1)}, u32[]{:S(2)}, u32[]{:S(2)}) collective-permute-start(bf16[64,1024]{1,0:T(8,128)(2,1)S(1)} %get-tuple-element.36), channel_id=1, source_target_pairs={{0,1},{1,0},{2,3},{3,2},{4,5},{5,4},{6,7},{7,6},{8,9},{9,8},{10,11... | collective-permute-start | bytes 393224 | tf_op jit(solution)/shard_map/got0/ppermute | solution.py:64
  33.5 6.0 %collective-permute-start.19 = (bf16[16,4096]{1,0:T(8,128)(2,1)S(1)}, bf16[16,4096]{1,0:T(8,128)(2,1)S(1)}, u32[]{:S(2)}, u32[]{:S(2)}) collective-permute-start(bf16[16,4096]{1,0:T(8,128)(2,1)S(1)} %get-tuple-element.51), channel_id=1, source_target_pairs={{0,4},{1,5},{2,6},{3,7},{4,0},{5,1},{6,2},{7,3},{8,12},{9,13},{10,... | collective-permute-start | bytes 393224 | tf_op jit(solution)/shard_map/cross_pb/ppermute | solution.py:64
  34.1 5.6 %collective-permute-start.18 = (bf16[16,4096]{1,0:T(8,128)(2,1)S(1)}, bf16[16,4096]{1,0:T(8,128)(2,1)S(1)}, u32[]{:S(2)}, u32[]{:S(2)}) collective-permute-start(bf16[16,4096]{1,0:T(8,128)(2,1)S(1)} %get-tuple-element.50), channel_id=1, source_target_pairs={{0,16},{1,17},{2,18},{3,19},{4,20},{5,21},{6,22},{7,23},{8,24},{9,... | collective-permute-start | bytes 393224 | tf_op jit(solution)/shard_map/cross_pa/ppermute | solution.py:64
  37.2 14.3 %copy-start = (s32[1024]{0:T(1024)S(1)}, s32[1024]{0:T(1024)}, u32[]{:S(2)}) copy-start(s32[1024]{0:T(1024)} %param.14) | copy-start | bytes 12292
  39.6 2.6 %collective-permute-start.21 = (bf16[16,4096]{1,0:T(8,128)(2,1)S(1)}, bf16[16,4096]{1,0:T(8,128)(2,1)S(1)}, u32[]{:S(2)}, u32[]{:S(2)}) collective-permute-start(bf16[16,4096]{1,0:T(8,128)(2,1)S(1)} %collective-permute-done.19.refs_1_), channel_id=1, source_target_pairs={{0,2},{1,3},{2,0},{3,1},{4,6},{5,7},{6,4},{7,5},{8,10},{9,11},{10,... | collective-permute-start | bytes 393224 | tf_op jit(solution)/shard_map/cross_pxb/ppermute | solution.py:64
  39.7 2.5 %collective-permute-start.20 = (bf16[16,4096]{1,0:T(8,128)(2,1)S(1)}, bf16[16,4096]{1,0:T(8,128)(2,1)S(1)}, u32[]{:S(2)}, u32[]{:S(2)}) collective-permute-start(bf16[16,4096]{1,0:T(8,128)(2,1)S(1)} %collective-permute-done.18.refs_0_), channel_id=1, source_target_pairs={{0,2},{1,3},{2,0},{3,1},{4,6},{5,7},{6,4},{7,5},{8,10},{9,11},{10,... | collective-permute-start | bytes 393224 | tf_op jit(solution)/shard_map/cross_pxa/ppermute | solution.py:64
  40.2 6.4 %collective-permute-start.13 = (bf16[64,1024]{1,0:T(8,128)(2,1)S(1)}, bf16[64,1024]{1,0:T(8,128)(2,1)S(1)}, u32[]{:S(2)}, u32[]{:S(2)}) collective-permute-start(bf16[64,1024]{1,0:T(8,128)(2,1)S(1)} %get-tuple-element.40), channel_id=1, source_target_pairs={{0,1},{1,0},{2,3},{3,2},{4,5},{5,4},{6,7},{7,6},{8,9},{9,8},{10,11... | collective-permute-start | bytes 393224 | tf_op jit(solution)/shard_map/got1/ppermute | solution.py:64
  40.7 8.7 %collective-permute-start.17 = (bf16[64,1024]{1,0:T(8,128)(2,1)S(1)}, bf16[64,1024]{1,0:T(8,128)(2,1)S(1)}, u32[]{:S(2)}, u32[]{:S(2)}) collective-permute-start(bf16[64,1024]{1,0:T(8,128)(2,1)S(1)} %get-tuple-element.43), channel_id=1, source_target_pairs={{0,1},{1,0},{2,3},{3,2},{4,5},{5,4},{6,7},{7,6},{8,9},{9,8},{10,11... | collective-permute-start | bytes 393224 | tf_op jit(solution)/shard_map/got2/ppermute | solution.py:64
  46.5 5.0 %collective-permute-start.22 = (bf16[64,1024]{1,0:T(8,128)(2,1)S(1)}, bf16[64,1024]{1,0:T(8,128)(2,1)S(1)}, u32[]{:S(2)}, u32[]{:S(2)}) collective-permute-start(bf16[64,1024]{1,0:T(8,128)(2,1)S(1)} %get-tuple-element.48), channel_id=1, source_target_pairs={{0,1},{1,0},{2,3},{3,2},{4,5},{5,4},{6,7},{7,6},{8,9},{9,8},{10,11... | collective-permute-start | bytes 393224 | tf_op jit(solution)/shard_map/got3/ppermute | solution.py:64
  (1 other events, 9.9 us)

commit v6 on v5

--- a/solution.py
+++ b/solution.py
@@ -187,7 +187,7 @@
         copy.wait()
 
 
-def score_kernel(weight_ref, train_ref, *refs, picks, stored, early):
+def score_kernel(weight_ref, train_ref, *refs, picks, stored, early, columns):
     inputs, refs = refs[: len(picks)], refs[len(picks) :]
     n_before = sum(taken for _, _, taken in early)
     before, outs = refs[:n_before], refs[n_before:]
@@ -197,10 +197,10 @@
     )
     _, z, _, layer = place()
     near_is_mine = z // 2 == layer
-    for at in range(0, train_ref.shape[0], STEP):
-        here = slice(at, at + STEP)
+    for at in range(*columns, STEP):
+        there, here = slice(at, at + STEP), slice(at - columns[0], at - columns[0] + STEP)
         value = lax.dot_general(
-            train_ref[here, :], queries, (((1,), (1,)), ((), ())), preferred_element_type=f32
+            train_ref[there, :], queries, (((1,), (1,)), ((), ())), preferred_element_type=f32
         )
         value = weight * value.T
         if stored:
@@ -210,7 +210,7 @@
             old, given = [], list(before)
             for first, rows, taken in early:
                 old.append(
-                    given.pop(0)[first : first + rows, here] if taken else value[first : first + rows]
+                    given.pop(0)[first : first + rows, there] if taken else value[first : first + rows]
                 )
             old, new = jnp.concatenate(old, axis=0), value[stored:]
             send[:, here] = jnp.where(near_is_mine, new, old).astype(send.dtype)
@@ -228,8 +228,9 @@
     )(*inputs)
 
 
-def call_scores(weight, train, inputs, stored=0, early=()):
-    n = train.shape[0]
+def call_scores(weight, train, inputs, stored=0, early=(), columns=None):
+    columns = columns or (0, train.shape[0])
+    n = columns[1] - columns[0]
     total = sum(count for _, rows in inputs for _, count in rows)
     outs = [jax.ShapeDtypeStruct((stored, n), f32)] if stored else []
     if early:
@@ -240,28 +241,57 @@
             picks=[rows for _, rows in inputs],
             stored=stored,
             early=[(first, rows, a is not None) for a, first, rows in early],
+            columns=columns,
         ),
         outs,
         [weight, train, *[a for a, _ in inputs], *[a for a, _, _ in early if a is not None]],
     )
 
 
-def final_kernel(train_ids, query_ids, *refs):
-    out = refs[-1]
+def final_kernel(train_ids, query_ids, *refs, groups, n_given):
+    given, refs = refs[:n_given], refs[n_given:]
+    *_, out, done, sems = refs
     part, z, core, layer = place()
     low = z % 2
     first = jnp.where(z // 2 == layer, low, 1 - low)
-    ids = train_ids[...]
-    for k in range(4):
-        keep, got = refs[2 * k], refs[2 * k + 1]
-        block = first if k < 2 else 1 - first
-        half = part if k % 2 == 0 else 1 - part
+    copies = []
+    for k, (which, terms) in enumerate(groups):
+        block = first if which < 2 else 1 - first
+        half = part if which % 2 == 0 else 1 - part
         for i, c in enumerate((core, 1 - core)):
             at = pl.multiple_of(((block * 2 + c) * 2 + half) * HALF, HALF)
-            here = slice(i * HALF, (i + 1) * HALF)
-            total = keep[here, :] + got[here, :].astype(f32)
-            same = query_ids[pl.ds(at, HALF), :] == ids
-            out[pl.ds(at, HALF), :] = jnp.where(same, jnp.float32(0.0), total)
+            to = slice((2 * k + i) * HALF, (2 * k + i + 1) * HALF)
+            ids = query_ids[pl.ds(at, HALF), :]
+            for keep, got, row, column in terms:
+                keep, got = given[keep], given[got]
+                columns = slice(column, column + keep.shape[1])
+                total = keep[row + i * HALF : row + (i + 1) * HALF, :]
+                total = total + got[row + i * HALF : row + (i + 1) * HALF, :].astype(f32)
+                same = ids == train_ids[:, columns]
+                done[to, columns] = jnp.where(same, jnp.float32(0.0), total)
+            copies.append(
+                pltpu.make_async_copy(done.at[to, :], out.at[pl.ds(at, HALF), :], sems.at[2 * k + i])
+            )
+            copies[-1].start()
+    for copy in copies:
+        copy.wait()
+
+
+def call_final(train_ids, query_ids, given, groups, before=None):
+    rows, n = query_ids.shape[0], train_ids.shape[1]
+    inputs = [train_ids, query_ids, *given] + ([] if before is None else [before])
+    return pl.pallas_call(
+        functools.partial(final_kernel, groups=groups, n_given=len(given)),
+        out_shape=jax.ShapeDtypeStruct((rows, n), f32),
+        in_specs=[VMEM] * (2 + len(given)) + ([] if before is None else [HBM]),
+        out_specs=HBM,
+        scratch_shapes=[
+            pltpu.VMEM((2 * len(groups) * HALF, n), f32),
+            pltpu.SemaphoreType.DMA((2 * len(groups),)),
+        ],
+        input_output_aliases={} if before is None else {len(inputs) - 1: 0},
+        compiler_params=pltpu.CompilerParams(vmem_limit_bytes=LIMIT),
+    )(*inputs)
 
 
 def small(
@@ -304,51 +334,70 @@
     def rows_of(*pieces):
         return [(piece, ((0, piece.shape[0]),)) for piece in pieces]
 
+    parts_of = lambda piece: (piece[:CHUNK], piece[CHUNK:])
     mine_x = to_core(mine, "mine_x")
-    rest_x = to_core(rest, "rest_x")
+    rest_a, rest_b = parts_of(rest)
+    rest_xa = to_core(rest_a, "rest_xa")
+    rest_xb = to_core(rest_b, "rest_xb")
     near = after(near, rest)
-    near_x = to_core(near, "near_x")
+    near_a, near_b = parts_of(near)
+    near_xa = to_core(near_a, "near_xa")
+    near_xb = to_core(near_b, "near_xb")
     near_p = to_part(near, "near_p")
-    far = after(far, near)
+    (early0,) = score(
+        rows_of(mine, mine_x, rest, rest_xa, rest_xb, near, near_xa, near_xb), stored=192
+    )
+
+    far = after(far, near, early0)
     cross = to_near(far, "cross")
-    far_p = to_part(far, "far_p")
-    far_xa = to_core(far[:CHUNK], "far_xa")
-    far_xb = to_core(far[CHUNK:], "far_xb")
-    early0, send0, keep0 = score(
-        rows_of(mine, mine_x, rest, rest_x, far, far_xa, far_xb), stored=128, early=[(None, 0, 64)]
-    )
+    far_a, far_b = parts_of(far)
+    far_pa = to_part(far_a, "far_pa")
+    far_pb = to_part(far_b, "far_pb")
+    far_xa = to_core(after(far_a, near_p), "far_xa")
+    far_xb = to_core(after(far_b, near_p), "far_xb")
+    send0, keep0 = score(rows_of(far, far_xa, far_xb), early=[(early0, 0, 64)])
     got0 = to_layer(send0, "got0")
 
-    near_p = after(near_p, send0)
+    far_pa, far_pb, near_p = after(far_pa, send0), after(far_pb, send0), after(near_p, send0)
     near_px = to_core(near_p, "near_px")
-    far_pxa = to_core(far_p[:CHUNK], "far_pxa")
-    far_pxb = to_core(far_p[CHUNK:], "far_pxb")
-    cross_pa = to_part(cross[:CHUNK], "cross_pa")
-    cross_pb = to_near(far_p[CHUNK:], "cross_pb")
-    cross_xa = to_core(cross[:CHUNK], "cross_xa")
-    cross_xb = to_core(cross[CHUNK:], "cross_xb")
+    far_pxa = to_core(far_pa, "far_pxa")
+    far_pxb = to_core(far_pb, "far_pxb")
+    cross_pb = to_near(far_pb, "cross_pb")
+    cross_a, cross_b = parts_of(cross)
+    cross_a = after(cross_a, send0)
+    cross_pa = to_part(cross_a, "cross_pa")
+    cross_xa = to_core(after(cross_a, far_pa, far_pb), "cross_xa")
+    cross_xb = to_core(after(cross_b, far_pa, far_pb), "cross_xb")
     early1, send1, keep1 = score(
-        rows_of(near, near_x, near_p, near_px, far_p, far_pxa, far_pxb),
-        stored=128,
-        early=[(early0, 64, 64)],
+        rows_of(near_p, near_px, far_pa, far_pb, far_pxa, far_pxb, cross, cross_xa, cross_xb),
+        stored=64,
+        early=[(early0, 64, 64), (early0, 128, 64)],
     )
     got1 = to_layer(send1, "got1")
 
-    send2, keep2 = score(rows_of(cross, cross_xa, cross_xb), early=[(early1, 0, 64)])
-    got2 = to_layer(send2, "got2")
-
-    cross_pa, cross_pb = after(cross_pa, send2, got0), after(cross_pb, send2, got0)
+    cross_pa, cross_pb = after(cross_pa, send1, got0), after(cross_pb, send1, got0)
     cross_pxa = to_core(cross_pa, "cross_pxa")
     cross_pxb = to_core(cross_pb, "cross_pxb")
-    send3, keep3 = score(
-        rows_of(cross_pa, cross_pb, cross_pxa, cross_pxb), early=[(early1, 64, 64)]
-    )
-    send3 = after(send3, got1)
+    last = rows_of(cross_pa, cross_pb, cross_pxa, cross_pxb)
+    n = train.shape[0]
+    send2, keep2 = score(last, early=[(early1, 0, 64)], columns=(0, n // 2))
+    got2 = to_layer(send2, "got2")
+    send3, keep3 = score(last, early=[(early1, 0, 64)], columns=(n // 2, n))
     got3 = to_layer(send3, "got3")
-    return kernel_call(
-        final_kernel,
-        shape((query_ids.shape[0], train_ids.shape[0]), f32),
-        [train_ids[None, :], query_ids[:, None], keep0, got0, keep1, got1, keep2, got2, keep3, got3],
+
+    train_ids, query_ids = train_ids[None, :], query_ids[:, None]
+    most = call_final(
+        train_ids,
+        query_ids,
+        [keep0, got0, keep1, got1],
+        ((0, [(0, 1, 0, 0)]), (1, [(2, 3, 0, 0)]), (2, [(2, 3, 64, 0)])),
+    )
+    return call_final(
+        train_ids,
+        query_ids,
+        [keep2, got2, keep3, got3],
+        ((3, [(0, 1, 0, 0), (2, 3, 0, n // 2)]),),
+        most,
     )
 
 

time: 52.8 us -> 54.3 us (1.028)
  the two profiles are of different devices: /device:TPU:0 before, /device:TPU:16 now
where the time goes in v6:
time: 54.3 us; the launch traced here: 54.1 us
  starting transfers between devices  21.9 us (40%)
  Pallas kernels  18.9 us (35%)
  waiting for transfers between devices  12.2 us (22%)
  between operations  0.82 us (2%)
    ppermute x26, starting transfers between devices, permute(): return lax.ppermute(value, AXES, pairs)  21.9 us
    pallas_call x7, Pallas kernels, kernel_call(): pl.pallas_call(kernel, out_shape=outs, in_specs=specs or [VMEM] * len(inp...  17.1 us
    ppermute x26, waiting for transfers between devices, permute(): return lax.ppermute(value, AXES, pairs)  12.2 us
    pallas_call x2, Pallas kernels, call_final(): pl.pallas_call(functools.partial(final_kernel, groups=groups, n_given=len...  1.84 us
  transfers between devices with their start and end apart: 26, of which 11 were waited for; matrix products, arithmetic and copies ran while one was open for 0% of the time, Pallas kernels for 28%

profile of v6, /device:TPU:16, one launch (start us, length us, event | category | flops | bytes accessed | tf_op | source)
XLA Modules:
  0.0 54.1 jit_solution(2397020445691149551)
XLA Ops:
  0.0 2.8 %shard_map.82 = (bf16[32,4096]{1,0:T(8,128)(2,1)S(1)}, bf16[2,256,256]{2,1,0:T(8,128)(2,1)S(1)}, bf16[2,256,512]{2,1,0:T(8,128)(2,1)S(1)}) custom-call(bf16[64,4096]{1,0:T(8,128)(2,1)} %bitcast.9, f32[64,64]{1,0:T(8,128)} %bitcast.11, f32[64,64]{1,0:T(8,128)} %bitcast.12), custom_call_target="tpu_custom_call" | custom-call | tf_op jit(solution)/shard_map/pallas_call | solution.py:221
  2.8 1.6 %collective-permute-start.1 = (bf16[32,4096]{1,0:T(8,128)(2,1)S(1)}, bf16[32,4096]{1,0:T(8,128)(2,1)S(1)}, u32[]{:S(2)}, u32[]{:S(2)}) collective-permute-start(bf16[32,4096]{1,0:T(8,128)(2,1)S(1)} %get-tuple-element.36.refs_0_), channel_id=1, source_target_pairs={{0,4},{1,5},{2,6},{3,7},{4,0},{5,1},{6,2},{7,3},{8,12},{9,13},{10,... | collective-permute-start | bytes 786440 | tf_op jit(solution)/shard_map/near/ppermute | solution.py:64
  5.1 4.3 %shard_map.83 = (bf16[32,4096]{1,0:T(8,128)(2,1)S(1)}, bf16[1024,4096]{1,0:T(8,128)(2,1)S(1)}, f32[8,256]{1,0:T(8,128)S(1)}) custom-call(f32[2]{0:T(128)} %weight_ref.1, s32[1]{0:T(128)S(6)} %copy.13.layer_ref, bf16[64,4096]{1,0:T(8,128)(2,1)} %bitcast.10, bf16[1024,4096]{1,0:T(8,128)(2,1)} %bitcast.8, bf16[2,256,256]{2,1,0:T(8,128)(2,1)S(1)} %get-tuple-element.32.lefts_ref, ...), custom_call_target="tpu_custom_call" | custom-call | tf_op jit(solution)/shard_map/pallas_call | solution.py:221
  10.1 2.0 %collective-permute-done.1.refs_5_ = bf16[32,4096]{1,0:T(8,128)(2,1)S(1)} collective-permute-done((bf16[32,4096]{1,0:T(8,128)(2,1)S(1)}, bf16[32,4096]{1,0:T(8,128)(2,1)S(1)}, u32[]{:S(2)}, u32[]{:S(2)}) %collective-permute-start.1) | collective-permute-done | bytes 262176 | tf_op jit(solution)/shard_map/near/ppermute | solution.py:64
  12.7 1.5 %collective-permute-start.8 = (bf16[32,4096]{1,0:T(8,128)(2,1)S(1)}, bf16[32,4096]{1,0:T(8,128)(2,1)S(1)}, u32[]{:S(2)}, u32[]{:S(2)}) collective-permute-start(bf16[32,4096]{1,0:T(8,128)(2,1)S(1)} %collective-permute-done.1.refs_5_), channel_id=1, source_target_pairs={{0,16},{1,17},{2,18},{3,19},{4,20},{5,21},{6,22},{7,23},{8,24},{9,... | collective-permute-start | bytes 786440 | tf_op jit(solution)/shard_map/near_p/ppermute | solution.py:64
  14.2 2.5 %shard_map.84.refs_3_.refs_9_.refs_10_ = f32[192,1024]{1,0:T(8,128)S(1)} custom-call(f32[8,256]{1,0:T(8,128)S(1)} %get-tuple-element.34.weight_ref, bf16[1024,4096]{1,0:T(8,128)(2,1)S(1)} %get-tuple-element.35.train_ref, bf16[32,4096]{1,0:T(8,128)(2,1)S(1)} %get-tuple-element.36.refs_0_, bf16[32,4096]{1,0:T(8,128)(2,1)S(1)} %collective-permute-done.2.refs_1_, ...), custom_call_target="tpu_custom_call" | custom-call | tf_op jit(solution)/shard_map/pallas_call | solution.py:221
  16.7 2.1 %collective-permute-done.refs_0_ = bf16[32,4096]{1,0:T(8,128)(2,1)S(1)} collective-permute-done((bf16[32,4096]{1,0:T(8,128)(2,1)S(1)}, bf16[32,4096]{1,0:T(8,128)(2,1)S(1)}, u32[]{:S(2)}, u32[]{:S(2)}) %collective-permute-start) | collective-permute-done | bytes 262176 | tf_op jit(solution)/shard_map/far/ppermute | solution.py:64
  18.8 4.0 %collective-permute-start.7 = (bf16[32,4096]{1,0:T(8,128)(2,1)S(1)}, bf16[32,4096]{1,0:T(8,128)(2,1)S(1)}, u32[]{:S(2)}, u32[]{:S(2)}) collective-permute-start(bf16[32,4096]{1,0:T(8,128)(2,1)S(1)} %collective-permute-done.refs_0_), channel_id=1, source_target_pairs={{0,4},{1,5},{2,6},{3,7},{4,0},{5,1},{6,2},{7,3},{8,12},{9,13},{10,... | collective-permute-start | bytes 786440 | tf_op jit(solution)/shard_map/cross/ppermute | solution.py:64
  23.4 1.0 %collective-permute-start.14 = (bf16[16,4096]{1,0:T(8,128)(2,1)S(1)}, bf16[16,4096]{1,0:T(8,128)(2,1)S(1)}, u32[]{:S(2)}, u32[]{:S(2)}) collective-permute-start(bf16[16,4096]{1,0:T(8,128)(2,1)S(1)} %get-tuple-element.41), channel_id=1, source_target_pairs={{0,16},{1,17},{2,18},{3,19},{4,20},{5,21},{6,22},{7,23},{8,24},{9,... | collective-permute-start | bytes 393224 | tf_op jit(solution)/shard_map/far_pb/ppermute | solution.py:64
  24.4 1.0 %collective-permute-start.13 = (bf16[16,4096]{1,0:T(8,128)(2,1)S(1)}, bf16[16,4096]{1,0:T(8,128)(2,1)S(1)}, u32[]{:S(2)}, u32[]{:S(2)}) collective-permute-start(bf16[16,4096]{1,0:T(8,128)(2,1)S(1)} %get-tuple-element.40), channel_id=1, source_target_pairs={{0,16},{1,17},{2,18},{3,19},{4,20},{5,21},{6,22},{7,23},{8,24},{9,... | collective-permute-start | bytes 393224 | tf_op jit(solution)/shard_map/far_pa/ppermute | solution.py:64
  25.4 2.4 %shard_map.85 = (bf16[64,1024]{1,0:T(8,128)(2,1)S(1)}, f32[64,1024]{1,0:T(8,128)S(1)}) custom-call(f32[8,256]{1,0:T(8,128)S(1)} %get-tuple-element.34.weight_ref, bf16[1024,4096]{1,0:T(8,128)(2,1)S(1)} %get-tuple-element.35.train_ref, bf16[32,4096]{1,0:T(8,128)(2,1)S(1)} %collective-permute-done.refs_0_, ...), custom_call_target="tpu_custom_call" | custom-call | tf_op jit(solution)/shard_map/pallas_call | solution.py:221
  27.9 1.2 %collective-permute-done.7.refs_6_ = bf16[32,4096]{1,0:T(8,128)(2,1)S(1)} collective-permute-done((bf16[32,4096]{1,0:T(8,128)(2,1)S(1)}, bf16[32,4096]{1,0:T(8,128)(2,1)S(1)}, u32[]{:S(2)}, u32[]{:S(2)}) %collective-permute-start.7) | collective-permute-done | bytes 262176 | tf_op jit(solution)/shard_map/cross/ppermute | solution.py:64
  29.8 1.9 %collective-permute-done.13.refs_2_ = bf16[16,4096]{1,0:T(8,128)(2,1)S(1)} collective-permute-done((bf16[16,4096]{1,0:T(8,128)(2,1)S(1)}, bf16[16,4096]{1,0:T(8,128)(2,1)S(1)}, u32[]{:S(2)}, u32[]{:S(2)}) %collective-permute-start.13) | collective-permute-done | bytes 131104 | tf_op jit(solution)/shard_map/far_pa/ppermute | solution.py:64
  33.0 1.5 %collective-permute-start.19 = (bf16[64,1024]{1,0:T(8,128)(2,1)S(1)}, bf16[64,1024]{1,0:T(8,128)(2,1)S(1)}, u32[]{:S(2)}, u32[]{:S(2)}) collective-permute-start(bf16[64,1024]{1,0:T(8,128)(2,1)S(1)} %get-tuple-element.42), channel_id=1, source_target_pairs={{0,1},{1,0},{2,3},{3,2},{4,5},{5,4},{6,7},{7,6},{8,9},{9,8},{10,11... | collective-permute-start | bytes 393224 | tf_op jit(solution)/shard_map/got0/ppermute | solution.py:64
  34.6 4.0 %collective-permute-start.20 = (bf16[16,4096]{1,0:T(8,128)(2,1)S(1)}, bf16[16,4096]{1,0:T(8,128)(2,1)S(1)}, u32[]{:S(2)}, u32[]{:S(2)}) collective-permute-start(bf16[16,4096]{1,0:T(8,128)(2,1)S(1)} %collective-permute-done.14.refs_3_), channel_id=1, source_target_pairs={{0,4},{1,5},{2,6},{3,7},{4,0},{5,1},{6,2},{7,3},{8,12},{9,13},{10,... | collective-permute-start | bytes 393224 | tf_op jit(solution)/shard_map/cross_pb/ppermute | solution.py:64
  38.6 1.5 %collective-permute-start.11 = (bf16[16,4096]{1,0:T(8,128)(2,1)S(1)}, bf16[16,4096]{1,0:T(8,128)(2,1)S(1)}, u32[]{:S(2)}, u32[]{:S(2)}) collective-permute-start(bf16[16,4096]{1,0:T(8,128)(2,1)S(1)} %get-tuple-element.47), channel_id=1, source_target_pairs={{0,16},{1,17},{2,18},{3,19},{4,20},{5,21},{6,22},{7,23},{8,24},{9,... | collective-permute-start | bytes 393224 | tf_op jit(solution)/shard_map/cross_pa/ppermute | solution.py:64
  40.1 2.5 %shard_map.86 = (f32[64,1024]{1,0:T(8,128)S(1)}, bf16[128,1024]{1,0:T(8,128)(2,1)S(1)}, f32[128,1024]{1,0:T(8,128)S(1)}) custom-call(f32[8,256]{1,0:T(8,128)S(1)} %get-tuple-element.34.weight_ref, bf16[1024,4096]{1,0:T(8,128)(2,1)S(1)} %get-tuple-element.35.train_ref, bf16[32,4096]{1,0:T(8,128)(2,1)S(1)} %collective-permute-done.8.refs_0_, ...), custom_call_target="tpu_custom_call" | custom-call | tf_op jit(solution)/shard_map/pallas_call | solution.py:221
  43.7 0.8 %collective-permute-done.22.refs_3_ = bf16[16,4096]{1,0:T(8,128)(2,1)S(1)} collective-permute-done((bf16[16,4096]{1,0:T(8,128)(2,1)S(1)}, bf16[16,4096]{1,0:T(8,128)(2,1)S(1)}, u32[]{:S(2)}, u32[]{:S(2)}) %collective-permute-start.22) | collective-permute-done | bytes 131104 | tf_op jit(solution)/shard_map/cross_pxb/ppermute | solution.py:64
  45.0 1.3 %shard_map.88 = (bf16[64,512]{1,0:T(8,128)(2,1)S(1)}, f32[64,512]{1,0:T(8,128)S(1)}) custom-call(f32[8,256]{1,0:T(8,128)S(1)} %get-tuple-element.34.weight_ref, bf16[1024,4096]{1,0:T(8,128)(2,1)S(1)} %get-tuple-element.35.train_ref, bf16[16,4096]{1,0:T(8,128)(2,1)S(1)} %collective-permute-done.11.refs_0_, ...), custom_call_target="tpu_custom_call" | custom-call | tf_op jit(solution)/shard_map/pallas_call | solution.py:221
  46.3 1.4 %collective-permute-start.24 = (bf16[64,512]{1,0:T(8,128)(2,1)S(1)}, bf16[64,512]{1,0:T(8,128)(2,1)S(1)}, u32[]{:S(2)}, u32[]{:S(2)}) collective-permute-start(bf16[64,512]{1,0:T(8,128)(2,1)S(1)} %get-tuple-element.56), channel_id=1, source_target_pairs={{0,1},{1,0},{2,3},{3,2},{4,5},{5,4},{6,7},{7,6},{8,9},{9,8},{10,11... | collective-permute-start | bytes 196616 | tf_op jit(solution)/shard_map/got3/ppermute | solution.py:64
  47.7 1.3 %shard_map.87 = (bf16[64,512]{1,0:T(8,128)(2,1)S(1)}, f32[64,512]{1,0:T(8,128)S(1)}) custom-call(f32[8,256]{1,0:T(8,128)S(1)} %get-tuple-element.34.weight_ref, bf16[1024,4096]{1,0:T(8,128)(2,1)S(1)} %get-tuple-element.35.train_ref, bf16[16,4096]{1,0:T(8,128)(2,1)S(1)} %collective-permute-done.11.refs_0_, ...), custom_call_target="tpu_custom_call" | custom-call | tf_op jit(solution)/shard_map/pallas_call | solution.py:221
  49.9 1.0 %collective-permute-done.25.refs_3_ = bf16[128,1024]{1,0:T(8,128)(2,1)S(1)} collective-permute-done((bf16[128,1024]{1,0:T(8,128)(2,1)S(1)}, bf16[128,1024]{1,0:T(8,128)(2,1)S(1)}, u32[]{:S(2)}, u32[]{:S(2)}) %collective-permute-start.25) | collective-permute-done | bytes 262176 | tf_op jit(solution)/shard_map/got1/ppermute | solution.py:64
  50.9 1.0 %shard_map.89.refs_4_ = f32[256,1024]{1,0:T(8,128)} custom-call(s32[1,1024]{1,0:T(1,128)S(1)} %bitcast.6, s32[256,1]{1,0:T(8,128)S(1)} %copy.11.query_ids, f32[64,1024]{1,0:T(8,128)S(1)} %get-tuple-element.57.refs_0_, bf16[64,1024]{1,0:T(8,128)(2,1)S(1)} %collective-permute-done.19.refs_1_, f32[128,1024]{1,0:T(8,128)S(1)} %get-tuple-element.58.refs_2_, ...), custom_call_target="tpu_custom_call" | custom-call | tf_op jit(solution)/shard_map/pallas_call | solution.py:283
  52.0 1.4 %collective-permute-done.23.refs_1_ = bf16[64,512]{1,0:T(8,128)(2,1)S(1)} collective-permute-done((bf16[64,512]{1,0:T(8,128)(2,1)S(1)}, bf16[64,512]{1,0:T(8,128)(2,1)S(1)}, u32[]{:S(2)}, u32[]{:S(2)}) %collective-permute-start.23) | collective-permute-done | bytes 65568 | tf_op jit(solution)/shard_map/got2/ppermute | solution.py:64
  (46 shorter events, 7.2 us)
Async XLA Ops:
  2.8 9.3 %collective-permute-start.1 = (bf16[32,4096]{1,0:T(8,128)(2,1)S(1)}, bf16[32,4096]{1,0:T(8,128)(2,1)S(1)}, u32[]{:S(2)}, u32[]{:S(2)}) collective-permute-start(bf16[32,4096]{1,0:T(8,128)(2,1)S(1)} %get-tuple-element.36.refs_0_), channel_id=1, source_target_pairs={{0,4},{1,5},{2,6},{3,7},{4,0},{5,1},{6,2},{7,3},{8,12},{9,13},{10,... | collective-permute-start | bytes 786440 | tf_op jit(solution)/shard_map/near/ppermute | solution.py:64
  4.5 9.7 %collective-permute-start.2 = (bf16[32,4096]{1,0:T(8,128)(2,1)S(1)}, bf16[32,4096]{1,0:T(8,128)(2,1)S(1)}, u32[]{:S(2)}, u32[]{:S(2)}) collective-permute-start(bf16[32,4096]{1,0:T(8,128)(2,1)S(1)} %get-tuple-element.36.refs_0_), channel_id=1, source_target_pairs={{0,2},{1,3},{2,0},{3,1},{4,6},{5,7},{6,4},{7,5},{8,10},{9,11},{10,... | collective-permute-start | bytes 786440 | tf_op jit(solution)/shard_map/mine_x/ppermute | solution.py:64
  4.5 14.3 %collective-permute-start = (bf16[32,4096]{1,0:T(8,128)(2,1)S(1)}, bf16[32,4096]{1,0:T(8,128)(2,1)S(1)}, u32[]{:S(2)}, u32[]{:S(2)}) collective-permute-start(bf16[32,4096]{1,0:T(8,128)(2,1)S(1)} %get-tuple-element.36.refs_0_), channel_id=1, source_target_pairs={{0,12},{1,13},{2,14},{3,15},{4,8},{5,9},{6,10},{7,11},{8,4},{9,5},... | collective-permute-start | bytes 786440 | tf_op jit(solution)/shard_map/far/ppermute | solution.py:64
  9.4 2.8 %collective-permute-start.3 = (bf16[16,4096]{1,0:T(8,128)(2,1)S(1)}, bf16[16,4096]{1,0:T(8,128)(2,1)S(1)}, u32[]{:S(2)}, u32[]{:S(2)}) collective-permute-start(bf16[16,4096]{1,0:T(8,128)(2,1)S(1)} %get-tuple-element.66), channel_id=1, source_target_pairs={{0,2},{1,3},{2,0},{3,1},{4,6},{5,7},{6,4},{7,5},{8,10},{9,11},{10,... | collective-permute-start | bytes 393224 | tf_op jit(solution)/shard_map/rest_xa/ppermute | solution.py:64
  10.0 2.7 %collective-permute-start.4 = (bf16[16,4096]{1,0:T(8,128)(2,1)S(1)}, bf16[16,4096]{1,0:T(8,128)(2,1)S(1)}, u32[]{:S(2)}, u32[]{:S(2)}) collective-permute-start(bf16[16,4096]{1,0:T(8,128)(2,1)S(1)} %get-tuple-element.65), channel_id=1, source_target_pairs={{0,2},{1,3},{2,0},{3,1},{4,6},{5,7},{6,4},{7,5},{8,10},{9,11},{10,... | collective-permute-start | bytes 393224 | tf_op jit(solution)/shard_map/rest_xb/ppermute | solution.py:64
  12.1 2.1 %collective-permute-start.5 = (bf16[16,4096]{1,0:T(8,128)(2,1)S(1)}, bf16[16,4096]{1,0:T(8,128)(2,1)S(1)}, u32[]{:S(2)}, u32[]{:S(2)}) collective-permute-start(bf16[16,4096]{1,0:T(8,128)(2,1)S(1)} %get-tuple-element.64), channel_id=1, source_target_pairs={{0,2},{1,3},{2,0},{3,1},{4,6},{5,7},{6,4},{7,5},{8,10},{9,11},{10,... | collective-permute-start | bytes 393224 | tf_op jit(solution)/shard_map/near_xa/ppermute | solution.py:64
  12.2 2.0 %collective-permute-start.6 = (bf16[16,4096]{1,0:T(8,128)(2,1)S(1)}, bf16[16,4096]{1,0:T(8,128)(2,1)S(1)}, u32[]{:S(2)}, u32[]{:S(2)}) collective-permute-start(bf16[16,4096]{1,0:T(8,128)(2,1)S(1)} %get-tuple-element.63), channel_id=1, source_target_pairs={{0,2},{1,3},{2,0},{3,1},{4,6},{5,7},{6,4},{7,5},{8,10},{9,11},{10,... | collective-permute-start | bytes 393224 | tf_op jit(solution)/shard_map/near_xb/ppermute | solution.py:64
  12.7 10.1 %collective-permute-start.8 = (bf16[32,4096]{1,0:T(8,128)(2,1)S(1)}, bf16[32,4096]{1,0:T(8,128)(2,1)S(1)}, u32[]{:S(2)}, u32[]{:S(2)}) collective-permute-start(bf16[32,4096]{1,0:T(8,128)(2,1)S(1)} %collective-permute-done.1.refs_5_), channel_id=1, source_target_pairs={{0,16},{1,17},{2,18},{3,19},{4,20},{5,21},{6,22},{7,23},{8,24},{9,... | collective-permute-start | bytes 786440 | tf_op jit(solution)/shard_map/near_p/ppermute | solution.py:64
  18.8 10.3 %collective-permute-start.7 = (bf16[32,4096]{1,0:T(8,128)(2,1)S(1)}, bf16[32,4096]{1,0:T(8,128)(2,1)S(1)}, u32[]{:S(2)}, u32[]{:S(2)}) collective-permute-start(bf16[32,4096]{1,0:T(8,128)(2,1)S(1)} %collective-permute-done.refs_0_), channel_id=1, source_target_pairs={{0,4},{1,5},{2,6},{3,7},{4,0},{5,1},{6,2},{7,3},{8,12},{9,13},{10,... | collective-permute-start | bytes 786440 | tf_op jit(solution)/shard_map/cross/ppermute | solution.py:64
  22.8 2.6 %collective-permute-start.10 = (bf16[16,4096]{1,0:T(8,128)(2,1)S(1)}, bf16[16,4096]{1,0:T(8,128)(2,1)S(1)}, u32[]{:S(2)}, u32[]{:S(2)}) collective-permute-start(bf16[16,4096]{1,0:T(8,128)(2,1)S(1)} %get-tuple-element.41), channel_id=1, source_target_pairs={{0,2},{1,3},{2,0},{3,1},{4,6},{5,7},{6,4},{7,5},{8,10},{9,11},{10,... | collective-permute-start | bytes 393224 | tf_op jit(solution)/shard_map/far_xb/ppermute | solution.py:64
  22.9 2.5 %collective-permute-start.9 = (bf16[16,4096]{1,0:T(8,128)(2,1)S(1)}, bf16[16,4096]{1,0:T(8,128)(2,1)S(1)}, u32[]{:S(2)}, u32[]{:S(2)}) collective-permute-start(bf16[16,4096]{1,0:T(8,128)(2,1)S(1)} %get-tuple-element.40), channel_id=1, source_target_pairs={{0,2},{1,3},{2,0},{3,1},{4,6},{5,7},{6,4},{7,5},{8,10},{9,11},{10,... | collective-permute-start | bytes 393224 | tf_op jit(solution)/shard_map/far_xa/ppermute | solution.py:64
  23.4 6.4 %collective-permute-start.14 = (bf16[16,4096]{1,0:T(8,128)(2,1)S(1)}, bf16[16,4096]{1,0:T(8,128)(2,1)S(1)}, u32[]{:S(2)}, u32[]{:S(2)}) collective-permute-start(bf16[16,4096]{1,0:T(8,128)(2,1)S(1)} %get-tuple-element.41), channel_id=1, source_target_pairs={{0,16},{1,17},{2,18},{3,19},{4,20},{5,21},{6,22},{7,23},{8,24},{9,... | collective-permute-start | bytes 393224 | tf_op jit(solution)/shard_map/far_pb/ppermute | solution.py:64
  24.4 7.3 %collective-permute-start.13 = (bf16[16,4096]{1,0:T(8,128)(2,1)S(1)}, bf16[16,4096]{1,0:T(8,128)(2,1)S(1)}, u32[]{:S(2)}, u32[]{:S(2)}) collective-permute-start(bf16[16,4096]{1,0:T(8,128)(2,1)S(1)} %get-tuple-element.40), channel_id=1, source_target_pairs={{0,16},{1,17},{2,18},{3,19},{4,20},{5,21},{6,22},{7,23},{8,24},{9,... | collective-permute-start | bytes 393224 | tf_op jit(solution)/shard_map/far_pa/ppermute | solution.py:64
  27.8 12.3 %collective-permute-start.12 = (bf16[32,4096]{1,0:T(8,128)(2,1)S(1)}, bf16[32,4096]{1,0:T(8,128)(2,1)S(1)}, u32[]{:S(2)}, u32[]{:S(2)}) collective-permute-start(bf16[32,4096]{1,0:T(8,128)(2,1)S(1)} %collective-permute-done.8.refs_0_), channel_id=1, source_target_pairs={{0,2},{1,3},{2,0},{3,1},{4,6},{5,7},{6,4},{7,5},{8,10},{9,11},{10,... | collective-permute-start | bytes 786440 | tf_op jit(solution)/shard_map/near_px/ppermute | solution.py:64
  31.7 2.9 %collective-permute-start.17 = (bf16[16,4096]{1,0:T(8,128)(2,1)S(1)}, bf16[16,4096]{1,0:T(8,128)(2,1)S(1)}, u32[]{:S(2)}, u32[]{:S(2)}) collective-permute-start(bf16[16,4096]{1,0:T(8,128)(2,1)S(1)} %get-tuple-element.47), channel_id=1, source_target_pairs={{0,2},{1,3},{2,0},{3,1},{4,6},{5,7},{6,4},{7,5},{8,10},{9,11},{10,... | collective-permute-start | bytes 393224 | tf_op jit(solution)/shard_map/cross_xa/ppermute | solution.py:64
  32.2 6.4 %collective-permute-start.16 = (bf16[16,4096]{1,0:T(8,128)(2,1)S(1)}, bf16[16,4096]{1,0:T(8,128)(2,1)S(1)}, u32[]{:S(2)}, u32[]{:S(2)}) collective-permute-start(bf16[16,4096]{1,0:T(8,128)(2,1)S(1)} %collective-permute-done.14.refs_3_), channel_id=1, source_target_pairs={{0,2},{1,3},{2,0},{3,1},{4,6},{5,7},{6,4},{7,5},{8,10},{9,11},{10,... | collective-permute-start | bytes 393224 | tf_op jit(solution)/shard_map/far_pxb/ppermute | solution.py:64
  32.2 7.9 %collective-permute-start.15 = (bf16[16,4096]{1,0:T(8,128)(2,1)S(1)}, bf16[16,4096]{1,0:T(8,128)(2,1)S(1)}, u32[]{:S(2)}, u32[]{:S(2)}) collective-permute-start(bf16[16,4096]{1,0:T(8,128)(2,1)S(1)} %collective-permute-done.13.refs_2_), channel_id=1, source_target_pairs={{0,2},{1,3},{2,0},{3,1},{4,6},{5,7},{6,4},{7,5},{8,10},{9,11},{10,... | collective-permute-start | bytes 393224 | tf_op jit(solution)/shard_map/far_pxa/ppermute | solution.py:64
  33.0 10.2 %collective-permute-start.19 = (bf16[64,1024]{1,0:T(8,128)(2,1)S(1)}, bf16[64,1024]{1,0:T(8,128)(2,1)S(1)}, u32[]{:S(2)}, u32[]{:S(2)}) collective-permute-start(bf16[64,1024]{1,0:T(8,128)(2,1)S(1)} %get-tuple-element.42), channel_id=1, source_target_pairs={{0,1},{1,0},{2,3},{3,2},{4,5},{5,4},{6,7},{7,6},{8,9},{9,8},{10,11... | collective-permute-start | bytes 393224 | tf_op jit(solution)/shard_map/got0/ppermute | solution.py:64
  34.6 8.6 %collective-permute-start.20 = (bf16[16,4096]{1,0:T(8,128)(2,1)S(1)}, bf16[16,4096]{1,0:T(8,128)(2,1)S(1)}, u32[]{:S(2)}, u32[]{:S(2)}) collective-permute-start(bf16[16,4096]{1,0:T(8,128)(2,1)S(1)} %collective-permute-done.14.refs_3_), channel_id=1, source_target_pairs={{0,4},{1,5},{2,6},{3,7},{4,0},{5,1},{6,2},{7,3},{8,12},{9,13},{10,... | collective-permute-start | bytes 393224 | tf_op jit(solution)/shard_map/cross_pb/ppermute | solution.py:64
  38.6 5.0 %collective-permute-start.11 = (bf16[16,4096]{1,0:T(8,128)(2,1)S(1)}, bf16[16,4096]{1,0:T(8,128)(2,1)S(1)}, u32[]{:S(2)}, u32[]{:S(2)}) collective-permute-start(bf16[16,4096]{1,0:T(8,128)(2,1)S(1)} %get-tuple-element.47), channel_id=1, source_target_pairs={{0,16},{1,17},{2,18},{3,19},{4,20},{5,21},{6,22},{7,23},{8,24},{9,... | collective-permute-start | bytes 393224 | tf_op jit(solution)/shard_map/cross_pa/ppermute | solution.py:64
  42.6 8.3 %collective-permute-start.25 = (bf16[128,1024]{1,0:T(8,128)(2,1)S(1)}, bf16[128,1024]{1,0:T(8,128)(2,1)S(1)}, u32[]{:S(2)}, u32[]{:S(2)}) collective-permute-start(bf16[128,1024]{1,0:T(8,128)(2,1)S(1)} %get-tuple-element.49), channel_id=1, source_target_pairs={{0,1},{1,0},{2,3},{3,2},{4,5},{5,4},{6,7},{7,6},{8,9},{9,8},{10,11... | collective-permute-start | bytes 786440 | tf_op jit(solution)/shard_map/got1/ppermute | solution.py:64
  43.2 1.4 %collective-permute-start.22 = (bf16[16,4096]{1,0:T(8,128)(2,1)S(1)}, bf16[16,4096]{1,0:T(8,128)(2,1)S(1)}, u32[]{:S(2)}, u32[]{:S(2)}) collective-permute-start(bf16[16,4096]{1,0:T(8,128)(2,1)S(1)} %collective-permute-done.20.refs_1_), channel_id=1, source_target_pairs={{0,2},{1,3},{2,0},{3,1},{4,6},{5,7},{6,4},{7,5},{8,10},{9,11},{10,... | collective-permute-start | bytes 393224 | tf_op jit(solution)/shard_map/cross_pxb/ppermute | solution.py:64
  46.3 5.7 %collective-permute-start.24 = (bf16[64,512]{1,0:T(8,128)(2,1)S(1)}, bf16[64,512]{1,0:T(8,128)(2,1)S(1)}, u32[]{:S(2)}, u32[]{:S(2)}) collective-permute-start(bf16[64,512]{1,0:T(8,128)(2,1)S(1)} %get-tuple-element.56), channel_id=1, source_target_pairs={{0,1},{1,0},{2,3},{3,2},{4,5},{5,4},{6,7},{7,6},{8,9},{9,8},{10,11... | collective-permute-start | bytes 196616 | tf_op jit(solution)/shard_map/got3/ppermute | solution.py:64
  49.0 4.3 %collective-permute-start.23 = (bf16[64,512]{1,0:T(8,128)(2,1)S(1)}, bf16[64,512]{1,0:T(8,128)(2,1)S(1)}, u32[]{:S(2)}, u32[]{:S(2)}) collective-permute-start(bf16[64,512]{1,0:T(8,128)(2,1)S(1)} %get-tuple-element.54), channel_id=1, source_target_pairs={{0,1},{1,0},{2,3},{3,2},{4,5},{5,4},{6,7},{7,6},{8,9},{9,8},{10,11... | collective-permute-start | bytes 196616 | tf_op jit(solution)/shard_map/got2/ppermute | solution.py:64
  (4 other events, 13.4 us)

commit v7 on v6

--- a/solution.py
+++ b/solution.py
@@ -168,26 +168,25 @@
     precond_rows(q_ref, lefts, rights, mine)
 
 
-def rest_kernel(
-    weight_ref, layer_ref, q_hbm, train_hbm, lefts_ref, rights_ref, rest, train, weight, q_ref, sems
-):
+def rest_kernel(weight_ref, layer_ref, q_hbm, lefts_ref, rights_ref, rest, weight, q_ref, sem):
     at = pl.multiple_of((1 - lax.axis_index("parts")) * HALF, HALF)
-    q_copy = pltpu.make_async_copy(q_hbm.at[pl.ds(at, HALF), :], q_ref, sems.at[0])
+    q_copy = pltpu.make_async_copy(q_hbm.at[pl.ds(at, HALF), :], q_ref, sem)
     q_copy.start()
-    copies = []
-    for k in range(train.shape[0] // STEP):
-        here = pl.ds(k * STEP, STEP)
-        copies.append(pltpu.make_async_copy(train_hbm.at[here, :], train.at[here, :], sems.at[1 + k]))
-        copies[-1].start()
     weight[...] = jnp.full(weight.shape, weight_ref[layer_ref[0]])
     lefts, rights = [lefts_ref[0], lefts_ref[1]], [rights_ref[0], rights_ref[1]]
     q_copy.wait()
     precond_rows(q_ref, lefts, rights, rest)
-    for copy in copies:
-        copy.wait()
-
-
-def score_kernel(weight_ref, train_ref, *refs, picks, stored, early, columns):
+
+
+def score_kernel(weight_ref, train_ref, *refs, picks, stored, early, columns, fetch):
+    if fetch:
+        *refs, train, sems = refs
+        copies = []
+        for k, at in enumerate(range(*columns, STEP)):
+            here = pl.ds(at, STEP)
+            copies.append(pltpu.make_async_copy(train_ref.at[here, :], train.at[here, :], sems.at[k]))
+            copies[-1].start()
+        train_ref = train
     inputs, refs = refs[: len(picks)], refs[len(picks) :]
     n_before = sum(taken for _, _, taken in early)
     before, outs = refs[:n_before], refs[n_before:]
@@ -199,6 +198,8 @@
     near_is_mine = z // 2 == layer
     for at in range(*columns, STEP):
         there, here = slice(at, at + STEP), slice(at - columns[0], at - columns[0] + STEP)
+        if fetch:
+            copies[at // STEP].wait()
         value = lax.dot_general(
             train_ref[there, :], queries, (((1,), (1,)), ((), ())), preferred_element_type=f32
         )
@@ -228,10 +229,11 @@
     )(*inputs)
 
 
-def call_scores(weight, train, inputs, stored=0, early=(), columns=None):
+def call_scores(weight, train, inputs, stored=0, early=(), columns=None, fetch=False):
     columns = columns or (0, train.shape[0])
     n = columns[1] - columns[0]
     total = sum(count for _, rows in inputs for _, count in rows)
+    others = [a for a, _ in inputs] + [a for a, _, _ in early if a is not None]
     outs = [jax.ShapeDtypeStruct((stored, n), f32)] if stored else []
     if early:
         outs += [jax.ShapeDtypeStruct((total - stored, n), t) for t in (bf16, f32)]
@@ -242,9 +244,12 @@
             stored=stored,
             early=[(first, rows, a is not None) for a, first, rows in early],
             columns=columns,
+            fetch=fetch,
         ),
-        outs,
-        [weight, train, *[a for a, _ in inputs], *[a for a, _, _ in early if a is not None]],
+        outs + ([jax.ShapeDtypeStruct(train.shape, train.dtype)] if fetch else []),
+        [weight, train, *others],
+        [VMEM, HBM if fetch else VMEM] + [VMEM] * len(others),
+        [pltpu.SemaphoreType.DMA((n // STEP,))] if fetch else [],
     )
 
 
@@ -322,81 +327,63 @@
     )
     near = to_near(mine, "near")
     far = to_far(mine, "far")
-    rest, train, weight = kernel_call(
+    rest, weight = kernel_call(
         rest_kernel,
-        [shape((HALF, width), bf16), shape(train.shape, bf16), shape((8, STEP), f32)],
-        [in_hbm(layer_weight), layer_of, queries, train, lefts, rights],
-        [SMEM, SMEM, HBM, HBM, VMEM, VMEM],
-        [pltpu.VMEM((HALF, width), bf16), pltpu.SemaphoreType.DMA((1 + train.shape[0] // STEP,))],
-    )
-    score = functools.partial(call_scores, weight, train)
+        [shape((HALF, width), bf16), shape((8, STEP), f32)],
+        [in_hbm(layer_weight), layer_of, queries, lefts, rights],
+        [SMEM, SMEM, HBM, VMEM, VMEM],
+        [pltpu.VMEM((HALF, width), bf16), pltpu.SemaphoreType.DMA],
+    )
 
     def rows_of(*pieces):
         return [(piece, ((0, piece.shape[0]),)) for piece in pieces]
 
-    parts_of = lambda piece: (piece[:CHUNK], piece[CHUNK:])
     mine_x = to_core(mine, "mine_x")
-    rest_a, rest_b = parts_of(rest)
-    rest_xa = to_core(rest_a, "rest_xa")
-    rest_xb = to_core(rest_b, "rest_xb")
-    near = after(near, rest)
-    near_a, near_b = parts_of(near)
-    near_xa = to_core(near_a, "near_xa")
-    near_xb = to_core(near_b, "near_xb")
+    rest_x = to_core(rest, "rest_x")
+    near_x = to_core(near, "near_x")
     near_p = to_part(near, "near_p")
-    (early0,) = score(
-        rows_of(mine, mine_x, rest, rest_xa, rest_xb, near, near_xa, near_xb), stored=192
-    )
-
-    far = after(far, near, early0)
+    far = after(far, near)
     cross = to_near(far, "cross")
-    far_a, far_b = parts_of(far)
-    far_pa = to_part(far_a, "far_pa")
-    far_pb = to_part(far_b, "far_pb")
-    far_xa = to_core(after(far_a, near_p), "far_xa")
-    far_xb = to_core(after(far_b, near_p), "far_xb")
-    send0, keep0 = score(rows_of(far, far_xa, far_xb), early=[(early0, 0, 64)])
+    far_p = to_part(far, "far_p")
+    far_x = to_core(far, "far_x")
+    rest_x = after(rest_x, far)
+    early0, train = call_scores(
+        weight, train, rows_of(mine, mine_x, rest, rest_x), stored=128, fetch=True
+    )
+    score = functools.partial(call_scores, weight, train)
+    near_p = after(near_p, early0)
+    near_px = to_core(near_p, "near_px")
+    far_px = to_core(far_p, "far_px")
+    cross_pa = to_part(cross[:CHUNK], "cross_pa")
+    cross_pb = to_near(far_p[CHUNK:], "cross_pb")
+    cross_x = to_core(cross, "cross_x")
+    early1, send0, keep0 = score(
+        rows_of(near, near_x, near_p, near_px, far, far_x, far_p, far_px),
+        stored=128,
+        early=[(early0, 0, 128)],
+    )
     got0 = to_layer(send0, "got0")
-
-    far_pa, far_pb, near_p = after(far_pa, send0), after(far_pb, send0), after(near_p, send0)
-    near_px = to_core(near_p, "near_px")
-    far_pxa = to_core(far_pa, "far_pxa")
-    far_pxb = to_core(far_pb, "far_pxb")
-    cross_pb = to_near(far_pb, "cross_pb")
-    cross_a, cross_b = parts_of(cross)
-    cross_a = after(cross_a, send0)
-    cross_pa = to_part(cross_a, "cross_pa")
-    cross_xa = to_core(after(cross_a, far_pa, far_pb), "cross_xa")
-    cross_xb = to_core(after(cross_b, far_pa, far_pb), "cross_xb")
-    early1, send1, keep1 = score(
-        rows_of(near_p, near_px, far_pa, far_pb, far_pxa, far_pxb, cross, cross_xa, cross_xb),
-        stored=64,
-        early=[(early0, 64, 64), (early0, 128, 64)],
-    )
-    got1 = to_layer(send1, "got1")
-
-    cross_pa, cross_pb = after(cross_pa, send1, got0), after(cross_pb, send1, got0)
+    cross_pa, cross_pb = after(cross_pa, send0), after(cross_pb, send0)
     cross_pxa = to_core(cross_pa, "cross_pxa")
     cross_pxb = to_core(cross_pb, "cross_pxb")
-    last = rows_of(cross_pa, cross_pb, cross_pxa, cross_pxb)
+    last = rows_of(cross, cross_x, cross_pa, cross_pb, cross_pxa, cross_pxb)
     n = train.shape[0]
-    send2, keep2 = score(last, early=[(early1, 0, 64)], columns=(0, n // 2))
+    send1, keep1 = score(last, early=[(early1, 0, 128)], columns=(0, n // 2))
+    got1 = to_layer(send1, "got1")
+    early1 = after(early1, send1)
+    send2, keep2 = score(last, early=[(early1, 0, 128)], columns=(n // 2, n))
+    send2 = after(send2, got0)
     got2 = to_layer(send2, "got2")
-    send3, keep3 = score(last, early=[(early1, 0, 64)], columns=(n // 2, n))
-    got3 = to_layer(send3, "got3")
 
     train_ids, query_ids = train_ids[None, :], query_ids[:, None]
     most = call_final(
-        train_ids,
-        query_ids,
-        [keep0, got0, keep1, got1],
-        ((0, [(0, 1, 0, 0)]), (1, [(2, 3, 0, 0)]), (2, [(2, 3, 64, 0)])),
+        train_ids, query_ids, [keep0, got0], ((0, [(0, 1, 0, 0)]), (1, [(0, 1, 64, 0)]))
     )
     return call_final(
         train_ids,
         query_ids,
-        [keep2, got2, keep3, got3],
-        ((3, [(0, 1, 0, 0), (2, 3, 0, n // 2)]),),
+        [keep1, got1, keep2, got2],
+        ((2, [(0, 1, 0, 0), (2, 3, 0, n // 2)]), (3, [(0, 1, 64, 0), (2, 3, 64, n // 2)])),
         most,
     )
 

time: 54.3 us -> 50 us (0.921)
  the two profiles are of different devices: /device:TPU:16 before, /device:TPU:0 now
where the time goes in v7:
time: 50 us; the launch traced here: 49.8 us
  Pallas kernels  20 us (40%)
  starting transfers between devices  17 us (34%)
  waiting for transfers between devices  11.9 us (24%)
  between operations  0.78 us (2%)
    pallas_call x6, Pallas kernels, kernel_call(): pl.pallas_call(kernel, out_shape=outs, in_specs=specs or [VMEM] * len(inp...  18.1 us
    ppermute x19, starting transfers between devices, permute(): return lax.ppermute(value, AXES, pairs)  17 us
    ppermute x19, waiting for transfers between devices, permute(): return lax.ppermute(value, AXES, pairs)  11.9 us
    pallas_call x2, Pallas kernels, call_final(): pl.pallas_call(functools.partial(final_kernel, groups=groups, n_given=len...  1.83 us
  transfers between devices with their start and end apart: 19, of which 8 were waited for; matrix products, arithmetic and copies ran while one was open for 0% of the time, Pallas kernels for 33%

profile of v7, /device:TPU:0, one launch (start us, length us, event | category | flops | bytes accessed | tf_op | source)
XLA Modules:
  0.0 49.8 jit_solution(5553629170723804375)
XLA Ops:
  0.0 2.8 %shard_map.82 = (bf16[32,4096]{1,0:T(8,128)(2,1)S(1)}, bf16[2,256,256]{2,1,0:T(8,128)(2,1)S(1)}, bf16[2,256,512]{2,1,0:T(8,128)(2,1)S(1)}) custom-call(bf16[64,4096]{1,0:T(8,128)(2,1)} %bitcast.9, f32[64,64]{1,0:T(8,128)} %bitcast.11, f32[64,64]{1,0:T(8,128)} %bitcast.12), custom_call_target="tpu_custom_call" | custom-call | tf_op jit(solution)/shard_map/pallas_call | solution.py:222
  2.8 3.1 %collective-permute-start.3 = (bf16[32,4096]{1,0:T(8,128)(2,1)S(1)}, bf16[32,4096]{1,0:T(8,128)(2,1)S(1)}, u32[]{:S(2)}, u32[]{:S(2)}) collective-permute-start(bf16[32,4096]{1,0:T(8,128)(2,1)S(1)} %get-tuple-element.29.refs_0_), channel_id=1, source_target_pairs={{0,4},{1,5},{2,6},{3,7},{4,0},{5,1},{6,2},{7,3},{8,12},{9,13},{10,... | collective-permute-start | bytes 786440 | tf_op jit(solution)/shard_map/near/ppermute | solution.py:64
  5.9 2.5 %collective-permute-start.2 = (bf16[32,4096]{1,0:T(8,128)(2,1)S(1)}, bf16[32,4096]{1,0:T(8,128)(2,1)S(1)}, u32[]{:S(2)}, u32[]{:S(2)}) collective-permute-start(bf16[32,4096]{1,0:T(8,128)(2,1)S(1)} %get-tuple-element.29.refs_0_), channel_id=1, source_target_pairs={{0,12},{1,13},{2,14},{3,15},{4,8},{5,9},{6,10},{7,11},{8,4},{9,5},... | collective-permute-start | bytes 786440 | tf_op jit(solution)/shard_map/far/ppermute | solution.py:64
  9.0 3.3 %shard_map.83 = (bf16[32,4096]{1,0:T(8,128)(2,1)S(1)}, f32[8,256]{1,0:T(8,128)S(1)}) custom-call(f32[2]{0:T(128)} %weight_ref.1, s32[1]{0:T(128)S(6)} %copy.13.layer_ref, bf16[64,4096]{1,0:T(8,128)(2,1)} %bitcast.10, bf16[2,256,256]{2,1,0:T(8,128)(2,1)S(1)} %get-tuple-element.26.lefts_ref, bf16[2,256,512]{2,1,0:T(8,128)(2,1)S(1)} %get-tuple-element.27.rights_ref), custom_call_target="tpu_custom_call" | custom-call | tf_op jit(solution)/shard_map/pallas_call | solution.py:222
  12.9 1.5 %collective-permute-start.8 = (bf16[32,4096]{1,0:T(8,128)(2,1)S(1)}, bf16[32,4096]{1,0:T(8,128)(2,1)S(1)}, u32[]{:S(2)}, u32[]{:S(2)}) collective-permute-start(bf16[32,4096]{1,0:T(8,128)(2,1)S(1)} %collective-permute-done.3.refs_0_), channel_id=1, source_target_pairs={{0,16},{1,17},{2,18},{3,19},{4,20},{5,21},{6,22},{7,23},{8,24},{9,... | collective-permute-start | bytes 786440 | tf_op jit(solution)/shard_map/near_p/ppermute | solution.py:64
  14.4 5.7 %collective-permute-done.2.refs_4_ = bf16[32,4096]{1,0:T(8,128)(2,1)S(1)} collective-permute-done((bf16[32,4096]{1,0:T(8,128)(2,1)S(1)}, bf16[32,4096]{1,0:T(8,128)(2,1)S(1)}, u32[]{:S(2)}, u32[]{:S(2)}) %collective-permute-start.2) | collective-permute-done | bytes 262176 | tf_op jit(solution)/shard_map/far/ppermute | solution.py:64
  20.1 1.5 %collective-permute-start.11 = (bf16[32,4096]{1,0:T(8,128)(2,1)S(1)}, bf16[32,4096]{1,0:T(8,128)(2,1)S(1)}, u32[]{:S(2)}, u32[]{:S(2)}) collective-permute-start(bf16[32,4096]{1,0:T(8,128)(2,1)S(1)} %collective-permute-done.2.refs_4_), channel_id=1, source_target_pairs={{0,16},{1,17},{2,18},{3,19},{4,20},{5,21},{6,22},{7,23},{8,24},{9,... | collective-permute-start | bytes 786440 | tf_op jit(solution)/shard_map/far_p/ppermute | solution.py:64
  21.6 0.6 %collective-permute-start.4 = (bf16[32,4096]{1,0:T(8,128)(2,1)S(1)}, bf16[32,4096]{1,0:T(8,128)(2,1)S(1)}, u32[]{:S(2)}, u32[]{:S(2)}) collective-permute-start(bf16[32,4096]{1,0:T(8,128)(2,1)S(1)} %collective-permute-done.2.refs_4_), channel_id=1, source_target_pairs={{0,4},{1,5},{2,6},{3,7},{4,0},{5,1},{6,2},{7,3},{8,12},{9,13},{10,... | collective-permute-start | bytes 786440 | tf_op jit(solution)/shard_map/cross/ppermute | solution.py:64
  22.4 6.8 %shard_map.84 = (f32[128,1024]{1,0:T(8,128)S(1)}, bf16[1024,4096]{1,0:T(8,128)(2,1)S(1)}) custom-call(f32[8,256]{1,0:T(8,128)S(1)} %get-tuple-element.28.weight_ref, bf16[1024,4096]{1,0:T(8,128)(2,1)} %bitcast.8, bf16[32,4096]{1,0:T(8,128)(2,1)S(1)} %get-tuple-element.29.refs_0_, bf16[32,4096]{1,0:T(8,128)(2,1)S(1)} %collective-permute-done.refs_1_, ...), custom_call_target="tpu_custom_call" | custom-call | tf_op jit(solution)/shard_map/pallas_call | solution.py:222
  30.4 1.0 %collective-permute-start.13 = (bf16[16,4096]{1,0:T(8,128)(2,1)S(1)}, bf16[16,4096]{1,0:T(8,128)(2,1)S(1)}, u32[]{:S(2)}, u32[]{:S(2)}) collective-permute-start(bf16[16,4096]{1,0:T(8,128)(2,1)S(1)} %slice.9), channel_id=1, source_target_pairs={{0,4},{1,5},{2,6},{3,7},{4,0},{5,1},{6,2},{7,3},{8,12},{9,13},{10,... | collective-permute-start | bytes 393224 | tf_op jit(solution)/shard_map/cross_pb/ppermute | solution.py:64
  31.4 0.6 %collective-permute-start.6 = (bf16[16,4096]{1,0:T(8,128)(2,1)S(1)}, bf16[16,4096]{1,0:T(8,128)(2,1)S(1)}, u32[]{:S(2)}, u32[]{:S(2)}) collective-permute-start(bf16[16,4096]{1,0:T(8,128)(2,1)S(1)} %slice.8), channel_id=1, source_target_pairs={{0,16},{1,17},{2,18},{3,19},{4,20},{5,21},{6,22},{7,23},{8,24},{9,... | collective-permute-start | bytes 393224 | tf_op jit(solution)/shard_map/cross_pa/ppermute | solution.py:64
  32.0 2.5 %shard_map.85 = (f32[128,1024]{1,0:T(8,128)S(1)}, bf16[128,1024]{1,0:T(8,128)(2,1)S(1)}, f32[128,1024]{1,0:T(8,128)S(1)}) custom-call(f32[8,256]{1,0:T(8,128)S(1)} %get-tuple-element.28.weight_ref, bf16[1024,4096]{1,0:T(8,128)(2,1)S(1)} %get-tuple-element.33.train_ref, bf16[32,4096]{1,0:T(8,128)(2,1)S(1)} %collective-permute-done.3.refs_0_, ...), custom_call_target="tpu_custom_call" | custom-call | tf_op jit(solution)/shard_map/pallas_call | solution.py:222
  34.5 1.6 %collective-permute-start.17 = (bf16[128,1024]{1,0:T(8,128)(2,1)S(1)}, bf16[128,1024]{1,0:T(8,128)(2,1)S(1)}, u32[]{:S(2)}, u32[]{:S(2)}) collective-permute-start(bf16[128,1024]{1,0:T(8,128)(2,1)S(1)} %get-tuple-element.36), channel_id=1, source_target_pairs={{0,1},{1,0},{2,3},{3,2},{4,5},{5,4},{6,7},{7,6},{8,9},{9,8},{10,11... | collective-permute-start | bytes 786440 | tf_op jit(solution)/shard_map/got0/ppermute | solution.py:64
  36.3 0.5 %collective-permute-done.6.refs_2_ = bf16[16,4096]{1,0:T(8,128)(2,1)S(1)} collective-permute-done((bf16[16,4096]{1,0:T(8,128)(2,1)S(1)}, bf16[16,4096]{1,0:T(8,128)(2,1)S(1)}, u32[]{:S(2)}, u32[]{:S(2)}) %collective-permute-start.6) | collective-permute-done | bytes 131104 | tf_op jit(solution)/shard_map/cross_pa/ppermute | solution.py:64
  36.9 0.6 %collective-permute-done.15.refs_5_ = bf16[16,4096]{1,0:T(8,128)(2,1)S(1)} collective-permute-done((bf16[16,4096]{1,0:T(8,128)(2,1)S(1)}, bf16[16,4096]{1,0:T(8,128)(2,1)S(1)}, u32[]{:S(2)}, u32[]{:S(2)}) %collective-permute-start.15) | collective-permute-done | bytes 131104 | tf_op jit(solution)/shard_map/cross_pxb/ppermute | solution.py:64
  37.5 0.8 %collective-permute-done.14.refs_4_ = bf16[16,4096]{1,0:T(8,128)(2,1)S(1)} collective-permute-done((bf16[16,4096]{1,0:T(8,128)(2,1)S(1)}, bf16[16,4096]{1,0:T(8,128)(2,1)S(1)}, u32[]{:S(2)}, u32[]{:S(2)}) %collective-permute-start.14) | collective-permute-done | bytes 131104 | tf_op jit(solution)/shard_map/cross_pxa/ppermute | solution.py:64
  38.2 1.3 %shard_map.86 = (bf16[128,512]{1,0:T(8,128)(2,1)S(1)}, f32[128,512]{1,0:T(8,128)S(1)}) custom-call(f32[8,256]{1,0:T(8,128)S(1)} %get-tuple-element.28.weight_ref, bf16[1024,4096]{1,0:T(8,128)(2,1)S(1)} %get-tuple-element.33.train_ref, bf16[32,4096]{1,0:T(8,128)(2,1)S(1)} %collective-permute-done.4.refs_0_, ...), custom_call_target="tpu_custom_call" | custom-call | tf_op jit(solution)/shard_map/pallas_call | solution.py:222
  39.6 1.6 %collective-permute-start.16 = (bf16[128,512]{1,0:T(8,128)(2,1)S(1)}, bf16[128,512]{1,0:T(8,128)(2,1)S(1)}, u32[]{:S(2)}, u32[]{:S(2)}) collective-permute-start(bf16[128,512]{1,0:T(8,128)(2,1)S(1)} %get-tuple-element.41), channel_id=1, source_target_pairs={{0,1},{1,0},{2,3},{3,2},{4,5},{5,4},{6,7},{7,6},{8,9},{9,8},{10,11... | collective-permute-start | bytes 393224 | tf_op jit(solution)/shard_map/got1/ppermute | solution.py:64
  41.2 1.3 %shard_map.87 = (bf16[128,512]{1,0:T(8,128)(2,1)S(1)}, f32[128,512]{1,0:T(8,128)S(1)}) custom-call(f32[8,256]{1,0:T(8,128)S(1)} %get-tuple-element.28.weight_ref, bf16[1024,4096]{1,0:T(8,128)(2,1)S(1)} %get-tuple-element.33.train_ref, bf16[32,4096]{1,0:T(8,128)(2,1)S(1)} %collective-permute-done.4.refs_0_, ...), custom_call_target="tpu_custom_call" | custom-call | tf_op jit(solution)/shard_map/pallas_call | solution.py:222
  42.5 1.2 %collective-permute-done.17.refs_1_ = bf16[128,1024]{1,0:T(8,128)(2,1)S(1)} collective-permute-done((bf16[128,1024]{1,0:T(8,128)(2,1)S(1)}, bf16[128,1024]{1,0:T(8,128)(2,1)S(1)}, u32[]{:S(2)}, u32[]{:S(2)}) %collective-permute-start.17) | collective-permute-done | bytes 262176 | tf_op jit(solution)/shard_map/got0/ppermute | solution.py:64
  43.7 1.5 %collective-permute-start.18 = (bf16[128,512]{1,0:T(8,128)(2,1)S(1)}, bf16[128,512]{1,0:T(8,128)(2,1)S(1)}, u32[]{:S(2)}, u32[]{:S(2)}) collective-permute-start(bf16[128,512]{1,0:T(8,128)(2,1)S(1)} %get-tuple-element.45), channel_id=1, source_target_pairs={{0,1},{1,0},{2,3},{3,2},{4,5},{5,4},{6,7},{7,6},{8,9},{9,8},{10,11... | collective-permute-start | bytes 393224 | tf_op jit(solution)/shard_map/got2/ppermute | solution.py:64
  45.4 0.9 %shard_map.88.refs_4_ = f32[256,1024]{1,0:T(8,128)} custom-call(s32[1,1024]{1,0:T(1,128)S(1)} %bitcast.6, s32[256,1]{1,0:T(8,128)S(1)} %copy.11.query_ids, f32[128,1024]{1,0:T(8,128)S(1)} %get-tuple-element.46.refs_0_, bf16[128,1024]{1,0:T(8,128)(2,1)S(1)} %collective-permute-done.17.refs_1_), custom_call_target="tpu_custom_call" | custom-call | tf_op jit(solution)/shard_map/pallas_call | solution.py:288
  46.5 2.4 %collective-permute-done.18.refs_3_ = bf16[128,512]{1,0:T(8,128)(2,1)S(1)} collective-permute-done((bf16[128,512]{1,0:T(8,128)(2,1)S(1)}, bf16[128,512]{1,0:T(8,128)(2,1)S(1)}, u32[]{:S(2)}, u32[]{:S(2)}) %collective-permute-start.18) | collective-permute-done | bytes 131104 | tf_op jit(solution)/shard_map/got2/ppermute | solution.py:64
  48.9 0.9 %shard_map.89 = f32[256,1024]{1,0:T(8,128)} custom-call(s32[1,1024]{1,0:T(1,128)S(1)} %bitcast.7, s32[256,1]{1,0:T(8,128)S(1)} %copy.11.query_ids, f32[128,512]{1,0:T(8,128)S(1)} %get-tuple-element.40.refs_0_, bf16[128,512]{1,0:T(8,128)(2,1)S(1)} %collective-permute-done.16.refs_1_, ...), custom_call_target="tpu_custom_call", output_to_operand_aliasing={{}: (6, {})} | custom-call | tf_op jit(solution)/shard_map/pallas_call | solution.py:288
  (29 shorter events, 2.5 us)
Async XLA Ops:
  2.8 10.1 %collective-permute-start.3 = (bf16[32,4096]{1,0:T(8,128)(2,1)S(1)}, bf16[32,4096]{1,0:T(8,128)(2,1)S(1)}, u32[]{:S(2)}, u32[]{:S(2)}) collective-permute-start(bf16[32,4096]{1,0:T(8,128)(2,1)S(1)} %get-tuple-element.29.refs_0_), channel_id=1, source_target_pairs={{0,4},{1,5},{2,6},{3,7},{4,0},{5,1},{6,2},{7,3},{8,12},{9,13},{10,... | collective-permute-start | bytes 786440 | tf_op jit(solution)/shard_map/near/ppermute | solution.py:64
  5.9 14.2 %collective-permute-start.2 = (bf16[32,4096]{1,0:T(8,128)(2,1)S(1)}, bf16[32,4096]{1,0:T(8,128)(2,1)S(1)}, u32[]{:S(2)}, u32[]{:S(2)}) collective-permute-start(bf16[32,4096]{1,0:T(8,128)(2,1)S(1)} %get-tuple-element.29.refs_0_), channel_id=1, source_target_pairs={{0,12},{1,13},{2,14},{3,15},{4,8},{5,9},{6,10},{7,11},{8,4},{9,5},... | collective-permute-start | bytes 786440 | tf_op jit(solution)/shard_map/far/ppermute | solution.py:64
  12.4 9.3 %collective-permute-start.1 = (bf16[32,4096]{1,0:T(8,128)(2,1)S(1)}, bf16[32,4096]{1,0:T(8,128)(2,1)S(1)}, u32[]{:S(2)}, u32[]{:S(2)}) collective-permute-start(bf16[32,4096]{1,0:T(8,128)(2,1)S(1)} %get-tuple-element.30.refs_2_), channel_id=1, source_target_pairs={{0,2},{1,3},{2,0},{3,1},{4,6},{5,7},{6,4},{7,5},{8,10},{9,11},{10,... | collective-permute-start | bytes 786440 | tf_op jit(solution)/shard_map/rest_x/ppermute | solution.py:64
  12.4 9.8 %collective-permute-start = (bf16[32,4096]{1,0:T(8,128)(2,1)S(1)}, bf16[32,4096]{1,0:T(8,128)(2,1)S(1)}, u32[]{:S(2)}, u32[]{:S(2)}) collective-permute-start(bf16[32,4096]{1,0:T(8,128)(2,1)S(1)} %get-tuple-element.29.refs_0_), channel_id=1, source_target_pairs={{0,2},{1,3},{2,0},{3,1},{4,6},{5,7},{6,4},{7,5},{8,10},{9,11},{10,... | collective-permute-start | bytes 786440 | tf_op jit(solution)/shard_map/mine_x/ppermute | solution.py:64
  12.9 16.3 %collective-permute-start.8 = (bf16[32,4096]{1,0:T(8,128)(2,1)S(1)}, bf16[32,4096]{1,0:T(8,128)(2,1)S(1)}, u32[]{:S(2)}, u32[]{:S(2)}) collective-permute-start(bf16[32,4096]{1,0:T(8,128)(2,1)S(1)} %collective-permute-done.3.refs_0_), channel_id=1, source_target_pairs={{0,16},{1,17},{2,18},{3,19},{4,20},{5,21},{6,22},{7,23},{8,24},{9,... | collective-permute-start | bytes 786440 | tf_op jit(solution)/shard_map/near_p/ppermute | solution.py:64
  20.1 9.5 %collective-permute-start.11 = (bf16[32,4096]{1,0:T(8,128)(2,1)S(1)}, bf16[32,4096]{1,0:T(8,128)(2,1)S(1)}, u32[]{:S(2)}, u32[]{:S(2)}) collective-permute-start(bf16[32,4096]{1,0:T(8,128)(2,1)S(1)} %collective-permute-done.2.refs_4_), channel_id=1, source_target_pairs={{0,16},{1,17},{2,18},{3,19},{4,20},{5,21},{6,22},{7,23},{8,24},{9,... | collective-permute-start | bytes 786440 | tf_op jit(solution)/shard_map/far_p/ppermute | solution.py:64
  21.6 9.8 %collective-permute-start.10 = (bf16[32,4096]{1,0:T(8,128)(2,1)S(1)}, bf16[32,4096]{1,0:T(8,128)(2,1)S(1)}, u32[]{:S(2)}, u32[]{:S(2)}) collective-permute-start(bf16[32,4096]{1,0:T(8,128)(2,1)S(1)} %collective-permute-done.2.refs_4_), channel_id=1, source_target_pairs={{0,2},{1,3},{2,0},{3,1},{4,6},{5,7},{6,4},{7,5},{8,10},{9,11},{10,... | collective-permute-start | bytes 786440 | tf_op jit(solution)/shard_map/far_x/ppermute | solution.py:64
  21.6 8.7 %collective-permute-start.4 = (bf16[32,4096]{1,0:T(8,128)(2,1)S(1)}, bf16[32,4096]{1,0:T(8,128)(2,1)S(1)}, u32[]{:S(2)}, u32[]{:S(2)}) collective-permute-start(bf16[32,4096]{1,0:T(8,128)(2,1)S(1)} %collective-permute-done.2.refs_4_), channel_id=1, source_target_pairs={{0,4},{1,5},{2,6},{3,7},{4,0},{5,1},{6,2},{7,3},{8,12},{9,13},{10,... | collective-permute-start | bytes 786440 | tf_op jit(solution)/shard_map/cross/ppermute | solution.py:64
  22.2 9.8 %collective-permute-start.7 = (bf16[32,4096]{1,0:T(8,128)(2,1)S(1)}, bf16[32,4096]{1,0:T(8,128)(2,1)S(1)}, u32[]{:S(2)}, u32[]{:S(2)}) collective-permute-start(bf16[32,4096]{1,0:T(8,128)(2,1)S(1)} %collective-permute-done.3.refs_0_), channel_id=1, source_target_pairs={{0,2},{1,3},{2,0},{3,1},{4,6},{5,7},{6,4},{7,5},{8,10},{9,11},{10,... | collective-permute-start | bytes 786440 | tf_op jit(solution)/shard_map/near_x/ppermute | solution.py:64
  29.2 2.8 %collective-permute-start.9 = (bf16[32,4096]{1,0:T(8,128)(2,1)S(1)}, bf16[32,4096]{1,0:T(8,128)(2,1)S(1)}, u32[]{:S(2)}, u32[]{:S(2)}) collective-permute-start(bf16[32,4096]{1,0:T(8,128)(2,1)S(1)} %collective-permute-done.8.refs_2_), channel_id=1, source_target_pairs={{0,2},{1,3},{2,0},{3,1},{4,6},{5,7},{6,4},{7,5},{8,10},{9,11},{10,... | collective-permute-start | bytes 786440 | tf_op jit(solution)/shard_map/near_px/ppermute | solution.py:64
  29.6 2.4 %collective-permute-start.12 = (bf16[32,4096]{1,0:T(8,128)(2,1)S(1)}, bf16[32,4096]{1,0:T(8,128)(2,1)S(1)}, u32[]{:S(2)}, u32[]{:S(2)}) collective-permute-start(bf16[32,4096]{1,0:T(8,128)(2,1)S(1)} %collective-permute-done.11.refs_6_), channel_id=1, source_target_pairs={{0,2},{1,3},{2,0},{3,1},{4,6},{5,7},{6,4},{7,5},{8,10},{9,11},{10,... | collective-permute-start | bytes 786440 | tf_op jit(solution)/shard_map/far_px/ppermute | solution.py:64
  30.4 5.8 %collective-permute-start.13 = (bf16[16,4096]{1,0:T(8,128)(2,1)S(1)}, bf16[16,4096]{1,0:T(8,128)(2,1)S(1)}, u32[]{:S(2)}, u32[]{:S(2)}) collective-permute-start(bf16[16,4096]{1,0:T(8,128)(2,1)S(1)} %slice.9), channel_id=1, source_target_pairs={{0,4},{1,5},{2,6},{3,7},{4,0},{5,1},{6,2},{7,3},{8,12},{9,13},{10,... | collective-permute-start | bytes 393224 | tf_op jit(solution)/shard_map/cross_pb/ppermute | solution.py:64
  31.4 5.5 %collective-permute-start.6 = (bf16[16,4096]{1,0:T(8,128)(2,1)S(1)}, bf16[16,4096]{1,0:T(8,128)(2,1)S(1)}, u32[]{:S(2)}, u32[]{:S(2)}) collective-permute-start(bf16[16,4096]{1,0:T(8,128)(2,1)S(1)} %slice.8), channel_id=1, source_target_pairs={{0,16},{1,17},{2,18},{3,19},{4,20},{5,21},{6,22},{7,23},{8,24},{9,... | collective-permute-start | bytes 393224 | tf_op jit(solution)/shard_map/cross_pa/ppermute | solution.py:64
  32.0 4.9 %collective-permute-start.5 = (bf16[32,4096]{1,0:T(8,128)(2,1)S(1)}, bf16[32,4096]{1,0:T(8,128)(2,1)S(1)}, u32[]{:S(2)}, u32[]{:S(2)}) collective-permute-start(bf16[32,4096]{1,0:T(8,128)(2,1)S(1)} %collective-permute-done.4.refs_0_), channel_id=1, source_target_pairs={{0,2},{1,3},{2,0},{3,1},{4,6},{5,7},{6,4},{7,5},{8,10},{9,11},{10,... | collective-permute-start | bytes 786440 | tf_op jit(solution)/shard_map/cross_x/ppermute | solution.py:64
  34.5 9.2 %collective-permute-start.17 = (bf16[128,1024]{1,0:T(8,128)(2,1)S(1)}, bf16[128,1024]{1,0:T(8,128)(2,1)S(1)}, u32[]{:S(2)}, u32[]{:S(2)}) collective-permute-start(bf16[128,1024]{1,0:T(8,128)(2,1)S(1)} %get-tuple-element.36), channel_id=1, source_target_pairs={{0,1},{1,0},{2,3},{3,2},{4,5},{5,4},{6,7},{7,6},{8,9},{9,8},{10,11... | collective-permute-start | bytes 786440 | tf_op jit(solution)/shard_map/got0/ppermute | solution.py:64
  36.1 1.3 %collective-permute-start.15 = (bf16[16,4096]{1,0:T(8,128)(2,1)S(1)}, bf16[16,4096]{1,0:T(8,128)(2,1)S(1)}, u32[]{:S(2)}, u32[]{:S(2)}) collective-permute-start(bf16[16,4096]{1,0:T(8,128)(2,1)S(1)} %collective-permute-done.13.refs_3_), channel_id=1, source_target_pairs={{0,2},{1,3},{2,0},{3,1},{4,6},{5,7},{6,4},{7,5},{8,10},{9,11},{10,... | collective-permute-start | bytes 393224 | tf_op jit(solution)/shard_map/cross_pxb/ppermute | solution.py:64
  36.9 1.3 %collective-permute-start.14 = (bf16[16,4096]{1,0:T(8,128)(2,1)S(1)}, bf16[16,4096]{1,0:T(8,128)(2,1)S(1)}, u32[]{:S(2)}, u32[]{:S(2)}) collective-permute-start(bf16[16,4096]{1,0:T(8,128)(2,1)S(1)} %collective-permute-done.6.refs_2_), channel_id=1, source_target_pairs={{0,2},{1,3},{2,0},{3,1},{4,6},{5,7},{6,4},{7,5},{8,10},{9,11},{10,... | collective-permute-start | bytes 393224 | tf_op jit(solution)/shard_map/cross_pxa/ppermute | solution.py:64
  38.2 7.0 %copy-start.1 = (s32[256]{0:T(256)S(1)}, s32[256]{0:T(256)}, u32[]{:S(2)}) copy-start(s32[256]{0:T(256)} %param.15) | copy-start | bytes 3076
  38.2 7.1 %copy-start = (s32[1024]{0:T(1024)S(1)}, s32[1024]{0:T(1024)}, u32[]{:S(2)}) copy-start(s32[1024]{0:T(1024)} %param.14) | copy-start | bytes 12292
  39.6 6.9 %collective-permute-start.16 = (bf16[128,512]{1,0:T(8,128)(2,1)S(1)}, bf16[128,512]{1,0:T(8,128)(2,1)S(1)}, u32[]{:S(2)}, u32[]{:S(2)}) collective-permute-start(bf16[128,512]{1,0:T(8,128)(2,1)S(1)} %get-tuple-element.41), channel_id=1, source_target_pairs={{0,1},{1,0},{2,3},{3,2},{4,5},{5,4},{6,7},{7,6},{8,9},{9,8},{10,11... | collective-permute-start | bytes 393224 | tf_op jit(solution)/shard_map/got1/ppermute | solution.py:64
  43.7 5.2 %collective-permute-start.18 = (bf16[128,512]{1,0:T(8,128)(2,1)S(1)}, bf16[128,512]{1,0:T(8,128)(2,1)S(1)}, u32[]{:S(2)}, u32[]{:S(2)}) collective-permute-start(bf16[128,512]{1,0:T(8,128)(2,1)S(1)} %get-tuple-element.45), channel_id=1, source_target_pairs={{0,1},{1,0},{2,3},{3,2},{4,5},{5,4},{6,7},{7,6},{8,9},{9,8},{10,11... | collective-permute-start | bytes 393224 | tf_op jit(solution)/shard_map/got2/ppermute | solution.py:64

commit v8 on v7

--- a/solution.py
+++ b/solution.py
@@ -178,15 +178,17 @@
     precond_rows(q_ref, lefts, rights, rest)
 
 
-def score_kernel(weight_ref, train_ref, *refs, picks, stored, early, columns, fetch):
-    if fetch:
-        *refs, train, sems = refs
-        copies = []
-        for k, at in enumerate(range(*columns, STEP)):
-            here = pl.ds(at, STEP)
-            copies.append(pltpu.make_async_copy(train_ref.at[here, :], train.at[here, :], sems.at[k]))
-            copies[-1].start()
-        train_ref = train
+def train_kernel(train_hbm, _, train, sems):
+    copies = []
+    for k in range(train.shape[0] // STEP):
+        here = pl.ds(k * STEP, STEP)
+        copies.append(pltpu.make_async_copy(train_hbm.at[here, :], train.at[here, :], sems.at[k]))
+        copies[-1].start()
+    for copy in copies:
+        copy.wait()
+
+
+def score_kernel(weight_ref, train_ref, *refs, picks, stored, early, columns):
     inputs, refs = refs[: len(picks)], refs[len(picks) :]
     n_before = sum(taken for _, _, taken in early)
     before, outs = refs[:n_before], refs[n_before:]
@@ -198,8 +200,6 @@
     near_is_mine = z // 2 == layer
     for at in range(*columns, STEP):
         there, here = slice(at, at + STEP), slice(at - columns[0], at - columns[0] + STEP)
-        if fetch:
-            copies[at // STEP].wait()
         value = lax.dot_general(
             train_ref[there, :], queries, (((1,), (1,)), ((), ())), preferred_element_type=f32
         )
@@ -229,7 +229,7 @@
     )(*inputs)
 
 
-def call_scores(weight, train, inputs, stored=0, early=(), columns=None, fetch=False):
+def call_scores(weight, train, inputs, stored=0, early=(), columns=None):
     columns = columns or (0, train.shape[0])
     n = columns[1] - columns[0]
     total = sum(count for _, rows in inputs for _, count in rows)
@@ -244,12 +244,9 @@
             stored=stored,
             early=[(first, rows, a is not None) for a, first, rows in early],
             columns=columns,
-            fetch=fetch,
         ),
-        outs + ([jax.ShapeDtypeStruct(train.shape, train.dtype)] if fetch else []),
+        outs,
         [weight, train, *others],
-        [VMEM, HBM if fetch else VMEM] + [VMEM] * len(others),
-        [pltpu.SemaphoreType.DMA((n // STEP,))] if fetch else [],
     )
 
 
@@ -326,7 +323,6 @@
         ],
     )
     near = to_near(mine, "near")
-    far = to_far(mine, "far")
     rest, weight = kernel_call(
         rest_kernel,
         [shape((HALF, width), bf16), shape((8, STEP), f32)],
@@ -334,56 +330,68 @@
         [SMEM, SMEM, HBM, VMEM, VMEM],
         [pltpu.VMEM((HALF, width), bf16), pltpu.SemaphoreType.DMA],
     )
+    far = to_far(after(mine, rest), "far")
+    (train,) = kernel_call(
+        train_kernel,
+        [shape(train.shape, bf16)],
+        [train, weight],
+        [HBM, VMEM],
+        [pltpu.SemaphoreType.DMA((train.shape[0] // STEP,))],
+    )
+    score = functools.partial(call_scores, weight, train)
 
     def rows_of(*pieces):
         return [(piece, ((0, piece.shape[0]),)) for piece in pieces]
 
     mine_x = to_core(mine, "mine_x")
     rest_x = to_core(rest, "rest_x")
+    near = after(near, train)
     near_x = to_core(near, "near_x")
     near_p = to_part(near, "near_p")
     far = after(far, near)
     cross = to_near(far, "cross")
     far_p = to_part(far, "far_p")
-    far_x = to_core(far, "far_x")
-    rest_x = after(rest_x, far)
-    early0, train = call_scores(
-        weight, train, rows_of(mine, mine_x, rest, rest_x), stored=128, fetch=True
-    )
-    score = functools.partial(call_scores, weight, train)
-    near_p = after(near_p, early0)
+    far_xa = to_core(after(far[:CHUNK], near_p), "far_xa")
+    far_xb = to_core(after(far[CHUNK:], near_p), "far_xb")
+    early0, send0, keep0 = score(
+        rows_of(mine, mine_x, rest, rest_x, far, far_xa, far_xb), stored=128, early=[(None, 0, 64)]
+    )
+    got0 = to_layer(send0, "got0")
+    near_p, far_p, cross = after(near_p, send0), after(far_p, send0), after(cross, send0)
     near_px = to_core(near_p, "near_px")
     far_px = to_core(far_p, "far_px")
     cross_pa = to_part(cross[:CHUNK], "cross_pa")
     cross_pb = to_near(far_p[CHUNK:], "cross_pb")
     cross_x = to_core(cross, "cross_x")
-    early1, send0, keep0 = score(
-        rows_of(near, near_x, near_p, near_px, far, far_x, far_p, far_px),
+    early1, send1, keep1 = score(
+        rows_of(near, near_x, near_p, near_px, far_p, far_px, cross, cross_x),
         stored=128,
-        early=[(early0, 0, 128)],
-    )
-    got0 = to_layer(send0, "got0")
-    cross_pa, cross_pb = after(cross_pa, send0), after(cross_pb, send0)
+        early=[(early0, 64, 64), (None, 0, 64)],
+    )
+    got1 = to_layer(send1, "got1")
+    cross_pa, cross_pb = after(cross_pa, send1, got0), after(cross_pb, send1, got0)
     cross_pxa = to_core(cross_pa, "cross_pxa")
     cross_pxb = to_core(cross_pb, "cross_pxb")
-    last = rows_of(cross, cross_x, cross_pa, cross_pb, cross_pxa, cross_pxb)
+    last = rows_of(cross_pa, cross_pb, cross_pxa, cross_pxb)
     n = train.shape[0]
-    send1, keep1 = score(last, early=[(early1, 0, 128)], columns=(0, n // 2))
-    got1 = to_layer(send1, "got1")
-    early1 = after(early1, send1)
-    send2, keep2 = score(last, early=[(early1, 0, 128)], columns=(n // 2, n))
-    send2 = after(send2, got0)
+    send2, keep2 = score(last, early=[(early1, 64, 64)], columns=(0, n // 2))
     got2 = to_layer(send2, "got2")
+    early1 = after(early1, send2)
+    send3, keep3 = score(last, early=[(early1, 64, 64)], columns=(n // 2, n))
+    got3 = to_layer(send3, "got3")
 
     train_ids, query_ids = train_ids[None, :], query_ids[:, None]
     most = call_final(
-        train_ids, query_ids, [keep0, got0], ((0, [(0, 1, 0, 0)]), (1, [(0, 1, 64, 0)]))
+        train_ids,
+        query_ids,
+        [keep0, got0, keep1, got1],
+        ((0, [(0, 1, 0, 0)]), (1, [(2, 3, 0, 0)]), (2, [(2, 3, 64, 0)])),
     )
     return call_final(
         train_ids,
         query_ids,
-        [keep1, got1, keep2, got2],
-        ((2, [(0, 1, 0, 0), (2, 3, 0, n // 2)]), (3, [(0, 1, 64, 0), (2, 3, 64, n // 2)])),
+        [keep2, got2, keep3, got3],
+        ((3, [(0, 1, 0, 0), (2, 3, 0, n // 2)]),),
         most,
     )
 

time: 50 us -> 50.9 us (1.018)
  starting transfers between devices: 17 us -> 21.9 us
  waiting for transfers between devices: 11.9 us -> 8.73 us
  Pallas kernels: 20 us -> 19.1 us
    ppermute x19 -> x21, starting transfers between devices: 17 us -> 21.9 us  [permute(): return lax.ppermute(value, AXES, pairs)]
    ppermute x19 -> x21, waiting for transfers between devices: 11.9 us -> 8.73 us  [permute(): return lax.ppermute(value, AXES, pairs)]
    pallas_call x6 -> x7, Pallas kernels: 18.1 us -> 17.2 us  [kernel_call(): pl.pallas_call(kernel, out_shape=outs, in_specs=specs or [VMEM] * len(inp...]
  transfers between devices with their start and end apart: 19 -> 21, of which waited for: 8 -> 8; matrix products, arithmetic and copies ran while one was open for 0% -> 0% of each run, Pallas kernels for 33% -> 30%
where the time goes in v8:
time: 50.9 us; the launch traced here: 50.7 us
  starting transfers between devices  21.9 us (43%)
  Pallas kernels  19.1 us (38%)
  waiting for transfers between devices  8.73 us (17%)
  between operations  0.82 us (2%)
    ppermute x21, starting transfers between devices, permute(): return lax.ppermute(value, AXES, pairs)  21.9 us
    pallas_call x7, Pallas kernels, kernel_call(): pl.pallas_call(kernel, out_shape=outs, in_specs=specs or [VMEM] * len(inp...  17.2 us
    ppermute x21, waiting for transfers between devices, permute(): return lax.ppermute(value, AXES, pairs)  8.73 us
    pallas_call x2, Pallas kernels, call_final(): pl.pallas_call(functools.partial(final_kernel, groups=groups, n_given=len...  1.85 us
  transfers between devices with their start and end apart: 21, of which 8 were waited for; matrix products, arithmetic and copies ran while one was open for 0% of the time, Pallas kernels for 30%

profile of v8, /device:TPU:0, one launch (start us, length us, event | category | flops | bytes accessed | tf_op | source)
XLA Modules:
  0.0 50.7 jit_solution(3107688877228285294)
XLA Ops:
  0.0 2.8 %shard_map.82 = (bf16[32,4096]{1,0:T(8,128)(2,1)S(1)}, bf16[2,256,256]{2,1,0:T(8,128)(2,1)S(1)}, bf16[2,256,512]{2,1,0:T(8,128)(2,1)S(1)}) custom-call(bf16[64,4096]{1,0:T(8,128)(2,1)} %bitcast.9, f32[64,64]{1,0:T(8,128)} %bitcast.11, f32[64,64]{1,0:T(8,128)} %bitcast.12), custom_call_target="tpu_custom_call" | custom-call | tf_op jit(solution)/shard_map/pallas_call | solution.py:222
  2.8 3.1 %collective-permute-start.1 = (bf16[32,4096]{1,0:T(8,128)(2,1)S(1)}, bf16[32,4096]{1,0:T(8,128)(2,1)S(1)}, u32[]{:S(2)}, u32[]{:S(2)}) collective-permute-start(bf16[32,4096]{1,0:T(8,128)(2,1)S(1)} %get-tuple-element.36.refs_0_), channel_id=1, source_target_pairs={{0,4},{1,5},{2,6},{3,7},{4,0},{5,1},{6,2},{7,3},{8,12},{9,13},{10,... | collective-permute-start | bytes 786440 | tf_op jit(solution)/shard_map/near/ppermute | solution.py:64
  6.6 3.3 %shard_map.83 = (bf16[32,4096]{1,0:T(8,128)(2,1)S(1)}, f32[8,256]{1,0:T(8,128)S(1)}) custom-call(f32[2]{0:T(128)} %weight_ref.1, s32[1]{0:T(128)S(6)} %copy.13.layer_ref, bf16[64,4096]{1,0:T(8,128)(2,1)} %bitcast.10, bf16[2,256,256]{2,1,0:T(8,128)(2,1)S(1)} %get-tuple-element.31.lefts_ref, bf16[2,256,512]{2,1,0:T(8,128)(2,1)S(1)} %get-tuple-element.32.rights_ref), custom_call_target="tpu_custom_call" | custom-call | tf_op jit(solution)/shard_map/pallas_call | solution.py:222
  9.9 2.5 %collective-permute-start = (bf16[32,4096]{1,0:T(8,128)(2,1)S(1)}, bf16[32,4096]{1,0:T(8,128)(2,1)S(1)}, u32[]{:S(2)}, u32[]{:S(2)}) collective-permute-start(bf16[32,4096]{1,0:T(8,128)(2,1)S(1)} %get-tuple-element.36.refs_0_), channel_id=1, source_target_pairs={{0,12},{1,13},{2,14},{3,15},{4,8},{5,9},{6,10},{7,11},{8,4},{9,5},... | collective-permute-start | bytes 786440 | tf_op jit(solution)/shard_map/far/ppermute | solution.py:64
  12.9 3.5 %shard_map.84.train_ref = bf16[1024,4096]{1,0:T(8,128)(2,1)S(1)} custom-call(bf16[1024,4096]{1,0:T(8,128)(2,1)} %bitcast.8, f32[8,256]{1,0:T(8,128)S(1)} %get-tuple-element.33._.weight_ref), custom_call_target="tpu_custom_call" | custom-call | tf_op jit(solution)/shard_map/pallas_call | solution.py:222
  16.4 1.6 %collective-permute-start.5 = (bf16[32,4096]{1,0:T(8,128)(2,1)S(1)}, bf16[32,4096]{1,0:T(8,128)(2,1)S(1)}, u32[]{:S(2)}, u32[]{:S(2)}) collective-permute-start(bf16[32,4096]{1,0:T(8,128)(2,1)S(1)} %collective-permute-done.1.refs_0_), channel_id=1, source_target_pairs={{0,16},{1,17},{2,18},{3,19},{4,20},{5,21},{6,22},{7,23},{8,24},{9,... | collective-permute-start | bytes 786440 | tf_op jit(solution)/shard_map/near_p/ppermute | solution.py:64
  18.0 2.1 %collective-permute-done.refs_4_ = bf16[32,4096]{1,0:T(8,128)(2,1)S(1)} collective-permute-done((bf16[32,4096]{1,0:T(8,128)(2,1)S(1)}, bf16[32,4096]{1,0:T(8,128)(2,1)S(1)}, u32[]{:S(2)}, u32[]{:S(2)}) %collective-permute-start) | collective-permute-done | bytes 262176 | tf_op jit(solution)/shard_map/far/ppermute | solution.py:64
  20.1 1.5 %collective-permute-start.11 = (bf16[32,4096]{1,0:T(8,128)(2,1)S(1)}, bf16[32,4096]{1,0:T(8,128)(2,1)S(1)}, u32[]{:S(2)}, u32[]{:S(2)}) collective-permute-start(bf16[32,4096]{1,0:T(8,128)(2,1)S(1)} %collective-permute-done.refs_4_), channel_id=1, source_target_pairs={{0,16},{1,17},{2,18},{3,19},{4,20},{5,21},{6,22},{7,23},{8,24},{9,... | collective-permute-start | bytes 786440 | tf_op jit(solution)/shard_map/far_p/ppermute | solution.py:64
  21.6 4.6 %collective-permute-start.2 = (bf16[32,4096]{1,0:T(8,128)(2,1)S(1)}, bf16[32,4096]{1,0:T(8,128)(2,1)S(1)}, u32[]{:S(2)}, u32[]{:S(2)}) collective-permute-start(bf16[32,4096]{1,0:T(8,128)(2,1)S(1)} %collective-permute-done.refs_4_), channel_id=1, source_target_pairs={{0,4},{1,5},{2,6},{3,7},{4,0},{5,1},{6,2},{7,3},{8,12},{9,13},{10,... | collective-permute-start | bytes 786440 | tf_op jit(solution)/shard_map/cross/ppermute | solution.py:64
  26.9 0.7 %collective-permute-done.7.refs_6_ = bf16[16,4096]{1,0:T(8,128)(2,1)S(1)} collective-permute-done((bf16[16,4096]{1,0:T(8,128)(2,1)S(1)}, bf16[16,4096]{1,0:T(8,128)(2,1)S(1)}, u32[]{:S(2)}, u32[]{:S(2)}) %collective-permute-start.7) | collective-permute-done | bytes 131104 | tf_op jit(solution)/shard_map/far_xb/ppermute | solution.py:64
  27.9 2.5 %shard_map.85 = (f32[128,1024]{1,0:T(8,128)S(1)}, bf16[64,1024]{1,0:T(8,128)(2,1)S(1)}, f32[64,1024]{1,0:T(8,128)S(1)}) custom-call(f32[8,256]{1,0:T(8,128)S(1)} %get-tuple-element.33._.weight_ref, bf16[1024,4096]{1,0:T(8,128)(2,1)S(1)} %shard_map.84.train_ref, bf16[32,4096]{1,0:T(8,128)(2,1)S(1)} %get-tuple-element.36.refs_0_, ...), custom_call_target="tpu_custom_call" | custom-call | tf_op jit(solution)/shard_map/pallas_call | solution.py:222
  31.4 1.6 %collective-permute-start.14 = (bf16[64,1024]{1,0:T(8,128)(2,1)S(1)}, bf16[64,1024]{1,0:T(8,128)(2,1)S(1)}, u32[]{:S(2)}, u32[]{:S(2)}) collective-permute-start(bf16[64,1024]{1,0:T(8,128)(2,1)S(1)} %get-tuple-element.41), channel_id=1, source_target_pairs={{0,1},{1,0},{2,3},{3,2},{4,5},{5,4},{6,7},{7,6},{8,9},{9,8},{10,11... | collective-permute-start | bytes 393224 | tf_op jit(solution)/shard_map/got0/ppermute | solution.py:64
  33.0 1.8 %collective-permute-start.15 = (bf16[16,4096]{1,0:T(8,128)(2,1)S(1)}, bf16[16,4096]{1,0:T(8,128)(2,1)S(1)}, u32[]{:S(2)}, u32[]{:S(2)}) collective-permute-start(bf16[16,4096]{1,0:T(8,128)(2,1)S(1)} %slice.15), channel_id=1, source_target_pairs={{0,4},{1,5},{2,6},{3,7},{4,0},{5,1},{6,2},{7,3},{8,12},{9,13},{10,... | collective-permute-start | bytes 393224 | tf_op jit(solution)/shard_map/cross_pb/ppermute | solution.py:64
  34.8 0.9 %collective-permute-start.8 = (bf16[16,4096]{1,0:T(8,128)(2,1)S(1)}, bf16[16,4096]{1,0:T(8,128)(2,1)S(1)}, u32[]{:S(2)}, u32[]{:S(2)}) collective-permute-start(bf16[16,4096]{1,0:T(8,128)(2,1)S(1)} %slice.14), channel_id=1, source_target_pairs={{0,16},{1,17},{2,18},{3,19},{4,20},{5,21},{6,22},{7,23},{8,24},{9,... | collective-permute-start | bytes 393224 | tf_op jit(solution)/shard_map/cross_pa/ppermute | solution.py:64
  35.7 2.5 %shard_map.86 = (f32[128,1024]{1,0:T(8,128)S(1)}, bf16[128,1024]{1,0:T(8,128)(2,1)S(1)}, f32[128,1024]{1,0:T(8,128)S(1)}) custom-call(f32[8,256]{1,0:T(8,128)S(1)} %get-tuple-element.33._.weight_ref, bf16[1024,4096]{1,0:T(8,128)(2,1)S(1)} %shard_map.84.train_ref, bf16[32,4096]{1,0:T(8,128)(2,1)S(1)} %collective-permute-done.1.refs_0_, ...), custom_call_target="tpu_custom_call" | custom-call | tf_op jit(solution)/shard_map/pallas_call | solution.py:222
  38.8 1.5 %collective-permute-done.8.refs_0_ = bf16[16,4096]{1,0:T(8,128)(2,1)S(1)} collective-permute-done((bf16[16,4096]{1,0:T(8,128)(2,1)S(1)}, bf16[16,4096]{1,0:T(8,128)(2,1)S(1)}, u32[]{:S(2)}, u32[]{:S(2)}) %collective-permute-start.8) | collective-permute-done | bytes 131104 | tf_op jit(solution)/shard_map/cross_pa/ppermute | solution.py:64
  40.3 1.3 %collective-permute-done.16.refs_2_ = bf16[16,4096]{1,0:T(8,128)(2,1)S(1)} collective-permute-done((bf16[16,4096]{1,0:T(8,128)(2,1)S(1)}, bf16[16,4096]{1,0:T(8,128)(2,1)S(1)}, u32[]{:S(2)}, u32[]{:S(2)}) %collective-permute-start.16) | collective-permute-done | bytes 131104 | tf_op jit(solution)/shard_map/cross_pxa/ppermute | solution.py:64
  41.6 1.3 %shard_map.87 = (bf16[64,512]{1,0:T(8,128)(2,1)S(1)}, f32[64,512]{1,0:T(8,128)S(1)}) custom-call(f32[8,256]{1,0:T(8,128)S(1)} %get-tuple-element.33._.weight_ref, bf16[1024,4096]{1,0:T(8,128)(2,1)S(1)} %shard_map.84.train_ref, bf16[16,4096]{1,0:T(8,128)(2,1)S(1)} %collective-permute-done.8.refs_0_, bf16[16,4096]{1,0:T(8,128)(2,1)S(1)} %collective-permute-done.15.refs_1_, ...), custom_call_target="tpu_custom_call" | custom-call | tf_op jit(solution)/shard_map/pallas_call | solution.py:222
  42.9 1.3 %shard_map.88 = (bf16[64,512]{1,0:T(8,128)(2,1)S(1)}, f32[64,512]{1,0:T(8,128)S(1)}) custom-call(f32[8,256]{1,0:T(8,128)S(1)} %get-tuple-element.33._.weight_ref, bf16[1024,4096]{1,0:T(8,128)(2,1)S(1)} %shard_map.84.train_ref, bf16[16,4096]{1,0:T(8,128)(2,1)S(1)} %collective-permute-done.8.refs_0_, bf16[16,4096]{1,0:T(8,128)(2,1)S(1)} %collective-permute-done.15.refs_1_, ...), custom_call_target="tpu_custom_call" | custom-call | tf_op jit(solution)/shard_map/pallas_call | solution.py:222
  44.8 1.6 %collective-permute-start.18 = (bf16[64,512]{1,0:T(8,128)(2,1)S(1)}, bf16[64,512]{1,0:T(8,128)(2,1)S(1)}, u32[]{:S(2)}, u32[]{:S(2)}) collective-permute-start(bf16[64,512]{1,0:T(8,128)(2,1)S(1)} %get-tuple-element.51), channel_id=1, source_target_pairs={{0,1},{1,0},{2,3},{3,2},{4,5},{5,4},{6,7},{7,6},{8,9},{9,8},{10,11... | collective-permute-start | bytes 196616 | tf_op jit(solution)/shard_map/got2/ppermute | solution.py:64
  46.5 1.0 %shard_map.89.refs_4_ = f32[256,1024]{1,0:T(8,128)} custom-call(s32[1,1024]{1,0:T(1,128)S(1)} %bitcast.6, s32[256,1]{1,0:T(8,128)S(1)} %copy.11.query_ids, f32[64,1024]{1,0:T(8,128)S(1)} %get-tuple-element.55.refs_0_, bf16[64,1024]{1,0:T(8,128)(2,1)S(1)} %collective-permute-done.14.refs_1_, f32[128,1024]{1,0:T(8,128)S(1)} %get-tuple-element.56.refs_2_, ...), custom_call_target="tpu_custom_call" | custom-call | tf_op jit(solution)/shard_map/pallas_call | solution.py:285
  47.5 1.6 %collective-permute-done.19.refs_3_ = bf16[64,512]{1,0:T(8,128)(2,1)S(1)} collective-permute-done((bf16[64,512]{1,0:T(8,128)(2,1)S(1)}, bf16[64,512]{1,0:T(8,128)(2,1)S(1)}, u32[]{:S(2)}, u32[]{:S(2)}) %collective-permute-start.19) | collective-permute-done | bytes 65568 | tf_op jit(solution)/shard_map/got3/ppermute | solution.py:64
  49.2 0.7 %collective-permute-done.18.refs_1_ = bf16[64,512]{1,0:T(8,128)(2,1)S(1)} collective-permute-done((bf16[64,512]{1,0:T(8,128)(2,1)S(1)}, bf16[64,512]{1,0:T(8,128)(2,1)S(1)}, u32[]{:S(2)}, u32[]{:S(2)}) %collective-permute-start.18) | collective-permute-done | bytes 65568 | tf_op jit(solution)/shard_map/got2/ppermute | solution.py:64
  49.9 0.8 %shard_map.90 = f32[256,1024]{1,0:T(8,128)} custom-call(s32[1,1024]{1,0:T(1,128)S(1)} %bitcast.7, s32[256,1]{1,0:T(8,128)S(1)} %copy.11.query_ids, f32[64,512]{1,0:T(8,128)S(1)} %get-tuple-element.50.refs_0_, bf16[64,512]{1,0:T(8,128)(2,1)S(1)} %collective-permute-done.18.refs_1_, ...), custom_call_target="tpu_custom_call", output_to_operand_aliasing={{}: (6, {})} | custom-call | tf_op jit(solution)/shard_map/pallas_call | solution.py:285
  (35 shorter events, 3.7 us)
Async XLA Ops:
  2.8 13.6 %collective-permute-start.1 = (bf16[32,4096]{1,0:T(8,128)(2,1)S(1)}, bf16[32,4096]{1,0:T(8,128)(2,1)S(1)}, u32[]{:S(2)}, u32[]{:S(2)}) collective-permute-start(bf16[32,4096]{1,0:T(8,128)(2,1)S(1)} %get-tuple-element.36.refs_0_), channel_id=1, source_target_pairs={{0,4},{1,5},{2,6},{3,7},{4,0},{5,1},{6,2},{7,3},{8,12},{9,13},{10,... | collective-permute-start | bytes 786440 | tf_op jit(solution)/shard_map/near/ppermute | solution.py:64
  9.9 10.2 %collective-permute-start = (bf16[32,4096]{1,0:T(8,128)(2,1)S(1)}, bf16[32,4096]{1,0:T(8,128)(2,1)S(1)}, u32[]{:S(2)}, u32[]{:S(2)}) collective-permute-start(bf16[32,4096]{1,0:T(8,128)(2,1)S(1)} %get-tuple-element.36.refs_0_), channel_id=1, source_target_pairs={{0,12},{1,13},{2,14},{3,15},{4,8},{5,9},{6,10},{7,11},{8,4},{9,5},... | collective-permute-start | bytes 786440 | tf_op jit(solution)/shard_map/far/ppermute | solution.py:64
  12.4 13.9 %collective-permute-start.4 = (bf16[32,4096]{1,0:T(8,128)(2,1)S(1)}, bf16[32,4096]{1,0:T(8,128)(2,1)S(1)}, u32[]{:S(2)}, u32[]{:S(2)}) collective-permute-start(bf16[32,4096]{1,0:T(8,128)(2,1)S(1)} %get-tuple-element.35.refs_2_), channel_id=1, source_target_pairs={{0,2},{1,3},{2,0},{3,1},{4,6},{5,7},{6,4},{7,5},{8,10},{9,11},{10,... | collective-permute-start | bytes 786440 | tf_op jit(solution)/shard_map/rest_x/ppermute | solution.py:64
  12.4 14.4 %collective-permute-start.3 = (bf16[32,4096]{1,0:T(8,128)(2,1)S(1)}, bf16[32,4096]{1,0:T(8,128)(2,1)S(1)}, u32[]{:S(2)}, u32[]{:S(2)}) collective-permute-start(bf16[32,4096]{1,0:T(8,128)(2,1)S(1)} %get-tuple-element.36.refs_0_), channel_id=1, source_target_pairs={{0,2},{1,3},{2,0},{3,1},{4,6},{5,7},{6,4},{7,5},{8,10},{9,11},{10,... | collective-permute-start | bytes 786440 | tf_op jit(solution)/shard_map/mine_x/ppermute | solution.py:64
  16.4 9.8 %collective-permute-start.5 = (bf16[32,4096]{1,0:T(8,128)(2,1)S(1)}, bf16[32,4096]{1,0:T(8,128)(2,1)S(1)}, u32[]{:S(2)}, u32[]{:S(2)}) collective-permute-start(bf16[32,4096]{1,0:T(8,128)(2,1)S(1)} %collective-permute-done.1.refs_0_), channel_id=1, source_target_pairs={{0,16},{1,17},{2,18},{3,19},{4,20},{5,21},{6,22},{7,23},{8,24},{9,... | collective-permute-start | bytes 786440 | tf_op jit(solution)/shard_map/near_p/ppermute | solution.py:64
  20.1 10.2 %collective-permute-start.11 = (bf16[32,4096]{1,0:T(8,128)(2,1)S(1)}, bf16[32,4096]{1,0:T(8,128)(2,1)S(1)}, u32[]{:S(2)}, u32[]{:S(2)}) collective-permute-start(bf16[32,4096]{1,0:T(8,128)(2,1)S(1)} %collective-permute-done.refs_4_), channel_id=1, source_target_pairs={{0,16},{1,17},{2,18},{3,19},{4,20},{5,21},{6,22},{7,23},{8,24},{9,... | collective-permute-start | bytes 786440 | tf_op jit(solution)/shard_map/far_p/ppermute | solution.py:64
  21.6 9.8 %collective-permute-start.2 = (bf16[32,4096]{1,0:T(8,128)(2,1)S(1)}, bf16[32,4096]{1,0:T(8,128)(2,1)S(1)}, u32[]{:S(2)}, u32[]{:S(2)}) collective-permute-start(bf16[32,4096]{1,0:T(8,128)(2,1)S(1)} %collective-permute-done.refs_4_), channel_id=1, source_target_pairs={{0,4},{1,5},{2,6},{3,7},{4,0},{5,1},{6,2},{7,3},{8,12},{9,13},{10,... | collective-permute-start | bytes 786440 | tf_op jit(solution)/shard_map/cross/ppermute | solution.py:64
  26.3 1.4 %collective-permute-start.7 = (bf16[16,4096]{1,0:T(8,128)(2,1)S(1)}, bf16[16,4096]{1,0:T(8,128)(2,1)S(1)}, u32[]{:S(2)}, u32[]{:S(2)}) collective-permute-start(bf16[16,4096]{1,0:T(8,128)(2,1)S(1)} %get-tuple-element.40), channel_id=1, source_target_pairs={{0,2},{1,3},{2,0},{3,1},{4,6},{5,7},{6,4},{7,5},{8,10},{9,11},{10,... | collective-permute-start | bytes 393224 | tf_op jit(solution)/shard_map/far_xb/ppermute | solution.py:64
  26.3 1.5 %collective-permute-start.6 = (bf16[16,4096]{1,0:T(8,128)(2,1)S(1)}, bf16[16,4096]{1,0:T(8,128)(2,1)S(1)}, u32[]{:S(2)}, u32[]{:S(2)}) collective-permute-start(bf16[16,4096]{1,0:T(8,128)(2,1)S(1)} %get-tuple-element.39), channel_id=1, source_target_pairs={{0,2},{1,3},{2,0},{3,1},{4,6},{5,7},{6,4},{7,5},{8,10},{9,11},{10,... | collective-permute-start | bytes 393224 | tf_op jit(solution)/shard_map/far_xa/ppermute | solution.py:64
  26.8 6.2 %collective-permute-start.9 = (bf16[32,4096]{1,0:T(8,128)(2,1)S(1)}, bf16[32,4096]{1,0:T(8,128)(2,1)S(1)}, u32[]{:S(2)}, u32[]{:S(2)}) collective-permute-start(bf16[32,4096]{1,0:T(8,128)(2,1)S(1)} %collective-permute-done.1.refs_0_), channel_id=1, source_target_pairs={{0,2},{1,3},{2,0},{3,1},{4,6},{5,7},{6,4},{7,5},{8,10},{9,11},{10,... | collective-permute-start | bytes 786440 | tf_op jit(solution)/shard_map/near_x/ppermute | solution.py:64
  30.3 4.5 %collective-permute-start.12 = (bf16[32,4096]{1,0:T(8,128)(2,1)S(1)}, bf16[32,4096]{1,0:T(8,128)(2,1)S(1)}, u32[]{:S(2)}, u32[]{:S(2)}) collective-permute-start(bf16[32,4096]{1,0:T(8,128)(2,1)S(1)} %collective-permute-done.11.refs_4_), channel_id=1, source_target_pairs={{0,2},{1,3},{2,0},{3,1},{4,6},{5,7},{6,4},{7,5},{8,10},{9,11},{10,... | collective-permute-start | bytes 786440 | tf_op jit(solution)/shard_map/far_px/ppermute | solution.py:64
  30.7 5.0 %collective-permute-start.10 = (bf16[32,4096]{1,0:T(8,128)(2,1)S(1)}, bf16[32,4096]{1,0:T(8,128)(2,1)S(1)}, u32[]{:S(2)}, u32[]{:S(2)}) collective-permute-start(bf16[32,4096]{1,0:T(8,128)(2,1)S(1)} %collective-permute-done.5.refs_2_), channel_id=1, source_target_pairs={{0,2},{1,3},{2,0},{3,1},{4,6},{5,7},{6,4},{7,5},{8,10},{9,11},{10,... | collective-permute-start | bytes 786440 | tf_op jit(solution)/shard_map/near_px/ppermute | solution.py:64
  31.4 4.3 %collective-permute-start.13 = (bf16[32,4096]{1,0:T(8,128)(2,1)S(1)}, bf16[32,4096]{1,0:T(8,128)(2,1)S(1)}, u32[]{:S(2)}, u32[]{:S(2)}) collective-permute-start(bf16[32,4096]{1,0:T(8,128)(2,1)S(1)} %collective-permute-done.2.refs_6_), channel_id=1, source_target_pairs={{0,2},{1,3},{2,0},{3,1},{4,6},{5,7},{6,4},{7,5},{8,10},{9,11},{10,... | collective-permute-start | bytes 786440 | tf_op jit(solution)/shard_map/cross_x/ppermute | solution.py:64
  31.4 7.3 %collective-permute-start.14 = (bf16[64,1024]{1,0:T(8,128)(2,1)S(1)}, bf16[64,1024]{1,0:T(8,128)(2,1)S(1)}, u32[]{:S(2)}, u32[]{:S(2)}) collective-permute-start(bf16[64,1024]{1,0:T(8,128)(2,1)S(1)} %get-tuple-element.41), channel_id=1, source_target_pairs={{0,1},{1,0},{2,3},{3,2},{4,5},{5,4},{6,7},{7,6},{8,9},{9,8},{10,11... | collective-permute-start | bytes 393224 | tf_op jit(solution)/shard_map/got0/ppermute | solution.py:64
  33.0 5.7 %collective-permute-start.15 = (bf16[16,4096]{1,0:T(8,128)(2,1)S(1)}, bf16[16,4096]{1,0:T(8,128)(2,1)S(1)}, u32[]{:S(2)}, u32[]{:S(2)}) collective-permute-start(bf16[16,4096]{1,0:T(8,128)(2,1)S(1)} %slice.15), channel_id=1, source_target_pairs={{0,4},{1,5},{2,6},{3,7},{4,0},{5,1},{6,2},{7,3},{8,12},{9,13},{10,... | collective-permute-start | bytes 393224 | tf_op jit(solution)/shard_map/cross_pb/ppermute | solution.py:64
  34.8 5.4 %collective-permute-start.8 = (bf16[16,4096]{1,0:T(8,128)(2,1)S(1)}, bf16[16,4096]{1,0:T(8,128)(2,1)S(1)}, u32[]{:S(2)}, u32[]{:S(2)}) collective-permute-start(bf16[16,4096]{1,0:T(8,128)(2,1)S(1)} %slice.14), channel_id=1, source_target_pairs={{0,16},{1,17},{2,18},{3,19},{4,20},{5,21},{6,22},{7,23},{8,24},{9,... | collective-permute-start | bytes 393224 | tf_op jit(solution)/shard_map/cross_pa/ppermute | solution.py:64
  38.2 8.3 %collective-permute-start.20 = (bf16[128,1024]{1,0:T(8,128)(2,1)S(1)}, bf16[128,1024]{1,0:T(8,128)(2,1)S(1)}, u32[]{:S(2)}, u32[]{:S(2)}) collective-permute-start(bf16[128,1024]{1,0:T(8,128)(2,1)S(1)} %get-tuple-element.46), channel_id=1, source_target_pairs={{0,1},{1,0},{2,3},{3,2},{4,5},{5,4},{6,7},{7,6},{8,9},{9,8},{10,11... | collective-permute-start | bytes 786440 | tf_op jit(solution)/shard_map/got1/ppermute | solution.py:64
  38.7 1.5 %collective-permute-start.17 = (bf16[16,4096]{1,0:T(8,128)(2,1)S(1)}, bf16[16,4096]{1,0:T(8,128)(2,1)S(1)}, u32[]{:S(2)}, u32[]{:S(2)}) collective-permute-start(bf16[16,4096]{1,0:T(8,128)(2,1)S(1)} %collective-permute-done.15.refs_1_), channel_id=1, source_target_pairs={{0,2},{1,3},{2,0},{3,1},{4,6},{5,7},{6,4},{7,5},{8,10},{9,11},{10,... | collective-permute-start | bytes 393224 | tf_op jit(solution)/shard_map/cross_pxb/ppermute | solution.py:64
  40.3 1.3 %collective-permute-start.16 = (bf16[16,4096]{1,0:T(8,128)(2,1)S(1)}, bf16[16,4096]{1,0:T(8,128)(2,1)S(1)}, u32[]{:S(2)}, u32[]{:S(2)}) collective-permute-start(bf16[16,4096]{1,0:T(8,128)(2,1)S(1)} %collective-permute-done.8.refs_0_), channel_id=1, source_target_pairs={{0,2},{1,3},{2,0},{3,1},{4,6},{5,7},{6,4},{7,5},{8,10},{9,11},{10,... | collective-permute-start | bytes 393224 | tf_op jit(solution)/shard_map/cross_pxa/ppermute | solution.py:64
  41.6 4.7 %copy-start.1 = (s32[256]{0:T(256)S(1)}, s32[256]{0:T(256)}, u32[]{:S(2)}) copy-start(s32[256]{0:T(256)} %param.15) | copy-start | bytes 3076
  41.6 4.9 %copy-start = (s32[1024]{0:T(1024)S(1)}, s32[1024]{0:T(1024)}, u32[]{:S(2)}) copy-start(s32[1024]{0:T(1024)} %param.14) | copy-start | bytes 12292
  44.2 4.9 %collective-permute-start.19 = (bf16[64,512]{1,0:T(8,128)(2,1)S(1)}, bf16[64,512]{1,0:T(8,128)(2,1)S(1)}, u32[]{:S(2)}, u32[]{:S(2)}) collective-permute-start(bf16[64,512]{1,0:T(8,128)(2,1)S(1)} %get-tuple-element.54), channel_id=1, source_target_pairs={{0,1},{1,0},{2,3},{3,2},{4,5},{5,4},{6,7},{7,6},{8,9},{9,8},{10,11... | collective-permute-start | bytes 196616 | tf_op jit(solution)/shard_map/got3/ppermute | solution.py:64
  44.8 5.1 %collective-permute-start.18 = (bf16[64,512]{1,0:T(8,128)(2,1)S(1)}, bf16[64,512]{1,0:T(8,128)(2,1)S(1)}, u32[]{:S(2)}, u32[]{:S(2)}) collective-permute-start(bf16[64,512]{1,0:T(8,128)(2,1)S(1)} %get-tuple-element.51), channel_id=1, source_target_pairs={{0,1},{1,0},{2,3},{3,2},{4,5},{5,4},{6,7},{7,6},{8,9},{9,8},{10,11... | collective-permute-start | bytes 196616 | tf_op jit(solution)/shard_map/got2/ppermute | solution.py:64

commit v9 on v8

--- a/solution.py
+++ b/solution.py
@@ -67,8 +67,8 @@
 to_part = functools.partial(permute, target=lambda p, z, c, l: (1 - p, z, c, l))
 to_core = functools.partial(permute, target=lambda p, z, c, l: (p, z, 1 - c, l))
 to_layer = functools.partial(permute, target=lambda p, z, c, l: (p, z, c, 1 - l))
-to_near = functools.partial(permute, target=lambda p, z, c, l: (p, z ^ 1, c, l))
-to_far = functools.partial(permute, target=lambda p, z, c, l: (p, z ^ 3, c, l))
+to_previous = functools.partial(permute, target=lambda p, z, c, l: (p, (z - 1) % CHIPS, c, l))
+to_next = functools.partial(permute, target=lambda p, z, c, l: (p, (z + 1) % CHIPS, c, l))
 
 
 def after(value, *others):
@@ -188,34 +188,70 @@
         copy.wait()
 
 
-def score_kernel(weight_ref, train_ref, *refs, picks, stored, early, columns):
-    inputs, refs = refs[: len(picks)], refs[len(picks) :]
-    n_before = sum(taken for _, _, taken in early)
-    before, outs = refs[:n_before], refs[n_before:]
+def scored(weight_ref, train_ref, pieces, columns, write):
     weight = weight_ref[0:1, :]
-    queries = jnp.concatenate(
-        [piece[at : at + n, :] for piece, rows in zip(inputs, picks) for at, n in rows], axis=0
-    )
+    queries = jnp.concatenate([piece[...] for piece in pieces], axis=0)
+    for at in range(*columns, STEP):
+        value = lax.dot_general(
+            train_ref[at : at + STEP, :],
+            queries,
+            (((1,), (1,)), ((), ())),
+            preferred_element_type=f32,
+        )
+        write(slice(at - columns[0], at - columns[0] + STEP), weight * value.T)
+
+
+def swap(theirs, ours, send, keep, here):
     _, z, _, layer = place()
-    near_is_mine = z // 2 == layer
-    for at in range(*columns, STEP):
-        there, here = slice(at, at + STEP), slice(at - columns[0], at - columns[0] + STEP)
-        value = lax.dot_general(
-            train_ref[there, :], queries, (((1,), (1,)), ((), ())), preferred_element_type=f32
-        )
-        value = weight * value.T
-        if stored:
-            outs[0][:, here] = value[:stored]
-        if early:
-            send, keep = outs[-2:]
-            old, given = [], list(before)
-            for first, rows, taken in early:
-                old.append(
-                    given.pop(0)[first : first + rows, there] if taken else value[first : first + rows]
-                )
-            old, new = jnp.concatenate(old, axis=0), value[stored:]
-            send[:, here] = jnp.where(near_is_mine, new, old).astype(send.dtype)
-            keep[:, here] = jnp.where(near_is_mine, old, new)
+    mine = z // 2 == layer
+    send[:, here] = jnp.where(mine, theirs, ours).astype(send.dtype)
+    keep[:, here] = jnp.where(mine, ours, theirs)
+
+
+def beside_across(a, b):
+    even = place()[1] % 2 == 0
+    return jnp.where(even, a, b), jnp.where(even, b, a)
+
+
+def first_kernel(weight_ref, train_ref, *refs, columns):
+    *pieces, own_p, beside, send, keep = refs
+
+    def write(here, value):
+        own_p[:, here] = value[64:128]
+        beside[:, here], across = beside_across(value[128:192], value[192:])
+        swap(across, value[:64], send, keep, here)
+
+    scored(weight_ref, train_ref, pieces, columns, write)
+
+
+def second_kernel(weight_ref, train_ref, own_p, *refs, columns):
+    *pieces, beside_p, send, keep = refs
+
+    def write(here, value):
+        beside_p[:, here], across = beside_across(value[:64], value[64:])
+        swap(across, own_p[:, here], send, keep, here)
+
+    scored(weight_ref, train_ref, pieces, columns, write)
+
+
+def third_kernel(weight_ref, train_ref, beside, beside_p, *refs, columns):
+    *pieces, send, keep = refs
+
+    def write(here, value):
+        there = slice(here.start + columns[0], here.stop + columns[0])
+        ours = jnp.concatenate([beside[:, there], beside_p[:, there]], axis=0)
+        swap(value, ours, send, keep, here)
+
+    scored(weight_ref, train_ref, pieces, columns, write)
+
+
+def call_scores(kernel, weight, train, inputs, outs, columns=None):
+    columns = columns or (0, train.shape[0])
+    return kernel_call(
+        functools.partial(kernel, columns=columns),
+        [jax.ShapeDtypeStruct((rows, columns[1] - columns[0]), t) for rows, t in outs],
+        [weight, train, *inputs],
+    )
 
 
 def kernel_call(kernel, outs, inputs, specs=None, scratch=()):
@@ -223,31 +259,10 @@
         kernel,
         out_shape=outs,
         in_specs=specs or [VMEM] * len(inputs),
-        out_specs=[VMEM] * len(outs) if isinstance(outs, list) else VMEM,
+        out_specs=[VMEM] * len(outs),
         scratch_shapes=scratch,
         compiler_params=pltpu.CompilerParams(vmem_limit_bytes=LIMIT),
     )(*inputs)
-
-
-def call_scores(weight, train, inputs, stored=0, early=(), columns=None):
-    columns = columns or (0, train.shape[0])
-    n = columns[1] - columns[0]
-    total = sum(count for _, rows in inputs for _, count in rows)
-    others = [a for a, _ in inputs] + [a for a, _, _ in early if a is not None]
-    outs = [jax.ShapeDtypeStruct((stored, n), f32)] if stored else []
-    if early:
-        outs += [jax.ShapeDtypeStruct((total - stored, n), t) for t in (bf16, f32)]
-    return kernel_call(
-        functools.partial(
-            score_kernel,
-            picks=[rows for _, rows in inputs],
-            stored=stored,
-            early=[(first, rows, a is not None) for a, first, rows in early],
-            columns=columns,
-        ),
-        outs,
-        [weight, train, *others],
-    )
 
 
 def final_kernel(train_ids, query_ids, *refs, groups, n_given):
@@ -322,7 +337,7 @@
             pltpu.SemaphoreType.DMA((3,)),
         ],
     )
-    near = to_near(mine, "near")
+    a = to_previous(mine, "a")
     rest, weight = kernel_call(
         rest_kernel,
         [shape((HALF, width), bf16), shape((8, STEP), f32)],
@@ -330,68 +345,62 @@
         [SMEM, SMEM, HBM, VMEM, VMEM],
         [pltpu.VMEM((HALF, width), bf16), pltpu.SemaphoreType.DMA],
     )
-    far = to_far(after(mine, rest), "far")
+    b = to_next(after(mine, rest), "b")
+    mine_x = to_core(mine, "mine_x")
+    rest_x = to_core(rest, "rest_x")
     (train,) = kernel_call(
         train_kernel,
         [shape(train.shape, bf16)],
-        [train, weight],
+        [train, after(weight, a, mine_x, rest_x)],
         [HBM, VMEM],
         [pltpu.SemaphoreType.DMA((train.shape[0] // STEP,))],
     )
-    score = functools.partial(call_scores, weight, train)
-
-    def rows_of(*pieces):
-        return [(piece, ((0, piece.shape[0]),)) for piece in pieces]
-
-    mine_x = to_core(mine, "mine_x")
-    rest_x = to_core(rest, "rest_x")
-    near = after(near, train)
-    near_x = to_core(near, "near_x")
-    near_p = to_part(near, "near_p")
-    far = after(far, near)
-    cross = to_near(far, "cross")
-    far_p = to_part(far, "far_p")
-    far_xa = to_core(after(far[:CHUNK], near_p), "far_xa")
-    far_xb = to_core(after(far[CHUNK:], near_p), "far_xb")
-    early0, send0, keep0 = score(
-        rows_of(mine, mine_x, rest, rest_x, far, far_xa, far_xb), stored=128, early=[(None, 0, 64)]
+    score = lambda kernel, *rest: call_scores(kernel, weight, train, *rest)
+
+    a_x = to_core(a, "a_x")
+    a_p = to_part(a, "a_p")
+    b = after(b, a, train, a_x)
+    b_p = to_part(b, "b_p")
+    c0 = to_next(b[:CHUNK], "c0")
+    c1 = to_previous(a[CHUNK:], "c1")
+    b_x = to_core(after(b, a_p), "b_x")
+    own_p, beside, send0, keep0 = score(
+        first_kernel,
+        [mine, mine_x, rest, rest_x, a, a_x, b, b_x],
+        [(64, f32), (64, f32), (64, bf16), (64, f32)],
     )
     got0 = to_layer(send0, "got0")
-    near_p, far_p, cross = after(near_p, send0), after(far_p, send0), after(cross, send0)
-    near_px = to_core(near_p, "near_px")
-    far_px = to_core(far_p, "far_px")
-    cross_pa = to_part(cross[:CHUNK], "cross_pa")
-    cross_pb = to_near(far_p[CHUNK:], "cross_pb")
-    cross_x = to_core(cross, "cross_x")
-    early1, send1, keep1 = score(
-        rows_of(near, near_x, near_p, near_px, far_p, far_px, cross, cross_x),
-        stored=128,
-        early=[(early0, 64, 64), (None, 0, 64)],
+
+    a_p, b_p, c0, c1 = [after(piece, send0) for piece in (a_p, b_p, c0, c1)]
+    c_p0 = to_part(c0, "c_p0")
+    c_p1 = to_previous(a_p[CHUNK:], "c_p1")
+    a_px0, a_px1 = to_core(a_p[:CHUNK], "a_px0"), to_core(a_p[CHUNK:], "a_px1")
+    b_px0, b_px1 = to_core(b_p[:CHUNK], "b_px0"), to_core(b_p[CHUNK:], "b_px1")
+    c_x0, c_x1 = to_core(c0, "c_x0"), to_core(c1, "c_x1")
+    beside_p, send1, keep1 = score(
+        second_kernel, [own_p, a_p, a_px0, a_px1, b_p, b_px0, b_px1], [(64, f32), (64, bf16), (64, f32)]
     )
     got1 = to_layer(send1, "got1")
-    cross_pa, cross_pb = after(cross_pa, send1, got0), after(cross_pb, send1, got0)
-    cross_pxa = to_core(cross_pa, "cross_pxa")
-    cross_pxb = to_core(cross_pb, "cross_pxb")
-    last = rows_of(cross_pa, cross_pb, cross_pxa, cross_pxb)
-    n = train.shape[0]
-    send2, keep2 = score(last, early=[(early1, 64, 64)], columns=(0, n // 2))
+
+    c_p0, c_p1 = after(c_p0, send1, got0), after(c_p1, send1, got0)
+    c_px0, c_px1 = to_core(c_p0, "c_px0"), to_core(c_p1, "c_px1")
+    last = [c0, c1, c_x0, c_x1, c_p0, c_p1, c_px0, c_px1]
+    n, outs = train.shape[0], [(128, bf16), (128, f32)]
+    send2, keep2 = score(third_kernel, [beside, beside_p, *last], outs, (0, n // 2))
     got2 = to_layer(send2, "got2")
-    early1 = after(early1, send2)
-    send3, keep3 = score(last, early=[(early1, 64, 64)], columns=(n // 2, n))
+    beside = after(beside, send2)
+    send3, keep3 = score(third_kernel, [beside, beside_p, *last], outs, (n // 2, n))
     got3 = to_layer(send3, "got3")
 
     train_ids, query_ids = train_ids[None, :], query_ids[:, None]
     most = call_final(
-        train_ids,
-        query_ids,
-        [keep0, got0, keep1, got1],
-        ((0, [(0, 1, 0, 0)]), (1, [(2, 3, 0, 0)]), (2, [(2, 3, 64, 0)])),
+        train_ids, query_ids, [keep0, got0, keep1, got1], ((0, [(0, 1, 0, 0)]), (1, [(2, 3, 0, 0)]))
     )
     return call_final(
         train_ids,
         query_ids,
         [keep2, got2, keep3, got3],
-        ((3, [(0, 1, 0, 0), (2, 3, 0, n // 2)]),),
+        ((2, [(0, 1, 0, 0), (2, 3, 0, n // 2)]), (3, [(0, 1, 64, 0), (2, 3, 64, n // 2)])),
         most,
     )
 

time: 50.9 us -> 56.8 us (1.12)
  waiting for transfers between devices: 8.73 us -> 15.4 us
  starting transfers between devices: 21.9 us -> 21.1 us
    ppermute x21 -> x24, waiting for transfers between devices: 8.73 us -> 15.4 us  [permute(): return lax.ppermute(value, AXES, pairs)]
    ppermute x21 -> x24, starting transfers between devices: 21.9 us -> 21.1 us  [permute(): return lax.ppermute(value, AXES, pairs)]
  transfers between devices with their start and end apart: 21 -> 24, of which waited for: 8 -> 11; matrix products, arithmetic and copies ran while one was open for 0% -> 0% of each run, Pallas kernels for 30% -> 27%
where the time goes in v9:
time: 56.8 us; the launch traced here: 56.6 us
  starting transfers between devices  21.1 us (37%)
  Pallas kernels  19.1 us (34%)
  waiting for transfers between devices  15.4 us (27%)
  between operations  0.82 us (1%)
    ppermute x24, starting transfers between devices, permute(): return lax.ppermute(value, AXES, pairs)  21.1 us
    pallas_call x7, Pallas kernels, kernel_call(): pl.pallas_call(kernel, out_shape=outs, in_specs=specs or [VMEM] * len(inp...  17.2 us
    ppermute x24, waiting for transfers between devices, permute(): return lax.ppermute(value, AXES, pairs)  15.4 us
    pallas_call x2, Pallas kernels, call_final(): pl.pallas_call(functools.partial(final_kernel, groups=groups, n_given=len...  1.83 us
  transfers between devices with their start and end apart: 24, of which 11 were waited for; matrix products, arithmetic and copies ran while one was open for 0% of the time, Pallas kernels for 27%

profile of v9, /device:TPU:0, one launch (start us, length us, event | category | flops | bytes accessed | tf_op | source)
XLA Modules:
  0.0 56.6 jit_solution(3904059115431581662)
XLA Ops:
  0.0 2.8 %shard_map.82 = (bf16[32,4096]{1,0:T(8,128)(2,1)S(1)}, bf16[2,256,256]{2,1,0:T(8,128)(2,1)S(1)}, bf16[2,256,512]{2,1,0:T(8,128)(2,1)S(1)}) custom-call(bf16[64,4096]{1,0:T(8,128)(2,1)} %bitcast.9, f32[64,64]{1,0:T(8,128)} %bitcast.11, f32[64,64]{1,0:T(8,128)} %bitcast.12), custom_call_target="tpu_custom_call" | custom-call | tf_op jit(solution)/shard_map/pallas_call | solution.py:258
  2.8 5.1 %collective-permute-start = (bf16[32,4096]{1,0:T(8,128)(2,1)S(1)}, bf16[32,4096]{1,0:T(8,128)(2,1)S(1)}, u32[]{:S(2)}, u32[]{:S(2)}) collective-permute-start(bf16[32,4096]{1,0:T(8,128)(2,1)S(1)} %get-tuple-element.38.refs_0_), channel_id=1, source_target_pairs={{0,12},{1,13},{2,14},{3,15},{4,0},{5,1},{6,2},{7,3},{8,4},{9,5},{1... | collective-permute-start | bytes 786440 | tf_op jit(solution)/shard_map/a/ppermute | solution.py:64
  8.6 3.3 %shard_map.83 = (bf16[32,4096]{1,0:T(8,128)(2,1)S(1)}, f32[8,256]{1,0:T(8,128)S(1)}) custom-call(f32[2]{0:T(128)} %weight_ref.1, s32[1]{0:T(128)S(6)} %copy.13.layer_ref, bf16[64,4096]{1,0:T(8,128)(2,1)} %bitcast.10, bf16[2,256,256]{2,1,0:T(8,128)(2,1)S(1)} %get-tuple-element.32.lefts_ref, bf16[2,256,512]{2,1,0:T(8,128)(2,1)S(1)} %get-tuple-element.33.rights_ref), custom_call_target="tpu_custom_call" | custom-call | tf_op jit(solution)/shard_map/pallas_call | solution.py:258
  11.9 0.6 %collective-permute-start.2 = (bf16[32,4096]{1,0:T(8,128)(2,1)S(1)}, bf16[32,4096]{1,0:T(8,128)(2,1)S(1)}, u32[]{:S(2)}, u32[]{:S(2)}) collective-permute-start(bf16[32,4096]{1,0:T(8,128)(2,1)S(1)} %get-tuple-element.36.refs_2_), channel_id=1, source_target_pairs={{0,2},{1,3},{2,0},{3,1},{4,6},{5,7},{6,4},{7,5},{8,10},{9,11},{10,... | collective-permute-start | bytes 786440 | tf_op jit(solution)/shard_map/rest_x/ppermute | solution.py:64
  12.5 1.6 %collective-permute-done.refs_4_ = bf16[32,4096]{1,0:T(8,128)(2,1)S(1)} collective-permute-done((bf16[32,4096]{1,0:T(8,128)(2,1)S(1)}, bf16[32,4096]{1,0:T(8,128)(2,1)S(1)}, u32[]{:S(2)}, u32[]{:S(2)}) %collective-permute-start) | collective-permute-done | bytes 262176 | tf_op jit(solution)/shard_map/a/ppermute | solution.py:64
  14.0 1.5 %collective-permute-start.5 = (bf16[32,4096]{1,0:T(8,128)(2,1)S(1)}, bf16[32,4096]{1,0:T(8,128)(2,1)S(1)}, u32[]{:S(2)}, u32[]{:S(2)}) collective-permute-start(bf16[32,4096]{1,0:T(8,128)(2,1)S(1)} %collective-permute-done.refs_4_), channel_id=1, source_target_pairs={{0,16},{1,17},{2,18},{3,19},{4,20},{5,21},{6,22},{7,23},{8,24},{9,... | collective-permute-start | bytes 786440 | tf_op jit(solution)/shard_map/a_p/ppermute | solution.py:64
  15.5 3.5 %shard_map.84.train_ref = bf16[1024,4096]{1,0:T(8,128)(2,1)S(1)} custom-call(bf16[1024,4096]{1,0:T(8,128)(2,1)} %bitcast.8, f32[8,256]{1,0:T(8,128)S(1)} %get-tuple-element.37._.weight_ref), custom_call_target="tpu_custom_call" | custom-call | tf_op jit(solution)/shard_map/pallas_call | solution.py:258
  19.0 3.5 %collective-permute-done.4.refs_6_ = bf16[32,4096]{1,0:T(8,128)(2,1)S(1)} collective-permute-done((bf16[32,4096]{1,0:T(8,128)(2,1)S(1)}, bf16[32,4096]{1,0:T(8,128)(2,1)S(1)}, u32[]{:S(2)}, u32[]{:S(2)}) %collective-permute-start.4) | collective-permute-done | bytes 262176 | tf_op jit(solution)/shard_map/b/ppermute | solution.py:64
  22.8 4.3 %collective-permute-start.13 = (bf16[16,4096]{1,0:T(8,128)(2,1)S(1)}, bf16[16,4096]{1,0:T(8,128)(2,1)S(1)}, u32[]{:S(2)}, u32[]{:S(2)}) collective-permute-start(bf16[16,4096]{1,0:T(8,128)(2,1)S(1)} %slice.25), channel_id=1, source_target_pairs={{0,12},{1,13},{2,14},{3,15},{4,0},{5,1},{6,2},{7,3},{8,4},{9,5},{1... | collective-permute-start | bytes 393224 | tf_op jit(solution)/shard_map/c1/ppermute | solution.py:64
  27.1 1.5 %collective-permute-start.9 = (bf16[32,4096]{1,0:T(8,128)(2,1)S(1)}, bf16[32,4096]{1,0:T(8,128)(2,1)S(1)}, u32[]{:S(2)}, u32[]{:S(2)}) collective-permute-start(bf16[32,4096]{1,0:T(8,128)(2,1)S(1)} %collective-permute-done.4.refs_6_), channel_id=1, source_target_pairs={{0,16},{1,17},{2,18},{3,19},{4,20},{5,21},{6,22},{7,23},{8,24},{9,... | collective-permute-start | bytes 786440 | tf_op jit(solution)/shard_map/b_p/ppermute | solution.py:64
  28.7 2.5 %shard_map.85 = (f32[64,1024]{1,0:T(8,128)S(1)}, f32[64,1024]{1,0:T(8,128)S(1)}, bf16[64,1024]{1,0:T(8,128)(2,1)S(1)}, f32[64,1024]{1,0:T(8,128)S(1)}) custom-call(f32[8,256]{1,0:T(8,128)S(1)} %get-tuple-element.37._.weight_ref, bf16[1024,4096]{1,0:T(8,128)(2,1)S(1)} %shard_map.84.train_ref, bf16[32,4096]{1,0:T(8,128)(2,1)S(1)} %get-tuple-element.38.refs_0_, ...), custom_call_target="tpu_custom_call" | custom-call | tf_op jit(solution)/shard_map/pallas_call | solution.py:258
  31.8 3.7 %collective-permute-done.9.refs_3_ = bf16[32,4096]{1,0:T(8,128)(2,1)S(1)} collective-permute-done((bf16[32,4096]{1,0:T(8,128)(2,1)S(1)}, bf16[32,4096]{1,0:T(8,128)(2,1)S(1)}, u32[]{:S(2)}, u32[]{:S(2)}) %collective-permute-start.9) | collective-permute-done | bytes 262176 | tf_op jit(solution)/shard_map/b_p/ppermute | solution.py:64
  36.1 1.5 %collective-permute-start.16 = (bf16[16,4096]{1,0:T(8,128)(2,1)S(1)}, bf16[16,4096]{1,0:T(8,128)(2,1)S(1)}, u32[]{:S(2)}, u32[]{:S(2)}) collective-permute-start(bf16[16,4096]{1,0:T(8,128)(2,1)S(1)} %collective-permute-done.12.refs_0_), channel_id=1, source_target_pairs={{0,16},{1,17},{2,18},{3,19},{4,20},{5,21},{6,22},{7,23},{8,24},{9,... | collective-permute-start | bytes 393224 | tf_op jit(solution)/shard_map/c_p0/ppermute | solution.py:64
  37.6 1.5 %collective-permute-start.17 = (bf16[64,1024]{1,0:T(8,128)(2,1)S(1)}, bf16[64,1024]{1,0:T(8,128)(2,1)S(1)}, u32[]{:S(2)}, u32[]{:S(2)}) collective-permute-start(bf16[64,1024]{1,0:T(8,128)(2,1)S(1)} %get-tuple-element.43), channel_id=1, source_target_pairs={{0,1},{1,0},{2,3},{3,2},{4,5},{5,4},{6,7},{7,6},{8,9},{9,8},{10,11... | collective-permute-start | bytes 393224 | tf_op jit(solution)/shard_map/got0/ppermute | solution.py:64
  40.1 2.4 %shard_map.86 = (f32[64,1024]{1,0:T(8,128)S(1)}, bf16[64,1024]{1,0:T(8,128)(2,1)S(1)}, f32[64,1024]{1,0:T(8,128)S(1)}) custom-call(f32[8,256]{1,0:T(8,128)S(1)} %get-tuple-element.37._.weight_ref, bf16[1024,4096]{1,0:T(8,128)(2,1)S(1)} %shard_map.84.train_ref, f32[64,1024]{1,0:T(8,128)S(1)} %get-tuple-element.42.own_p, ...), custom_call_target="tpu_custom_call" | custom-call | tf_op jit(solution)/shard_map/pallas_call | solution.py:258
  42.8 1.3 %collective-permute-done.18.refs_5_ = bf16[16,4096]{1,0:T(8,128)(2,1)S(1)} collective-permute-done((bf16[16,4096]{1,0:T(8,128)(2,1)S(1)}, bf16[16,4096]{1,0:T(8,128)(2,1)S(1)}, u32[]{:S(2)}, u32[]{:S(2)}) %collective-permute-start.18) | collective-permute-done | bytes 131104 | tf_op jit(solution)/shard_map/c_p1/ppermute | solution.py:64
  45.7 1.3 %shard_map.87 = (bf16[128,512]{1,0:T(8,128)(2,1)S(1)}, f32[128,512]{1,0:T(8,128)S(1)}) custom-call(f32[8,256]{1,0:T(8,128)S(1)} %get-tuple-element.37._.weight_ref, bf16[1024,4096]{1,0:T(8,128)(2,1)S(1)} %shard_map.84.train_ref, f32[64,1024]{1,0:T(8,128)S(1)} %get-tuple-element.54.beside, f32[64,1024]{1,0:T(8,128)S(1)} %get-tuple-element.46.beside_p, ...), custom_call_target="tpu_custom_call" | custom-call | tf_op jit(solution)/shard_map/pallas_call | solution.py:258
  47.0 1.1 %collective-permute-start.21 = (bf16[128,512]{1,0:T(8,128)(2,1)S(1)}, bf16[128,512]{1,0:T(8,128)(2,1)S(1)}, u32[]{:S(2)}, u32[]{:S(2)}) collective-permute-start(bf16[128,512]{1,0:T(8,128)(2,1)S(1)} %get-tuple-element.53), channel_id=1, source_target_pairs={{0,1},{1,0},{2,3},{3,2},{4,5},{5,4},{6,7},{7,6},{8,9},{9,8},{10,11... | collective-permute-start | bytes 393224 | tf_op jit(solution)/shard_map/got2/ppermute | solution.py:64
  48.1 1.3 %shard_map.88 = (bf16[128,512]{1,0:T(8,128)(2,1)S(1)}, f32[128,512]{1,0:T(8,128)S(1)}) custom-call(f32[8,256]{1,0:T(8,128)S(1)} %get-tuple-element.37._.weight_ref, bf16[1024,4096]{1,0:T(8,128)(2,1)S(1)} %shard_map.84.train_ref, f32[64,1024]{1,0:T(8,128)S(1)} %get-tuple-element.54.beside, f32[64,1024]{1,0:T(8,128)S(1)} %get-tuple-element.46.beside_p, ...), custom_call_target="tpu_custom_call" | custom-call | tf_op jit(solution)/shard_map/pallas_call | solution.py:258
  49.5 1.1 %collective-permute-start.22 = (bf16[128,512]{1,0:T(8,128)(2,1)S(1)}, bf16[128,512]{1,0:T(8,128)(2,1)S(1)}, u32[]{:S(2)}, u32[]{:S(2)}) collective-permute-start(bf16[128,512]{1,0:T(8,128)(2,1)S(1)} %get-tuple-element.56), channel_id=1, source_target_pairs={{0,1},{1,0},{2,3},{3,2},{4,5},{5,4},{6,7},{7,6},{8,9},{9,8},{10,11... | collective-permute-start | bytes 393224 | tf_op jit(solution)/shard_map/got3/ppermute | solution.py:64
  50.7 0.9 %shard_map.89.refs_4_ = f32[256,1024]{1,0:T(8,128)} custom-call(s32[1,1024]{1,0:T(1,128)S(1)} %bitcast.6, s32[256,1]{1,0:T(8,128)S(1)} %copy.11.query_ids, f32[64,1024]{1,0:T(8,128)S(1)} %get-tuple-element.57.refs_0_, bf16[64,1024]{1,0:T(8,128)(2,1)S(1)} %collective-permute-done.17.refs_1_, f32[64,1024]{1,0:T(8,128)S(1)} %get-tuple-element.58.refs_2_, ...), custom_call_target="tpu_custom_call" | custom-call | tf_op jit(solution)/shard_map/pallas_call | solution.py:300
  51.6 1.8 %collective-permute-done.21.refs_1_ = bf16[128,512]{1,0:T(8,128)(2,1)S(1)} collective-permute-done((bf16[128,512]{1,0:T(8,128)(2,1)S(1)}, bf16[128,512]{1,0:T(8,128)(2,1)S(1)}, u32[]{:S(2)}, u32[]{:S(2)}) %collective-permute-start.21) | collective-permute-done | bytes 131104 | tf_op jit(solution)/shard_map/got2/ppermute | solution.py:64
  53.4 2.3 %collective-permute-done.22.refs_3_ = bf16[128,512]{1,0:T(8,128)(2,1)S(1)} collective-permute-done((bf16[128,512]{1,0:T(8,128)(2,1)S(1)}, bf16[128,512]{1,0:T(8,128)(2,1)S(1)}, u32[]{:S(2)}, u32[]{:S(2)}) %collective-permute-start.22) | collective-permute-done | bytes 131104 | tf_op jit(solution)/shard_map/got3/ppermute | solution.py:64
  55.7 0.9 %shard_map.90 = f32[256,1024]{1,0:T(8,128)} custom-call(s32[1,1024]{1,0:T(1,128)S(1)} %bitcast.7, s32[256,1]{1,0:T(8,128)S(1)} %copy.11.query_ids, f32[128,512]{1,0:T(8,128)S(1)} %get-tuple-element.52.refs_0_, bf16[128,512]{1,0:T(8,128)(2,1)S(1)} %collective-permute-done.21.refs_1_, ...), custom_call_target="tpu_custom_call", output_to_operand_aliasing={{}: (6, {})} | custom-call | tf_op jit(solution)/shard_map/pallas_call | solution.py:300
  (42 shorter events, 4.4 us)
Async XLA Ops:
  2.8 11.2 %collective-permute-start = (bf16[32,4096]{1,0:T(8,128)(2,1)S(1)}, bf16[32,4096]{1,0:T(8,128)(2,1)S(1)}, u32[]{:S(2)}, u32[]{:S(2)}) collective-permute-start(bf16[32,4096]{1,0:T(8,128)(2,1)S(1)} %get-tuple-element.38.refs_0_), channel_id=1, source_target_pairs={{0,12},{1,13},{2,14},{3,15},{4,0},{5,1},{6,2},{7,3},{8,4},{9,5},{1... | collective-permute-start | bytes 786440 | tf_op jit(solution)/shard_map/a/ppermute | solution.py:64
  7.9 7.6 %collective-permute-start.1 = (bf16[32,4096]{1,0:T(8,128)(2,1)S(1)}, bf16[32,4096]{1,0:T(8,128)(2,1)S(1)}, u32[]{:S(2)}, u32[]{:S(2)}) collective-permute-start(bf16[32,4096]{1,0:T(8,128)(2,1)S(1)} %get-tuple-element.38.refs_0_), channel_id=1, source_target_pairs={{0,2},{1,3},{2,0},{3,1},{4,6},{5,7},{6,4},{7,5},{8,10},{9,11},{10,... | collective-permute-start | bytes 786440 | tf_op jit(solution)/shard_map/mine_x/ppermute | solution.py:64
  11.9 3.6 %collective-permute-start.2 = (bf16[32,4096]{1,0:T(8,128)(2,1)S(1)}, bf16[32,4096]{1,0:T(8,128)(2,1)S(1)}, u32[]{:S(2)}, u32[]{:S(2)}) collective-permute-start(bf16[32,4096]{1,0:T(8,128)(2,1)S(1)} %get-tuple-element.36.refs_2_), channel_id=1, source_target_pairs={{0,2},{1,3},{2,0},{3,1},{4,6},{5,7},{6,4},{7,5},{8,10},{9,11},{10,... | collective-permute-start | bytes 786440 | tf_op jit(solution)/shard_map/rest_x/ppermute | solution.py:64
  12.5 10.1 %collective-permute-start.4 = (bf16[32,4096]{1,0:T(8,128)(2,1)S(1)}, bf16[32,4096]{1,0:T(8,128)(2,1)S(1)}, u32[]{:S(2)}, u32[]{:S(2)}) collective-permute-start(bf16[32,4096]{1,0:T(8,128)(2,1)S(1)} %get-tuple-element.38.refs_0_), channel_id=1, source_target_pairs={{0,4},{1,5},{2,6},{3,7},{4,8},{5,9},{6,10},{7,11},{8,12},{9,13},{1... | collective-permute-start | bytes 786440 | tf_op jit(solution)/shard_map/b/ppermute | solution.py:64
  14.0 8.5 %collective-permute-start.3 = (bf16[32,4096]{1,0:T(8,128)(2,1)S(1)}, bf16[32,4096]{1,0:T(8,128)(2,1)S(1)}, u32[]{:S(2)}, u32[]{:S(2)}) collective-permute-start(bf16[32,4096]{1,0:T(8,128)(2,1)S(1)} %collective-permute-done.refs_4_), channel_id=1, source_target_pairs={{0,2},{1,3},{2,0},{3,1},{4,6},{5,7},{6,4},{7,5},{8,10},{9,11},{10,... | collective-permute-start | bytes 786440 | tf_op jit(solution)/shard_map/a_x/ppermute | solution.py:64
  14.0 8.7 %collective-permute-start.5 = (bf16[32,4096]{1,0:T(8,128)(2,1)S(1)}, bf16[32,4096]{1,0:T(8,128)(2,1)S(1)}, u32[]{:S(2)}, u32[]{:S(2)}) collective-permute-start(bf16[32,4096]{1,0:T(8,128)(2,1)S(1)} %collective-permute-done.refs_4_), channel_id=1, source_target_pairs={{0,16},{1,17},{2,18},{3,19},{4,20},{5,21},{6,22},{7,23},{8,24},{9,... | collective-permute-start | bytes 786440 | tf_op jit(solution)/shard_map/a_p/ppermute | solution.py:64
  22.8 5.9 %collective-permute-start.6 = (bf16[32,4096]{1,0:T(8,128)(2,1)S(1)}, bf16[32,4096]{1,0:T(8,128)(2,1)S(1)}, u32[]{:S(2)}, u32[]{:S(2)}) collective-permute-start(bf16[32,4096]{1,0:T(8,128)(2,1)S(1)} %collective-permute-done.4.refs_6_), channel_id=1, source_target_pairs={{0,2},{1,3},{2,0},{3,1},{4,6},{5,7},{6,4},{7,5},{8,10},{9,11},{10,... | collective-permute-start | bytes 786440 | tf_op jit(solution)/shard_map/b_x/ppermute | solution.py:64
  22.8 13.4 %collective-permute-start.13 = (bf16[16,4096]{1,0:T(8,128)(2,1)S(1)}, bf16[16,4096]{1,0:T(8,128)(2,1)S(1)}, u32[]{:S(2)}, u32[]{:S(2)}) collective-permute-start(bf16[16,4096]{1,0:T(8,128)(2,1)S(1)} %slice.25), channel_id=1, source_target_pairs={{0,12},{1,13},{2,14},{3,15},{4,0},{5,1},{6,2},{7,3},{8,4},{9,5},{1... | collective-permute-start | bytes 393224 | tf_op jit(solution)/shard_map/c1/ppermute | solution.py:64
  27.1 8.4 %collective-permute-start.9 = (bf16[32,4096]{1,0:T(8,128)(2,1)S(1)}, bf16[32,4096]{1,0:T(8,128)(2,1)S(1)}, u32[]{:S(2)}, u32[]{:S(2)}) collective-permute-start(bf16[32,4096]{1,0:T(8,128)(2,1)S(1)} %collective-permute-done.4.refs_6_), channel_id=1, source_target_pairs={{0,16},{1,17},{2,18},{3,19},{4,20},{5,21},{6,22},{7,23},{8,24},{9,... | collective-permute-start | bytes 786440 | tf_op jit(solution)/shard_map/b_p/ppermute | solution.py:64
  28.6 7.2 %collective-permute-start.12 = (bf16[16,4096]{1,0:T(8,128)(2,1)S(1)}, bf16[16,4096]{1,0:T(8,128)(2,1)S(1)}, u32[]{:S(2)}, u32[]{:S(2)}) collective-permute-start(bf16[16,4096]{1,0:T(8,128)(2,1)S(1)} %slice.23), channel_id=1, source_target_pairs={{0,4},{1,5},{2,6},{3,7},{4,8},{5,9},{6,10},{7,11},{8,12},{9,13},{1... | collective-permute-start | bytes 393224 | tf_op jit(solution)/shard_map/c0/ppermute | solution.py:64
  31.2 6.4 %collective-permute-start.7 = (bf16[16,4096]{1,0:T(8,128)(2,1)S(1)}, bf16[16,4096]{1,0:T(8,128)(2,1)S(1)}, u32[]{:S(2)}, u32[]{:S(2)}) collective-permute-start(bf16[16,4096]{1,0:T(8,128)(2,1)S(1)} %get-tuple-element.62), channel_id=1, source_target_pairs={{0,2},{1,3},{2,0},{3,1},{4,6},{5,7},{6,4},{7,5},{8,10},{9,11},{10,... | collective-permute-start | bytes 393224 | tf_op jit(solution)/shard_map/a_px0/ppermute | solution.py:64
  31.3 7.9 %collective-permute-start.8 = (bf16[16,4096]{1,0:T(8,128)(2,1)S(1)}, bf16[16,4096]{1,0:T(8,128)(2,1)S(1)}, u32[]{:S(2)}, u32[]{:S(2)}) collective-permute-start(bf16[16,4096]{1,0:T(8,128)(2,1)S(1)} %get-tuple-element.61), channel_id=1, source_target_pairs={{0,2},{1,3},{2,0},{3,1},{4,6},{5,7},{6,4},{7,5},{8,10},{9,11},{10,... | collective-permute-start | bytes 393224 | tf_op jit(solution)/shard_map/a_px1/ppermute | solution.py:64
  35.6 4.0 %collective-permute-start.10 = (bf16[16,4096]{1,0:T(8,128)(2,1)S(1)}, bf16[16,4096]{1,0:T(8,128)(2,1)S(1)}, u32[]{:S(2)}, u32[]{:S(2)}) collective-permute-start(bf16[16,4096]{1,0:T(8,128)(2,1)S(1)} %get-tuple-element.60), channel_id=1, source_target_pairs={{0,2},{1,3},{2,0},{3,1},{4,6},{5,7},{6,4},{7,5},{8,10},{9,11},{10,... | collective-permute-start | bytes 393224 | tf_op jit(solution)/shard_map/b_px0/ppermute | solution.py:64
  35.8 3.7 %collective-permute-start.11 = (bf16[16,4096]{1,0:T(8,128)(2,1)S(1)}, bf16[16,4096]{1,0:T(8,128)(2,1)S(1)}, u32[]{:S(2)}, u32[]{:S(2)}) collective-permute-start(bf16[16,4096]{1,0:T(8,128)(2,1)S(1)} %get-tuple-element.59), channel_id=1, source_target_pairs={{0,2},{1,3},{2,0},{3,1},{4,6},{5,7},{6,4},{7,5},{8,10},{9,11},{10,... | collective-permute-start | bytes 393224 | tf_op jit(solution)/shard_map/b_px1/ppermute | solution.py:64
  36.1 6.3 %collective-permute-start.16 = (bf16[16,4096]{1,0:T(8,128)(2,1)S(1)}, bf16[16,4096]{1,0:T(8,128)(2,1)S(1)}, u32[]{:S(2)}, u32[]{:S(2)}) collective-permute-start(bf16[16,4096]{1,0:T(8,128)(2,1)S(1)} %collective-permute-done.12.refs_0_), channel_id=1, source_target_pairs={{0,16},{1,17},{2,18},{3,19},{4,20},{5,21},{6,22},{7,23},{8,24},{9,... | collective-permute-start | bytes 393224 | tf_op jit(solution)/shard_map/c_p0/ppermute | solution.py:64
  37.6 5.2 %collective-permute-start.17 = (bf16[64,1024]{1,0:T(8,128)(2,1)S(1)}, bf16[64,1024]{1,0:T(8,128)(2,1)S(1)}, u32[]{:S(2)}, u32[]{:S(2)}) collective-permute-start(bf16[64,1024]{1,0:T(8,128)(2,1)S(1)} %get-tuple-element.43), channel_id=1, source_target_pairs={{0,1},{1,0},{2,3},{3,2},{4,5},{5,4},{6,7},{7,6},{8,9},{9,8},{10,11... | collective-permute-start | bytes 393224 | tf_op jit(solution)/shard_map/got0/ppermute | solution.py:64
  39.2 5.0 %collective-permute-start.18 = (bf16[16,4096]{1,0:T(8,128)(2,1)S(1)}, bf16[16,4096]{1,0:T(8,128)(2,1)S(1)}, u32[]{:S(2)}, u32[]{:S(2)}) collective-permute-start(bf16[16,4096]{1,0:T(8,128)(2,1)S(1)} %get-tuple-element.61), channel_id=1, source_target_pairs={{0,12},{1,13},{2,14},{3,15},{4,0},{5,1},{6,2},{7,3},{8,4},{9,5},{1... | collective-permute-start | bytes 393224 | tf_op jit(solution)/shard_map/c_p1/ppermute | solution.py:64
  39.5 5.6 %collective-permute-start.14 = (bf16[16,4096]{1,0:T(8,128)(2,1)S(1)}, bf16[16,4096]{1,0:T(8,128)(2,1)S(1)}, u32[]{:S(2)}, u32[]{:S(2)}) collective-permute-start(bf16[16,4096]{1,0:T(8,128)(2,1)S(1)} %collective-permute-done.12.refs_0_), channel_id=1, source_target_pairs={{0,2},{1,3},{2,0},{3,1},{4,6},{5,7},{6,4},{7,5},{8,10},{9,11},{10,... | collective-permute-start | bytes 393224 | tf_op jit(solution)/shard_map/c_x0/ppermute | solution.py:64
  39.5 5.6 %collective-permute-start.15 = (bf16[16,4096]{1,0:T(8,128)(2,1)S(1)}, bf16[16,4096]{1,0:T(8,128)(2,1)S(1)}, u32[]{:S(2)}, u32[]{:S(2)}) collective-permute-start(bf16[16,4096]{1,0:T(8,128)(2,1)S(1)} %collective-permute-done.13.refs_1_), channel_id=1, source_target_pairs={{0,2},{1,3},{2,0},{3,1},{4,6},{5,7},{6,4},{7,5},{8,10},{9,11},{10,... | collective-permute-start | bytes 393224 | tf_op jit(solution)/shard_map/c_x1/ppermute | solution.py:64
  44.1 1.3 %collective-permute-start.19 = (bf16[16,4096]{1,0:T(8,128)(2,1)S(1)}, bf16[16,4096]{1,0:T(8,128)(2,1)S(1)}, u32[]{:S(2)}, u32[]{:S(2)}) collective-permute-start(bf16[16,4096]{1,0:T(8,128)(2,1)S(1)} %collective-permute-done.16.refs_4_), channel_id=1, source_target_pairs={{0,2},{1,3},{2,0},{3,1},{4,6},{5,7},{6,4},{7,5},{8,10},{9,11},{10,... | collective-permute-start | bytes 393224 | tf_op jit(solution)/shard_map/c_px0/ppermute | solution.py:64
  44.1 1.5 %collective-permute-start.20 = (bf16[16,4096]{1,0:T(8,128)(2,1)S(1)}, bf16[16,4096]{1,0:T(8,128)(2,1)S(1)}, u32[]{:S(2)}, u32[]{:S(2)}) collective-permute-start(bf16[16,4096]{1,0:T(8,128)(2,1)S(1)} %collective-permute-done.18.refs_5_), channel_id=1, source_target_pairs={{0,2},{1,3},{2,0},{3,1},{4,6},{5,7},{6,4},{7,5},{8,10},{9,11},{10,... | collective-permute-start | bytes 393224 | tf_op jit(solution)/shard_map/c_px1/ppermute | solution.py:64
  44.7 6.0 %collective-permute-start.23 = (bf16[64,1024]{1,0:T(8,128)(2,1)S(1)}, bf16[64,1024]{1,0:T(8,128)(2,1)S(1)}, u32[]{:S(2)}, u32[]{:S(2)}) collective-permute-start(bf16[64,1024]{1,0:T(8,128)(2,1)S(1)} %get-tuple-element.49), channel_id=1, source_target_pairs={{0,1},{1,0},{2,3},{3,2},{4,5},{5,4},{6,7},{7,6},{8,9},{9,8},{10,11... | collective-permute-start | bytes 393224 | tf_op jit(solution)/shard_map/got1/ppermute | solution.py:64
  47.0 6.4 %collective-permute-start.21 = (bf16[128,512]{1,0:T(8,128)(2,1)S(1)}, bf16[128,512]{1,0:T(8,128)(2,1)S(1)}, u32[]{:S(2)}, u32[]{:S(2)}) collective-permute-start(bf16[128,512]{1,0:T(8,128)(2,1)S(1)} %get-tuple-element.53), channel_id=1, source_target_pairs={{0,1},{1,0},{2,3},{3,2},{4,5},{5,4},{6,7},{7,6},{8,9},{9,8},{10,11... | collective-permute-start | bytes 393224 | tf_op jit(solution)/shard_map/got2/ppermute | solution.py:64
  49.5 6.2 %collective-permute-start.22 = (bf16[128,512]{1,0:T(8,128)(2,1)S(1)}, bf16[128,512]{1,0:T(8,128)(2,1)S(1)}, u32[]{:S(2)}, u32[]{:S(2)}) collective-permute-start(bf16[128,512]{1,0:T(8,128)(2,1)S(1)} %get-tuple-element.56), channel_id=1, source_target_pairs={{0,1},{1,0},{2,3},{3,2},{4,5},{5,4},{6,7},{7,6},{8,9},{9,8},{10,11... | collective-permute-start | bytes 393224 | tf_op jit(solution)/shard_map/got3/ppermute | solution.py:64
  (2 other events, 9.9 us)

commit v10 on v7

--- a/solution.py
+++ b/solution.py
@@ -168,25 +168,26 @@
     precond_rows(q_ref, lefts, rights, mine)
 
 
-def rest_kernel(weight_ref, layer_ref, q_hbm, lefts_ref, rights_ref, rest, weight, q_ref, sem):
+def rest_kernel(
+    weight_ref, layer_ref, q_hbm, train_hbm, lefts_ref, rights_ref, rest, train, weight, q_ref, sems
+):
     at = pl.multiple_of((1 - lax.axis_index("parts")) * HALF, HALF)
-    q_copy = pltpu.make_async_copy(q_hbm.at[pl.ds(at, HALF), :], q_ref, sem)
+    q_copy = pltpu.make_async_copy(q_hbm.at[pl.ds(at, HALF), :], q_ref, sems.at[0])
     q_copy.start()
+    copies = []
+    for k in range(train.shape[0] // STEP):
+        here = pl.ds(k * STEP, STEP)
+        copies.append(pltpu.make_async_copy(train_hbm.at[here, :], train.at[here, :], sems.at[1 + k]))
+        copies[-1].start()
     weight[...] = jnp.full(weight.shape, weight_ref[layer_ref[0]])
     lefts, rights = [lefts_ref[0], lefts_ref[1]], [rights_ref[0], rights_ref[1]]
     q_copy.wait()
     precond_rows(q_ref, lefts, rights, rest)
-
-
-def score_kernel(weight_ref, train_ref, *refs, picks, stored, early, columns, fetch):
-    if fetch:
-        *refs, train, sems = refs
-        copies = []
-        for k, at in enumerate(range(*columns, STEP)):
-            here = pl.ds(at, STEP)
-            copies.append(pltpu.make_async_copy(train_ref.at[here, :], train.at[here, :], sems.at[k]))
-            copies[-1].start()
-        train_ref = train
+    for copy in copies:
+        copy.wait()
+
+
+def score_kernel(weight_ref, train_ref, *refs, picks, stored, early, columns):
     inputs, refs = refs[: len(picks)], refs[len(picks) :]
     n_before = sum(taken for _, _, taken in early)
     before, outs = refs[:n_before], refs[n_before:]
@@ -198,8 +199,6 @@
     near_is_mine = z // 2 == layer
     for at in range(*columns, STEP):
         there, here = slice(at, at + STEP), slice(at - columns[0], at - columns[0] + STEP)
-        if fetch:
-            copies[at // STEP].wait()
         value = lax.dot_general(
             train_ref[there, :], queries, (((1,), (1,)), ((), ())), preferred_element_type=f32
         )
@@ -229,7 +228,7 @@
     )(*inputs)
 
 
-def call_scores(weight, train, inputs, stored=0, early=(), columns=None, fetch=False):
+def call_scores(weight, train, inputs, stored=0, early=(), columns=None):
     columns = columns or (0, train.shape[0])
     n = columns[1] - columns[0]
     total = sum(count for _, rows in inputs for _, count in rows)
@@ -244,12 +243,9 @@
             stored=stored,
             early=[(first, rows, a is not None) for a, first, rows in early],
             columns=columns,
-            fetch=fetch,
         ),
-        outs + ([jax.ShapeDtypeStruct(train.shape, train.dtype)] if fetch else []),
+        outs,
         [weight, train, *others],
-        [VMEM, HBM if fetch else VMEM] + [VMEM] * len(others),
-        [pltpu.SemaphoreType.DMA((n // STEP,))] if fetch else [],
     )
 
 
@@ -327,13 +323,14 @@
     )
     near = to_near(mine, "near")
     far = to_far(mine, "far")
-    rest, weight = kernel_call(
+    rest, train, weight = kernel_call(
         rest_kernel,
-        [shape((HALF, width), bf16), shape((8, STEP), f32)],
-        [in_hbm(layer_weight), layer_of, queries, lefts, rights],
-        [SMEM, SMEM, HBM, VMEM, VMEM],
-        [pltpu.VMEM((HALF, width), bf16), pltpu.SemaphoreType.DMA],
-    )
+        [shape((HALF, width), bf16), shape(train.shape, bf16), shape((8, STEP), f32)],
+        [in_hbm(layer_weight), layer_of, queries, train, lefts, rights],
+        [SMEM, SMEM, HBM, HBM, VMEM, VMEM],
+        [pltpu.VMEM((HALF, width), bf16), pltpu.SemaphoreType.DMA((1 + train.shape[0] // STEP,))],
+    )
+    score = functools.partial(call_scores, weight, train)
 
     def rows_of(*pieces):
         return [(piece, ((0, piece.shape[0]),)) for piece in pieces]
@@ -347,10 +344,7 @@
     far_p = to_part(far, "far_p")
     far_x = to_core(far, "far_x")
     rest_x = after(rest_x, far)
-    early0, train = call_scores(
-        weight, train, rows_of(mine, mine_x, rest, rest_x), stored=128, fetch=True
-    )
-    score = functools.partial(call_scores, weight, train)
+    (early0,) = score(rows_of(mine, mine_x, rest, rest_x), stored=128)
     near_p = after(near_p, early0)
     near_px = to_core(near_p, "near_px")
     far_px = to_core(far_p, "far_px")

time: 50 us -> 48.2 us (0.964)
  Pallas kernels: 20 us -> 16.5 us
  waiting for transfers between devices: 11.9 us -> 13.5 us
    pallas_call x6, Pallas kernels: 18.1 us -> 14.7 us  [kernel_call(): pl.pallas_call(kernel, out_shape=outs, in_specs=specs or [VMEM] * len(inp...]
    ppermute x19, waiting for transfers between devices: 11.9 us -> 13.5 us  [permute(): return lax.ppermute(value, AXES, pairs)]
  transfers between devices with their start and end apart: 19 -> 19, of which waited for: 8 -> 8; matrix products, arithmetic and copies ran while one was open for 0% -> 0% of each run, Pallas kernels for 33% -> 27%
where the time goes in v10:
time: 48.2 us; the launch traced here: 48 us
  starting transfers between devices  17 us (35%)
  Pallas kernels  16.5 us (34%)
  waiting for transfers between devices  13.5 us (28%)
  between operations  0.79 us (2%)
    ppermute x19, starting transfers between devices, permute(): return lax.ppermute(value, AXES, pairs)  17 us
    pallas_call x6, Pallas kernels, kernel_call(): pl.pallas_call(kernel, out_shape=outs, in_specs=specs or [VMEM] * len(inp...  14.7 us
    ppermute x19, waiting for transfers between devices, permute(): return lax.ppermute(value, AXES, pairs)  13.5 us
    pallas_call x2, Pallas kernels, call_final(): pl.pallas_call(functools.partial(final_kernel, groups=groups, n_given=len...  1.83 us
  transfers between devices with their start and end apart: 19, of which 8 were waited for; matrix products, arithmetic and copies ran while one was open for 0% of the time, Pallas kernels for 27%

profile of v10, /device:TPU:0, one launch (start us, length us, event | category | flops | bytes accessed | tf_op | source)
XLA Modules:
  0.0 48.0 jit_solution(3964951406418997527)
XLA Ops:
  0.0 2.8 %shard_map.82 = (bf16[32,4096]{1,0:T(8,128)(2,1)S(1)}, bf16[2,256,256]{2,1,0:T(8,128)(2,1)S(1)}, bf16[2,256,512]{2,1,0:T(8,128)(2,1)S(1)}) custom-call(bf16[64,4096]{1,0:T(8,128)(2,1)} %bitcast.9, f32[64,64]{1,0:T(8,128)} %bitcast.11, f32[64,64]{1,0:T(8,128)} %bitcast.12), custom_call_target="tpu_custom_call" | custom-call | tf_op jit(solution)/shard_map/pallas_call | solution.py:221
  2.8 3.1 %collective-permute-start.1 = (bf16[32,4096]{1,0:T(8,128)(2,1)S(1)}, bf16[32,4096]{1,0:T(8,128)(2,1)S(1)}, u32[]{:S(2)}, u32[]{:S(2)}) collective-permute-start(bf16[32,4096]{1,0:T(8,128)(2,1)S(1)} %get-tuple-element.29.refs_0_), channel_id=1, source_target_pairs={{0,4},{1,5},{2,6},{3,7},{4,0},{5,1},{6,2},{7,3},{8,12},{9,13},{10,... | collective-permute-start | bytes 786440 | tf_op jit(solution)/shard_map/near/ppermute | solution.py:64
  5.9 2.5 %collective-permute-start = (bf16[32,4096]{1,0:T(8,128)(2,1)S(1)}, bf16[32,4096]{1,0:T(8,128)(2,1)S(1)}, u32[]{:S(2)}, u32[]{:S(2)}) collective-permute-start(bf16[32,4096]{1,0:T(8,128)(2,1)S(1)} %get-tuple-element.29.refs_0_), channel_id=1, source_target_pairs={{0,12},{1,13},{2,14},{3,15},{4,8},{5,9},{6,10},{7,11},{8,4},{9,5},... | collective-permute-start | bytes 786440 | tf_op jit(solution)/shard_map/far/ppermute | solution.py:64
  9.0 4.3 %shard_map.83 = (bf16[32,4096]{1,0:T(8,128)(2,1)S(1)}, bf16[1024,4096]{1,0:T(8,128)(2,1)S(1)}, f32[8,256]{1,0:T(8,128)S(1)}) custom-call(f32[2]{0:T(128)} %weight_ref.1, s32[1]{0:T(128)S(6)} %copy.13.layer_ref, bf16[64,4096]{1,0:T(8,128)(2,1)} %bitcast.10, bf16[1024,4096]{1,0:T(8,128)(2,1)} %bitcast.8, bf16[2,256,256]{2,1,0:T(8,128)(2,1)S(1)} %get-tuple-element.25.lefts_ref, ...), custom_call_target="tpu_custom_call" | custom-call | tf_op jit(solution)/shard_map/pallas_call | solution.py:221
  13.9 1.5 %collective-permute-start.6 = (bf16[32,4096]{1,0:T(8,128)(2,1)S(1)}, bf16[32,4096]{1,0:T(8,128)(2,1)S(1)}, u32[]{:S(2)}, u32[]{:S(2)}) collective-permute-start(bf16[32,4096]{1,0:T(8,128)(2,1)S(1)} %collective-permute-done.1.refs_0_), channel_id=1, source_target_pairs={{0,16},{1,17},{2,18},{3,19},{4,20},{5,21},{6,22},{7,23},{8,24},{9,... | collective-permute-start | bytes 786440 | tf_op jit(solution)/shard_map/near_p/ppermute | solution.py:64
  15.4 4.7 %collective-permute-done.refs_4_ = bf16[32,4096]{1,0:T(8,128)(2,1)S(1)} collective-permute-done((bf16[32,4096]{1,0:T(8,128)(2,1)S(1)}, bf16[32,4096]{1,0:T(8,128)(2,1)S(1)}, u32[]{:S(2)}, u32[]{:S(2)}) %collective-permute-start) | collective-permute-done | bytes 262176 | tf_op jit(solution)/shard_map/far/ppermute | solution.py:64
  20.1 1.5 %collective-permute-start.11 = (bf16[32,4096]{1,0:T(8,128)(2,1)S(1)}, bf16[32,4096]{1,0:T(8,128)(2,1)S(1)}, u32[]{:S(2)}, u32[]{:S(2)}) collective-permute-start(bf16[32,4096]{1,0:T(8,128)(2,1)S(1)} %collective-permute-done.refs_4_), channel_id=1, source_target_pairs={{0,16},{1,17},{2,18},{3,19},{4,20},{5,21},{6,22},{7,23},{8,24},{9,... | collective-permute-start | bytes 786440 | tf_op jit(solution)/shard_map/far_p/ppermute | solution.py:64
  21.6 0.6 %collective-permute-start.2 = (bf16[32,4096]{1,0:T(8,128)(2,1)S(1)}, bf16[32,4096]{1,0:T(8,128)(2,1)S(1)}, u32[]{:S(2)}, u32[]{:S(2)}) collective-permute-start(bf16[32,4096]{1,0:T(8,128)(2,1)S(1)} %collective-permute-done.refs_4_), channel_id=1, source_target_pairs={{0,4},{1,5},{2,6},{3,7},{4,0},{5,1},{6,2},{7,3},{8,12},{9,13},{10,... | collective-permute-start | bytes 786440 | tf_op jit(solution)/shard_map/cross/ppermute | solution.py:64
  22.2 0.5 %collective-permute-start.5 = (bf16[32,4096]{1,0:T(8,128)(2,1)S(1)}, bf16[32,4096]{1,0:T(8,128)(2,1)S(1)}, u32[]{:S(2)}, u32[]{:S(2)}) collective-permute-start(bf16[32,4096]{1,0:T(8,128)(2,1)S(1)} %collective-permute-done.1.refs_0_), channel_id=1, source_target_pairs={{0,2},{1,3},{2,0},{3,1},{4,6},{5,7},{6,4},{7,5},{8,10},{9,11},{10,... | collective-permute-start | bytes 786440 | tf_op jit(solution)/shard_map/near_x/ppermute | solution.py:64
  22.7 2.4 %shard_map.84.refs_8_ = f32[128,1024]{1,0:T(8,128)S(1)} custom-call(f32[8,256]{1,0:T(8,128)S(1)} %get-tuple-element.27.weight_ref, bf16[1024,4096]{1,0:T(8,128)(2,1)S(1)} %get-tuple-element.28.train_ref, bf16[32,4096]{1,0:T(8,128)(2,1)S(1)} %get-tuple-element.29.refs_0_, bf16[32,4096]{1,0:T(8,128)(2,1)S(1)} %collective-permute-done.7.refs_1_, ...), custom_call_target="tpu_custom_call" | custom-call | tf_op jit(solution)/shard_map/pallas_call | solution.py:221
  25.3 2.5 %collective-permute-done.11.refs_6_ = bf16[32,4096]{1,0:T(8,128)(2,1)S(1)} collective-permute-done((bf16[32,4096]{1,0:T(8,128)(2,1)S(1)}, bf16[32,4096]{1,0:T(8,128)(2,1)S(1)}, u32[]{:S(2)}, u32[]{:S(2)}) %collective-permute-start.11) | collective-permute-done | bytes 262176 | tf_op jit(solution)/shard_map/far_p/ppermute | solution.py:64
  27.8 0.6 %collective-permute-done.2.refs_0_ = bf16[32,4096]{1,0:T(8,128)(2,1)S(1)} collective-permute-done((bf16[32,4096]{1,0:T(8,128)(2,1)S(1)}, bf16[32,4096]{1,0:T(8,128)(2,1)S(1)}, u32[]{:S(2)}, u32[]{:S(2)}) %collective-permute-start.2) | collective-permute-done | bytes 262176 | tf_op jit(solution)/shard_map/cross/ppermute | solution.py:64
  28.8 1.4 %collective-permute-start.4 = (bf16[16,4096]{1,0:T(8,128)(2,1)S(1)}, bf16[16,4096]{1,0:T(8,128)(2,1)S(1)}, u32[]{:S(2)}, u32[]{:S(2)}) collective-permute-start(bf16[16,4096]{1,0:T(8,128)(2,1)S(1)} %slice.8), channel_id=1, source_target_pairs={{0,16},{1,17},{2,18},{3,19},{4,20},{5,21},{6,22},{7,23},{8,24},{9,... | collective-permute-start | bytes 393224 | tf_op jit(solution)/shard_map/cross_pa/ppermute | solution.py:64
  30.2 2.5 %shard_map.85 = (f32[128,1024]{1,0:T(8,128)S(1)}, bf16[128,1024]{1,0:T(8,128)(2,1)S(1)}, f32[128,1024]{1,0:T(8,128)S(1)}) custom-call(f32[8,256]{1,0:T(8,128)S(1)} %get-tuple-element.27.weight_ref, bf16[1024,4096]{1,0:T(8,128)(2,1)S(1)} %get-tuple-element.28.train_ref, bf16[32,4096]{1,0:T(8,128)(2,1)S(1)} %collective-permute-done.1.refs_0_, ...), custom_call_target="tpu_custom_call" | custom-call | tf_op jit(solution)/shard_map/pallas_call | solution.py:221
  32.7 1.6 %collective-permute-start.17 = (bf16[128,1024]{1,0:T(8,128)(2,1)S(1)}, bf16[128,1024]{1,0:T(8,128)(2,1)S(1)}, u32[]{:S(2)}, u32[]{:S(2)}) collective-permute-start(bf16[128,1024]{1,0:T(8,128)(2,1)S(1)} %get-tuple-element.34), channel_id=1, source_target_pairs={{0,1},{1,0},{2,3},{3,2},{4,5},{5,4},{6,7},{7,6},{8,9},{9,8},{10,11... | collective-permute-start | bytes 786440 | tf_op jit(solution)/shard_map/got0/ppermute | solution.py:64
  34.8 0.8 %collective-permute-done.15.refs_5_ = bf16[16,4096]{1,0:T(8,128)(2,1)S(1)} collective-permute-done((bf16[16,4096]{1,0:T(8,128)(2,1)S(1)}, bf16[16,4096]{1,0:T(8,128)(2,1)S(1)}, u32[]{:S(2)}, u32[]{:S(2)}) %collective-permute-start.15) | collective-permute-done | bytes 131104 | tf_op jit(solution)/shard_map/cross_pxb/ppermute | solution.py:64
  35.9 1.3 %shard_map.86 = (bf16[128,512]{1,0:T(8,128)(2,1)S(1)}, f32[128,512]{1,0:T(8,128)S(1)}) custom-call(f32[8,256]{1,0:T(8,128)S(1)} %get-tuple-element.27.weight_ref, bf16[1024,4096]{1,0:T(8,128)(2,1)S(1)} %get-tuple-element.28.train_ref, bf16[32,4096]{1,0:T(8,128)(2,1)S(1)} %collective-permute-done.2.refs_0_, ...), custom_call_target="tpu_custom_call" | custom-call | tf_op jit(solution)/shard_map/pallas_call | solution.py:221
  37.2 1.4 %collective-permute-start.16 = (bf16[128,512]{1,0:T(8,128)(2,1)S(1)}, bf16[128,512]{1,0:T(8,128)(2,1)S(1)}, u32[]{:S(2)}, u32[]{:S(2)}) collective-permute-start(bf16[128,512]{1,0:T(8,128)(2,1)S(1)} %get-tuple-element.39), channel_id=1, source_target_pairs={{0,1},{1,0},{2,3},{3,2},{4,5},{5,4},{6,7},{7,6},{8,9},{9,8},{10,11... | collective-permute-start | bytes 393224 | tf_op jit(solution)/shard_map/got1/ppermute | solution.py:64
  38.6 1.3 %shard_map.87 = (bf16[128,512]{1,0:T(8,128)(2,1)S(1)}, f32[128,512]{1,0:T(8,128)S(1)}) custom-call(f32[8,256]{1,0:T(8,128)S(1)} %get-tuple-element.27.weight_ref, bf16[1024,4096]{1,0:T(8,128)(2,1)S(1)} %get-tuple-element.28.train_ref, bf16[32,4096]{1,0:T(8,128)(2,1)S(1)} %collective-permute-done.2.refs_0_, ...), custom_call_target="tpu_custom_call" | custom-call | tf_op jit(solution)/shard_map/pallas_call | solution.py:221
  39.9 1.9 %collective-permute-done.17.refs_1_ = bf16[128,1024]{1,0:T(8,128)(2,1)S(1)} collective-permute-done((bf16[128,1024]{1,0:T(8,128)(2,1)S(1)}, bf16[128,1024]{1,0:T(8,128)(2,1)S(1)}, u32[]{:S(2)}, u32[]{:S(2)}) %collective-permute-start.17) | collective-permute-done | bytes 262176 | tf_op jit(solution)/shard_map/got0/ppermute | solution.py:64
  41.9 1.5 %collective-permute-start.18 = (bf16[128,512]{1,0:T(8,128)(2,1)S(1)}, bf16[128,512]{1,0:T(8,128)(2,1)S(1)}, u32[]{:S(2)}, u32[]{:S(2)}) collective-permute-start(bf16[128,512]{1,0:T(8,128)(2,1)S(1)} %get-tuple-element.43), channel_id=1, source_target_pairs={{0,1},{1,0},{2,3},{3,2},{4,5},{5,4},{6,7},{7,6},{8,9},{9,8},{10,11... | collective-permute-start | bytes 393224 | tf_op jit(solution)/shard_map/got2/ppermute | solution.py:64
  43.5 0.9 %shard_map.88.refs_4_ = f32[256,1024]{1,0:T(8,128)} custom-call(s32[1,1024]{1,0:T(1,128)S(1)} %bitcast.6, s32[256,1]{1,0:T(8,128)S(1)} %copy.11.query_ids, f32[128,1024]{1,0:T(8,128)S(1)} %get-tuple-element.44.refs_0_, bf16[128,1024]{1,0:T(8,128)(2,1)S(1)} %collective-permute-done.17.refs_1_), custom_call_target="tpu_custom_call" | custom-call | tf_op jit(solution)/shard_map/pallas_call | solution.py:284
  44.7 2.4 %collective-permute-done.18.refs_3_ = bf16[128,512]{1,0:T(8,128)(2,1)S(1)} collective-permute-done((bf16[128,512]{1,0:T(8,128)(2,1)S(1)}, bf16[128,512]{1,0:T(8,128)(2,1)S(1)}, u32[]{:S(2)}, u32[]{:S(2)}) %collective-permute-start.18) | collective-permute-done | bytes 131104 | tf_op jit(solution)/shard_map/got2/ppermute | solution.py:64
  47.1 0.9 %shard_map.89 = f32[256,1024]{1,0:T(8,128)} custom-call(s32[1,1024]{1,0:T(1,128)S(1)} %bitcast.7, s32[256,1]{1,0:T(8,128)S(1)} %copy.11.query_ids, f32[128,512]{1,0:T(8,128)S(1)} %get-tuple-element.38.refs_0_, bf16[128,512]{1,0:T(8,128)(2,1)S(1)} %collective-permute-done.16.refs_1_, ...), custom_call_target="tpu_custom_call", output_to_operand_aliasing={{}: (6, {})} | custom-call | tf_op jit(solution)/shard_map/pallas_call | solution.py:284
  (29 shorter events, 2.1 us)
Async XLA Ops:
  2.8 11.1 %collective-permute-start.1 = (bf16[32,4096]{1,0:T(8,128)(2,1)S(1)}, bf16[32,4096]{1,0:T(8,128)(2,1)S(1)}, u32[]{:S(2)}, u32[]{:S(2)}) collective-permute-start(bf16[32,4096]{1,0:T(8,128)(2,1)S(1)} %get-tuple-element.29.refs_0_), channel_id=1, source_target_pairs={{0,4},{1,5},{2,6},{3,7},{4,0},{5,1},{6,2},{7,3},{8,12},{9,13},{10,... | collective-permute-start | bytes 786440 | tf_op jit(solution)/shard_map/near/ppermute | solution.py:64
  5.9 14.2 %collective-permute-start = (bf16[32,4096]{1,0:T(8,128)(2,1)S(1)}, bf16[32,4096]{1,0:T(8,128)(2,1)S(1)}, u32[]{:S(2)}, u32[]{:S(2)}) collective-permute-start(bf16[32,4096]{1,0:T(8,128)(2,1)S(1)} %get-tuple-element.29.refs_0_), channel_id=1, source_target_pairs={{0,12},{1,13},{2,14},{3,15},{4,8},{5,9},{6,10},{7,11},{8,4},{9,5},... | collective-permute-start | bytes 786440 | tf_op jit(solution)/shard_map/far/ppermute | solution.py:64
  13.3 8.9 %collective-permute-start.8 = (bf16[32,4096]{1,0:T(8,128)(2,1)S(1)}, bf16[32,4096]{1,0:T(8,128)(2,1)S(1)}, u32[]{:S(2)}, u32[]{:S(2)}) collective-permute-start(bf16[32,4096]{1,0:T(8,128)(2,1)S(1)} %get-tuple-element.31.refs_2_), channel_id=1, source_target_pairs={{0,2},{1,3},{2,0},{3,1},{4,6},{5,7},{6,4},{7,5},{8,10},{9,11},{10,... | collective-permute-start | bytes 786440 | tf_op jit(solution)/shard_map/rest_x/ppermute | solution.py:64
  13.4 8.8 %collective-permute-start.7 = (bf16[32,4096]{1,0:T(8,128)(2,1)S(1)}, bf16[32,4096]{1,0:T(8,128)(2,1)S(1)}, u32[]{:S(2)}, u32[]{:S(2)}) collective-permute-start(bf16[32,4096]{1,0:T(8,128)(2,1)S(1)} %get-tuple-element.29.refs_0_), channel_id=1, source_target_pairs={{0,2},{1,3},{2,0},{3,1},{4,6},{5,7},{6,4},{7,5},{8,10},{9,11},{10,... | collective-permute-start | bytes 786440 | tf_op jit(solution)/shard_map/mine_x/ppermute | solution.py:64
  13.9 11.2 %collective-permute-start.6 = (bf16[32,4096]{1,0:T(8,128)(2,1)S(1)}, bf16[32,4096]{1,0:T(8,128)(2,1)S(1)}, u32[]{:S(2)}, u32[]{:S(2)}) collective-permute-start(bf16[32,4096]{1,0:T(8,128)(2,1)S(1)} %collective-permute-done.1.refs_0_), channel_id=1, source_target_pairs={{0,16},{1,17},{2,18},{3,19},{4,20},{5,21},{6,22},{7,23},{8,24},{9,... | collective-permute-start | bytes 786440 | tf_op jit(solution)/shard_map/near_p/ppermute | solution.py:64
  20.1 7.7 %collective-permute-start.11 = (bf16[32,4096]{1,0:T(8,128)(2,1)S(1)}, bf16[32,4096]{1,0:T(8,128)(2,1)S(1)}, u32[]{:S(2)}, u32[]{:S(2)}) collective-permute-start(bf16[32,4096]{1,0:T(8,128)(2,1)S(1)} %collective-permute-done.refs_4_), channel_id=1, source_target_pairs={{0,16},{1,17},{2,18},{3,19},{4,20},{5,21},{6,22},{7,23},{8,24},{9,... | collective-permute-start | bytes 786440 | tf_op jit(solution)/shard_map/far_p/ppermute | solution.py:64
  21.6 6.8 %collective-permute-start.2 = (bf16[32,4096]{1,0:T(8,128)(2,1)S(1)}, bf16[32,4096]{1,0:T(8,128)(2,1)S(1)}, u32[]{:S(2)}, u32[]{:S(2)}) collective-permute-start(bf16[32,4096]{1,0:T(8,128)(2,1)S(1)} %collective-permute-done.refs_4_), channel_id=1, source_target_pairs={{0,4},{1,5},{2,6},{3,7},{4,0},{5,1},{6,2},{7,3},{8,12},{9,13},{10,... | collective-permute-start | bytes 786440 | tf_op jit(solution)/shard_map/cross/ppermute | solution.py:64
  22.2 6.6 %collective-permute-start.10 = (bf16[32,4096]{1,0:T(8,128)(2,1)S(1)}, bf16[32,4096]{1,0:T(8,128)(2,1)S(1)}, u32[]{:S(2)}, u32[]{:S(2)}) collective-permute-start(bf16[32,4096]{1,0:T(8,128)(2,1)S(1)} %collective-permute-done.refs_4_), channel_id=1, source_target_pairs={{0,2},{1,3},{2,0},{3,1},{4,6},{5,7},{6,4},{7,5},{8,10},{9,11},{10,... | collective-permute-start | bytes 786440 | tf_op jit(solution)/shard_map/far_x/ppermute | solution.py:64
  22.2 8.0 %collective-permute-start.5 = (bf16[32,4096]{1,0:T(8,128)(2,1)S(1)}, bf16[32,4096]{1,0:T(8,128)(2,1)S(1)}, u32[]{:S(2)}, u32[]{:S(2)}) collective-permute-start(bf16[32,4096]{1,0:T(8,128)(2,1)S(1)} %collective-permute-done.1.refs_0_), channel_id=1, source_target_pairs={{0,2},{1,3},{2,0},{3,1},{4,6},{5,7},{6,4},{7,5},{8,10},{9,11},{10,... | collective-permute-start | bytes 786440 | tf_op jit(solution)/shard_map/near_x/ppermute | solution.py:64
  25.1 5.0 %collective-permute-start.9 = (bf16[32,4096]{1,0:T(8,128)(2,1)S(1)}, bf16[32,4096]{1,0:T(8,128)(2,1)S(1)}, u32[]{:S(2)}, u32[]{:S(2)}) collective-permute-start(bf16[32,4096]{1,0:T(8,128)(2,1)S(1)} %collective-permute-done.6.refs_2_), channel_id=1, source_target_pairs={{0,2},{1,3},{2,0},{3,1},{4,6},{5,7},{6,4},{7,5},{8,10},{9,11},{10,... | collective-permute-start | bytes 786440 | tf_op jit(solution)/shard_map/near_px/ppermute | solution.py:64
  27.8 2.4 %collective-permute-start.12 = (bf16[32,4096]{1,0:T(8,128)(2,1)S(1)}, bf16[32,4096]{1,0:T(8,128)(2,1)S(1)}, u32[]{:S(2)}, u32[]{:S(2)}) collective-permute-start(bf16[32,4096]{1,0:T(8,128)(2,1)S(1)} %collective-permute-done.11.refs_6_), channel_id=1, source_target_pairs={{0,2},{1,3},{2,0},{3,1},{4,6},{5,7},{6,4},{7,5},{8,10},{9,11},{10,... | collective-permute-start | bytes 786440 | tf_op jit(solution)/shard_map/far_px/ppermute | solution.py:64
  28.5 5.8 %collective-permute-start.13 = (bf16[16,4096]{1,0:T(8,128)(2,1)S(1)}, bf16[16,4096]{1,0:T(8,128)(2,1)S(1)}, u32[]{:S(2)}, u32[]{:S(2)}) collective-permute-start(bf16[16,4096]{1,0:T(8,128)(2,1)S(1)} %slice.9), channel_id=1, source_target_pairs={{0,4},{1,5},{2,6},{3,7},{4,0},{5,1},{6,2},{7,3},{8,12},{9,13},{10,... | collective-permute-start | bytes 393224 | tf_op jit(solution)/shard_map/cross_pb/ppermute | solution.py:64
  28.8 5.7 %collective-permute-start.4 = (bf16[16,4096]{1,0:T(8,128)(2,1)S(1)}, bf16[16,4096]{1,0:T(8,128)(2,1)S(1)}, u32[]{:S(2)}, u32[]{:S(2)}) collective-permute-start(bf16[16,4096]{1,0:T(8,128)(2,1)S(1)} %slice.8), channel_id=1, source_target_pairs={{0,16},{1,17},{2,18},{3,19},{4,20},{5,21},{6,22},{7,23},{8,24},{9,... | collective-permute-start | bytes 393224 | tf_op jit(solution)/shard_map/cross_pa/ppermute | solution.py:64
  30.2 4.6 %collective-permute-start.3 = (bf16[32,4096]{1,0:T(8,128)(2,1)S(1)}, bf16[32,4096]{1,0:T(8,128)(2,1)S(1)}, u32[]{:S(2)}, u32[]{:S(2)}) collective-permute-start(bf16[32,4096]{1,0:T(8,128)(2,1)S(1)} %collective-permute-done.2.refs_0_), channel_id=1, source_target_pairs={{0,2},{1,3},{2,0},{3,1},{4,6},{5,7},{6,4},{7,5},{8,10},{9,11},{10,... | collective-permute-start | bytes 786440 | tf_op jit(solution)/shard_map/cross_x/ppermute | solution.py:64
  32.7 9.2 %collective-permute-start.17 = (bf16[128,1024]{1,0:T(8,128)(2,1)S(1)}, bf16[128,1024]{1,0:T(8,128)(2,1)S(1)}, u32[]{:S(2)}, u32[]{:S(2)}) collective-permute-start(bf16[128,1024]{1,0:T(8,128)(2,1)S(1)} %get-tuple-element.34), channel_id=1, source_target_pairs={{0,1},{1,0},{2,3},{3,2},{4,5},{5,4},{6,7},{7,6},{8,9},{9,8},{10,11... | collective-permute-start | bytes 786440 | tf_op jit(solution)/shard_map/got0/ppermute | solution.py:64
  34.3 1.3 %collective-permute-start.15 = (bf16[16,4096]{1,0:T(8,128)(2,1)S(1)}, bf16[16,4096]{1,0:T(8,128)(2,1)S(1)}, u32[]{:S(2)}, u32[]{:S(2)}) collective-permute-start(bf16[16,4096]{1,0:T(8,128)(2,1)S(1)} %collective-permute-done.13.refs_3_), channel_id=1, source_target_pairs={{0,2},{1,3},{2,0},{3,1},{4,6},{5,7},{6,4},{7,5},{8,10},{9,11},{10,... | collective-permute-start | bytes 393224 | tf_op jit(solution)/shard_map/cross_pxb/ppermute | solution.py:64
  34.5 1.3 %collective-permute-start.14 = (bf16[16,4096]{1,0:T(8,128)(2,1)S(1)}, bf16[16,4096]{1,0:T(8,128)(2,1)S(1)}, u32[]{:S(2)}, u32[]{:S(2)}) collective-permute-start(bf16[16,4096]{1,0:T(8,128)(2,1)S(1)} %collective-permute-done.4.refs_2_), channel_id=1, source_target_pairs={{0,2},{1,3},{2,0},{3,1},{4,6},{5,7},{6,4},{7,5},{8,10},{9,11},{10,... | collective-permute-start | bytes 393224 | tf_op jit(solution)/shard_map/cross_pxa/ppermute | solution.py:64
  35.9 7.5 %copy-start.1 = (s32[256]{0:T(256)S(1)}, s32[256]{0:T(256)}, u32[]{:S(2)}) copy-start(s32[256]{0:T(256)} %param.15) | copy-start | bytes 3076
  35.9 7.7 %copy-start = (s32[1024]{0:T(1024)S(1)}, s32[1024]{0:T(1024)}, u32[]{:S(2)}) copy-start(s32[1024]{0:T(1024)} %param.14) | copy-start | bytes 12292
  37.2 7.5 %collective-permute-start.16 = (bf16[128,512]{1,0:T(8,128)(2,1)S(1)}, bf16[128,512]{1,0:T(8,128)(2,1)S(1)}, u32[]{:S(2)}, u32[]{:S(2)}) collective-permute-start(bf16[128,512]{1,0:T(8,128)(2,1)S(1)} %get-tuple-element.39), channel_id=1, source_target_pairs={{0,1},{1,0},{2,3},{3,2},{4,5},{5,4},{6,7},{7,6},{8,9},{9,8},{10,11... | collective-permute-start | bytes 393224 | tf_op jit(solution)/shard_map/got1/ppermute | solution.py:64
  41.9 5.2 %collective-permute-start.18 = (bf16[128,512]{1,0:T(8,128)(2,1)S(1)}, bf16[128,512]{1,0:T(8,128)(2,1)S(1)}, u32[]{:S(2)}, u32[]{:S(2)}) collective-permute-start(bf16[128,512]{1,0:T(8,128)(2,1)S(1)} %get-tuple-element.43), channel_id=1, source_target_pairs={{0,1},{1,0},{2,3},{3,2},{4,5},{5,4},{6,7},{7,6},{8,9},{9,8},{10,11... | collective-permute-start | bytes 393224 | tf_op jit(solution)/shard_map/got2/ppermute | solution.py:64

commit v11 on v10

--- a/solution.py
+++ b/solution.py
@@ -342,42 +342,46 @@
     far = after(far, near)
     cross = to_near(far, "cross")
     far_p = to_part(far, "far_p")
-    far_x = to_core(far, "far_x")
-    rest_x = after(rest_x, far)
-    (early0,) = score(rows_of(mine, mine_x, rest, rest_x), stored=128)
-    near_p = after(near_p, early0)
+    far_xa = to_core(far[:CHUNK], "far_xa")
+    far_xb = to_core(far[CHUNK:], "far_xb")
     near_px = to_core(near_p, "near_px")
+    (early,) = score(rows_of(mine, mine_x, rest, rest_x, near, near_x), stored=192)
+    far_xb = after(far_xb, near_px)
+    send0, keep0 = score(rows_of(far, far_xa, far_xb), early=[(early, 0, 64)])
+    got0 = to_layer(send0, "got0")
+
+    far_p, cross = after(far_p, send0), after(cross, send0)
+    cross_p = to_near(far_p, "cross_p")
     far_px = to_core(far_p, "far_px")
-    cross_pa = to_part(cross[:CHUNK], "cross_pa")
-    cross_pb = to_near(far_p[CHUNK:], "cross_pb")
     cross_x = to_core(cross, "cross_x")
-    early1, send0, keep0 = score(
-        rows_of(near, near_x, near_p, near_px, far, far_x, far_p, far_px),
-        stored=128,
-        early=[(early0, 0, 128)],
-    )
-    got0 = to_layer(send0, "got0")
-    cross_pa, cross_pb = after(cross_pa, send0), after(cross_pb, send0)
-    cross_pxa = to_core(cross_pa, "cross_pxa")
-    cross_pxb = to_core(cross_pb, "cross_pxb")
-    last = rows_of(cross, cross_x, cross_pa, cross_pb, cross_pxa, cross_pxb)
-    n = train.shape[0]
-    send1, keep1 = score(last, early=[(early1, 0, 128)], columns=(0, n // 2))
+    send1, keep1 = score(rows_of(far_p, far_px, cross, cross_x), early=[(early, 64, 128)])
     got1 = to_layer(send1, "got1")
-    early1 = after(early1, send1)
-    send2, keep2 = score(last, early=[(early1, 0, 128)], columns=(n // 2, n))
-    send2 = after(send2, got0)
+
+    cross_p = after(cross_p, send1, got0)
+    cross_px0 = to_core(cross_p[:CHUNK], "cross_px0")
+    cross_px1 = to_core(cross_p[CHUNK:], "cross_px1")
+    last = rows_of(near_p, near_px, cross_p, cross_px0, cross_px1)
+    n, itself = train.shape[0], [(None, 0, 64)]
+    _, send2, keep2 = score(last, stored=64, early=itself, columns=(0, n // 2))
     got2 = to_layer(send2, "got2")
+    cross_p = after(cross_p, send2)
+    last = rows_of(near_p, near_px, cross_p, cross_px0, cross_px1)
+    _, send3, keep3 = score(last, stored=64, early=itself, columns=(n // 2, n))
+    send3 = after(send3, got1)
+    got3 = to_layer(send3, "got3")
 
     train_ids, query_ids = train_ids[None, :], query_ids[:, None]
     most = call_final(
-        train_ids, query_ids, [keep0, got0], ((0, [(0, 1, 0, 0)]), (1, [(0, 1, 64, 0)]))
+        train_ids,
+        query_ids,
+        [keep0, got0, keep1, got1],
+        ((0, [(0, 1, 0, 0)]), (1, [(2, 3, 0, 0)]), (2, [(2, 3, 64, 0)])),
     )
     return call_final(
         train_ids,
         query_ids,
-        [keep1, got1, keep2, got2],
-        ((2, [(0, 1, 0, 0), (2, 3, 0, n // 2)]), (3, [(0, 1, 64, 0), (2, 3, 64, n // 2)])),
+        [keep2, got2, keep3, got3],
+        ((3, [(0, 1, 0, 0), (2, 3, 0, n // 2)]),),
         most,
     )
 

time: 48.2 us -> 52.9 us (1.098)
  the two profiles are of different devices: /device:TPU:0 before, /device:TPU:26 now
where the time goes in v11:
time: 52.9 us; the launch traced here: 52.7 us
  waiting for transfers between devices  20.4 us (39%)
  Pallas kernels  20.2 us (38%)
  starting transfers between devices  11.1 us (21%)
  between operations  0.82 us (2%)
    ppermute x20, waiting for transfers between devices, permute(): return lax.ppermute(value, AXES, pairs)  20.4 us
    pallas_call x7, Pallas kernels, kernel_call(): pl.pallas_call(kernel, out_shape=outs, in_specs=specs or [VMEM] * len(inp...  18.4 us
    ppermute x20, starting transfers between devices, permute(): return lax.ppermute(value, AXES, pairs)  11.1 us
    pallas_call x2, Pallas kernels, call_final(): pl.pallas_call(functools.partial(final_kernel, groups=groups, n_given=len...  1.85 us
  transfers between devices with their start and end apart: 20, of which 7 were waited for; matrix products, arithmetic and copies ran while one was open for 0% of the time, Pallas kernels for 31%

profile of v11, /device:TPU:26, one launch (start us, length us, event | category | flops | bytes accessed | tf_op | source)
XLA Modules:
  0.0 52.7 jit_solution(6170100377900784769)
XLA Ops:
  0.0 2.8 %shard_map.82 = (bf16[32,4096]{1,0:T(8,128)(2,1)S(1)}, bf16[2,256,256]{2,1,0:T(8,128)(2,1)S(1)}, bf16[2,256,512]{2,1,0:T(8,128)(2,1)S(1)}) custom-call(bf16[64,4096]{1,0:T(8,128)(2,1)} %bitcast.9, f32[64,64]{1,0:T(8,128)} %bitcast.11, f32[64,64]{1,0:T(8,128)} %bitcast.12), custom_call_target="tpu_custom_call" | custom-call | tf_op jit(solution)/shard_map/pallas_call | solution.py:221
  2.8 0.5 collective-permute-start
  3.3 1.3 %collective-permute-start.3 = (bf16[32,4096]{1,0:T(8,128)(2,1)S(1)}, bf16[32,4096]{1,0:T(8,128)(2,1)S(1)}, u32[]{:S(2)}, u32[]{:S(2)}) collective-permute-start(bf16[32,4096]{1,0:T(8,128)(2,1)S(1)} %get-tuple-element.30.refs_0_), channel_id=1, source_target_pairs={{0,12},{1,13},{2,14},{3,15},{4,8},{5,9},{6,10},{7,11},{8,4},{9,5},... | collective-permute-start | bytes 786440 | tf_op jit(solution)/shard_map/far/ppermute | solution.py:64
  5.3 4.3 %shard_map.83 = (bf16[32,4096]{1,0:T(8,128)(2,1)S(1)}, bf16[1024,4096]{1,0:T(8,128)(2,1)S(1)}, f32[8,256]{1,0:T(8,128)S(1)}) custom-call(f32[2]{0:T(128)} %weight_ref.1, s32[1]{0:T(128)S(6)} %copy.13.layer_ref, bf16[64,4096]{1,0:T(8,128)(2,1)} %bitcast.10, bf16[1024,4096]{1,0:T(8,128)(2,1)} %bitcast.8, bf16[2,256,256]{2,1,0:T(8,128)(2,1)S(1)} %get-tuple-element.26.lefts_ref, ...), custom_call_target="tpu_custom_call" | custom-call | tf_op jit(solution)/shard_map/pallas_call | solution.py:221
  9.7 6.8 %collective-permute-done.refs_4_ = bf16[32,4096]{1,0:T(8,128)(2,1)S(1)} collective-permute-done((bf16[32,4096]{1,0:T(8,128)(2,1)S(1)}, bf16[32,4096]{1,0:T(8,128)(2,1)S(1)}, u32[]{:S(2)}, u32[]{:S(2)}) %collective-permute-start) | collective-permute-done | bytes 262176 | tf_op jit(solution)/shard_map/near/ppermute | solution.py:64
  16.5 0.5 %collective-permute-start.1 = (bf16[32,4096]{1,0:T(8,128)(2,1)S(1)}, bf16[32,4096]{1,0:T(8,128)(2,1)S(1)}, u32[]{:S(2)}, u32[]{:S(2)}) collective-permute-start(bf16[32,4096]{1,0:T(8,128)(2,1)S(1)} %collective-permute-done.refs_4_), channel_id=1, source_target_pairs={{0,16},{1,17},{2,18},{3,19},{4,20},{5,21},{6,22},{7,23},{8,24},{9,... | collective-permute-start | bytes 786440 | tf_op jit(solution)/shard_map/near_p/ppermute | solution.py:64
  17.1 1.2 %collective-permute-start.12 = (bf16[32,4096]{1,0:T(8,128)(2,1)S(1)}, bf16[32,4096]{1,0:T(8,128)(2,1)S(1)}, u32[]{:S(2)}, u32[]{:S(2)}) collective-permute-start(bf16[32,4096]{1,0:T(8,128)(2,1)S(1)} %collective-permute-done.3.refs_0_), channel_id=1, source_target_pairs={{0,4},{1,5},{2,6},{3,7},{4,0},{5,1},{6,2},{7,3},{8,12},{9,13},{10,... | collective-permute-start | bytes 786440 | tf_op jit(solution)/shard_map/cross/ppermute | solution.py:64
  18.3 0.5 %collective-permute-start.4 = (bf16[32,4096]{1,0:T(8,128)(2,1)S(1)}, bf16[32,4096]{1,0:T(8,128)(2,1)S(1)}, u32[]{:S(2)}, u32[]{:S(2)}) collective-permute-start(bf16[32,4096]{1,0:T(8,128)(2,1)S(1)} %collective-permute-done.3.refs_0_), channel_id=1, source_target_pairs={{0,16},{1,17},{2,18},{3,19},{4,20},{5,21},{6,22},{7,23},{8,24},{9,... | collective-permute-start | bytes 786440 | tf_op jit(solution)/shard_map/far_p/ppermute | solution.py:64
  18.8 6.8 %collective-permute-done.1.refs_0_ = bf16[32,4096]{1,0:T(8,128)(2,1)S(1)} collective-permute-done((bf16[32,4096]{1,0:T(8,128)(2,1)S(1)}, bf16[32,4096]{1,0:T(8,128)(2,1)S(1)}, u32[]{:S(2)}, u32[]{:S(2)}) %collective-permute-start.1) | collective-permute-done | bytes 262176 | tf_op jit(solution)/shard_map/near_p/ppermute | solution.py:64
  25.7 0.6 %collective-permute-start.6 = (bf16[16,4096]{1,0:T(8,128)(2,1)S(1)}, bf16[16,4096]{1,0:T(8,128)(2,1)S(1)}, u32[]{:S(2)}, u32[]{:S(2)}) collective-permute-start(bf16[16,4096]{1,0:T(8,128)(2,1)S(1)} %get-tuple-element.49), channel_id=1, source_target_pairs={{0,2},{1,3},{2,0},{3,1},{4,6},{5,7},{6,4},{7,5},{8,10},{9,11},{10,... | collective-permute-start | bytes 393224 | tf_op jit(solution)/shard_map/far_xb/ppermute | solution.py:64
  26.3 2.5 %shard_map.84.refs_3_.refs_4_ = f32[192,1024]{1,0:T(8,128)S(1)} custom-call(f32[8,256]{1,0:T(8,128)S(1)} %get-tuple-element.28.weight_ref, bf16[1024,4096]{1,0:T(8,128)(2,1)S(1)} %get-tuple-element.29.train_ref, bf16[32,4096]{1,0:T(8,128)(2,1)S(1)} %get-tuple-element.30.refs_0_, bf16[32,4096]{1,0:T(8,128)(2,1)S(1)} %collective-permute-done.7.refs_1_, ...), custom_call_target="tpu_custom_call" | custom-call | tf_op jit(solution)/shard_map/pallas_call | solution.py:221
  28.9 2.4 %shard_map.85 = (bf16[64,1024]{1,0:T(8,128)(2,1)S(1)}, f32[64,1024]{1,0:T(8,128)S(1)}) custom-call(f32[8,256]{1,0:T(8,128)S(1)} %get-tuple-element.28.weight_ref, bf16[1024,4096]{1,0:T(8,128)(2,1)S(1)} %get-tuple-element.29.train_ref, bf16[32,4096]{1,0:T(8,128)(2,1)S(1)} %collective-permute-done.3.refs_0_, ...), custom_call_target="tpu_custom_call" | custom-call | tf_op jit(solution)/shard_map/pallas_call | solution.py:221
  31.3 0.5 collective-permute-start.13
  31.8 1.5 %collective-permute-start.14 = (bf16[64,1024]{1,0:T(8,128)(2,1)S(1)}, bf16[64,1024]{1,0:T(8,128)(2,1)S(1)}, u32[]{:S(2)}, u32[]{:S(2)}) collective-permute-start(bf16[64,1024]{1,0:T(8,128)(2,1)S(1)} %get-tuple-element.34), channel_id=1, source_target_pairs={{0,1},{1,0},{2,3},{3,2},{4,5},{5,4},{6,7},{7,6},{8,9},{9,8},{10,11... | collective-permute-start | bytes 393224 | tf_op jit(solution)/shard_map/got0/ppermute | solution.py:64
  33.4 2.4 %shard_map.86 = (bf16[128,1024]{1,0:T(8,128)(2,1)S(1)}, f32[128,1024]{1,0:T(8,128)S(1)}) custom-call(f32[8,256]{1,0:T(8,128)S(1)} %get-tuple-element.28.weight_ref, bf16[1024,4096]{1,0:T(8,128)(2,1)S(1)} %get-tuple-element.29.train_ref, bf16[32,4096]{1,0:T(8,128)(2,1)S(1)} %collective-permute-done.4.refs_0_, ...), custom_call_target="tpu_custom_call" | custom-call | tf_op jit(solution)/shard_map/pallas_call | solution.py:221
  35.8 1.5 %collective-permute-start.18 = (bf16[128,1024]{1,0:T(8,128)(2,1)S(1)}, bf16[128,1024]{1,0:T(8,128)(2,1)S(1)}, u32[]{:S(2)}, u32[]{:S(2)}) collective-permute-start(bf16[128,1024]{1,0:T(8,128)(2,1)S(1)} %get-tuple-element.37), channel_id=1, source_target_pairs={{0,1},{1,0},{2,3},{3,2},{4,5},{5,4},{6,7},{7,6},{8,9},{9,8},{10,11... | collective-permute-start | bytes 786440 | tf_op jit(solution)/shard_map/got1/ppermute | solution.py:64
  37.7 2.8 %collective-permute-done.10.refs_2_ = bf16[32,4096]{1,0:T(8,128)(2,1)S(1)} collective-permute-done((bf16[32,4096]{1,0:T(8,128)(2,1)S(1)}, bf16[32,4096]{1,0:T(8,128)(2,1)S(1)}, u32[]{:S(2)}, u32[]{:S(2)}) %collective-permute-start.10) | collective-permute-done | bytes 262176 | tf_op jit(solution)/shard_map/cross_p/ppermute | solution.py:64
  41.1 0.8 %collective-permute-done.15.refs_3_ = bf16[16,4096]{1,0:T(8,128)(2,1)S(1)} collective-permute-done((bf16[16,4096]{1,0:T(8,128)(2,1)S(1)}, bf16[16,4096]{1,0:T(8,128)(2,1)S(1)}, u32[]{:S(2)}, u32[]{:S(2)}) %collective-permute-start.15) | collective-permute-done | bytes 131104 | tf_op jit(solution)/shard_map/cross_px0/ppermute | solution.py:64
  42.1 2.0 %shard_map.87 = (f32[64,512]{1,0:T(8,128)}, bf16[64,512]{1,0:T(8,128)(2,1)S(1)}, f32[64,512]{1,0:T(8,128)S(1)}) custom-call(f32[8,256]{1,0:T(8,128)S(1)} %get-tuple-element.28.weight_ref, bf16[1024,4096]{1,0:T(8,128)(2,1)S(1)} %get-tuple-element.29.train_ref, bf16[32,4096]{1,0:T(8,128)(2,1)S(1)} %collective-permute-done.1.refs_0_, ...), custom_call_target="tpu_custom_call" | custom-call | tf_op jit(solution)/shard_map/pallas_call | solution.py:221
  44.1 1.6 %collective-permute-start.17 = (bf16[64,512]{1,0:T(8,128)(2,1)S(1)}, bf16[64,512]{1,0:T(8,128)(2,1)S(1)}, u32[]{:S(2)}, u32[]{:S(2)}) collective-permute-start(bf16[64,512]{1,0:T(8,128)(2,1)S(1)} %get-tuple-element.40), channel_id=1, source_target_pairs={{0,1},{1,0},{2,3},{3,2},{4,5},{5,4},{6,7},{7,6},{8,9},{9,8},{10,11... | collective-permute-start | bytes 196616 | tf_op jit(solution)/shard_map/got2/ppermute | solution.py:64
  45.6 2.0 %shard_map.88 = (f32[64,512]{1,0:T(8,128)}, bf16[64,512]{1,0:T(8,128)(2,1)S(1)}, f32[64,512]{1,0:T(8,128)S(1)}) custom-call(f32[8,256]{1,0:T(8,128)S(1)} %get-tuple-element.28.weight_ref, bf16[1024,4096]{1,0:T(8,128)(2,1)S(1)} %get-tuple-element.29.train_ref, bf16[32,4096]{1,0:T(8,128)(2,1)S(1)} %collective-permute-done.1.refs_0_, ...), custom_call_target="tpu_custom_call" | custom-call | tf_op jit(solution)/shard_map/pallas_call | solution.py:221
  48.3 1.0 %shard_map.89.refs_4_ = f32[256,1024]{1,0:T(8,128)} custom-call(s32[1,1024]{1,0:T(1,128)S(1)} %bitcast.6, s32[256,1]{1,0:T(8,128)S(1)} %copy.11.query_ids, f32[64,1024]{1,0:T(8,128)S(1)} %get-tuple-element.45.refs_0_, bf16[64,1024]{1,0:T(8,128)(2,1)S(1)} %collective-permute-done.14.refs_1_, f32[128,1024]{1,0:T(8,128)S(1)} %get-tuple-element.46.refs_2_, ...), custom_call_target="tpu_custom_call" | custom-call | tf_op jit(solution)/shard_map/pallas_call | solution.py:284
  49.3 2.6 %collective-permute-done.19.refs_3_ = bf16[64,512]{1,0:T(8,128)(2,1)S(1)} collective-permute-done((bf16[64,512]{1,0:T(8,128)(2,1)S(1)}, bf16[64,512]{1,0:T(8,128)(2,1)S(1)}, u32[]{:S(2)}, u32[]{:S(2)}) %collective-permute-start.19) | collective-permute-done | bytes 65568 | tf_op jit(solution)/shard_map/got3/ppermute | solution.py:64
  51.9 0.8 %shard_map.90 = f32[256,1024]{1,0:T(8,128)} custom-call(s32[1,1024]{1,0:T(1,128)S(1)} %bitcast.7, s32[256,1]{1,0:T(8,128)S(1)} %copy.11.query_ids, f32[64,512]{1,0:T(8,128)S(1)} %get-tuple-element.39.refs_0_, bf16[64,512]{1,0:T(8,128)(2,1)S(1)} %collective-permute-done.17.refs_1_, ...), custom_call_target="tpu_custom_call", output_to_operand_aliasing={{}: (6, {})} | custom-call | tf_op jit(solution)/shard_map/pallas_call | solution.py:284
  (32 shorter events, 2.0 us)
Async XLA Ops:
  2.8 13.7 %collective-permute-start = (bf16[32,4096]{1,0:T(8,128)(2,1)S(1)}, bf16[32,4096]{1,0:T(8,128)(2,1)S(1)}, u32[]{:S(2)}, u32[]{:S(2)}) collective-permute-start(bf16[32,4096]{1,0:T(8,128)(2,1)S(1)} %get-tuple-element.30.refs_0_), channel_id=1, source_target_pairs={{0,4},{1,5},{2,6},{3,7},{4,0},{5,1},{6,2},{7,3},{8,12},{9,13},{10,... | collective-permute-start | bytes 786440 | tf_op jit(solution)/shard_map/near/ppermute | solution.py:64
  3.3 13.8 %collective-permute-start.3 = (bf16[32,4096]{1,0:T(8,128)(2,1)S(1)}, bf16[32,4096]{1,0:T(8,128)(2,1)S(1)}, u32[]{:S(2)}, u32[]{:S(2)}) collective-permute-start(bf16[32,4096]{1,0:T(8,128)(2,1)S(1)} %get-tuple-element.30.refs_0_), channel_id=1, source_target_pairs={{0,12},{1,13},{2,14},{3,15},{4,8},{5,9},{6,10},{7,11},{8,4},{9,5},... | collective-permute-start | bytes 786440 | tf_op jit(solution)/shard_map/far/ppermute | solution.py:64
  9.6 9.2 %collective-permute-start.8 = (bf16[32,4096]{1,0:T(8,128)(2,1)S(1)}, bf16[32,4096]{1,0:T(8,128)(2,1)S(1)}, u32[]{:S(2)}, u32[]{:S(2)}) collective-permute-start(bf16[32,4096]{1,0:T(8,128)(2,1)S(1)} %get-tuple-element.33.refs_2_), channel_id=1, source_target_pairs={{0,2},{1,3},{2,0},{3,1},{4,6},{5,7},{6,4},{7,5},{8,10},{9,11},{10,... | collective-permute-start | bytes 786440 | tf_op jit(solution)/shard_map/rest_x/ppermute | solution.py:64
  16.5 9.1 %collective-permute-start.1 = (bf16[32,4096]{1,0:T(8,128)(2,1)S(1)}, bf16[32,4096]{1,0:T(8,128)(2,1)S(1)}, u32[]{:S(2)}, u32[]{:S(2)}) collective-permute-start(bf16[32,4096]{1,0:T(8,128)(2,1)S(1)} %collective-permute-done.refs_4_), channel_id=1, source_target_pairs={{0,16},{1,17},{2,18},{3,19},{4,20},{5,21},{6,22},{7,23},{8,24},{9,... | collective-permute-start | bytes 786440 | tf_op jit(solution)/shard_map/near_p/ppermute | solution.py:64
  17.1 8.6 %collective-permute-start.7 = (bf16[32,4096]{1,0:T(8,128)(2,1)S(1)}, bf16[32,4096]{1,0:T(8,128)(2,1)S(1)}, u32[]{:S(2)}, u32[]{:S(2)}) collective-permute-start(bf16[32,4096]{1,0:T(8,128)(2,1)S(1)} %get-tuple-element.30.refs_0_), channel_id=1, source_target_pairs={{0,2},{1,3},{2,0},{3,1},{4,6},{5,7},{6,4},{7,5},{8,10},{9,11},{10,... | collective-permute-start | bytes 786440 | tf_op jit(solution)/shard_map/mine_x/ppermute | solution.py:64
  17.1 14.2 %collective-permute-start.12 = (bf16[32,4096]{1,0:T(8,128)(2,1)S(1)}, bf16[32,4096]{1,0:T(8,128)(2,1)S(1)}, u32[]{:S(2)}, u32[]{:S(2)}) collective-permute-start(bf16[32,4096]{1,0:T(8,128)(2,1)S(1)} %collective-permute-done.3.refs_0_), channel_id=1, source_target_pairs={{0,4},{1,5},{2,6},{3,7},{4,0},{5,1},{6,2},{7,3},{8,12},{9,13},{10,... | collective-permute-start | bytes 786440 | tf_op jit(solution)/shard_map/cross/ppermute | solution.py:64
  18.3 13.5 %collective-permute-start.4 = (bf16[32,4096]{1,0:T(8,128)(2,1)S(1)}, bf16[32,4096]{1,0:T(8,128)(2,1)S(1)}, u32[]{:S(2)}, u32[]{:S(2)}) collective-permute-start(bf16[32,4096]{1,0:T(8,128)(2,1)S(1)} %collective-permute-done.3.refs_0_), channel_id=1, source_target_pairs={{0,16},{1,17},{2,18},{3,19},{4,20},{5,21},{6,22},{7,23},{8,24},{9,... | collective-permute-start | bytes 786440 | tf_op jit(solution)/shard_map/far_p/ppermute | solution.py:64
  18.8 7.4 %collective-permute-start.9 = (bf16[32,4096]{1,0:T(8,128)(2,1)S(1)}, bf16[32,4096]{1,0:T(8,128)(2,1)S(1)}, u32[]{:S(2)}, u32[]{:S(2)}) collective-permute-start(bf16[32,4096]{1,0:T(8,128)(2,1)S(1)} %collective-permute-done.refs_4_), channel_id=1, source_target_pairs={{0,2},{1,3},{2,0},{3,1},{4,6},{5,7},{6,4},{7,5},{8,10},{9,11},{10,... | collective-permute-start | bytes 786440 | tf_op jit(solution)/shard_map/near_x/ppermute | solution.py:64
  25.6 3.2 %collective-permute-start.2 = (bf16[32,4096]{1,0:T(8,128)(2,1)S(1)}, bf16[32,4096]{1,0:T(8,128)(2,1)S(1)}, u32[]{:S(2)}, u32[]{:S(2)}) collective-permute-start(bf16[32,4096]{1,0:T(8,128)(2,1)S(1)} %collective-permute-done.1.refs_0_), channel_id=1, source_target_pairs={{0,2},{1,3},{2,0},{3,1},{4,6},{5,7},{6,4},{7,5},{8,10},{9,11},{10,... | collective-permute-start | bytes 786440 | tf_op jit(solution)/shard_map/near_px/ppermute | solution.py:64
  25.7 3.1 %collective-permute-start.6 = (bf16[16,4096]{1,0:T(8,128)(2,1)S(1)}, bf16[16,4096]{1,0:T(8,128)(2,1)S(1)}, u32[]{:S(2)}, u32[]{:S(2)}) collective-permute-start(bf16[16,4096]{1,0:T(8,128)(2,1)S(1)} %get-tuple-element.49), channel_id=1, source_target_pairs={{0,2},{1,3},{2,0},{3,1},{4,6},{5,7},{6,4},{7,5},{8,10},{9,11},{10,... | collective-permute-start | bytes 393224 | tf_op jit(solution)/shard_map/far_xb/ppermute | solution.py:64
  26.2 2.6 %collective-permute-start.5 = (bf16[16,4096]{1,0:T(8,128)(2,1)S(1)}, bf16[16,4096]{1,0:T(8,128)(2,1)S(1)}, u32[]{:S(2)}, u32[]{:S(2)}) collective-permute-start(bf16[16,4096]{1,0:T(8,128)(2,1)S(1)} %get-tuple-element.50), channel_id=1, source_target_pairs={{0,2},{1,3},{2,0},{3,1},{4,6},{5,7},{6,4},{7,5},{8,10},{9,11},{10,... | collective-permute-start | bytes 393224 | tf_op jit(solution)/shard_map/far_xa/ppermute | solution.py:64
  31.3 2.1 %collective-permute-start.13 = (bf16[32,4096]{1,0:T(8,128)(2,1)S(1)}, bf16[32,4096]{1,0:T(8,128)(2,1)S(1)}, u32[]{:S(2)}, u32[]{:S(2)}) collective-permute-start(bf16[32,4096]{1,0:T(8,128)(2,1)S(1)} %collective-permute-done.12.refs_2_), channel_id=1, source_target_pairs={{0,2},{1,3},{2,0},{3,1},{4,6},{5,7},{6,4},{7,5},{8,10},{9,11},{10,... | collective-permute-start | bytes 786440 | tf_op jit(solution)/shard_map/cross_x/ppermute | solution.py:64
  31.7 1.6 %collective-permute-start.11 = (bf16[32,4096]{1,0:T(8,128)(2,1)S(1)}, bf16[32,4096]{1,0:T(8,128)(2,1)S(1)}, u32[]{:S(2)}, u32[]{:S(2)}) collective-permute-start(bf16[32,4096]{1,0:T(8,128)(2,1)S(1)} %collective-permute-done.4.refs_0_), channel_id=1, source_target_pairs={{0,2},{1,3},{2,0},{3,1},{4,6},{5,7},{6,4},{7,5},{8,10},{9,11},{10,... | collective-permute-start | bytes 786440 | tf_op jit(solution)/shard_map/far_px/ppermute | solution.py:64
  31.8 8.6 %collective-permute-start.10 = (bf16[32,4096]{1,0:T(8,128)(2,1)S(1)}, bf16[32,4096]{1,0:T(8,128)(2,1)S(1)}, u32[]{:S(2)}, u32[]{:S(2)}) collective-permute-start(bf16[32,4096]{1,0:T(8,128)(2,1)S(1)} %collective-permute-done.4.refs_0_), channel_id=1, source_target_pairs={{0,4},{1,5},{2,6},{3,7},{4,0},{5,1},{6,2},{7,3},{8,12},{9,13},{10,... | collective-permute-start | bytes 786440 | tf_op jit(solution)/shard_map/cross_p/ppermute | solution.py:64
  31.8 5.8 %collective-permute-start.14 = (bf16[64,1024]{1,0:T(8,128)(2,1)S(1)}, bf16[64,1024]{1,0:T(8,128)(2,1)S(1)}, u32[]{:S(2)}, u32[]{:S(2)}) collective-permute-start(bf16[64,1024]{1,0:T(8,128)(2,1)S(1)} %get-tuple-element.34), channel_id=1, source_target_pairs={{0,1},{1,0},{2,3},{3,2},{4,5},{5,4},{6,7},{7,6},{8,9},{9,8},{10,11... | collective-permute-start | bytes 393224 | tf_op jit(solution)/shard_map/got0/ppermute | solution.py:64
  35.8 11.8 %collective-permute-start.18 = (bf16[128,1024]{1,0:T(8,128)(2,1)S(1)}, bf16[128,1024]{1,0:T(8,128)(2,1)S(1)}, u32[]{:S(2)}, u32[]{:S(2)}) collective-permute-start(bf16[128,1024]{1,0:T(8,128)(2,1)S(1)} %get-tuple-element.37), channel_id=1, source_target_pairs={{0,1},{1,0},{2,3},{3,2},{4,5},{5,4},{6,7},{7,6},{8,9},{9,8},{10,11... | collective-permute-start | bytes 786440 | tf_op jit(solution)/shard_map/got1/ppermute | solution.py:64
  40.5 1.4 %collective-permute-start.15 = (bf16[16,4096]{1,0:T(8,128)(2,1)S(1)}, bf16[16,4096]{1,0:T(8,128)(2,1)S(1)}, u32[]{:S(2)}, u32[]{:S(2)}) collective-permute-start(bf16[16,4096]{1,0:T(8,128)(2,1)S(1)} %get-tuple-element.48), channel_id=1, source_target_pairs={{0,2},{1,3},{2,0},{3,1},{4,6},{5,7},{6,4},{7,5},{8,10},{9,11},{10,... | collective-permute-start | bytes 393224 | tf_op jit(solution)/shard_map/cross_px0/ppermute | solution.py:64
  40.6 7.5 %copy-start.1 = (s32[256]{0:T(256)S(1)}, s32[256]{0:T(256)}, u32[]{:S(2)}) copy-start(s32[256]{0:T(256)} %param.15) | copy-start | bytes 3076
  40.6 7.7 %copy-start = (s32[1024]{0:T(1024)S(1)}, s32[1024]{0:T(1024)}, u32[]{:S(2)}) copy-start(s32[1024]{0:T(1024)} %param.14) | copy-start | bytes 12292
  40.6 1.5 %collective-permute-start.16 = (bf16[16,4096]{1,0:T(8,128)(2,1)S(1)}, bf16[16,4096]{1,0:T(8,128)(2,1)S(1)}, u32[]{:S(2)}, u32[]{:S(2)}) collective-permute-start(bf16[16,4096]{1,0:T(8,128)(2,1)S(1)} %get-tuple-element.47), channel_id=1, source_target_pairs={{0,2},{1,3},{2,0},{3,1},{4,6},{5,7},{6,4},{7,5},{8,10},{9,11},{10,... | collective-permute-start | bytes 393224 | tf_op jit(solution)/shard_map/cross_px1/ppermute | solution.py:64
  44.1 5.2 %collective-permute-start.17 = (bf16[64,512]{1,0:T(8,128)(2,1)S(1)}, bf16[64,512]{1,0:T(8,128)(2,1)S(1)}, u32[]{:S(2)}, u32[]{:S(2)}) collective-permute-start(bf16[64,512]{1,0:T(8,128)(2,1)S(1)} %get-tuple-element.40), channel_id=1, source_target_pairs={{0,1},{1,0},{2,3},{3,2},{4,5},{5,4},{6,7},{7,6},{8,9},{9,8},{10,11... | collective-permute-start | bytes 196616 | tf_op jit(solution)/shard_map/got2/ppermute | solution.py:64
  47.6 4.3 %collective-permute-start.19 = (bf16[64,512]{1,0:T(8,128)(2,1)S(1)}, bf16[64,512]{1,0:T(8,128)(2,1)S(1)}, u32[]{:S(2)}, u32[]{:S(2)}) collective-permute-start(bf16[64,512]{1,0:T(8,128)(2,1)S(1)} %get-tuple-element.44), channel_id=1, source_target_pairs={{0,1},{1,0},{2,3},{3,2},{4,5},{5,4},{6,7},{7,6},{8,9},{9,8},{10,11... | collective-permute-start | bytes 196616 | tf_op jit(solution)/shard_map/got3/ppermute | solution.py:64

commit v12 on v10

--- a/solution.py
+++ b/solution.py
@@ -256,22 +256,20 @@
     low = z % 2
     first = jnp.where(z // 2 == layer, low, 1 - low)
     copies = []
-    for k, (which, terms) in enumerate(groups):
+    for k, (which, keep, got, row, column) in enumerate(groups):
         block = first if which < 2 else 1 - first
         half = part if which % 2 == 0 else 1 - part
+        keep, got = given[keep], given[got]
+        columns = pl.ds(column, keep.shape[1])
         for i, c in enumerate((core, 1 - core)):
             at = pl.multiple_of(((block * 2 + c) * 2 + half) * HALF, HALF)
-            to = slice((2 * k + i) * HALF, (2 * k + i + 1) * HALF)
-            ids = query_ids[pl.ds(at, HALF), :]
-            for keep, got, row, column in terms:
-                keep, got = given[keep], given[got]
-                columns = slice(column, column + keep.shape[1])
-                total = keep[row + i * HALF : row + (i + 1) * HALF, :]
-                total = total + got[row + i * HALF : row + (i + 1) * HALF, :].astype(f32)
-                same = ids == train_ids[:, columns]
-                done[to, columns] = jnp.where(same, jnp.float32(0.0), total)
+            here, j = slice(row + i * HALF, row + (i + 1) * HALF), 2 * k + i
+            total = keep[here, :] + got[here, :].astype(f32)
+            same = query_ids[pl.ds(at, HALF), :] == train_ids[:, columns]
+            slot = done.at[j * HALF : (j + 1) * HALF, : keep.shape[1]]
+            slot[...] = jnp.where(same, jnp.float32(0.0), total)
             copies.append(
-                pltpu.make_async_copy(done.at[to, :], out.at[pl.ds(at, HALF), :], sems.at[2 * k + i])
+                pltpu.make_async_copy(slot, out.at[pl.ds(at, HALF), columns], sems.at[j])
             )
             copies[-1].start()
     for copy in copies:
@@ -287,7 +285,7 @@
         in_specs=[VMEM] * (2 + len(given)) + ([] if before is None else [HBM]),
         out_specs=HBM,
         scratch_shapes=[
-            pltpu.VMEM((2 * len(groups) * HALF, n), f32),
+            pltpu.VMEM((2 * len(groups) * HALF, max(a.shape[1] for a in given)), f32),
             pltpu.SemaphoreType.DMA((2 * len(groups),)),
         ],
         input_output_aliases={} if before is None else {len(inputs) - 1: 0},
@@ -339,6 +337,7 @@
     rest_x = to_core(rest, "rest_x")
     near_x = to_core(near, "near_x")
     near_p = to_part(near, "near_p")
+    mine_x = after(mine_x, near_x)
     far = after(far, near)
     cross = to_near(far, "cross")
     far_p = to_part(far, "far_p")
@@ -347,38 +346,44 @@
     (early0,) = score(rows_of(mine, mine_x, rest, rest_x), stored=128)
     near_p = after(near_p, early0)
     near_px = to_core(near_p, "near_px")
-    far_px = to_core(far_p, "far_px")
-    cross_pa = to_part(cross[:CHUNK], "cross_pa")
-    cross_pb = to_near(far_p[CHUNK:], "cross_pb")
+
+    far_px0 = to_core(far_p[:CHUNK], "far_px0")
+    far_px1 = to_core(far_p[CHUNK:], "far_px1")
+    cross_pa = to_part(after(cross[:CHUNK], far_x), "cross_pa")
+    cross_pb = to_near(after(far_p[CHUNK:], far_x), "cross_pb")
     cross_x = to_core(cross, "cross_x")
+    far_px1 = after(far_px1, cross_x)
     early1, send0, keep0 = score(
-        rows_of(near, near_x, near_p, near_px, far, far_x, far_p, far_px),
+        rows_of(near, near_x, near_p, near_px, far, far_x, far_p, far_px0, far_px1),
         stored=128,
         early=[(early0, 0, 128)],
     )
     got0 = to_layer(send0, "got0")
     cross_pa, cross_pb = after(cross_pa, send0), after(cross_pb, send0)
-    cross_pxa = to_core(cross_pa, "cross_pxa")
-    cross_pxb = to_core(cross_pb, "cross_pxb")
+    def by_columns(piece, name):
+        parts = [to_core(part, name) for part in jnp.split(piece, 2, axis=1)]
+        return jnp.concatenate(parts, axis=1)
+
+    cross_pxa, cross_pxb = by_columns(cross_pa, "cross_pxa"), by_columns(cross_pb, "cross_pxb")
     last = rows_of(cross, cross_x, cross_pa, cross_pb, cross_pxa, cross_pxb)
     n = train.shape[0]
-    send1, keep1 = score(last, early=[(early1, 0, 128)], columns=(0, n // 2))
+    cut = n * 3 // 4
+    send1, keep1 = score(last, early=[(early1, 0, 128)], columns=(0, cut))
     got1 = to_layer(send1, "got1")
     early1 = after(early1, send1)
-    send2, keep2 = score(last, early=[(early1, 0, 128)], columns=(n // 2, n))
+    send2, keep2 = score(last, early=[(early1, 0, 128)], columns=(cut, n))
     send2 = after(send2, got0)
     got2 = to_layer(send2, "got2")
 
     train_ids, query_ids = train_ids[None, :], query_ids[:, None]
     most = call_final(
-        train_ids, query_ids, [keep0, got0], ((0, [(0, 1, 0, 0)]), (1, [(0, 1, 64, 0)]))
-    )
-    return call_final(
         train_ids,
         query_ids,
-        [keep1, got1, keep2, got2],
-        ((2, [(0, 1, 0, 0), (2, 3, 0, n // 2)]), (3, [(0, 1, 64, 0), (2, 3, 64, n // 2)])),
-        most,
+        [keep0, got0, keep1, got1],
+        ((0, 0, 1, 0, 0), (1, 0, 1, 64, 0), (2, 2, 3, 0, 0), (3, 2, 3, 64, 0)),
+    )
+    return call_final(
+        train_ids, query_ids, [keep2, got2], ((2, 0, 1, 0, cut), (3, 0, 1, 64, cut)), most
     )
 
 

time: 48.2 us -> 52.6 us (1.091)
  the two profiles are of different devices: /device:TPU:0 before, /device:TPU:16 now
where the time goes in v12:
time: 52.6 us; the launch traced here: 52.5 us
  starting transfers between devices  18.4 us (35%)
  Pallas kernels  16.6 us (32%)
  waiting for transfers between devices  16.5 us (31%)
  between operations  0.82 us (2%)
    ppermute x22, starting transfers between devices, permute(): return lax.ppermute(value, AXES, pairs)  18.4 us
    ppermute x22, waiting for transfers between devices, permute(): return lax.ppermute(value, AXES, pairs)  16.5 us
    pallas_call x6, Pallas kernels, kernel_call(): pl.pallas_call(kernel, out_shape=outs, in_specs=specs or [VMEM] * len(inp...  14.7 us
    pallas_call x2, Pallas kernels, call_final(): pl.pallas_call(functools.partial(final_kernel, groups=groups, n_given=len...  1.87 us
  transfers between devices with their start and end apart: 22, of which 9 were waited for; matrix products, arithmetic and copies ran while one was open for 0% of the time, Pallas kernels for 25%

profile of v12, /device:TPU:16, one launch (start us, length us, event | category | flops | bytes accessed | tf_op | source)
XLA Modules:
  0.0 52.5 jit_solution(1508307347568791006)
XLA Ops:
  0.0 2.8 %shard_map.82 = (bf16[32,4096]{1,0:T(8,128)(2,1)S(1)}, bf16[2,256,256]{2,1,0:T(8,128)(2,1)S(1)}, bf16[2,256,512]{2,1,0:T(8,128)(2,1)S(1)}) custom-call(bf16[64,4096]{1,0:T(8,128)(2,1)} %bitcast.9, f32[64,64]{1,0:T(8,128)} %bitcast.11, f32[64,64]{1,0:T(8,128)} %bitcast.12), custom_call_target="tpu_custom_call" | custom-call | tf_op jit(solution)/shard_map/pallas_call | solution.py:221
  2.8 1.6 %collective-permute-start.1 = (bf16[32,4096]{1,0:T(8,128)(2,1)S(1)}, bf16[32,4096]{1,0:T(8,128)(2,1)S(1)}, u32[]{:S(2)}, u32[]{:S(2)}) collective-permute-start(bf16[32,4096]{1,0:T(8,128)(2,1)S(1)} %get-tuple-element.33.refs_0_), channel_id=1, source_target_pairs={{0,4},{1,5},{2,6},{3,7},{4,0},{5,1},{6,2},{7,3},{8,12},{9,13},{10,... | collective-permute-start | bytes 786440 | tf_op jit(solution)/shard_map/near/ppermute | solution.py:64
  5.1 4.3 %shard_map.83 = (bf16[32,4096]{1,0:T(8,128)(2,1)S(1)}, bf16[1024,4096]{1,0:T(8,128)(2,1)S(1)}, f32[8,256]{1,0:T(8,128)S(1)}) custom-call(f32[2]{0:T(128)} %weight_ref.1, s32[1]{0:T(128)S(6)} %copy.15.layer_ref, bf16[64,4096]{1,0:T(8,128)(2,1)} %bitcast.10, bf16[1024,4096]{1,0:T(8,128)(2,1)} %bitcast.8, bf16[2,256,256]{2,1,0:T(8,128)(2,1)S(1)} %get-tuple-element.29.lefts_ref, ...), custom_call_target="tpu_custom_call" | custom-call | tf_op jit(solution)/shard_map/pallas_call | solution.py:221
  10.0 2.1 %collective-permute-done.1.refs_0_ = bf16[32,4096]{1,0:T(8,128)(2,1)S(1)} collective-permute-done((bf16[32,4096]{1,0:T(8,128)(2,1)S(1)}, bf16[32,4096]{1,0:T(8,128)(2,1)S(1)}, u32[]{:S(2)}, u32[]{:S(2)}) %collective-permute-start.1) | collective-permute-done | bytes 262176 | tf_op jit(solution)/shard_map/near/ppermute | solution.py:64
  12.1 1.5 %collective-permute-start.7 = (bf16[32,4096]{1,0:T(8,128)(2,1)S(1)}, bf16[32,4096]{1,0:T(8,128)(2,1)S(1)}, u32[]{:S(2)}, u32[]{:S(2)}) collective-permute-start(bf16[32,4096]{1,0:T(8,128)(2,1)S(1)} %collective-permute-done.1.refs_0_), channel_id=1, source_target_pairs={{0,16},{1,17},{2,18},{3,19},{4,20},{5,21},{6,22},{7,23},{8,24},{9,... | collective-permute-start | bytes 786440 | tf_op jit(solution)/shard_map/near_p/ppermute | solution.py:64
  13.6 4.3 %collective-permute-done.refs_4_ = bf16[32,4096]{1,0:T(8,128)(2,1)S(1)} collective-permute-done((bf16[32,4096]{1,0:T(8,128)(2,1)S(1)}, bf16[32,4096]{1,0:T(8,128)(2,1)S(1)}, u32[]{:S(2)}, u32[]{:S(2)}) %collective-permute-start) | collective-permute-done | bytes 262176 | tf_op jit(solution)/shard_map/far/ppermute | solution.py:64
  17.8 1.8 %collective-permute-start.2 = (bf16[32,4096]{1,0:T(8,128)(2,1)S(1)}, bf16[32,4096]{1,0:T(8,128)(2,1)S(1)}, u32[]{:S(2)}, u32[]{:S(2)}) collective-permute-start(bf16[32,4096]{1,0:T(8,128)(2,1)S(1)} %collective-permute-done.refs_4_), channel_id=1, source_target_pairs={{0,4},{1,5},{2,6},{3,7},{4,0},{5,1},{6,2},{7,3},{8,12},{9,13},{10,... | collective-permute-start | bytes 786440 | tf_op jit(solution)/shard_map/cross/ppermute | solution.py:64
  20.2 2.4 %shard_map.84.refs_9_ = f32[128,1024]{1,0:T(8,128)S(1)} custom-call(f32[8,256]{1,0:T(8,128)S(1)} %get-tuple-element.31.weight_ref, bf16[1024,4096]{1,0:T(8,128)(2,1)S(1)} %get-tuple-element.32.train_ref, bf16[32,4096]{1,0:T(8,128)(2,1)S(1)} %get-tuple-element.33.refs_0_, bf16[32,4096]{1,0:T(8,128)(2,1)S(1)} %collective-permute-done.8.refs_1_, ...), custom_call_target="tpu_custom_call" | custom-call | tf_op jit(solution)/shard_map/pallas_call | solution.py:221
  22.6 0.6 %collective-permute-start.10 = (bf16[32,4096]{1,0:T(8,128)(2,1)S(1)}, bf16[32,4096]{1,0:T(8,128)(2,1)S(1)}, u32[]{:S(2)}, u32[]{:S(2)}) collective-permute-start(bf16[32,4096]{1,0:T(8,128)(2,1)S(1)} %collective-permute-done.7.refs_2_), channel_id=1, source_target_pairs={{0,2},{1,3},{2,0},{3,1},{4,6},{5,7},{6,4},{7,5},{8,10},{9,11},{10,... | collective-permute-start | bytes 786440 | tf_op jit(solution)/shard_map/near_px/ppermute | solution.py:64
  23.2 3.1 %collective-permute-done.2.refs_0_ = bf16[32,4096]{1,0:T(8,128)(2,1)S(1)} collective-permute-done((bf16[32,4096]{1,0:T(8,128)(2,1)S(1)}, bf16[32,4096]{1,0:T(8,128)(2,1)S(1)}, u32[]{:S(2)}, u32[]{:S(2)}) %collective-permute-start.2) | collective-permute-done | bytes 262176 | tf_op jit(solution)/shard_map/cross/ppermute | solution.py:64
  26.3 1.5 %collective-permute-done.11.refs_6_ = bf16[32,4096]{1,0:T(8,128)(2,1)S(1)} collective-permute-done((bf16[32,4096]{1,0:T(8,128)(2,1)S(1)}, bf16[32,4096]{1,0:T(8,128)(2,1)S(1)}, u32[]{:S(2)}, u32[]{:S(2)}) %collective-permute-start.11) | collective-permute-done | bytes 262176 | tf_op jit(solution)/shard_map/far_p/ppermute | solution.py:64
  28.4 4.7 %collective-permute-start.14 = (bf16[16,4096]{1,0:T(8,128)(2,1)S(1)}, bf16[16,4096]{1,0:T(8,128)(2,1)S(1)}, u32[]{:S(2)}, u32[]{:S(2)}) collective-permute-start(bf16[16,4096]{1,0:T(8,128)(2,1)S(1)} %get-tuple-element.43), channel_id=1, source_target_pairs={{0,4},{1,5},{2,6},{3,7},{4,0},{5,1},{6,2},{7,3},{8,12},{9,13},{10,... | collective-permute-start | bytes 393224 | tf_op jit(solution)/shard_map/cross_pb/ppermute | solution.py:64
  33.1 1.6 %collective-permute-start.5 = (bf16[16,4096]{1,0:T(8,128)(2,1)S(1)}, bf16[16,4096]{1,0:T(8,128)(2,1)S(1)}, u32[]{:S(2)}, u32[]{:S(2)}) collective-permute-start(bf16[16,4096]{1,0:T(8,128)(2,1)S(1)} %slice.13), channel_id=1, source_target_pairs={{0,16},{1,17},{2,18},{3,19},{4,20},{5,21},{6,22},{7,23},{8,24},{9,... | collective-permute-start | bytes 393224 | tf_op jit(solution)/shard_map/cross_pa/ppermute | solution.py:64
  34.7 2.5 %shard_map.85 = (f32[128,1024]{1,0:T(8,128)S(1)}, bf16[128,1024]{1,0:T(8,128)(2,1)S(1)}, f32[128,1024]{1,0:T(8,128)S(1)}) custom-call(f32[8,256]{1,0:T(8,128)S(1)} %get-tuple-element.31.weight_ref, bf16[1024,4096]{1,0:T(8,128)(2,1)S(1)} %get-tuple-element.32.train_ref, bf16[32,4096]{1,0:T(8,128)(2,1)S(1)} %collective-permute-done.1.refs_0_, ...), custom_call_target="tpu_custom_call" | custom-call | tf_op jit(solution)/shard_map/pallas_call | solution.py:221
  37.2 1.6 %collective-permute-start.19 = (bf16[128,1024]{1,0:T(8,128)(2,1)S(1)}, bf16[128,1024]{1,0:T(8,128)(2,1)S(1)}, u32[]{:S(2)}, u32[]{:S(2)}) collective-permute-start(bf16[128,1024]{1,0:T(8,128)(2,1)S(1)} %get-tuple-element.41), channel_id=1, source_target_pairs={{0,1},{1,0},{2,3},{3,2},{4,5},{5,4},{6,7},{7,6},{8,9},{9,8},{10,11... | collective-permute-start | bytes 786440 | tf_op jit(solution)/shard_map/got0/ppermute | solution.py:64
  40.1 0.6 %collective-permute-done.15 = bf16[16,2048]{1,0:T(8,128)(2,1)S(1)} collective-permute-done((bf16[16,2048]{1,0:T(8,128)(2,1)S(1)}, bf16[16,2048]{1,0:T(8,128)(2,1)S(1)}, u32[]{:S(2)}, u32[]{:S(2)}) %collective-permute-start.15) | collective-permute-done | bytes 65568 | tf_op jit(solution)/shard_map/cross_pxa/ppermute | solution.py:64
  40.9 1.9 %shard_map.86 = (bf16[128,768]{1,0:T(8,128)(2,1)S(1)}, f32[128,768]{1,0:T(8,128)S(1)}) custom-call(f32[8,256]{1,0:T(8,128)S(1)} %get-tuple-element.31.weight_ref, bf16[1024,4096]{1,0:T(8,128)(2,1)S(1)} %get-tuple-element.32.train_ref, bf16[32,4096]{1,0:T(8,128)(2,1)S(1)} %collective-permute-done.2.refs_0_, ...), custom_call_target="tpu_custom_call" | custom-call | tf_op jit(solution)/shard_map/pallas_call | solution.py:221
  42.8 0.6 %collective-permute-start.21 = (bf16[128,768]{1,0:T(8,128)(2,1)S(1)}, bf16[128,768]{1,0:T(8,128)(2,1)S(1)}, u32[]{:S(2)}, u32[]{:S(2)}) collective-permute-start(bf16[128,768]{1,0:T(8,128)(2,1)S(1)} %get-tuple-element.46), channel_id=1, source_target_pairs={{0,1},{1,0},{2,3},{3,2},{4,5},{5,4},{6,7},{7,6},{8,9},{9,8},{10,11... | collective-permute-start | bytes 589832 | tf_op jit(solution)/shard_map/got1/ppermute | solution.py:64
  43.4 0.8 %shard_map.87 = (bf16[128,256]{1,0:T(8,128)(2,1)S(1)}, f32[128,256]{1,0:T(8,128)S(1)}) custom-call(f32[8,256]{1,0:T(8,128)S(1)} %get-tuple-element.31.weight_ref, bf16[1024,4096]{1,0:T(8,128)(2,1)S(1)} %get-tuple-element.32.train_ref, bf16[32,4096]{1,0:T(8,128)(2,1)S(1)} %collective-permute-done.2.refs_0_, ...), custom_call_target="tpu_custom_call" | custom-call | tf_op jit(solution)/shard_map/pallas_call | solution.py:221
  44.1 0.8 %collective-permute-done.19.refs_1_ = bf16[128,1024]{1,0:T(8,128)(2,1)S(1)} collective-permute-done((bf16[128,1024]{1,0:T(8,128)(2,1)S(1)}, bf16[128,1024]{1,0:T(8,128)(2,1)S(1)}, u32[]{:S(2)}, u32[]{:S(2)}) %collective-permute-start.19) | collective-permute-done | bytes 262176 | tf_op jit(solution)/shard_map/got0/ppermute | solution.py:64
  45.0 1.7 %collective-permute-start.20 = (bf16[128,256]{1,0:T(8,128)(2,1)S(1)}, bf16[128,256]{1,0:T(8,128)(2,1)S(1)}, u32[]{:S(2)}, u32[]{:S(2)}) collective-permute-start(bf16[128,256]{1,0:T(8,128)(2,1)S(1)} %get-tuple-element.50), channel_id=1, source_target_pairs={{0,1},{1,0},{2,3},{3,2},{4,5},{5,4},{6,7},{7,6},{8,9},{9,8},{10,11... | collective-permute-start | bytes 196616 | tf_op jit(solution)/shard_map/got2/ppermute | solution.py:64
  46.8 3.8 %collective-permute-done.21.refs_3_ = bf16[128,768]{1,0:T(8,128)(2,1)S(1)} collective-permute-done((bf16[128,768]{1,0:T(8,128)(2,1)S(1)}, bf16[128,768]{1,0:T(8,128)(2,1)S(1)}, u32[]{:S(2)}, u32[]{:S(2)}) %collective-permute-start.21) | collective-permute-done | bytes 196640 | tf_op jit(solution)/shard_map/got1/ppermute | solution.py:64
  50.6 1.1 %shard_map.88.refs_2_ = f32[256,1024]{1,0:T(8,128)} custom-call(s32[1,1024]{1,0:T(1,128)S(1)} %bitcast.6, s32[256,1]{1,0:T(8,128)S(1)} %copy.11.query_ids, f32[128,1024]{1,0:T(8,128)S(1)} %get-tuple-element.51.refs_0_, bf16[128,1024]{1,0:T(8,128)(2,1)S(1)} %collective-permute-done.19.refs_1_, f32[128,768]{1,0:T(8,128)S(1)} %get-tuple-element.52.refs_2_, ...), custom_call_target="tpu_custom_call" | custom-call | tf_op jit(solution)/shard_map/pallas_call | solution.py:282
  51.7 0.8 %shard_map.89 = f32[256,1024]{1,0:T(8,128)} custom-call(s32[1,1024]{1,0:T(1,128)S(1)} %bitcast.7, s32[256,1]{1,0:T(8,128)S(1)} %copy.11.query_ids, f32[128,256]{1,0:T(8,128)S(1)} %get-tuple-element.48.refs_0_, bf16[128,256]{1,0:T(8,128)(2,1)S(1)} %collective-permute-done.20.refs_1_, f32[256,1024]{1,0:T(8,128)} %shard_map.88.refs_2_), custom_call_target="tpu_custom_call", output_to_operand_aliasing={{}: (4, {})} | custom-call | tf_op jit(solution)/shard_map/pallas_call | solution.py:282
  (41 shorter events, 3.4 us)
Async XLA Ops:
  2.8 9.3 %collective-permute-start.1 = (bf16[32,4096]{1,0:T(8,128)(2,1)S(1)}, bf16[32,4096]{1,0:T(8,128)(2,1)S(1)}, u32[]{:S(2)}, u32[]{:S(2)}) collective-permute-start(bf16[32,4096]{1,0:T(8,128)(2,1)S(1)} %get-tuple-element.33.refs_0_), channel_id=1, source_target_pairs={{0,4},{1,5},{2,6},{3,7},{4,0},{5,1},{6,2},{7,3},{8,12},{9,13},{10,... | collective-permute-start | bytes 786440 | tf_op jit(solution)/shard_map/near/ppermute | solution.py:64
  4.5 13.4 %collective-permute-start = (bf16[32,4096]{1,0:T(8,128)(2,1)S(1)}, bf16[32,4096]{1,0:T(8,128)(2,1)S(1)}, u32[]{:S(2)}, u32[]{:S(2)}) collective-permute-start(bf16[32,4096]{1,0:T(8,128)(2,1)S(1)} %get-tuple-element.33.refs_0_), channel_id=1, source_target_pairs={{0,12},{1,13},{2,14},{3,15},{4,8},{5,9},{6,10},{7,11},{8,4},{9,5},... | collective-permute-start | bytes 786440 | tf_op jit(solution)/shard_map/far/ppermute | solution.py:64
  9.4 10.2 %collective-permute-start.9 = (bf16[32,4096]{1,0:T(8,128)(2,1)S(1)}, bf16[32,4096]{1,0:T(8,128)(2,1)S(1)}, u32[]{:S(2)}, u32[]{:S(2)}) collective-permute-start(bf16[32,4096]{1,0:T(8,128)(2,1)S(1)} %get-tuple-element.37.refs_2_), channel_id=1, source_target_pairs={{0,2},{1,3},{2,0},{3,1},{4,6},{5,7},{6,4},{7,5},{8,10},{9,11},{10,... | collective-permute-start | bytes 786440 | tf_op jit(solution)/shard_map/rest_x/ppermute | solution.py:64
  9.5 10.7 %collective-permute-start.8 = (bf16[32,4096]{1,0:T(8,128)(2,1)S(1)}, bf16[32,4096]{1,0:T(8,128)(2,1)S(1)}, u32[]{:S(2)}, u32[]{:S(2)}) collective-permute-start(bf16[32,4096]{1,0:T(8,128)(2,1)S(1)} %get-tuple-element.33.refs_0_), channel_id=1, source_target_pairs={{0,2},{1,3},{2,0},{3,1},{4,6},{5,7},{6,4},{7,5},{8,10},{9,11},{10,... | collective-permute-start | bytes 786440 | tf_op jit(solution)/shard_map/mine_x/ppermute | solution.py:64
  12.1 8.1 %collective-permute-start.6 = (bf16[32,4096]{1,0:T(8,128)(2,1)S(1)}, bf16[32,4096]{1,0:T(8,128)(2,1)S(1)}, u32[]{:S(2)}, u32[]{:S(2)}) collective-permute-start(bf16[32,4096]{1,0:T(8,128)(2,1)S(1)} %collective-permute-done.1.refs_0_), channel_id=1, source_target_pairs={{0,2},{1,3},{2,0},{3,1},{4,6},{5,7},{6,4},{7,5},{8,10},{9,11},{10,... | collective-permute-start | bytes 786440 | tf_op jit(solution)/shard_map/near_x/ppermute | solution.py:64
  12.1 10.5 %collective-permute-start.7 = (bf16[32,4096]{1,0:T(8,128)(2,1)S(1)}, bf16[32,4096]{1,0:T(8,128)(2,1)S(1)}, u32[]{:S(2)}, u32[]{:S(2)}) collective-permute-start(bf16[32,4096]{1,0:T(8,128)(2,1)S(1)} %collective-permute-done.1.refs_0_), channel_id=1, source_target_pairs={{0,16},{1,17},{2,18},{3,19},{4,20},{5,21},{6,22},{7,23},{8,24},{9,... | collective-permute-start | bytes 786440 | tf_op jit(solution)/shard_map/near_p/ppermute | solution.py:64
  17.8 8.5 %collective-permute-start.2 = (bf16[32,4096]{1,0:T(8,128)(2,1)S(1)}, bf16[32,4096]{1,0:T(8,128)(2,1)S(1)}, u32[]{:S(2)}, u32[]{:S(2)}) collective-permute-start(bf16[32,4096]{1,0:T(8,128)(2,1)S(1)} %collective-permute-done.refs_4_), channel_id=1, source_target_pairs={{0,4},{1,5},{2,6},{3,7},{4,0},{5,1},{6,2},{7,3},{8,12},{9,13},{10,... | collective-permute-start | bytes 786440 | tf_op jit(solution)/shard_map/cross/ppermute | solution.py:64
  19.6 8.2 %collective-permute-start.11 = (bf16[32,4096]{1,0:T(8,128)(2,1)S(1)}, bf16[32,4096]{1,0:T(8,128)(2,1)S(1)}, u32[]{:S(2)}, u32[]{:S(2)}) collective-permute-start(bf16[32,4096]{1,0:T(8,128)(2,1)S(1)} %collective-permute-done.refs_4_), channel_id=1, source_target_pairs={{0,16},{1,17},{2,18},{3,19},{4,20},{5,21},{6,22},{7,23},{8,24},{9,... | collective-permute-start | bytes 786440 | tf_op jit(solution)/shard_map/far_p/ppermute | solution.py:64
  20.2 8.2 %collective-permute-start.4 = (bf16[32,4096]{1,0:T(8,128)(2,1)S(1)}, bf16[32,4096]{1,0:T(8,128)(2,1)S(1)}, u32[]{:S(2)}, u32[]{:S(2)}) collective-permute-start(bf16[32,4096]{1,0:T(8,128)(2,1)S(1)} %collective-permute-done.refs_4_), channel_id=1, source_target_pairs={{0,2},{1,3},{2,0},{3,1},{4,6},{5,7},{6,4},{7,5},{8,10},{9,11},{10,... | collective-permute-start | bytes 786440 | tf_op jit(solution)/shard_map/far_x/ppermute | solution.py:64
  22.6 12.0 %collective-permute-start.10 = (bf16[32,4096]{1,0:T(8,128)(2,1)S(1)}, bf16[32,4096]{1,0:T(8,128)(2,1)S(1)}, u32[]{:S(2)}, u32[]{:S(2)}) collective-permute-start(bf16[32,4096]{1,0:T(8,128)(2,1)S(1)} %collective-permute-done.7.refs_2_), channel_id=1, source_target_pairs={{0,2},{1,3},{2,0},{3,1},{4,6},{5,7},{6,4},{7,5},{8,10},{9,11},{10,... | collective-permute-start | bytes 786440 | tf_op jit(solution)/shard_map/near_px/ppermute | solution.py:64
  26.3 8.3 %collective-permute-start.3 = (bf16[32,4096]{1,0:T(8,128)(2,1)S(1)}, bf16[32,4096]{1,0:T(8,128)(2,1)S(1)}, u32[]{:S(2)}, u32[]{:S(2)}) collective-permute-start(bf16[32,4096]{1,0:T(8,128)(2,1)S(1)} %collective-permute-done.2.refs_0_), channel_id=1, source_target_pairs={{0,2},{1,3},{2,0},{3,1},{4,6},{5,7},{6,4},{7,5},{8,10},{9,11},{10,... | collective-permute-start | bytes 786440 | tf_op jit(solution)/shard_map/cross_x/ppermute | solution.py:64
  27.8 5.3 %collective-permute-start.13 = (bf16[16,4096]{1,0:T(8,128)(2,1)S(1)}, bf16[16,4096]{1,0:T(8,128)(2,1)S(1)}, u32[]{:S(2)}, u32[]{:S(2)}) collective-permute-start(bf16[16,4096]{1,0:T(8,128)(2,1)S(1)} %get-tuple-element.43), channel_id=1, source_target_pairs={{0,2},{1,3},{2,0},{3,1},{4,6},{5,7},{6,4},{7,5},{8,10},{9,11},{10,... | collective-permute-start | bytes 393224 | tf_op jit(solution)/shard_map/far_px1/ppermute | solution.py:64
  27.9 6.8 %collective-permute-start.12 = (bf16[16,4096]{1,0:T(8,128)(2,1)S(1)}, bf16[16,4096]{1,0:T(8,128)(2,1)S(1)}, u32[]{:S(2)}, u32[]{:S(2)}) collective-permute-start(bf16[16,4096]{1,0:T(8,128)(2,1)S(1)} %get-tuple-element.54), channel_id=1, source_target_pairs={{0,2},{1,3},{2,0},{3,1},{4,6},{5,7},{6,4},{7,5},{8,10},{9,11},{10,... | collective-permute-start | bytes 393224 | tf_op jit(solution)/shard_map/far_px0/ppermute | solution.py:64
  28.4 10.4 %collective-permute-start.14 = (bf16[16,4096]{1,0:T(8,128)(2,1)S(1)}, bf16[16,4096]{1,0:T(8,128)(2,1)S(1)}, u32[]{:S(2)}, u32[]{:S(2)}) collective-permute-start(bf16[16,4096]{1,0:T(8,128)(2,1)S(1)} %get-tuple-element.43), channel_id=1, source_target_pairs={{0,4},{1,5},{2,6},{3,7},{4,0},{5,1},{6,2},{7,3},{8,12},{9,13},{10,... | collective-permute-start | bytes 393224 | tf_op jit(solution)/shard_map/cross_pb/ppermute | solution.py:64
  33.1 6.3 %collective-permute-start.5 = (bf16[16,4096]{1,0:T(8,128)(2,1)S(1)}, bf16[16,4096]{1,0:T(8,128)(2,1)S(1)}, u32[]{:S(2)}, u32[]{:S(2)}) collective-permute-start(bf16[16,4096]{1,0:T(8,128)(2,1)S(1)} %slice.13), channel_id=1, source_target_pairs={{0,16},{1,17},{2,18},{3,19},{4,20},{5,21},{6,22},{7,23},{8,24},{9,... | collective-permute-start | bytes 393224 | tf_op jit(solution)/shard_map/cross_pa/ppermute | solution.py:64
  37.2 7.8 %collective-permute-start.19 = (bf16[128,1024]{1,0:T(8,128)(2,1)S(1)}, bf16[128,1024]{1,0:T(8,128)(2,1)S(1)}, u32[]{:S(2)}, u32[]{:S(2)}) collective-permute-start(bf16[128,1024]{1,0:T(8,128)(2,1)S(1)} %get-tuple-element.41), channel_id=1, source_target_pairs={{0,1},{1,0},{2,3},{3,2},{4,5},{5,4},{6,7},{7,6},{8,9},{9,8},{10,11... | collective-permute-start | bytes 786440 | tf_op jit(solution)/shard_map/got0/ppermute | solution.py:64
  38.8 1.3 %collective-permute-start.17 = (bf16[16,2048]{1,0:T(8,128)(2,1)S(1)}, bf16[16,2048]{1,0:T(8,128)(2,1)S(1)}, u32[]{:S(2)}, u32[]{:S(2)}) collective-permute-start(bf16[16,2048]{1,0:T(8,128)(2,1)S(1)} %get-tuple-element.56), channel_id=1, source_target_pairs={{0,2},{1,3},{2,0},{3,1},{4,6},{5,7},{6,4},{7,5},{8,10},{9,11},{10,... | collective-permute-start | bytes 196616 | tf_op jit(solution)/shard_map/cross_pxb/ppermute | solution.py:64
  38.9 1.8 %collective-permute-start.18 = (bf16[16,2048]{1,0:T(8,128)(2,1)S(1)}, bf16[16,2048]{1,0:T(8,128)(2,1)S(1)}, u32[]{:S(2)}, u32[]{:S(2)}) collective-permute-start(bf16[16,2048]{1,0:T(8,128)(2,1)S(1)} %get-tuple-element.55), channel_id=1, source_target_pairs={{0,2},{1,3},{2,0},{3,1},{4,6},{5,7},{6,4},{7,5},{8,10},{9,11},{10,... | collective-permute-start | bytes 196616 | tf_op jit(solution)/shard_map/cross_pxb/ppermute | solution.py:64
  39.4 1.3 %collective-permute-start.15 = (bf16[16,2048]{1,0:T(8,128)(2,1)S(1)}, bf16[16,2048]{1,0:T(8,128)(2,1)S(1)}, u32[]{:S(2)}, u32[]{:S(2)}) collective-permute-start(bf16[16,2048]{1,0:T(8,128)(2,1)S(1)} %get-tuple-element.58), channel_id=1, source_target_pairs={{0,2},{1,3},{2,0},{3,1},{4,6},{5,7},{6,4},{7,5},{8,10},{9,11},{10,... | collective-permute-start | bytes 196616 | tf_op jit(solution)/shard_map/cross_pxa/ppermute | solution.py:64
  39.5 1.3 %collective-permute-start.16 = (bf16[16,2048]{1,0:T(8,128)(2,1)S(1)}, bf16[16,2048]{1,0:T(8,128)(2,1)S(1)}, u32[]{:S(2)}, u32[]{:S(2)}) collective-permute-start(bf16[16,2048]{1,0:T(8,128)(2,1)S(1)} %get-tuple-element.57), channel_id=1, source_target_pairs={{0,2},{1,3},{2,0},{3,1},{4,6},{5,7},{6,4},{7,5},{8,10},{9,11},{10,... | collective-permute-start | bytes 196616 | tf_op jit(solution)/shard_map/cross_pxa/ppermute | solution.py:64
  40.9 5.8 %copy-start.1 = (s32[256]{0:T(256)S(1)}, s32[256]{0:T(256)}, u32[]{:S(2)}) copy-start(s32[256]{0:T(256)} %param.15) | copy-start | bytes 3076
  40.9 9.7 %copy-start = (s32[1024]{0:T(1024)S(1)}, s32[1024]{0:T(1024)}, u32[]{:S(2)}) copy-start(s32[1024]{0:T(1024)} %param.14) | copy-start | bytes 12292
  42.8 7.8 %collective-permute-start.21 = (bf16[128,768]{1,0:T(8,128)(2,1)S(1)}, bf16[128,768]{1,0:T(8,128)(2,1)S(1)}, u32[]{:S(2)}, u32[]{:S(2)}) collective-permute-start(bf16[128,768]{1,0:T(8,128)(2,1)S(1)} %get-tuple-element.46), channel_id=1, source_target_pairs={{0,1},{1,0},{2,3},{3,2},{4,5},{5,4},{6,7},{7,6},{8,9},{9,8},{10,11... | collective-permute-start | bytes 589832 | tf_op jit(solution)/shard_map/got1/ppermute | solution.py:64
  45.0 6.7 %collective-permute-start.20 = (bf16[128,256]{1,0:T(8,128)(2,1)S(1)}, bf16[128,256]{1,0:T(8,128)(2,1)S(1)}, u32[]{:S(2)}, u32[]{:S(2)}) collective-permute-start(bf16[128,256]{1,0:T(8,128)(2,1)S(1)} %get-tuple-element.50), channel_id=1, source_target_pairs={{0,1},{1,0},{2,3},{3,2},{4,5},{5,4},{6,7},{7,6},{8,9},{9,8},{10,11... | collective-permute-start | bytes 196616 | tf_op jit(solution)/shard_map/got2/ppermute | solution.py:64

commit v13 on v12

--- a/solution.py
+++ b/solution.py
@@ -337,7 +337,6 @@
     rest_x = to_core(rest, "rest_x")
     near_x = to_core(near, "near_x")
     near_p = to_part(near, "near_p")
-    mine_x = after(mine_x, near_x)
     far = after(far, near)
     cross = to_near(far, "cross")
     far_p = to_part(far, "far_p")
@@ -349,10 +348,10 @@
 
     far_px0 = to_core(far_p[:CHUNK], "far_px0")
     far_px1 = to_core(far_p[CHUNK:], "far_px1")
-    cross_pa = to_part(after(cross[:CHUNK], far_x), "cross_pa")
-    cross_pb = to_near(after(far_p[CHUNK:], far_x), "cross_pb")
+    cross_pa = to_part(after(cross[:CHUNK], far_x, near_x), "cross_pa")
+    cross_pb = to_near(after(far_p[CHUNK:], far_x, near_x), "cross_pb")
     cross_x = to_core(cross, "cross_x")
-    far_px1 = after(far_px1, cross_x)
+    far_px1 = after(far_px1, cross)
     early1, send0, keep0 = score(
         rows_of(near, near_x, near_p, near_px, far, far_x, far_p, far_px0, far_px1),
         stored=128,

time: 52.6 us -> 49.2 us (0.935)
  the two profiles are of different devices: /device:TPU:16 before, /device:TPU:0 now
where the time goes in v13:
time: 49.2 us; the launch traced here: 49 us
  starting transfers between devices  18.4 us (37%)
  Pallas kernels  16.6 us (34%)
  waiting for transfers between devices  13 us (26%)
  between operations  0.84 us (2%)
    ppermute x22, starting transfers between devices, permute(): return lax.ppermute(value, AXES, pairs)  18.4 us
    pallas_call x6, Pallas kernels, kernel_call(): pl.pallas_call(kernel, out_shape=outs, in_specs=specs or [VMEM] * len(inp...  14.7 us
    ppermute x22, waiting for transfers between devices, permute(): return lax.ppermute(value, AXES, pairs)  13 us
    pallas_call x2, Pallas kernels, call_final(): pl.pallas_call(functools.partial(final_kernel, groups=groups, n_given=len...  1.87 us
  transfers between devices with their start and end apart: 22, of which 7 were waited for; matrix products, arithmetic and copies ran while one was open for 0% of the time, Pallas kernels for 26%

profile of v13, /device:TPU:0, one launch (start us, length us, event | category | flops | bytes accessed | tf_op | source)
XLA Modules:
  0.0 49.0 jit_solution(16766572229723439545)
XLA Ops:
  0.0 2.8 %shard_map.82 = (bf16[32,4096]{1,0:T(8,128)(2,1)S(1)}, bf16[2,256,256]{2,1,0:T(8,128)(2,1)S(1)}, bf16[2,256,512]{2,1,0:T(8,128)(2,1)S(1)}) custom-call(bf16[64,4096]{1,0:T(8,128)(2,1)} %bitcast.9, f32[64,64]{1,0:T(8,128)} %bitcast.11, f32[64,64]{1,0:T(8,128)} %bitcast.12), custom_call_target="tpu_custom_call" | custom-call | tf_op jit(solution)/shard_map/pallas_call | solution.py:221
  2.8 3.1 %collective-permute-start.1 = (bf16[32,4096]{1,0:T(8,128)(2,1)S(1)}, bf16[32,4096]{1,0:T(8,128)(2,1)S(1)}, u32[]{:S(2)}, u32[]{:S(2)}) collective-permute-start(bf16[32,4096]{1,0:T(8,128)(2,1)S(1)} %get-tuple-element.32.refs_0_), channel_id=1, source_target_pairs={{0,4},{1,5},{2,6},{3,7},{4,0},{5,1},{6,2},{7,3},{8,12},{9,13},{10,... | collective-permute-start | bytes 786440 | tf_op jit(solution)/shard_map/near/ppermute | solution.py:64
  5.9 2.5 %collective-permute-start = (bf16[32,4096]{1,0:T(8,128)(2,1)S(1)}, bf16[32,4096]{1,0:T(8,128)(2,1)S(1)}, u32[]{:S(2)}, u32[]{:S(2)}) collective-permute-start(bf16[32,4096]{1,0:T(8,128)(2,1)S(1)} %get-tuple-element.32.refs_0_), channel_id=1, source_target_pairs={{0,12},{1,13},{2,14},{3,15},{4,8},{5,9},{6,10},{7,11},{8,4},{9,5},... | collective-permute-start | bytes 786440 | tf_op jit(solution)/shard_map/far/ppermute | solution.py:64
  9.0 4.3 %shard_map.83 = (bf16[32,4096]{1,0:T(8,128)(2,1)S(1)}, bf16[1024,4096]{1,0:T(8,128)(2,1)S(1)}, f32[8,256]{1,0:T(8,128)S(1)}) custom-call(f32[2]{0:T(128)} %weight_ref.1, s32[1]{0:T(128)S(6)} %copy.15.layer_ref, bf16[64,4096]{1,0:T(8,128)(2,1)} %bitcast.10, bf16[1024,4096]{1,0:T(8,128)(2,1)} %bitcast.8, bf16[2,256,256]{2,1,0:T(8,128)(2,1)S(1)} %get-tuple-element.28.lefts_ref, ...), custom_call_target="tpu_custom_call" | custom-call | tf_op jit(solution)/shard_map/pallas_call | solution.py:221
  13.9 1.5 %collective-permute-start.7 = (bf16[32,4096]{1,0:T(8,128)(2,1)S(1)}, bf16[32,4096]{1,0:T(8,128)(2,1)S(1)}, u32[]{:S(2)}, u32[]{:S(2)}) collective-permute-start(bf16[32,4096]{1,0:T(8,128)(2,1)S(1)} %collective-permute-done.1.refs_0_), channel_id=1, source_target_pairs={{0,16},{1,17},{2,18},{3,19},{4,20},{5,21},{6,22},{7,23},{8,24},{9,... | collective-permute-start | bytes 786440 | tf_op jit(solution)/shard_map/near_p/ppermute | solution.py:64
  15.4 4.7 %collective-permute-done.refs_4_ = bf16[32,4096]{1,0:T(8,128)(2,1)S(1)} collective-permute-done((bf16[32,4096]{1,0:T(8,128)(2,1)S(1)}, bf16[32,4096]{1,0:T(8,128)(2,1)S(1)}, u32[]{:S(2)}, u32[]{:S(2)}) %collective-permute-start) | collective-permute-done | bytes 262176 | tf_op jit(solution)/shard_map/far/ppermute | solution.py:64
  20.1 1.5 %collective-permute-start.11 = (bf16[32,4096]{1,0:T(8,128)(2,1)S(1)}, bf16[32,4096]{1,0:T(8,128)(2,1)S(1)}, u32[]{:S(2)}, u32[]{:S(2)}) collective-permute-start(bf16[32,4096]{1,0:T(8,128)(2,1)S(1)} %collective-permute-done.refs_4_), channel_id=1, source_target_pairs={{0,16},{1,17},{2,18},{3,19},{4,20},{5,21},{6,22},{7,23},{8,24},{9,... | collective-permute-start | bytes 786440 | tf_op jit(solution)/shard_map/far_p/ppermute | solution.py:64
  21.6 0.6 %collective-permute-start.2 = (bf16[32,4096]{1,0:T(8,128)(2,1)S(1)}, bf16[32,4096]{1,0:T(8,128)(2,1)S(1)}, u32[]{:S(2)}, u32[]{:S(2)}) collective-permute-start(bf16[32,4096]{1,0:T(8,128)(2,1)S(1)} %collective-permute-done.refs_4_), channel_id=1, source_target_pairs={{0,4},{1,5},{2,6},{3,7},{4,0},{5,1},{6,2},{7,3},{8,12},{9,13},{10,... | collective-permute-start | bytes 786440 | tf_op jit(solution)/shard_map/cross/ppermute | solution.py:64
  22.2 0.5 %collective-permute-start.5 = (bf16[32,4096]{1,0:T(8,128)(2,1)S(1)}, bf16[32,4096]{1,0:T(8,128)(2,1)S(1)}, u32[]{:S(2)}, u32[]{:S(2)}) collective-permute-start(bf16[32,4096]{1,0:T(8,128)(2,1)S(1)} %collective-permute-done.1.refs_0_), channel_id=1, source_target_pairs={{0,2},{1,3},{2,0},{3,1},{4,6},{5,7},{6,4},{7,5},{8,10},{9,11},{10,... | collective-permute-start | bytes 786440 | tf_op jit(solution)/shard_map/near_x/ppermute | solution.py:64
  22.7 2.4 %shard_map.84.refs_9_ = f32[128,1024]{1,0:T(8,128)S(1)} custom-call(f32[8,256]{1,0:T(8,128)S(1)} %get-tuple-element.30.weight_ref, bf16[1024,4096]{1,0:T(8,128)(2,1)S(1)} %get-tuple-element.31.train_ref, bf16[32,4096]{1,0:T(8,128)(2,1)S(1)} %get-tuple-element.32.refs_0_, bf16[32,4096]{1,0:T(8,128)(2,1)S(1)} %collective-permute-done.8.refs_1_, ...), custom_call_target="tpu_custom_call" | custom-call | tf_op jit(solution)/shard_map/pallas_call | solution.py:221
  25.3 2.5 %collective-permute-done.11.refs_6_ = bf16[32,4096]{1,0:T(8,128)(2,1)S(1)} collective-permute-done((bf16[32,4096]{1,0:T(8,128)(2,1)S(1)}, bf16[32,4096]{1,0:T(8,128)(2,1)S(1)}, u32[]{:S(2)}, u32[]{:S(2)}) %collective-permute-start.11) | collective-permute-done | bytes 262176 | tf_op jit(solution)/shard_map/far_p/ppermute | solution.py:64
  28.4 0.7 %collective-permute-start.14 = (bf16[16,4096]{1,0:T(8,128)(2,1)S(1)}, bf16[16,4096]{1,0:T(8,128)(2,1)S(1)}, u32[]{:S(2)}, u32[]{:S(2)}) collective-permute-start(bf16[16,4096]{1,0:T(8,128)(2,1)S(1)} %get-tuple-element.41), channel_id=1, source_target_pairs={{0,4},{1,5},{2,6},{3,7},{4,0},{5,1},{6,2},{7,3},{8,12},{9,13},{10,... | collective-permute-start | bytes 393224 | tf_op jit(solution)/shard_map/cross_pb/ppermute | solution.py:64
  29.1 1.6 %collective-permute-start.6 = (bf16[16,4096]{1,0:T(8,128)(2,1)S(1)}, bf16[16,4096]{1,0:T(8,128)(2,1)S(1)}, u32[]{:S(2)}, u32[]{:S(2)}) collective-permute-start(bf16[16,4096]{1,0:T(8,128)(2,1)S(1)} %slice.13), channel_id=1, source_target_pairs={{0,16},{1,17},{2,18},{3,19},{4,20},{5,21},{6,22},{7,23},{8,24},{9,... | collective-permute-start | bytes 393224 | tf_op jit(solution)/shard_map/cross_pa/ppermute | solution.py:64
  30.7 2.5 %shard_map.85 = (f32[128,1024]{1,0:T(8,128)S(1)}, bf16[128,1024]{1,0:T(8,128)(2,1)S(1)}, f32[128,1024]{1,0:T(8,128)S(1)}) custom-call(f32[8,256]{1,0:T(8,128)S(1)} %get-tuple-element.30.weight_ref, bf16[1024,4096]{1,0:T(8,128)(2,1)S(1)} %get-tuple-element.31.train_ref, bf16[32,4096]{1,0:T(8,128)(2,1)S(1)} %collective-permute-done.1.refs_0_, ...), custom_call_target="tpu_custom_call" | custom-call | tf_op jit(solution)/shard_map/pallas_call | solution.py:221
  33.2 1.6 %collective-permute-start.19 = (bf16[128,1024]{1,0:T(8,128)(2,1)S(1)}, bf16[128,1024]{1,0:T(8,128)(2,1)S(1)}, u32[]{:S(2)}, u32[]{:S(2)}) collective-permute-start(bf16[128,1024]{1,0:T(8,128)(2,1)S(1)} %get-tuple-element.39), channel_id=1, source_target_pairs={{0,1},{1,0},{2,3},{3,2},{4,5},{5,4},{6,7},{7,6},{8,9},{9,8},{10,11... | collective-permute-start | bytes 786440 | tf_op jit(solution)/shard_map/got0/ppermute | solution.py:64
  36.7 0.6 %collective-permute-done.16 = bf16[16,2048]{1,0:T(8,128)(2,1)S(1)} collective-permute-done((bf16[16,2048]{1,0:T(8,128)(2,1)S(1)}, bf16[16,2048]{1,0:T(8,128)(2,1)S(1)}, u32[]{:S(2)}, u32[]{:S(2)}) %collective-permute-start.16) | collective-permute-done | bytes 65568 | tf_op jit(solution)/shard_map/cross_pxa/ppermute | solution.py:64
  37.4 1.9 %shard_map.86 = (bf16[128,768]{1,0:T(8,128)(2,1)S(1)}, f32[128,768]{1,0:T(8,128)S(1)}) custom-call(f32[8,256]{1,0:T(8,128)S(1)} %get-tuple-element.30.weight_ref, bf16[1024,4096]{1,0:T(8,128)(2,1)S(1)} %get-tuple-element.31.train_ref, bf16[32,4096]{1,0:T(8,128)(2,1)S(1)} %collective-permute-done.2.refs_0_, ...), custom_call_target="tpu_custom_call" | custom-call | tf_op jit(solution)/shard_map/pallas_call | solution.py:221
  39.3 0.7 %collective-permute-start.21 = (bf16[128,768]{1,0:T(8,128)(2,1)S(1)}, bf16[128,768]{1,0:T(8,128)(2,1)S(1)}, u32[]{:S(2)}, u32[]{:S(2)}) collective-permute-start(bf16[128,768]{1,0:T(8,128)(2,1)S(1)} %get-tuple-element.44), channel_id=1, source_target_pairs={{0,1},{1,0},{2,3},{3,2},{4,5},{5,4},{6,7},{7,6},{8,9},{9,8},{10,11... | collective-permute-start | bytes 589832 | tf_op jit(solution)/shard_map/got1/ppermute | solution.py:64
  40.0 0.8 %shard_map.87 = (bf16[128,256]{1,0:T(8,128)(2,1)S(1)}, f32[128,256]{1,0:T(8,128)S(1)}) custom-call(f32[8,256]{1,0:T(8,128)S(1)} %get-tuple-element.30.weight_ref, bf16[1024,4096]{1,0:T(8,128)(2,1)S(1)} %get-tuple-element.31.train_ref, bf16[32,4096]{1,0:T(8,128)(2,1)S(1)} %collective-permute-done.2.refs_0_, ...), custom_call_target="tpu_custom_call" | custom-call | tf_op jit(solution)/shard_map/pallas_call | solution.py:221
  40.8 1.2 %collective-permute-done.19.refs_1_ = bf16[128,1024]{1,0:T(8,128)(2,1)S(1)} collective-permute-done((bf16[128,1024]{1,0:T(8,128)(2,1)S(1)}, bf16[128,1024]{1,0:T(8,128)(2,1)S(1)}, u32[]{:S(2)}, u32[]{:S(2)}) %collective-permute-start.19) | collective-permute-done | bytes 262176 | tf_op jit(solution)/shard_map/got0/ppermute | solution.py:64
  42.0 1.9 %collective-permute-start.20 = (bf16[128,256]{1,0:T(8,128)(2,1)S(1)}, bf16[128,256]{1,0:T(8,128)(2,1)S(1)}, u32[]{:S(2)}, u32[]{:S(2)}) collective-permute-start(bf16[128,256]{1,0:T(8,128)(2,1)S(1)} %get-tuple-element.48), channel_id=1, source_target_pairs={{0,1},{1,0},{2,3},{3,2},{4,5},{5,4},{6,7},{7,6},{8,9},{9,8},{10,11... | collective-permute-start | bytes 196616 | tf_op jit(solution)/shard_map/got2/ppermute | solution.py:64
  44.0 3.1 %collective-permute-done.21.refs_3_ = bf16[128,768]{1,0:T(8,128)(2,1)S(1)} collective-permute-done((bf16[128,768]{1,0:T(8,128)(2,1)S(1)}, bf16[128,768]{1,0:T(8,128)(2,1)S(1)}, u32[]{:S(2)}, u32[]{:S(2)}) %collective-permute-start.21) | collective-permute-done | bytes 196640 | tf_op jit(solution)/shard_map/got1/ppermute | solution.py:64
  47.1 1.1 %shard_map.88.refs_2_ = f32[256,1024]{1,0:T(8,128)} custom-call(s32[1,1024]{1,0:T(1,128)S(1)} %bitcast.6, s32[256,1]{1,0:T(8,128)S(1)} %copy.11.query_ids, f32[128,1024]{1,0:T(8,128)S(1)} %get-tuple-element.49.refs_0_, bf16[128,1024]{1,0:T(8,128)(2,1)S(1)} %collective-permute-done.19.refs_1_, f32[128,768]{1,0:T(8,128)S(1)} %get-tuple-element.50.refs_2_, ...), custom_call_target="tpu_custom_call" | custom-call | tf_op jit(solution)/shard_map/pallas_call | solution.py:282
  48.2 0.8 %shard_map.89 = f32[256,1024]{1,0:T(8,128)} custom-call(s32[1,1024]{1,0:T(1,128)S(1)} %bitcast.7, s32[256,1]{1,0:T(8,128)S(1)} %copy.11.query_ids, f32[128,256]{1,0:T(8,128)S(1)} %get-tuple-element.46.refs_0_, bf16[128,256]{1,0:T(8,128)(2,1)S(1)} %collective-permute-done.20.refs_1_, f32[256,1024]{1,0:T(8,128)} %shard_map.88.refs_2_), custom_call_target="tpu_custom_call", output_to_operand_aliasing={{}: (4, {})} | custom-call | tf_op jit(solution)/shard_map/pallas_call | solution.py:282
  (41 shorter events, 3.4 us)
Async XLA Ops:
  2.8 11.1 %collective-permute-start.1 = (bf16[32,4096]{1,0:T(8,128)(2,1)S(1)}, bf16[32,4096]{1,0:T(8,128)(2,1)S(1)}, u32[]{:S(2)}, u32[]{:S(2)}) collective-permute-start(bf16[32,4096]{1,0:T(8,128)(2,1)S(1)} %get-tuple-element.32.refs_0_), channel_id=1, source_target_pairs={{0,4},{1,5},{2,6},{3,7},{4,0},{5,1},{6,2},{7,3},{8,12},{9,13},{10,... | collective-permute-start | bytes 786440 | tf_op jit(solution)/shard_map/near/ppermute | solution.py:64
  5.9 14.2 %collective-permute-start = (bf16[32,4096]{1,0:T(8,128)(2,1)S(1)}, bf16[32,4096]{1,0:T(8,128)(2,1)S(1)}, u32[]{:S(2)}, u32[]{:S(2)}) collective-permute-start(bf16[32,4096]{1,0:T(8,128)(2,1)S(1)} %get-tuple-element.32.refs_0_), channel_id=1, source_target_pairs={{0,12},{1,13},{2,14},{3,15},{4,8},{5,9},{6,10},{7,11},{8,4},{9,5},... | collective-permute-start | bytes 786440 | tf_op jit(solution)/shard_map/far/ppermute | solution.py:64
  13.3 8.9 %collective-permute-start.9 = (bf16[32,4096]{1,0:T(8,128)(2,1)S(1)}, bf16[32,4096]{1,0:T(8,128)(2,1)S(1)}, u32[]{:S(2)}, u32[]{:S(2)}) collective-permute-start(bf16[32,4096]{1,0:T(8,128)(2,1)S(1)} %get-tuple-element.35.refs_2_), channel_id=1, source_target_pairs={{0,2},{1,3},{2,0},{3,1},{4,6},{5,7},{6,4},{7,5},{8,10},{9,11},{10,... | collective-permute-start | bytes 786440 | tf_op jit(solution)/shard_map/rest_x/ppermute | solution.py:64
  13.4 8.8 %collective-permute-start.8 = (bf16[32,4096]{1,0:T(8,128)(2,1)S(1)}, bf16[32,4096]{1,0:T(8,128)(2,1)S(1)}, u32[]{:S(2)}, u32[]{:S(2)}) collective-permute-start(bf16[32,4096]{1,0:T(8,128)(2,1)S(1)} %get-tuple-element.32.refs_0_), channel_id=1, source_target_pairs={{0,2},{1,3},{2,0},{3,1},{4,6},{5,7},{6,4},{7,5},{8,10},{9,11},{10,... | collective-permute-start | bytes 786440 | tf_op jit(solution)/shard_map/mine_x/ppermute | solution.py:64
  13.9 11.2 %collective-permute-start.7 = (bf16[32,4096]{1,0:T(8,128)(2,1)S(1)}, bf16[32,4096]{1,0:T(8,128)(2,1)S(1)}, u32[]{:S(2)}, u32[]{:S(2)}) collective-permute-start(bf16[32,4096]{1,0:T(8,128)(2,1)S(1)} %collective-permute-done.1.refs_0_), channel_id=1, source_target_pairs={{0,16},{1,17},{2,18},{3,19},{4,20},{5,21},{6,22},{7,23},{8,24},{9,... | collective-permute-start | bytes 786440 | tf_op jit(solution)/shard_map/near_p/ppermute | solution.py:64
  20.1 7.7 %collective-permute-start.11 = (bf16[32,4096]{1,0:T(8,128)(2,1)S(1)}, bf16[32,4096]{1,0:T(8,128)(2,1)S(1)}, u32[]{:S(2)}, u32[]{:S(2)}) collective-permute-start(bf16[32,4096]{1,0:T(8,128)(2,1)S(1)} %collective-permute-done.refs_4_), channel_id=1, source_target_pairs={{0,16},{1,17},{2,18},{3,19},{4,20},{5,21},{6,22},{7,23},{8,24},{9,... | collective-permute-start | bytes 786440 | tf_op jit(solution)/shard_map/far_p/ppermute | solution.py:64
  21.6 7.5 %collective-permute-start.2 = (bf16[32,4096]{1,0:T(8,128)(2,1)S(1)}, bf16[32,4096]{1,0:T(8,128)(2,1)S(1)}, u32[]{:S(2)}, u32[]{:S(2)}) collective-permute-start(bf16[32,4096]{1,0:T(8,128)(2,1)S(1)} %collective-permute-done.refs_4_), channel_id=1, source_target_pairs={{0,4},{1,5},{2,6},{3,7},{4,0},{5,1},{6,2},{7,3},{8,12},{9,13},{10,... | collective-permute-start | bytes 786440 | tf_op jit(solution)/shard_map/cross/ppermute | solution.py:64
  22.2 5.7 %collective-permute-start.4 = (bf16[32,4096]{1,0:T(8,128)(2,1)S(1)}, bf16[32,4096]{1,0:T(8,128)(2,1)S(1)}, u32[]{:S(2)}, u32[]{:S(2)}) collective-permute-start(bf16[32,4096]{1,0:T(8,128)(2,1)S(1)} %collective-permute-done.refs_4_), channel_id=1, source_target_pairs={{0,2},{1,3},{2,0},{3,1},{4,6},{5,7},{6,4},{7,5},{8,10},{9,11},{10,... | collective-permute-start | bytes 786440 | tf_op jit(solution)/shard_map/far_x/ppermute | solution.py:64
  22.2 6.2 %collective-permute-start.5 = (bf16[32,4096]{1,0:T(8,128)(2,1)S(1)}, bf16[32,4096]{1,0:T(8,128)(2,1)S(1)}, u32[]{:S(2)}, u32[]{:S(2)}) collective-permute-start(bf16[32,4096]{1,0:T(8,128)(2,1)S(1)} %collective-permute-done.1.refs_0_), channel_id=1, source_target_pairs={{0,2},{1,3},{2,0},{3,1},{4,6},{5,7},{6,4},{7,5},{8,10},{9,11},{10,... | collective-permute-start | bytes 786440 | tf_op jit(solution)/shard_map/near_x/ppermute | solution.py:64
  25.1 5.5 %collective-permute-start.10 = (bf16[32,4096]{1,0:T(8,128)(2,1)S(1)}, bf16[32,4096]{1,0:T(8,128)(2,1)S(1)}, u32[]{:S(2)}, u32[]{:S(2)}) collective-permute-start(bf16[32,4096]{1,0:T(8,128)(2,1)S(1)} %collective-permute-done.7.refs_2_), channel_id=1, source_target_pairs={{0,2},{1,3},{2,0},{3,1},{4,6},{5,7},{6,4},{7,5},{8,10},{9,11},{10,... | collective-permute-start | bytes 786440 | tf_op jit(solution)/shard_map/near_px/ppermute | solution.py:64
  27.8 2.8 %collective-permute-start.13 = (bf16[16,4096]{1,0:T(8,128)(2,1)S(1)}, bf16[16,4096]{1,0:T(8,128)(2,1)S(1)}, u32[]{:S(2)}, u32[]{:S(2)}) collective-permute-start(bf16[16,4096]{1,0:T(8,128)(2,1)S(1)} %get-tuple-element.41), channel_id=1, source_target_pairs={{0,2},{1,3},{2,0},{3,1},{4,6},{5,7},{6,4},{7,5},{8,10},{9,11},{10,... | collective-permute-start | bytes 393224 | tf_op jit(solution)/shard_map/far_px1/ppermute | solution.py:64
  27.9 2.8 %collective-permute-start.12 = (bf16[16,4096]{1,0:T(8,128)(2,1)S(1)}, bf16[16,4096]{1,0:T(8,128)(2,1)S(1)}, u32[]{:S(2)}, u32[]{:S(2)}) collective-permute-start(bf16[16,4096]{1,0:T(8,128)(2,1)S(1)} %get-tuple-element.52), channel_id=1, source_target_pairs={{0,2},{1,3},{2,0},{3,1},{4,6},{5,7},{6,4},{7,5},{8,10},{9,11},{10,... | collective-permute-start | bytes 393224 | tf_op jit(solution)/shard_map/far_px0/ppermute | solution.py:64
  28.4 6.4 %collective-permute-start.14 = (bf16[16,4096]{1,0:T(8,128)(2,1)S(1)}, bf16[16,4096]{1,0:T(8,128)(2,1)S(1)}, u32[]{:S(2)}, u32[]{:S(2)}) collective-permute-start(bf16[16,4096]{1,0:T(8,128)(2,1)S(1)} %get-tuple-element.41), channel_id=1, source_target_pairs={{0,4},{1,5},{2,6},{3,7},{4,0},{5,1},{6,2},{7,3},{8,12},{9,13},{10,... | collective-permute-start | bytes 393224 | tf_op jit(solution)/shard_map/cross_pb/ppermute | solution.py:64
  29.1 6.3 %collective-permute-start.6 = (bf16[16,4096]{1,0:T(8,128)(2,1)S(1)}, bf16[16,4096]{1,0:T(8,128)(2,1)S(1)}, u32[]{:S(2)}, u32[]{:S(2)}) collective-permute-start(bf16[16,4096]{1,0:T(8,128)(2,1)S(1)} %slice.13), channel_id=1, source_target_pairs={{0,16},{1,17},{2,18},{3,19},{4,20},{5,21},{6,22},{7,23},{8,24},{9,... | collective-permute-start | bytes 393224 | tf_op jit(solution)/shard_map/cross_pa/ppermute | solution.py:64
  30.7 6.7 %collective-permute-start.3 = (bf16[32,4096]{1,0:T(8,128)(2,1)S(1)}, bf16[32,4096]{1,0:T(8,128)(2,1)S(1)}, u32[]{:S(2)}, u32[]{:S(2)}) collective-permute-start(bf16[32,4096]{1,0:T(8,128)(2,1)S(1)} %collective-permute-done.2.refs_0_), channel_id=1, source_target_pairs={{0,2},{1,3},{2,0},{3,1},{4,6},{5,7},{6,4},{7,5},{8,10},{9,11},{10,... | collective-permute-start | bytes 786440 | tf_op jit(solution)/shard_map/cross_x/ppermute | solution.py:64
  33.2 8.8 %collective-permute-start.19 = (bf16[128,1024]{1,0:T(8,128)(2,1)S(1)}, bf16[128,1024]{1,0:T(8,128)(2,1)S(1)}, u32[]{:S(2)}, u32[]{:S(2)}) collective-permute-start(bf16[128,1024]{1,0:T(8,128)(2,1)S(1)} %get-tuple-element.39), channel_id=1, source_target_pairs={{0,1},{1,0},{2,3},{3,2},{4,5},{5,4},{6,7},{7,6},{8,9},{9,8},{10,11... | collective-permute-start | bytes 786440 | tf_op jit(solution)/shard_map/got0/ppermute | solution.py:64
  34.8 1.3 %collective-permute-start.17 = (bf16[16,2048]{1,0:T(8,128)(2,1)S(1)}, bf16[16,2048]{1,0:T(8,128)(2,1)S(1)}, u32[]{:S(2)}, u32[]{:S(2)}) collective-permute-start(bf16[16,2048]{1,0:T(8,128)(2,1)S(1)} %get-tuple-element.54), channel_id=1, source_target_pairs={{0,2},{1,3},{2,0},{3,1},{4,6},{5,7},{6,4},{7,5},{8,10},{9,11},{10,... | collective-permute-start | bytes 196616 | tf_op jit(solution)/shard_map/cross_pxb/ppermute | solution.py:64
  35.1 1.7 %collective-permute-start.18 = (bf16[16,2048]{1,0:T(8,128)(2,1)S(1)}, bf16[16,2048]{1,0:T(8,128)(2,1)S(1)}, u32[]{:S(2)}, u32[]{:S(2)}) collective-permute-start(bf16[16,2048]{1,0:T(8,128)(2,1)S(1)} %get-tuple-element.53), channel_id=1, source_target_pairs={{0,2},{1,3},{2,0},{3,1},{4,6},{5,7},{6,4},{7,5},{8,10},{9,11},{10,... | collective-permute-start | bytes 196616 | tf_op jit(solution)/shard_map/cross_pxb/ppermute | solution.py:64
  35.4 1.3 %collective-permute-start.15 = (bf16[16,2048]{1,0:T(8,128)(2,1)S(1)}, bf16[16,2048]{1,0:T(8,128)(2,1)S(1)}, u32[]{:S(2)}, u32[]{:S(2)}) collective-permute-start(bf16[16,2048]{1,0:T(8,128)(2,1)S(1)} %get-tuple-element.56), channel_id=1, source_target_pairs={{0,2},{1,3},{2,0},{3,1},{4,6},{5,7},{6,4},{7,5},{8,10},{9,11},{10,... | collective-permute-start | bytes 196616 | tf_op jit(solution)/shard_map/cross_pxa/ppermute | solution.py:64
  36.1 1.3 %collective-permute-start.16 = (bf16[16,2048]{1,0:T(8,128)(2,1)S(1)}, bf16[16,2048]{1,0:T(8,128)(2,1)S(1)}, u32[]{:S(2)}, u32[]{:S(2)}) collective-permute-start(bf16[16,2048]{1,0:T(8,128)(2,1)S(1)} %get-tuple-element.55), channel_id=1, source_target_pairs={{0,2},{1,3},{2,0},{3,1},{4,6},{5,7},{6,4},{7,5},{8,10},{9,11},{10,... | collective-permute-start | bytes 196616 | tf_op jit(solution)/shard_map/cross_pxa/ppermute | solution.py:64
  37.4 6.5 %copy-start.1 = (s32[256]{0:T(256)S(1)}, s32[256]{0:T(256)}, u32[]{:S(2)}) copy-start(s32[256]{0:T(256)} %param.15) | copy-start | bytes 3076
  37.4 9.7 %copy-start = (s32[1024]{0:T(1024)S(1)}, s32[1024]{0:T(1024)}, u32[]{:S(2)}) copy-start(s32[1024]{0:T(1024)} %param.14) | copy-start | bytes 12292
  39.3 7.8 %collective-permute-start.21 = (bf16[128,768]{1,0:T(8,128)(2,1)S(1)}, bf16[128,768]{1,0:T(8,128)(2,1)S(1)}, u32[]{:S(2)}, u32[]{:S(2)}) collective-permute-start(bf16[128,768]{1,0:T(8,128)(2,1)S(1)} %get-tuple-element.44), channel_id=1, source_target_pairs={{0,1},{1,0},{2,3},{3,2},{4,5},{5,4},{6,7},{7,6},{8,9},{9,8},{10,11... | collective-permute-start | bytes 589832 | tf_op jit(solution)/shard_map/got1/ppermute | solution.py:64
  42.0 6.2 %collective-permute-start.20 = (bf16[128,256]{1,0:T(8,128)(2,1)S(1)}, bf16[128,256]{1,0:T(8,128)(2,1)S(1)}, u32[]{:S(2)}, u32[]{:S(2)}) collective-permute-start(bf16[128,256]{1,0:T(8,128)(2,1)S(1)} %get-tuple-element.48), channel_id=1, source_target_pairs={{0,1},{1,0},{2,3},{3,2},{4,5},{5,4},{6,7},{7,6},{8,9},{9,8},{10,11... | collective-permute-start | bytes 196616 | tf_op jit(solution)/shard_map/got2/ppermute | solution.py:64

commit v14 on v13

--- a/solution.py
+++ b/solution.py
@@ -333,56 +333,59 @@
     def rows_of(*pieces):
         return [(piece, ((0, piece.shape[0]),)) for piece in pieces]
 
-    mine_x = to_core(mine, "mine_x")
+    mine_x = to_core(after(mine, rest), "mine_x")
     rest_x = to_core(rest, "rest_x")
+    near = after(near, rest)
     near_x = to_core(near, "near_x")
     near_p = to_part(near, "near_p")
     far = after(far, near)
     cross = to_near(far, "cross")
     far_p = to_part(far, "far_p")
-    far_x = to_core(far, "far_x")
-    rest_x = after(rest_x, far)
+    far_x = to_core(after(far, rest_x), "far_x")
+    mine_x = after(mine_x, far)
     (early0,) = score(rows_of(mine, mine_x, rest, rest_x), stored=128)
+    send0, keep0 = score(rows_of(far, far_x), early=[(early0, 0, 64)])
+    got0 = to_layer(send0, "got0")
+
     near_p = after(near_p, early0)
     near_px = to_core(near_p, "near_px")
-
-    far_px0 = to_core(far_p[:CHUNK], "far_px0")
-    far_px1 = to_core(far_p[CHUNK:], "far_px1")
-    cross_pa = to_part(after(cross[:CHUNK], far_x, near_x), "cross_pa")
-    cross_pb = to_near(after(far_p[CHUNK:], far_x, near_x), "cross_pb")
+    far_p, cross = after(far_p, near_px, send0), after(cross, send0)
+    far_px = to_core(far_p, "far_px")
+    cross_pa = to_part(cross[:CHUNK], "cross_pa")
+    cross_pb = to_near(far_p[CHUNK:], "cross_pb")
     cross_x = to_core(cross, "cross_x")
-    far_px1 = after(far_px1, cross)
-    early1, send0, keep0 = score(
-        rows_of(near, near_x, near_p, near_px, far, far_x, far_p, far_px0, far_px1),
+    early1, send1, keep1 = score(
+        rows_of(near, near_x, near_p, near_px, far_p, far_px, cross, cross_x),
         stored=128,
-        early=[(early0, 0, 128)],
-    )
-    got0 = to_layer(send0, "got0")
-    cross_pa, cross_pb = after(cross_pa, send0), after(cross_pb, send0)
-    def by_columns(piece, name):
-        parts = [to_core(part, name) for part in jnp.split(piece, 2, axis=1)]
-        return jnp.concatenate(parts, axis=1)
-
-    cross_pxa, cross_pxb = by_columns(cross_pa, "cross_pxa"), by_columns(cross_pb, "cross_pxb")
-    last = rows_of(cross, cross_x, cross_pa, cross_pb, cross_pxa, cross_pxb)
+        early=[(early0, 64, 64), (None, 0, 64)],
+    )
+    got1 = to_layer(send1, "got1")
+    cross_pa, cross_pb = after(cross_pa, send1, got0), after(cross_pb, send1, got0)
+    cross_pxa = to_core(cross_pa, "cross_pxa")
+    cross_pxb = to_core(cross_pb, "cross_pxb")
+    last = rows_of(cross_pa, cross_pb, cross_pxa, cross_pxb)
     n = train.shape[0]
-    cut = n * 3 // 4
-    send1, keep1 = score(last, early=[(early1, 0, 128)], columns=(0, cut))
-    got1 = to_layer(send1, "got1")
-    early1 = after(early1, send1)
-    send2, keep2 = score(last, early=[(early1, 0, 128)], columns=(cut, n))
-    send2 = after(send2, got0)
+    cut = n // 2
+    send2, keep2 = score(last, early=[(early1, 64, 64)], columns=(0, cut))
     got2 = to_layer(send2, "got2")
+    early1 = after(early1, send2)
+    send3, keep3 = score(last, early=[(early1, 64, 64)], columns=(cut, n))
+    send3 = after(send3, got1)
+    got3 = to_layer(send3, "got3")
 
     train_ids, query_ids = train_ids[None, :], query_ids[:, None]
     most = call_final(
         train_ids,
         query_ids,
         [keep0, got0, keep1, got1],
-        ((0, 0, 1, 0, 0), (1, 0, 1, 64, 0), (2, 2, 3, 0, 0), (3, 2, 3, 64, 0)),
+        ((0, 0, 1, 0, 0), (1, 2, 3, 0, 0), (2, 2, 3, 64, 0)),
     )
     return call_final(
-        train_ids, query_ids, [keep2, got2], ((2, 0, 1, 0, cut), (3, 0, 1, 64, cut)), most
+        train_ids,
+        query_ids,
+        [keep2, got2, keep3, got3],
+        ((3, 0, 1, 0, 0), (3, 2, 3, 0, cut)),
+        most,
     )
 
 

time: 49.2 us -> 47.8 us (0.972)
  starting transfers between devices: 18.4 us -> 15.5 us
  Pallas kernels: 16.6 us -> 18.9 us
  waiting for transfers between devices: 13 us -> 12.3 us
    ppermute x22 -> x20, starting transfers between devices: 18.4 us -> 15.5 us  [permute(): return lax.ppermute(value, AXES, pairs)]
    pallas_call x6 -> x7, Pallas kernels: 14.7 us -> 17 us  [kernel_call(): pl.pallas_call(kernel, out_shape=outs, in_specs=specs or [VMEM] * len(inp...]
    ppermute x22 -> x20, waiting for transfers between devices: 13 us -> 12.3 us  [permute(): return lax.ppermute(value, AXES, pairs)]
  transfers between devices with their start and end apart: 22 -> 20, of which waited for: 7 -> 8; matrix products, arithmetic and copies ran while one was open for 0% -> 0% of each run, Pallas kernels for 26% -> 32%
where the time goes in v14:
time: 47.8 us; the launch traced here: 47.6 us
  Pallas kernels  18.9 us (40%)
  starting transfers between devices  15.5 us (32%)
  waiting for transfers between devices  12.3 us (26%)
  between operations  0.8 us (2%)
    pallas_call x7, Pallas kernels, kernel_call(): pl.pallas_call(kernel, out_shape=outs, in_specs=specs or [VMEM] * len(inp...  17 us
    ppermute x20, starting transfers between devices, permute(): return lax.ppermute(value, AXES, pairs)  15.5 us
    ppermute x20, waiting for transfers between devices, permute(): return lax.ppermute(value, AXES, pairs)  12.3 us
    pallas_call x2, Pallas kernels, call_final(): pl.pallas_call(functools.partial(final_kernel, groups=groups, n_given=len...  1.85 us
  transfers between devices with their start and end apart: 20, of which 8 were waited for; matrix products, arithmetic and copies ran while one was open for 0% of the time, Pallas kernels for 32%

profile of v14, /device:TPU:0, one launch (start us, length us, event | category | flops | bytes accessed | tf_op | source)
XLA Modules:
  0.0 47.6 jit_solution(7602408887538277064)
XLA Ops:
  0.0 2.8 %shard_map.82 = (bf16[32,4096]{1,0:T(8,128)(2,1)S(1)}, bf16[2,256,256]{2,1,0:T(8,128)(2,1)S(1)}, bf16[2,256,512]{2,1,0:T(8,128)(2,1)S(1)}) custom-call(bf16[64,4096]{1,0:T(8,128)(2,1)} %bitcast.9, f32[64,64]{1,0:T(8,128)} %bitcast.11, f32[64,64]{1,0:T(8,128)} %bitcast.12), custom_call_target="tpu_custom_call" | custom-call | tf_op jit(solution)/shard_map/pallas_call | solution.py:221
  2.8 3.1 %collective-permute-start.1 = (bf16[32,4096]{1,0:T(8,128)(2,1)S(1)}, bf16[32,4096]{1,0:T(8,128)(2,1)S(1)}, u32[]{:S(2)}, u32[]{:S(2)}) collective-permute-start(bf16[32,4096]{1,0:T(8,128)(2,1)S(1)} %get-tuple-element.41.refs_0_), channel_id=1, source_target_pairs={{0,4},{1,5},{2,6},{3,7},{4,0},{5,1},{6,2},{7,3},{8,12},{9,13},{10,... | collective-permute-start | bytes 786440 | tf_op jit(solution)/shard_map/near/ppermute | solution.py:64
  5.9 2.5 %collective-permute-start = (bf16[32,4096]{1,0:T(8,128)(2,1)S(1)}, bf16[32,4096]{1,0:T(8,128)(2,1)S(1)}, u32[]{:S(2)}, u32[]{:S(2)}) collective-permute-start(bf16[32,4096]{1,0:T(8,128)(2,1)S(1)} %get-tuple-element.41.refs_0_), channel_id=1, source_target_pairs={{0,12},{1,13},{2,14},{3,15},{4,8},{5,9},{6,10},{7,11},{8,4},{9,5},... | collective-permute-start | bytes 786440 | tf_op jit(solution)/shard_map/far/ppermute | solution.py:64
  9.0 4.3 %shard_map.83 = (bf16[32,4096]{1,0:T(8,128)(2,1)S(1)}, bf16[1024,4096]{1,0:T(8,128)(2,1)S(1)}, f32[8,256]{1,0:T(8,128)S(1)}) custom-call(f32[2]{0:T(128)} %weight_ref.1, s32[1]{0:T(128)S(6)} %copy.13.layer_ref, bf16[64,4096]{1,0:T(8,128)(2,1)} %bitcast.10, bf16[1024,4096]{1,0:T(8,128)(2,1)} %bitcast.8, bf16[2,256,256]{2,1,0:T(8,128)(2,1)S(1)} %get-tuple-element.32.lefts_ref, ...), custom_call_target="tpu_custom_call" | custom-call | tf_op jit(solution)/shard_map/pallas_call | solution.py:221
  13.9 1.5 %collective-permute-start.8 = (bf16[32,4096]{1,0:T(8,128)(2,1)S(1)}, bf16[32,4096]{1,0:T(8,128)(2,1)S(1)}, u32[]{:S(2)}, u32[]{:S(2)}) collective-permute-start(bf16[32,4096]{1,0:T(8,128)(2,1)S(1)} %collective-permute-done.1.refs_0_), channel_id=1, source_target_pairs={{0,16},{1,17},{2,18},{3,19},{4,20},{5,21},{6,22},{7,23},{8,24},{9,... | collective-permute-start | bytes 786440 | tf_op jit(solution)/shard_map/near_p/ppermute | solution.py:64
  15.4 4.7 %collective-permute-done.refs_0_ = bf16[32,4096]{1,0:T(8,128)(2,1)S(1)} collective-permute-done((bf16[32,4096]{1,0:T(8,128)(2,1)S(1)}, bf16[32,4096]{1,0:T(8,128)(2,1)S(1)}, u32[]{:S(2)}, u32[]{:S(2)}) %collective-permute-start) | collective-permute-done | bytes 262176 | tf_op jit(solution)/shard_map/far/ppermute | solution.py:64
  20.1 1.5 %collective-permute-start.10 = (bf16[32,4096]{1,0:T(8,128)(2,1)S(1)}, bf16[32,4096]{1,0:T(8,128)(2,1)S(1)}, u32[]{:S(2)}, u32[]{:S(2)}) collective-permute-start(bf16[32,4096]{1,0:T(8,128)(2,1)S(1)} %collective-permute-done.refs_0_), channel_id=1, source_target_pairs={{0,16},{1,17},{2,18},{3,19},{4,20},{5,21},{6,22},{7,23},{8,24},{9,... | collective-permute-start | bytes 786440 | tf_op jit(solution)/shard_map/far_p/ppermute | solution.py:64
  22.2 2.4 %shard_map.84.refs_2_.refs_8_ = f32[128,1024]{1,0:T(8,128)S(1)} custom-call(f32[8,256]{1,0:T(8,128)S(1)} %get-tuple-element.34.weight_ref, bf16[1024,4096]{1,0:T(8,128)(2,1)S(1)} %get-tuple-element.35.train_ref, bf16[32,4096]{1,0:T(8,128)(2,1)S(1)} %get-tuple-element.41.refs_0_, bf16[32,4096]{1,0:T(8,128)(2,1)S(1)} %collective-permute-done.5.refs_1_, ...), custom_call_target="tpu_custom_call" | custom-call | tf_op jit(solution)/shard_map/pallas_call | solution.py:221
  25.3 2.4 %shard_map.85 = (bf16[64,1024]{1,0:T(8,128)(2,1)S(1)}, f32[64,1024]{1,0:T(8,128)S(1)}) custom-call(f32[8,256]{1,0:T(8,128)S(1)} %get-tuple-element.34.weight_ref, bf16[1024,4096]{1,0:T(8,128)(2,1)S(1)} %get-tuple-element.35.train_ref, bf16[32,4096]{1,0:T(8,128)(2,1)S(1)} %collective-permute-done.refs_0_, ...), custom_call_target="tpu_custom_call" | custom-call | tf_op jit(solution)/shard_map/pallas_call | solution.py:221
  27.7 0.8 %collective-permute-done.2.refs_6_ = bf16[32,4096]{1,0:T(8,128)(2,1)S(1)} collective-permute-done((bf16[32,4096]{1,0:T(8,128)(2,1)S(1)}, bf16[32,4096]{1,0:T(8,128)(2,1)S(1)}, u32[]{:S(2)}, u32[]{:S(2)}) %collective-permute-start.2) | collective-permute-done | bytes 262176 | tf_op jit(solution)/shard_map/cross/ppermute | solution.py:64
  29.0 1.5 %collective-permute-start.13 = (bf16[64,1024]{1,0:T(8,128)(2,1)S(1)}, bf16[64,1024]{1,0:T(8,128)(2,1)S(1)}, u32[]{:S(2)}, u32[]{:S(2)}) collective-permute-start(bf16[64,1024]{1,0:T(8,128)(2,1)S(1)} %get-tuple-element.43), channel_id=1, source_target_pairs={{0,1},{1,0},{2,3},{3,2},{4,5},{5,4},{6,7},{7,6},{8,9},{9,8},{10,11... | collective-permute-start | bytes 393224 | tf_op jit(solution)/shard_map/got0/ppermute | solution.py:64
  30.5 0.9 %collective-permute-start.14 = (bf16[16,4096]{1,0:T(8,128)(2,1)S(1)}, bf16[16,4096]{1,0:T(8,128)(2,1)S(1)}, u32[]{:S(2)}, u32[]{:S(2)}) collective-permute-start(bf16[16,4096]{1,0:T(8,128)(2,1)S(1)} %slice.7), channel_id=1, source_target_pairs={{0,4},{1,5},{2,6},{3,7},{4,0},{5,1},{6,2},{7,3},{8,12},{9,13},{10,... | collective-permute-start | bytes 393224 | tf_op jit(solution)/shard_map/cross_pb/ppermute | solution.py:64
  31.4 0.6 %collective-permute-start.6 = (bf16[16,4096]{1,0:T(8,128)(2,1)S(1)}, bf16[16,4096]{1,0:T(8,128)(2,1)S(1)}, u32[]{:S(2)}, u32[]{:S(2)}) collective-permute-start(bf16[16,4096]{1,0:T(8,128)(2,1)S(1)} %slice.6), channel_id=1, source_target_pairs={{0,16},{1,17},{2,18},{3,19},{4,20},{5,21},{6,22},{7,23},{8,24},{9,... | collective-permute-start | bytes 393224 | tf_op jit(solution)/shard_map/cross_pa/ppermute | solution.py:64
  32.0 2.5 %shard_map.86 = (f32[128,1024]{1,0:T(8,128)S(1)}, bf16[128,1024]{1,0:T(8,128)(2,1)S(1)}, f32[128,1024]{1,0:T(8,128)S(1)}) custom-call(f32[8,256]{1,0:T(8,128)S(1)} %get-tuple-element.34.weight_ref, bf16[1024,4096]{1,0:T(8,128)(2,1)S(1)} %get-tuple-element.35.train_ref, bf16[32,4096]{1,0:T(8,128)(2,1)S(1)} %collective-permute-done.1.refs_0_, ...), custom_call_target="tpu_custom_call" | custom-call | tf_op jit(solution)/shard_map/pallas_call | solution.py:221
  35.1 0.7 %collective-permute-done.14.refs_1_ = bf16[16,4096]{1,0:T(8,128)(2,1)S(1)} collective-permute-done((bf16[16,4096]{1,0:T(8,128)(2,1)S(1)}, bf16[16,4096]{1,0:T(8,128)(2,1)S(1)}, u32[]{:S(2)}, u32[]{:S(2)}) %collective-permute-start.14) | collective-permute-done | bytes 131104 | tf_op jit(solution)/shard_map/cross_pb/ppermute | solution.py:64
  35.8 0.9 %collective-permute-done.6.refs_0_ = bf16[16,4096]{1,0:T(8,128)(2,1)S(1)} collective-permute-done((bf16[16,4096]{1,0:T(8,128)(2,1)S(1)}, bf16[16,4096]{1,0:T(8,128)(2,1)S(1)}, u32[]{:S(2)}, u32[]{:S(2)}) %collective-permute-start.6) | collective-permute-done | bytes 131104 | tf_op jit(solution)/shard_map/cross_pa/ppermute | solution.py:64
  37.1 1.0 %collective-permute-done.15.refs_2_ = bf16[16,4096]{1,0:T(8,128)(2,1)S(1)} collective-permute-done((bf16[16,4096]{1,0:T(8,128)(2,1)S(1)}, bf16[16,4096]{1,0:T(8,128)(2,1)S(1)}, u32[]{:S(2)}, u32[]{:S(2)}) %collective-permute-start.15) | collective-permute-done | bytes 131104 | tf_op jit(solution)/shard_map/cross_pxa/ppermute | solution.py:64
  38.1 1.3 %shard_map.87 = (bf16[64,512]{1,0:T(8,128)(2,1)S(1)}, f32[64,512]{1,0:T(8,128)S(1)}) custom-call(f32[8,256]{1,0:T(8,128)S(1)} %get-tuple-element.34.weight_ref, bf16[1024,4096]{1,0:T(8,128)(2,1)S(1)} %get-tuple-element.35.train_ref, bf16[16,4096]{1,0:T(8,128)(2,1)S(1)} %collective-permute-done.6.refs_0_, ...), custom_call_target="tpu_custom_call" | custom-call | tf_op jit(solution)/shard_map/pallas_call | solution.py:221
  39.4 0.6 %collective-permute-start.17 = (bf16[64,512]{1,0:T(8,128)(2,1)S(1)}, bf16[64,512]{1,0:T(8,128)(2,1)S(1)}, u32[]{:S(2)}, u32[]{:S(2)}) collective-permute-start(bf16[64,512]{1,0:T(8,128)(2,1)S(1)} %get-tuple-element.52), channel_id=1, source_target_pairs={{0,1},{1,0},{2,3},{3,2},{4,5},{5,4},{6,7},{7,6},{8,9},{9,8},{10,11... | collective-permute-start | bytes 196616 | tf_op jit(solution)/shard_map/got2/ppermute | solution.py:64
  40.0 1.3 %shard_map.88 = (bf16[64,512]{1,0:T(8,128)(2,1)S(1)}, f32[64,512]{1,0:T(8,128)S(1)}) custom-call(f32[8,256]{1,0:T(8,128)S(1)} %get-tuple-element.34.weight_ref, bf16[1024,4096]{1,0:T(8,128)(2,1)S(1)} %get-tuple-element.35.train_ref, bf16[16,4096]{1,0:T(8,128)(2,1)S(1)} %collective-permute-done.6.refs_0_, ...), custom_call_target="tpu_custom_call" | custom-call | tf_op jit(solution)/shard_map/pallas_call | solution.py:221
  41.3 1.2 %collective-permute-done.18.refs_3_ = bf16[128,1024]{1,0:T(8,128)(2,1)S(1)} collective-permute-done((bf16[128,1024]{1,0:T(8,128)(2,1)S(1)}, bf16[128,1024]{1,0:T(8,128)(2,1)S(1)}, u32[]{:S(2)}, u32[]{:S(2)}) %collective-permute-start.18) | collective-permute-done | bytes 262176 | tf_op jit(solution)/shard_map/got1/ppermute | solution.py:64
  43.1 1.0 %shard_map.89.refs_4_ = f32[256,1024]{1,0:T(8,128)} custom-call(s32[1,1024]{1,0:T(1,128)S(1)} %bitcast.6, s32[256,1]{1,0:T(8,128)S(1)} %copy.11.query_ids, f32[64,1024]{1,0:T(8,128)S(1)} %get-tuple-element.57.refs_0_, bf16[64,1024]{1,0:T(8,128)(2,1)S(1)} %collective-permute-done.13.refs_1_, f32[128,1024]{1,0:T(8,128)S(1)} %get-tuple-element.58.refs_2_, ...), custom_call_target="tpu_custom_call" | custom-call | tf_op jit(solution)/shard_map/pallas_call | solution.py:282
  44.2 2.5 %collective-permute-done.19.refs_3_ = bf16[64,512]{1,0:T(8,128)(2,1)S(1)} collective-permute-done((bf16[64,512]{1,0:T(8,128)(2,1)S(1)}, bf16[64,512]{1,0:T(8,128)(2,1)S(1)}, u32[]{:S(2)}, u32[]{:S(2)}) %collective-permute-start.19) | collective-permute-done | bytes 65568 | tf_op jit(solution)/shard_map/got3/ppermute | solution.py:64
  46.7 0.8 %shard_map.90 = f32[256,1024]{1,0:T(8,128)} custom-call(s32[1,1024]{1,0:T(1,128)S(1)} %bitcast.7, s32[256,1]{1,0:T(8,128)S(1)} %copy.11.query_ids, f32[64,512]{1,0:T(8,128)S(1)} %get-tuple-element.51.refs_0_, bf16[64,512]{1,0:T(8,128)(2,1)S(1)} %collective-permute-done.17.refs_1_, ...), custom_call_target="tpu_custom_call", output_to_operand_aliasing={{}: (6, {})} | custom-call | tf_op jit(solution)/shard_map/pallas_call | solution.py:282
  (32 shorter events, 4.0 us)
Async XLA Ops:
  2.8 11.1 %collective-permute-start.1 = (bf16[32,4096]{1,0:T(8,128)(2,1)S(1)}, bf16[32,4096]{1,0:T(8,128)(2,1)S(1)}, u32[]{:S(2)}, u32[]{:S(2)}) collective-permute-start(bf16[32,4096]{1,0:T(8,128)(2,1)S(1)} %get-tuple-element.41.refs_0_), channel_id=1, source_target_pairs={{0,4},{1,5},{2,6},{3,7},{4,0},{5,1},{6,2},{7,3},{8,12},{9,13},{10,... | collective-permute-start | bytes 786440 | tf_op jit(solution)/shard_map/near/ppermute | solution.py:64
  5.9 14.2 %collective-permute-start = (bf16[32,4096]{1,0:T(8,128)(2,1)S(1)}, bf16[32,4096]{1,0:T(8,128)(2,1)S(1)}, u32[]{:S(2)}, u32[]{:S(2)}) collective-permute-start(bf16[32,4096]{1,0:T(8,128)(2,1)S(1)} %get-tuple-element.41.refs_0_), channel_id=1, source_target_pairs={{0,12},{1,13},{2,14},{3,15},{4,8},{5,9},{6,10},{7,11},{8,4},{9,5},... | collective-permute-start | bytes 786440 | tf_op jit(solution)/shard_map/far/ppermute | solution.py:64
  13.3 8.9 %collective-permute-start.5 = (bf16[32,4096]{1,0:T(8,128)(2,1)S(1)}, bf16[32,4096]{1,0:T(8,128)(2,1)S(1)}, u32[]{:S(2)}, u32[]{:S(2)}) collective-permute-start(bf16[32,4096]{1,0:T(8,128)(2,1)S(1)} %get-tuple-element.41.refs_0_), channel_id=1, source_target_pairs={{0,2},{1,3},{2,0},{3,1},{4,6},{5,7},{6,4},{7,5},{8,10},{9,11},{10,... | collective-permute-start | bytes 786440 | tf_op jit(solution)/shard_map/mine_x/ppermute | solution.py:64
  13.4 8.8 %collective-permute-start.3 = (bf16[32,4096]{1,0:T(8,128)(2,1)S(1)}, bf16[32,4096]{1,0:T(8,128)(2,1)S(1)}, u32[]{:S(2)}, u32[]{:S(2)}) collective-permute-start(bf16[32,4096]{1,0:T(8,128)(2,1)S(1)} %get-tuple-element.37.refs_2_), channel_id=1, source_target_pairs={{0,2},{1,3},{2,0},{3,1},{4,6},{5,7},{6,4},{7,5},{8,10},{9,11},{10,... | collective-permute-start | bytes 786440 | tf_op jit(solution)/shard_map/rest_x/ppermute | solution.py:64
  13.9 10.7 %collective-permute-start.8 = (bf16[32,4096]{1,0:T(8,128)(2,1)S(1)}, bf16[32,4096]{1,0:T(8,128)(2,1)S(1)}, u32[]{:S(2)}, u32[]{:S(2)}) collective-permute-start(bf16[32,4096]{1,0:T(8,128)(2,1)S(1)} %collective-permute-done.1.refs_0_), channel_id=1, source_target_pairs={{0,16},{1,17},{2,18},{3,19},{4,20},{5,21},{6,22},{7,23},{8,24},{9,... | collective-permute-start | bytes 786440 | tf_op jit(solution)/shard_map/near_p/ppermute | solution.py:64
  20.1 8.3 %collective-permute-start.10 = (bf16[32,4096]{1,0:T(8,128)(2,1)S(1)}, bf16[32,4096]{1,0:T(8,128)(2,1)S(1)}, u32[]{:S(2)}, u32[]{:S(2)}) collective-permute-start(bf16[32,4096]{1,0:T(8,128)(2,1)S(1)} %collective-permute-done.refs_0_), channel_id=1, source_target_pairs={{0,16},{1,17},{2,18},{3,19},{4,20},{5,21},{6,22},{7,23},{8,24},{9,... | collective-permute-start | bytes 786440 | tf_op jit(solution)/shard_map/far_p/ppermute | solution.py:64
  21.6 6.8 %collective-permute-start.2 = (bf16[32,4096]{1,0:T(8,128)(2,1)S(1)}, bf16[32,4096]{1,0:T(8,128)(2,1)S(1)}, u32[]{:S(2)}, u32[]{:S(2)}) collective-permute-start(bf16[32,4096]{1,0:T(8,128)(2,1)S(1)} %collective-permute-done.refs_0_), channel_id=1, source_target_pairs={{0,4},{1,5},{2,6},{3,7},{4,0},{5,1},{6,2},{7,3},{8,12},{9,13},{10,... | collective-permute-start | bytes 786440 | tf_op jit(solution)/shard_map/cross/ppermute | solution.py:64
  22.2 3.1 %collective-permute-start.4 = (bf16[32,4096]{1,0:T(8,128)(2,1)S(1)}, bf16[32,4096]{1,0:T(8,128)(2,1)S(1)}, u32[]{:S(2)}, u32[]{:S(2)}) collective-permute-start(bf16[32,4096]{1,0:T(8,128)(2,1)S(1)} %collective-permute-done.refs_0_), channel_id=1, source_target_pairs={{0,2},{1,3},{2,0},{3,1},{4,6},{5,7},{6,4},{7,5},{8,10},{9,11},{10,... | collective-permute-start | bytes 786440 | tf_op jit(solution)/shard_map/far_x/ppermute | solution.py:64
  24.6 3.8 %collective-permute-start.9 = (bf16[32,4096]{1,0:T(8,128)(2,1)S(1)}, bf16[32,4096]{1,0:T(8,128)(2,1)S(1)}, u32[]{:S(2)}, u32[]{:S(2)}) collective-permute-start(bf16[32,4096]{1,0:T(8,128)(2,1)S(1)} %collective-permute-done.8.refs_2_), channel_id=1, source_target_pairs={{0,2},{1,3},{2,0},{3,1},{4,6},{5,7},{6,4},{7,5},{8,10},{9,11},{10,... | collective-permute-start | bytes 786440 | tf_op jit(solution)/shard_map/near_px/ppermute | solution.py:64
  25.2 6.2 %collective-permute-start.7 = (bf16[32,4096]{1,0:T(8,128)(2,1)S(1)}, bf16[32,4096]{1,0:T(8,128)(2,1)S(1)}, u32[]{:S(2)}, u32[]{:S(2)}) collective-permute-start(bf16[32,4096]{1,0:T(8,128)(2,1)S(1)} %collective-permute-done.1.refs_0_), channel_id=1, source_target_pairs={{0,2},{1,3},{2,0},{3,1},{4,6},{5,7},{6,4},{7,5},{8,10},{9,11},{10,... | collective-permute-start | bytes 786440 | tf_op jit(solution)/shard_map/near_x/ppermute | solution.py:64
  28.5 3.5 %collective-permute-start.12 = (bf16[32,4096]{1,0:T(8,128)(2,1)S(1)}, bf16[32,4096]{1,0:T(8,128)(2,1)S(1)}, u32[]{:S(2)}, u32[]{:S(2)}) collective-permute-start(bf16[32,4096]{1,0:T(8,128)(2,1)S(1)} %collective-permute-done.2.refs_6_), channel_id=1, source_target_pairs={{0,2},{1,3},{2,0},{3,1},{4,6},{5,7},{6,4},{7,5},{8,10},{9,11},{10,... | collective-permute-start | bytes 786440 | tf_op jit(solution)/shard_map/cross_x/ppermute | solution.py:64
  28.5 3.5 %collective-permute-start.11 = (bf16[32,4096]{1,0:T(8,128)(2,1)S(1)}, bf16[32,4096]{1,0:T(8,128)(2,1)S(1)}, u32[]{:S(2)}, u32[]{:S(2)}) collective-permute-start(bf16[32,4096]{1,0:T(8,128)(2,1)S(1)} %collective-permute-done.10.refs_4_), channel_id=1, source_target_pairs={{0,2},{1,3},{2,0},{3,1},{4,6},{5,7},{6,4},{7,5},{8,10},{9,11},{10,... | collective-permute-start | bytes 786440 | tf_op jit(solution)/shard_map/far_px/ppermute | solution.py:64
  29.0 6.1 %collective-permute-start.13 = (bf16[64,1024]{1,0:T(8,128)(2,1)S(1)}, bf16[64,1024]{1,0:T(8,128)(2,1)S(1)}, u32[]{:S(2)}, u32[]{:S(2)}) collective-permute-start(bf16[64,1024]{1,0:T(8,128)(2,1)S(1)} %get-tuple-element.43), channel_id=1, source_target_pairs={{0,1},{1,0},{2,3},{3,2},{4,5},{5,4},{6,7},{7,6},{8,9},{9,8},{10,11... | collective-permute-start | bytes 393224 | tf_op jit(solution)/shard_map/got0/ppermute | solution.py:64
  30.5 5.3 %collective-permute-start.14 = (bf16[16,4096]{1,0:T(8,128)(2,1)S(1)}, bf16[16,4096]{1,0:T(8,128)(2,1)S(1)}, u32[]{:S(2)}, u32[]{:S(2)}) collective-permute-start(bf16[16,4096]{1,0:T(8,128)(2,1)S(1)} %slice.7), channel_id=1, source_target_pairs={{0,4},{1,5},{2,6},{3,7},{4,0},{5,1},{6,2},{7,3},{8,12},{9,13},{10,... | collective-permute-start | bytes 393224 | tf_op jit(solution)/shard_map/cross_pb/ppermute | solution.py:64
  31.4 5.3 %collective-permute-start.6 = (bf16[16,4096]{1,0:T(8,128)(2,1)S(1)}, bf16[16,4096]{1,0:T(8,128)(2,1)S(1)}, u32[]{:S(2)}, u32[]{:S(2)}) collective-permute-start(bf16[16,4096]{1,0:T(8,128)(2,1)S(1)} %slice.6), channel_id=1, source_target_pairs={{0,16},{1,17},{2,18},{3,19},{4,20},{5,21},{6,22},{7,23},{8,24},{9,... | collective-permute-start | bytes 393224 | tf_op jit(solution)/shard_map/cross_pa/ppermute | solution.py:64
  34.5 8.0 %collective-permute-start.18 = (bf16[128,1024]{1,0:T(8,128)(2,1)S(1)}, bf16[128,1024]{1,0:T(8,128)(2,1)S(1)}, u32[]{:S(2)}, u32[]{:S(2)}) collective-permute-start(bf16[128,1024]{1,0:T(8,128)(2,1)S(1)} %get-tuple-element.47), channel_id=1, source_target_pairs={{0,1},{1,0},{2,3},{3,2},{4,5},{5,4},{6,7},{7,6},{8,9},{9,8},{10,11... | collective-permute-start | bytes 786440 | tf_op jit(solution)/shard_map/got1/ppermute | solution.py:64
  35.8 1.3 %collective-permute-start.16 = (bf16[16,4096]{1,0:T(8,128)(2,1)S(1)}, bf16[16,4096]{1,0:T(8,128)(2,1)S(1)}, u32[]{:S(2)}, u32[]{:S(2)}) collective-permute-start(bf16[16,4096]{1,0:T(8,128)(2,1)S(1)} %collective-permute-done.14.refs_1_), channel_id=1, source_target_pairs={{0,2},{1,3},{2,0},{3,1},{4,6},{5,7},{6,4},{7,5},{8,10},{9,11},{10,... | collective-permute-start | bytes 393224 | tf_op jit(solution)/shard_map/cross_pxb/ppermute | solution.py:64
  36.7 1.3 %collective-permute-start.15 = (bf16[16,4096]{1,0:T(8,128)(2,1)S(1)}, bf16[16,4096]{1,0:T(8,128)(2,1)S(1)}, u32[]{:S(2)}, u32[]{:S(2)}) collective-permute-start(bf16[16,4096]{1,0:T(8,128)(2,1)S(1)} %collective-permute-done.6.refs_0_), channel_id=1, source_target_pairs={{0,2},{1,3},{2,0},{3,1},{4,6},{5,7},{6,4},{7,5},{8,10},{9,11},{10,... | collective-permute-start | bytes 393224 | tf_op jit(solution)/shard_map/cross_pxa/ppermute | solution.py:64
  38.1 4.9 %copy-start.1 = (s32[256]{0:T(256)S(1)}, s32[256]{0:T(256)}, u32[]{:S(2)}) copy-start(s32[256]{0:T(256)} %param.15) | copy-start | bytes 3076
  38.1 5.1 %copy-start = (s32[1024]{0:T(1024)S(1)}, s32[1024]{0:T(1024)}, u32[]{:S(2)}) copy-start(s32[1024]{0:T(1024)} %param.14) | copy-start | bytes 12292
  39.4 4.8 %collective-permute-start.17 = (bf16[64,512]{1,0:T(8,128)(2,1)S(1)}, bf16[64,512]{1,0:T(8,128)(2,1)S(1)}, u32[]{:S(2)}, u32[]{:S(2)}) collective-permute-start(bf16[64,512]{1,0:T(8,128)(2,1)S(1)} %get-tuple-element.52), channel_id=1, source_target_pairs={{0,1},{1,0},{2,3},{3,2},{4,5},{5,4},{6,7},{7,6},{8,9},{9,8},{10,11... | collective-permute-start | bytes 196616 | tf_op jit(solution)/shard_map/got2/ppermute | solution.py:64
  42.5 4.3 %collective-permute-start.19 = (bf16[64,512]{1,0:T(8,128)(2,1)S(1)}, bf16[64,512]{1,0:T(8,128)(2,1)S(1)}, u32[]{:S(2)}, u32[]{:S(2)}) collective-permute-start(bf16[64,512]{1,0:T(8,128)(2,1)S(1)} %get-tuple-element.56), channel_id=1, source_target_pairs={{0,1},{1,0},{2,3},{3,2},{4,5},{5,4},{6,7},{7,6},{8,9},{9,8},{10,11... | collective-permute-start | bytes 196616 | tf_op jit(solution)/shard_map/got3/ppermute | solution.py:64

commit v15 on v14

--- a/solution.py
+++ b/solution.py
@@ -364,14 +364,8 @@
     cross_pxa = to_core(cross_pa, "cross_pxa")
     cross_pxb = to_core(cross_pb, "cross_pxb")
     last = rows_of(cross_pa, cross_pb, cross_pxa, cross_pxb)
-    n = train.shape[0]
-    cut = n // 2
-    send2, keep2 = score(last, early=[(early1, 64, 64)], columns=(0, cut))
+    send2, keep2 = score(last, early=[(early1, 64, 64)])
     got2 = to_layer(send2, "got2")
-    early1 = after(early1, send2)
-    send3, keep3 = score(last, early=[(early1, 64, 64)], columns=(cut, n))
-    send3 = after(send3, got1)
-    got3 = to_layer(send3, "got3")
 
     train_ids, query_ids = train_ids[None, :], query_ids[:, None]
     most = call_final(
@@ -383,8 +377,8 @@
     return call_final(
         train_ids,
         query_ids,
-        [keep2, got2, keep3, got3],
-        ((3, 0, 1, 0, 0), (3, 2, 3, 0, cut)),
+        [keep2, got2],
+        ((3, 0, 1, 0, 0),),
         most,
     )
 

time: 47.8 us -> 47.1 us (0.985)
  starting transfers between devices: 15.5 us -> 15 us
    ppermute x20 -> x19, starting transfers between devices: 15.5 us -> 15 us  [permute(): return lax.ppermute(value, AXES, pairs)]
    pallas_call x7 -> x6, Pallas kernels: 17 us -> 16.8 us  [kernel_call(): pl.pallas_call(kernel, out_shape=outs, in_specs=specs or [VMEM] * len(inp...]
    ppermute x20 -> x19, waiting for transfers between devices: 12.3 us -> 12.4 us  [permute(): return lax.ppermute(value, AXES, pairs)]
  transfers between devices with their start and end apart: 20 -> 19, of which waited for: 8 -> 8; matrix products, arithmetic and copies ran while one was open for 0% -> 0% of each run, Pallas kernels for 32% -> 32%
where the time goes in v15:
time: 47.1 us; the launch traced here: 46.9 us
  Pallas kernels  18.6 us (39%)
  starting transfers between devices  15 us (32%)
  waiting for transfers between devices  12.4 us (26%)
  between operations  0.79 us (2%)
    pallas_call x6, Pallas kernels, kernel_call(): pl.pallas_call(kernel, out_shape=outs, in_specs=specs or [VMEM] * len(inp...  16.8 us
    ppermute x19, starting transfers between devices, permute(): return lax.ppermute(value, AXES, pairs)  15 us
    ppermute x19, waiting for transfers between devices, permute(): return lax.ppermute(value, AXES, pairs)  12.4 us
    pallas_call x2, Pallas kernels, call_final(): pl.pallas_call(functools.partial(final_kernel, groups=groups, n_given=len...  1.84 us
  transfers between devices with their start and end apart: 19, of which 8 were waited for; matrix products, arithmetic and copies ran while one was open for 0% of the time, Pallas kernels for 32%

profile of v15, /device:TPU:0, one launch (start us, length us, event | category | flops | bytes accessed | tf_op | source)
XLA Modules:
  0.0 46.9 jit_solution(871579515493789483)
XLA Ops:
  0.0 2.8 %shard_map.82 = (bf16[32,4096]{1,0:T(8,128)(2,1)S(1)}, bf16[2,256,256]{2,1,0:T(8,128)(2,1)S(1)}, bf16[2,256,512]{2,1,0:T(8,128)(2,1)S(1)}) custom-call(bf16[64,4096]{1,0:T(8,128)(2,1)} %bitcast.9, f32[64,64]{1,0:T(8,128)} %bitcast.11, f32[64,64]{1,0:T(8,128)} %bitcast.12), custom_call_target="tpu_custom_call" | custom-call | tf_op jit(solution)/shard_map/pallas_call | solution.py:221
  2.8 3.1 %collective-permute-start.1 = (bf16[32,4096]{1,0:T(8,128)(2,1)S(1)}, bf16[32,4096]{1,0:T(8,128)(2,1)S(1)}, u32[]{:S(2)}, u32[]{:S(2)}) collective-permute-start(bf16[32,4096]{1,0:T(8,128)(2,1)S(1)} %get-tuple-element.37.refs_0_), channel_id=1, source_target_pairs={{0,4},{1,5},{2,6},{3,7},{4,0},{5,1},{6,2},{7,3},{8,12},{9,13},{10,... | collective-permute-start | bytes 786440 | tf_op jit(solution)/shard_map/near/ppermute | solution.py:64
  5.9 2.5 %collective-permute-start = (bf16[32,4096]{1,0:T(8,128)(2,1)S(1)}, bf16[32,4096]{1,0:T(8,128)(2,1)S(1)}, u32[]{:S(2)}, u32[]{:S(2)}) collective-permute-start(bf16[32,4096]{1,0:T(8,128)(2,1)S(1)} %get-tuple-element.37.refs_0_), channel_id=1, source_target_pairs={{0,12},{1,13},{2,14},{3,15},{4,8},{5,9},{6,10},{7,11},{8,4},{9,5},... | collective-permute-start | bytes 786440 | tf_op jit(solution)/shard_map/far/ppermute | solution.py:64
  9.0 4.3 %shard_map.83 = (bf16[32,4096]{1,0:T(8,128)(2,1)S(1)}, bf16[1024,4096]{1,0:T(8,128)(2,1)S(1)}, f32[8,256]{1,0:T(8,128)S(1)}) custom-call(f32[2]{0:T(128)} %weight_ref.1, s32[1]{0:T(128)S(6)} %copy.13.layer_ref, bf16[64,4096]{1,0:T(8,128)(2,1)} %bitcast.10, bf16[1024,4096]{1,0:T(8,128)(2,1)} %bitcast.8, bf16[2,256,256]{2,1,0:T(8,128)(2,1)S(1)} %get-tuple-element.28.lefts_ref, ...), custom_call_target="tpu_custom_call" | custom-call | tf_op jit(solution)/shard_map/pallas_call | solution.py:221
  13.9 1.5 %collective-permute-start.8 = (bf16[32,4096]{1,0:T(8,128)(2,1)S(1)}, bf16[32,4096]{1,0:T(8,128)(2,1)S(1)}, u32[]{:S(2)}, u32[]{:S(2)}) collective-permute-start(bf16[32,4096]{1,0:T(8,128)(2,1)S(1)} %collective-permute-done.1.refs_0_), channel_id=1, source_target_pairs={{0,16},{1,17},{2,18},{3,19},{4,20},{5,21},{6,22},{7,23},{8,24},{9,... | collective-permute-start | bytes 786440 | tf_op jit(solution)/shard_map/near_p/ppermute | solution.py:64
  15.4 4.7 %collective-permute-done.refs_0_ = bf16[32,4096]{1,0:T(8,128)(2,1)S(1)} collective-permute-done((bf16[32,4096]{1,0:T(8,128)(2,1)S(1)}, bf16[32,4096]{1,0:T(8,128)(2,1)S(1)}, u32[]{:S(2)}, u32[]{:S(2)}) %collective-permute-start) | collective-permute-done | bytes 262176 | tf_op jit(solution)/shard_map/far/ppermute | solution.py:64
  20.1 1.5 %collective-permute-start.10 = (bf16[32,4096]{1,0:T(8,128)(2,1)S(1)}, bf16[32,4096]{1,0:T(8,128)(2,1)S(1)}, u32[]{:S(2)}, u32[]{:S(2)}) collective-permute-start(bf16[32,4096]{1,0:T(8,128)(2,1)S(1)} %collective-permute-done.refs_0_), channel_id=1, source_target_pairs={{0,16},{1,17},{2,18},{3,19},{4,20},{5,21},{6,22},{7,23},{8,24},{9,... | collective-permute-start | bytes 786440 | tf_op jit(solution)/shard_map/far_p/ppermute | solution.py:64
  22.2 2.4 %shard_map.84.refs_2_.refs_8_ = f32[128,1024]{1,0:T(8,128)S(1)} custom-call(f32[8,256]{1,0:T(8,128)S(1)} %get-tuple-element.30.weight_ref, bf16[1024,4096]{1,0:T(8,128)(2,1)S(1)} %get-tuple-element.31.train_ref, bf16[32,4096]{1,0:T(8,128)(2,1)S(1)} %get-tuple-element.37.refs_0_, bf16[32,4096]{1,0:T(8,128)(2,1)S(1)} %collective-permute-done.5.refs_1_, ...), custom_call_target="tpu_custom_call" | custom-call | tf_op jit(solution)/shard_map/pallas_call | solution.py:221
  24.6 0.6 %collective-permute-start.9 = (bf16[32,4096]{1,0:T(8,128)(2,1)S(1)}, bf16[32,4096]{1,0:T(8,128)(2,1)S(1)}, u32[]{:S(2)}, u32[]{:S(2)}) collective-permute-start(bf16[32,4096]{1,0:T(8,128)(2,1)S(1)} %collective-permute-done.8.refs_2_), channel_id=1, source_target_pairs={{0,2},{1,3},{2,0},{3,1},{4,6},{5,7},{6,4},{7,5},{8,10},{9,11},{10,... | collective-permute-start | bytes 786440 | tf_op jit(solution)/shard_map/near_px/ppermute | solution.py:64
  25.3 2.4 %shard_map.85 = (bf16[64,1024]{1,0:T(8,128)(2,1)S(1)}, f32[64,1024]{1,0:T(8,128)S(1)}) custom-call(f32[8,256]{1,0:T(8,128)S(1)} %get-tuple-element.30.weight_ref, bf16[1024,4096]{1,0:T(8,128)(2,1)S(1)} %get-tuple-element.31.train_ref, bf16[32,4096]{1,0:T(8,128)(2,1)S(1)} %collective-permute-done.refs_0_, ...), custom_call_target="tpu_custom_call" | custom-call | tf_op jit(solution)/shard_map/pallas_call | solution.py:221
  27.7 0.8 %collective-permute-done.2.refs_6_ = bf16[32,4096]{1,0:T(8,128)(2,1)S(1)} collective-permute-done((bf16[32,4096]{1,0:T(8,128)(2,1)S(1)}, bf16[32,4096]{1,0:T(8,128)(2,1)S(1)}, u32[]{:S(2)}, u32[]{:S(2)}) %collective-permute-start.2) | collective-permute-done | bytes 262176 | tf_op jit(solution)/shard_map/cross/ppermute | solution.py:64
  29.0 1.5 %collective-permute-start.13 = (bf16[64,1024]{1,0:T(8,128)(2,1)S(1)}, bf16[64,1024]{1,0:T(8,128)(2,1)S(1)}, u32[]{:S(2)}, u32[]{:S(2)}) collective-permute-start(bf16[64,1024]{1,0:T(8,128)(2,1)S(1)} %get-tuple-element.39), channel_id=1, source_target_pairs={{0,1},{1,0},{2,3},{3,2},{4,5},{5,4},{6,7},{7,6},{8,9},{9,8},{10,11... | collective-permute-start | bytes 393224 | tf_op jit(solution)/shard_map/got0/ppermute | solution.py:64
  30.5 0.9 %collective-permute-start.14 = (bf16[16,4096]{1,0:T(8,128)(2,1)S(1)}, bf16[16,4096]{1,0:T(8,128)(2,1)S(1)}, u32[]{:S(2)}, u32[]{:S(2)}) collective-permute-start(bf16[16,4096]{1,0:T(8,128)(2,1)S(1)} %slice.7), channel_id=1, source_target_pairs={{0,4},{1,5},{2,6},{3,7},{4,0},{5,1},{6,2},{7,3},{8,12},{9,13},{10,... | collective-permute-start | bytes 393224 | tf_op jit(solution)/shard_map/cross_pb/ppermute | solution.py:64
  31.4 0.6 %collective-permute-start.6 = (bf16[16,4096]{1,0:T(8,128)(2,1)S(1)}, bf16[16,4096]{1,0:T(8,128)(2,1)S(1)}, u32[]{:S(2)}, u32[]{:S(2)}) collective-permute-start(bf16[16,4096]{1,0:T(8,128)(2,1)S(1)} %slice.6), channel_id=1, source_target_pairs={{0,16},{1,17},{2,18},{3,19},{4,20},{5,21},{6,22},{7,23},{8,24},{9,... | collective-permute-start | bytes 393224 | tf_op jit(solution)/shard_map/cross_pa/ppermute | solution.py:64
  32.0 2.5 %shard_map.86 = (f32[128,1024]{1,0:T(8,128)S(1)}, bf16[128,1024]{1,0:T(8,128)(2,1)S(1)}, f32[128,1024]{1,0:T(8,128)S(1)}) custom-call(f32[8,256]{1,0:T(8,128)S(1)} %get-tuple-element.30.weight_ref, bf16[1024,4096]{1,0:T(8,128)(2,1)S(1)} %get-tuple-element.31.train_ref, bf16[32,4096]{1,0:T(8,128)(2,1)S(1)} %collective-permute-done.1.refs_0_, ...), custom_call_target="tpu_custom_call" | custom-call | tf_op jit(solution)/shard_map/pallas_call | solution.py:221
  34.5 0.6 %collective-permute-start.18 = (bf16[128,1024]{1,0:T(8,128)(2,1)S(1)}, bf16[128,1024]{1,0:T(8,128)(2,1)S(1)}, u32[]{:S(2)}, u32[]{:S(2)}) collective-permute-start(bf16[128,1024]{1,0:T(8,128)(2,1)S(1)} %get-tuple-element.43), channel_id=1, source_target_pairs={{0,1},{1,0},{2,3},{3,2},{4,5},{5,4},{6,7},{7,6},{8,9},{9,8},{10,11... | collective-permute-start | bytes 786440 | tf_op jit(solution)/shard_map/got1/ppermute | solution.py:64
  35.1 0.7 %collective-permute-done.14.refs_1_ = bf16[16,4096]{1,0:T(8,128)(2,1)S(1)} collective-permute-done((bf16[16,4096]{1,0:T(8,128)(2,1)S(1)}, bf16[16,4096]{1,0:T(8,128)(2,1)S(1)}, u32[]{:S(2)}, u32[]{:S(2)}) %collective-permute-start.14) | collective-permute-done | bytes 131104 | tf_op jit(solution)/shard_map/cross_pb/ppermute | solution.py:64
  35.8 1.0 %collective-permute-done.6.refs_0_ = bf16[16,4096]{1,0:T(8,128)(2,1)S(1)} collective-permute-done((bf16[16,4096]{1,0:T(8,128)(2,1)S(1)}, bf16[16,4096]{1,0:T(8,128)(2,1)S(1)}, u32[]{:S(2)}, u32[]{:S(2)}) %collective-permute-start.6) | collective-permute-done | bytes 131104 | tf_op jit(solution)/shard_map/cross_pa/ppermute | solution.py:64
  37.1 1.0 %collective-permute-done.15.refs_2_ = bf16[16,4096]{1,0:T(8,128)(2,1)S(1)} collective-permute-done((bf16[16,4096]{1,0:T(8,128)(2,1)S(1)}, bf16[16,4096]{1,0:T(8,128)(2,1)S(1)}, u32[]{:S(2)}, u32[]{:S(2)}) %collective-permute-start.15) | collective-permute-done | bytes 131104 | tf_op jit(solution)/shard_map/cross_pxa/ppermute | solution.py:64
  38.1 2.4 %shard_map.87 = (bf16[64,1024]{1,0:T(8,128)(2,1)S(1)}, f32[64,1024]{1,0:T(8,128)S(1)}) custom-call(f32[8,256]{1,0:T(8,128)S(1)} %get-tuple-element.30.weight_ref, bf16[1024,4096]{1,0:T(8,128)(2,1)S(1)} %get-tuple-element.31.train_ref, bf16[16,4096]{1,0:T(8,128)(2,1)S(1)} %collective-permute-done.6.refs_0_, ...), custom_call_target="tpu_custom_call" | custom-call | tf_op jit(solution)/shard_map/pallas_call | solution.py:221
  41.2 1.2 %collective-permute-done.18.refs_3_ = bf16[128,1024]{1,0:T(8,128)(2,1)S(1)} collective-permute-done((bf16[128,1024]{1,0:T(8,128)(2,1)S(1)}, bf16[128,1024]{1,0:T(8,128)(2,1)S(1)}, u32[]{:S(2)}, u32[]{:S(2)}) %collective-permute-start.18) | collective-permute-done | bytes 262176 | tf_op jit(solution)/shard_map/got1/ppermute | solution.py:64
  42.4 1.0 %shard_map.88.refs_2_ = f32[256,1024]{1,0:T(8,128)} custom-call(s32[1,1024]{1,0:T(1,128)S(1)} %bitcast.6, s32[256,1]{1,0:T(8,128)S(1)} %copy.11.query_ids, f32[64,1024]{1,0:T(8,128)S(1)} %get-tuple-element.49.refs_0_, bf16[64,1024]{1,0:T(8,128)(2,1)S(1)} %collective-permute-done.13.refs_1_, f32[128,1024]{1,0:T(8,128)S(1)} %get-tuple-element.50.refs_2_, ...), custom_call_target="tpu_custom_call" | custom-call | tf_op jit(solution)/shard_map/pallas_call | solution.py:282
  43.4 2.7 %collective-permute-done.17.refs_1_ = bf16[64,1024]{1,0:T(8,128)(2,1)S(1)} collective-permute-done((bf16[64,1024]{1,0:T(8,128)(2,1)S(1)}, bf16[64,1024]{1,0:T(8,128)(2,1)S(1)}, u32[]{:S(2)}, u32[]{:S(2)}) %collective-permute-start.17) | collective-permute-done | bytes 131104 | tf_op jit(solution)/shard_map/got2/ppermute | solution.py:64
  46.1 0.8 %shard_map.89 = f32[256,1024]{1,0:T(8,128)} custom-call(s32[1,1024]{1,0:T(1,128)S(1)} %bitcast.7, s32[256,1]{1,0:T(8,128)S(1)} %copy.11.query_ids, f32[64,1024]{1,0:T(8,128)S(1)} %get-tuple-element.47.refs_0_, bf16[64,1024]{1,0:T(8,128)(2,1)S(1)} %collective-permute-done.17.refs_1_, f32[256,1024]{1,0:T(8,128)} %shard_map.88.refs_2_), custom_call_target="tpu_custom_call", output_to_operand_aliasing={{}: (4, {})} | custom-call | tf_op jit(solution)/shard_map/pallas_call | solution.py:282
  (29 shorter events, 2.8 us)
Async XLA Ops:
  2.8 11.1 %collective-permute-start.1 = (bf16[32,4096]{1,0:T(8,128)(2,1)S(1)}, bf16[32,4096]{1,0:T(8,128)(2,1)S(1)}, u32[]{:S(2)}, u32[]{:S(2)}) collective-permute-start(bf16[32,4096]{1,0:T(8,128)(2,1)S(1)} %get-tuple-element.37.refs_0_), channel_id=1, source_target_pairs={{0,4},{1,5},{2,6},{3,7},{4,0},{5,1},{6,2},{7,3},{8,12},{9,13},{10,... | collective-permute-start | bytes 786440 | tf_op jit(solution)/shard_map/near/ppermute | solution.py:64
  5.9 14.2 %collective-permute-start = (bf16[32,4096]{1,0:T(8,128)(2,1)S(1)}, bf16[32,4096]{1,0:T(8,128)(2,1)S(1)}, u32[]{:S(2)}, u32[]{:S(2)}) collective-permute-start(bf16[32,4096]{1,0:T(8,128)(2,1)S(1)} %get-tuple-element.37.refs_0_), channel_id=1, source_target_pairs={{0,12},{1,13},{2,14},{3,15},{4,8},{5,9},{6,10},{7,11},{8,4},{9,5},... | collective-permute-start | bytes 786440 | tf_op jit(solution)/shard_map/far/ppermute | solution.py:64
  13.3 8.9 %collective-permute-start.5 = (bf16[32,4096]{1,0:T(8,128)(2,1)S(1)}, bf16[32,4096]{1,0:T(8,128)(2,1)S(1)}, u32[]{:S(2)}, u32[]{:S(2)}) collective-permute-start(bf16[32,4096]{1,0:T(8,128)(2,1)S(1)} %get-tuple-element.37.refs_0_), channel_id=1, source_target_pairs={{0,2},{1,3},{2,0},{3,1},{4,6},{5,7},{6,4},{7,5},{8,10},{9,11},{10,... | collective-permute-start | bytes 786440 | tf_op jit(solution)/shard_map/mine_x/ppermute | solution.py:64
  13.4 8.8 %collective-permute-start.3 = (bf16[32,4096]{1,0:T(8,128)(2,1)S(1)}, bf16[32,4096]{1,0:T(8,128)(2,1)S(1)}, u32[]{:S(2)}, u32[]{:S(2)}) collective-permute-start(bf16[32,4096]{1,0:T(8,128)(2,1)S(1)} %get-tuple-element.33.refs_2_), channel_id=1, source_target_pairs={{0,2},{1,3},{2,0},{3,1},{4,6},{5,7},{6,4},{7,5},{8,10},{9,11},{10,... | collective-permute-start | bytes 786440 | tf_op jit(solution)/shard_map/rest_x/ppermute | solution.py:64
  13.9 10.7 %collective-permute-start.8 = (bf16[32,4096]{1,0:T(8,128)(2,1)S(1)}, bf16[32,4096]{1,0:T(8,128)(2,1)S(1)}, u32[]{:S(2)}, u32[]{:S(2)}) collective-permute-start(bf16[32,4096]{1,0:T(8,128)(2,1)S(1)} %collective-permute-done.1.refs_0_), channel_id=1, source_target_pairs={{0,16},{1,17},{2,18},{3,19},{4,20},{5,21},{6,22},{7,23},{8,24},{9,... | collective-permute-start | bytes 786440 | tf_op jit(solution)/shard_map/near_p/ppermute | solution.py:64
  20.1 8.3 %collective-permute-start.10 = (bf16[32,4096]{1,0:T(8,128)(2,1)S(1)}, bf16[32,4096]{1,0:T(8,128)(2,1)S(1)}, u32[]{:S(2)}, u32[]{:S(2)}) collective-permute-start(bf16[32,4096]{1,0:T(8,128)(2,1)S(1)} %collective-permute-done.refs_0_), channel_id=1, source_target_pairs={{0,16},{1,17},{2,18},{3,19},{4,20},{5,21},{6,22},{7,23},{8,24},{9,... | collective-permute-start | bytes 786440 | tf_op jit(solution)/shard_map/far_p/ppermute | solution.py:64
  21.6 6.8 %collective-permute-start.2 = (bf16[32,4096]{1,0:T(8,128)(2,1)S(1)}, bf16[32,4096]{1,0:T(8,128)(2,1)S(1)}, u32[]{:S(2)}, u32[]{:S(2)}) collective-permute-start(bf16[32,4096]{1,0:T(8,128)(2,1)S(1)} %collective-permute-done.refs_0_), channel_id=1, source_target_pairs={{0,4},{1,5},{2,6},{3,7},{4,0},{5,1},{6,2},{7,3},{8,12},{9,13},{10,... | collective-permute-start | bytes 786440 | tf_op jit(solution)/shard_map/cross/ppermute | solution.py:64
  22.2 3.1 %collective-permute-start.4 = (bf16[32,4096]{1,0:T(8,128)(2,1)S(1)}, bf16[32,4096]{1,0:T(8,128)(2,1)S(1)}, u32[]{:S(2)}, u32[]{:S(2)}) collective-permute-start(bf16[32,4096]{1,0:T(8,128)(2,1)S(1)} %collective-permute-done.refs_0_), channel_id=1, source_target_pairs={{0,2},{1,3},{2,0},{3,1},{4,6},{5,7},{6,4},{7,5},{8,10},{9,11},{10,... | collective-permute-start | bytes 786440 | tf_op jit(solution)/shard_map/far_x/ppermute | solution.py:64
  24.6 3.8 %collective-permute-start.9 = (bf16[32,4096]{1,0:T(8,128)(2,1)S(1)}, bf16[32,4096]{1,0:T(8,128)(2,1)S(1)}, u32[]{:S(2)}, u32[]{:S(2)}) collective-permute-start(bf16[32,4096]{1,0:T(8,128)(2,1)S(1)} %collective-permute-done.8.refs_2_), channel_id=1, source_target_pairs={{0,2},{1,3},{2,0},{3,1},{4,6},{5,7},{6,4},{7,5},{8,10},{9,11},{10,... | collective-permute-start | bytes 786440 | tf_op jit(solution)/shard_map/near_px/ppermute | solution.py:64
  25.2 6.2 %collective-permute-start.7 = (bf16[32,4096]{1,0:T(8,128)(2,1)S(1)}, bf16[32,4096]{1,0:T(8,128)(2,1)S(1)}, u32[]{:S(2)}, u32[]{:S(2)}) collective-permute-start(bf16[32,4096]{1,0:T(8,128)(2,1)S(1)} %collective-permute-done.1.refs_0_), channel_id=1, source_target_pairs={{0,2},{1,3},{2,0},{3,1},{4,6},{5,7},{6,4},{7,5},{8,10},{9,11},{10,... | collective-permute-start | bytes 786440 | tf_op jit(solution)/shard_map/near_x/ppermute | solution.py:64
  28.5 3.6 %collective-permute-start.12 = (bf16[32,4096]{1,0:T(8,128)(2,1)S(1)}, bf16[32,4096]{1,0:T(8,128)(2,1)S(1)}, u32[]{:S(2)}, u32[]{:S(2)}) collective-permute-start(bf16[32,4096]{1,0:T(8,128)(2,1)S(1)} %collective-permute-done.2.refs_6_), channel_id=1, source_target_pairs={{0,2},{1,3},{2,0},{3,1},{4,6},{5,7},{6,4},{7,5},{8,10},{9,11},{10,... | collective-permute-start | bytes 786440 | tf_op jit(solution)/shard_map/cross_x/ppermute | solution.py:64
  28.5 3.5 %collective-permute-start.11 = (bf16[32,4096]{1,0:T(8,128)(2,1)S(1)}, bf16[32,4096]{1,0:T(8,128)(2,1)S(1)}, u32[]{:S(2)}, u32[]{:S(2)}) collective-permute-start(bf16[32,4096]{1,0:T(8,128)(2,1)S(1)} %collective-permute-done.10.refs_4_), channel_id=1, source_target_pairs={{0,2},{1,3},{2,0},{3,1},{4,6},{5,7},{6,4},{7,5},{8,10},{9,11},{10,... | collective-permute-start | bytes 786440 | tf_op jit(solution)/shard_map/far_px/ppermute | solution.py:64
  29.0 6.1 %collective-permute-start.13 = (bf16[64,1024]{1,0:T(8,128)(2,1)S(1)}, bf16[64,1024]{1,0:T(8,128)(2,1)S(1)}, u32[]{:S(2)}, u32[]{:S(2)}) collective-permute-start(bf16[64,1024]{1,0:T(8,128)(2,1)S(1)} %get-tuple-element.39), channel_id=1, source_target_pairs={{0,1},{1,0},{2,3},{3,2},{4,5},{5,4},{6,7},{7,6},{8,9},{9,8},{10,11... | collective-permute-start | bytes 393224 | tf_op jit(solution)/shard_map/got0/ppermute | solution.py:64
  30.5 5.3 %collective-permute-start.14 = (bf16[16,4096]{1,0:T(8,128)(2,1)S(1)}, bf16[16,4096]{1,0:T(8,128)(2,1)S(1)}, u32[]{:S(2)}, u32[]{:S(2)}) collective-permute-start(bf16[16,4096]{1,0:T(8,128)(2,1)S(1)} %slice.7), channel_id=1, source_target_pairs={{0,4},{1,5},{2,6},{3,7},{4,0},{5,1},{6,2},{7,3},{8,12},{9,13},{10,... | collective-permute-start | bytes 393224 | tf_op jit(solution)/shard_map/cross_pb/ppermute | solution.py:64
  31.4 9.7 %copy-start.1 = (s32[256]{0:T(256)S(1)}, s32[256]{0:T(256)}, u32[]{:S(2)}) copy-start(s32[256]{0:T(256)} %param.15) | copy-start | bytes 3076
  31.4 11.0 %copy-start = (s32[1024]{0:T(1024)S(1)}, s32[1024]{0:T(1024)}, u32[]{:S(2)}) copy-start(s32[1024]{0:T(1024)} %param.14) | copy-start | bytes 12292
  31.4 5.3 %collective-permute-start.6 = (bf16[16,4096]{1,0:T(8,128)(2,1)S(1)}, bf16[16,4096]{1,0:T(8,128)(2,1)S(1)}, u32[]{:S(2)}, u32[]{:S(2)}) collective-permute-start(bf16[16,4096]{1,0:T(8,128)(2,1)S(1)} %slice.6), channel_id=1, source_target_pairs={{0,16},{1,17},{2,18},{3,19},{4,20},{5,21},{6,22},{7,23},{8,24},{9,... | collective-permute-start | bytes 393224 | tf_op jit(solution)/shard_map/cross_pa/ppermute | solution.py:64
  34.5 7.9 %collective-permute-start.18 = (bf16[128,1024]{1,0:T(8,128)(2,1)S(1)}, bf16[128,1024]{1,0:T(8,128)(2,1)S(1)}, u32[]{:S(2)}, u32[]{:S(2)}) collective-permute-start(bf16[128,1024]{1,0:T(8,128)(2,1)S(1)} %get-tuple-element.43), channel_id=1, source_target_pairs={{0,1},{1,0},{2,3},{3,2},{4,5},{5,4},{6,7},{7,6},{8,9},{9,8},{10,11... | collective-permute-start | bytes 786440 | tf_op jit(solution)/shard_map/got1/ppermute | solution.py:64
  35.8 1.3 %collective-permute-start.16 = (bf16[16,4096]{1,0:T(8,128)(2,1)S(1)}, bf16[16,4096]{1,0:T(8,128)(2,1)S(1)}, u32[]{:S(2)}, u32[]{:S(2)}) collective-permute-start(bf16[16,4096]{1,0:T(8,128)(2,1)S(1)} %collective-permute-done.14.refs_1_), channel_id=1, source_target_pairs={{0,2},{1,3},{2,0},{3,1},{4,6},{5,7},{6,4},{7,5},{8,10},{9,11},{10,... | collective-permute-start | bytes 393224 | tf_op jit(solution)/shard_map/cross_pxb/ppermute | solution.py:64
  36.7 1.3 %collective-permute-start.15 = (bf16[16,4096]{1,0:T(8,128)(2,1)S(1)}, bf16[16,4096]{1,0:T(8,128)(2,1)S(1)}, u32[]{:S(2)}, u32[]{:S(2)}) collective-permute-start(bf16[16,4096]{1,0:T(8,128)(2,1)S(1)} %collective-permute-done.6.refs_0_), channel_id=1, source_target_pairs={{0,2},{1,3},{2,0},{3,1},{4,6},{5,7},{6,4},{7,5},{8,10},{9,11},{10,... | collective-permute-start | bytes 393224 | tf_op jit(solution)/shard_map/cross_pxa/ppermute | solution.py:64
  40.5 5.6 %collective-permute-start.17 = (bf16[64,1024]{1,0:T(8,128)(2,1)S(1)}, bf16[64,1024]{1,0:T(8,128)(2,1)S(1)}, u32[]{:S(2)}, u32[]{:S(2)}) collective-permute-start(bf16[64,1024]{1,0:T(8,128)(2,1)S(1)} %get-tuple-element.48), channel_id=1, source_target_pairs={{0,1},{1,0},{2,3},{3,2},{4,5},{5,4},{6,7},{7,6},{8,9},{9,8},{10,11... | collective-permute-start | bytes 393224 | tf_op jit(solution)/shard_map/got2/ppermute | solution.py:64

commit v16 on v15

--- a/solution.py
+++ b/solution.py
@@ -341,21 +341,23 @@
     far = after(far, near)
     cross = to_near(far, "cross")
     far_p = to_part(far, "far_p")
-    far_x = to_core(after(far, rest_x), "far_x")
+    far_x = to_core(after(far, rest_x, mine_x), "far_x")
     mine_x = after(mine_x, far)
-    (early0,) = score(rows_of(mine, mine_x, rest, rest_x), stored=128)
-    send0, keep0 = score(rows_of(far, far_x), early=[(early0, 0, 64)])
+    early0, send0, keep0 = score(
+        rows_of(mine, mine_x, rest, rest_x, far, far_x), stored=128, early=[(None, 0, 64)]
+    )
     got0 = to_layer(send0, "got0")
 
-    near_p = after(near_p, early0)
     near_px = to_core(near_p, "near_px")
-    far_p, cross = after(far_p, near_px, send0), after(cross, send0)
-    far_px = to_core(far_p, "far_px")
-    cross_pa = to_part(cross[:CHUNK], "cross_pa")
+    far_p, cross = after(far_p, near_px, near_x, send0), after(cross, send0)
+    far_px0 = to_core(far_p[:CHUNK], "far_px0")
+    far_px1 = to_core(far_p[CHUNK:], "far_px1")
+    cross_x = to_core(cross, "cross_x")
+    cross_pa = to_part(after(cross[:CHUNK], cross_x), "cross_pa")
     cross_pb = to_near(far_p[CHUNK:], "cross_pb")
-    cross_x = to_core(cross, "cross_x")
+    cross_x = after(cross_x, got0)
     early1, send1, keep1 = score(
-        rows_of(near, near_x, near_p, near_px, far_p, far_px, cross, cross_x),
+        rows_of(near, near_x, near_p, near_px, far_p, far_px0, far_px1, cross, cross_x),
         stored=128,
         early=[(early0, 64, 64), (None, 0, 64)],
     )

time: 47.1 us -> 48 us (1.019)
  starting transfers between devices: 15 us -> 18.5 us
  Pallas kernels: 18.6 us -> 16.3 us
  waiting for transfers between devices: 12.4 us -> 11.7 us
    ppermute x19 -> x20, starting transfers between devices: 15 us -> 18.5 us  [permute(): return lax.ppermute(value, AXES, pairs)]
    pallas_call x6 -> x5, Pallas kernels: 16.8 us -> 14.5 us  [kernel_call(): pl.pallas_call(kernel, out_shape=outs, in_specs=specs or [VMEM] * len(inp...]
    ppermute x19 -> x20, waiting for transfers between devices: 12.4 us -> 11.7 us  [permute(): return lax.ppermute(value, AXES, pairs)]
  transfers between devices with their start and end apart: 19 -> 20, of which waited for: 8 -> 7; matrix products, arithmetic and copies ran while one was open for 0% -> 0% of each run, Pallas kernels for 32% -> 27%
where the time goes in v16:
time: 48 us; the launch traced here: 47.5 us
  starting transfers between devices  18.5 us (39%)
  Pallas kernels  16.3 us (34%)
  waiting for transfers between devices  11.7 us (24%)
  between operations  0.77 us (2%)
    ppermute x20, starting transfers between devices, permute(): return lax.ppermute(value, AXES, pairs)  18.5 us
    pallas_call x5, Pallas kernels, kernel_call(): pl.pallas_call(kernel, out_shape=outs, in_specs=specs or [VMEM] * len(inp...  14.5 us
    ppermute x20, waiting for transfers between devices, permute(): return lax.ppermute(value, AXES, pairs)  11.7 us
    pallas_call x2, Pallas kernels, call_final(): pl.pallas_call(functools.partial(final_kernel, groups=groups, n_given=len...  1.84 us
  transfers between devices with their start and end apart: 20, of which 7 were waited for; matrix products, arithmetic and copies ran while one was open for 0% of the time, Pallas kernels for 27%

profile of v16, /device:TPU:0, one launch (start us, length us, event | category | flops | bytes accessed | tf_op | source)
XLA Modules:
  0.0 47.5 jit_solution(6123719507077445761)
XLA Ops:
  0.0 2.8 %shard_map.82 = (bf16[32,4096]{1,0:T(8,128)(2,1)S(1)}, bf16[2,256,256]{2,1,0:T(8,128)(2,1)S(1)}, bf16[2,256,512]{2,1,0:T(8,128)(2,1)S(1)}) custom-call(bf16[64,4096]{1,0:T(8,128)(2,1)} %bitcast.9, f32[64,64]{1,0:T(8,128)} %bitcast.11, f32[64,64]{1,0:T(8,128)} %bitcast.12), custom_call_target="tpu_custom_call" | custom-call | tf_op jit(solution)/shard_map/pallas_call | solution.py:221
  2.8 3.1 %collective-permute-start.1 = (bf16[32,4096]{1,0:T(8,128)(2,1)S(1)}, bf16[32,4096]{1,0:T(8,128)(2,1)S(1)}, u32[]{:S(2)}, u32[]{:S(2)}) collective-permute-start(bf16[32,4096]{1,0:T(8,128)(2,1)S(1)} %get-tuple-element.38.refs_0_), channel_id=1, source_target_pairs={{0,4},{1,5},{2,6},{3,7},{4,0},{5,1},{6,2},{7,3},{8,12},{9,13},{10,... | collective-permute-start | bytes 786440 | tf_op jit(solution)/shard_map/near/ppermute | solution.py:64
  5.9 2.5 %collective-permute-start = (bf16[32,4096]{1,0:T(8,128)(2,1)S(1)}, bf16[32,4096]{1,0:T(8,128)(2,1)S(1)}, u32[]{:S(2)}, u32[]{:S(2)}) collective-permute-start(bf16[32,4096]{1,0:T(8,128)(2,1)S(1)} %get-tuple-element.38.refs_0_), channel_id=1, source_target_pairs={{0,12},{1,13},{2,14},{3,15},{4,8},{5,9},{6,10},{7,11},{8,4},{9,5},... | collective-permute-start | bytes 786440 | tf_op jit(solution)/shard_map/far/ppermute | solution.py:64
  9.0 4.3 %shard_map.83 = (bf16[32,4096]{1,0:T(8,128)(2,1)S(1)}, bf16[1024,4096]{1,0:T(8,128)(2,1)S(1)}, f32[8,256]{1,0:T(8,128)S(1)}) custom-call(f32[2]{0:T(128)} %weight_ref.1, s32[1]{0:T(128)S(6)} %copy.13.layer_ref, bf16[64,4096]{1,0:T(8,128)(2,1)} %bitcast.10, bf16[1024,4096]{1,0:T(8,128)(2,1)} %bitcast.8, bf16[2,256,256]{2,1,0:T(8,128)(2,1)S(1)} %get-tuple-element.30.lefts_ref, ...), custom_call_target="tpu_custom_call" | custom-call | tf_op jit(solution)/shard_map/pallas_call | solution.py:221
  13.9 1.5 %collective-permute-start.9 = (bf16[32,4096]{1,0:T(8,128)(2,1)S(1)}, bf16[32,4096]{1,0:T(8,128)(2,1)S(1)}, u32[]{:S(2)}, u32[]{:S(2)}) collective-permute-start(bf16[32,4096]{1,0:T(8,128)(2,1)S(1)} %collective-permute-done.1.refs_0_), channel_id=1, source_target_pairs={{0,16},{1,17},{2,18},{3,19},{4,20},{5,21},{6,22},{7,23},{8,24},{9,... | collective-permute-start | bytes 786440 | tf_op jit(solution)/shard_map/near_p/ppermute | solution.py:64
  15.4 4.7 %collective-permute-done.refs_4_ = bf16[32,4096]{1,0:T(8,128)(2,1)S(1)} collective-permute-done((bf16[32,4096]{1,0:T(8,128)(2,1)S(1)}, bf16[32,4096]{1,0:T(8,128)(2,1)S(1)}, u32[]{:S(2)}, u32[]{:S(2)}) %collective-permute-start) | collective-permute-done | bytes 262176 | tf_op jit(solution)/shard_map/far/ppermute | solution.py:64
  20.1 0.6 %collective-permute-start.2 = (bf16[32,4096]{1,0:T(8,128)(2,1)S(1)}, bf16[32,4096]{1,0:T(8,128)(2,1)S(1)}, u32[]{:S(2)}, u32[]{:S(2)}) collective-permute-start(bf16[32,4096]{1,0:T(8,128)(2,1)S(1)} %collective-permute-done.refs_4_), channel_id=1, source_target_pairs={{0,4},{1,5},{2,6},{3,7},{4,0},{5,1},{6,2},{7,3},{8,12},{9,13},{10,... | collective-permute-start | bytes 786440 | tf_op jit(solution)/shard_map/cross/ppermute | solution.py:64
  20.8 1.5 %collective-permute-start.11 = (bf16[32,4096]{1,0:T(8,128)(2,1)S(1)}, bf16[32,4096]{1,0:T(8,128)(2,1)S(1)}, u32[]{:S(2)}, u32[]{:S(2)}) collective-permute-start(bf16[32,4096]{1,0:T(8,128)(2,1)S(1)} %collective-permute-done.refs_4_), channel_id=1, source_target_pairs={{0,16},{1,17},{2,18},{3,19},{4,20},{5,21},{6,22},{7,23},{8,24},{9,... | collective-permute-start | bytes 786440 | tf_op jit(solution)/shard_map/far_p/ppermute | solution.py:64
  22.3 0.5 %collective-permute-start.10 = (bf16[32,4096]{1,0:T(8,128)(2,1)S(1)}, bf16[32,4096]{1,0:T(8,128)(2,1)S(1)}, u32[]{:S(2)}, u32[]{:S(2)}) collective-permute-start(bf16[32,4096]{1,0:T(8,128)(2,1)S(1)} %collective-permute-done.9.refs_2_), channel_id=1, source_target_pairs={{0,2},{1,3},{2,0},{3,1},{4,6},{5,7},{6,4},{7,5},{8,10},{9,11},{10,... | collective-permute-start | bytes 786440 | tf_op jit(solution)/shard_map/near_px/ppermute | solution.py:64
  22.8 2.5 %shard_map.84 = (f32[128,1024]{1,0:T(8,128)S(1)}, bf16[64,1024]{1,0:T(8,128)(2,1)S(1)}, f32[64,1024]{1,0:T(8,128)S(1)}) custom-call(f32[8,256]{1,0:T(8,128)S(1)} %get-tuple-element.32.weight_ref, bf16[1024,4096]{1,0:T(8,128)(2,1)S(1)} %get-tuple-element.33.train_ref, bf16[32,4096]{1,0:T(8,128)(2,1)S(1)} %get-tuple-element.38.refs_0_, ...), custom_call_target="tpu_custom_call" | custom-call | tf_op jit(solution)/shard_map/pallas_call | solution.py:221
  25.3 1.6 %collective-permute-start.14 = (bf16[64,1024]{1,0:T(8,128)(2,1)S(1)}, bf16[64,1024]{1,0:T(8,128)(2,1)S(1)}, u32[]{:S(2)}, u32[]{:S(2)}) collective-permute-start(bf16[64,1024]{1,0:T(8,128)(2,1)S(1)} %get-tuple-element.41), channel_id=1, source_target_pairs={{0,1},{1,0},{2,3},{3,2},{4,5},{5,4},{6,7},{7,6},{8,9},{9,8},{10,11... | collective-permute-start | bytes 393224 | tf_op jit(solution)/shard_map/got0/ppermute | solution.py:64
  26.9 2.0 %collective-permute-done.2.refs_7_ = bf16[32,4096]{1,0:T(8,128)(2,1)S(1)} collective-permute-done((bf16[32,4096]{1,0:T(8,128)(2,1)S(1)}, bf16[32,4096]{1,0:T(8,128)(2,1)S(1)}, u32[]{:S(2)}, u32[]{:S(2)}) %collective-permute-start.2) | collective-permute-done | bytes 262176 | tf_op jit(solution)/shard_map/cross/ppermute | solution.py:64
  29.8 1.5 %collective-permute-start.15 = (bf16[16,4096]{1,0:T(8,128)(2,1)S(1)}, bf16[16,4096]{1,0:T(8,128)(2,1)S(1)}, u32[]{:S(2)}, u32[]{:S(2)}) collective-permute-start(bf16[16,4096]{1,0:T(8,128)(2,1)S(1)} %get-tuple-element.55), channel_id=1, source_target_pairs={{0,4},{1,5},{2,6},{3,7},{4,0},{5,1},{6,2},{7,3},{8,12},{9,13},{10,... | collective-permute-start | bytes 393224 | tf_op jit(solution)/shard_map/cross_pb/ppermute | solution.py:64
  31.3 1.5 %collective-permute-start.7 = (bf16[16,4096]{1,0:T(8,128)(2,1)S(1)}, bf16[16,4096]{1,0:T(8,128)(2,1)S(1)}, u32[]{:S(2)}, u32[]{:S(2)}) collective-permute-start(bf16[16,4096]{1,0:T(8,128)(2,1)S(1)} %slice.10), channel_id=1, source_target_pairs={{0,16},{1,17},{2,18},{3,19},{4,20},{5,21},{6,22},{7,23},{8,24},{9,... | collective-permute-start | bytes 393224 | tf_op jit(solution)/shard_map/cross_pa/ppermute | solution.py:64
  32.8 2.5 %shard_map.85 = (f32[128,1024]{1,0:T(8,128)S(1)}, bf16[128,1024]{1,0:T(8,128)(2,1)S(1)}, f32[128,1024]{1,0:T(8,128)S(1)}) custom-call(f32[8,256]{1,0:T(8,128)S(1)} %get-tuple-element.32.weight_ref, bf16[1024,4096]{1,0:T(8,128)(2,1)S(1)} %get-tuple-element.33.train_ref, bf16[32,4096]{1,0:T(8,128)(2,1)S(1)} %collective-permute-done.1.refs_0_, ...), custom_call_target="tpu_custom_call" | custom-call | tf_op jit(solution)/shard_map/pallas_call | solution.py:221
  35.3 1.6 %collective-permute-start.19 = (bf16[128,1024]{1,0:T(8,128)(2,1)S(1)}, bf16[128,1024]{1,0:T(8,128)(2,1)S(1)}, u32[]{:S(2)}, u32[]{:S(2)}) collective-permute-start(bf16[128,1024]{1,0:T(8,128)(2,1)S(1)} %get-tuple-element.47), channel_id=1, source_target_pairs={{0,1},{1,0},{2,3},{3,2},{4,5},{5,4},{6,7},{7,6},{8,9},{9,8},{10,11... | collective-permute-start | bytes 786440 | tf_op jit(solution)/shard_map/got1/ppermute | solution.py:64
  36.9 0.5 %collective-permute-start.16 = (bf16[16,4096]{1,0:T(8,128)(2,1)S(1)}, bf16[16,4096]{1,0:T(8,128)(2,1)S(1)}, u32[]{:S(2)}, u32[]{:S(2)}) collective-permute-start(bf16[16,4096]{1,0:T(8,128)(2,1)S(1)} %collective-permute-done.7.refs_0_), channel_id=1, source_target_pairs={{0,2},{1,3},{2,0},{3,1},{4,6},{5,7},{6,4},{7,5},{8,10},{9,11},{10,... | collective-permute-start | bytes 393224 | tf_op jit(solution)/shard_map/cross_pxa/ppermute | solution.py:64
  37.4 0.8 %collective-permute-done.17.refs_3_ = bf16[16,4096]{1,0:T(8,128)(2,1)S(1)} collective-permute-done((bf16[16,4096]{1,0:T(8,128)(2,1)S(1)}, bf16[16,4096]{1,0:T(8,128)(2,1)S(1)}, u32[]{:S(2)}, u32[]{:S(2)}) %collective-permute-start.17) | collective-permute-done | bytes 131104 | tf_op jit(solution)/shard_map/cross_pxb/ppermute | solution.py:64
  38.5 2.4 %shard_map.86 = (bf16[64,1024]{1,0:T(8,128)(2,1)S(1)}, f32[64,1024]{1,0:T(8,128)S(1)}) custom-call(f32[8,256]{1,0:T(8,128)S(1)} %get-tuple-element.32.weight_ref, bf16[1024,4096]{1,0:T(8,128)(2,1)S(1)} %get-tuple-element.33.train_ref, bf16[16,4096]{1,0:T(8,128)(2,1)S(1)} %collective-permute-done.7.refs_0_, ...), custom_call_target="tpu_custom_call" | custom-call | tf_op jit(solution)/shard_map/pallas_call | solution.py:221
  40.9 1.0 %collective-permute-start.18 = (bf16[64,1024]{1,0:T(8,128)(2,1)S(1)}, bf16[64,1024]{1,0:T(8,128)(2,1)S(1)}, u32[]{:S(2)}, u32[]{:S(2)}) collective-permute-start(bf16[64,1024]{1,0:T(8,128)(2,1)S(1)} %get-tuple-element.52), channel_id=1, source_target_pairs={{0,1},{1,0},{2,3},{3,2},{4,5},{5,4},{6,7},{7,6},{8,9},{9,8},{10,11... | collective-permute-start | bytes 393224 | tf_op jit(solution)/shard_map/got2/ppermute | solution.py:64
  42.0 1.2 %collective-permute-done.19.refs_3_ = bf16[128,1024]{1,0:T(8,128)(2,1)S(1)} collective-permute-done((bf16[128,1024]{1,0:T(8,128)(2,1)S(1)}, bf16[128,1024]{1,0:T(8,128)(2,1)S(1)}, u32[]{:S(2)}, u32[]{:S(2)}) %collective-permute-start.19) | collective-permute-done | bytes 262176 | tf_op jit(solution)/shard_map/got1/ppermute | solution.py:64
  43.1 1.0 %shard_map.87.refs_2_ = f32[256,1024]{1,0:T(8,128)} custom-call(s32[1,1024]{1,0:T(1,128)S(1)} %bitcast.6, s32[256,1]{1,0:T(8,128)S(1)} %copy.11.query_ids, f32[64,1024]{1,0:T(8,128)S(1)} %get-tuple-element.53.refs_0_, bf16[64,1024]{1,0:T(8,128)(2,1)S(1)} %collective-permute-done.14.refs_1_, f32[128,1024]{1,0:T(8,128)S(1)} %get-tuple-element.54.refs_2_, ...), custom_call_target="tpu_custom_call" | custom-call | tf_op jit(solution)/shard_map/pallas_call | solution.py:282
  44.2 2.5 %collective-permute-done.18.refs_1_ = bf16[64,1024]{1,0:T(8,128)(2,1)S(1)} collective-permute-done((bf16[64,1024]{1,0:T(8,128)(2,1)S(1)}, bf16[64,1024]{1,0:T(8,128)(2,1)S(1)}, u32[]{:S(2)}, u32[]{:S(2)}) %collective-permute-start.18) | collective-permute-done | bytes 131104 | tf_op jit(solution)/shard_map/got2/ppermute | solution.py:64
  46.6 0.8 %shard_map.88 = f32[256,1024]{1,0:T(8,128)} custom-call(s32[1,1024]{1,0:T(1,128)S(1)} %bitcast.7, s32[256,1]{1,0:T(8,128)S(1)} %copy.11.query_ids, f32[64,1024]{1,0:T(8,128)S(1)} %get-tuple-element.51.refs_0_, bf16[64,1024]{1,0:T(8,128)(2,1)S(1)} %collective-permute-done.18.refs_1_, f32[256,1024]{1,0:T(8,128)} %shard_map.87.refs_2_), custom_call_target="tpu_custom_call", output_to_operand_aliasing={{}: (4, {})} | custom-call | tf_op jit(solution)/shard_map/pallas_call | solution.py:282
  (30 shorter events, 1.8 us)
Async XLA Ops:
  2.8 11.1 %collective-permute-start.1 = (bf16[32,4096]{1,0:T(8,128)(2,1)S(1)}, bf16[32,4096]{1,0:T(8,128)(2,1)S(1)}, u32[]{:S(2)}, u32[]{:S(2)}) collective-permute-start(bf16[32,4096]{1,0:T(8,128)(2,1)S(1)} %get-tuple-element.38.refs_0_), channel_id=1, source_target_pairs={{0,4},{1,5},{2,6},{3,7},{4,0},{5,1},{6,2},{7,3},{8,12},{9,13},{10,... | collective-permute-start | bytes 786440 | tf_op jit(solution)/shard_map/near/ppermute | solution.py:64
  5.9 14.2 %collective-permute-start = (bf16[32,4096]{1,0:T(8,128)(2,1)S(1)}, bf16[32,4096]{1,0:T(8,128)(2,1)S(1)}, u32[]{:S(2)}, u32[]{:S(2)}) collective-permute-start(bf16[32,4096]{1,0:T(8,128)(2,1)S(1)} %get-tuple-element.38.refs_0_), channel_id=1, source_target_pairs={{0,12},{1,13},{2,14},{3,15},{4,8},{5,9},{6,10},{7,11},{8,4},{9,5},... | collective-permute-start | bytes 786440 | tf_op jit(solution)/shard_map/far/ppermute | solution.py:64
  13.3 6.8 %collective-permute-start.3 = (bf16[32,4096]{1,0:T(8,128)(2,1)S(1)}, bf16[32,4096]{1,0:T(8,128)(2,1)S(1)}, u32[]{:S(2)}, u32[]{:S(2)}) collective-permute-start(bf16[32,4096]{1,0:T(8,128)(2,1)S(1)} %get-tuple-element.38.refs_0_), channel_id=1, source_target_pairs={{0,2},{1,3},{2,0},{3,1},{4,6},{5,7},{6,4},{7,5},{8,10},{9,11},{10,... | collective-permute-start | bytes 786440 | tf_op jit(solution)/shard_map/mine_x/ppermute | solution.py:64
  13.4 6.7 %collective-permute-start.4 = (bf16[32,4096]{1,0:T(8,128)(2,1)S(1)}, bf16[32,4096]{1,0:T(8,128)(2,1)S(1)}, u32[]{:S(2)}, u32[]{:S(2)}) collective-permute-start(bf16[32,4096]{1,0:T(8,128)(2,1)S(1)} %get-tuple-element.35.refs_2_), channel_id=1, source_target_pairs={{0,2},{1,3},{2,0},{3,1},{4,6},{5,7},{6,4},{7,5},{8,10},{9,11},{10,... | collective-permute-start | bytes 786440 | tf_op jit(solution)/shard_map/rest_x/ppermute | solution.py:64
  13.9 8.4 %collective-permute-start.9 = (bf16[32,4096]{1,0:T(8,128)(2,1)S(1)}, bf16[32,4096]{1,0:T(8,128)(2,1)S(1)}, u32[]{:S(2)}, u32[]{:S(2)}) collective-permute-start(bf16[32,4096]{1,0:T(8,128)(2,1)S(1)} %collective-permute-done.1.refs_0_), channel_id=1, source_target_pairs={{0,16},{1,17},{2,18},{3,19},{4,20},{5,21},{6,22},{7,23},{8,24},{9,... | collective-permute-start | bytes 786440 | tf_op jit(solution)/shard_map/near_p/ppermute | solution.py:64
  20.1 2.7 %collective-permute-start.5 = (bf16[32,4096]{1,0:T(8,128)(2,1)S(1)}, bf16[32,4096]{1,0:T(8,128)(2,1)S(1)}, u32[]{:S(2)}, u32[]{:S(2)}) collective-permute-start(bf16[32,4096]{1,0:T(8,128)(2,1)S(1)} %collective-permute-done.refs_4_), channel_id=1, source_target_pairs={{0,2},{1,3},{2,0},{3,1},{4,6},{5,7},{6,4},{7,5},{8,10},{9,11},{10,... | collective-permute-start | bytes 786440 | tf_op jit(solution)/shard_map/far_x/ppermute | solution.py:64
  20.1 8.7 %collective-permute-start.2 = (bf16[32,4096]{1,0:T(8,128)(2,1)S(1)}, bf16[32,4096]{1,0:T(8,128)(2,1)S(1)}, u32[]{:S(2)}, u32[]{:S(2)}) collective-permute-start(bf16[32,4096]{1,0:T(8,128)(2,1)S(1)} %collective-permute-done.refs_4_), channel_id=1, source_target_pairs={{0,4},{1,5},{2,6},{3,7},{4,0},{5,1},{6,2},{7,3},{8,12},{9,13},{10,... | collective-permute-start | bytes 786440 | tf_op jit(solution)/shard_map/cross/ppermute | solution.py:64
  20.8 8.4 %collective-permute-start.11 = (bf16[32,4096]{1,0:T(8,128)(2,1)S(1)}, bf16[32,4096]{1,0:T(8,128)(2,1)S(1)}, u32[]{:S(2)}, u32[]{:S(2)}) collective-permute-start(bf16[32,4096]{1,0:T(8,128)(2,1)S(1)} %collective-permute-done.refs_4_), channel_id=1, source_target_pairs={{0,16},{1,17},{2,18},{3,19},{4,20},{5,21},{6,22},{7,23},{8,24},{9,... | collective-permute-start | bytes 786440 | tf_op jit(solution)/shard_map/far_p/ppermute | solution.py:64
  22.3 6.9 %collective-permute-start.8 = (bf16[32,4096]{1,0:T(8,128)(2,1)S(1)}, bf16[32,4096]{1,0:T(8,128)(2,1)S(1)}, u32[]{:S(2)}, u32[]{:S(2)}) collective-permute-start(bf16[32,4096]{1,0:T(8,128)(2,1)S(1)} %collective-permute-done.1.refs_0_), channel_id=1, source_target_pairs={{0,2},{1,3},{2,0},{3,1},{4,6},{5,7},{6,4},{7,5},{8,10},{9,11},{10,... | collective-permute-start | bytes 786440 | tf_op jit(solution)/shard_map/near_x/ppermute | solution.py:64
  22.3 6.9 %collective-permute-start.10 = (bf16[32,4096]{1,0:T(8,128)(2,1)S(1)}, bf16[32,4096]{1,0:T(8,128)(2,1)S(1)}, u32[]{:S(2)}, u32[]{:S(2)}) collective-permute-start(bf16[32,4096]{1,0:T(8,128)(2,1)S(1)} %collective-permute-done.9.refs_2_), channel_id=1, source_target_pairs={{0,2},{1,3},{2,0},{3,1},{4,6},{5,7},{6,4},{7,5},{8,10},{9,11},{10,... | collective-permute-start | bytes 786440 | tf_op jit(solution)/shard_map/near_px/ppermute | solution.py:64
  25.3 7.5 %collective-permute-start.14 = (bf16[64,1024]{1,0:T(8,128)(2,1)S(1)}, bf16[64,1024]{1,0:T(8,128)(2,1)S(1)}, u32[]{:S(2)}, u32[]{:S(2)}) collective-permute-start(bf16[64,1024]{1,0:T(8,128)(2,1)S(1)} %get-tuple-element.41), channel_id=1, source_target_pairs={{0,1},{1,0},{2,3},{3,2},{4,5},{5,4},{6,7},{7,6},{8,9},{9,8},{10,11... | collective-permute-start | bytes 393224 | tf_op jit(solution)/shard_map/got0/ppermute | solution.py:64
  28.9 2.4 %collective-permute-start.6 = (bf16[32,4096]{1,0:T(8,128)(2,1)S(1)}, bf16[32,4096]{1,0:T(8,128)(2,1)S(1)}, u32[]{:S(2)}, u32[]{:S(2)}) collective-permute-start(bf16[32,4096]{1,0:T(8,128)(2,1)S(1)} %collective-permute-done.2.refs_7_), channel_id=1, source_target_pairs={{0,2},{1,3},{2,0},{3,1},{4,6},{5,7},{6,4},{7,5},{8,10},{9,11},{10,... | collective-permute-start | bytes 786440 | tf_op jit(solution)/shard_map/cross_x/ppermute | solution.py:64
  29.2 3.6 %collective-permute-start.12 = (bf16[16,4096]{1,0:T(8,128)(2,1)S(1)}, bf16[16,4096]{1,0:T(8,128)(2,1)S(1)}, u32[]{:S(2)}, u32[]{:S(2)}) collective-permute-start(bf16[16,4096]{1,0:T(8,128)(2,1)S(1)} %get-tuple-element.56), channel_id=1, source_target_pairs={{0,2},{1,3},{2,0},{3,1},{4,6},{5,7},{6,4},{7,5},{8,10},{9,11},{10,... | collective-permute-start | bytes 393224 | tf_op jit(solution)/shard_map/far_px0/ppermute | solution.py:64
  29.5 3.3 %collective-permute-start.13 = (bf16[16,4096]{1,0:T(8,128)(2,1)S(1)}, bf16[16,4096]{1,0:T(8,128)(2,1)S(1)}, u32[]{:S(2)}, u32[]{:S(2)}) collective-permute-start(bf16[16,4096]{1,0:T(8,128)(2,1)S(1)} %get-tuple-element.55), channel_id=1, source_target_pairs={{0,2},{1,3},{2,0},{3,1},{4,6},{5,7},{6,4},{7,5},{8,10},{9,11},{10,... | collective-permute-start | bytes 393224 | tf_op jit(solution)/shard_map/far_px1/ppermute | solution.py:64
  29.8 7.2 %collective-permute-start.15 = (bf16[16,4096]{1,0:T(8,128)(2,1)S(1)}, bf16[16,4096]{1,0:T(8,128)(2,1)S(1)}, u32[]{:S(2)}, u32[]{:S(2)}) collective-permute-start(bf16[16,4096]{1,0:T(8,128)(2,1)S(1)} %get-tuple-element.55), channel_id=1, source_target_pairs={{0,4},{1,5},{2,6},{3,7},{4,0},{5,1},{6,2},{7,3},{8,12},{9,13},{10,... | collective-permute-start | bytes 393224 | tf_op jit(solution)/shard_map/cross_pb/ppermute | solution.py:64
  31.3 5.6 %collective-permute-start.7 = (bf16[16,4096]{1,0:T(8,128)(2,1)S(1)}, bf16[16,4096]{1,0:T(8,128)(2,1)S(1)}, u32[]{:S(2)}, u32[]{:S(2)}) collective-permute-start(bf16[16,4096]{1,0:T(8,128)(2,1)S(1)} %slice.10), channel_id=1, source_target_pairs={{0,16},{1,17},{2,18},{3,19},{4,20},{5,21},{6,22},{7,23},{8,24},{9,... | collective-permute-start | bytes 393224 | tf_op jit(solution)/shard_map/cross_pa/ppermute | solution.py:64
  32.8 9.0 %copy-start.1 = (s32[256]{0:T(256)S(1)}, s32[256]{0:T(256)}, u32[]{:S(2)}) copy-start(s32[256]{0:T(256)} %param.15) | copy-start | bytes 3076
  32.8 10.3 %copy-start = (s32[1024]{0:T(1024)S(1)}, s32[1024]{0:T(1024)}, u32[]{:S(2)}) copy-start(s32[1024]{0:T(1024)} %param.14) | copy-start | bytes 12292
  35.3 7.8 %collective-permute-start.19 = (bf16[128,1024]{1,0:T(8,128)(2,1)S(1)}, bf16[128,1024]{1,0:T(8,128)(2,1)S(1)}, u32[]{:S(2)}, u32[]{:S(2)}) collective-permute-start(bf16[128,1024]{1,0:T(8,128)(2,1)S(1)} %get-tuple-element.47), channel_id=1, source_target_pairs={{0,1},{1,0},{2,3},{3,2},{4,5},{5,4},{6,7},{7,6},{8,9},{9,8},{10,11... | collective-permute-start | bytes 786440 | tf_op jit(solution)/shard_map/got1/ppermute | solution.py:64
  36.9 1.3 %collective-permute-start.17 = (bf16[16,4096]{1,0:T(8,128)(2,1)S(1)}, bf16[16,4096]{1,0:T(8,128)(2,1)S(1)}, u32[]{:S(2)}, u32[]{:S(2)}) collective-permute-start(bf16[16,4096]{1,0:T(8,128)(2,1)S(1)} %collective-permute-done.15.refs_1_), channel_id=1, source_target_pairs={{0,2},{1,3},{2,0},{3,1},{4,6},{5,7},{6,4},{7,5},{8,10},{9,11},{10,... | collective-permute-start | bytes 393224 | tf_op jit(solution)/shard_map/cross_pxb/ppermute | solution.py:64
  36.9 1.5 %collective-permute-start.16 = (bf16[16,4096]{1,0:T(8,128)(2,1)S(1)}, bf16[16,4096]{1,0:T(8,128)(2,1)S(1)}, u32[]{:S(2)}, u32[]{:S(2)}) collective-permute-start(bf16[16,4096]{1,0:T(8,128)(2,1)S(1)} %collective-permute-done.7.refs_0_), channel_id=1, source_target_pairs={{0,2},{1,3},{2,0},{3,1},{4,6},{5,7},{6,4},{7,5},{8,10},{9,11},{10,... | collective-permute-start | bytes 393224 | tf_op jit(solution)/shard_map/cross_pxa/ppermute | solution.py:64
  40.9 5.8 %collective-permute-start.18 = (bf16[64,1024]{1,0:T(8,128)(2,1)S(1)}, bf16[64,1024]{1,0:T(8,128)(2,1)S(1)}, u32[]{:S(2)}, u32[]{:S(2)}) collective-permute-start(bf16[64,1024]{1,0:T(8,128)(2,1)S(1)} %get-tuple-element.52), channel_id=1, source_target_pairs={{0,1},{1,0},{2,3},{3,2},{4,5},{5,4},{6,7},{7,6},{8,9},{9,8},{10,11... | collective-permute-start | bytes 393224 | tf_op jit(solution)/shard_map/got2/ppermute | solution.py:64

commit v17 on v15

--- a/solution.py
+++ b/solution.py
@@ -68,7 +68,7 @@
 to_core = functools.partial(permute, target=lambda p, z, c, l: (p, z, 1 - c, l))
 to_layer = functools.partial(permute, target=lambda p, z, c, l: (p, z, c, 1 - l))
 to_near = functools.partial(permute, target=lambda p, z, c, l: (p, z ^ 1, c, l))
-to_far = functools.partial(permute, target=lambda p, z, c, l: (p, z ^ 3, c, l))
+to_middle = functools.partial(permute, target=lambda p, z, c, l: (p, z ^ 3 if 0 < z < 3 else z, c, l))
 
 
 def after(value, *others):
@@ -254,7 +254,8 @@
     *_, out, done, sems = refs
     part, z, core, layer = place()
     low = z % 2
-    first = jnp.where(z // 2 == layer, low, 1 - low)
+    inner = (z + 1) // 2 == 1
+    first = jnp.where((z // 2 == layer) | ~inner, low, 1 - low)
     copies = []
     for k, (which, keep, got, row, column) in enumerate(groups):
         block = first if which < 2 else 1 - first
@@ -320,7 +321,7 @@
         ],
     )
     near = to_near(mine, "near")
-    far = to_far(mine, "far")
+    middle = to_middle(mine, "middle")
     rest, train, weight = kernel_call(
         rest_kernel,
         [shape((HALF, width), bf16), shape(train.shape, bf16), shape((8, STEP), f32)],
@@ -336,13 +337,16 @@
     mine_x = to_core(after(mine, rest), "mine_x")
     rest_x = to_core(rest, "rest_x")
     near = after(near, rest)
+    near_p = to_part(near, "near_p")
+    middle_near = to_middle(near, "middle_near")
+    outward = to_near(after(middle, near), "outward")
+    inner = (place()[1] + 1) // 2 == 1
     near_x = to_core(near, "near_x")
-    near_p = to_part(near, "near_p")
-    far = after(far, near)
-    cross = to_near(far, "cross")
+    far = jnp.where(inner, middle, outward)
     far_p = to_part(far, "far_p")
+    outward_near = to_near(after(middle_near, far), "outward_near")
+    cross = jnp.where(inner, middle_near, outward_near)
     far_x = to_core(after(far, rest_x), "far_x")
-    mine_x = after(mine_x, far)
     (early0,) = score(rows_of(mine, mine_x, rest, rest_x), stored=128)
     send0, keep0 = score(rows_of(far, far_x), early=[(early0, 0, 64)])
     got0 = to_layer(send0, "got0")
@@ -351,8 +355,7 @@
     near_px = to_core(near_p, "near_px")
     far_p, cross = after(far_p, near_px, send0), after(cross, send0)
     far_px = to_core(far_p, "far_px")
-    cross_pa = to_part(cross[:CHUNK], "cross_pa")
-    cross_pb = to_near(far_p[CHUNK:], "cross_pb")
+    cross_p = to_part(cross, "cross_p")
     cross_x = to_core(cross, "cross_x")
     early1, send1, keep1 = score(
         rows_of(near, near_x, near_p, near_px, far_p, far_px, cross, cross_x),
@@ -360,10 +363,10 @@
         early=[(early0, 64, 64), (None, 0, 64)],
     )
     got1 = to_layer(send1, "got1")
-    cross_pa, cross_pb = after(cross_pa, send1, got0), after(cross_pb, send1, got0)
-    cross_pxa = to_core(cross_pa, "cross_pxa")
-    cross_pxb = to_core(cross_pb, "cross_pxb")
-    last = rows_of(cross_pa, cross_pb, cross_pxa, cross_pxb)
+    cross_p = after(cross_p, send1, got0)
+    cross_pxa = to_core(cross_p[:CHUNK], "cross_pxa")
+    cross_pxb = to_core(cross_p[CHUNK:], "cross_pxb")
+    last = rows_of(cross_p, cross_pxa, cross_pxb)
     send2, keep2 = score(last, early=[(early1, 64, 64)])
     got2 = to_layer(send2, "got2")
 

time: 47.1 us -> 56.8 us (1.21)
  local copies, waits for them, and re-layouts: 0.16 us -> 6.81 us
  starting transfers between devices: 15 us -> 20.1 us
  waiting for transfers between devices: 12.4 us -> 10.1 us
    unnamed x4 -> x10, local copies, waits for them, and re-layouts: 0.01 us -> 6.66 us
    ppermute x19 -> x20, starting transfers between devices: 15 us -> 20.1 us  [permute(): return lax.ppermute(value, AXES, pairs)]
    ppermute x19 -> x20, waiting for transfers between devices: 12.4 us -> 10.1 us  [permute(): return lax.ppermute(value, AXES, pairs)]
  transfers between devices with their start and end apart: 19 -> 20, of which waited for: 8 -> 7; matrix products, arithmetic and copies ran while one was open for 0% -> 0% of each run, Pallas kernels for 32% -> 27%
where the time goes in v17:
time: 56.8 us; the launch traced here: 56.6 us
  starting transfers between devices  20.1 us (35%)
  Pallas kernels  18.6 us (33%)
  waiting for transfers between devices  10.1 us (18%)
  local copies, waits for them, and re-layouts  6.81 us (12%)
  between operations  0.85 us (1%)
    ppermute x20, starting transfers between devices, permute(): return lax.ppermute(value, AXES, pairs)  20.1 us
    pallas_call x6, Pallas kernels, kernel_call(): pl.pallas_call(kernel, out_shape=outs, in_specs=specs or [VMEM] * len(inp...  16.8 us
    ppermute x20, waiting for transfers between devices, permute(): return lax.ppermute(value, AXES, pairs)  10.1 us
    unnamed x10, local copies, waits for them, and re-layouts  6.66 us
    pallas_call x2, Pallas kernels, call_final(): pl.pallas_call(functools.partial(final_kernel, groups=groups, n_given=len...  1.86 us
  transfers between devices with their start and end apart: 20, of which 7 were waited for; matrix products, arithmetic and copies ran while one was open for 0% of the time, Pallas kernels for 27%

profile of v17, /device:TPU:0, one launch (start us, length us, event | category | flops | bytes accessed | tf_op | source)
XLA Modules:
  0.0 56.6 jit_solution(2349721761059787640)
XLA Ops:
  0.0 2.8 %shard_map.82 = (bf16[32,4096]{1,0:T(8,128)(2,1)S(1)}, bf16[2,256,256]{2,1,0:T(8,128)(2,1)S(1)}, bf16[2,256,512]{2,1,0:T(8,128)(2,1)S(1)}) custom-call(bf16[64,4096]{1,0:T(8,128)(2,1)} %bitcast.9, f32[64,64]{1,0:T(8,128)} %bitcast.11, f32[64,64]{1,0:T(8,128)} %bitcast.12), custom_call_target="tpu_custom_call" | custom-call | tf_op jit(solution)/shard_map/pallas_call | solution.py:221
  2.8 3.1 %collective-permute-start = (bf16[32,4096]{1,0:T(8,128)(2,1)S(1)}, bf16[32,4096]{1,0:T(8,128)(2,1)S(1)}, u32[]{:S(2)}, u32[]{:S(2)}) collective-permute-start(bf16[32,4096]{1,0:T(8,128)(2,1)S(1)} %get-tuple-element.37.refs_0_), channel_id=1, source_target_pairs={{0,4},{1,5},{2,6},{3,7},{4,0},{5,1},{6,2},{7,3},{8,12},{9,13},{10,... | collective-permute-start | bytes 786440 | tf_op jit(solution)/shard_map/near/ppermute | solution.py:64
  5.9 0.7 %collective-permute-start.2 = (bf16[32,4096]{1,0:T(8,128)(2,1)S(1)}, bf16[32,4096]{1,0:T(8,128)(2,1)S(1)}, u32[]{:S(2)}, u32[]{:S(2)}) collective-permute-start(bf16[32,4096]{1,0:T(8,128)(2,1)S(1)} %get-tuple-element.37.refs_0_), channel_id=1, source_target_pairs={{0,0},{1,1},{2,2},{3,3},{4,8},{5,9},{6,10},{7,11},{8,4},{9,5},{10,... | collective-permute-start | bytes 786440 | tf_op jit(solution)/shard_map/middle/ppermute | solution.py:64
  7.2 4.3 %shard_map.83 = (bf16[32,4096]{1,0:T(8,128)(2,1)S(1)}, bf16[1024,4096]{1,0:T(8,128)(2,1)S(1)}, f32[8,256]{1,0:T(8,128)S(1)}) custom-call(f32[2]{0:T(128)} %weight_ref.1, s32[1]{0:T(128)S(6)} %copy.13.layer_ref, bf16[64,4096]{1,0:T(8,128)(2,1)} %bitcast.10, bf16[1024,4096]{1,0:T(8,128)(2,1)} %bitcast.8, bf16[2,256,256]{2,1,0:T(8,128)(2,1)S(1)} %get-tuple-element.27.lefts_ref, ...), custom_call_target="tpu_custom_call" | custom-call | tf_op jit(solution)/shard_map/pallas_call | solution.py:221
  11.5 3.3 %copy-done = bf16[1024,4096]{1,0:T(8,128)(2,1)} copy-done((bf16[1024,4096]{1,0:T(8,128)(2,1)}, bf16[1024,4096]{1,0:T(8,128)(2,1)S(1)}, u32[]{:S(2)}) %copy-start) | copy-done | bytes 8388632
  15.3 4.4 %collective-permute-start.3 = (bf16[32,4096]{1,0:T(8,128)(2,1)S(1)}, bf16[32,4096]{1,0:T(8,128)(2,1)S(1)}, u32[]{:S(2)}, u32[]{:S(2)}) collective-permute-start(bf16[32,4096]{1,0:T(8,128)(2,1)S(1)} %collective-permute-done.2), channel_id=1, source_target_pairs={{0,4},{1,5},{2,6},{3,7},{4,0},{5,1},{6,2},{7,3},{8,12},{9,13},{10,... | collective-permute-start | bytes 786440 | tf_op jit(solution)/shard_map/outward/ppermute | solution.py:64
  19.7 1.5 %collective-permute-start.10 = (bf16[32,4096]{1,0:T(8,128)(2,1)S(1)}, bf16[32,4096]{1,0:T(8,128)(2,1)S(1)}, u32[]{:S(2)}, u32[]{:S(2)}) collective-permute-start(bf16[32,4096]{1,0:T(8,128)(2,1)S(1)} %collective-permute-done.refs_0_), channel_id=1, source_target_pairs={{0,16},{1,17},{2,18},{3,19},{4,20},{5,21},{6,22},{7,23},{8,24},{9,... | collective-permute-start | bytes 786440 | tf_op jit(solution)/shard_map/near_p/ppermute | solution.py:64
  21.9 3.4 %copy-done.1 = bf16[1024,4096]{1,0:T(8,128)(2,1)S(1)} copy-done((bf16[1024,4096]{1,0:T(8,128)(2,1)S(1)}, bf16[1024,4096]{1,0:T(8,128)(2,1)}, u32[]{:S(2)}) %copy-start.1) | copy-done | bytes 8388632
  25.3 2.4 %shard_map.84.refs_2_.refs_8_ = f32[128,1024]{1,0:T(8,128)S(1)} custom-call(f32[8,256]{1,0:T(8,128)S(1)} %get-tuple-element.29.weight_ref, bf16[1024,4096]{1,0:T(8,128)(2,1)S(1)} %copy-done.1, bf16[32,4096]{1,0:T(8,128)(2,1)S(1)} %get-tuple-element.37.refs_0_, bf16[32,4096]{1,0:T(8,128)(2,1)S(1)} %collective-permute-done.7.refs_1_, ...), custom_call_target="tpu_custom_call" | custom-call | tf_op jit(solution)/shard_map/pallas_call | solution.py:221
  28.8 2.3 %collective-permute-start.4 = (bf16[32,4096]{1,0:T(8,128)(2,1)S(1)}, bf16[32,4096]{1,0:T(8,128)(2,1)S(1)}, u32[]{:S(2)}, u32[]{:S(2)}) collective-permute-start(bf16[32,4096]{1,0:T(8,128)(2,1)S(1)} %collective-permute-done.1), channel_id=1, source_target_pairs={{0,4},{1,5},{2,6},{3,7},{4,0},{5,1},{6,2},{7,3},{8,12},{9,13},{10,... | collective-permute-start | bytes 786440 | tf_op jit(solution)/shard_map/outward_near/ppermute | solution.py:64
  31.2 2.4 %shard_map.85 = (bf16[64,1024]{1,0:T(8,128)(2,1)S(1)}, f32[64,1024]{1,0:T(8,128)S(1)}) custom-call(f32[8,256]{1,0:T(8,128)S(1)} %get-tuple-element.29.weight_ref, bf16[1024,4096]{1,0:T(8,128)(2,1)S(1)} %copy-done.2, bf16[32,4096]{1,0:T(8,128)(2,1)S(1)} %broadcast_select_fusion.1.refs_0_, bf16[32,4096]{1,0:T(8,128)(2,1)S(1)} %collective-permute-done.6.refs_1_, ...), custom_call_target="tpu_custom_call" | custom-call | tf_op jit(solution)/shard_map/pallas_call | solution.py:221
  33.6 1.9 %collective-permute-done.12.refs_4_ = bf16[32,4096]{1,0:T(8,128)(2,1)S(1)} collective-permute-done((bf16[32,4096]{1,0:T(8,128)(2,1)S(1)}, bf16[32,4096]{1,0:T(8,128)(2,1)S(1)}, u32[]{:S(2)}, u32[]{:S(2)}) %collective-permute-start.12) | collective-permute-done | bytes 262176 | tf_op jit(solution)/shard_map/far_p/ppermute | solution.py:64
  35.5 1.6 %collective-permute-done.4 = bf16[32,4096]{1,0:T(8,128)(2,1)S(1)} collective-permute-done((bf16[32,4096]{1,0:T(8,128)(2,1)S(1)}, bf16[32,4096]{1,0:T(8,128)(2,1)S(1)}, u32[]{:S(2)}, u32[]{:S(2)}) %collective-permute-start.4) | collective-permute-done | bytes 262176 | tf_op jit(solution)/shard_map/outward_near/ppermute | solution.py:64
  37.3 1.6 %collective-permute-start.8 = (bf16[32,4096]{1,0:T(8,128)(2,1)S(1)}, bf16[32,4096]{1,0:T(8,128)(2,1)S(1)}, u32[]{:S(2)}, u32[]{:S(2)}) collective-permute-start(bf16[32,4096]{1,0:T(8,128)(2,1)S(1)} %broadcast_select_fusion.refs_6_), channel_id=1, source_target_pairs={{0,16},{1,17},{2,18},{3,19},{4,20},{5,21},{6,22},{7,23},{8,24},{9,... | collective-permute-start | bytes 786440 | tf_op jit(solution)/shard_map/cross_p/ppermute | solution.py:64
  38.8 1.5 %collective-permute-start.15 = (bf16[64,1024]{1,0:T(8,128)(2,1)S(1)}, bf16[64,1024]{1,0:T(8,128)(2,1)S(1)}, u32[]{:S(2)}, u32[]{:S(2)}) collective-permute-start(bf16[64,1024]{1,0:T(8,128)(2,1)S(1)} %get-tuple-element.38), channel_id=1, source_target_pairs={{0,1},{1,0},{2,3},{3,2},{4,5},{5,4},{6,7},{7,6},{8,9},{9,8},{10,11... | collective-permute-start | bytes 393224 | tf_op jit(solution)/shard_map/got0/ppermute | solution.py:64
  40.4 2.5 %shard_map.86 = (f32[128,1024]{1,0:T(8,128)S(1)}, bf16[128,1024]{1,0:T(8,128)(2,1)S(1)}, f32[128,1024]{1,0:T(8,128)S(1)}) custom-call(f32[8,256]{1,0:T(8,128)S(1)} %get-tuple-element.29.weight_ref, bf16[1024,4096]{1,0:T(8,128)(2,1)S(1)} %copy-done.2, bf16[32,4096]{1,0:T(8,128)(2,1)S(1)} %collective-permute-done.refs_0_, ...), custom_call_target="tpu_custom_call" | custom-call | tf_op jit(solution)/shard_map/pallas_call | solution.py:221
  43.4 1.0 %collective-permute-done.15.refs_1_ = bf16[64,1024]{1,0:T(8,128)(2,1)S(1)} collective-permute-done((bf16[64,1024]{1,0:T(8,128)(2,1)S(1)}, bf16[64,1024]{1,0:T(8,128)(2,1)S(1)}, u32[]{:S(2)}, u32[]{:S(2)}) %collective-permute-start.15) | collective-permute-done | bytes 131104 | tf_op jit(solution)/shard_map/got0/ppermute | solution.py:64
  44.4 1.6 %collective-permute-done.8.refs_0_ = bf16[32,4096]{1,0:T(8,128)(2,1)S(1)} collective-permute-done((bf16[32,4096]{1,0:T(8,128)(2,1)S(1)}, bf16[32,4096]{1,0:T(8,128)(2,1)S(1)}, u32[]{:S(2)}, u32[]{:S(2)}) %collective-permute-start.8) | collective-permute-done | bytes 262176 | tf_op jit(solution)/shard_map/cross_p/ppermute | solution.py:64
  46.6 0.8 %collective-permute-done.16.refs_1_ = bf16[16,4096]{1,0:T(8,128)(2,1)S(1)} collective-permute-done((bf16[16,4096]{1,0:T(8,128)(2,1)S(1)}, bf16[16,4096]{1,0:T(8,128)(2,1)S(1)}, u32[]{:S(2)}, u32[]{:S(2)}) %collective-permute-start.16) | collective-permute-done | bytes 131104 | tf_op jit(solution)/shard_map/cross_pxa/ppermute | solution.py:64
  47.6 2.4 %shard_map.87 = (bf16[64,1024]{1,0:T(8,128)(2,1)S(1)}, f32[64,1024]{1,0:T(8,128)S(1)}) custom-call(f32[8,256]{1,0:T(8,128)S(1)} %get-tuple-element.29.weight_ref, bf16[1024,4096]{1,0:T(8,128)(2,1)S(1)} %copy-done.2, bf16[32,4096]{1,0:T(8,128)(2,1)S(1)} %collective-permute-done.8.refs_0_, bf16[16,4096]{1,0:T(8,128)(2,1)S(1)} %collective-permute-done.16.refs_1_, ...), custom_call_target="tpu_custom_call" | custom-call | tf_op jit(solution)/shard_map/pallas_call | solution.py:221
  50.0 1.6 %collective-permute-start.18 = (bf16[64,1024]{1,0:T(8,128)(2,1)S(1)}, bf16[64,1024]{1,0:T(8,128)(2,1)S(1)}, u32[]{:S(2)}, u32[]{:S(2)}) collective-permute-start(bf16[64,1024]{1,0:T(8,128)(2,1)S(1)} %get-tuple-element.46), channel_id=1, source_target_pairs={{0,1},{1,0},{2,3},{3,2},{4,5},{5,4},{6,7},{7,6},{8,9},{9,8},{10,11... | collective-permute-start | bytes 393224 | tf_op jit(solution)/shard_map/got2/ppermute | solution.py:64
  51.7 1.0 %shard_map.88.refs_2_ = f32[256,1024]{1,0:T(8,128)} custom-call(s32[1,1024]{1,0:T(1,128)S(1)} %bitcast.6, s32[256,1]{1,0:T(8,128)S(1)} %copy.11.query_ids, f32[64,1024]{1,0:T(8,128)S(1)} %get-tuple-element.47.refs_0_, bf16[64,1024]{1,0:T(8,128)(2,1)S(1)} %collective-permute-done.15.refs_1_, f32[128,1024]{1,0:T(8,128)S(1)} %get-tuple-element.48.refs_2_, ...), custom_call_target="tpu_custom_call" | custom-call | tf_op jit(solution)/shard_map/pallas_call | solution.py:283
  52.8 3.0 %collective-permute-done.18.refs_1_ = bf16[64,1024]{1,0:T(8,128)(2,1)S(1)} collective-permute-done((bf16[64,1024]{1,0:T(8,128)(2,1)S(1)}, bf16[64,1024]{1,0:T(8,128)(2,1)S(1)}, u32[]{:S(2)}, u32[]{:S(2)}) %collective-permute-start.18) | collective-permute-done | bytes 131104 | tf_op jit(solution)/shard_map/got2/ppermute | solution.py:64
  55.8 0.8 %shard_map.89 = f32[256,1024]{1,0:T(8,128)} custom-call(s32[1,1024]{1,0:T(1,128)S(1)} %bitcast.7, s32[256,1]{1,0:T(8,128)S(1)} %copy.11.query_ids, f32[64,1024]{1,0:T(8,128)S(1)} %get-tuple-element.45.refs_0_, bf16[64,1024]{1,0:T(8,128)(2,1)S(1)} %collective-permute-done.18.refs_1_, f32[256,1024]{1,0:T(8,128)} %shard_map.88.refs_2_), custom_call_target="tpu_custom_call", output_to_operand_aliasing={{}: (4, {})} | custom-call | tf_op jit(solution)/shard_map/pallas_call | solution.py:283
  (38 shorter events, 3.9 us)
Async XLA Ops:
  2.8 12.5 %collective-permute-start = (bf16[32,4096]{1,0:T(8,128)(2,1)S(1)}, bf16[32,4096]{1,0:T(8,128)(2,1)S(1)}, u32[]{:S(2)}, u32[]{:S(2)}) collective-permute-start(bf16[32,4096]{1,0:T(8,128)(2,1)S(1)} %get-tuple-element.37.refs_0_), channel_id=1, source_target_pairs={{0,4},{1,5},{2,6},{3,7},{4,0},{5,1},{6,2},{7,3},{8,12},{9,13},{10,... | collective-permute-start | bytes 786440 | tf_op jit(solution)/shard_map/near/ppermute | solution.py:64
  5.9 9.4 %collective-permute-start.2 = (bf16[32,4096]{1,0:T(8,128)(2,1)S(1)}, bf16[32,4096]{1,0:T(8,128)(2,1)S(1)}, u32[]{:S(2)}, u32[]{:S(2)}) collective-permute-start(bf16[32,4096]{1,0:T(8,128)(2,1)S(1)} %get-tuple-element.37.refs_0_), channel_id=1, source_target_pairs={{0,0},{1,1},{2,2},{3,3},{4,8},{5,9},{6,10},{7,11},{8,4},{9,5},{10,... | collective-permute-start | bytes 786440 | tf_op jit(solution)/shard_map/middle/ppermute | solution.py:64
  14.8 7.1 %collective-permute-start.5 = (bf16[32,4096]{1,0:T(8,128)(2,1)S(1)}, bf16[32,4096]{1,0:T(8,128)(2,1)S(1)}, u32[]{:S(2)}, u32[]{:S(2)}) collective-permute-start(bf16[32,4096]{1,0:T(8,128)(2,1)S(1)} %get-tuple-element.32.refs_2_), channel_id=1, source_target_pairs={{0,2},{1,3},{2,0},{3,1},{4,6},{5,7},{6,4},{7,5},{8,10},{9,11},{10,... | collective-permute-start | bytes 786440 | tf_op jit(solution)/shard_map/rest_x/ppermute | solution.py:64
  14.8 7.1 %collective-permute-start.7 = (bf16[32,4096]{1,0:T(8,128)(2,1)S(1)}, bf16[32,4096]{1,0:T(8,128)(2,1)S(1)}, u32[]{:S(2)}, u32[]{:S(2)}) collective-permute-start(bf16[32,4096]{1,0:T(8,128)(2,1)S(1)} %get-tuple-element.37.refs_0_), channel_id=1, source_target_pairs={{0,2},{1,3},{2,0},{3,1},{4,6},{5,7},{6,4},{7,5},{8,10},{9,11},{10,... | collective-permute-start | bytes 786440 | tf_op jit(solution)/shard_map/mine_x/ppermute | solution.py:64
  15.3 12.4 %collective-permute-start.3 = (bf16[32,4096]{1,0:T(8,128)(2,1)S(1)}, bf16[32,4096]{1,0:T(8,128)(2,1)S(1)}, u32[]{:S(2)}, u32[]{:S(2)}) collective-permute-start(bf16[32,4096]{1,0:T(8,128)(2,1)S(1)} %collective-permute-done.2), channel_id=1, source_target_pairs={{0,4},{1,5},{2,6},{3,7},{4,0},{5,1},{6,2},{7,3},{8,12},{9,13},{10,... | collective-permute-start | bytes 786440 | tf_op jit(solution)/shard_map/outward/ppermute | solution.py:64
  19.7 8.6 %collective-permute-start.10 = (bf16[32,4096]{1,0:T(8,128)(2,1)S(1)}, bf16[32,4096]{1,0:T(8,128)(2,1)S(1)}, u32[]{:S(2)}, u32[]{:S(2)}) collective-permute-start(bf16[32,4096]{1,0:T(8,128)(2,1)S(1)} %collective-permute-done.refs_0_), channel_id=1, source_target_pairs={{0,16},{1,17},{2,18},{3,19},{4,20},{5,21},{6,22},{7,23},{8,24},{9,... | collective-permute-start | bytes 786440 | tf_op jit(solution)/shard_map/near_p/ppermute | solution.py:64
  21.2 7.7 %collective-permute-start.1 = (bf16[32,4096]{1,0:T(8,128)(2,1)S(1)}, bf16[32,4096]{1,0:T(8,128)(2,1)S(1)}, u32[]{:S(2)}, u32[]{:S(2)}) collective-permute-start(bf16[32,4096]{1,0:T(8,128)(2,1)S(1)} %collective-permute-done.refs_0_), channel_id=1, source_target_pairs={{0,0},{1,1},{2,2},{3,3},{4,8},{5,9},{6,10},{7,11},{8,4},{9,5},{10,... | collective-permute-start | bytes 786440 | tf_op jit(solution)/shard_map/middle_near/ppermute | solution.py:64
  21.9 3.4 %copy-start.1 = (bf16[1024,4096]{1,0:T(8,128)(2,1)S(1)}, bf16[1024,4096]{1,0:T(8,128)(2,1)}, u32[]{:S(2)}) copy-start(bf16[1024,4096]{1,0:T(8,128)(2,1)} %copy-done) | copy-start | bytes 25165828
  25.3 5.9 %copy-start.2 = (bf16[1024,4096]{1,0:T(8,128)(2,1)S(1)}, bf16[1024,4096]{1,0:T(8,128)(2,1)}, u32[]{:S(2)}) copy-start(bf16[1024,4096]{1,0:T(8,128)(2,1)} %copy-done) | copy-start | bytes 25165828
  27.7 7.8 %collective-permute-start.12 = (bf16[32,4096]{1,0:T(8,128)(2,1)S(1)}, bf16[32,4096]{1,0:T(8,128)(2,1)S(1)}, u32[]{:S(2)}, u32[]{:S(2)}) collective-permute-start(bf16[32,4096]{1,0:T(8,128)(2,1)S(1)} %broadcast_select_fusion.1.refs_0_), channel_id=1, source_target_pairs={{0,16},{1,17},{2,18},{3,19},{4,20},{5,21},{6,22},{7,23},{8,24},{9,... | collective-permute-start | bytes 786440 | tf_op jit(solution)/shard_map/far_p/ppermute | solution.py:64
  28.3 2.9 %collective-permute-start.6 = (bf16[32,4096]{1,0:T(8,128)(2,1)S(1)}, bf16[32,4096]{1,0:T(8,128)(2,1)S(1)}, u32[]{:S(2)}, u32[]{:S(2)}) collective-permute-start(bf16[32,4096]{1,0:T(8,128)(2,1)S(1)} %broadcast_select_fusion.1.refs_0_), channel_id=1, source_target_pairs={{0,2},{1,3},{2,0},{3,1},{4,6},{5,7},{6,4},{7,5},{8,10},{9,11},{10,... | collective-permute-start | bytes 786440 | tf_op jit(solution)/shard_map/far_x/ppermute | solution.py:64
  28.3 7.2 %collective-permute-start.11 = (bf16[32,4096]{1,0:T(8,128)(2,1)S(1)}, bf16[32,4096]{1,0:T(8,128)(2,1)S(1)}, u32[]{:S(2)}, u32[]{:S(2)}) collective-permute-start(bf16[32,4096]{1,0:T(8,128)(2,1)S(1)} %collective-permute-done.10.refs_2_), channel_id=1, source_target_pairs={{0,2},{1,3},{2,0},{3,1},{4,6},{5,7},{6,4},{7,5},{8,10},{9,11},{10,... | collective-permute-start | bytes 786440 | tf_op jit(solution)/shard_map/near_px/ppermute | solution.py:64
  28.8 8.3 %collective-permute-start.4 = (bf16[32,4096]{1,0:T(8,128)(2,1)S(1)}, bf16[32,4096]{1,0:T(8,128)(2,1)S(1)}, u32[]{:S(2)}, u32[]{:S(2)}) collective-permute-start(bf16[32,4096]{1,0:T(8,128)(2,1)S(1)} %collective-permute-done.1), channel_id=1, source_target_pairs={{0,4},{1,5},{2,6},{3,7},{4,0},{5,1},{6,2},{7,3},{8,12},{9,13},{10,... | collective-permute-start | bytes 786440 | tf_op jit(solution)/shard_map/outward_near/ppermute | solution.py:64
  31.2 9.2 %collective-permute-start.9 = (bf16[32,4096]{1,0:T(8,128)(2,1)S(1)}, bf16[32,4096]{1,0:T(8,128)(2,1)S(1)}, u32[]{:S(2)}, u32[]{:S(2)}) collective-permute-start(bf16[32,4096]{1,0:T(8,128)(2,1)S(1)} %collective-permute-done.refs_0_), channel_id=1, source_target_pairs={{0,2},{1,3},{2,0},{3,1},{4,6},{5,7},{6,4},{7,5},{8,10},{9,11},{10,... | collective-permute-start | bytes 786440 | tf_op jit(solution)/shard_map/near_x/ppermute | solution.py:64
  35.5 4.8 %collective-permute-start.13 = (bf16[32,4096]{1,0:T(8,128)(2,1)S(1)}, bf16[32,4096]{1,0:T(8,128)(2,1)S(1)}, u32[]{:S(2)}, u32[]{:S(2)}) collective-permute-start(bf16[32,4096]{1,0:T(8,128)(2,1)S(1)} %collective-permute-done.12.refs_4_), channel_id=1, source_target_pairs={{0,2},{1,3},{2,0},{3,1},{4,6},{5,7},{6,4},{7,5},{8,10},{9,11},{10,... | collective-permute-start | bytes 786440 | tf_op jit(solution)/shard_map/far_px/ppermute | solution.py:64
  37.2 14.4 %copy-start.4 = (s32[256]{0:T(256)S(1)}, s32[256]{0:T(256)}, u32[]{:S(2)}) copy-start(s32[256]{0:T(256)} %param.15) | copy-start | bytes 3076
  37.2 14.6 %copy-start.3 = (s32[1024]{0:T(1024)S(1)}, s32[1024]{0:T(1024)}, u32[]{:S(2)}) copy-start(s32[1024]{0:T(1024)} %param.14) | copy-start | bytes 12292
  37.2 3.2 %collective-permute-start.14 = (bf16[32,4096]{1,0:T(8,128)(2,1)S(1)}, bf16[32,4096]{1,0:T(8,128)(2,1)S(1)}, u32[]{:S(2)}, u32[]{:S(2)}) collective-permute-start(bf16[32,4096]{1,0:T(8,128)(2,1)S(1)} %broadcast_select_fusion.refs_6_), channel_id=1, source_target_pairs={{0,2},{1,3},{2,0},{3,1},{4,6},{5,7},{6,4},{7,5},{8,10},{9,11},{10,... | collective-permute-start | bytes 786440 | tf_op jit(solution)/shard_map/cross_x/ppermute | solution.py:64
  37.3 8.7 %collective-permute-start.8 = (bf16[32,4096]{1,0:T(8,128)(2,1)S(1)}, bf16[32,4096]{1,0:T(8,128)(2,1)S(1)}, u32[]{:S(2)}, u32[]{:S(2)}) collective-permute-start(bf16[32,4096]{1,0:T(8,128)(2,1)S(1)} %broadcast_select_fusion.refs_6_), channel_id=1, source_target_pairs={{0,16},{1,17},{2,18},{3,19},{4,20},{5,21},{6,22},{7,23},{8,24},{9,... | collective-permute-start | bytes 786440 | tf_op jit(solution)/shard_map/cross_p/ppermute | solution.py:64
  38.8 5.6 %collective-permute-start.15 = (bf16[64,1024]{1,0:T(8,128)(2,1)S(1)}, bf16[64,1024]{1,0:T(8,128)(2,1)S(1)}, u32[]{:S(2)}, u32[]{:S(2)}) collective-permute-start(bf16[64,1024]{1,0:T(8,128)(2,1)S(1)} %get-tuple-element.38), channel_id=1, source_target_pairs={{0,1},{1,0},{2,3},{3,2},{4,5},{5,4},{6,7},{7,6},{8,9},{9,8},{10,11... | collective-permute-start | bytes 393224 | tf_op jit(solution)/shard_map/got0/ppermute | solution.py:64
  42.9 8.9 %collective-permute-start.19 = (bf16[128,1024]{1,0:T(8,128)(2,1)S(1)}, bf16[128,1024]{1,0:T(8,128)(2,1)S(1)}, u32[]{:S(2)}, u32[]{:S(2)}) collective-permute-start(bf16[128,1024]{1,0:T(8,128)(2,1)S(1)} %get-tuple-element.42), channel_id=1, source_target_pairs={{0,1},{1,0},{2,3},{3,2},{4,5},{5,4},{6,7},{7,6},{8,9},{9,8},{10,11... | collective-permute-start | bytes 786440 | tf_op jit(solution)/shard_map/got1/ppermute | solution.py:64
  46.0 1.4 %collective-permute-start.16 = (bf16[16,4096]{1,0:T(8,128)(2,1)S(1)}, bf16[16,4096]{1,0:T(8,128)(2,1)S(1)}, u32[]{:S(2)}, u32[]{:S(2)}) collective-permute-start(bf16[16,4096]{1,0:T(8,128)(2,1)S(1)} %get-tuple-element.50), channel_id=1, source_target_pairs={{0,2},{1,3},{2,0},{3,1},{4,6},{5,7},{6,4},{7,5},{8,10},{9,11},{10,... | collective-permute-start | bytes 393224 | tf_op jit(solution)/shard_map/cross_pxa/ppermute | solution.py:64
  46.1 1.5 %collective-permute-start.17 = (bf16[16,4096]{1,0:T(8,128)(2,1)S(1)}, bf16[16,4096]{1,0:T(8,128)(2,1)S(1)}, u32[]{:S(2)}, u32[]{:S(2)}) collective-permute-start(bf16[16,4096]{1,0:T(8,128)(2,1)S(1)} %get-tuple-element.49), channel_id=1, source_target_pairs={{0,2},{1,3},{2,0},{3,1},{4,6},{5,7},{6,4},{7,5},{8,10},{9,11},{10,... | collective-permute-start | bytes 393224 | tf_op jit(solution)/shard_map/cross_pxb/ppermute | solution.py:64
  50.0 5.8 %collective-permute-start.18 = (bf16[64,1024]{1,0:T(8,128)(2,1)S(1)}, bf16[64,1024]{1,0:T(8,128)(2,1)S(1)}, u32[]{:S(2)}, u32[]{:S(2)}) collective-permute-start(bf16[64,1024]{1,0:T(8,128)(2,1)S(1)} %get-tuple-element.46), channel_id=1, source_target_pairs={{0,1},{1,0},{2,3},{3,2},{4,5},{5,4},{6,7},{7,6},{8,9},{9,8},{10,11... | collective-permute-start | bytes 393224 | tf_op jit(solution)/shard_map/got2/ppermute | solution.py:64
  (1 other events, 3.3 us)

commit v18 on v15

--- a/solution.py
+++ b/solution.py
@@ -114,38 +114,42 @@
 
 
 def precond_rows(q_ref, lefts, rights, out):
-    for at in range(0, q_ref.shape[0], CHUNK):
-        values = precond_chunk(q_ref[at : at + CHUNK, :], lefts, rights)
-        for t, value in enumerate(values):
-            out[at : at + CHUNK, t * 256 : (t + 1) * 256] = value
-
-
-def precond_chunk(q, lefts, rights):
-    tiles = q.shape[1] // 256
+    rows, width = q_ref.shape
+    tiles, chunks = width // 256, range(rows // CHUNK)
+    side_by_side = functools.partial(jnp.concatenate, axis=1)
     r, c = iota((256, 256), 0), iota((256, 256), 1)
     swap = jnp.where((r // 16 == c % 16) & (r % 16 == c // 16), 1.0, 0.0).astype(bf16)
-    x = jnp.concatenate([q[:, t * 256 : (t + 1) * 256] for t in range(tiles)], axis=0)
-    x = dot(swap, x).astype(bf16)
+
+    def of_chunk(k):
+        q = q_ref[k * CHUNK : (k + 1) * CHUNK, :]
+        return jnp.concatenate([q[:, t * 256 : (t + 1) * 256] for t in range(tiles)], axis=0)
+
+    x = dot(swap, side_by_side([of_chunk(k) for k in chunks])).astype(bf16)
+    x = jnp.concatenate([x[:, k * 256 : (k + 1) * 256] for k in chunks], axis=0)
     z = dot(x, rights[0]) + dot(x, rights[1])
     sets = []
-    for first in range(0, 16, 4):
-        rows = [
+    for first in range(0, rows, 4):
+        pieces = [
             z[query * 16 : (query + 1) * 16, s * 128 : (s + 1) * 128]
             for query in range(first, first + 4)
             for s in range(4)
         ]
-        sets.append(jnp.concatenate(rows, axis=0))
-    high, low = split(jnp.concatenate(sets, axis=1), 2)
+        sets.append(jnp.concatenate(pieces, axis=0))
+    high, low = split(side_by_side(sets), 2)
     z = dot(lefts[0], high) + (dot(lefts[0], low) + dot(lefts[1], high))
     side = iota((16, 128), 1) < 64
-    rows = []
-    for first in range(4):
-        for k in range(4):
-            o = z[k * 64 : (k + 1) * 64, first * 128 : (first + 1) * 128]
-            pair = [jnp.where(side, o[0:16], o[16:32]), jnp.where(side, o[32:48], o[48:64])]
-            rows.append(jnp.concatenate(pair, axis=1))
-    y = dot(swap, jnp.concatenate(rows, axis=0).astype(bf16)).astype(bf16)
-    return [y[t * 16 : (t + 1) * 16] for t in range(tiles)]
+    y = []
+    for query in range(rows):
+        k, group = query % 4, query // 4
+        o = z[k * 64 : (k + 1) * 64, group * 128 : (group + 1) * 128]
+        pair = [jnp.where(side, o[0:16], o[16:32]), jnp.where(side, o[32:48], o[48:64])]
+        y.append(side_by_side(pair))
+    y = [jnp.concatenate(y[k * CHUNK : (k + 1) * CHUNK], axis=0) for k in chunks]
+    y = dot(swap, side_by_side(y).astype(bf16)).astype(bf16)
+    for k in chunks:
+        for t in range(tiles):
+            value = y[t * 16 : (t + 1) * 16, k * 256 : (k + 1) * 256]
+            out[k * CHUNK : (k + 1) * CHUNK, t * 256 : (t + 1) * 256] = value
 
 
 def own_kernel(q_hbm, left_hbm, right_hbm, mine, lefts_ref, rights_ref, q_ref, left, right, sems):

time: 47.1 us -> 46.7 us (level)
  no operation moved by 1% of the time
where the time goes in v18:
time: 46.7 us; the launch traced here: 46.5 us
  Pallas kernels  18.2 us (39%)
  starting transfers between devices  15 us (32%)
  waiting for transfers between devices  12.4 us (27%)
  between operations  0.79 us (2%)
    pallas_call x6, Pallas kernels, kernel_call(): pl.pallas_call(kernel, out_shape=outs, in_specs=specs or [VMEM] * len(inp...  16.4 us
    ppermute x19, starting transfers between devices, permute(): return lax.ppermute(value, AXES, pairs)  15 us
    ppermute x19, waiting for transfers between devices, permute(): return lax.ppermute(value, AXES, pairs)  12.4 us
    pallas_call x2, Pallas kernels, call_final(): pl.pallas_call(functools.partial(final_kernel, groups=groups, n_given=len...  1.84 us
  transfers between devices with their start and end apart: 19, of which 8 were waited for; matrix products, arithmetic and copies ran while one was open for 0% of the time, Pallas kernels for 32%

profile of v18, /device:TPU:0, one launch (start us, length us, event | category | flops | bytes accessed | tf_op | source)
XLA Modules:
  0.0 46.5 jit_solution(7465571683683450738)
XLA Ops:
  0.0 2.4 %shard_map.82 = (bf16[32,4096]{1,0:T(8,128)(2,1)S(1)}, bf16[2,256,256]{2,1,0:T(8,128)(2,1)S(1)}, bf16[2,256,512]{2,1,0:T(8,128)(2,1)S(1)}) custom-call(bf16[64,4096]{1,0:T(8,128)(2,1)} %bitcast.9, f32[64,64]{1,0:T(8,128)} %bitcast.11, f32[64,64]{1,0:T(8,128)} %bitcast.12), custom_call_target="tpu_custom_call" | custom-call | tf_op jit(solution)/shard_map/pallas_call | solution.py:225
  2.4 3.1 %collective-permute-start.1 = (bf16[32,4096]{1,0:T(8,128)(2,1)S(1)}, bf16[32,4096]{1,0:T(8,128)(2,1)S(1)}, u32[]{:S(2)}, u32[]{:S(2)}) collective-permute-start(bf16[32,4096]{1,0:T(8,128)(2,1)S(1)} %get-tuple-element.37.refs_0_), channel_id=1, source_target_pairs={{0,4},{1,5},{2,6},{3,7},{4,0},{5,1},{6,2},{7,3},{8,12},{9,13},{10,... | collective-permute-start | bytes 786440 | tf_op jit(solution)/shard_map/near/ppermute | solution.py:64
  5.5 2.5 %collective-permute-start = (bf16[32,4096]{1,0:T(8,128)(2,1)S(1)}, bf16[32,4096]{1,0:T(8,128)(2,1)S(1)}, u32[]{:S(2)}, u32[]{:S(2)}) collective-permute-start(bf16[32,4096]{1,0:T(8,128)(2,1)S(1)} %get-tuple-element.37.refs_0_), channel_id=1, source_target_pairs={{0,12},{1,13},{2,14},{3,15},{4,8},{5,9},{6,10},{7,11},{8,4},{9,5},... | collective-permute-start | bytes 786440 | tf_op jit(solution)/shard_map/far/ppermute | solution.py:64
  8.6 4.3 %shard_map.83 = (bf16[32,4096]{1,0:T(8,128)(2,1)S(1)}, bf16[1024,4096]{1,0:T(8,128)(2,1)S(1)}, f32[8,256]{1,0:T(8,128)S(1)}) custom-call(f32[2]{0:T(128)} %weight_ref.1, s32[1]{0:T(128)S(6)} %copy.13.layer_ref, bf16[64,4096]{1,0:T(8,128)(2,1)} %bitcast.10, bf16[1024,4096]{1,0:T(8,128)(2,1)} %bitcast.8, bf16[2,256,256]{2,1,0:T(8,128)(2,1)S(1)} %get-tuple-element.28.lefts_ref, ...), custom_call_target="tpu_custom_call" | custom-call | tf_op jit(solution)/shard_map/pallas_call | solution.py:225
  13.5 1.5 %collective-permute-start.8 = (bf16[32,4096]{1,0:T(8,128)(2,1)S(1)}, bf16[32,4096]{1,0:T(8,128)(2,1)S(1)}, u32[]{:S(2)}, u32[]{:S(2)}) collective-permute-start(bf16[32,4096]{1,0:T(8,128)(2,1)S(1)} %collective-permute-done.1.refs_0_), channel_id=1, source_target_pairs={{0,16},{1,17},{2,18},{3,19},{4,20},{5,21},{6,22},{7,23},{8,24},{9,... | collective-permute-start | bytes 786440 | tf_op jit(solution)/shard_map/near_p/ppermute | solution.py:64
  15.0 4.7 %collective-permute-done.refs_0_ = bf16[32,4096]{1,0:T(8,128)(2,1)S(1)} collective-permute-done((bf16[32,4096]{1,0:T(8,128)(2,1)S(1)}, bf16[32,4096]{1,0:T(8,128)(2,1)S(1)}, u32[]{:S(2)}, u32[]{:S(2)}) %collective-permute-start) | collective-permute-done | bytes 262176 | tf_op jit(solution)/shard_map/far/ppermute | solution.py:64
  19.7 1.5 %collective-permute-start.10 = (bf16[32,4096]{1,0:T(8,128)(2,1)S(1)}, bf16[32,4096]{1,0:T(8,128)(2,1)S(1)}, u32[]{:S(2)}, u32[]{:S(2)}) collective-permute-start(bf16[32,4096]{1,0:T(8,128)(2,1)S(1)} %collective-permute-done.refs_0_), channel_id=1, source_target_pairs={{0,16},{1,17},{2,18},{3,19},{4,20},{5,21},{6,22},{7,23},{8,24},{9,... | collective-permute-start | bytes 786440 | tf_op jit(solution)/shard_map/far_p/ppermute | solution.py:64
  21.2 0.6 %collective-permute-start.2 = (bf16[32,4096]{1,0:T(8,128)(2,1)S(1)}, bf16[32,4096]{1,0:T(8,128)(2,1)S(1)}, u32[]{:S(2)}, u32[]{:S(2)}) collective-permute-start(bf16[32,4096]{1,0:T(8,128)(2,1)S(1)} %collective-permute-done.refs_0_), channel_id=1, source_target_pairs={{0,4},{1,5},{2,6},{3,7},{4,0},{5,1},{6,2},{7,3},{8,12},{9,13},{10,... | collective-permute-start | bytes 786440 | tf_op jit(solution)/shard_map/cross/ppermute | solution.py:64
  21.8 2.4 %shard_map.84.refs_2_.refs_8_ = f32[128,1024]{1,0:T(8,128)S(1)} custom-call(f32[8,256]{1,0:T(8,128)S(1)} %get-tuple-element.30.weight_ref, bf16[1024,4096]{1,0:T(8,128)(2,1)S(1)} %get-tuple-element.31.train_ref, bf16[32,4096]{1,0:T(8,128)(2,1)S(1)} %get-tuple-element.37.refs_0_, bf16[32,4096]{1,0:T(8,128)(2,1)S(1)} %collective-permute-done.5.refs_1_, ...), custom_call_target="tpu_custom_call" | custom-call | tf_op jit(solution)/shard_map/pallas_call | solution.py:225
  24.9 2.4 %shard_map.85 = (bf16[64,1024]{1,0:T(8,128)(2,1)S(1)}, f32[64,1024]{1,0:T(8,128)S(1)}) custom-call(f32[8,256]{1,0:T(8,128)S(1)} %get-tuple-element.30.weight_ref, bf16[1024,4096]{1,0:T(8,128)(2,1)S(1)} %get-tuple-element.31.train_ref, bf16[32,4096]{1,0:T(8,128)(2,1)S(1)} %collective-permute-done.refs_0_, ...), custom_call_target="tpu_custom_call" | custom-call | tf_op jit(solution)/shard_map/pallas_call | solution.py:225
  27.3 0.8 %collective-permute-done.2.refs_6_ = bf16[32,4096]{1,0:T(8,128)(2,1)S(1)} collective-permute-done((bf16[32,4096]{1,0:T(8,128)(2,1)S(1)}, bf16[32,4096]{1,0:T(8,128)(2,1)S(1)}, u32[]{:S(2)}, u32[]{:S(2)}) %collective-permute-start.2) | collective-permute-done | bytes 262176 | tf_op jit(solution)/shard_map/cross/ppermute | solution.py:64
  28.5 1.5 %collective-permute-start.13 = (bf16[64,1024]{1,0:T(8,128)(2,1)S(1)}, bf16[64,1024]{1,0:T(8,128)(2,1)S(1)}, u32[]{:S(2)}, u32[]{:S(2)}) collective-permute-start(bf16[64,1024]{1,0:T(8,128)(2,1)S(1)} %get-tuple-element.39), channel_id=1, source_target_pairs={{0,1},{1,0},{2,3},{3,2},{4,5},{5,4},{6,7},{7,6},{8,9},{9,8},{10,11... | collective-permute-start | bytes 393224 | tf_op jit(solution)/shard_map/got0/ppermute | solution.py:64
  30.1 0.9 %collective-permute-start.14 = (bf16[16,4096]{1,0:T(8,128)(2,1)S(1)}, bf16[16,4096]{1,0:T(8,128)(2,1)S(1)}, u32[]{:S(2)}, u32[]{:S(2)}) collective-permute-start(bf16[16,4096]{1,0:T(8,128)(2,1)S(1)} %slice.7), channel_id=1, source_target_pairs={{0,4},{1,5},{2,6},{3,7},{4,0},{5,1},{6,2},{7,3},{8,12},{9,13},{10,... | collective-permute-start | bytes 393224 | tf_op jit(solution)/shard_map/cross_pb/ppermute | solution.py:64
  31.0 0.6 %collective-permute-start.6 = (bf16[16,4096]{1,0:T(8,128)(2,1)S(1)}, bf16[16,4096]{1,0:T(8,128)(2,1)S(1)}, u32[]{:S(2)}, u32[]{:S(2)}) collective-permute-start(bf16[16,4096]{1,0:T(8,128)(2,1)S(1)} %slice.6), channel_id=1, source_target_pairs={{0,16},{1,17},{2,18},{3,19},{4,20},{5,21},{6,22},{7,23},{8,24},{9,... | collective-permute-start | bytes 393224 | tf_op jit(solution)/shard_map/cross_pa/ppermute | solution.py:64
  31.6 2.5 %shard_map.86 = (f32[128,1024]{1,0:T(8,128)S(1)}, bf16[128,1024]{1,0:T(8,128)(2,1)S(1)}, f32[128,1024]{1,0:T(8,128)S(1)}) custom-call(f32[8,256]{1,0:T(8,128)S(1)} %get-tuple-element.30.weight_ref, bf16[1024,4096]{1,0:T(8,128)(2,1)S(1)} %get-tuple-element.31.train_ref, bf16[32,4096]{1,0:T(8,128)(2,1)S(1)} %collective-permute-done.1.refs_0_, ...), custom_call_target="tpu_custom_call" | custom-call | tf_op jit(solution)/shard_map/pallas_call | solution.py:225
  34.1 0.6 %collective-permute-start.18 = (bf16[128,1024]{1,0:T(8,128)(2,1)S(1)}, bf16[128,1024]{1,0:T(8,128)(2,1)S(1)}, u32[]{:S(2)}, u32[]{:S(2)}) collective-permute-start(bf16[128,1024]{1,0:T(8,128)(2,1)S(1)} %get-tuple-element.43), channel_id=1, source_target_pairs={{0,1},{1,0},{2,3},{3,2},{4,5},{5,4},{6,7},{7,6},{8,9},{9,8},{10,11... | collective-permute-start | bytes 786440 | tf_op jit(solution)/shard_map/got1/ppermute | solution.py:64
  34.7 0.6 %collective-permute-done.14.refs_1_ = bf16[16,4096]{1,0:T(8,128)(2,1)S(1)} collective-permute-done((bf16[16,4096]{1,0:T(8,128)(2,1)S(1)}, bf16[16,4096]{1,0:T(8,128)(2,1)S(1)}, u32[]{:S(2)}, u32[]{:S(2)}) %collective-permute-start.14) | collective-permute-done | bytes 131104 | tf_op jit(solution)/shard_map/cross_pb/ppermute | solution.py:64
  35.3 1.0 %collective-permute-done.6.refs_0_ = bf16[16,4096]{1,0:T(8,128)(2,1)S(1)} collective-permute-done((bf16[16,4096]{1,0:T(8,128)(2,1)S(1)}, bf16[16,4096]{1,0:T(8,128)(2,1)S(1)}, u32[]{:S(2)}, u32[]{:S(2)}) %collective-permute-start.6) | collective-permute-done | bytes 131104 | tf_op jit(solution)/shard_map/cross_pa/ppermute | solution.py:64
  36.7 1.0 %collective-permute-done.15.refs_2_ = bf16[16,4096]{1,0:T(8,128)(2,1)S(1)} collective-permute-done((bf16[16,4096]{1,0:T(8,128)(2,1)S(1)}, bf16[16,4096]{1,0:T(8,128)(2,1)S(1)}, u32[]{:S(2)}, u32[]{:S(2)}) %collective-permute-start.15) | collective-permute-done | bytes 131104 | tf_op jit(solution)/shard_map/cross_pxa/ppermute | solution.py:64
  37.7 2.4 %shard_map.87 = (bf16[64,1024]{1,0:T(8,128)(2,1)S(1)}, f32[64,1024]{1,0:T(8,128)S(1)}) custom-call(f32[8,256]{1,0:T(8,128)S(1)} %get-tuple-element.30.weight_ref, bf16[1024,4096]{1,0:T(8,128)(2,1)S(1)} %get-tuple-element.31.train_ref, bf16[16,4096]{1,0:T(8,128)(2,1)S(1)} %collective-permute-done.6.refs_0_, ...), custom_call_target="tpu_custom_call" | custom-call | tf_op jit(solution)/shard_map/pallas_call | solution.py:225
  40.8 1.2 %collective-permute-done.18.refs_3_ = bf16[128,1024]{1,0:T(8,128)(2,1)S(1)} collective-permute-done((bf16[128,1024]{1,0:T(8,128)(2,1)S(1)}, bf16[128,1024]{1,0:T(8,128)(2,1)S(1)}, u32[]{:S(2)}, u32[]{:S(2)}) %collective-permute-start.18) | collective-permute-done | bytes 262176 | tf_op jit(solution)/shard_map/got1/ppermute | solution.py:64
  42.0 1.0 %shard_map.88.refs_2_ = f32[256,1024]{1,0:T(8,128)} custom-call(s32[1,1024]{1,0:T(1,128)S(1)} %bitcast.6, s32[256,1]{1,0:T(8,128)S(1)} %copy.11.query_ids, f32[64,1024]{1,0:T(8,128)S(1)} %get-tuple-element.49.refs_0_, bf16[64,1024]{1,0:T(8,128)(2,1)S(1)} %collective-permute-done.13.refs_1_, f32[128,1024]{1,0:T(8,128)S(1)} %get-tuple-element.50.refs_2_, ...), custom_call_target="tpu_custom_call" | custom-call | tf_op jit(solution)/shard_map/pallas_call | solution.py:286
  43.0 2.7 %collective-permute-done.17.refs_1_ = bf16[64,1024]{1,0:T(8,128)(2,1)S(1)} collective-permute-done((bf16[64,1024]{1,0:T(8,128)(2,1)S(1)}, bf16[64,1024]{1,0:T(8,128)(2,1)S(1)}, u32[]{:S(2)}, u32[]{:S(2)}) %collective-permute-start.17) | collective-permute-done | bytes 131104 | tf_op jit(solution)/shard_map/got2/ppermute | solution.py:64
  45.7 0.8 %shard_map.89 = f32[256,1024]{1,0:T(8,128)} custom-call(s32[1,1024]{1,0:T(1,128)S(1)} %bitcast.7, s32[256,1]{1,0:T(8,128)S(1)} %copy.11.query_ids, f32[64,1024]{1,0:T(8,128)S(1)} %get-tuple-element.47.refs_0_, bf16[64,1024]{1,0:T(8,128)(2,1)S(1)} %collective-permute-done.17.refs_1_, f32[256,1024]{1,0:T(8,128)} %shard_map.88.refs_2_), custom_call_target="tpu_custom_call", output_to_operand_aliasing={{}: (4, {})} | custom-call | tf_op jit(solution)/shard_map/pallas_call | solution.py:286
  (29 shorter events, 2.8 us)
Async XLA Ops:
  2.4 11.1 %collective-permute-start.1 = (bf16[32,4096]{1,0:T(8,128)(2,1)S(1)}, bf16[32,4096]{1,0:T(8,128)(2,1)S(1)}, u32[]{:S(2)}, u32[]{:S(2)}) collective-permute-start(bf16[32,4096]{1,0:T(8,128)(2,1)S(1)} %get-tuple-element.37.refs_0_), channel_id=1, source_target_pairs={{0,4},{1,5},{2,6},{3,7},{4,0},{5,1},{6,2},{7,3},{8,12},{9,13},{10,... | collective-permute-start | bytes 786440 | tf_op jit(solution)/shard_map/near/ppermute | solution.py:64
  5.5 14.2 %collective-permute-start = (bf16[32,4096]{1,0:T(8,128)(2,1)S(1)}, bf16[32,4096]{1,0:T(8,128)(2,1)S(1)}, u32[]{:S(2)}, u32[]{:S(2)}) collective-permute-start(bf16[32,4096]{1,0:T(8,128)(2,1)S(1)} %get-tuple-element.37.refs_0_), channel_id=1, source_target_pairs={{0,12},{1,13},{2,14},{3,15},{4,8},{5,9},{6,10},{7,11},{8,4},{9,5},... | collective-permute-start | bytes 786440 | tf_op jit(solution)/shard_map/far/ppermute | solution.py:64
  12.9 8.9 %collective-permute-start.5 = (bf16[32,4096]{1,0:T(8,128)(2,1)S(1)}, bf16[32,4096]{1,0:T(8,128)(2,1)S(1)}, u32[]{:S(2)}, u32[]{:S(2)}) collective-permute-start(bf16[32,4096]{1,0:T(8,128)(2,1)S(1)} %get-tuple-element.37.refs_0_), channel_id=1, source_target_pairs={{0,2},{1,3},{2,0},{3,1},{4,6},{5,7},{6,4},{7,5},{8,10},{9,11},{10,... | collective-permute-start | bytes 786440 | tf_op jit(solution)/shard_map/mine_x/ppermute | solution.py:64
  13.0 8.8 %collective-permute-start.3 = (bf16[32,4096]{1,0:T(8,128)(2,1)S(1)}, bf16[32,4096]{1,0:T(8,128)(2,1)S(1)}, u32[]{:S(2)}, u32[]{:S(2)}) collective-permute-start(bf16[32,4096]{1,0:T(8,128)(2,1)S(1)} %get-tuple-element.33.refs_2_), channel_id=1, source_target_pairs={{0,2},{1,3},{2,0},{3,1},{4,6},{5,7},{6,4},{7,5},{8,10},{9,11},{10,... | collective-permute-start | bytes 786440 | tf_op jit(solution)/shard_map/rest_x/ppermute | solution.py:64
  13.5 10.8 %collective-permute-start.8 = (bf16[32,4096]{1,0:T(8,128)(2,1)S(1)}, bf16[32,4096]{1,0:T(8,128)(2,1)S(1)}, u32[]{:S(2)}, u32[]{:S(2)}) collective-permute-start(bf16[32,4096]{1,0:T(8,128)(2,1)S(1)} %collective-permute-done.1.refs_0_), channel_id=1, source_target_pairs={{0,16},{1,17},{2,18},{3,19},{4,20},{5,21},{6,22},{7,23},{8,24},{9,... | collective-permute-start | bytes 786440 | tf_op jit(solution)/shard_map/near_p/ppermute | solution.py:64
  19.7 8.3 %collective-permute-start.10 = (bf16[32,4096]{1,0:T(8,128)(2,1)S(1)}, bf16[32,4096]{1,0:T(8,128)(2,1)S(1)}, u32[]{:S(2)}, u32[]{:S(2)}) collective-permute-start(bf16[32,4096]{1,0:T(8,128)(2,1)S(1)} %collective-permute-done.refs_0_), channel_id=1, source_target_pairs={{0,16},{1,17},{2,18},{3,19},{4,20},{5,21},{6,22},{7,23},{8,24},{9,... | collective-permute-start | bytes 786440 | tf_op jit(solution)/shard_map/far_p/ppermute | solution.py:64
  21.2 6.8 %collective-permute-start.2 = (bf16[32,4096]{1,0:T(8,128)(2,1)S(1)}, bf16[32,4096]{1,0:T(8,128)(2,1)S(1)}, u32[]{:S(2)}, u32[]{:S(2)}) collective-permute-start(bf16[32,4096]{1,0:T(8,128)(2,1)S(1)} %collective-permute-done.refs_0_), channel_id=1, source_target_pairs={{0,4},{1,5},{2,6},{3,7},{4,0},{5,1},{6,2},{7,3},{8,12},{9,13},{10,... | collective-permute-start | bytes 786440 | tf_op jit(solution)/shard_map/cross/ppermute | solution.py:64
  21.8 3.1 %collective-permute-start.4 = (bf16[32,4096]{1,0:T(8,128)(2,1)S(1)}, bf16[32,4096]{1,0:T(8,128)(2,1)S(1)}, u32[]{:S(2)}, u32[]{:S(2)}) collective-permute-start(bf16[32,4096]{1,0:T(8,128)(2,1)S(1)} %collective-permute-done.refs_0_), channel_id=1, source_target_pairs={{0,2},{1,3},{2,0},{3,1},{4,6},{5,7},{6,4},{7,5},{8,10},{9,11},{10,... | collective-permute-start | bytes 786440 | tf_op jit(solution)/shard_map/far_x/ppermute | solution.py:64
  24.2 3.8 %collective-permute-start.9 = (bf16[32,4096]{1,0:T(8,128)(2,1)S(1)}, bf16[32,4096]{1,0:T(8,128)(2,1)S(1)}, u32[]{:S(2)}, u32[]{:S(2)}) collective-permute-start(bf16[32,4096]{1,0:T(8,128)(2,1)S(1)} %collective-permute-done.8.refs_2_), channel_id=1, source_target_pairs={{0,2},{1,3},{2,0},{3,1},{4,6},{5,7},{6,4},{7,5},{8,10},{9,11},{10,... | collective-permute-start | bytes 786440 | tf_op jit(solution)/shard_map/near_px/ppermute | solution.py:64
  24.8 6.2 %collective-permute-start.7 = (bf16[32,4096]{1,0:T(8,128)(2,1)S(1)}, bf16[32,4096]{1,0:T(8,128)(2,1)S(1)}, u32[]{:S(2)}, u32[]{:S(2)}) collective-permute-start(bf16[32,4096]{1,0:T(8,128)(2,1)S(1)} %collective-permute-done.1.refs_0_), channel_id=1, source_target_pairs={{0,2},{1,3},{2,0},{3,1},{4,6},{5,7},{6,4},{7,5},{8,10},{9,11},{10,... | collective-permute-start | bytes 786440 | tf_op jit(solution)/shard_map/near_x/ppermute | solution.py:64
  28.0 3.6 %collective-permute-start.12 = (bf16[32,4096]{1,0:T(8,128)(2,1)S(1)}, bf16[32,4096]{1,0:T(8,128)(2,1)S(1)}, u32[]{:S(2)}, u32[]{:S(2)}) collective-permute-start(bf16[32,4096]{1,0:T(8,128)(2,1)S(1)} %collective-permute-done.2.refs_6_), channel_id=1, source_target_pairs={{0,2},{1,3},{2,0},{3,1},{4,6},{5,7},{6,4},{7,5},{8,10},{9,11},{10,... | collective-permute-start | bytes 786440 | tf_op jit(solution)/shard_map/cross_x/ppermute | solution.py:64
  28.0 3.5 %collective-permute-start.11 = (bf16[32,4096]{1,0:T(8,128)(2,1)S(1)}, bf16[32,4096]{1,0:T(8,128)(2,1)S(1)}, u32[]{:S(2)}, u32[]{:S(2)}) collective-permute-start(bf16[32,4096]{1,0:T(8,128)(2,1)S(1)} %collective-permute-done.10.refs_4_), channel_id=1, source_target_pairs={{0,2},{1,3},{2,0},{3,1},{4,6},{5,7},{6,4},{7,5},{8,10},{9,11},{10,... | collective-permute-start | bytes 786440 | tf_op jit(solution)/shard_map/far_px/ppermute | solution.py:64
  28.5 6.1 %collective-permute-start.13 = (bf16[64,1024]{1,0:T(8,128)(2,1)S(1)}, bf16[64,1024]{1,0:T(8,128)(2,1)S(1)}, u32[]{:S(2)}, u32[]{:S(2)}) collective-permute-start(bf16[64,1024]{1,0:T(8,128)(2,1)S(1)} %get-tuple-element.39), channel_id=1, source_target_pairs={{0,1},{1,0},{2,3},{3,2},{4,5},{5,4},{6,7},{7,6},{8,9},{9,8},{10,11... | collective-permute-start | bytes 393224 | tf_op jit(solution)/shard_map/got0/ppermute | solution.py:64
  30.1 5.3 %collective-permute-start.14 = (bf16[16,4096]{1,0:T(8,128)(2,1)S(1)}, bf16[16,4096]{1,0:T(8,128)(2,1)S(1)}, u32[]{:S(2)}, u32[]{:S(2)}) collective-permute-start(bf16[16,4096]{1,0:T(8,128)(2,1)S(1)} %slice.7), channel_id=1, source_target_pairs={{0,4},{1,5},{2,6},{3,7},{4,0},{5,1},{6,2},{7,3},{8,12},{9,13},{10,... | collective-permute-start | bytes 393224 | tf_op jit(solution)/shard_map/cross_pb/ppermute | solution.py:64
  30.9 9.7 %copy-start.1 = (s32[256]{0:T(256)S(1)}, s32[256]{0:T(256)}, u32[]{:S(2)}) copy-start(s32[256]{0:T(256)} %param.15) | copy-start | bytes 3076
  31.0 11.0 %copy-start = (s32[1024]{0:T(1024)S(1)}, s32[1024]{0:T(1024)}, u32[]{:S(2)}) copy-start(s32[1024]{0:T(1024)} %param.14) | copy-start | bytes 12292
  31.0 5.3 %collective-permute-start.6 = (bf16[16,4096]{1,0:T(8,128)(2,1)S(1)}, bf16[16,4096]{1,0:T(8,128)(2,1)S(1)}, u32[]{:S(2)}, u32[]{:S(2)}) collective-permute-start(bf16[16,4096]{1,0:T(8,128)(2,1)S(1)} %slice.6), channel_id=1, source_target_pairs={{0,16},{1,17},{2,18},{3,19},{4,20},{5,21},{6,22},{7,23},{8,24},{9,... | collective-permute-start | bytes 393224 | tf_op jit(solution)/shard_map/cross_pa/ppermute | solution.py:64
  34.1 7.9 %collective-permute-start.18 = (bf16[128,1024]{1,0:T(8,128)(2,1)S(1)}, bf16[128,1024]{1,0:T(8,128)(2,1)S(1)}, u32[]{:S(2)}, u32[]{:S(2)}) collective-permute-start(bf16[128,1024]{1,0:T(8,128)(2,1)S(1)} %get-tuple-element.43), channel_id=1, source_target_pairs={{0,1},{1,0},{2,3},{3,2},{4,5},{5,4},{6,7},{7,6},{8,9},{9,8},{10,11... | collective-permute-start | bytes 786440 | tf_op jit(solution)/shard_map/got1/ppermute | solution.py:64
  35.3 1.3 %collective-permute-start.16 = (bf16[16,4096]{1,0:T(8,128)(2,1)S(1)}, bf16[16,4096]{1,0:T(8,128)(2,1)S(1)}, u32[]{:S(2)}, u32[]{:S(2)}) collective-permute-start(bf16[16,4096]{1,0:T(8,128)(2,1)S(1)} %collective-permute-done.14.refs_1_), channel_id=1, source_target_pairs={{0,2},{1,3},{2,0},{3,1},{4,6},{5,7},{6,4},{7,5},{8,10},{9,11},{10,... | collective-permute-start | bytes 393224 | tf_op jit(solution)/shard_map/cross_pxb/ppermute | solution.py:64
  36.3 1.3 %collective-permute-start.15 = (bf16[16,4096]{1,0:T(8,128)(2,1)S(1)}, bf16[16,4096]{1,0:T(8,128)(2,1)S(1)}, u32[]{:S(2)}, u32[]{:S(2)}) collective-permute-start(bf16[16,4096]{1,0:T(8,128)(2,1)S(1)} %collective-permute-done.6.refs_0_), channel_id=1, source_target_pairs={{0,2},{1,3},{2,0},{3,1},{4,6},{5,7},{6,4},{7,5},{8,10},{9,11},{10,... | collective-permute-start | bytes 393224 | tf_op jit(solution)/shard_map/cross_pxa/ppermute | solution.py:64
  40.1 5.6 %collective-permute-start.17 = (bf16[64,1024]{1,0:T(8,128)(2,1)S(1)}, bf16[64,1024]{1,0:T(8,128)(2,1)S(1)}, u32[]{:S(2)}, u32[]{:S(2)}) collective-permute-start(bf16[64,1024]{1,0:T(8,128)(2,1)S(1)} %get-tuple-element.48), channel_id=1, source_target_pairs={{0,1},{1,0},{2,3},{3,2},{4,5},{5,4},{6,7},{7,6},{8,9},{9,8},{10,11... | collective-permute-start | bytes 393224 | tf_op jit(solution)/shard_map/got2/ppermute | solution.py:64

commit v19 on v18

--- a/solution.py
+++ b/solution.py
@@ -232,14 +232,14 @@
     )(*inputs)
 
 
-def call_scores(weight, train, inputs, stored=0, early=(), columns=None):
+def call_scores(weight, train, inputs, stored=0, early=(), columns=None, sent=bf16):
     columns = columns or (0, train.shape[0])
     n = columns[1] - columns[0]
     total = sum(count for _, rows in inputs for _, count in rows)
     others = [a for a, _ in inputs] + [a for a, _, _ in early if a is not None]
     outs = [jax.ShapeDtypeStruct((stored, n), f32)] if stored else []
     if early:
-        outs += [jax.ShapeDtypeStruct((total - stored, n), t) for t in (bf16, f32)]
+        outs += [jax.ShapeDtypeStruct((total - stored, n), t) for t in (sent, f32)]
     return kernel_call(
         functools.partial(
             score_kernel,
@@ -348,18 +348,19 @@
     far_x = to_core(after(far, rest_x), "far_x")
     mine_x = after(mine_x, far)
     (early0,) = score(rows_of(mine, mine_x, rest, rest_x), stored=128)
-    send0, keep0 = score(rows_of(far, far_x), early=[(early0, 0, 64)])
+    send0, keep0 = score(rows_of(far, far_x), early=[(early0, 0, 64)], sent=f32)
     got0 = to_layer(send0, "got0")
 
     near_p = after(near_p, early0)
     near_px = to_core(near_p, "near_px")
     far_p, cross = after(far_p, near_px, send0), after(cross, send0)
-    far_px = to_core(far_p, "far_px")
+    far_px0 = to_core(far_p[:CHUNK], "far_px0")
+    far_px1 = to_core(far_p[CHUNK:], "far_px1")
     cross_pa = to_part(cross[:CHUNK], "cross_pa")
     cross_pb = to_near(far_p[CHUNK:], "cross_pb")
     cross_x = to_core(cross, "cross_x")
     early1, send1, keep1 = score(
-        rows_of(near, near_x, near_p, near_px, far_p, far_px, cross, cross_x),
+        rows_of(near, near_x, near_p, near_px, far_p, far_px0, far_px1, cross, cross_x),
         stored=128,
         early=[(early0, 64, 64), (None, 0, 64)],
     )

time: 46.7 us -> 47 us (level)
  starting transfers between devices: 15 us -> 16.6 us
  waiting for transfers between devices: 12.4 us -> 11.1 us
    ppermute x19 -> x20, starting transfers between devices: 15 us -> 16.6 us  [permute(): return lax.ppermute(value, AXES, pairs)]
    ppermute x19 -> x20, waiting for transfers between devices: 12.4 us -> 11.1 us  [permute(): return lax.ppermute(value, AXES, pairs)]
  transfers between devices with their start and end apart: 19 -> 20, of which waited for: 8 -> 7; matrix products, arithmetic and copies ran while one was open for 0% -> 0% of each run, Pallas kernels for 32% -> 32%
where the time goes in v19:
time: 47 us; the launch traced here: 46.8 us
  Pallas kernels  18.2 us (39%)
  starting transfers between devices  16.6 us (35%)
  waiting for transfers between devices  11.1 us (24%)
  between operations  0.79 us (2%)
    ppermute x20, starting transfers between devices, permute(): return lax.ppermute(value, AXES, pairs)  16.6 us
    pallas_call x6, Pallas kernels, kernel_call(): pl.pallas_call(kernel, out_shape=outs, in_specs=specs or [VMEM] * len(inp...  16.3 us
    ppermute x20, waiting for transfers between devices, permute(): return lax.ppermute(value, AXES, pairs)  11.1 us
    pallas_call x2, Pallas kernels, call_final(): pl.pallas_call(functools.partial(final_kernel, groups=groups, n_given=len...  1.84 us
  transfers between devices with their start and end apart: 20, of which 7 were waited for; matrix products, arithmetic and copies ran while one was open for 0% of the time, Pallas kernels for 32%

profile of v19, /device:TPU:0, one launch (start us, length us, event | category | flops | bytes accessed | tf_op | source)
XLA Modules:
  0.0 46.8 jit_solution(10765044950539280940)
XLA Ops:
  0.0 2.4 %shard_map.82 = (bf16[32,4096]{1,0:T(8,128)(2,1)S(1)}, bf16[2,256,256]{2,1,0:T(8,128)(2,1)S(1)}, bf16[2,256,512]{2,1,0:T(8,128)(2,1)S(1)}) custom-call(bf16[64,4096]{1,0:T(8,128)(2,1)} %bitcast.9, f32[64,64]{1,0:T(8,128)} %bitcast.11, f32[64,64]{1,0:T(8,128)} %bitcast.12), custom_call_target="tpu_custom_call" | custom-call | tf_op jit(solution)/shard_map/pallas_call | solution.py:225
  2.4 3.1 %collective-permute-start.1 = (bf16[32,4096]{1,0:T(8,128)(2,1)S(1)}, bf16[32,4096]{1,0:T(8,128)(2,1)S(1)}, u32[]{:S(2)}, u32[]{:S(2)}) collective-permute-start(bf16[32,4096]{1,0:T(8,128)(2,1)S(1)} %get-tuple-element.37.refs_0_), channel_id=1, source_target_pairs={{0,4},{1,5},{2,6},{3,7},{4,0},{5,1},{6,2},{7,3},{8,12},{9,13},{10,... | collective-permute-start | bytes 786440 | tf_op jit(solution)/shard_map/near/ppermute | solution.py:64
  5.5 2.5 %collective-permute-start = (bf16[32,4096]{1,0:T(8,128)(2,1)S(1)}, bf16[32,4096]{1,0:T(8,128)(2,1)S(1)}, u32[]{:S(2)}, u32[]{:S(2)}) collective-permute-start(bf16[32,4096]{1,0:T(8,128)(2,1)S(1)} %get-tuple-element.37.refs_0_), channel_id=1, source_target_pairs={{0,12},{1,13},{2,14},{3,15},{4,8},{5,9},{6,10},{7,11},{8,4},{9,5},... | collective-permute-start | bytes 786440 | tf_op jit(solution)/shard_map/far/ppermute | solution.py:64
  8.6 4.3 %shard_map.83 = (bf16[32,4096]{1,0:T(8,128)(2,1)S(1)}, bf16[1024,4096]{1,0:T(8,128)(2,1)S(1)}, f32[8,256]{1,0:T(8,128)S(1)}) custom-call(f32[2]{0:T(128)} %weight_ref.1, s32[1]{0:T(128)S(6)} %copy.13.layer_ref, bf16[64,4096]{1,0:T(8,128)(2,1)} %bitcast.10, bf16[1024,4096]{1,0:T(8,128)(2,1)} %bitcast.8, bf16[2,256,256]{2,1,0:T(8,128)(2,1)S(1)} %get-tuple-element.28.lefts_ref, ...), custom_call_target="tpu_custom_call" | custom-call | tf_op jit(solution)/shard_map/pallas_call | solution.py:225
  13.5 1.5 %collective-permute-start.8 = (bf16[32,4096]{1,0:T(8,128)(2,1)S(1)}, bf16[32,4096]{1,0:T(8,128)(2,1)S(1)}, u32[]{:S(2)}, u32[]{:S(2)}) collective-permute-start(bf16[32,4096]{1,0:T(8,128)(2,1)S(1)} %collective-permute-done.1.refs_0_), channel_id=1, source_target_pairs={{0,16},{1,17},{2,18},{3,19},{4,20},{5,21},{6,22},{7,23},{8,24},{9,... | collective-permute-start | bytes 786440 | tf_op jit(solution)/shard_map/near_p/ppermute | solution.py:64
  15.0 4.7 %collective-permute-done.refs_0_ = bf16[32,4096]{1,0:T(8,128)(2,1)S(1)} collective-permute-done((bf16[32,4096]{1,0:T(8,128)(2,1)S(1)}, bf16[32,4096]{1,0:T(8,128)(2,1)S(1)}, u32[]{:S(2)}, u32[]{:S(2)}) %collective-permute-start) | collective-permute-done | bytes 262176 | tf_op jit(solution)/shard_map/far/ppermute | solution.py:64
  19.7 1.5 %collective-permute-start.10 = (bf16[32,4096]{1,0:T(8,128)(2,1)S(1)}, bf16[32,4096]{1,0:T(8,128)(2,1)S(1)}, u32[]{:S(2)}, u32[]{:S(2)}) collective-permute-start(bf16[32,4096]{1,0:T(8,128)(2,1)S(1)} %collective-permute-done.refs_0_), channel_id=1, source_target_pairs={{0,16},{1,17},{2,18},{3,19},{4,20},{5,21},{6,22},{7,23},{8,24},{9,... | collective-permute-start | bytes 786440 | tf_op jit(solution)/shard_map/far_p/ppermute | solution.py:64
  21.8 2.4 %shard_map.84.refs_2_.refs_9_ = f32[128,1024]{1,0:T(8,128)S(1)} custom-call(f32[8,256]{1,0:T(8,128)S(1)} %get-tuple-element.30.weight_ref, bf16[1024,4096]{1,0:T(8,128)(2,1)S(1)} %get-tuple-element.31.train_ref, bf16[32,4096]{1,0:T(8,128)(2,1)S(1)} %get-tuple-element.37.refs_0_, bf16[32,4096]{1,0:T(8,128)(2,1)S(1)} %collective-permute-done.5.refs_1_, ...), custom_call_target="tpu_custom_call" | custom-call | tf_op jit(solution)/shard_map/pallas_call | solution.py:225
  24.2 0.6 %collective-permute-start.9 = (bf16[32,4096]{1,0:T(8,128)(2,1)S(1)}, bf16[32,4096]{1,0:T(8,128)(2,1)S(1)}, u32[]{:S(2)}, u32[]{:S(2)}) collective-permute-start(bf16[32,4096]{1,0:T(8,128)(2,1)S(1)} %collective-permute-done.8.refs_2_), channel_id=1, source_target_pairs={{0,2},{1,3},{2,0},{3,1},{4,6},{5,7},{6,4},{7,5},{8,10},{9,11},{10,... | collective-permute-start | bytes 786440 | tf_op jit(solution)/shard_map/near_px/ppermute | solution.py:64
  24.9 2.4 %shard_map.85 = (f32[64,1024]{1,0:T(8,128)S(1)}, f32[64,1024]{1,0:T(8,128)S(1)}) custom-call(f32[8,256]{1,0:T(8,128)S(1)} %get-tuple-element.30.weight_ref, bf16[1024,4096]{1,0:T(8,128)(2,1)S(1)} %get-tuple-element.31.train_ref, bf16[32,4096]{1,0:T(8,128)(2,1)S(1)} %collective-permute-done.refs_0_, bf16[32,4096]{1,0:T(8,128)(2,1)S(1)} %collective-permute-done.4.refs_1_, ...), custom_call_target="tpu_custom_call" | custom-call | tf_op jit(solution)/shard_map/pallas_call | solution.py:225
  27.3 1.6 %collective-permute-start.14 = (f32[64,1024]{1,0:T(8,128)S(1)}, f32[64,1024]{1,0:T(8,128)S(1)}, u32[]{:S(2)}, u32[]{:S(2)}) collective-permute-start(f32[64,1024]{1,0:T(8,128)S(1)} %get-tuple-element.39), channel_id=1, source_target_pairs={{0,1},{1,0},{2,3},{3,2},{4,5},{5,4},{6,7},{7,6},{8,9},{9,8},{10,11... | collective-permute-start | bytes 786440 | tf_op jit(solution)/shard_map/got0/ppermute | solution.py:64
  29.6 1.5 %collective-permute-start.15 = (bf16[16,4096]{1,0:T(8,128)(2,1)S(1)}, bf16[16,4096]{1,0:T(8,128)(2,1)S(1)}, u32[]{:S(2)}, u32[]{:S(2)}) collective-permute-start(bf16[16,4096]{1,0:T(8,128)(2,1)S(1)} %get-tuple-element.51), channel_id=1, source_target_pairs={{0,4},{1,5},{2,6},{3,7},{4,0},{5,1},{6,2},{7,3},{8,12},{9,13},{10,... | collective-permute-start | bytes 393224 | tf_op jit(solution)/shard_map/cross_pb/ppermute | solution.py:64
  31.1 0.6 %collective-permute-start.6 = (bf16[16,4096]{1,0:T(8,128)(2,1)S(1)}, bf16[16,4096]{1,0:T(8,128)(2,1)S(1)}, u32[]{:S(2)}, u32[]{:S(2)}) collective-permute-start(bf16[16,4096]{1,0:T(8,128)(2,1)S(1)} %slice.10), channel_id=1, source_target_pairs={{0,16},{1,17},{2,18},{3,19},{4,20},{5,21},{6,22},{7,23},{8,24},{9,... | collective-permute-start | bytes 393224 | tf_op jit(solution)/shard_map/cross_pa/ppermute | solution.py:64
  31.7 2.5 %shard_map.86 = (f32[128,1024]{1,0:T(8,128)S(1)}, bf16[128,1024]{1,0:T(8,128)(2,1)S(1)}, f32[128,1024]{1,0:T(8,128)S(1)}) custom-call(f32[8,256]{1,0:T(8,128)S(1)} %get-tuple-element.30.weight_ref, bf16[1024,4096]{1,0:T(8,128)(2,1)S(1)} %get-tuple-element.31.train_ref, bf16[32,4096]{1,0:T(8,128)(2,1)S(1)} %collective-permute-done.1.refs_0_, ...), custom_call_target="tpu_custom_call" | custom-call | tf_op jit(solution)/shard_map/pallas_call | solution.py:225
  34.2 0.6 %collective-permute-start.19 = (bf16[128,1024]{1,0:T(8,128)(2,1)S(1)}, bf16[128,1024]{1,0:T(8,128)(2,1)S(1)}, u32[]{:S(2)}, u32[]{:S(2)}) collective-permute-start(bf16[128,1024]{1,0:T(8,128)(2,1)S(1)} %get-tuple-element.43), channel_id=1, source_target_pairs={{0,1},{1,0},{2,3},{3,2},{4,5},{5,4},{6,7},{7,6},{8,9},{9,8},{10,11... | collective-permute-start | bytes 786440 | tf_op jit(solution)/shard_map/got1/ppermute | solution.py:64
  34.8 1.2 %collective-permute-done.14.refs_1_ = f32[64,1024]{1,0:T(8,128)S(1)} collective-permute-done((f32[64,1024]{1,0:T(8,128)S(1)}, f32[64,1024]{1,0:T(8,128)S(1)}, u32[]{:S(2)}, u32[]{:S(2)}) %collective-permute-start.14) | collective-permute-done | bytes 262176 | tf_op jit(solution)/shard_map/got0/ppermute | solution.py:64
  36.0 0.7 %collective-permute-done.6.refs_0_ = bf16[16,4096]{1,0:T(8,128)(2,1)S(1)} collective-permute-done((bf16[16,4096]{1,0:T(8,128)(2,1)S(1)}, bf16[16,4096]{1,0:T(8,128)(2,1)S(1)}, u32[]{:S(2)}, u32[]{:S(2)}) %collective-permute-start.6) | collective-permute-done | bytes 131104 | tf_op jit(solution)/shard_map/cross_pa/ppermute | solution.py:64
  36.7 0.7 %collective-permute-done.17.refs_3_ = bf16[16,4096]{1,0:T(8,128)(2,1)S(1)} collective-permute-done((bf16[16,4096]{1,0:T(8,128)(2,1)S(1)}, bf16[16,4096]{1,0:T(8,128)(2,1)S(1)}, u32[]{:S(2)}, u32[]{:S(2)}) %collective-permute-start.17) | collective-permute-done | bytes 131104 | tf_op jit(solution)/shard_map/cross_pxb/ppermute | solution.py:64
  37.3 0.7 %collective-permute-done.16.refs_2_ = bf16[16,4096]{1,0:T(8,128)(2,1)S(1)} collective-permute-done((bf16[16,4096]{1,0:T(8,128)(2,1)S(1)}, bf16[16,4096]{1,0:T(8,128)(2,1)S(1)}, u32[]{:S(2)}, u32[]{:S(2)}) %collective-permute-start.16) | collective-permute-done | bytes 131104 | tf_op jit(solution)/shard_map/cross_pxa/ppermute | solution.py:64
  38.0 2.4 %shard_map.87 = (bf16[64,1024]{1,0:T(8,128)(2,1)S(1)}, f32[64,1024]{1,0:T(8,128)S(1)}) custom-call(f32[8,256]{1,0:T(8,128)S(1)} %get-tuple-element.30.weight_ref, bf16[1024,4096]{1,0:T(8,128)(2,1)S(1)} %get-tuple-element.31.train_ref, bf16[16,4096]{1,0:T(8,128)(2,1)S(1)} %collective-permute-done.6.refs_0_, ...), custom_call_target="tpu_custom_call" | custom-call | tf_op jit(solution)/shard_map/pallas_call | solution.py:225
  40.4 1.3 %collective-permute-start.18 = (bf16[64,1024]{1,0:T(8,128)(2,1)S(1)}, bf16[64,1024]{1,0:T(8,128)(2,1)S(1)}, u32[]{:S(2)}, u32[]{:S(2)}) collective-permute-start(bf16[64,1024]{1,0:T(8,128)(2,1)S(1)} %get-tuple-element.48), channel_id=1, source_target_pairs={{0,1},{1,0},{2,3},{3,2},{4,5},{5,4},{6,7},{7,6},{8,9},{9,8},{10,11... | collective-permute-start | bytes 393224 | tf_op jit(solution)/shard_map/got2/ppermute | solution.py:64
  42.3 1.0 %shard_map.88.refs_2_ = f32[256,1024]{1,0:T(8,128)} custom-call(s32[1,1024]{1,0:T(1,128)S(1)} %bitcast.6, s32[256,1]{1,0:T(8,128)S(1)} %copy.11.query_ids, f32[64,1024]{1,0:T(8,128)S(1)} %get-tuple-element.49.refs_0_, f32[64,1024]{1,0:T(8,128)S(1)} %collective-permute-done.14.refs_1_, f32[128,1024]{1,0:T(8,128)S(1)} %get-tuple-element.50.refs_2_, ...), custom_call_target="tpu_custom_call" | custom-call | tf_op jit(solution)/shard_map/pallas_call | solution.py:286
  43.3 2.7 %collective-permute-done.18.refs_1_ = bf16[64,1024]{1,0:T(8,128)(2,1)S(1)} collective-permute-done((bf16[64,1024]{1,0:T(8,128)(2,1)S(1)}, bf16[64,1024]{1,0:T(8,128)(2,1)S(1)}, u32[]{:S(2)}, u32[]{:S(2)}) %collective-permute-start.18) | collective-permute-done | bytes 131104 | tf_op jit(solution)/shard_map/got2/ppermute | solution.py:64
  46.0 0.8 %shard_map.89 = f32[256,1024]{1,0:T(8,128)} custom-call(s32[1,1024]{1,0:T(1,128)S(1)} %bitcast.7, s32[256,1]{1,0:T(8,128)S(1)} %copy.11.query_ids, f32[64,1024]{1,0:T(8,128)S(1)} %get-tuple-element.47.refs_0_, bf16[64,1024]{1,0:T(8,128)(2,1)S(1)} %collective-permute-done.18.refs_1_, f32[256,1024]{1,0:T(8,128)} %shard_map.88.refs_2_), custom_call_target="tpu_custom_call", output_to_operand_aliasing={{}: (4, {})} | custom-call | tf_op jit(solution)/shard_map/pallas_call | solution.py:286
  (31 shorter events, 2.6 us)
Async XLA Ops:
  2.4 11.1 %collective-permute-start.1 = (bf16[32,4096]{1,0:T(8,128)(2,1)S(1)}, bf16[32,4096]{1,0:T(8,128)(2,1)S(1)}, u32[]{:S(2)}, u32[]{:S(2)}) collective-permute-start(bf16[32,4096]{1,0:T(8,128)(2,1)S(1)} %get-tuple-element.37.refs_0_), channel_id=1, source_target_pairs={{0,4},{1,5},{2,6},{3,7},{4,0},{5,1},{6,2},{7,3},{8,12},{9,13},{10,... | collective-permute-start | bytes 786440 | tf_op jit(solution)/shard_map/near/ppermute | solution.py:64
  5.5 14.2 %collective-permute-start = (bf16[32,4096]{1,0:T(8,128)(2,1)S(1)}, bf16[32,4096]{1,0:T(8,128)(2,1)S(1)}, u32[]{:S(2)}, u32[]{:S(2)}) collective-permute-start(bf16[32,4096]{1,0:T(8,128)(2,1)S(1)} %get-tuple-element.37.refs_0_), channel_id=1, source_target_pairs={{0,12},{1,13},{2,14},{3,15},{4,8},{5,9},{6,10},{7,11},{8,4},{9,5},... | collective-permute-start | bytes 786440 | tf_op jit(solution)/shard_map/far/ppermute | solution.py:64
  12.9 8.9 %collective-permute-start.3 = (bf16[32,4096]{1,0:T(8,128)(2,1)S(1)}, bf16[32,4096]{1,0:T(8,128)(2,1)S(1)}, u32[]{:S(2)}, u32[]{:S(2)}) collective-permute-start(bf16[32,4096]{1,0:T(8,128)(2,1)S(1)} %get-tuple-element.33.refs_2_), channel_id=1, source_target_pairs={{0,2},{1,3},{2,0},{3,1},{4,6},{5,7},{6,4},{7,5},{8,10},{9,11},{10,... | collective-permute-start | bytes 786440 | tf_op jit(solution)/shard_map/rest_x/ppermute | solution.py:64
  13.0 8.8 %collective-permute-start.5 = (bf16[32,4096]{1,0:T(8,128)(2,1)S(1)}, bf16[32,4096]{1,0:T(8,128)(2,1)S(1)}, u32[]{:S(2)}, u32[]{:S(2)}) collective-permute-start(bf16[32,4096]{1,0:T(8,128)(2,1)S(1)} %get-tuple-element.37.refs_0_), channel_id=1, source_target_pairs={{0,2},{1,3},{2,0},{3,1},{4,6},{5,7},{6,4},{7,5},{8,10},{9,11},{10,... | collective-permute-start | bytes 786440 | tf_op jit(solution)/shard_map/mine_x/ppermute | solution.py:64
  13.5 10.7 %collective-permute-start.8 = (bf16[32,4096]{1,0:T(8,128)(2,1)S(1)}, bf16[32,4096]{1,0:T(8,128)(2,1)S(1)}, u32[]{:S(2)}, u32[]{:S(2)}) collective-permute-start(bf16[32,4096]{1,0:T(8,128)(2,1)S(1)} %collective-permute-done.1.refs_0_), channel_id=1, source_target_pairs={{0,16},{1,17},{2,18},{3,19},{4,20},{5,21},{6,22},{7,23},{8,24},{9,... | collective-permute-start | bytes 786440 | tf_op jit(solution)/shard_map/near_p/ppermute | solution.py:64
  19.7 9.3 %collective-permute-start.10 = (bf16[32,4096]{1,0:T(8,128)(2,1)S(1)}, bf16[32,4096]{1,0:T(8,128)(2,1)S(1)}, u32[]{:S(2)}, u32[]{:S(2)}) collective-permute-start(bf16[32,4096]{1,0:T(8,128)(2,1)S(1)} %collective-permute-done.refs_0_), channel_id=1, source_target_pairs={{0,16},{1,17},{2,18},{3,19},{4,20},{5,21},{6,22},{7,23},{8,24},{9,... | collective-permute-start | bytes 786440 | tf_op jit(solution)/shard_map/far_p/ppermute | solution.py:64
  21.2 7.7 %collective-permute-start.2 = (bf16[32,4096]{1,0:T(8,128)(2,1)S(1)}, bf16[32,4096]{1,0:T(8,128)(2,1)S(1)}, u32[]{:S(2)}, u32[]{:S(2)}) collective-permute-start(bf16[32,4096]{1,0:T(8,128)(2,1)S(1)} %collective-permute-done.refs_0_), channel_id=1, source_target_pairs={{0,4},{1,5},{2,6},{3,7},{4,0},{5,1},{6,2},{7,3},{8,12},{9,13},{10,... | collective-permute-start | bytes 786440 | tf_op jit(solution)/shard_map/cross/ppermute | solution.py:64
  21.8 3.1 %collective-permute-start.4 = (bf16[32,4096]{1,0:T(8,128)(2,1)S(1)}, bf16[32,4096]{1,0:T(8,128)(2,1)S(1)}, u32[]{:S(2)}, u32[]{:S(2)}) collective-permute-start(bf16[32,4096]{1,0:T(8,128)(2,1)S(1)} %collective-permute-done.refs_0_), channel_id=1, source_target_pairs={{0,2},{1,3},{2,0},{3,1},{4,6},{5,7},{6,4},{7,5},{8,10},{9,11},{10,... | collective-permute-start | bytes 786440 | tf_op jit(solution)/shard_map/far_x/ppermute | solution.py:64
  24.2 4.8 %collective-permute-start.9 = (bf16[32,4096]{1,0:T(8,128)(2,1)S(1)}, bf16[32,4096]{1,0:T(8,128)(2,1)S(1)}, u32[]{:S(2)}, u32[]{:S(2)}) collective-permute-start(bf16[32,4096]{1,0:T(8,128)(2,1)S(1)} %collective-permute-done.8.refs_2_), channel_id=1, source_target_pairs={{0,2},{1,3},{2,0},{3,1},{4,6},{5,7},{6,4},{7,5},{8,10},{9,11},{10,... | collective-permute-start | bytes 786440 | tf_op jit(solution)/shard_map/near_px/ppermute | solution.py:64
  24.8 4.8 %collective-permute-start.7 = (bf16[32,4096]{1,0:T(8,128)(2,1)S(1)}, bf16[32,4096]{1,0:T(8,128)(2,1)S(1)}, u32[]{:S(2)}, u32[]{:S(2)}) collective-permute-start(bf16[32,4096]{1,0:T(8,128)(2,1)S(1)} %collective-permute-done.1.refs_0_), channel_id=1, source_target_pairs={{0,2},{1,3},{2,0},{3,1},{4,6},{5,7},{6,4},{7,5},{8,10},{9,11},{10,... | collective-permute-start | bytes 786440 | tf_op jit(solution)/shard_map/near_x/ppermute | solution.py:64
  27.3 8.7 %collective-permute-start.14 = (f32[64,1024]{1,0:T(8,128)S(1)}, f32[64,1024]{1,0:T(8,128)S(1)}, u32[]{:S(2)}, u32[]{:S(2)}) collective-permute-start(f32[64,1024]{1,0:T(8,128)S(1)} %get-tuple-element.39), channel_id=1, source_target_pairs={{0,1},{1,0},{2,3},{3,2},{4,5},{5,4},{6,7},{7,6},{8,9},{9,8},{10,11... | collective-permute-start | bytes 786440 | tf_op jit(solution)/shard_map/got0/ppermute | solution.py:64
  28.9 2.3 %collective-permute-start.13 = (bf16[32,4096]{1,0:T(8,128)(2,1)S(1)}, bf16[32,4096]{1,0:T(8,128)(2,1)S(1)}, u32[]{:S(2)}, u32[]{:S(2)}) collective-permute-start(bf16[32,4096]{1,0:T(8,128)(2,1)S(1)} %collective-permute-done.2.refs_7_), channel_id=1, source_target_pairs={{0,2},{1,3},{2,0},{3,1},{4,6},{5,7},{6,4},{7,5},{8,10},{9,11},{10,... | collective-permute-start | bytes 786440 | tf_op jit(solution)/shard_map/cross_x/ppermute | solution.py:64
  29.0 2.7 %collective-permute-start.11 = (bf16[16,4096]{1,0:T(8,128)(2,1)S(1)}, bf16[16,4096]{1,0:T(8,128)(2,1)S(1)}, u32[]{:S(2)}, u32[]{:S(2)}) collective-permute-start(bf16[16,4096]{1,0:T(8,128)(2,1)S(1)} %get-tuple-element.52), channel_id=1, source_target_pairs={{0,2},{1,3},{2,0},{3,1},{4,6},{5,7},{6,4},{7,5},{8,10},{9,11},{10,... | collective-permute-start | bytes 393224 | tf_op jit(solution)/shard_map/far_px0/ppermute | solution.py:64
  29.5 2.3 %collective-permute-start.12 = (bf16[16,4096]{1,0:T(8,128)(2,1)S(1)}, bf16[16,4096]{1,0:T(8,128)(2,1)S(1)}, u32[]{:S(2)}, u32[]{:S(2)}) collective-permute-start(bf16[16,4096]{1,0:T(8,128)(2,1)S(1)} %get-tuple-element.51), channel_id=1, source_target_pairs={{0,2},{1,3},{2,0},{3,1},{4,6},{5,7},{6,4},{7,5},{8,10},{9,11},{10,... | collective-permute-start | bytes 393224 | tf_op jit(solution)/shard_map/far_px1/ppermute | solution.py:64
  29.6 6.4 %collective-permute-start.15 = (bf16[16,4096]{1,0:T(8,128)(2,1)S(1)}, bf16[16,4096]{1,0:T(8,128)(2,1)S(1)}, u32[]{:S(2)}, u32[]{:S(2)}) collective-permute-start(bf16[16,4096]{1,0:T(8,128)(2,1)S(1)} %get-tuple-element.51), channel_id=1, source_target_pairs={{0,4},{1,5},{2,6},{3,7},{4,0},{5,1},{6,2},{7,3},{8,12},{9,13},{10,... | collective-permute-start | bytes 393224 | tf_op jit(solution)/shard_map/cross_pb/ppermute | solution.py:64
  31.1 10.6 %copy-start.1 = (s32[256]{0:T(256)S(1)}, s32[256]{0:T(256)}, u32[]{:S(2)}) copy-start(s32[256]{0:T(256)} %param.15) | copy-start | bytes 3076
  31.1 11.2 %copy-start = (s32[1024]{0:T(1024)S(1)}, s32[1024]{0:T(1024)}, u32[]{:S(2)}) copy-start(s32[1024]{0:T(1024)} %param.14) | copy-start | bytes 12292
  31.1 5.5 %collective-permute-start.6 = (bf16[16,4096]{1,0:T(8,128)(2,1)S(1)}, bf16[16,4096]{1,0:T(8,128)(2,1)S(1)}, u32[]{:S(2)}, u32[]{:S(2)}) collective-permute-start(bf16[16,4096]{1,0:T(8,128)(2,1)S(1)} %slice.10), channel_id=1, source_target_pairs={{0,16},{1,17},{2,18},{3,19},{4,20},{5,21},{6,22},{7,23},{8,24},{9,... | collective-permute-start | bytes 393224 | tf_op jit(solution)/shard_map/cross_pa/ppermute | solution.py:64
  34.2 8.1 %collective-permute-start.19 = (bf16[128,1024]{1,0:T(8,128)(2,1)S(1)}, bf16[128,1024]{1,0:T(8,128)(2,1)S(1)}, u32[]{:S(2)}, u32[]{:S(2)}) collective-permute-start(bf16[128,1024]{1,0:T(8,128)(2,1)S(1)} %get-tuple-element.43), channel_id=1, source_target_pairs={{0,1},{1,0},{2,3},{3,2},{4,5},{5,4},{6,7},{7,6},{8,9},{9,8},{10,11... | collective-permute-start | bytes 786440 | tf_op jit(solution)/shard_map/got1/ppermute | solution.py:64
  36.0 1.3 %collective-permute-start.17 = (bf16[16,4096]{1,0:T(8,128)(2,1)S(1)}, bf16[16,4096]{1,0:T(8,128)(2,1)S(1)}, u32[]{:S(2)}, u32[]{:S(2)}) collective-permute-start(bf16[16,4096]{1,0:T(8,128)(2,1)S(1)} %collective-permute-done.15.refs_1_), channel_id=1, source_target_pairs={{0,2},{1,3},{2,0},{3,1},{4,6},{5,7},{6,4},{7,5},{8,10},{9,11},{10,... | collective-permute-start | bytes 393224 | tf_op jit(solution)/shard_map/cross_pxb/ppermute | solution.py:64
  36.7 1.3 %collective-permute-start.16 = (bf16[16,4096]{1,0:T(8,128)(2,1)S(1)}, bf16[16,4096]{1,0:T(8,128)(2,1)S(1)}, u32[]{:S(2)}, u32[]{:S(2)}) collective-permute-start(bf16[16,4096]{1,0:T(8,128)(2,1)S(1)} %collective-permute-done.6.refs_0_), channel_id=1, source_target_pairs={{0,2},{1,3},{2,0},{3,1},{4,6},{5,7},{6,4},{7,5},{8,10},{9,11},{10,... | collective-permute-start | bytes 393224 | tf_op jit(solution)/shard_map/cross_pxa/ppermute | solution.py:64
  40.4 5.6 %collective-permute-start.18 = (bf16[64,1024]{1,0:T(8,128)(2,1)S(1)}, bf16[64,1024]{1,0:T(8,128)(2,1)S(1)}, u32[]{:S(2)}, u32[]{:S(2)}) collective-permute-start(bf16[64,1024]{1,0:T(8,128)(2,1)S(1)} %get-tuple-element.48), channel_id=1, source_target_pairs={{0,1},{1,0},{2,3},{3,2},{4,5},{5,4},{6,7},{7,6},{8,9},{9,8},{10,11... | collective-permute-start | bytes 393224 | tf_op jit(solution)/shard_map/got2/ppermute | solution.py:64

commit v20 on v18

--- a/solution.py
+++ b/solution.py
@@ -368,8 +368,14 @@
     cross_pxa = to_core(cross_pa, "cross_pxa")
     cross_pxb = to_core(cross_pb, "cross_pxb")
     last = rows_of(cross_pa, cross_pb, cross_pxa, cross_pxb)
-    send2, keep2 = score(last, early=[(early1, 64, 64)])
+    n = train.shape[0]
+    cut = n * 3 // 4
+    send2, keep2 = score(last, early=[(early1, 64, 64)], columns=(0, cut))
     got2 = to_layer(send2, "got2")
+    early1 = after(early1, send2)
+    send3, keep3 = score(last, early=[(early1, 64, 64)], columns=(cut, n))
+    send3 = after(send3, got1)
+    got3 = to_layer(send3, "got3")
 
     train_ids, query_ids = train_ids[None, :], query_ids[:, None]
     most = call_final(
@@ -381,8 +387,8 @@
     return call_final(
         train_ids,
         query_ids,
-        [keep2, got2],
-        ((3, 0, 1, 0, 0),),
+        [keep2, got2, keep3, got3],
+        ((3, 0, 1, 0, 0), (3, 2, 3, 0, cut)),
         most,
     )
 

time: 46.7 us -> 46.8 us (level)
  waiting for transfers between devices: 12.4 us -> 11.8 us
  starting transfers between devices: 15 us -> 15.5 us
    ppermute x19 -> x20, waiting for transfers between devices: 12.4 us -> 11.8 us  [permute(): return lax.ppermute(value, AXES, pairs)]
    ppermute x19 -> x20, starting transfers between devices: 15 us -> 15.5 us  [permute(): return lax.ppermute(value, AXES, pairs)]
    pallas_call x6 -> x7, Pallas kernels: 16.4 us -> 16.6 us  [kernel_call(): pl.pallas_call(kernel, out_shape=outs, in_specs=specs or [VMEM] * len(inp...]
  transfers between devices with their start and end apart: 19 -> 20, of which waited for: 8 -> 9; matrix products, arithmetic and copies ran while one was open for 0% -> 0% of each run, Pallas kernels for 32% -> 33%
where the time goes in v20:
time: 46.8 us; the launch traced here: 46.7 us
  Pallas kernels  18.4 us (39%)
  starting transfers between devices  15.5 us (33%)
  waiting for transfers between devices  11.8 us (25%)
  between operations  0.79 us (2%)
    pallas_call x7, Pallas kernels, kernel_call(): pl.pallas_call(kernel, out_shape=outs, in_specs=specs or [VMEM] * len(inp...  16.6 us
    ppermute x20, starting transfers between devices, permute(): return lax.ppermute(value, AXES, pairs)  15.5 us
    ppermute x20, waiting for transfers between devices, permute(): return lax.ppermute(value, AXES, pairs)  11.8 us
    pallas_call x2, Pallas kernels, call_final(): pl.pallas_call(functools.partial(final_kernel, groups=groups, n_given=len...  1.85 us
  transfers between devices with their start and end apart: 20, of which 9 were waited for; matrix products, arithmetic and copies ran while one was open for 0% of the time, Pallas kernels for 33%

profile of v20, /device:TPU:0, one launch (start us, length us, event | category | flops | bytes accessed | tf_op | source)
XLA Modules:
  0.0 46.7 jit_solution(7364356120134473652)
XLA Ops:
  0.0 2.4 %shard_map.82 = (bf16[32,4096]{1,0:T(8,128)(2,1)S(1)}, bf16[2,256,256]{2,1,0:T(8,128)(2,1)S(1)}, bf16[2,256,512]{2,1,0:T(8,128)(2,1)S(1)}) custom-call(bf16[64,4096]{1,0:T(8,128)(2,1)} %bitcast.9, f32[64,64]{1,0:T(8,128)} %bitcast.11, f32[64,64]{1,0:T(8,128)} %bitcast.12), custom_call_target="tpu_custom_call" | custom-call | tf_op jit(solution)/shard_map/pallas_call | solution.py:225
  2.4 3.1 %collective-permute-start.1 = (bf16[32,4096]{1,0:T(8,128)(2,1)S(1)}, bf16[32,4096]{1,0:T(8,128)(2,1)S(1)}, u32[]{:S(2)}, u32[]{:S(2)}) collective-permute-start(bf16[32,4096]{1,0:T(8,128)(2,1)S(1)} %get-tuple-element.41.refs_0_), channel_id=1, source_target_pairs={{0,4},{1,5},{2,6},{3,7},{4,0},{5,1},{6,2},{7,3},{8,12},{9,13},{10,... | collective-permute-start | bytes 786440 | tf_op jit(solution)/shard_map/near/ppermute | solution.py:64
  5.5 2.5 %collective-permute-start = (bf16[32,4096]{1,0:T(8,128)(2,1)S(1)}, bf16[32,4096]{1,0:T(8,128)(2,1)S(1)}, u32[]{:S(2)}, u32[]{:S(2)}) collective-permute-start(bf16[32,4096]{1,0:T(8,128)(2,1)S(1)} %get-tuple-element.41.refs_0_), channel_id=1, source_target_pairs={{0,12},{1,13},{2,14},{3,15},{4,8},{5,9},{6,10},{7,11},{8,4},{9,5},... | collective-permute-start | bytes 786440 | tf_op jit(solution)/shard_map/far/ppermute | solution.py:64
  8.6 4.3 %shard_map.83 = (bf16[32,4096]{1,0:T(8,128)(2,1)S(1)}, bf16[1024,4096]{1,0:T(8,128)(2,1)S(1)}, f32[8,256]{1,0:T(8,128)S(1)}) custom-call(f32[2]{0:T(128)} %weight_ref.1, s32[1]{0:T(128)S(6)} %copy.13.layer_ref, bf16[64,4096]{1,0:T(8,128)(2,1)} %bitcast.10, bf16[1024,4096]{1,0:T(8,128)(2,1)} %bitcast.8, bf16[2,256,256]{2,1,0:T(8,128)(2,1)S(1)} %get-tuple-element.32.lefts_ref, ...), custom_call_target="tpu_custom_call" | custom-call | tf_op jit(solution)/shard_map/pallas_call | solution.py:225
  13.5 1.5 %collective-permute-start.8 = (bf16[32,4096]{1,0:T(8,128)(2,1)S(1)}, bf16[32,4096]{1,0:T(8,128)(2,1)S(1)}, u32[]{:S(2)}, u32[]{:S(2)}) collective-permute-start(bf16[32,4096]{1,0:T(8,128)(2,1)S(1)} %collective-permute-done.1.refs_0_), channel_id=1, source_target_pairs={{0,16},{1,17},{2,18},{3,19},{4,20},{5,21},{6,22},{7,23},{8,24},{9,... | collective-permute-start | bytes 786440 | tf_op jit(solution)/shard_map/near_p/ppermute | solution.py:64
  15.0 4.7 %collective-permute-done.refs_0_ = bf16[32,4096]{1,0:T(8,128)(2,1)S(1)} collective-permute-done((bf16[32,4096]{1,0:T(8,128)(2,1)S(1)}, bf16[32,4096]{1,0:T(8,128)(2,1)S(1)}, u32[]{:S(2)}, u32[]{:S(2)}) %collective-permute-start) | collective-permute-done | bytes 262176 | tf_op jit(solution)/shard_map/far/ppermute | solution.py:64
  19.7 1.5 %collective-permute-start.10 = (bf16[32,4096]{1,0:T(8,128)(2,1)S(1)}, bf16[32,4096]{1,0:T(8,128)(2,1)S(1)}, u32[]{:S(2)}, u32[]{:S(2)}) collective-permute-start(bf16[32,4096]{1,0:T(8,128)(2,1)S(1)} %collective-permute-done.refs_0_), channel_id=1, source_target_pairs={{0,16},{1,17},{2,18},{3,19},{4,20},{5,21},{6,22},{7,23},{8,24},{9,... | collective-permute-start | bytes 786440 | tf_op jit(solution)/shard_map/far_p/ppermute | solution.py:64
  21.8 2.4 %shard_map.84.refs_2_.refs_8_ = f32[128,1024]{1,0:T(8,128)S(1)} custom-call(f32[8,256]{1,0:T(8,128)S(1)} %get-tuple-element.34.weight_ref, bf16[1024,4096]{1,0:T(8,128)(2,1)S(1)} %get-tuple-element.35.train_ref, bf16[32,4096]{1,0:T(8,128)(2,1)S(1)} %get-tuple-element.41.refs_0_, bf16[32,4096]{1,0:T(8,128)(2,1)S(1)} %collective-permute-done.5.refs_1_, ...), custom_call_target="tpu_custom_call" | custom-call | tf_op jit(solution)/shard_map/pallas_call | solution.py:225
  24.9 2.4 %shard_map.85 = (bf16[64,1024]{1,0:T(8,128)(2,1)S(1)}, f32[64,1024]{1,0:T(8,128)S(1)}) custom-call(f32[8,256]{1,0:T(8,128)S(1)} %get-tuple-element.34.weight_ref, bf16[1024,4096]{1,0:T(8,128)(2,1)S(1)} %get-tuple-element.35.train_ref, bf16[32,4096]{1,0:T(8,128)(2,1)S(1)} %collective-permute-done.refs_0_, ...), custom_call_target="tpu_custom_call" | custom-call | tf_op jit(solution)/shard_map/pallas_call | solution.py:225
  27.3 0.8 %collective-permute-done.2.refs_6_ = bf16[32,4096]{1,0:T(8,128)(2,1)S(1)} collective-permute-done((bf16[32,4096]{1,0:T(8,128)(2,1)S(1)}, bf16[32,4096]{1,0:T(8,128)(2,1)S(1)}, u32[]{:S(2)}, u32[]{:S(2)}) %collective-permute-start.2) | collective-permute-done | bytes 262176 | tf_op jit(solution)/shard_map/cross/ppermute | solution.py:64
  28.5 1.5 %collective-permute-start.13 = (bf16[64,1024]{1,0:T(8,128)(2,1)S(1)}, bf16[64,1024]{1,0:T(8,128)(2,1)S(1)}, u32[]{:S(2)}, u32[]{:S(2)}) collective-permute-start(bf16[64,1024]{1,0:T(8,128)(2,1)S(1)} %get-tuple-element.43), channel_id=1, source_target_pairs={{0,1},{1,0},{2,3},{3,2},{4,5},{5,4},{6,7},{7,6},{8,9},{9,8},{10,11... | collective-permute-start | bytes 393224 | tf_op jit(solution)/shard_map/got0/ppermute | solution.py:64
  30.1 0.9 %collective-permute-start.14 = (bf16[16,4096]{1,0:T(8,128)(2,1)S(1)}, bf16[16,4096]{1,0:T(8,128)(2,1)S(1)}, u32[]{:S(2)}, u32[]{:S(2)}) collective-permute-start(bf16[16,4096]{1,0:T(8,128)(2,1)S(1)} %slice.7), channel_id=1, source_target_pairs={{0,4},{1,5},{2,6},{3,7},{4,0},{5,1},{6,2},{7,3},{8,12},{9,13},{10,... | collective-permute-start | bytes 393224 | tf_op jit(solution)/shard_map/cross_pb/ppermute | solution.py:64
  31.0 0.6 %collective-permute-start.6 = (bf16[16,4096]{1,0:T(8,128)(2,1)S(1)}, bf16[16,4096]{1,0:T(8,128)(2,1)S(1)}, u32[]{:S(2)}, u32[]{:S(2)}) collective-permute-start(bf16[16,4096]{1,0:T(8,128)(2,1)S(1)} %slice.6), channel_id=1, source_target_pairs={{0,16},{1,17},{2,18},{3,19},{4,20},{5,21},{6,22},{7,23},{8,24},{9,... | collective-permute-start | bytes 393224 | tf_op jit(solution)/shard_map/cross_pa/ppermute | solution.py:64
  31.6 2.5 %shard_map.86 = (f32[128,1024]{1,0:T(8,128)S(1)}, bf16[128,1024]{1,0:T(8,128)(2,1)S(1)}, f32[128,1024]{1,0:T(8,128)S(1)}) custom-call(f32[8,256]{1,0:T(8,128)S(1)} %get-tuple-element.34.weight_ref, bf16[1024,4096]{1,0:T(8,128)(2,1)S(1)} %get-tuple-element.35.train_ref, bf16[32,4096]{1,0:T(8,128)(2,1)S(1)} %collective-permute-done.1.refs_0_, ...), custom_call_target="tpu_custom_call" | custom-call | tf_op jit(solution)/shard_map/pallas_call | solution.py:225
  34.7 0.7 %collective-permute-done.14.refs_1_ = bf16[16,4096]{1,0:T(8,128)(2,1)S(1)} collective-permute-done((bf16[16,4096]{1,0:T(8,128)(2,1)S(1)}, bf16[16,4096]{1,0:T(8,128)(2,1)S(1)}, u32[]{:S(2)}, u32[]{:S(2)}) %collective-permute-start.14) | collective-permute-done | bytes 131104 | tf_op jit(solution)/shard_map/cross_pb/ppermute | solution.py:64
  35.3 1.0 %collective-permute-done.6.refs_0_ = bf16[16,4096]{1,0:T(8,128)(2,1)S(1)} collective-permute-done((bf16[16,4096]{1,0:T(8,128)(2,1)S(1)}, bf16[16,4096]{1,0:T(8,128)(2,1)S(1)}, u32[]{:S(2)}, u32[]{:S(2)}) %collective-permute-start.6) | collective-permute-done | bytes 131104 | tf_op jit(solution)/shard_map/cross_pa/ppermute | solution.py:64
  36.7 1.0 %collective-permute-done.15.refs_2_ = bf16[16,4096]{1,0:T(8,128)(2,1)S(1)} collective-permute-done((bf16[16,4096]{1,0:T(8,128)(2,1)S(1)}, bf16[16,4096]{1,0:T(8,128)(2,1)S(1)}, u32[]{:S(2)}, u32[]{:S(2)}) %collective-permute-start.15) | collective-permute-done | bytes 131104 | tf_op jit(solution)/shard_map/cross_pxa/ppermute | solution.py:64
  37.6 1.9 %shard_map.87 = (bf16[64,768]{1,0:T(8,128)(2,1)S(1)}, f32[64,768]{1,0:T(8,128)S(1)}) custom-call(f32[8,256]{1,0:T(8,128)S(1)} %get-tuple-element.34.weight_ref, bf16[1024,4096]{1,0:T(8,128)(2,1)S(1)} %get-tuple-element.35.train_ref, bf16[16,4096]{1,0:T(8,128)(2,1)S(1)} %collective-permute-done.6.refs_0_, ...), custom_call_target="tpu_custom_call" | custom-call | tf_op jit(solution)/shard_map/pallas_call | solution.py:225
  40.1 0.7 %shard_map.88 = (bf16[64,256]{1,0:T(8,128)(2,1)S(1)}, f32[64,256]{1,0:T(8,128)S(1)}) custom-call(f32[8,256]{1,0:T(8,128)S(1)} %get-tuple-element.34.weight_ref, bf16[1024,4096]{1,0:T(8,128)(2,1)S(1)} %get-tuple-element.35.train_ref, bf16[16,4096]{1,0:T(8,128)(2,1)S(1)} %collective-permute-done.6.refs_0_, ...), custom_call_target="tpu_custom_call" | custom-call | tf_op jit(solution)/shard_map/pallas_call | solution.py:225
  40.8 1.1 %collective-permute-done.18.refs_3_ = bf16[128,1024]{1,0:T(8,128)(2,1)S(1)} collective-permute-done((bf16[128,1024]{1,0:T(8,128)(2,1)S(1)}, bf16[128,1024]{1,0:T(8,128)(2,1)S(1)}, u32[]{:S(2)}, u32[]{:S(2)}) %collective-permute-start.18) | collective-permute-done | bytes 262176 | tf_op jit(solution)/shard_map/got1/ppermute | solution.py:64
  42.6 1.0 %shard_map.89.refs_4_ = f32[256,1024]{1,0:T(8,128)} custom-call(s32[1,1024]{1,0:T(1,128)S(1)} %bitcast.6, s32[256,1]{1,0:T(8,128)S(1)} %copy.11.query_ids, f32[64,1024]{1,0:T(8,128)S(1)} %get-tuple-element.57.refs_0_, bf16[64,1024]{1,0:T(8,128)(2,1)S(1)} %collective-permute-done.13.refs_1_, f32[128,1024]{1,0:T(8,128)S(1)} %get-tuple-element.58.refs_2_, ...), custom_call_target="tpu_custom_call" | custom-call | tf_op jit(solution)/shard_map/pallas_call | solution.py:286
  43.7 1.1 %collective-permute-done.17.refs_1_ = bf16[64,768]{1,0:T(8,128)(2,1)S(1)} collective-permute-done((bf16[64,768]{1,0:T(8,128)(2,1)S(1)}, bf16[64,768]{1,0:T(8,128)(2,1)S(1)}, u32[]{:S(2)}, u32[]{:S(2)}) %collective-permute-start.17) | collective-permute-done | bytes 98336 | tf_op jit(solution)/shard_map/got2/ppermute | solution.py:64
  44.8 1.1 %collective-permute-done.19.refs_3_ = bf16[64,256]{1,0:T(8,128)(2,1)S(1)} collective-permute-done((bf16[64,256]{1,0:T(8,128)(2,1)S(1)}, bf16[64,256]{1,0:T(8,128)(2,1)S(1)}, u32[]{:S(2)}, u32[]{:S(2)}) %collective-permute-start.19) | collective-permute-done | bytes 32800 | tf_op jit(solution)/shard_map/got3/ppermute | solution.py:64
  45.9 0.8 %shard_map.90 = f32[256,1024]{1,0:T(8,128)} custom-call(s32[1,1024]{1,0:T(1,128)S(1)} %bitcast.7, s32[256,1]{1,0:T(8,128)S(1)} %copy.11.query_ids, f32[64,768]{1,0:T(8,128)S(1)} %get-tuple-element.51.refs_0_, bf16[64,768]{1,0:T(8,128)(2,1)S(1)} %collective-permute-done.17.refs_1_, ...), custom_call_target="tpu_custom_call", output_to_operand_aliasing={{}: (6, {})} | custom-call | tf_op jit(solution)/shard_map/pallas_call | solution.py:286
  (32 shorter events, 4.5 us)
Async XLA Ops:
  2.4 11.1 %collective-permute-start.1 = (bf16[32,4096]{1,0:T(8,128)(2,1)S(1)}, bf16[32,4096]{1,0:T(8,128)(2,1)S(1)}, u32[]{:S(2)}, u32[]{:S(2)}) collective-permute-start(bf16[32,4096]{1,0:T(8,128)(2,1)S(1)} %get-tuple-element.41.refs_0_), channel_id=1, source_target_pairs={{0,4},{1,5},{2,6},{3,7},{4,0},{5,1},{6,2},{7,3},{8,12},{9,13},{10,... | collective-permute-start | bytes 786440 | tf_op jit(solution)/shard_map/near/ppermute | solution.py:64
  5.5 14.2 %collective-permute-start = (bf16[32,4096]{1,0:T(8,128)(2,1)S(1)}, bf16[32,4096]{1,0:T(8,128)(2,1)S(1)}, u32[]{:S(2)}, u32[]{:S(2)}) collective-permute-start(bf16[32,4096]{1,0:T(8,128)(2,1)S(1)} %get-tuple-element.41.refs_0_), channel_id=1, source_target_pairs={{0,12},{1,13},{2,14},{3,15},{4,8},{5,9},{6,10},{7,11},{8,4},{9,5},... | collective-permute-start | bytes 786440 | tf_op jit(solution)/shard_map/far/ppermute | solution.py:64
  12.9 8.9 %collective-permute-start.5 = (bf16[32,4096]{1,0:T(8,128)(2,1)S(1)}, bf16[32,4096]{1,0:T(8,128)(2,1)S(1)}, u32[]{:S(2)}, u32[]{:S(2)}) collective-permute-start(bf16[32,4096]{1,0:T(8,128)(2,1)S(1)} %get-tuple-element.41.refs_0_), channel_id=1, source_target_pairs={{0,2},{1,3},{2,0},{3,1},{4,6},{5,7},{6,4},{7,5},{8,10},{9,11},{10,... | collective-permute-start | bytes 786440 | tf_op jit(solution)/shard_map/mine_x/ppermute | solution.py:64
  13.0 8.8 %collective-permute-start.3 = (bf16[32,4096]{1,0:T(8,128)(2,1)S(1)}, bf16[32,4096]{1,0:T(8,128)(2,1)S(1)}, u32[]{:S(2)}, u32[]{:S(2)}) collective-permute-start(bf16[32,4096]{1,0:T(8,128)(2,1)S(1)} %get-tuple-element.37.refs_2_), channel_id=1, source_target_pairs={{0,2},{1,3},{2,0},{3,1},{4,6},{5,7},{6,4},{7,5},{8,10},{9,11},{10,... | collective-permute-start | bytes 786440 | tf_op jit(solution)/shard_map/rest_x/ppermute | solution.py:64
  13.5 10.8 %collective-permute-start.8 = (bf16[32,4096]{1,0:T(8,128)(2,1)S(1)}, bf16[32,4096]{1,0:T(8,128)(2,1)S(1)}, u32[]{:S(2)}, u32[]{:S(2)}) collective-permute-start(bf16[32,4096]{1,0:T(8,128)(2,1)S(1)} %collective-permute-done.1.refs_0_), channel_id=1, source_target_pairs={{0,16},{1,17},{2,18},{3,19},{4,20},{5,21},{6,22},{7,23},{8,24},{9,... | collective-permute-start | bytes 786440 | tf_op jit(solution)/shard_map/near_p/ppermute | solution.py:64
  19.7 8.3 %collective-permute-start.10 = (bf16[32,4096]{1,0:T(8,128)(2,1)S(1)}, bf16[32,4096]{1,0:T(8,128)(2,1)S(1)}, u32[]{:S(2)}, u32[]{:S(2)}) collective-permute-start(bf16[32,4096]{1,0:T(8,128)(2,1)S(1)} %collective-permute-done.refs_0_), channel_id=1, source_target_pairs={{0,16},{1,17},{2,18},{3,19},{4,20},{5,21},{6,22},{7,23},{8,24},{9,... | collective-permute-start | bytes 786440 | tf_op jit(solution)/shard_map/far_p/ppermute | solution.py:64
  21.2 6.8 %collective-permute-start.2 = (bf16[32,4096]{1,0:T(8,128)(2,1)S(1)}, bf16[32,4096]{1,0:T(8,128)(2,1)S(1)}, u32[]{:S(2)}, u32[]{:S(2)}) collective-permute-start(bf16[32,4096]{1,0:T(8,128)(2,1)S(1)} %collective-permute-done.refs_0_), channel_id=1, source_target_pairs={{0,4},{1,5},{2,6},{3,7},{4,0},{5,1},{6,2},{7,3},{8,12},{9,13},{10,... | collective-permute-start | bytes 786440 | tf_op jit(solution)/shard_map/cross/ppermute | solution.py:64
  21.8 3.1 %collective-permute-start.4 = (bf16[32,4096]{1,0:T(8,128)(2,1)S(1)}, bf16[32,4096]{1,0:T(8,128)(2,1)S(1)}, u32[]{:S(2)}, u32[]{:S(2)}) collective-permute-start(bf16[32,4096]{1,0:T(8,128)(2,1)S(1)} %collective-permute-done.refs_0_), channel_id=1, source_target_pairs={{0,2},{1,3},{2,0},{3,1},{4,6},{5,7},{6,4},{7,5},{8,10},{9,11},{10,... | collective-permute-start | bytes 786440 | tf_op jit(solution)/shard_map/far_x/ppermute | solution.py:64
  24.2 3.8 %collective-permute-start.9 = (bf16[32,4096]{1,0:T(8,128)(2,1)S(1)}, bf16[32,4096]{1,0:T(8,128)(2,1)S(1)}, u32[]{:S(2)}, u32[]{:S(2)}) collective-permute-start(bf16[32,4096]{1,0:T(8,128)(2,1)S(1)} %collective-permute-done.8.refs_2_), channel_id=1, source_target_pairs={{0,2},{1,3},{2,0},{3,1},{4,6},{5,7},{6,4},{7,5},{8,10},{9,11},{10,... | collective-permute-start | bytes 786440 | tf_op jit(solution)/shard_map/near_px/ppermute | solution.py:64
  24.8 6.2 %collective-permute-start.7 = (bf16[32,4096]{1,0:T(8,128)(2,1)S(1)}, bf16[32,4096]{1,0:T(8,128)(2,1)S(1)}, u32[]{:S(2)}, u32[]{:S(2)}) collective-permute-start(bf16[32,4096]{1,0:T(8,128)(2,1)S(1)} %collective-permute-done.1.refs_0_), channel_id=1, source_target_pairs={{0,2},{1,3},{2,0},{3,1},{4,6},{5,7},{6,4},{7,5},{8,10},{9,11},{10,... | collective-permute-start | bytes 786440 | tf_op jit(solution)/shard_map/near_x/ppermute | solution.py:64
  28.0 3.5 %collective-permute-start.12 = (bf16[32,4096]{1,0:T(8,128)(2,1)S(1)}, bf16[32,4096]{1,0:T(8,128)(2,1)S(1)}, u32[]{:S(2)}, u32[]{:S(2)}) collective-permute-start(bf16[32,4096]{1,0:T(8,128)(2,1)S(1)} %collective-permute-done.2.refs_6_), channel_id=1, source_target_pairs={{0,2},{1,3},{2,0},{3,1},{4,6},{5,7},{6,4},{7,5},{8,10},{9,11},{10,... | collective-permute-start | bytes 786440 | tf_op jit(solution)/shard_map/cross_x/ppermute | solution.py:64
  28.0 3.5 %collective-permute-start.11 = (bf16[32,4096]{1,0:T(8,128)(2,1)S(1)}, bf16[32,4096]{1,0:T(8,128)(2,1)S(1)}, u32[]{:S(2)}, u32[]{:S(2)}) collective-permute-start(bf16[32,4096]{1,0:T(8,128)(2,1)S(1)} %collective-permute-done.10.refs_4_), channel_id=1, source_target_pairs={{0,2},{1,3},{2,0},{3,1},{4,6},{5,7},{6,4},{7,5},{8,10},{9,11},{10,... | collective-permute-start | bytes 786440 | tf_op jit(solution)/shard_map/far_px/ppermute | solution.py:64
  28.5 6.1 %collective-permute-start.13 = (bf16[64,1024]{1,0:T(8,128)(2,1)S(1)}, bf16[64,1024]{1,0:T(8,128)(2,1)S(1)}, u32[]{:S(2)}, u32[]{:S(2)}) collective-permute-start(bf16[64,1024]{1,0:T(8,128)(2,1)S(1)} %get-tuple-element.43), channel_id=1, source_target_pairs={{0,1},{1,0},{2,3},{3,2},{4,5},{5,4},{6,7},{7,6},{8,9},{9,8},{10,11... | collective-permute-start | bytes 393224 | tf_op jit(solution)/shard_map/got0/ppermute | solution.py:64
  30.1 5.3 %collective-permute-start.14 = (bf16[16,4096]{1,0:T(8,128)(2,1)S(1)}, bf16[16,4096]{1,0:T(8,128)(2,1)S(1)}, u32[]{:S(2)}, u32[]{:S(2)}) collective-permute-start(bf16[16,4096]{1,0:T(8,128)(2,1)S(1)} %slice.7), channel_id=1, source_target_pairs={{0,4},{1,5},{2,6},{3,7},{4,0},{5,1},{6,2},{7,3},{8,12},{9,13},{10,... | collective-permute-start | bytes 393224 | tf_op jit(solution)/shard_map/cross_pb/ppermute | solution.py:64
  31.0 5.3 %collective-permute-start.6 = (bf16[16,4096]{1,0:T(8,128)(2,1)S(1)}, bf16[16,4096]{1,0:T(8,128)(2,1)S(1)}, u32[]{:S(2)}, u32[]{:S(2)}) collective-permute-start(bf16[16,4096]{1,0:T(8,128)(2,1)S(1)} %slice.6), channel_id=1, source_target_pairs={{0,16},{1,17},{2,18},{3,19},{4,20},{5,21},{6,22},{7,23},{8,24},{9,... | collective-permute-start | bytes 393224 | tf_op jit(solution)/shard_map/cross_pa/ppermute | solution.py:64
  34.1 7.9 %collective-permute-start.18 = (bf16[128,1024]{1,0:T(8,128)(2,1)S(1)}, bf16[128,1024]{1,0:T(8,128)(2,1)S(1)}, u32[]{:S(2)}, u32[]{:S(2)}) collective-permute-start(bf16[128,1024]{1,0:T(8,128)(2,1)S(1)} %get-tuple-element.47), channel_id=1, source_target_pairs={{0,1},{1,0},{2,3},{3,2},{4,5},{5,4},{6,7},{7,6},{8,9},{9,8},{10,11... | collective-permute-start | bytes 786440 | tf_op jit(solution)/shard_map/got1/ppermute | solution.py:64
  35.3 1.3 %collective-permute-start.16 = (bf16[16,4096]{1,0:T(8,128)(2,1)S(1)}, bf16[16,4096]{1,0:T(8,128)(2,1)S(1)}, u32[]{:S(2)}, u32[]{:S(2)}) collective-permute-start(bf16[16,4096]{1,0:T(8,128)(2,1)S(1)} %collective-permute-done.14.refs_1_), channel_id=1, source_target_pairs={{0,2},{1,3},{2,0},{3,1},{4,6},{5,7},{6,4},{7,5},{8,10},{9,11},{10,... | collective-permute-start | bytes 393224 | tf_op jit(solution)/shard_map/cross_pxb/ppermute | solution.py:64
  36.3 1.3 %collective-permute-start.15 = (bf16[16,4096]{1,0:T(8,128)(2,1)S(1)}, bf16[16,4096]{1,0:T(8,128)(2,1)S(1)}, u32[]{:S(2)}, u32[]{:S(2)}) collective-permute-start(bf16[16,4096]{1,0:T(8,128)(2,1)S(1)} %collective-permute-done.6.refs_0_), channel_id=1, source_target_pairs={{0,2},{1,3},{2,0},{3,1},{4,6},{5,7},{6,4},{7,5},{8,10},{9,11},{10,... | collective-permute-start | bytes 393224 | tf_op jit(solution)/shard_map/cross_pxa/ppermute | solution.py:64
  37.6 4.8 %copy-start.1 = (s32[256]{0:T(256)S(1)}, s32[256]{0:T(256)}, u32[]{:S(2)}) copy-start(s32[256]{0:T(256)} %param.15) | copy-start | bytes 3076
  37.6 5.0 %copy-start = (s32[1024]{0:T(1024)S(1)}, s32[1024]{0:T(1024)}, u32[]{:S(2)}) copy-start(s32[1024]{0:T(1024)} %param.14) | copy-start | bytes 12292
  39.5 5.3 %collective-permute-start.17 = (bf16[64,768]{1,0:T(8,128)(2,1)S(1)}, bf16[64,768]{1,0:T(8,128)(2,1)S(1)}, u32[]{:S(2)}, u32[]{:S(2)}) collective-permute-start(bf16[64,768]{1,0:T(8,128)(2,1)S(1)} %get-tuple-element.52), channel_id=1, source_target_pairs={{0,1},{1,0},{2,3},{3,2},{4,5},{5,4},{6,7},{7,6},{8,9},{9,8},{10,11... | collective-permute-start | bytes 294920 | tf_op jit(solution)/shard_map/got2/ppermute | solution.py:64
  41.9 3.9 %collective-permute-start.19 = (bf16[64,256]{1,0:T(8,128)(2,1)S(1)}, bf16[64,256]{1,0:T(8,128)(2,1)S(1)}, u32[]{:S(2)}, u32[]{:S(2)}) collective-permute-start(bf16[64,256]{1,0:T(8,128)(2,1)S(1)} %get-tuple-element.56), channel_id=1, source_target_pairs={{0,1},{1,0},{2,3},{3,2},{4,5},{5,4},{6,7},{7,6},{8,9},{9,8},{10,11... | collective-permute-start | bytes 98312 | tf_op jit(solution)/shard_map/got3/ppermute | solution.py:64

commit v21 on v18

--- a/solution.py
+++ b/solution.py
@@ -355,8 +355,7 @@
     near_px = to_core(near_p, "near_px")
     far_p, cross = after(far_p, near_px, send0), after(cross, send0)
     far_px = to_core(far_p, "far_px")
-    cross_pa = to_part(cross[:CHUNK], "cross_pa")
-    cross_pb = to_near(far_p[CHUNK:], "cross_pb")
+    cross_p = to_near(far_p, "cross_p")
     cross_x = to_core(cross, "cross_x")
     early1, send1, keep1 = score(
         rows_of(near, near_x, near_p, near_px, far_p, far_px, cross, cross_x),
@@ -364,10 +363,10 @@
         early=[(early0, 64, 64), (None, 0, 64)],
     )
     got1 = to_layer(send1, "got1")
-    cross_pa, cross_pb = after(cross_pa, send1, got0), after(cross_pb, send1, got0)
-    cross_pxa = to_core(cross_pa, "cross_pxa")
-    cross_pxb = to_core(cross_pb, "cross_pxb")
-    last = rows_of(cross_pa, cross_pb, cross_pxa, cross_pxb)
+    cross_p = after(cross_p, send1, got0)
+    cross_pxa = to_core(cross_p[:CHUNK], "cross_pxa")
+    cross_pxb = to_core(cross_p[CHUNK:], "cross_pxb")
+    last = rows_of(cross_p, cross_pxa, cross_pxb)
     send2, keep2 = score(last, early=[(early1, 64, 64)])
     got2 = to_layer(send2, "got2")
 

time: 46.7 us -> 47.3 us (1.013)
  starting transfers between devices: 15 us -> 16.6 us
  waiting for transfers between devices: 12.4 us -> 11.4 us
    ppermute x19 -> x18, starting transfers between devices: 15 us -> 16.6 us  [permute(): return lax.ppermute(value, AXES, pairs)]
    ppermute x19 -> x18, waiting for transfers between devices: 12.4 us -> 11.4 us  [permute(): return lax.ppermute(value, AXES, pairs)]
  transfers between devices with their start and end apart: 19 -> 18, of which waited for: 8 -> 6; matrix products, arithmetic and copies ran while one was open for 0% -> 0% of each run, Pallas kernels for 32% -> 32%
where the time goes in v21:
time: 47.3 us; the launch traced here: 47.2 us
  Pallas kernels  18.2 us (38%)
  starting transfers between devices  16.6 us (35%)
  waiting for transfers between devices  11.4 us (24%)
  between operations  0.81 us (2%)
    ppermute x18, starting transfers between devices, permute(): return lax.ppermute(value, AXES, pairs)  16.6 us
    pallas_call x6, Pallas kernels, kernel_call(): pl.pallas_call(kernel, out_shape=outs, in_specs=specs or [VMEM] * len(inp...  16.4 us
    ppermute x18, waiting for transfers between devices, permute(): return lax.ppermute(value, AXES, pairs)  11.4 us
    pallas_call x2, Pallas kernels, call_final(): pl.pallas_call(functools.partial(final_kernel, groups=groups, n_given=len...  1.85 us
  transfers between devices with their start and end apart: 18, of which 6 were waited for; matrix products, arithmetic and copies ran while one was open for 0% of the time, Pallas kernels for 32%

profile of v21, /device:TPU:0, one launch (start us, length us, event | category | flops | bytes accessed | tf_op | source)
XLA Modules:
  0.0 47.2 jit_solution(850508760512600967)
XLA Ops:
  0.0 2.4 %shard_map.82 = (bf16[32,4096]{1,0:T(8,128)(2,1)S(1)}, bf16[2,256,256]{2,1,0:T(8,128)(2,1)S(1)}, bf16[2,256,512]{2,1,0:T(8,128)(2,1)S(1)}) custom-call(bf16[64,4096]{1,0:T(8,128)(2,1)} %bitcast.9, f32[64,64]{1,0:T(8,128)} %bitcast.11, f32[64,64]{1,0:T(8,128)} %bitcast.12), custom_call_target="tpu_custom_call" | custom-call | tf_op jit(solution)/shard_map/pallas_call | solution.py:225
  2.4 3.1 %collective-permute-start.1 = (bf16[32,4096]{1,0:T(8,128)(2,1)S(1)}, bf16[32,4096]{1,0:T(8,128)(2,1)S(1)}, u32[]{:S(2)}, u32[]{:S(2)}) collective-permute-start(bf16[32,4096]{1,0:T(8,128)(2,1)S(1)} %get-tuple-element.35.refs_0_), channel_id=1, source_target_pairs={{0,4},{1,5},{2,6},{3,7},{4,0},{5,1},{6,2},{7,3},{8,12},{9,13},{10,... | collective-permute-start | bytes 786440 | tf_op jit(solution)/shard_map/near/ppermute | solution.py:64
  5.5 2.5 %collective-permute-start = (bf16[32,4096]{1,0:T(8,128)(2,1)S(1)}, bf16[32,4096]{1,0:T(8,128)(2,1)S(1)}, u32[]{:S(2)}, u32[]{:S(2)}) collective-permute-start(bf16[32,4096]{1,0:T(8,128)(2,1)S(1)} %get-tuple-element.35.refs_0_), channel_id=1, source_target_pairs={{0,12},{1,13},{2,14},{3,15},{4,8},{5,9},{6,10},{7,11},{8,4},{9,5},... | collective-permute-start | bytes 786440 | tf_op jit(solution)/shard_map/far/ppermute | solution.py:64
  8.6 4.3 %shard_map.83 = (bf16[32,4096]{1,0:T(8,128)(2,1)S(1)}, bf16[1024,4096]{1,0:T(8,128)(2,1)S(1)}, f32[8,256]{1,0:T(8,128)S(1)}) custom-call(f32[2]{0:T(128)} %weight_ref.1, s32[1]{0:T(128)S(6)} %copy.13.layer_ref, bf16[64,4096]{1,0:T(8,128)(2,1)} %bitcast.10, bf16[1024,4096]{1,0:T(8,128)(2,1)} %bitcast.8, bf16[2,256,256]{2,1,0:T(8,128)(2,1)S(1)} %get-tuple-element.27.lefts_ref, ...), custom_call_target="tpu_custom_call" | custom-call | tf_op jit(solution)/shard_map/pallas_call | solution.py:225
  13.5 1.5 %collective-permute-start.3 = (bf16[32,4096]{1,0:T(8,128)(2,1)S(1)}, bf16[32,4096]{1,0:T(8,128)(2,1)S(1)}, u32[]{:S(2)}, u32[]{:S(2)}) collective-permute-start(bf16[32,4096]{1,0:T(8,128)(2,1)S(1)} %collective-permute-done.1.refs_0_), channel_id=1, source_target_pairs={{0,16},{1,17},{2,18},{3,19},{4,20},{5,21},{6,22},{7,23},{8,24},{9,... | collective-permute-start | bytes 786440 | tf_op jit(solution)/shard_map/near_p/ppermute | solution.py:64
  15.0 4.7 %collective-permute-done.refs_0_ = bf16[32,4096]{1,0:T(8,128)(2,1)S(1)} collective-permute-done((bf16[32,4096]{1,0:T(8,128)(2,1)S(1)}, bf16[32,4096]{1,0:T(8,128)(2,1)S(1)}, u32[]{:S(2)}, u32[]{:S(2)}) %collective-permute-start) | collective-permute-done | bytes 262176 | tf_op jit(solution)/shard_map/far/ppermute | solution.py:64
  19.7 0.6 %collective-permute-start.11 = (bf16[32,4096]{1,0:T(8,128)(2,1)S(1)}, bf16[32,4096]{1,0:T(8,128)(2,1)S(1)}, u32[]{:S(2)}, u32[]{:S(2)}) collective-permute-start(bf16[32,4096]{1,0:T(8,128)(2,1)S(1)} %collective-permute-done.refs_0_), channel_id=1, source_target_pairs={{0,4},{1,5},{2,6},{3,7},{4,0},{5,1},{6,2},{7,3},{8,12},{9,13},{10,... | collective-permute-start | bytes 786440 | tf_op jit(solution)/shard_map/cross/ppermute | solution.py:64
  20.3 1.5 %collective-permute-start.2 = (bf16[32,4096]{1,0:T(8,128)(2,1)S(1)}, bf16[32,4096]{1,0:T(8,128)(2,1)S(1)}, u32[]{:S(2)}, u32[]{:S(2)}) collective-permute-start(bf16[32,4096]{1,0:T(8,128)(2,1)S(1)} %collective-permute-done.refs_0_), channel_id=1, source_target_pairs={{0,16},{1,17},{2,18},{3,19},{4,20},{5,21},{6,22},{7,23},{8,24},{9,... | collective-permute-start | bytes 786440 | tf_op jit(solution)/shard_map/far_p/ppermute | solution.py:64
  21.8 2.4 %shard_map.84.refs_2_.refs_8_ = f32[128,1024]{1,0:T(8,128)S(1)} custom-call(f32[8,256]{1,0:T(8,128)S(1)} %get-tuple-element.29.weight_ref, bf16[1024,4096]{1,0:T(8,128)(2,1)S(1)} %get-tuple-element.30.train_ref, bf16[32,4096]{1,0:T(8,128)(2,1)S(1)} %get-tuple-element.35.refs_0_, bf16[32,4096]{1,0:T(8,128)(2,1)S(1)} %collective-permute-done.4.refs_1_, ...), custom_call_target="tpu_custom_call" | custom-call | tf_op jit(solution)/shard_map/pallas_call | solution.py:225
  24.2 0.6 %collective-permute-start.6 = (bf16[32,4096]{1,0:T(8,128)(2,1)S(1)}, bf16[32,4096]{1,0:T(8,128)(2,1)S(1)}, u32[]{:S(2)}, u32[]{:S(2)}) collective-permute-start(bf16[32,4096]{1,0:T(8,128)(2,1)S(1)} %collective-permute-done.3.refs_2_), channel_id=1, source_target_pairs={{0,2},{1,3},{2,0},{3,1},{4,6},{5,7},{6,4},{7,5},{8,10},{9,11},{10,... | collective-permute-start | bytes 786440 | tf_op jit(solution)/shard_map/near_px/ppermute | solution.py:64
  24.9 2.4 %shard_map.85 = (bf16[64,1024]{1,0:T(8,128)(2,1)S(1)}, f32[64,1024]{1,0:T(8,128)S(1)}) custom-call(f32[8,256]{1,0:T(8,128)S(1)} %get-tuple-element.29.weight_ref, bf16[1024,4096]{1,0:T(8,128)(2,1)S(1)} %get-tuple-element.30.train_ref, bf16[32,4096]{1,0:T(8,128)(2,1)S(1)} %collective-permute-done.refs_0_, ...), custom_call_target="tpu_custom_call" | custom-call | tf_op jit(solution)/shard_map/pallas_call | solution.py:225
  27.3 0.5 %collective-permute-start.12 = (bf16[32,4096]{1,0:T(8,128)(2,1)S(1)}, bf16[32,4096]{1,0:T(8,128)(2,1)S(1)}, u32[]{:S(2)}, u32[]{:S(2)}) collective-permute-start(bf16[32,4096]{1,0:T(8,128)(2,1)S(1)} %collective-permute-done.11.refs_6_), channel_id=1, source_target_pairs={{0,2},{1,3},{2,0},{3,1},{4,6},{5,7},{6,4},{7,5},{8,10},{9,11},{10,... | collective-permute-start | bytes 786440 | tf_op jit(solution)/shard_map/cross_x/ppermute | solution.py:64
  27.9 1.5 %collective-permute-start.8 = (bf16[32,4096]{1,0:T(8,128)(2,1)S(1)}, bf16[32,4096]{1,0:T(8,128)(2,1)S(1)}, u32[]{:S(2)}, u32[]{:S(2)}) collective-permute-start(bf16[32,4096]{1,0:T(8,128)(2,1)S(1)} %collective-permute-done.2.refs_4_), channel_id=1, source_target_pairs={{0,4},{1,5},{2,6},{3,7},{4,0},{5,1},{6,2},{7,3},{8,12},{9,13},{10,... | collective-permute-start | bytes 786440 | tf_op jit(solution)/shard_map/cross_p/ppermute | solution.py:64
  29.4 1.5 %collective-permute-start.13 = (bf16[64,1024]{1,0:T(8,128)(2,1)S(1)}, bf16[64,1024]{1,0:T(8,128)(2,1)S(1)}, u32[]{:S(2)}, u32[]{:S(2)}) collective-permute-start(bf16[64,1024]{1,0:T(8,128)(2,1)S(1)} %get-tuple-element.39), channel_id=1, source_target_pairs={{0,1},{1,0},{2,3},{3,2},{4,5},{5,4},{6,7},{7,6},{8,9},{9,8},{10,11... | collective-permute-start | bytes 393224 | tf_op jit(solution)/shard_map/got0/ppermute | solution.py:64
  30.9 2.5 %shard_map.86 = (f32[128,1024]{1,0:T(8,128)S(1)}, bf16[128,1024]{1,0:T(8,128)(2,1)S(1)}, f32[128,1024]{1,0:T(8,128)S(1)}) custom-call(f32[8,256]{1,0:T(8,128)S(1)} %get-tuple-element.29.weight_ref, bf16[1024,4096]{1,0:T(8,128)(2,1)S(1)} %get-tuple-element.30.train_ref, bf16[32,4096]{1,0:T(8,128)(2,1)S(1)} %collective-permute-done.1.refs_0_, ...), custom_call_target="tpu_custom_call" | custom-call | tf_op jit(solution)/shard_map/pallas_call | solution.py:225
  33.4 0.6 %collective-permute-start.17 = (bf16[128,1024]{1,0:T(8,128)(2,1)S(1)}, bf16[128,1024]{1,0:T(8,128)(2,1)S(1)}, u32[]{:S(2)}, u32[]{:S(2)}) collective-permute-start(bf16[128,1024]{1,0:T(8,128)(2,1)S(1)} %get-tuple-element.42), channel_id=1, source_target_pairs={{0,1},{1,0},{2,3},{3,2},{4,5},{5,4},{6,7},{7,6},{8,9},{9,8},{10,11... | collective-permute-start | bytes 786440 | tf_op jit(solution)/shard_map/got1/ppermute | solution.py:64
  34.0 0.9 %collective-permute-done.13.refs_1_ = bf16[64,1024]{1,0:T(8,128)(2,1)S(1)} collective-permute-done((bf16[64,1024]{1,0:T(8,128)(2,1)S(1)}, bf16[64,1024]{1,0:T(8,128)(2,1)S(1)}, u32[]{:S(2)}, u32[]{:S(2)}) %collective-permute-start.13) | collective-permute-done | bytes 131104 | tf_op jit(solution)/shard_map/got0/ppermute | solution.py:64
  34.9 1.6 %collective-permute-done.8.refs_0_ = bf16[32,4096]{1,0:T(8,128)(2,1)S(1)} collective-permute-done((bf16[32,4096]{1,0:T(8,128)(2,1)S(1)}, bf16[32,4096]{1,0:T(8,128)(2,1)S(1)}, u32[]{:S(2)}, u32[]{:S(2)}) %collective-permute-start.8) | collective-permute-done | bytes 262176 | tf_op jit(solution)/shard_map/cross_p/ppermute | solution.py:64
  37.1 0.8 %collective-permute-done.14.refs_1_ = bf16[16,4096]{1,0:T(8,128)(2,1)S(1)} collective-permute-done((bf16[16,4096]{1,0:T(8,128)(2,1)S(1)}, bf16[16,4096]{1,0:T(8,128)(2,1)S(1)}, u32[]{:S(2)}, u32[]{:S(2)}) %collective-permute-start.14) | collective-permute-done | bytes 131104 | tf_op jit(solution)/shard_map/cross_pxa/ppermute | solution.py:64
  38.2 2.4 %shard_map.87 = (bf16[64,1024]{1,0:T(8,128)(2,1)S(1)}, f32[64,1024]{1,0:T(8,128)S(1)}) custom-call(f32[8,256]{1,0:T(8,128)S(1)} %get-tuple-element.29.weight_ref, bf16[1024,4096]{1,0:T(8,128)(2,1)S(1)} %get-tuple-element.30.train_ref, bf16[32,4096]{1,0:T(8,128)(2,1)S(1)} %collective-permute-done.8.refs_0_, ...), custom_call_target="tpu_custom_call" | custom-call | tf_op jit(solution)/shard_map/pallas_call | solution.py:225
  40.6 1.6 %collective-permute-start.16 = (bf16[64,1024]{1,0:T(8,128)(2,1)S(1)}, bf16[64,1024]{1,0:T(8,128)(2,1)S(1)}, u32[]{:S(2)}, u32[]{:S(2)}) collective-permute-start(bf16[64,1024]{1,0:T(8,128)(2,1)S(1)} %get-tuple-element.46), channel_id=1, source_target_pairs={{0,1},{1,0},{2,3},{3,2},{4,5},{5,4},{6,7},{7,6},{8,9},{9,8},{10,11... | collective-permute-start | bytes 393224 | tf_op jit(solution)/shard_map/got2/ppermute | solution.py:64
  42.3 1.0 %shard_map.88.refs_2_ = f32[256,1024]{1,0:T(8,128)} custom-call(s32[1,1024]{1,0:T(1,128)S(1)} %bitcast.6, s32[256,1]{1,0:T(8,128)S(1)} %copy.11.query_ids, f32[64,1024]{1,0:T(8,128)S(1)} %get-tuple-element.47.refs_0_, bf16[64,1024]{1,0:T(8,128)(2,1)S(1)} %collective-permute-done.13.refs_1_, f32[128,1024]{1,0:T(8,128)S(1)} %get-tuple-element.48.refs_2_, ...), custom_call_target="tpu_custom_call" | custom-call | tf_op jit(solution)/shard_map/pallas_call | solution.py:286
  43.4 3.0 %collective-permute-done.16.refs_1_ = bf16[64,1024]{1,0:T(8,128)(2,1)S(1)} collective-permute-done((bf16[64,1024]{1,0:T(8,128)(2,1)S(1)}, bf16[64,1024]{1,0:T(8,128)(2,1)S(1)}, u32[]{:S(2)}, u32[]{:S(2)}) %collective-permute-start.16) | collective-permute-done | bytes 131104 | tf_op jit(solution)/shard_map/got2/ppermute | solution.py:64
  46.4 0.8 %shard_map.89 = f32[256,1024]{1,0:T(8,128)} custom-call(s32[1,1024]{1,0:T(1,128)S(1)} %bitcast.7, s32[256,1]{1,0:T(8,128)S(1)} %copy.11.query_ids, f32[64,1024]{1,0:T(8,128)S(1)} %get-tuple-element.45.refs_0_, bf16[64,1024]{1,0:T(8,128)(2,1)S(1)} %collective-permute-done.16.refs_1_, f32[256,1024]{1,0:T(8,128)} %shard_map.88.refs_2_), custom_call_target="tpu_custom_call", output_to_operand_aliasing={{}: (4, {})} | custom-call | tf_op jit(solution)/shard_map/pallas_call | solution.py:286
  (26 shorter events, 1.7 us)
Async XLA Ops:
  2.4 11.1 %collective-permute-start.1 = (bf16[32,4096]{1,0:T(8,128)(2,1)S(1)}, bf16[32,4096]{1,0:T(8,128)(2,1)S(1)}, u32[]{:S(2)}, u32[]{:S(2)}) collective-permute-start(bf16[32,4096]{1,0:T(8,128)(2,1)S(1)} %get-tuple-element.35.refs_0_), channel_id=1, source_target_pairs={{0,4},{1,5},{2,6},{3,7},{4,0},{5,1},{6,2},{7,3},{8,12},{9,13},{10,... | collective-permute-start | bytes 786440 | tf_op jit(solution)/shard_map/near/ppermute | solution.py:64
  5.5 14.2 %collective-permute-start = (bf16[32,4096]{1,0:T(8,128)(2,1)S(1)}, bf16[32,4096]{1,0:T(8,128)(2,1)S(1)}, u32[]{:S(2)}, u32[]{:S(2)}) collective-permute-start(bf16[32,4096]{1,0:T(8,128)(2,1)S(1)} %get-tuple-element.35.refs_0_), channel_id=1, source_target_pairs={{0,12},{1,13},{2,14},{3,15},{4,8},{5,9},{6,10},{7,11},{8,4},{9,5},... | collective-permute-start | bytes 786440 | tf_op jit(solution)/shard_map/far/ppermute | solution.py:64
  12.9 8.9 %collective-permute-start.4 = (bf16[32,4096]{1,0:T(8,128)(2,1)S(1)}, bf16[32,4096]{1,0:T(8,128)(2,1)S(1)}, u32[]{:S(2)}, u32[]{:S(2)}) collective-permute-start(bf16[32,4096]{1,0:T(8,128)(2,1)S(1)} %get-tuple-element.35.refs_0_), channel_id=1, source_target_pairs={{0,2},{1,3},{2,0},{3,1},{4,6},{5,7},{6,4},{7,5},{8,10},{9,11},{10,... | collective-permute-start | bytes 786440 | tf_op jit(solution)/shard_map/mine_x/ppermute | solution.py:64
  13.0 8.8 %collective-permute-start.5 = (bf16[32,4096]{1,0:T(8,128)(2,1)S(1)}, bf16[32,4096]{1,0:T(8,128)(2,1)S(1)}, u32[]{:S(2)}, u32[]{:S(2)}) collective-permute-start(bf16[32,4096]{1,0:T(8,128)(2,1)S(1)} %get-tuple-element.32.refs_2_), channel_id=1, source_target_pairs={{0,2},{1,3},{2,0},{3,1},{4,6},{5,7},{6,4},{7,5},{8,10},{9,11},{10,... | collective-permute-start | bytes 786440 | tf_op jit(solution)/shard_map/rest_x/ppermute | solution.py:64
  13.5 10.8 %collective-permute-start.3 = (bf16[32,4096]{1,0:T(8,128)(2,1)S(1)}, bf16[32,4096]{1,0:T(8,128)(2,1)S(1)}, u32[]{:S(2)}, u32[]{:S(2)}) collective-permute-start(bf16[32,4096]{1,0:T(8,128)(2,1)S(1)} %collective-permute-done.1.refs_0_), channel_id=1, source_target_pairs={{0,16},{1,17},{2,18},{3,19},{4,20},{5,21},{6,22},{7,23},{8,24},{9,... | collective-permute-start | bytes 786440 | tf_op jit(solution)/shard_map/near_p/ppermute | solution.py:64
  19.7 7.6 %collective-permute-start.11 = (bf16[32,4096]{1,0:T(8,128)(2,1)S(1)}, bf16[32,4096]{1,0:T(8,128)(2,1)S(1)}, u32[]{:S(2)}, u32[]{:S(2)}) collective-permute-start(bf16[32,4096]{1,0:T(8,128)(2,1)S(1)} %collective-permute-done.refs_0_), channel_id=1, source_target_pairs={{0,4},{1,5},{2,6},{3,7},{4,0},{5,1},{6,2},{7,3},{8,12},{9,13},{10,... | collective-permute-start | bytes 786440 | tf_op jit(solution)/shard_map/cross/ppermute | solution.py:64
  20.3 7.5 %collective-permute-start.2 = (bf16[32,4096]{1,0:T(8,128)(2,1)S(1)}, bf16[32,4096]{1,0:T(8,128)(2,1)S(1)}, u32[]{:S(2)}, u32[]{:S(2)}) collective-permute-start(bf16[32,4096]{1,0:T(8,128)(2,1)S(1)} %collective-permute-done.refs_0_), channel_id=1, source_target_pairs={{0,16},{1,17},{2,18},{3,19},{4,20},{5,21},{6,22},{7,23},{8,24},{9,... | collective-permute-start | bytes 786440 | tf_op jit(solution)/shard_map/far_p/ppermute | solution.py:64
  21.8 3.1 %collective-permute-start.7 = (bf16[32,4096]{1,0:T(8,128)(2,1)S(1)}, bf16[32,4096]{1,0:T(8,128)(2,1)S(1)}, u32[]{:S(2)}, u32[]{:S(2)}) collective-permute-start(bf16[32,4096]{1,0:T(8,128)(2,1)S(1)} %collective-permute-done.refs_0_), channel_id=1, source_target_pairs={{0,2},{1,3},{2,0},{3,1},{4,6},{5,7},{6,4},{7,5},{8,10},{9,11},{10,... | collective-permute-start | bytes 786440 | tf_op jit(solution)/shard_map/far_x/ppermute | solution.py:64
  24.2 3.6 %collective-permute-start.6 = (bf16[32,4096]{1,0:T(8,128)(2,1)S(1)}, bf16[32,4096]{1,0:T(8,128)(2,1)S(1)}, u32[]{:S(2)}, u32[]{:S(2)}) collective-permute-start(bf16[32,4096]{1,0:T(8,128)(2,1)S(1)} %collective-permute-done.3.refs_2_), channel_id=1, source_target_pairs={{0,2},{1,3},{2,0},{3,1},{4,6},{5,7},{6,4},{7,5},{8,10},{9,11},{10,... | collective-permute-start | bytes 786440 | tf_op jit(solution)/shard_map/near_px/ppermute | solution.py:64
  24.8 6.1 %collective-permute-start.9 = (bf16[32,4096]{1,0:T(8,128)(2,1)S(1)}, bf16[32,4096]{1,0:T(8,128)(2,1)S(1)}, u32[]{:S(2)}, u32[]{:S(2)}) collective-permute-start(bf16[32,4096]{1,0:T(8,128)(2,1)S(1)} %collective-permute-done.1.refs_0_), channel_id=1, source_target_pairs={{0,2},{1,3},{2,0},{3,1},{4,6},{5,7},{6,4},{7,5},{8,10},{9,11},{10,... | collective-permute-start | bytes 786440 | tf_op jit(solution)/shard_map/near_x/ppermute | solution.py:64
  27.3 14.9 %copy-start.1 = (s32[256]{0:T(256)S(1)}, s32[256]{0:T(256)}, u32[]{:S(2)}) copy-start(s32[256]{0:T(256)} %param.15) | copy-start | bytes 3076
  27.3 15.0 %copy-start = (s32[1024]{0:T(1024)S(1)}, s32[1024]{0:T(1024)}, u32[]{:S(2)}) copy-start(s32[1024]{0:T(1024)} %param.14) | copy-start | bytes 12292
  27.3 3.6 %collective-permute-start.12 = (bf16[32,4096]{1,0:T(8,128)(2,1)S(1)}, bf16[32,4096]{1,0:T(8,128)(2,1)S(1)}, u32[]{:S(2)}, u32[]{:S(2)}) collective-permute-start(bf16[32,4096]{1,0:T(8,128)(2,1)S(1)} %collective-permute-done.11.refs_6_), channel_id=1, source_target_pairs={{0,2},{1,3},{2,0},{3,1},{4,6},{5,7},{6,4},{7,5},{8,10},{9,11},{10,... | collective-permute-start | bytes 786440 | tf_op jit(solution)/shard_map/cross_x/ppermute | solution.py:64
  27.8 3.1 %collective-permute-start.10 = (bf16[32,4096]{1,0:T(8,128)(2,1)S(1)}, bf16[32,4096]{1,0:T(8,128)(2,1)S(1)}, u32[]{:S(2)}, u32[]{:S(2)}) collective-permute-start(bf16[32,4096]{1,0:T(8,128)(2,1)S(1)} %collective-permute-done.2.refs_4_), channel_id=1, source_target_pairs={{0,2},{1,3},{2,0},{3,1},{4,6},{5,7},{6,4},{7,5},{8,10},{9,11},{10,... | collective-permute-start | bytes 786440 | tf_op jit(solution)/shard_map/far_px/ppermute | solution.py:64
  27.9 8.6 %collective-permute-start.8 = (bf16[32,4096]{1,0:T(8,128)(2,1)S(1)}, bf16[32,4096]{1,0:T(8,128)(2,1)S(1)}, u32[]{:S(2)}, u32[]{:S(2)}) collective-permute-start(bf16[32,4096]{1,0:T(8,128)(2,1)S(1)} %collective-permute-done.2.refs_4_), channel_id=1, source_target_pairs={{0,4},{1,5},{2,6},{3,7},{4,0},{5,1},{6,2},{7,3},{8,12},{9,13},{10,... | collective-permute-start | bytes 786440 | tf_op jit(solution)/shard_map/cross_p/ppermute | solution.py:64
  29.4 5.6 %collective-permute-start.13 = (bf16[64,1024]{1,0:T(8,128)(2,1)S(1)}, bf16[64,1024]{1,0:T(8,128)(2,1)S(1)}, u32[]{:S(2)}, u32[]{:S(2)}) collective-permute-start(bf16[64,1024]{1,0:T(8,128)(2,1)S(1)} %get-tuple-element.39), channel_id=1, source_target_pairs={{0,1},{1,0},{2,3},{3,2},{4,5},{5,4},{6,7},{7,6},{8,9},{9,8},{10,11... | collective-permute-start | bytes 393224 | tf_op jit(solution)/shard_map/got0/ppermute | solution.py:64
  33.4 8.9 %collective-permute-start.17 = (bf16[128,1024]{1,0:T(8,128)(2,1)S(1)}, bf16[128,1024]{1,0:T(8,128)(2,1)S(1)}, u32[]{:S(2)}, u32[]{:S(2)}) collective-permute-start(bf16[128,1024]{1,0:T(8,128)(2,1)S(1)} %get-tuple-element.42), channel_id=1, source_target_pairs={{0,1},{1,0},{2,3},{3,2},{4,5},{5,4},{6,7},{7,6},{8,9},{9,8},{10,11... | collective-permute-start | bytes 786440 | tf_op jit(solution)/shard_map/got1/ppermute | solution.py:64
  36.6 1.4 %collective-permute-start.14 = (bf16[16,4096]{1,0:T(8,128)(2,1)S(1)}, bf16[16,4096]{1,0:T(8,128)(2,1)S(1)}, u32[]{:S(2)}, u32[]{:S(2)}) collective-permute-start(bf16[16,4096]{1,0:T(8,128)(2,1)S(1)} %get-tuple-element.50), channel_id=1, source_target_pairs={{0,2},{1,3},{2,0},{3,1},{4,6},{5,7},{6,4},{7,5},{8,10},{9,11},{10,... | collective-permute-start | bytes 393224 | tf_op jit(solution)/shard_map/cross_pxa/ppermute | solution.py:64
  36.6 1.5 %collective-permute-start.15 = (bf16[16,4096]{1,0:T(8,128)(2,1)S(1)}, bf16[16,4096]{1,0:T(8,128)(2,1)S(1)}, u32[]{:S(2)}, u32[]{:S(2)}) collective-permute-start(bf16[16,4096]{1,0:T(8,128)(2,1)S(1)} %get-tuple-element.49), channel_id=1, source_target_pairs={{0,2},{1,3},{2,0},{3,1},{4,6},{5,7},{6,4},{7,5},{8,10},{9,11},{10,... | collective-permute-start | bytes 393224 | tf_op jit(solution)/shard_map/cross_pxb/ppermute | solution.py:64
  40.6 5.8 %collective-permute-start.16 = (bf16[64,1024]{1,0:T(8,128)(2,1)S(1)}, bf16[64,1024]{1,0:T(8,128)(2,1)S(1)}, u32[]{:S(2)}, u32[]{:S(2)}) collective-permute-start(bf16[64,1024]{1,0:T(8,128)(2,1)S(1)} %get-tuple-element.46), channel_id=1, source_target_pairs={{0,1},{1,0},{2,3},{3,2},{4,5},{5,4},{6,7},{7,6},{8,9},{9,8},{10,11... | collective-permute-start | bytes 393224 | tf_op jit(solution)/shard_map/got2/ppermute | solution.py:64

commit v22 on v21

--- a/solution.py
+++ b/solution.py
@@ -367,8 +367,14 @@
     cross_pxa = to_core(cross_p[:CHUNK], "cross_pxa")
     cross_pxb = to_core(cross_p[CHUNK:], "cross_pxb")
     last = rows_of(cross_p, cross_pxa, cross_pxb)
-    send2, keep2 = score(last, early=[(early1, 64, 64)])
+    n = train.shape[0]
+    cut = n // 2
+    send2, keep2 = score(last, early=[(early1, 64, 64)], columns=(0, cut))
     got2 = to_layer(send2, "got2")
+    early1 = after(early1, send2)
+    send3, keep3 = score(last, early=[(early1, 64, 64)], columns=(cut, n))
+    send3 = after(send3, got1)
+    got3 = to_layer(send3, "got3")
 
     train_ids, query_ids = train_ids[None, :], query_ids[:, None]
     most = call_final(
@@ -380,8 +386,8 @@
     return call_final(
         train_ids,
         query_ids,
-        [keep2, got2],
-        ((3, 0, 1, 0, 0),),
+        [keep2, got2, keep3, got3],
+        ((3, 0, 1, 0, 0), (3, 2, 3, 0, cut)),
         most,
     )
 

time: 47.3 us -> 47.7 us (level)
  starting transfers between devices: 16.6 us -> 17.2 us
  waiting for transfers between devices: 11.4 us -> 10.9 us
    ppermute x18 -> x19, starting transfers between devices: 16.6 us -> 17.2 us  [permute(): return lax.ppermute(value, AXES, pairs)]
    ppermute x18 -> x19, waiting for transfers between devices: 11.4 us -> 10.9 us  [permute(): return lax.ppermute(value, AXES, pairs)]
    pallas_call x6 -> x7, Pallas kernels: 16.4 us -> 16.6 us  [kernel_call(): pl.pallas_call(kernel, out_shape=outs, in_specs=specs or [VMEM] * len(inp...]
  transfers between devices with their start and end apart: 18 -> 19, of which waited for: 6 -> 6; matrix products, arithmetic and copies ran while one was open for 0% -> 0% of each run, Pallas kernels for 32% -> 32%
where the time goes in v22:
time: 47.7 us; the launch traced here: 47.5 us
  Pallas kernels  18.5 us (39%)
  starting transfers between devices  17.2 us (36%)
  waiting for transfers between devices  10.9 us (23%)
  between operations  0.81 us (2%)
    ppermute x19, starting transfers between devices, permute(): return lax.ppermute(value, AXES, pairs)  17.2 us
    pallas_call x7, Pallas kernels, kernel_call(): pl.pallas_call(kernel, out_shape=outs, in_specs=specs or [VMEM] * len(inp...  16.6 us
    ppermute x19, waiting for transfers between devices, permute(): return lax.ppermute(value, AXES, pairs)  10.9 us
    pallas_call x2, Pallas kernels, call_final(): pl.pallas_call(functools.partial(final_kernel, groups=groups, n_given=len...  1.85 us
  transfers between devices with their start and end apart: 19, of which 6 were waited for; matrix products, arithmetic and copies ran while one was open for 0% of the time, Pallas kernels for 32%

profile of v22, /device:TPU:0, one launch (start us, length us, event | category | flops | bytes accessed | tf_op | source)
XLA Modules:
  0.0 47.5 jit_solution(12624068822329154321)
XLA Ops:
  0.0 2.4 %shard_map.82 = (bf16[32,4096]{1,0:T(8,128)(2,1)S(1)}, bf16[2,256,256]{2,1,0:T(8,128)(2,1)S(1)}, bf16[2,256,512]{2,1,0:T(8,128)(2,1)S(1)}) custom-call(bf16[64,4096]{1,0:T(8,128)(2,1)} %bitcast.9, f32[64,64]{1,0:T(8,128)} %bitcast.11, f32[64,64]{1,0:T(8,128)} %bitcast.12), custom_call_target="tpu_custom_call" | custom-call | tf_op jit(solution)/shard_map/pallas_call | solution.py:225
  2.4 3.1 %collective-permute-start.1 = (bf16[32,4096]{1,0:T(8,128)(2,1)S(1)}, bf16[32,4096]{1,0:T(8,128)(2,1)S(1)}, u32[]{:S(2)}, u32[]{:S(2)}) collective-permute-start(bf16[32,4096]{1,0:T(8,128)(2,1)S(1)} %get-tuple-element.39.refs_0_), channel_id=1, source_target_pairs={{0,4},{1,5},{2,6},{3,7},{4,0},{5,1},{6,2},{7,3},{8,12},{9,13},{10,... | collective-permute-start | bytes 786440 | tf_op jit(solution)/shard_map/near/ppermute | solution.py:64
  5.5 2.5 %collective-permute-start = (bf16[32,4096]{1,0:T(8,128)(2,1)S(1)}, bf16[32,4096]{1,0:T(8,128)(2,1)S(1)}, u32[]{:S(2)}, u32[]{:S(2)}) collective-permute-start(bf16[32,4096]{1,0:T(8,128)(2,1)S(1)} %get-tuple-element.39.refs_0_), channel_id=1, source_target_pairs={{0,12},{1,13},{2,14},{3,15},{4,8},{5,9},{6,10},{7,11},{8,4},{9,5},... | collective-permute-start | bytes 786440 | tf_op jit(solution)/shard_map/far/ppermute | solution.py:64
  8.6 4.3 %shard_map.83 = (bf16[32,4096]{1,0:T(8,128)(2,1)S(1)}, bf16[1024,4096]{1,0:T(8,128)(2,1)S(1)}, f32[8,256]{1,0:T(8,128)S(1)}) custom-call(f32[2]{0:T(128)} %weight_ref.1, s32[1]{0:T(128)S(6)} %copy.13.layer_ref, bf16[64,4096]{1,0:T(8,128)(2,1)} %bitcast.10, bf16[1024,4096]{1,0:T(8,128)(2,1)} %bitcast.8, bf16[2,256,256]{2,1,0:T(8,128)(2,1)S(1)} %get-tuple-element.31.lefts_ref, ...), custom_call_target="tpu_custom_call" | custom-call | tf_op jit(solution)/shard_map/pallas_call | solution.py:225
  13.5 1.5 %collective-permute-start.3 = (bf16[32,4096]{1,0:T(8,128)(2,1)S(1)}, bf16[32,4096]{1,0:T(8,128)(2,1)S(1)}, u32[]{:S(2)}, u32[]{:S(2)}) collective-permute-start(bf16[32,4096]{1,0:T(8,128)(2,1)S(1)} %collective-permute-done.1.refs_0_), channel_id=1, source_target_pairs={{0,16},{1,17},{2,18},{3,19},{4,20},{5,21},{6,22},{7,23},{8,24},{9,... | collective-permute-start | bytes 786440 | tf_op jit(solution)/shard_map/near_p/ppermute | solution.py:64
  15.0 4.7 %collective-permute-done.refs_0_ = bf16[32,4096]{1,0:T(8,128)(2,1)S(1)} collective-permute-done((bf16[32,4096]{1,0:T(8,128)(2,1)S(1)}, bf16[32,4096]{1,0:T(8,128)(2,1)S(1)}, u32[]{:S(2)}, u32[]{:S(2)}) %collective-permute-start) | collective-permute-done | bytes 262176 | tf_op jit(solution)/shard_map/far/ppermute | solution.py:64
  19.7 0.6 %collective-permute-start.11 = (bf16[32,4096]{1,0:T(8,128)(2,1)S(1)}, bf16[32,4096]{1,0:T(8,128)(2,1)S(1)}, u32[]{:S(2)}, u32[]{:S(2)}) collective-permute-start(bf16[32,4096]{1,0:T(8,128)(2,1)S(1)} %collective-permute-done.refs_0_), channel_id=1, source_target_pairs={{0,4},{1,5},{2,6},{3,7},{4,0},{5,1},{6,2},{7,3},{8,12},{9,13},{10,... | collective-permute-start | bytes 786440 | tf_op jit(solution)/shard_map/cross/ppermute | solution.py:64
  20.3 1.5 %collective-permute-start.2 = (bf16[32,4096]{1,0:T(8,128)(2,1)S(1)}, bf16[32,4096]{1,0:T(8,128)(2,1)S(1)}, u32[]{:S(2)}, u32[]{:S(2)}) collective-permute-start(bf16[32,4096]{1,0:T(8,128)(2,1)S(1)} %collective-permute-done.refs_0_), channel_id=1, source_target_pairs={{0,16},{1,17},{2,18},{3,19},{4,20},{5,21},{6,22},{7,23},{8,24},{9,... | collective-permute-start | bytes 786440 | tf_op jit(solution)/shard_map/far_p/ppermute | solution.py:64
  21.8 2.4 %shard_map.84.refs_2_.refs_8_ = f32[128,1024]{1,0:T(8,128)S(1)} custom-call(f32[8,256]{1,0:T(8,128)S(1)} %get-tuple-element.33.weight_ref, bf16[1024,4096]{1,0:T(8,128)(2,1)S(1)} %get-tuple-element.34.train_ref, bf16[32,4096]{1,0:T(8,128)(2,1)S(1)} %get-tuple-element.39.refs_0_, bf16[32,4096]{1,0:T(8,128)(2,1)S(1)} %collective-permute-done.4.refs_1_, ...), custom_call_target="tpu_custom_call" | custom-call | tf_op jit(solution)/shard_map/pallas_call | solution.py:225
  24.9 2.4 %shard_map.85 = (bf16[64,1024]{1,0:T(8,128)(2,1)S(1)}, f32[64,1024]{1,0:T(8,128)S(1)}) custom-call(f32[8,256]{1,0:T(8,128)S(1)} %get-tuple-element.33.weight_ref, bf16[1024,4096]{1,0:T(8,128)(2,1)S(1)} %get-tuple-element.34.train_ref, bf16[32,4096]{1,0:T(8,128)(2,1)S(1)} %collective-permute-done.refs_0_, ...), custom_call_target="tpu_custom_call" | custom-call | tf_op jit(solution)/shard_map/pallas_call | solution.py:225
  27.9 1.5 %collective-permute-start.8 = (bf16[32,4096]{1,0:T(8,128)(2,1)S(1)}, bf16[32,4096]{1,0:T(8,128)(2,1)S(1)}, u32[]{:S(2)}, u32[]{:S(2)}) collective-permute-start(bf16[32,4096]{1,0:T(8,128)(2,1)S(1)} %collective-permute-done.2.refs_4_), channel_id=1, source_target_pairs={{0,4},{1,5},{2,6},{3,7},{4,0},{5,1},{6,2},{7,3},{8,12},{9,13},{10,... | collective-permute-start | bytes 786440 | tf_op jit(solution)/shard_map/cross_p/ppermute | solution.py:64
  29.3 1.5 %collective-permute-start.13 = (bf16[64,1024]{1,0:T(8,128)(2,1)S(1)}, bf16[64,1024]{1,0:T(8,128)(2,1)S(1)}, u32[]{:S(2)}, u32[]{:S(2)}) collective-permute-start(bf16[64,1024]{1,0:T(8,128)(2,1)S(1)} %get-tuple-element.43), channel_id=1, source_target_pairs={{0,1},{1,0},{2,3},{3,2},{4,5},{5,4},{6,7},{7,6},{8,9},{9,8},{10,11... | collective-permute-start | bytes 393224 | tf_op jit(solution)/shard_map/got0/ppermute | solution.py:64
  30.9 2.5 %shard_map.86 = (f32[128,1024]{1,0:T(8,128)S(1)}, bf16[128,1024]{1,0:T(8,128)(2,1)S(1)}, f32[128,1024]{1,0:T(8,128)S(1)}) custom-call(f32[8,256]{1,0:T(8,128)S(1)} %get-tuple-element.33.weight_ref, bf16[1024,4096]{1,0:T(8,128)(2,1)S(1)} %get-tuple-element.34.train_ref, bf16[32,4096]{1,0:T(8,128)(2,1)S(1)} %collective-permute-done.1.refs_0_, ...), custom_call_target="tpu_custom_call" | custom-call | tf_op jit(solution)/shard_map/pallas_call | solution.py:225
  33.4 0.6 %collective-permute-start.17 = (bf16[128,1024]{1,0:T(8,128)(2,1)S(1)}, bf16[128,1024]{1,0:T(8,128)(2,1)S(1)}, u32[]{:S(2)}, u32[]{:S(2)}) collective-permute-start(bf16[128,1024]{1,0:T(8,128)(2,1)S(1)} %get-tuple-element.46), channel_id=1, source_target_pairs={{0,1},{1,0},{2,3},{3,2},{4,5},{5,4},{6,7},{7,6},{8,9},{9,8},{10,11... | collective-permute-start | bytes 786440 | tf_op jit(solution)/shard_map/got1/ppermute | solution.py:64
  34.0 0.9 %collective-permute-done.13.refs_1_ = bf16[64,1024]{1,0:T(8,128)(2,1)S(1)} collective-permute-done((bf16[64,1024]{1,0:T(8,128)(2,1)S(1)}, bf16[64,1024]{1,0:T(8,128)(2,1)S(1)}, u32[]{:S(2)}, u32[]{:S(2)}) %collective-permute-start.13) | collective-permute-done | bytes 131104 | tf_op jit(solution)/shard_map/got0/ppermute | solution.py:64
  34.9 1.6 %collective-permute-done.8.refs_0_ = bf16[32,4096]{1,0:T(8,128)(2,1)S(1)} collective-permute-done((bf16[32,4096]{1,0:T(8,128)(2,1)S(1)}, bf16[32,4096]{1,0:T(8,128)(2,1)S(1)}, u32[]{:S(2)}, u32[]{:S(2)}) %collective-permute-start.8) | collective-permute-done | bytes 262176 | tf_op jit(solution)/shard_map/cross_p/ppermute | solution.py:64
  37.1 0.8 %collective-permute-done.14.refs_1_ = bf16[16,4096]{1,0:T(8,128)(2,1)S(1)} collective-permute-done((bf16[16,4096]{1,0:T(8,128)(2,1)S(1)}, bf16[16,4096]{1,0:T(8,128)(2,1)S(1)}, u32[]{:S(2)}, u32[]{:S(2)}) %collective-permute-start.14) | collective-permute-done | bytes 131104 | tf_op jit(solution)/shard_map/cross_pxa/ppermute | solution.py:64
  38.2 1.3 %shard_map.87 = (bf16[64,512]{1,0:T(8,128)(2,1)S(1)}, f32[64,512]{1,0:T(8,128)S(1)}) custom-call(f32[8,256]{1,0:T(8,128)S(1)} %get-tuple-element.33.weight_ref, bf16[1024,4096]{1,0:T(8,128)(2,1)S(1)} %get-tuple-element.34.train_ref, bf16[32,4096]{1,0:T(8,128)(2,1)S(1)} %collective-permute-done.8.refs_0_, ...), custom_call_target="tpu_custom_call" | custom-call | tf_op jit(solution)/shard_map/pallas_call | solution.py:225
  39.5 1.6 %collective-permute-start.16 = (bf16[64,512]{1,0:T(8,128)(2,1)S(1)}, bf16[64,512]{1,0:T(8,128)(2,1)S(1)}, u32[]{:S(2)}, u32[]{:S(2)}) collective-permute-start(bf16[64,512]{1,0:T(8,128)(2,1)S(1)} %get-tuple-element.50), channel_id=1, source_target_pairs={{0,1},{1,0},{2,3},{3,2},{4,5},{5,4},{6,7},{7,6},{8,9},{9,8},{10,11... | collective-permute-start | bytes 196616 | tf_op jit(solution)/shard_map/got2/ppermute | solution.py:64
  41.1 1.3 %shard_map.88 = (bf16[64,512]{1,0:T(8,128)(2,1)S(1)}, f32[64,512]{1,0:T(8,128)S(1)}) custom-call(f32[8,256]{1,0:T(8,128)S(1)} %get-tuple-element.33.weight_ref, bf16[1024,4096]{1,0:T(8,128)(2,1)S(1)} %get-tuple-element.34.train_ref, bf16[32,4096]{1,0:T(8,128)(2,1)S(1)} %collective-permute-done.8.refs_0_, ...), custom_call_target="tpu_custom_call" | custom-call | tf_op jit(solution)/shard_map/pallas_call | solution.py:225
  42.4 0.6 %collective-permute-start.18 = (bf16[64,512]{1,0:T(8,128)(2,1)S(1)}, bf16[64,512]{1,0:T(8,128)(2,1)S(1)}, u32[]{:S(2)}, u32[]{:S(2)}) collective-permute-start(bf16[64,512]{1,0:T(8,128)(2,1)S(1)} %get-tuple-element.54), channel_id=1, source_target_pairs={{0,1},{1,0},{2,3},{3,2},{4,5},{5,4},{6,7},{7,6},{8,9},{9,8},{10,11... | collective-permute-start | bytes 196616 | tf_op jit(solution)/shard_map/got3/ppermute | solution.py:64
  43.1 1.0 %shard_map.89.refs_4_ = f32[256,1024]{1,0:T(8,128)} custom-call(s32[1,1024]{1,0:T(1,128)S(1)} %bitcast.6, s32[256,1]{1,0:T(8,128)S(1)} %copy.11.query_ids, f32[64,1024]{1,0:T(8,128)S(1)} %get-tuple-element.55.refs_0_, bf16[64,1024]{1,0:T(8,128)(2,1)S(1)} %collective-permute-done.13.refs_1_, f32[128,1024]{1,0:T(8,128)S(1)} %get-tuple-element.56.refs_2_, ...), custom_call_target="tpu_custom_call" | custom-call | tf_op jit(solution)/shard_map/pallas_call | solution.py:286
  44.2 2.6 %collective-permute-done.18.refs_3_ = bf16[64,512]{1,0:T(8,128)(2,1)S(1)} collective-permute-done((bf16[64,512]{1,0:T(8,128)(2,1)S(1)}, bf16[64,512]{1,0:T(8,128)(2,1)S(1)}, u32[]{:S(2)}, u32[]{:S(2)}) %collective-permute-start.18) | collective-permute-done | bytes 65568 | tf_op jit(solution)/shard_map/got3/ppermute | solution.py:64
  46.7 0.8 %shard_map.90 = f32[256,1024]{1,0:T(8,128)} custom-call(s32[1,1024]{1,0:T(1,128)S(1)} %bitcast.7, s32[256,1]{1,0:T(8,128)S(1)} %copy.11.query_ids, f32[64,512]{1,0:T(8,128)S(1)} %get-tuple-element.49.refs_0_, bf16[64,512]{1,0:T(8,128)(2,1)S(1)} %collective-permute-done.16.refs_1_, ...), custom_call_target="tpu_custom_call", output_to_operand_aliasing={{}: (6, {})} | custom-call | tf_op jit(solution)/shard_map/pallas_call | solution.py:286
  (29 shorter events, 2.8 us)
Async XLA Ops:
  2.4 11.1 %collective-permute-start.1 = (bf16[32,4096]{1,0:T(8,128)(2,1)S(1)}, bf16[32,4096]{1,0:T(8,128)(2,1)S(1)}, u32[]{:S(2)}, u32[]{:S(2)}) collective-permute-start(bf16[32,4096]{1,0:T(8,128)(2,1)S(1)} %get-tuple-element.39.refs_0_), channel_id=1, source_target_pairs={{0,4},{1,5},{2,6},{3,7},{4,0},{5,1},{6,2},{7,3},{8,12},{9,13},{10,... | collective-permute-start | bytes 786440 | tf_op jit(solution)/shard_map/near/ppermute | solution.py:64
  5.5 14.2 %collective-permute-start = (bf16[32,4096]{1,0:T(8,128)(2,1)S(1)}, bf16[32,4096]{1,0:T(8,128)(2,1)S(1)}, u32[]{:S(2)}, u32[]{:S(2)}) collective-permute-start(bf16[32,4096]{1,0:T(8,128)(2,1)S(1)} %get-tuple-element.39.refs_0_), channel_id=1, source_target_pairs={{0,12},{1,13},{2,14},{3,15},{4,8},{5,9},{6,10},{7,11},{8,4},{9,5},... | collective-permute-start | bytes 786440 | tf_op jit(solution)/shard_map/far/ppermute | solution.py:64
  12.9 8.9 %collective-permute-start.4 = (bf16[32,4096]{1,0:T(8,128)(2,1)S(1)}, bf16[32,4096]{1,0:T(8,128)(2,1)S(1)}, u32[]{:S(2)}, u32[]{:S(2)}) collective-permute-start(bf16[32,4096]{1,0:T(8,128)(2,1)S(1)} %get-tuple-element.39.refs_0_), channel_id=1, source_target_pairs={{0,2},{1,3},{2,0},{3,1},{4,6},{5,7},{6,4},{7,5},{8,10},{9,11},{10,... | collective-permute-start | bytes 786440 | tf_op jit(solution)/shard_map/mine_x/ppermute | solution.py:64
  13.0 8.8 %collective-permute-start.5 = (bf16[32,4096]{1,0:T(8,128)(2,1)S(1)}, bf16[32,4096]{1,0:T(8,128)(2,1)S(1)}, u32[]{:S(2)}, u32[]{:S(2)}) collective-permute-start(bf16[32,4096]{1,0:T(8,128)(2,1)S(1)} %get-tuple-element.36.refs_2_), channel_id=1, source_target_pairs={{0,2},{1,3},{2,0},{3,1},{4,6},{5,7},{6,4},{7,5},{8,10},{9,11},{10,... | collective-permute-start | bytes 786440 | tf_op jit(solution)/shard_map/rest_x/ppermute | solution.py:64
  13.5 10.8 %collective-permute-start.3 = (bf16[32,4096]{1,0:T(8,128)(2,1)S(1)}, bf16[32,4096]{1,0:T(8,128)(2,1)S(1)}, u32[]{:S(2)}, u32[]{:S(2)}) collective-permute-start(bf16[32,4096]{1,0:T(8,128)(2,1)S(1)} %collective-permute-done.1.refs_0_), channel_id=1, source_target_pairs={{0,16},{1,17},{2,18},{3,19},{4,20},{5,21},{6,22},{7,23},{8,24},{9,... | collective-permute-start | bytes 786440 | tf_op jit(solution)/shard_map/near_p/ppermute | solution.py:64
  19.7 7.6 %collective-permute-start.11 = (bf16[32,4096]{1,0:T(8,128)(2,1)S(1)}, bf16[32,4096]{1,0:T(8,128)(2,1)S(1)}, u32[]{:S(2)}, u32[]{:S(2)}) collective-permute-start(bf16[32,4096]{1,0:T(8,128)(2,1)S(1)} %collective-permute-done.refs_0_), channel_id=1, source_target_pairs={{0,4},{1,5},{2,6},{3,7},{4,0},{5,1},{6,2},{7,3},{8,12},{9,13},{10,... | collective-permute-start | bytes 786440 | tf_op jit(solution)/shard_map/cross/ppermute | solution.py:64
  20.3 7.5 %collective-permute-start.2 = (bf16[32,4096]{1,0:T(8,128)(2,1)S(1)}, bf16[32,4096]{1,0:T(8,128)(2,1)S(1)}, u32[]{:S(2)}, u32[]{:S(2)}) collective-permute-start(bf16[32,4096]{1,0:T(8,128)(2,1)S(1)} %collective-permute-done.refs_0_), channel_id=1, source_target_pairs={{0,16},{1,17},{2,18},{3,19},{4,20},{5,21},{6,22},{7,23},{8,24},{9,... | collective-permute-start | bytes 786440 | tf_op jit(solution)/shard_map/far_p/ppermute | solution.py:64
  21.8 3.1 %collective-permute-start.7 = (bf16[32,4096]{1,0:T(8,128)(2,1)S(1)}, bf16[32,4096]{1,0:T(8,128)(2,1)S(1)}, u32[]{:S(2)}, u32[]{:S(2)}) collective-permute-start(bf16[32,4096]{1,0:T(8,128)(2,1)S(1)} %collective-permute-done.refs_0_), channel_id=1, source_target_pairs={{0,2},{1,3},{2,0},{3,1},{4,6},{5,7},{6,4},{7,5},{8,10},{9,11},{10,... | collective-permute-start | bytes 786440 | tf_op jit(solution)/shard_map/far_x/ppermute | solution.py:64
  24.2 3.6 %collective-permute-start.6 = (bf16[32,4096]{1,0:T(8,128)(2,1)S(1)}, bf16[32,4096]{1,0:T(8,128)(2,1)S(1)}, u32[]{:S(2)}, u32[]{:S(2)}) collective-permute-start(bf16[32,4096]{1,0:T(8,128)(2,1)S(1)} %collective-permute-done.3.refs_2_), channel_id=1, source_target_pairs={{0,2},{1,3},{2,0},{3,1},{4,6},{5,7},{6,4},{7,5},{8,10},{9,11},{10,... | collective-permute-start | bytes 786440 | tf_op jit(solution)/shard_map/near_px/ppermute | solution.py:64
  24.8 6.1 %collective-permute-start.9 = (bf16[32,4096]{1,0:T(8,128)(2,1)S(1)}, bf16[32,4096]{1,0:T(8,128)(2,1)S(1)}, u32[]{:S(2)}, u32[]{:S(2)}) collective-permute-start(bf16[32,4096]{1,0:T(8,128)(2,1)S(1)} %collective-permute-done.1.refs_0_), channel_id=1, source_target_pairs={{0,2},{1,3},{2,0},{3,1},{4,6},{5,7},{6,4},{7,5},{8,10},{9,11},{10,... | collective-permute-start | bytes 786440 | tf_op jit(solution)/shard_map/near_x/ppermute | solution.py:64
  27.3 3.6 %collective-permute-start.12 = (bf16[32,4096]{1,0:T(8,128)(2,1)S(1)}, bf16[32,4096]{1,0:T(8,128)(2,1)S(1)}, u32[]{:S(2)}, u32[]{:S(2)}) collective-permute-start(bf16[32,4096]{1,0:T(8,128)(2,1)S(1)} %collective-permute-done.11.refs_6_), channel_id=1, source_target_pairs={{0,2},{1,3},{2,0},{3,1},{4,6},{5,7},{6,4},{7,5},{8,10},{9,11},{10,... | collective-permute-start | bytes 786440 | tf_op jit(solution)/shard_map/cross_x/ppermute | solution.py:64
  27.8 3.1 %collective-permute-start.10 = (bf16[32,4096]{1,0:T(8,128)(2,1)S(1)}, bf16[32,4096]{1,0:T(8,128)(2,1)S(1)}, u32[]{:S(2)}, u32[]{:S(2)}) collective-permute-start(bf16[32,4096]{1,0:T(8,128)(2,1)S(1)} %collective-permute-done.2.refs_4_), channel_id=1, source_target_pairs={{0,2},{1,3},{2,0},{3,1},{4,6},{5,7},{6,4},{7,5},{8,10},{9,11},{10,... | collective-permute-start | bytes 786440 | tf_op jit(solution)/shard_map/far_px/ppermute | solution.py:64
  27.9 8.6 %collective-permute-start.8 = (bf16[32,4096]{1,0:T(8,128)(2,1)S(1)}, bf16[32,4096]{1,0:T(8,128)(2,1)S(1)}, u32[]{:S(2)}, u32[]{:S(2)}) collective-permute-start(bf16[32,4096]{1,0:T(8,128)(2,1)S(1)} %collective-permute-done.2.refs_4_), channel_id=1, source_target_pairs={{0,4},{1,5},{2,6},{3,7},{4,0},{5,1},{6,2},{7,3},{8,12},{9,13},{10,... | collective-permute-start | bytes 786440 | tf_op jit(solution)/shard_map/cross_p/ppermute | solution.py:64
  29.3 5.6 %collective-permute-start.13 = (bf16[64,1024]{1,0:T(8,128)(2,1)S(1)}, bf16[64,1024]{1,0:T(8,128)(2,1)S(1)}, u32[]{:S(2)}, u32[]{:S(2)}) collective-permute-start(bf16[64,1024]{1,0:T(8,128)(2,1)S(1)} %get-tuple-element.43), channel_id=1, source_target_pairs={{0,1},{1,0},{2,3},{3,2},{4,5},{5,4},{6,7},{7,6},{8,9},{9,8},{10,11... | collective-permute-start | bytes 393224 | tf_op jit(solution)/shard_map/got0/ppermute | solution.py:64
  33.4 9.0 %collective-permute-start.17 = (bf16[128,1024]{1,0:T(8,128)(2,1)S(1)}, bf16[128,1024]{1,0:T(8,128)(2,1)S(1)}, u32[]{:S(2)}, u32[]{:S(2)}) collective-permute-start(bf16[128,1024]{1,0:T(8,128)(2,1)S(1)} %get-tuple-element.46), channel_id=1, source_target_pairs={{0,1},{1,0},{2,3},{3,2},{4,5},{5,4},{6,7},{7,6},{8,9},{9,8},{10,11... | collective-permute-start | bytes 786440 | tf_op jit(solution)/shard_map/got1/ppermute | solution.py:64
  36.5 1.4 %collective-permute-start.14 = (bf16[16,4096]{1,0:T(8,128)(2,1)S(1)}, bf16[16,4096]{1,0:T(8,128)(2,1)S(1)}, u32[]{:S(2)}, u32[]{:S(2)}) collective-permute-start(bf16[16,4096]{1,0:T(8,128)(2,1)S(1)} %get-tuple-element.58), channel_id=1, source_target_pairs={{0,2},{1,3},{2,0},{3,1},{4,6},{5,7},{6,4},{7,5},{8,10},{9,11},{10,... | collective-permute-start | bytes 393224 | tf_op jit(solution)/shard_map/cross_pxa/ppermute | solution.py:64
  36.6 1.5 %collective-permute-start.15 = (bf16[16,4096]{1,0:T(8,128)(2,1)S(1)}, bf16[16,4096]{1,0:T(8,128)(2,1)S(1)}, u32[]{:S(2)}, u32[]{:S(2)}) collective-permute-start(bf16[16,4096]{1,0:T(8,128)(2,1)S(1)} %get-tuple-element.57), channel_id=1, source_target_pairs={{0,2},{1,3},{2,0},{3,1},{4,6},{5,7},{6,4},{7,5},{8,10},{9,11},{10,... | collective-permute-start | bytes 393224 | tf_op jit(solution)/shard_map/cross_pxb/ppermute | solution.py:64
  38.1 4.8 %copy-start.1 = (s32[256]{0:T(256)S(1)}, s32[256]{0:T(256)}, u32[]{:S(2)}) copy-start(s32[256]{0:T(256)} %param.15) | copy-start | bytes 3076
  38.1 5.0 %copy-start = (s32[1024]{0:T(1024)S(1)}, s32[1024]{0:T(1024)}, u32[]{:S(2)}) copy-start(s32[1024]{0:T(1024)} %param.14) | copy-start | bytes 12292
  39.5 4.7 %collective-permute-start.16 = (bf16[64,512]{1,0:T(8,128)(2,1)S(1)}, bf16[64,512]{1,0:T(8,128)(2,1)S(1)}, u32[]{:S(2)}, u32[]{:S(2)}) collective-permute-start(bf16[64,512]{1,0:T(8,128)(2,1)S(1)} %get-tuple-element.50), channel_id=1, source_target_pairs={{0,1},{1,0},{2,3},{3,2},{4,5},{5,4},{6,7},{7,6},{8,9},{9,8},{10,11... | collective-permute-start | bytes 196616 | tf_op jit(solution)/shard_map/got2/ppermute | solution.py:64
  42.4 4.3 %collective-permute-start.18 = (bf16[64,512]{1,0:T(8,128)(2,1)S(1)}, bf16[64,512]{1,0:T(8,128)(2,1)S(1)}, u32[]{:S(2)}, u32[]{:S(2)}) collective-permute-start(bf16[64,512]{1,0:T(8,128)(2,1)S(1)} %get-tuple-element.54), channel_id=1, source_target_pairs={{0,1},{1,0},{2,3},{3,2},{4,5},{5,4},{6,7},{7,6},{8,9},{9,8},{10,11... | collective-permute-start | bytes 196616 | tf_op jit(solution)/shard_map/got3/ppermute | solution.py:64

commit v23 on v18

--- a/solution.py
+++ b/solution.py
@@ -363,11 +363,10 @@
         stored=128,
         early=[(early0, 64, 64), (None, 0, 64)],
     )
-    got1 = to_layer(send1, "got1")
-    cross_pa, cross_pb = after(cross_pa, send1, got0), after(cross_pb, send1, got0)
-    cross_pxa = to_core(cross_pa, "cross_pxa")
-    cross_pxb = to_core(cross_pb, "cross_pxb")
-    last = rows_of(cross_pa, cross_pb, cross_pxa, cross_pxb)
+    got1 = to_layer(after(send1, got0), "got1")
+    cross_pa, cross_pb = after(cross_pa, send1), after(cross_pb, send1)
+    cross_px = to_core(jnp.concatenate([cross_pa, cross_pb], axis=0), "cross_px")
+    last = rows_of(cross_pa, cross_pb, cross_px)
     send2, keep2 = score(last, early=[(early1, 64, 64)])
     got2 = to_layer(send2, "got2")
 

time: 46.7 us -> 47.7 us (1.021)
  starting transfers between devices: 15 us -> 16.8 us
  waiting for transfers between devices: 12.4 us -> 11.5 us
    ppermute x19 -> x18, starting transfers between devices: 15 us -> 16.8 us  [permute(): return lax.ppermute(value, AXES, pairs)]
    ppermute x19 -> x18, waiting for transfers between devices: 12.4 us -> 11.5 us  [permute(): return lax.ppermute(value, AXES, pairs)]
  transfers between devices with their start and end apart: 19 -> 18, of which waited for: 8 -> 6; matrix products, arithmetic and copies ran while one was open for 0% -> 0% of each run, Pallas kernels for 32% -> 32%
where the time goes in v23:
time: 47.7 us; the launch traced here: 47.5 us
  Pallas kernels  18.2 us (38%)
  starting transfers between devices  16.8 us (35%)
  waiting for transfers between devices  11.5 us (24%)
  between operations  0.8 us (2%)
    ppermute x18, starting transfers between devices, permute(): return lax.ppermute(value, AXES, pairs)  16.8 us
    pallas_call x6, Pallas kernels, kernel_call(): pl.pallas_call(kernel, out_shape=outs, in_specs=specs or [VMEM] * len(inp...  16.4 us
    ppermute x18, waiting for transfers between devices, permute(): return lax.ppermute(value, AXES, pairs)  11.5 us
    pallas_call x2, Pallas kernels, call_final(): pl.pallas_call(functools.partial(final_kernel, groups=groups, n_given=len...  1.84 us
  transfers between devices with their start and end apart: 18, of which 6 were waited for; matrix products, arithmetic and copies ran while one was open for 0% of the time, Pallas kernels for 32%

profile of v23, /device:TPU:0, one launch (start us, length us, event | category | flops | bytes accessed | tf_op | source)
XLA Modules:
  0.0 47.5 jit_solution(11006179894395927439)
XLA Ops:
  0.0 2.4 %shard_map.82 = (bf16[32,4096]{1,0:T(8,128)(2,1)S(1)}, bf16[2,256,256]{2,1,0:T(8,128)(2,1)S(1)}, bf16[2,256,512]{2,1,0:T(8,128)(2,1)S(1)}) custom-call(bf16[64,4096]{1,0:T(8,128)(2,1)} %bitcast.9, f32[64,64]{1,0:T(8,128)} %bitcast.11, f32[64,64]{1,0:T(8,128)} %bitcast.12), custom_call_target="tpu_custom_call" | custom-call | tf_op jit(solution)/shard_map/pallas_call | solution.py:225
  2.4 3.1 %collective-permute-start.1 = (bf16[32,4096]{1,0:T(8,128)(2,1)S(1)}, bf16[32,4096]{1,0:T(8,128)(2,1)S(1)}, u32[]{:S(2)}, u32[]{:S(2)}) collective-permute-start(bf16[32,4096]{1,0:T(8,128)(2,1)S(1)} %get-tuple-element.38.refs_0_), channel_id=1, source_target_pairs={{0,4},{1,5},{2,6},{3,7},{4,0},{5,1},{6,2},{7,3},{8,12},{9,13},{10,... | collective-permute-start | bytes 786440 | tf_op jit(solution)/shard_map/near/ppermute | solution.py:64
  5.5 2.5 %collective-permute-start = (bf16[32,4096]{1,0:T(8,128)(2,1)S(1)}, bf16[32,4096]{1,0:T(8,128)(2,1)S(1)}, u32[]{:S(2)}, u32[]{:S(2)}) collective-permute-start(bf16[32,4096]{1,0:T(8,128)(2,1)S(1)} %get-tuple-element.38.refs_0_), channel_id=1, source_target_pairs={{0,12},{1,13},{2,14},{3,15},{4,8},{5,9},{6,10},{7,11},{8,4},{9,5},... | collective-permute-start | bytes 786440 | tf_op jit(solution)/shard_map/far/ppermute | solution.py:64
  8.6 4.3 %shard_map.83 = (bf16[32,4096]{1,0:T(8,128)(2,1)S(1)}, bf16[1024,4096]{1,0:T(8,128)(2,1)S(1)}, f32[8,256]{1,0:T(8,128)S(1)}) custom-call(f32[2]{0:T(128)} %weight_ref.1, s32[1]{0:T(128)S(6)} %copy.13.layer_ref, bf16[64,4096]{1,0:T(8,128)(2,1)} %bitcast.10, bf16[1024,4096]{1,0:T(8,128)(2,1)} %bitcast.8, bf16[2,256,256]{2,1,0:T(8,128)(2,1)S(1)} %get-tuple-element.29.lefts_ref, ...), custom_call_target="tpu_custom_call" | custom-call | tf_op jit(solution)/shard_map/pallas_call | solution.py:225
  13.5 1.5 %collective-permute-start.8 = (bf16[32,4096]{1,0:T(8,128)(2,1)S(1)}, bf16[32,4096]{1,0:T(8,128)(2,1)S(1)}, u32[]{:S(2)}, u32[]{:S(2)}) collective-permute-start(bf16[32,4096]{1,0:T(8,128)(2,1)S(1)} %collective-permute-done.1.refs_0_), channel_id=1, source_target_pairs={{0,16},{1,17},{2,18},{3,19},{4,20},{5,21},{6,22},{7,23},{8,24},{9,... | collective-permute-start | bytes 786440 | tf_op jit(solution)/shard_map/near_p/ppermute | solution.py:64
  15.0 4.7 %collective-permute-done.refs_0_ = bf16[32,4096]{1,0:T(8,128)(2,1)S(1)} collective-permute-done((bf16[32,4096]{1,0:T(8,128)(2,1)S(1)}, bf16[32,4096]{1,0:T(8,128)(2,1)S(1)}, u32[]{:S(2)}, u32[]{:S(2)}) %collective-permute-start) | collective-permute-done | bytes 262176 | tf_op jit(solution)/shard_map/far/ppermute | solution.py:64
  19.7 1.5 %collective-permute-start.10 = (bf16[32,4096]{1,0:T(8,128)(2,1)S(1)}, bf16[32,4096]{1,0:T(8,128)(2,1)S(1)}, u32[]{:S(2)}, u32[]{:S(2)}) collective-permute-start(bf16[32,4096]{1,0:T(8,128)(2,1)S(1)} %collective-permute-done.refs_0_), channel_id=1, source_target_pairs={{0,16},{1,17},{2,18},{3,19},{4,20},{5,21},{6,22},{7,23},{8,24},{9,... | collective-permute-start | bytes 786440 | tf_op jit(solution)/shard_map/far_p/ppermute | solution.py:64
  21.2 0.6 %collective-permute-start.2 = (bf16[32,4096]{1,0:T(8,128)(2,1)S(1)}, bf16[32,4096]{1,0:T(8,128)(2,1)S(1)}, u32[]{:S(2)}, u32[]{:S(2)}) collective-permute-start(bf16[32,4096]{1,0:T(8,128)(2,1)S(1)} %collective-permute-done.refs_0_), channel_id=1, source_target_pairs={{0,4},{1,5},{2,6},{3,7},{4,0},{5,1},{6,2},{7,3},{8,12},{9,13},{10,... | collective-permute-start | bytes 786440 | tf_op jit(solution)/shard_map/cross/ppermute | solution.py:64
  21.8 2.4 %shard_map.84.refs_2_.refs_8_ = f32[128,1024]{1,0:T(8,128)S(1)} custom-call(f32[8,256]{1,0:T(8,128)S(1)} %get-tuple-element.31.weight_ref, bf16[1024,4096]{1,0:T(8,128)(2,1)S(1)} %get-tuple-element.32.train_ref, bf16[32,4096]{1,0:T(8,128)(2,1)S(1)} %get-tuple-element.38.refs_0_, bf16[32,4096]{1,0:T(8,128)(2,1)S(1)} %collective-permute-done.5.refs_1_, ...), custom_call_target="tpu_custom_call" | custom-call | tf_op jit(solution)/shard_map/pallas_call | solution.py:225
  24.2 0.6 %collective-permute-start.9 = (bf16[32,4096]{1,0:T(8,128)(2,1)S(1)}, bf16[32,4096]{1,0:T(8,128)(2,1)S(1)}, u32[]{:S(2)}, u32[]{:S(2)}) collective-permute-start(bf16[32,4096]{1,0:T(8,128)(2,1)S(1)} %collective-permute-done.8.refs_2_), channel_id=1, source_target_pairs={{0,2},{1,3},{2,0},{3,1},{4,6},{5,7},{6,4},{7,5},{8,10},{9,11},{10,... | collective-permute-start | bytes 786440 | tf_op jit(solution)/shard_map/near_px/ppermute | solution.py:64
  24.9 2.4 %shard_map.85 = (bf16[64,1024]{1,0:T(8,128)(2,1)S(1)}, f32[64,1024]{1,0:T(8,128)S(1)}) custom-call(f32[8,256]{1,0:T(8,128)S(1)} %get-tuple-element.31.weight_ref, bf16[1024,4096]{1,0:T(8,128)(2,1)S(1)} %get-tuple-element.32.train_ref, bf16[32,4096]{1,0:T(8,128)(2,1)S(1)} %collective-permute-done.refs_0_, ...), custom_call_target="tpu_custom_call" | custom-call | tf_op jit(solution)/shard_map/pallas_call | solution.py:225
  27.3 0.8 %collective-permute-done.2.refs_6_ = bf16[32,4096]{1,0:T(8,128)(2,1)S(1)} collective-permute-done((bf16[32,4096]{1,0:T(8,128)(2,1)S(1)}, bf16[32,4096]{1,0:T(8,128)(2,1)S(1)}, u32[]{:S(2)}, u32[]{:S(2)}) %collective-permute-start.2) | collective-permute-done | bytes 262176 | tf_op jit(solution)/shard_map/cross/ppermute | solution.py:64
  28.6 0.9 %collective-permute-start.13 = (bf16[16,4096]{1,0:T(8,128)(2,1)S(1)}, bf16[16,4096]{1,0:T(8,128)(2,1)S(1)}, u32[]{:S(2)}, u32[]{:S(2)}) collective-permute-start(bf16[16,4096]{1,0:T(8,128)(2,1)S(1)} %slice.7), channel_id=1, source_target_pairs={{0,4},{1,5},{2,6},{3,7},{4,0},{5,1},{6,2},{7,3},{8,12},{9,13},{10,... | collective-permute-start | bytes 393224 | tf_op jit(solution)/shard_map/cross_pb/ppermute | solution.py:64
  29.4 0.6 %collective-permute-start.6 = (bf16[16,4096]{1,0:T(8,128)(2,1)S(1)}, bf16[16,4096]{1,0:T(8,128)(2,1)S(1)}, u32[]{:S(2)}, u32[]{:S(2)}) collective-permute-start(bf16[16,4096]{1,0:T(8,128)(2,1)S(1)} %slice.6), channel_id=1, source_target_pairs={{0,16},{1,17},{2,18},{3,19},{4,20},{5,21},{6,22},{7,23},{8,24},{9,... | collective-permute-start | bytes 393224 | tf_op jit(solution)/shard_map/cross_pa/ppermute | solution.py:64
  30.1 1.5 %collective-permute-start.16 = (bf16[64,1024]{1,0:T(8,128)(2,1)S(1)}, bf16[64,1024]{1,0:T(8,128)(2,1)S(1)}, u32[]{:S(2)}, u32[]{:S(2)}) collective-permute-start(bf16[64,1024]{1,0:T(8,128)(2,1)S(1)} %get-tuple-element.40), channel_id=1, source_target_pairs={{0,1},{1,0},{2,3},{3,2},{4,5},{5,4},{6,7},{7,6},{8,9},{9,8},{10,11... | collective-permute-start | bytes 393224 | tf_op jit(solution)/shard_map/got0/ppermute | solution.py:64
  31.6 2.5 %shard_map.86 = (f32[128,1024]{1,0:T(8,128)S(1)}, bf16[128,1024]{1,0:T(8,128)(2,1)S(1)}, f32[128,1024]{1,0:T(8,128)S(1)}) custom-call(f32[8,256]{1,0:T(8,128)S(1)} %get-tuple-element.31.weight_ref, bf16[1024,4096]{1,0:T(8,128)(2,1)S(1)} %get-tuple-element.32.train_ref, bf16[32,4096]{1,0:T(8,128)(2,1)S(1)} %collective-permute-done.1.refs_0_, ...), custom_call_target="tpu_custom_call" | custom-call | tf_op jit(solution)/shard_map/pallas_call | solution.py:225
  34.1 1.0 %collective-permute-done.6.refs_0_ = bf16[16,4096]{1,0:T(8,128)(2,1)S(1)} collective-permute-done((bf16[16,4096]{1,0:T(8,128)(2,1)S(1)}, bf16[16,4096]{1,0:T(8,128)(2,1)S(1)}, u32[]{:S(2)}, u32[]{:S(2)}) %collective-permute-start.6) | collective-permute-done | bytes 131104 | tf_op jit(solution)/shard_map/cross_pa/ppermute | solution.py:64
  35.3 1.5 %collective-permute-start.17 = (bf16[128,1024]{1,0:T(8,128)(2,1)S(1)}, bf16[128,1024]{1,0:T(8,128)(2,1)S(1)}, u32[]{:S(2)}, u32[]{:S(2)}) collective-permute-start(bf16[128,1024]{1,0:T(8,128)(2,1)S(1)} %get-tuple-element.52), channel_id=1, source_target_pairs={{0,1},{1,0},{2,3},{3,2},{4,5},{5,4},{6,7},{7,6},{8,9},{9,8},{10,11... | collective-permute-start | bytes 786440 | tf_op jit(solution)/shard_map/got1/ppermute | solution.py:64
  36.8 2.4 %shard_map.87 = (bf16[64,1024]{1,0:T(8,128)(2,1)S(1)}, f32[64,1024]{1,0:T(8,128)S(1)}) custom-call(f32[8,256]{1,0:T(8,128)S(1)} %get-tuple-element.31.weight_ref, bf16[1024,4096]{1,0:T(8,128)(2,1)S(1)} %get-tuple-element.32.train_ref, bf16[16,4096]{1,0:T(8,128)(2,1)S(1)} %collective-permute-done.6.refs_0_, ...), custom_call_target="tpu_custom_call" | custom-call | tf_op jit(solution)/shard_map/pallas_call | solution.py:225
  39.2 1.4 %collective-permute-start.15 = (bf16[64,1024]{1,0:T(8,128)(2,1)S(1)}, bf16[64,1024]{1,0:T(8,128)(2,1)S(1)}, u32[]{:S(2)}, u32[]{:S(2)}) collective-permute-start(bf16[64,1024]{1,0:T(8,128)(2,1)S(1)} %get-tuple-element.49), channel_id=1, source_target_pairs={{0,1},{1,0},{2,3},{3,2},{4,5},{5,4},{6,7},{7,6},{8,9},{9,8},{10,11... | collective-permute-start | bytes 393224 | tf_op jit(solution)/shard_map/got2/ppermute | solution.py:64
  40.8 3.6 %collective-permute-done.17.refs_3_ = bf16[128,1024]{1,0:T(8,128)(2,1)S(1)} collective-permute-done((bf16[128,1024]{1,0:T(8,128)(2,1)S(1)}, bf16[128,1024]{1,0:T(8,128)(2,1)S(1)}, u32[]{:S(2)}, u32[]{:S(2)}) %collective-permute-start.17) | collective-permute-done | bytes 262176 | tf_op jit(solution)/shard_map/got1/ppermute | solution.py:64
  44.5 1.0 %shard_map.88.refs_2_ = f32[256,1024]{1,0:T(8,128)} custom-call(s32[1,1024]{1,0:T(1,128)S(1)} %bitcast.6, s32[256,1]{1,0:T(8,128)S(1)} %copy.11.query_ids, f32[64,1024]{1,0:T(8,128)S(1)} %get-tuple-element.50.refs_0_, bf16[64,1024]{1,0:T(8,128)(2,1)S(1)} %collective-permute-done.16.refs_1_, f32[128,1024]{1,0:T(8,128)S(1)} %get-tuple-element.51.refs_2_, ...), custom_call_target="tpu_custom_call" | custom-call | tf_op jit(solution)/shard_map/pallas_call | solution.py:286
  45.5 1.2 %collective-permute-done.15.refs_1_ = bf16[64,1024]{1,0:T(8,128)(2,1)S(1)} collective-permute-done((bf16[64,1024]{1,0:T(8,128)(2,1)S(1)}, bf16[64,1024]{1,0:T(8,128)(2,1)S(1)}, u32[]{:S(2)}, u32[]{:S(2)}) %collective-permute-start.15) | collective-permute-done | bytes 131104 | tf_op jit(solution)/shard_map/got2/ppermute | solution.py:64
  46.7 0.8 %shard_map.89 = f32[256,1024]{1,0:T(8,128)} custom-call(s32[1,1024]{1,0:T(1,128)S(1)} %bitcast.7, s32[256,1]{1,0:T(8,128)S(1)} %copy.11.query_ids, f32[64,1024]{1,0:T(8,128)S(1)} %get-tuple-element.48.refs_0_, bf16[64,1024]{1,0:T(8,128)(2,1)S(1)} %collective-permute-done.15.refs_1_, f32[256,1024]{1,0:T(8,128)} %shard_map.88.refs_2_), custom_call_target="tpu_custom_call", output_to_operand_aliasing={{}: (4, {})} | custom-call | tf_op jit(solution)/shard_map/pallas_call | solution.py:286
  (28 shorter events, 1.6 us)
Async XLA Ops:
  2.4 11.1 %collective-permute-start.1 = (bf16[32,4096]{1,0:T(8,128)(2,1)S(1)}, bf16[32,4096]{1,0:T(8,128)(2,1)S(1)}, u32[]{:S(2)}, u32[]{:S(2)}) collective-permute-start(bf16[32,4096]{1,0:T(8,128)(2,1)S(1)} %get-tuple-element.38.refs_0_), channel_id=1, source_target_pairs={{0,4},{1,5},{2,6},{3,7},{4,0},{5,1},{6,2},{7,3},{8,12},{9,13},{10,... | collective-permute-start | bytes 786440 | tf_op jit(solution)/shard_map/near/ppermute | solution.py:64
  5.5 14.2 %collective-permute-start = (bf16[32,4096]{1,0:T(8,128)(2,1)S(1)}, bf16[32,4096]{1,0:T(8,128)(2,1)S(1)}, u32[]{:S(2)}, u32[]{:S(2)}) collective-permute-start(bf16[32,4096]{1,0:T(8,128)(2,1)S(1)} %get-tuple-element.38.refs_0_), channel_id=1, source_target_pairs={{0,12},{1,13},{2,14},{3,15},{4,8},{5,9},{6,10},{7,11},{8,4},{9,5},... | collective-permute-start | bytes 786440 | tf_op jit(solution)/shard_map/far/ppermute | solution.py:64
  12.9 8.9 %collective-permute-start.5 = (bf16[32,4096]{1,0:T(8,128)(2,1)S(1)}, bf16[32,4096]{1,0:T(8,128)(2,1)S(1)}, u32[]{:S(2)}, u32[]{:S(2)}) collective-permute-start(bf16[32,4096]{1,0:T(8,128)(2,1)S(1)} %get-tuple-element.38.refs_0_), channel_id=1, source_target_pairs={{0,2},{1,3},{2,0},{3,1},{4,6},{5,7},{6,4},{7,5},{8,10},{9,11},{10,... | collective-permute-start | bytes 786440 | tf_op jit(solution)/shard_map/mine_x/ppermute | solution.py:64
  13.0 8.8 %collective-permute-start.3 = (bf16[32,4096]{1,0:T(8,128)(2,1)S(1)}, bf16[32,4096]{1,0:T(8,128)(2,1)S(1)}, u32[]{:S(2)}, u32[]{:S(2)}) collective-permute-start(bf16[32,4096]{1,0:T(8,128)(2,1)S(1)} %get-tuple-element.34.refs_2_), channel_id=1, source_target_pairs={{0,2},{1,3},{2,0},{3,1},{4,6},{5,7},{6,4},{7,5},{8,10},{9,11},{10,... | collective-permute-start | bytes 786440 | tf_op jit(solution)/shard_map/rest_x/ppermute | solution.py:64
  13.5 10.8 %collective-permute-start.8 = (bf16[32,4096]{1,0:T(8,128)(2,1)S(1)}, bf16[32,4096]{1,0:T(8,128)(2,1)S(1)}, u32[]{:S(2)}, u32[]{:S(2)}) collective-permute-start(bf16[32,4096]{1,0:T(8,128)(2,1)S(1)} %collective-permute-done.1.refs_0_), channel_id=1, source_target_pairs={{0,16},{1,17},{2,18},{3,19},{4,20},{5,21},{6,22},{7,23},{8,24},{9,... | collective-permute-start | bytes 786440 | tf_op jit(solution)/shard_map/near_p/ppermute | solution.py:64
  19.7 8.3 %collective-permute-start.10 = (bf16[32,4096]{1,0:T(8,128)(2,1)S(1)}, bf16[32,4096]{1,0:T(8,128)(2,1)S(1)}, u32[]{:S(2)}, u32[]{:S(2)}) collective-permute-start(bf16[32,4096]{1,0:T(8,128)(2,1)S(1)} %collective-permute-done.refs_0_), channel_id=1, source_target_pairs={{0,16},{1,17},{2,18},{3,19},{4,20},{5,21},{6,22},{7,23},{8,24},{9,... | collective-permute-start | bytes 786440 | tf_op jit(solution)/shard_map/far_p/ppermute | solution.py:64
  21.2 6.8 %collective-permute-start.2 = (bf16[32,4096]{1,0:T(8,128)(2,1)S(1)}, bf16[32,4096]{1,0:T(8,128)(2,1)S(1)}, u32[]{:S(2)}, u32[]{:S(2)}) collective-permute-start(bf16[32,4096]{1,0:T(8,128)(2,1)S(1)} %collective-permute-done.refs_0_), channel_id=1, source_target_pairs={{0,4},{1,5},{2,6},{3,7},{4,0},{5,1},{6,2},{7,3},{8,12},{9,13},{10,... | collective-permute-start | bytes 786440 | tf_op jit(solution)/shard_map/cross/ppermute | solution.py:64
  21.8 3.1 %collective-permute-start.4 = (bf16[32,4096]{1,0:T(8,128)(2,1)S(1)}, bf16[32,4096]{1,0:T(8,128)(2,1)S(1)}, u32[]{:S(2)}, u32[]{:S(2)}) collective-permute-start(bf16[32,4096]{1,0:T(8,128)(2,1)S(1)} %collective-permute-done.refs_0_), channel_id=1, source_target_pairs={{0,2},{1,3},{2,0},{3,1},{4,6},{5,7},{6,4},{7,5},{8,10},{9,11},{10,... | collective-permute-start | bytes 786440 | tf_op jit(solution)/shard_map/far_x/ppermute | solution.py:64
  24.2 3.8 %collective-permute-start.9 = (bf16[32,4096]{1,0:T(8,128)(2,1)S(1)}, bf16[32,4096]{1,0:T(8,128)(2,1)S(1)}, u32[]{:S(2)}, u32[]{:S(2)}) collective-permute-start(bf16[32,4096]{1,0:T(8,128)(2,1)S(1)} %collective-permute-done.8.refs_2_), channel_id=1, source_target_pairs={{0,2},{1,3},{2,0},{3,1},{4,6},{5,7},{6,4},{7,5},{8,10},{9,11},{10,... | collective-permute-start | bytes 786440 | tf_op jit(solution)/shard_map/near_px/ppermute | solution.py:64
  24.8 5.3 %collective-permute-start.7 = (bf16[32,4096]{1,0:T(8,128)(2,1)S(1)}, bf16[32,4096]{1,0:T(8,128)(2,1)S(1)}, u32[]{:S(2)}, u32[]{:S(2)}) collective-permute-start(bf16[32,4096]{1,0:T(8,128)(2,1)S(1)} %collective-permute-done.1.refs_0_), channel_id=1, source_target_pairs={{0,2},{1,3},{2,0},{3,1},{4,6},{5,7},{6,4},{7,5},{8,10},{9,11},{10,... | collective-permute-start | bytes 786440 | tf_op jit(solution)/shard_map/near_x/ppermute | solution.py:64
  28.0 3.5 %collective-permute-start.12 = (bf16[32,4096]{1,0:T(8,128)(2,1)S(1)}, bf16[32,4096]{1,0:T(8,128)(2,1)S(1)}, u32[]{:S(2)}, u32[]{:S(2)}) collective-permute-start(bf16[32,4096]{1,0:T(8,128)(2,1)S(1)} %collective-permute-done.2.refs_6_), channel_id=1, source_target_pairs={{0,2},{1,3},{2,0},{3,1},{4,6},{5,7},{6,4},{7,5},{8,10},{9,11},{10,... | collective-permute-start | bytes 786440 | tf_op jit(solution)/shard_map/cross_x/ppermute | solution.py:64
  28.0 3.5 %collective-permute-start.11 = (bf16[32,4096]{1,0:T(8,128)(2,1)S(1)}, bf16[32,4096]{1,0:T(8,128)(2,1)S(1)}, u32[]{:S(2)}, u32[]{:S(2)}) collective-permute-start(bf16[32,4096]{1,0:T(8,128)(2,1)S(1)} %collective-permute-done.10.refs_4_), channel_id=1, source_target_pairs={{0,2},{1,3},{2,0},{3,1},{4,6},{5,7},{6,4},{7,5},{8,10},{9,11},{10,... | collective-permute-start | bytes 786440 | tf_op jit(solution)/shard_map/far_px/ppermute | solution.py:64
  28.6 5.5 %collective-permute-start.13 = (bf16[16,4096]{1,0:T(8,128)(2,1)S(1)}, bf16[16,4096]{1,0:T(8,128)(2,1)S(1)}, u32[]{:S(2)}, u32[]{:S(2)}) collective-permute-start(bf16[16,4096]{1,0:T(8,128)(2,1)S(1)} %slice.7), channel_id=1, source_target_pairs={{0,4},{1,5},{2,6},{3,7},{4,0},{5,1},{6,2},{7,3},{8,12},{9,13},{10,... | collective-permute-start | bytes 393224 | tf_op jit(solution)/shard_map/cross_pb/ppermute | solution.py:64
  29.4 11.2 %copy-start.1 = (s32[256]{0:T(256)S(1)}, s32[256]{0:T(256)}, u32[]{:S(2)}) copy-start(s32[256]{0:T(256)} %param.15) | copy-start | bytes 3076
  29.4 15.0 %copy-start = (s32[1024]{0:T(1024)S(1)}, s32[1024]{0:T(1024)}, u32[]{:S(2)}) copy-start(s32[1024]{0:T(1024)} %param.14) | copy-start | bytes 12292
  29.4 5.6 %collective-permute-start.6 = (bf16[16,4096]{1,0:T(8,128)(2,1)S(1)}, bf16[16,4096]{1,0:T(8,128)(2,1)S(1)}, u32[]{:S(2)}, u32[]{:S(2)}) collective-permute-start(bf16[16,4096]{1,0:T(8,128)(2,1)S(1)} %slice.6), channel_id=1, source_target_pairs={{0,16},{1,17},{2,18},{3,19},{4,20},{5,21},{6,22},{7,23},{8,24},{9,... | collective-permute-start | bytes 393224 | tf_op jit(solution)/shard_map/cross_pa/ppermute | solution.py:64
  30.1 5.3 %collective-permute-start.16 = (bf16[64,1024]{1,0:T(8,128)(2,1)S(1)}, bf16[64,1024]{1,0:T(8,128)(2,1)S(1)}, u32[]{:S(2)}, u32[]{:S(2)}) collective-permute-start(bf16[64,1024]{1,0:T(8,128)(2,1)S(1)} %get-tuple-element.40), channel_id=1, source_target_pairs={{0,1},{1,0},{2,3},{3,2},{4,5},{5,4},{6,7},{7,6},{8,9},{9,8},{10,11... | collective-permute-start | bytes 393224 | tf_op jit(solution)/shard_map/got0/ppermute | solution.py:64
  35.1 1.8 %collective-permute-start.14 = (bf16[32,4096]{1,0:T(8,128)(2,1)S(1)}, bf16[32,4096]{1,0:T(8,128)(2,1)S(1)}, u32[]{:S(2)}, u32[]{:S(2)}) collective-permute-start(bf16[32,4096]{1,0:T(8,128)(2,1)S(1)} %pad_maximum_fusion), channel_id=1, source_target_pairs={{0,2},{1,3},{2,0},{3,1},{4,6},{5,7},{6,4},{7,5},{8,10},{9,11},{10,... | collective-permute-start | bytes 786440 | tf_op jit(solution)/shard_map/cross_px/ppermute | solution.py:64
  35.3 9.1 %collective-permute-start.17 = (bf16[128,1024]{1,0:T(8,128)(2,1)S(1)}, bf16[128,1024]{1,0:T(8,128)(2,1)S(1)}, u32[]{:S(2)}, u32[]{:S(2)}) collective-permute-start(bf16[128,1024]{1,0:T(8,128)(2,1)S(1)} %get-tuple-element.52), channel_id=1, source_target_pairs={{0,1},{1,0},{2,3},{3,2},{4,5},{5,4},{6,7},{7,6},{8,9},{9,8},{10,11... | collective-permute-start | bytes 786440 | tf_op jit(solution)/shard_map/got1/ppermute | solution.py:64
  39.2 7.5 %collective-permute-start.15 = (bf16[64,1024]{1,0:T(8,128)(2,1)S(1)}, bf16[64,1024]{1,0:T(8,128)(2,1)S(1)}, u32[]{:S(2)}, u32[]{:S(2)}) collective-permute-start(bf16[64,1024]{1,0:T(8,128)(2,1)S(1)} %get-tuple-element.49), channel_id=1, source_target_pairs={{0,1},{1,0},{2,3},{3,2},{4,5},{5,4},{6,7},{7,6},{8,9},{9,8},{10,11... | collective-permute-start | bytes 393224 | tf_op jit(solution)/shard_map/got2/ppermute | solution.py:64

commit v24 on v18

--- a/solution.py
+++ b/solution.py
@@ -355,7 +355,7 @@
     near_px = to_core(near_p, "near_px")
     far_p, cross = after(far_p, near_px, send0), after(cross, send0)
     far_px = to_core(far_p, "far_px")
-    cross_pa = to_part(cross[:CHUNK], "cross_pa")
+    cross_pa = to_near(far_p[:CHUNK], "cross_pa")
     cross_pb = to_near(far_p[CHUNK:], "cross_pb")
     cross_x = to_core(cross, "cross_x")
     early1, send1, keep1 = score(

time: 46.7 us -> 48.2 us (1.032)
  waiting for transfers between devices: 12.4 us -> 13.2 us
  starting transfers between devices: 15 us -> 15.7 us
    ppermute x19, waiting for transfers between devices: 12.4 us -> 13.2 us  [permute(): return lax.ppermute(value, AXES, pairs)]
    ppermute x19, starting transfers between devices: 15 us -> 15.7 us  [permute(): return lax.ppermute(value, AXES, pairs)]
  transfers between devices with their start and end apart: 19 -> 19, of which waited for: 8 -> 5; matrix products, arithmetic and copies ran while one was open for 0% -> 0% of each run, Pallas kernels for 32% -> 31%
where the time goes in v24:
time: 48.2 us; the launch traced here: 48 us
  Pallas kernels  18.2 us (38%)
  starting transfers between devices  15.7 us (33%)
  waiting for transfers between devices  13.2 us (27%)
  between operations  0.77 us (2%)
    pallas_call x6, Pallas kernels, kernel_call(): pl.pallas_call(kernel, out_shape=outs, in_specs=specs or [VMEM] * len(inp...  16.4 us
    ppermute x19, starting transfers between devices, permute(): return lax.ppermute(value, AXES, pairs)  15.7 us
    ppermute x19, waiting for transfers between devices, permute(): return lax.ppermute(value, AXES, pairs)  13.2 us
    pallas_call x2, Pallas kernels, call_final(): pl.pallas_call(functools.partial(final_kernel, groups=groups, n_given=len...  1.85 us
  transfers between devices with their start and end apart: 19, of which 5 were waited for; matrix products, arithmetic and copies ran while one was open for 0% of the time, Pallas kernels for 31%

profile of v24, /device:TPU:0, one launch (start us, length us, event | category | flops | bytes accessed | tf_op | source)
XLA Modules:
  0.0 48.0 jit_solution(11245322191628367812)
XLA Ops:
  0.0 2.4 %shard_map.82 = (bf16[32,4096]{1,0:T(8,128)(2,1)S(1)}, bf16[2,256,256]{2,1,0:T(8,128)(2,1)S(1)}, bf16[2,256,512]{2,1,0:T(8,128)(2,1)S(1)}) custom-call(bf16[64,4096]{1,0:T(8,128)(2,1)} %bitcast.9, f32[64,64]{1,0:T(8,128)} %bitcast.11, f32[64,64]{1,0:T(8,128)} %bitcast.12), custom_call_target="tpu_custom_call" | custom-call | tf_op jit(solution)/shard_map/pallas_call | solution.py:225
  2.4 3.1 %collective-permute-start.1 = (bf16[32,4096]{1,0:T(8,128)(2,1)S(1)}, bf16[32,4096]{1,0:T(8,128)(2,1)S(1)}, u32[]{:S(2)}, u32[]{:S(2)}) collective-permute-start(bf16[32,4096]{1,0:T(8,128)(2,1)S(1)} %get-tuple-element.36.refs_0_), channel_id=1, source_target_pairs={{0,4},{1,5},{2,6},{3,7},{4,0},{5,1},{6,2},{7,3},{8,12},{9,13},{10,... | collective-permute-start | bytes 786440 | tf_op jit(solution)/shard_map/near/ppermute | solution.py:64
  5.5 2.5 %collective-permute-start = (bf16[32,4096]{1,0:T(8,128)(2,1)S(1)}, bf16[32,4096]{1,0:T(8,128)(2,1)S(1)}, u32[]{:S(2)}, u32[]{:S(2)}) collective-permute-start(bf16[32,4096]{1,0:T(8,128)(2,1)S(1)} %get-tuple-element.36.refs_0_), channel_id=1, source_target_pairs={{0,12},{1,13},{2,14},{3,15},{4,8},{5,9},{6,10},{7,11},{8,4},{9,5},... | collective-permute-start | bytes 786440 | tf_op jit(solution)/shard_map/far/ppermute | solution.py:64
  8.6 4.3 %shard_map.83 = (bf16[32,4096]{1,0:T(8,128)(2,1)S(1)}, bf16[1024,4096]{1,0:T(8,128)(2,1)S(1)}, f32[8,256]{1,0:T(8,128)S(1)}) custom-call(f32[2]{0:T(128)} %weight_ref.1, s32[1]{0:T(128)S(6)} %copy.13.layer_ref, bf16[64,4096]{1,0:T(8,128)(2,1)} %bitcast.10, bf16[1024,4096]{1,0:T(8,128)(2,1)} %bitcast.8, bf16[2,256,256]{2,1,0:T(8,128)(2,1)S(1)} %get-tuple-element.28.lefts_ref, ...), custom_call_target="tpu_custom_call" | custom-call | tf_op jit(solution)/shard_map/pallas_call | solution.py:225
  13.5 1.5 %collective-permute-start.3 = (bf16[32,4096]{1,0:T(8,128)(2,1)S(1)}, bf16[32,4096]{1,0:T(8,128)(2,1)S(1)}, u32[]{:S(2)}, u32[]{:S(2)}) collective-permute-start(bf16[32,4096]{1,0:T(8,128)(2,1)S(1)} %collective-permute-done.1.refs_0_), channel_id=1, source_target_pairs={{0,16},{1,17},{2,18},{3,19},{4,20},{5,21},{6,22},{7,23},{8,24},{9,... | collective-permute-start | bytes 786440 | tf_op jit(solution)/shard_map/near_p/ppermute | solution.py:64
  15.0 4.7 %collective-permute-done.refs_0_ = bf16[32,4096]{1,0:T(8,128)(2,1)S(1)} collective-permute-done((bf16[32,4096]{1,0:T(8,128)(2,1)S(1)}, bf16[32,4096]{1,0:T(8,128)(2,1)S(1)}, u32[]{:S(2)}, u32[]{:S(2)}) %collective-permute-start) | collective-permute-done | bytes 262176 | tf_op jit(solution)/shard_map/far/ppermute | solution.py:64
  19.7 0.6 %collective-permute-start.11 = (bf16[32,4096]{1,0:T(8,128)(2,1)S(1)}, bf16[32,4096]{1,0:T(8,128)(2,1)S(1)}, u32[]{:S(2)}, u32[]{:S(2)}) collective-permute-start(bf16[32,4096]{1,0:T(8,128)(2,1)S(1)} %collective-permute-done.refs_0_), channel_id=1, source_target_pairs={{0,4},{1,5},{2,6},{3,7},{4,0},{5,1},{6,2},{7,3},{8,12},{9,13},{10,... | collective-permute-start | bytes 786440 | tf_op jit(solution)/shard_map/cross/ppermute | solution.py:64
  20.3 1.5 %collective-permute-start.2 = (bf16[32,4096]{1,0:T(8,128)(2,1)S(1)}, bf16[32,4096]{1,0:T(8,128)(2,1)S(1)}, u32[]{:S(2)}, u32[]{:S(2)}) collective-permute-start(bf16[32,4096]{1,0:T(8,128)(2,1)S(1)} %collective-permute-done.refs_0_), channel_id=1, source_target_pairs={{0,16},{1,17},{2,18},{3,19},{4,20},{5,21},{6,22},{7,23},{8,24},{9,... | collective-permute-start | bytes 786440 | tf_op jit(solution)/shard_map/far_p/ppermute | solution.py:64
  21.8 2.4 %shard_map.84.refs_2_.refs_8_ = f32[128,1024]{1,0:T(8,128)S(1)} custom-call(f32[8,256]{1,0:T(8,128)S(1)} %get-tuple-element.30.weight_ref, bf16[1024,4096]{1,0:T(8,128)(2,1)S(1)} %get-tuple-element.31.train_ref, bf16[32,4096]{1,0:T(8,128)(2,1)S(1)} %get-tuple-element.36.refs_0_, bf16[32,4096]{1,0:T(8,128)(2,1)S(1)} %collective-permute-done.4.refs_1_, ...), custom_call_target="tpu_custom_call" | custom-call | tf_op jit(solution)/shard_map/pallas_call | solution.py:225
  24.2 0.6 %collective-permute-start.6 = (bf16[32,4096]{1,0:T(8,128)(2,1)S(1)}, bf16[32,4096]{1,0:T(8,128)(2,1)S(1)}, u32[]{:S(2)}, u32[]{:S(2)}) collective-permute-start(bf16[32,4096]{1,0:T(8,128)(2,1)S(1)} %collective-permute-done.3.refs_2_), channel_id=1, source_target_pairs={{0,2},{1,3},{2,0},{3,1},{4,6},{5,7},{6,4},{7,5},{8,10},{9,11},{10,... | collective-permute-start | bytes 786440 | tf_op jit(solution)/shard_map/near_px/ppermute | solution.py:64
  24.9 2.4 %shard_map.85 = (bf16[64,1024]{1,0:T(8,128)(2,1)S(1)}, f32[64,1024]{1,0:T(8,128)S(1)}) custom-call(f32[8,256]{1,0:T(8,128)S(1)} %get-tuple-element.30.weight_ref, bf16[1024,4096]{1,0:T(8,128)(2,1)S(1)} %get-tuple-element.31.train_ref, bf16[32,4096]{1,0:T(8,128)(2,1)S(1)} %collective-permute-done.refs_0_, ...), custom_call_target="tpu_custom_call" | custom-call | tf_op jit(solution)/shard_map/pallas_call | solution.py:225
  27.3 1.6 %collective-permute-start.13 = (bf16[64,1024]{1,0:T(8,128)(2,1)S(1)}, bf16[64,1024]{1,0:T(8,128)(2,1)S(1)}, u32[]{:S(2)}, u32[]{:S(2)}) collective-permute-start(bf16[64,1024]{1,0:T(8,128)(2,1)S(1)} %get-tuple-element.40), channel_id=1, source_target_pairs={{0,1},{1,0},{2,3},{3,2},{4,5},{5,4},{6,7},{7,6},{8,9},{9,8},{10,11... | collective-permute-start | bytes 393224 | tf_op jit(solution)/shard_map/got0/ppermute | solution.py:64
  29.4 1.5 %collective-permute-start.14 = (bf16[16,4096]{1,0:T(8,128)(2,1)S(1)}, bf16[16,4096]{1,0:T(8,128)(2,1)S(1)}, u32[]{:S(2)}, u32[]{:S(2)}) collective-permute-start(bf16[16,4096]{1,0:T(8,128)(2,1)S(1)} %get-tuple-element.51), channel_id=1, source_target_pairs={{0,4},{1,5},{2,6},{3,7},{4,0},{5,1},{6,2},{7,3},{8,12},{9,13},{10,... | collective-permute-start | bytes 393224 | tf_op jit(solution)/shard_map/cross_pb/ppermute | solution.py:64
  30.9 0.6 %collective-permute-start.8 = (bf16[16,4096]{1,0:T(8,128)(2,1)S(1)}, bf16[16,4096]{1,0:T(8,128)(2,1)S(1)}, u32[]{:S(2)}, u32[]{:S(2)}) collective-permute-start(bf16[16,4096]{1,0:T(8,128)(2,1)S(1)} %get-tuple-element.52), channel_id=1, source_target_pairs={{0,4},{1,5},{2,6},{3,7},{4,0},{5,1},{6,2},{7,3},{8,12},{9,13},{10,... | collective-permute-start | bytes 393224 | tf_op jit(solution)/shard_map/cross_pa/ppermute | solution.py:64
  31.5 2.5 %shard_map.86 = (f32[128,1024]{1,0:T(8,128)S(1)}, bf16[128,1024]{1,0:T(8,128)(2,1)S(1)}, f32[128,1024]{1,0:T(8,128)S(1)}) custom-call(f32[8,256]{1,0:T(8,128)S(1)} %get-tuple-element.30.weight_ref, bf16[1024,4096]{1,0:T(8,128)(2,1)S(1)} %get-tuple-element.31.train_ref, bf16[32,4096]{1,0:T(8,128)(2,1)S(1)} %collective-permute-done.1.refs_0_, ...), custom_call_target="tpu_custom_call" | custom-call | tf_op jit(solution)/shard_map/pallas_call | solution.py:225
  34.0 0.6 %collective-permute-start.18 = (bf16[128,1024]{1,0:T(8,128)(2,1)S(1)}, bf16[128,1024]{1,0:T(8,128)(2,1)S(1)}, u32[]{:S(2)}, u32[]{:S(2)}) collective-permute-start(bf16[128,1024]{1,0:T(8,128)(2,1)S(1)} %get-tuple-element.43), channel_id=1, source_target_pairs={{0,1},{1,0},{2,3},{3,2},{4,5},{5,4},{6,7},{7,6},{8,9},{9,8},{10,11... | collective-permute-start | bytes 786440 | tf_op jit(solution)/shard_map/got1/ppermute | solution.py:64
  34.6 1.2 %collective-permute-done.14.refs_1_ = bf16[16,4096]{1,0:T(8,128)(2,1)S(1)} collective-permute-done((bf16[16,4096]{1,0:T(8,128)(2,1)S(1)}, bf16[16,4096]{1,0:T(8,128)(2,1)S(1)}, u32[]{:S(2)}, u32[]{:S(2)}) %collective-permute-start.14) | collective-permute-done | bytes 131104 | tf_op jit(solution)/shard_map/cross_pb/ppermute | solution.py:64
  35.8 2.0 %collective-permute-done.8.refs_0_ = bf16[16,4096]{1,0:T(8,128)(2,1)S(1)} collective-permute-done((bf16[16,4096]{1,0:T(8,128)(2,1)S(1)}, bf16[16,4096]{1,0:T(8,128)(2,1)S(1)}, u32[]{:S(2)}, u32[]{:S(2)}) %collective-permute-start.8) | collective-permute-done | bytes 131104 | tf_op jit(solution)/shard_map/cross_pa/ppermute | solution.py:64
  37.8 1.3 %collective-permute-done.15.refs_2_ = bf16[16,4096]{1,0:T(8,128)(2,1)S(1)} collective-permute-done((bf16[16,4096]{1,0:T(8,128)(2,1)S(1)}, bf16[16,4096]{1,0:T(8,128)(2,1)S(1)}, u32[]{:S(2)}, u32[]{:S(2)}) %collective-permute-start.15) | collective-permute-done | bytes 131104 | tf_op jit(solution)/shard_map/cross_pxa/ppermute | solution.py:64
  39.2 2.4 %shard_map.87 = (bf16[64,1024]{1,0:T(8,128)(2,1)S(1)}, f32[64,1024]{1,0:T(8,128)S(1)}) custom-call(f32[8,256]{1,0:T(8,128)S(1)} %get-tuple-element.30.weight_ref, bf16[1024,4096]{1,0:T(8,128)(2,1)S(1)} %get-tuple-element.31.train_ref, bf16[16,4096]{1,0:T(8,128)(2,1)S(1)} %collective-permute-done.8.refs_0_, ...), custom_call_target="tpu_custom_call" | custom-call | tf_op jit(solution)/shard_map/pallas_call | solution.py:225
  41.6 0.6 %collective-permute-start.17 = (bf16[64,1024]{1,0:T(8,128)(2,1)S(1)}, bf16[64,1024]{1,0:T(8,128)(2,1)S(1)}, u32[]{:S(2)}, u32[]{:S(2)}) collective-permute-start(bf16[64,1024]{1,0:T(8,128)(2,1)S(1)} %get-tuple-element.48), channel_id=1, source_target_pairs={{0,1},{1,0},{2,3},{3,2},{4,5},{5,4},{6,7},{7,6},{8,9},{9,8},{10,11... | collective-permute-start | bytes 393224 | tf_op jit(solution)/shard_map/got2/ppermute | solution.py:64
  42.3 1.0 %shard_map.88.refs_2_ = f32[256,1024]{1,0:T(8,128)} custom-call(s32[1,1024]{1,0:T(1,128)S(1)} %bitcast.6, s32[256,1]{1,0:T(8,128)S(1)} %copy.11.query_ids, f32[64,1024]{1,0:T(8,128)S(1)} %get-tuple-element.49.refs_0_, bf16[64,1024]{1,0:T(8,128)(2,1)S(1)} %collective-permute-done.13.refs_1_, f32[128,1024]{1,0:T(8,128)S(1)} %get-tuple-element.50.refs_2_, ...), custom_call_target="tpu_custom_call" | custom-call | tf_op jit(solution)/shard_map/pallas_call | solution.py:286
  43.4 3.8 %collective-permute-done.17.refs_1_ = bf16[64,1024]{1,0:T(8,128)(2,1)S(1)} collective-permute-done((bf16[64,1024]{1,0:T(8,128)(2,1)S(1)}, bf16[64,1024]{1,0:T(8,128)(2,1)S(1)}, u32[]{:S(2)}, u32[]{:S(2)}) %collective-permute-start.17) | collective-permute-done | bytes 131104 | tf_op jit(solution)/shard_map/got2/ppermute | solution.py:64
  47.2 0.8 %shard_map.89 = f32[256,1024]{1,0:T(8,128)} custom-call(s32[1,1024]{1,0:T(1,128)S(1)} %bitcast.7, s32[256,1]{1,0:T(8,128)S(1)} %copy.11.query_ids, f32[64,1024]{1,0:T(8,128)S(1)} %get-tuple-element.47.refs_0_, bf16[64,1024]{1,0:T(8,128)(2,1)S(1)} %collective-permute-done.17.refs_1_, f32[256,1024]{1,0:T(8,128)} %shard_map.88.refs_2_), custom_call_target="tpu_custom_call", output_to_operand_aliasing={{}: (4, {})} | custom-call | tf_op jit(solution)/shard_map/pallas_call | solution.py:286
  (28 shorter events, 1.4 us)
Async XLA Ops:
  2.4 11.1 %collective-permute-start.1 = (bf16[32,4096]{1,0:T(8,128)(2,1)S(1)}, bf16[32,4096]{1,0:T(8,128)(2,1)S(1)}, u32[]{:S(2)}, u32[]{:S(2)}) collective-permute-start(bf16[32,4096]{1,0:T(8,128)(2,1)S(1)} %get-tuple-element.36.refs_0_), channel_id=1, source_target_pairs={{0,4},{1,5},{2,6},{3,7},{4,0},{5,1},{6,2},{7,3},{8,12},{9,13},{10,... | collective-permute-start | bytes 786440 | tf_op jit(solution)/shard_map/near/ppermute | solution.py:64
  5.5 14.2 %collective-permute-start = (bf16[32,4096]{1,0:T(8,128)(2,1)S(1)}, bf16[32,4096]{1,0:T(8,128)(2,1)S(1)}, u32[]{:S(2)}, u32[]{:S(2)}) collective-permute-start(bf16[32,4096]{1,0:T(8,128)(2,1)S(1)} %get-tuple-element.36.refs_0_), channel_id=1, source_target_pairs={{0,12},{1,13},{2,14},{3,15},{4,8},{5,9},{6,10},{7,11},{8,4},{9,5},... | collective-permute-start | bytes 786440 | tf_op jit(solution)/shard_map/far/ppermute | solution.py:64
  12.9 8.9 %collective-permute-start.5 = (bf16[32,4096]{1,0:T(8,128)(2,1)S(1)}, bf16[32,4096]{1,0:T(8,128)(2,1)S(1)}, u32[]{:S(2)}, u32[]{:S(2)}) collective-permute-start(bf16[32,4096]{1,0:T(8,128)(2,1)S(1)} %get-tuple-element.33.refs_2_), channel_id=1, source_target_pairs={{0,2},{1,3},{2,0},{3,1},{4,6},{5,7},{6,4},{7,5},{8,10},{9,11},{10,... | collective-permute-start | bytes 786440 | tf_op jit(solution)/shard_map/rest_x/ppermute | solution.py:64
  13.0 8.8 %collective-permute-start.4 = (bf16[32,4096]{1,0:T(8,128)(2,1)S(1)}, bf16[32,4096]{1,0:T(8,128)(2,1)S(1)}, u32[]{:S(2)}, u32[]{:S(2)}) collective-permute-start(bf16[32,4096]{1,0:T(8,128)(2,1)S(1)} %get-tuple-element.36.refs_0_), channel_id=1, source_target_pairs={{0,2},{1,3},{2,0},{3,1},{4,6},{5,7},{6,4},{7,5},{8,10},{9,11},{10,... | collective-permute-start | bytes 786440 | tf_op jit(solution)/shard_map/mine_x/ppermute | solution.py:64
  13.5 10.7 %collective-permute-start.3 = (bf16[32,4096]{1,0:T(8,128)(2,1)S(1)}, bf16[32,4096]{1,0:T(8,128)(2,1)S(1)}, u32[]{:S(2)}, u32[]{:S(2)}) collective-permute-start(bf16[32,4096]{1,0:T(8,128)(2,1)S(1)} %collective-permute-done.1.refs_0_), channel_id=1, source_target_pairs={{0,16},{1,17},{2,18},{3,19},{4,20},{5,21},{6,22},{7,23},{8,24},{9,... | collective-permute-start | bytes 786440 | tf_op jit(solution)/shard_map/near_p/ppermute | solution.py:64
  19.7 9.2 %collective-permute-start.11 = (bf16[32,4096]{1,0:T(8,128)(2,1)S(1)}, bf16[32,4096]{1,0:T(8,128)(2,1)S(1)}, u32[]{:S(2)}, u32[]{:S(2)}) collective-permute-start(bf16[32,4096]{1,0:T(8,128)(2,1)S(1)} %collective-permute-done.refs_0_), channel_id=1, source_target_pairs={{0,4},{1,5},{2,6},{3,7},{4,0},{5,1},{6,2},{7,3},{8,12},{9,13},{10,... | collective-permute-start | bytes 786440 | tf_op jit(solution)/shard_map/cross/ppermute | solution.py:64
  20.3 8.7 %collective-permute-start.2 = (bf16[32,4096]{1,0:T(8,128)(2,1)S(1)}, bf16[32,4096]{1,0:T(8,128)(2,1)S(1)}, u32[]{:S(2)}, u32[]{:S(2)}) collective-permute-start(bf16[32,4096]{1,0:T(8,128)(2,1)S(1)} %collective-permute-done.refs_0_), channel_id=1, source_target_pairs={{0,16},{1,17},{2,18},{3,19},{4,20},{5,21},{6,22},{7,23},{8,24},{9,... | collective-permute-start | bytes 786440 | tf_op jit(solution)/shard_map/far_p/ppermute | solution.py:64
  21.8 3.1 %collective-permute-start.7 = (bf16[32,4096]{1,0:T(8,128)(2,1)S(1)}, bf16[32,4096]{1,0:T(8,128)(2,1)S(1)}, u32[]{:S(2)}, u32[]{:S(2)}) collective-permute-start(bf16[32,4096]{1,0:T(8,128)(2,1)S(1)} %collective-permute-done.refs_0_), channel_id=1, source_target_pairs={{0,2},{1,3},{2,0},{3,1},{4,6},{5,7},{6,4},{7,5},{8,10},{9,11},{10,... | collective-permute-start | bytes 786440 | tf_op jit(solution)/shard_map/far_x/ppermute | solution.py:64
  24.2 4.8 %collective-permute-start.6 = (bf16[32,4096]{1,0:T(8,128)(2,1)S(1)}, bf16[32,4096]{1,0:T(8,128)(2,1)S(1)}, u32[]{:S(2)}, u32[]{:S(2)}) collective-permute-start(bf16[32,4096]{1,0:T(8,128)(2,1)S(1)} %collective-permute-done.3.refs_2_), channel_id=1, source_target_pairs={{0,2},{1,3},{2,0},{3,1},{4,6},{5,7},{6,4},{7,5},{8,10},{9,11},{10,... | collective-permute-start | bytes 786440 | tf_op jit(solution)/shard_map/near_px/ppermute | solution.py:64
  24.8 6.1 %collective-permute-start.9 = (bf16[32,4096]{1,0:T(8,128)(2,1)S(1)}, bf16[32,4096]{1,0:T(8,128)(2,1)S(1)}, u32[]{:S(2)}, u32[]{:S(2)}) collective-permute-start(bf16[32,4096]{1,0:T(8,128)(2,1)S(1)} %collective-permute-done.1.refs_0_), channel_id=1, source_target_pairs={{0,2},{1,3},{2,0},{3,1},{4,6},{5,7},{6,4},{7,5},{8,10},{9,11},{10,... | collective-permute-start | bytes 786440 | tf_op jit(solution)/shard_map/near_x/ppermute | solution.py:64
  27.3 7.3 %collective-permute-start.13 = (bf16[64,1024]{1,0:T(8,128)(2,1)S(1)}, bf16[64,1024]{1,0:T(8,128)(2,1)S(1)}, u32[]{:S(2)}, u32[]{:S(2)}) collective-permute-start(bf16[64,1024]{1,0:T(8,128)(2,1)S(1)} %get-tuple-element.40), channel_id=1, source_target_pairs={{0,1},{1,0},{2,3},{3,2},{4,5},{5,4},{6,7},{7,6},{8,9},{9,8},{10,11... | collective-permute-start | bytes 393224 | tf_op jit(solution)/shard_map/got0/ppermute | solution.py:64
  28.9 2.6 %collective-permute-start.12 = (bf16[32,4096]{1,0:T(8,128)(2,1)S(1)}, bf16[32,4096]{1,0:T(8,128)(2,1)S(1)}, u32[]{:S(2)}, u32[]{:S(2)}) collective-permute-start(bf16[32,4096]{1,0:T(8,128)(2,1)S(1)} %collective-permute-done.11.refs_6_), channel_id=1, source_target_pairs={{0,2},{1,3},{2,0},{3,1},{4,6},{5,7},{6,4},{7,5},{8,10},{9,11},{10,... | collective-permute-start | bytes 786440 | tf_op jit(solution)/shard_map/cross_x/ppermute | solution.py:64
  29.0 2.5 %collective-permute-start.10 = (bf16[32,4096]{1,0:T(8,128)(2,1)S(1)}, bf16[32,4096]{1,0:T(8,128)(2,1)S(1)}, u32[]{:S(2)}, u32[]{:S(2)}) collective-permute-start(bf16[32,4096]{1,0:T(8,128)(2,1)S(1)} %collective-permute-done.2.refs_4_), channel_id=1, source_target_pairs={{0,2},{1,3},{2,0},{3,1},{4,6},{5,7},{6,4},{7,5},{8,10},{9,11},{10,... | collective-permute-start | bytes 786440 | tf_op jit(solution)/shard_map/far_px/ppermute | solution.py:64
  29.4 6.4 %collective-permute-start.14 = (bf16[16,4096]{1,0:T(8,128)(2,1)S(1)}, bf16[16,4096]{1,0:T(8,128)(2,1)S(1)}, u32[]{:S(2)}, u32[]{:S(2)}) collective-permute-start(bf16[16,4096]{1,0:T(8,128)(2,1)S(1)} %get-tuple-element.51), channel_id=1, source_target_pairs={{0,4},{1,5},{2,6},{3,7},{4,0},{5,1},{6,2},{7,3},{8,12},{9,13},{10,... | collective-permute-start | bytes 393224 | tf_op jit(solution)/shard_map/cross_pb/ppermute | solution.py:64
  30.9 11.2 %copy-start.1 = (s32[256]{0:T(256)S(1)}, s32[256]{0:T(256)}, u32[]{:S(2)}) copy-start(s32[256]{0:T(256)} %param.15) | copy-start | bytes 3076
  30.9 11.4 %copy-start = (s32[1024]{0:T(1024)S(1)}, s32[1024]{0:T(1024)}, u32[]{:S(2)}) copy-start(s32[1024]{0:T(1024)} %param.14) | copy-start | bytes 12292
  30.9 6.9 %collective-permute-start.8 = (bf16[16,4096]{1,0:T(8,128)(2,1)S(1)}, bf16[16,4096]{1,0:T(8,128)(2,1)S(1)}, u32[]{:S(2)}, u32[]{:S(2)}) collective-permute-start(bf16[16,4096]{1,0:T(8,128)(2,1)S(1)} %get-tuple-element.52), channel_id=1, source_target_pairs={{0,4},{1,5},{2,6},{3,7},{4,0},{5,1},{6,2},{7,3},{8,12},{9,13},{10,... | collective-permute-start | bytes 393224 | tf_op jit(solution)/shard_map/cross_pa/ppermute | solution.py:64
  34.0 8.3 %collective-permute-start.18 = (bf16[128,1024]{1,0:T(8,128)(2,1)S(1)}, bf16[128,1024]{1,0:T(8,128)(2,1)S(1)}, u32[]{:S(2)}, u32[]{:S(2)}) collective-permute-start(bf16[128,1024]{1,0:T(8,128)(2,1)S(1)} %get-tuple-element.43), channel_id=1, source_target_pairs={{0,1},{1,0},{2,3},{3,2},{4,5},{5,4},{6,7},{7,6},{8,9},{9,8},{10,11... | collective-permute-start | bytes 786440 | tf_op jit(solution)/shard_map/got1/ppermute | solution.py:64
  35.8 2.0 %collective-permute-start.16 = (bf16[16,4096]{1,0:T(8,128)(2,1)S(1)}, bf16[16,4096]{1,0:T(8,128)(2,1)S(1)}, u32[]{:S(2)}, u32[]{:S(2)}) collective-permute-start(bf16[16,4096]{1,0:T(8,128)(2,1)S(1)} %collective-permute-done.14.refs_1_), channel_id=1, source_target_pairs={{0,2},{1,3},{2,0},{3,1},{4,6},{5,7},{6,4},{7,5},{8,10},{9,11},{10,... | collective-permute-start | bytes 393224 | tf_op jit(solution)/shard_map/cross_pxb/ppermute | solution.py:64
  37.8 1.3 %collective-permute-start.15 = (bf16[16,4096]{1,0:T(8,128)(2,1)S(1)}, bf16[16,4096]{1,0:T(8,128)(2,1)S(1)}, u32[]{:S(2)}, u32[]{:S(2)}) collective-permute-start(bf16[16,4096]{1,0:T(8,128)(2,1)S(1)} %collective-permute-done.8.refs_0_), channel_id=1, source_target_pairs={{0,2},{1,3},{2,0},{3,1},{4,6},{5,7},{6,4},{7,5},{8,10},{9,11},{10,... | collective-permute-start | bytes 393224 | tf_op jit(solution)/shard_map/cross_pxa/ppermute | solution.py:64
  41.6 5.6 %collective-permute-start.17 = (bf16[64,1024]{1,0:T(8,128)(2,1)S(1)}, bf16[64,1024]{1,0:T(8,128)(2,1)S(1)}, u32[]{:S(2)}, u32[]{:S(2)}) collective-permute-start(bf16[64,1024]{1,0:T(8,128)(2,1)S(1)} %get-tuple-element.48), channel_id=1, source_target_pairs={{0,1},{1,0},{2,3},{3,2},{4,5},{5,4},{6,7},{7,6},{8,9},{9,8},{10,11... | collective-permute-start | bytes 393224 | tf_op jit(solution)/shard_map/got2/ppermute | solution.py:64
